TPU v7x, 32 devices: a whole 2x2x4 slice. The times are simulated.
32 devices in a mesh: parts: 2 (over x), expert: 16 (over z, y, core).
Axes of the slice: x: 2, y: 2, z: 4, core: 2. Of those that a mesh axis runs over, the one named last changes fastest.
Arguments:
- activations: bfloat16 [768, 6144], P(('parts', 'expert')), parts along dimension 0, may hold values from -6 to 6
- expert_ids: int32 [768, 2], P(('parts', 'expert')), parts along dimension 0, may hold values from 0 to 3, all different within a row; in each aligned block of 24 rows (0 to 23, 24 to 47, ...) at most 16 rows name the same one
- route_logits: float32 [768, 2], P(('parts', 'expert')), parts along dimension 0, may hold values from -6 to 6
- norm_gain: float32 [6144], replicated, may hold values from 0.25 to 1.75
- w_gate: bfloat16 [18432, 6144], P('expert'), may hold values from -0.078125 to 0.078125
- w_up: bfloat16 [18432, 6144], P('expert'), may hold values from -0.078125 to 0.078125
- w_down: bfloat16 [18432, 6144], P('expert'), may hold values from -0.09375 to 0.09375
Outputs:
- mixed: bfloat16 [768, 6144], P(('parts', 'expert')), parts along dimension 0
There are 2 independent parts, one for each index of `parts`. A program takes and returns all parts, laid end to end along the dimension named above; an argument that names none is the same for every part. Nothing has to cross between parts.
Inputs may be any that keep to these rules, and one draw needn't show every extreme that they name: `expert_ids`: each row names two different experts; among the rows of one device no expert is named more than 16 times, a bound that some block reaches.
All inputs are finite; a program needn't handle non-finite values.
Results may differ from a plain program's by a relative error of at most 0.0054.
Values may be sent and summed in bfloat16 or wider, within the bound.
No kernel may reach another device: no remote copies, remote signals or barrier semaphores. Data moves between devices by JAX's collectives and lax.ppermute only.
A program may use at most 128 MiB of HBM per device.

v0:
```python
import jax
import jax.numpy as jnp
from jax import lax
from jax.sharding import PartitionSpec as P

EXPERTS = 4
CAP = 16


def on_device(activations, expert_ids, route_logits, norm_gain, w_gate, w_up, w_down):
    group = lax.axis_size("expert") // EXPERTS
    tok_rows = activations.shape[0]
    width = activations.shape[1]
    values = activations.astype(jnp.float32)
    mean_sq = jnp.mean(values * values, axis=-1, keepdims=True)
    normed = (values * lax.rsqrt(mean_sq + 1e-06) * norm_gain).astype(jnp.bfloat16)
    flat_ids = expert_ids.reshape(-1)
    one_hot = (flat_ids[:, None] == jnp.arange(EXPERTS, dtype=jnp.int32)[None, :]).astype(jnp.int32)
    ranking = jnp.cumsum(one_hot, axis=0) - one_hot
    slot_index = jnp.sum(ranking * one_hot, axis=1)
    position = flat_ids * CAP + slot_index
    row_owner = jnp.arange(2 * tok_rows, dtype=jnp.int32) // 2 + 1
    source_rows = jnp.zeros((EXPERTS * CAP,), jnp.int32).at[position].set(row_owner)
    live = source_rows > 0
    safe = jnp.maximum(source_rows - 1, 0)
    send_rows = jnp.where(live[:, None], normed[safe], jnp.zeros((), jnp.bfloat16))
    send_rows = send_rows.reshape(EXPERTS, CAP, width)
    copies = jnp.broadcast_to(send_rows[:, None], (EXPERTS, group, CAP, width))
    copies = copies.reshape(EXPERTS * group, CAP, width)
    received = lax.all_to_all(copies, "expert", split_axis=0, concat_axis=0, tiled=True)
    senders = received.shape[0]
    slots = received.shape[1]
    rows = received.reshape(senders * slots, width)
    gate = lax.dot_general(
        rows, w_gate, (((1,), (1,)), ((), ())), preferred_element_type=jnp.float32
    )
    upper = lax.dot_general(
        rows, w_up, (((1,), (1,)), ((), ())), preferred_element_type=jnp.float32
    )
    hidden = (jax.nn.silu(gate) * upper).astype(jnp.bfloat16)
    partial_rows = jnp.dot(hidden, w_down, preferred_element_type=jnp.float32).astype(jnp.bfloat16)
    partials = partial_rows.reshape(senders, slots, width)
    returned = lax.all_to_all(partials, "expert", split_axis=0, concat_axis=0, tiled=True)
    returned = returned.reshape(EXPERTS, group, CAP, width)
    expert_out = jnp.sum(returned.astype(jnp.float32), axis=1).astype(jnp.bfloat16)
    out_rows = expert_out.reshape(EXPERTS * CAP, width)[position].reshape(tok_rows, 2, width)
    weights = jax.nn.sigmoid(route_logits - route_logits[:, ::-1])
    mixed = (
        values
        + weights[:, 0:1] * out_rows[:, 0].astype(jnp.float32)
        + weights[:, 1:2] * out_rows[:, 1].astype(jnp.float32)
    )
    return mixed.astype(jnp.bfloat16)


def solution(mesh):
    in_specs = (
        P(("parts", "expert"), None),
        P(("parts", "expert"), None),
        P(("parts", "expert"), None),
        P(),
        P("expert", None),
        P("expert", None),
        P("expert", None),
    )
    out_specs = P(("parts", "expert"), None)
    return jax.shard_map(
        on_device, mesh=mesh, in_specs=in_specs, out_specs=out_specs, check_vma=False
    )
```

profile of v0, /device:TPU:13, one launch (start us, length us, event | category | flops | bytes accessed | tf_op | source)
XLA Modules:
  0.0 190.2 jit_solution(12825646408779112157)
XLA Ops:
  0.0 0.8 copy.11
  0.8 0.7 broadcast_multiply_fusion
  1.4 0.1 eq.15
  1.5 0.1 fusion.6
  1.6 0.1 reduce_window_sum.11
  1.7 0.2 select_reduce_fusion
  1.9 0.1 copy.10
  2.0 0.1 mul.69
  2.1 0.7 scatter_custom_fusion
  2.9 1.1 fusion.1
  4.0 0.1 broadcast_in_dim.28
  4.1 1.1 fusion.3
  5.2 1.0 gather_fusion
  6.2 0.1 broadcast_select_fusion
  6.3 0.4 broadcast_in_dim.32
  6.7 76.1 %all_to_all.10 = bf16[16,16,6144]{2,1,0:T(8,128)(2,1)S(1)} all-to-all(bf16[16,16,6144]{2,1,0:T(8,128)(2,1)S(1)} %bitcast.34), channel_id=1, replica_groups=mesh['parts'=2,'expert'=16] {'expert'}, dimensions={0} | all-to-all | bytes 6291456 | tf_op jit(solution)/shard_map/all_to_all | solution.py:30
  82.9 7.5 %fusion.12 = f32[256,1152]{1,0:T(8,128)S(1)} fusion(bf16[256,6144]{1,0:T(8,128)(2,1)S(1)} %bitcast.36, bf16[1152,6144]{1,0:T(8,128)(2,1)} %param.11), kind=kOutput, calls=%fused_computation.43 | convolution fusion | flops 3623878656 | bytes 18481152 | tf_op jit(solution)/shard_map/dot_general | solution.py:34
  90.4 7.8 %fusion = bf16[256,1152]{1,0:T(8,128)(2,1)S(1)} fusion(bf16[256,6144]{1,0:T(8,128)(2,1)S(1)} %bitcast.37, bf16[1152,6144]{1,0:T(8,128)(2,1)} %param.12, f32[256,1152]{1,0:T(8,128)S(1)} %fusion.12), kind=kOutput, calls=%fused_computation.6 | convolution fusion | flops 3625648128 | bytes 19070976 | tf_op jit(solution)/shard_map/dot_general | solution.py:37
  98.2 11.0 %convolution_convert_fusion = bf16[256,6144]{1,0:T(8,128)(2,1)} fusion(bf16[256,1152]{1,0:T(8,128)(2,1)S(1)} %fusion, bf16[1152,6144]{1,0:T(8,128)(2,1)} %param.13), kind=kOutput, calls=%fused_computation.3 | convolution fusion | flops 3625451520 | bytes 17891328 | tf_op jit(solution)/shard_map/dot_general | solution.py:41
  109.2 0.0 copy-start.1
  109.2 5.3 %all-to-all-start.1 = ((bf16[16,16,6144]{2,1,0:T(8,128)(2,1)}), bf16[16,16,6144]{2,1,0:T(8,128)(2,1)}, u32[]{:S(2)}, u32[]{:S(2)}) async-start(bf16[16,16,6144]{2,1,0:T(8,128)(2,1)} %bitcast.6), calls=%async_computation.1 | async-start | bytes 6291456 | tf_op jit(solution)/shard_map/all_to_all | solution.py:43
  114.5 0.0 copy-done.1
  114.6 69.9 %all-to-all-done.1 = bf16[16,16,6144]{2,1,0:T(8,128)(2,1)} async-done(((bf16[16,16,6144]{2,1,0:T(8,128)(2,1)}), bf16[16,16,6144]{2,1,0:T(8,128)(2,1)}, u32[]{:S(2)}, u32[]{:S(2)}) %all-to-all-start.1) | async-done | bytes 3145760 | tf_op jit(solution)/shard_map/all_to_all | solution.py:43
  184.5 2.4 %bitcast_reduce_fusion = bf16[4,16,6144]{2,1,0:T(8,128)(2,1)S(1)} fusion(bf16[16,16,6144]{2,1,0:T(8,128)(2,1)} %all-to-all-done.1), kind=kLoop, calls=%fused_computation.4 | loop fusion | flops 1179648 | bytes 3932160 | tf_op jit(solution)/shard_map/reduce_sum | solution.py:45
  186.9 0.0 copy-start
  186.9 0.9 gather_fusion.1
  187.8 0.4 reshape.79
  188.2 0.8 fusion.11
  189.0 0.0 copy-done
  189.1 1.1 fusion.5
  (10 shorter events, 0.1 us)
Async XLA Ops:
  109.2 5.3 %copy-start.1 = (f32[24,2]{0,1:T(2,128)S(1)}, f32[24,2]{0,1:T(2,128)}, u32[]{:S(2)}) copy-start(f32[24,2]{0,1:T(2,128)} %param.9) | copy-start | bytes 580
  109.2 75.3 %all-to-all-start.1 = ((bf16[16,16,6144]{2,1,0:T(8,128)(2,1)}), bf16[16,16,6144]{2,1,0:T(8,128)(2,1)}, u32[]{:S(2)}, u32[]{:S(2)}) async-start(bf16[16,16,6144]{2,1,0:T(8,128)(2,1)} %bitcast.6), calls=%async_computation.1 | async-start | bytes 6291456 | tf_op jit(solution)/shard_map/all_to_all | solution.py:43
  186.9 2.1 %copy-start = (bf16[24,6144]{1,0:T(8,128)(2,1)S(1)}, bf16[24,6144]{1,0:T(8,128)(2,1)}, u32[]{:S(2)}) copy-start(bf16[24,6144]{1,0:T(8,128)(2,1)} %param.7) | copy-start | bytes 884740
where the time goes:
time: 191 us; the launch traced here: 190 us
  blocking collectives  76.1 us (40%)
  waiting for transfers between devices  69.9 us (37%)
  matrix products  26.3 us (14%)
  other arithmetic  6.91 us (4%)
  local copies, waits for them, and re-layouts  5.38 us (3%)
  starting transfers between devices  5.33 us (3%)
    all_to_all x1, blocking collectives, on_device(): lax.all_to_all(copies, 'expert', split_axis=0, concat_axis=0, tiled=True)  76.1 us
    all_to_all x1, waiting for transfers between devices, on_device(): lax.all_to_all(partials, 'expert', split_axis=0, concat_axis=0, tiled=True)  69.9 us
    dot_general x1, matrix products, on_device(): jnp.dot(hidden, w_down, preferred_element_type=jnp.float32)  11 us
    dot_general x1, matrix products, on_device(): lax.dot_general(rows, w_up, (((1,), (1,)), ((), ())), preferred_element_t...  7.84 us
    dot_general x1, matrix products, on_device(): lax.dot_general(rows, w_gate, (((1,), (1,)), ((), ())), preferred_element...  7.52 us
    all_to_all x1, starting transfers between devices, on_device(): lax.all_to_all(partials, 'expert', split_axis=0, concat_axis=0, tiled=True)  5.33 us
  transfers between devices with their start and end apart: 1, of which 1 were waited for; matrix products, arithmetic and copies ran while one was open for 0% of the time, Pallas kernels for 0%

commit v1 on v0

v1 whole, which is shorter than its diff:
```python
import functools

import jax
import jax.numpy as jnp
from jax import lax
from jax.experimental import pallas as pl
from jax.experimental.pallas import tpu as pltpu
from jax.sharding import PartitionSpec as P

EXPERTS = 4
CAP = 16
CHUNKS = 4
MIB = 1 << 20


def choices(ids, plane):
    tokens = ids.shape[0]
    shape = (tokens, EXPERTS * CAP)
    lane = lax.broadcasted_iota(jnp.int32, shape, 1)
    expert = lax.rem(lane // CAP + plane, EXPERTS)
    slot = (lane % CAP).astype(jnp.float32)
    first = ids[:, 0:1] == expert
    second = ids[:, 1:2] == expert
    named = (first | second).astype(jnp.float32)
    earlier = lax.broadcasted_iota(jnp.int32, (tokens, tokens), 0) > lax.broadcasted_iota(
        jnp.int32, (tokens, tokens), 1
    )
    rank = jnp.dot(earlier.astype(jnp.float32), named, preferred_element_type=jnp.float32)
    here = rank == slot
    return first & here, second & here


def pack_kernel(group, ids_ref, act_ref, gain_ref, *out_refs):
    plane = lax.axis_index("expert") // group
    values = act_ref[...].astype(jnp.float32)
    mean_sq = jnp.mean(values * values, axis=-1, keepdims=True)
    normed = (values * lax.rsqrt(mean_sq + 1e-06) * gain_ref[...]).astype(jnp.bfloat16)
    first, second = choices(ids_ref[...], plane)
    pick = (first | second).astype(jnp.float32).astype(jnp.bfloat16)
    width = out_refs[0].shape[1]
    for k in range(len(out_refs) // EXPERTS):
        rows = lax.dot_general(
            pick,
            normed[:, k * width : (k + 1) * width],
            (((0,), (0,)), ((), ())),
            preferred_element_type=jnp.float32,
        ).astype(jnp.bfloat16)
        for s in range(EXPERTS):
            out_refs[k * EXPERTS + s][...] = rows[s * CAP : (s + 1) * CAP]


def pack(group, ids, activations, gain):
    width = activations.shape[1]
    part = width // CHUNKS
    return pl.pallas_call(
        functools.partial(pack_kernel, group),
        out_shape=[jax.ShapeDtypeStruct((CAP, part), jnp.bfloat16)] * (CHUNKS * EXPERTS),
        compiler_params=pltpu.CompilerParams(vmem_limit_bytes=16 * MIB),
        name="norm_and_pack",
    )(ids, activations, gain.reshape(1, width))


def gate_up_kernel(count, begin, end, *refs):
    pieces, refs = refs[:count], refs[count:]
    gate_w, up_w, refs = refs[0], refs[1], refs[2:]
    held, refs = refs[-1], refs[:-1]

    @pl.when(pl.program_id(0) == 0)
    def _():
        at = 0
        for piece in pieces:
            held[at : at + piece.shape[0], :] = piece[...]
            at += piece.shape[0]

    dims = (((1,), (1,)), ((), ()))
    gate = lax.dot_general(held[...], gate_w[...], dims, preferred_element_type=jnp.float32)
    upper = lax.dot_general(held[...], up_w[...], dims, preferred_element_type=jnp.float32)
    if not begin:
        gate = gate + refs[0][...]
        upper = upper + refs[1][...]
        refs = refs[2:]
    if end:
        refs[0][...] = (jax.nn.silu(gate) * upper).astype(jnp.bfloat16)
    else:
        refs[0][...] = gate
        refs[1][...] = upper


def gate_up(k, pieces, w_gate, w_up, totals):
    begin, end = k == 0, k == CHUNKS - 1
    hidden = w_gate.shape[0]
    part = pieces[0].shape[1]
    rows = sum(p.shape[0] for p in pieces)
    block = 384 if hidden % 384 == 0 else hidden
    total_spec = pl.BlockSpec((rows, block), lambda h: (0, h))
    weight_spec = pl.BlockSpec((block, part), lambda h: (h, k))
    in_specs = [pl.BlockSpec(p.shape, lambda h: (0, 0)) for p in pieces] + [weight_spec] * 2
    in_specs += [total_spec] * len(totals)
    total = jax.ShapeDtypeStruct((rows, hidden), jnp.float32)
    if end:
        out_shape = [jax.ShapeDtypeStruct((rows, hidden), jnp.bfloat16)]
        aliases = {}
    else:
        out_shape = [total, total]
        aliases = {} if begin else {len(pieces) + 2: 0, len(pieces) + 3: 1}
    return pl.pallas_call(
        functools.partial(gate_up_kernel, len(pieces), begin, end),
        grid=(hidden // block,),
        in_specs=in_specs,
        out_specs=[total_spec] * len(out_shape),
        out_shape=out_shape,
        scratch_shapes=[pltpu.VMEM((rows, part), jnp.bfloat16)],
        input_output_aliases=aliases,
        compiler_params=pltpu.CompilerParams(vmem_limit_bytes=24 * MIB),
        cost_estimate=pl.CostEstimate(
            flops=4 * rows * hidden * part,
            bytes_accessed=4 * hidden * part + 16 * rows * hidden,
            transcendentals=0,
        ),
        name="gate_up",
    )(*pieces, w_gate, w_up, *totals)


def down_kernel(hidden_ref, w_ref, keep_ref, send_ref):
    out = jnp.dot(hidden_ref[...], w_ref[...], preferred_element_type=jnp.float32)
    out = out.astype(jnp.bfloat16)
    half = keep_ref.shape[0]
    keep_ref[...] = out[:half]
    send_ref[...] = out[half:]


def down(k, hidden, w_down):
    rows, depth = hidden.shape
    part = w_down.shape[1] // CHUNKS
    block = 512
    steps = part // block
    half = pl.BlockSpec((rows // 2, block), lambda c: (0, c))
    return pl.pallas_call(
        down_kernel,
        grid=(steps,),
        in_specs=[
            pl.BlockSpec((rows, depth), lambda c: (0, 0)),
            pl.BlockSpec((depth, block), lambda c: (0, k * steps + c)),
        ],
        out_specs=[half, half],
        out_shape=[jax.ShapeDtypeStruct((rows // 2, part), jnp.bfloat16)] * 2,
        compiler_params=pltpu.CompilerParams(vmem_limit_bytes=24 * MIB),
        cost_estimate=pl.CostEstimate(
            flops=2 * rows * depth * part,
            bytes_accessed=2 * (depth * part + rows * depth + rows * part),
            transcendentals=0,
        ),
        name="down",
    )(hidden, w_down)


def mix_kernel(group, ids_ref, logits_ref, act_ref, *refs):
    pieces, out_ref = refs[:-1], refs[-1]
    plane = lax.axis_index("expert") // group
    first, second = choices(ids_ref[...], plane)
    first = first.astype(jnp.float32).astype(jnp.bfloat16)
    second = second.astype(jnp.float32).astype(jnp.bfloat16)
    logits = logits_ref[...]
    lead = logits[:, 0:1] - logits[:, 1:2]
    weight_first = jax.nn.sigmoid(lead)
    weight_second = jax.nn.sigmoid(-lead)
    part = pieces[0].shape[1]
    for k in range(len(pieces) // EXPERTS):
        rows = jnp.concatenate([p[...] for p in pieces[k * EXPERTS : (k + 1) * EXPERTS]], axis=0)
        out_first = jnp.dot(first, rows, preferred_element_type=jnp.float32)
        out_second = jnp.dot(second, rows, preferred_element_type=jnp.float32)
        columns = slice(k * part, (k + 1) * part)
        values = act_ref[:, columns].astype(jnp.float32)
        out_ref[:, columns] = (
            values + weight_first * out_first + weight_second * out_second
        ).astype(jnp.bfloat16)


def mix(group, ids, logits, activations, pieces):
    return pl.pallas_call(
        functools.partial(mix_kernel, group),
        out_shape=jax.ShapeDtypeStruct(activations.shape, jnp.bfloat16),
        compiler_params=pltpu.CompilerParams(vmem_limit_bytes=16 * MIB),
        name="mix",
    )(ids, logits, activations, *pieces)


def on_device(activations, expert_ids, route_logits, norm_gain, w_gate, w_up, w_down):
    devices = lax.axis_size("expert")
    group = devices // EXPERTS

    def shift(x, s):
        return lax.ppermute(
            x, "expert", [(i, (i + s * group) % devices) for i in range(devices)]
        )

    def swap(x, bit):
        return lax.ppermute(x, "expert", [(i, i ^ bit) for i in range(devices)])

    packed = pack(group, expert_ids, activations, norm_gain)
    totals = []
    for k in range(CHUNKS):
        own = packed[k * EXPERTS : (k + 1) * EXPERTS]
        gathered = [own[0]] + [shift(own[s], s) for s in range(1, EXPERTS)]
        pieces = [jnp.concatenate(gathered, axis=0)]
        bit = group // 2
        while bit:
            block = pieces[0] if len(pieces) == 1 else jnp.concatenate(pieces, axis=0)
            pieces.append(swap(block, bit))
            bit //= 2
        totals = gate_up(k, pieces, w_gate, w_up, totals)
    hidden = totals[0]
    returned = []
    for k in range(CHUNKS):
        keep, send = down(k, hidden, w_down)
        bit = 1
        while bit < group:
            arrived = swap(send, bit)
            total = keep.astype(jnp.float32) + arrived.astype(jnp.float32)
            total = total.astype(jnp.bfloat16)
            half = total.shape[0] // 2
            keep, send = total[:half], total[half:]
            bit *= 2
        blocks = [total[s * CAP : (s + 1) * CAP] for s in range(EXPERTS)]
        returned.append(blocks[0])
        returned += [shift(blocks[s], -s) for s in range(1, EXPERTS)]
    return mix(group, expert_ids, route_logits, activations, returned)


def solution(mesh):
    in_specs = (
        P(("parts", "expert"), None),
        P(("parts", "expert"), None),
        P(("parts", "expert"), None),
        P(),
        P("expert", None),
        P("expert", None),
        P("expert", None),
    )
    out_specs = P(("parts", "expert"), None)
    return jax.shard_map(
        on_device, mesh=mesh, in_specs=in_specs, out_specs=out_specs, check_vma=False
    )
```

time: 191 us -> 119 us (0.62)
  the two profiles are of different devices: /device:TPU:13 before, /device:TPU:0 now
where the time goes in v1:
time: 119 us
  starting transfers between devices  43.7 us (37%)
  Pallas kernels  31.1 us (26%)
  waiting for transfers between devices  27.7 us (23%)
  local copies, waits for them, and re-layouts  15.1 us (13%)
    ppermute x24, starting transfers between devices, shift(): lax.ppermute(x, 'expert', [(i, (i + s * group) % devices) for i in range(...  33.6 us
    ppermute x16, waiting for transfers between devices, swap(): return lax.ppermute(x, 'expert', [(i, i ^ bit) for i in range(devices)])  21.7 us
    pallas_call x4, Pallas kernels, gate_up(): pl.pallas_call(functools.partial(gate_up_kernel, len(pieces), begin, end)...  21.7 us
    unnamed x52, local copies, waits for them, and re-layouts  14.2 us
    ppermute x16, starting transfers between devices, swap(): return lax.ppermute(x, 'expert', [(i, i ^ bit) for i in range(devices)])  10.1 us
    pallas_call x4, Pallas kernels, down(): pl.pallas_call(down_kernel, grid=(steps,), in_specs=[pl.BlockSpec((rows,...  7.53 us
    ppermute x24, waiting for transfers between devices, shift(): lax.ppermute(x, 'expert', [(i, (i + s * group) % devices) for i in range(...  5.98 us
  transfers between devices with their start and end apart: 40, of which 13 were waited for; matrix products, arithmetic and copies ran while one was open for 3% of the time, Pallas kernels for 19%

profile of v1, /device:TPU:0, one launch (start us, length us, event | category | flops | bytes accessed | tf_op | source)
XLA Modules:
  0.0 118.5 jit_solution(16892227974765289827)
XLA Ops:
  0.0 0.8 copy.13.ids_ref
  0.8 1.0 copy-done.2
  1.7 0.7 copy-done.8
  2.5 0.6 norm_and_pack.1
  3.1 3.1 %collective-permute-start.15 = (bf16[16,1536]{1,0:T(8,128)(2,1)S(1)}, bf16[16,1536]{1,0:T(8,128)(2,1)S(1)}, u32[]{:S(2)}, u32[]{:S(2)}) collective-permute-start(bf16[16,1536]{1,0:T(8,128)(2,1)S(1)} %get-tuple-element.48), channel_id=1, source_target_pairs={{0,4},{1,5},{2,6},{3,7},{4,8},{5,9},{6,10},{7,11},{8,12},{9,13},{1... | collective-permute-start | bytes 147464 | tf_op jit(solution)/shard_map/ppermute | solution.py:193
  6.1 2.6 %collective-permute-start.16 = (bf16[16,1536]{1,0:T(8,128)(2,1)S(1)}, bf16[16,1536]{1,0:T(8,128)(2,1)S(1)}, u32[]{:S(2)}, u32[]{:S(2)}) collective-permute-start(bf16[16,1536]{1,0:T(8,128)(2,1)S(1)} %get-tuple-element.49), channel_id=1, source_target_pairs={{0,8},{1,9},{2,10},{3,11},{4,12},{5,13},{6,14},{7,15},{8,0},{9,1},... | collective-permute-start | bytes 147464 | tf_op jit(solution)/shard_map/ppermute | solution.py:193
  8.7 1.3 %collective-permute-start.17 = (bf16[16,1536]{1,0:T(8,128)(2,1)S(1)}, bf16[16,1536]{1,0:T(8,128)(2,1)S(1)}, u32[]{:S(2)}, u32[]{:S(2)}) collective-permute-start(bf16[16,1536]{1,0:T(8,128)(2,1)S(1)} %get-tuple-element.50), channel_id=1, source_target_pairs={{0,12},{1,13},{2,14},{3,15},{4,0},{5,1},{6,2},{7,3},{8,4},{9,5},{1... | collective-permute-start | bytes 147464 | tf_op jit(solution)/shard_map/ppermute | solution.py:193
  10.1 0.7 collective-permute-start.10
  11.1 0.6 constant_dynamic-update-slice_fusion.8
  11.7 2.8 %collective-permute-start.12 = (bf16[16,1536]{1,0:T(8,128)(2,1)S(1)}, bf16[16,1536]{1,0:T(8,128)(2,1)S(1)}, u32[]{:S(2)}, u32[]{:S(2)}) collective-permute-start(bf16[16,1536]{1,0:T(8,128)(2,1)S(1)} %get-tuple-element.46), channel_id=1, source_target_pairs={{0,12},{1,13},{2,14},{3,15},{4,0},{5,1},{6,2},{7,3},{8,4},{9,5},{1... | collective-permute-start | bytes 147464 | tf_op jit(solution)/shard_map/ppermute | solution.py:193
  14.6 0.6 collective-permute-start.5
  15.2 1.5 %collective-permute-start.6 = (bf16[16,1536]{1,0:T(8,128)(2,1)S(1)}, bf16[16,1536]{1,0:T(8,128)(2,1)S(1)}, u32[]{:S(2)}, u32[]{:S(2)}) collective-permute-start(bf16[16,1536]{1,0:T(8,128)(2,1)S(1)} %get-tuple-element.41), channel_id=1, source_target_pairs={{0,8},{1,9},{2,10},{3,11},{4,12},{5,13},{6,14},{7,15},{8,0},{9,1},... | collective-permute-start | bytes 147464 | tf_op jit(solution)/shard_map/ppermute | solution.py:193
  16.8 3.0 %collective-permute-start.7 = (bf16[16,1536]{1,0:T(8,128)(2,1)S(1)}, bf16[16,1536]{1,0:T(8,128)(2,1)S(1)}, u32[]{:S(2)}, u32[]{:S(2)}) collective-permute-start(bf16[16,1536]{1,0:T(8,128)(2,1)S(1)} %get-tuple-element.42), channel_id=1, source_target_pairs={{0,12},{1,13},{2,14},{3,15},{4,0},{5,1},{6,2},{7,3},{8,4},{9,5},{1... | collective-permute-start | bytes 147464 | tf_op jit(solution)/shard_map/ppermute | solution.py:193
  19.8 1.4 %collective-permute-start.1 = (bf16[16,1536]{1,0:T(8,128)(2,1)S(1)}, bf16[16,1536]{1,0:T(8,128)(2,1)S(1)}, u32[]{:S(2)}, u32[]{:S(2)}) collective-permute-start(bf16[16,1536]{1,0:T(8,128)(2,1)S(1)} %get-tuple-element.37), channel_id=1, source_target_pairs={{0,8},{1,9},{2,10},{3,11},{4,12},{5,13},{6,14},{7,15},{8,0},{9,1},... | collective-permute-start | bytes 147464 | tf_op jit(solution)/shard_map/ppermute | solution.py:193
  21.3 2.5 %collective-permute-start.2 = (bf16[16,1536]{1,0:T(8,128)(2,1)S(1)}, bf16[16,1536]{1,0:T(8,128)(2,1)S(1)}, u32[]{:S(2)}, u32[]{:S(2)}) collective-permute-start(bf16[16,1536]{1,0:T(8,128)(2,1)S(1)} %get-tuple-element.38), channel_id=1, source_target_pairs={{0,12},{1,13},{2,14},{3,15},{4,0},{5,1},{6,2},{7,3},{8,4},{9,5},{1... | collective-permute-start | bytes 147464 | tf_op jit(solution)/shard_map/ppermute | solution.py:193
  23.8 1.6 %collective-permute-start.18 = (bf16[64,1536]{1,0:T(8,128)(2,1)S(1)}, bf16[64,1536]{1,0:T(8,128)(2,1)S(1)}, u32[]{:S(2)}, u32[]{:S(2)}) collective-permute-start(bf16[64,1536]{1,0:T(8,128)(2,1)S(1)} %get-tuple-element.82.refs_0_), channel_id=1, source_target_pairs={{0,2},{1,3},{2,0},{3,1},{4,6},{5,7},{6,4},{7,5},{8,10},{9,11},{10,... | collective-permute-start | bytes 589832 | tf_op jit(solution)/shard_map/ppermute | solution.py:198
  25.4 0.6 collective-permute-start.13
  26.0 1.6 %collective-permute-start.8 = (bf16[64,1536]{1,0:T(8,128)(2,1)S(1)}, bf16[64,1536]{1,0:T(8,128)(2,1)S(1)}, u32[]{:S(2)}, u32[]{:S(2)}) collective-permute-start(bf16[64,1536]{1,0:T(8,128)(2,1)S(1)} %get-tuple-element.98.refs_0_), channel_id=1, source_target_pairs={{0,2},{1,3},{2,0},{3,1},{4,6},{5,7},{6,4},{7,5},{8,10},{9,11},{10,... | collective-permute-start | bytes 589832 | tf_op jit(solution)/shard_map/ppermute | solution.py:198
  27.6 0.6 constant_dynamic-update-slice_fusion.7
  28.2 0.6 constant_dynamic-update-slice_fusion.6
  28.8 0.6 constant_dynamic-update-slice_fusion.5
  29.4 0.5 collective-permute-start.3
  29.9 1.8 %collective-permute-done.18.refs_1_ = bf16[64,1536]{1,0:T(8,128)(2,1)S(1)} collective-permute-done((bf16[64,1536]{1,0:T(8,128)(2,1)S(1)}, bf16[64,1536]{1,0:T(8,128)(2,1)S(1)}, u32[]{:S(2)}, u32[]{:S(2)}) %collective-permute-start.18) | collective-permute-done | bytes 196640 | tf_op jit(solution)/shard_map/ppermute | solution.py:198
  31.8 4.0 %collective-permute-done.13.refs_1_ = bf16[64,1536]{1,0:T(8,128)(2,1)S(1)} collective-permute-done((bf16[64,1536]{1,0:T(8,128)(2,1)S(1)}, bf16[64,1536]{1,0:T(8,128)(2,1)S(1)}, u32[]{:S(2)}, u32[]{:S(2)}) %collective-permute-start.13) | collective-permute-done | bytes 196640 | tf_op jit(solution)/shard_map/ppermute | solution.py:198
  35.9 2.0 %collective-permute-done.8.refs_1_ = bf16[64,1536]{1,0:T(8,128)(2,1)S(1)} collective-permute-done((bf16[64,1536]{1,0:T(8,128)(2,1)S(1)}, bf16[64,1536]{1,0:T(8,128)(2,1)S(1)}, u32[]{:S(2)}, u32[]{:S(2)}) %collective-permute-start.8) | collective-permute-done | bytes 196640 | tf_op jit(solution)/shard_map/ppermute | solution.py:198
  38.0 2.0 %collective-permute-done.3.refs_1_ = bf16[64,1536]{1,0:T(8,128)(2,1)S(1)} collective-permute-done((bf16[64,1536]{1,0:T(8,128)(2,1)S(1)}, bf16[64,1536]{1,0:T(8,128)(2,1)S(1)}, u32[]{:S(2)}, u32[]{:S(2)}) %collective-permute-start.3) | collective-permute-done | bytes 196640 | tf_op jit(solution)/shard_map/ppermute | solution.py:198
  40.0 0.7 constant_dynamic-update-slice_fusion.4
  40.8 5.0 %copy-done = bf16[1152,6144]{1,0:T(8,128)(2,1)S(1)} copy-done((bf16[1152,6144]{1,0:T(8,128)(2,1)S(1)}, bf16[1152,6144]{1,0:T(8,128)(2,1)}, u32[]{:S(2)}) %copy-start) | copy-done | bytes 14155800
  45.8 5.5 %gate_up.4 = (f32[256,1152]{1,0:T(8,128)S(1)}, f32[256,1152]{1,0:T(8,128)S(1)}) custom-call(bf16[64,1536]{1,0:T(8,128)(2,1)S(1)} %get-tuple-element.82.refs_0_, bf16[64,1536]{1,0:T(8,128)(2,1)S(1)} %collective-permute-done.18.refs_1_, bf16[128,1536]{1,0:T(8,128)(2,1)S(1)} %collective-permute-done.19.refs_2_, bf16[1152,6144]{1,0:T(8,128)(2,1)S(1)} %copy-done, ...), custom_call_target="tpu_custom_call" | custom-call | flops 1811939328 | bytes 11796480 | tf_op jit(solution)/shard_map/gate_up/pallas_call | solution.py:106
  51.3 0.5 copy-done.1
  51.9 5.5 %gate_up.5 = (f32[256,1152]{1,0:T(8,128)S(1)}, f32[256,1152]{1,0:T(8,128)S(1)}) custom-call(bf16[64,1536]{1,0:T(8,128)(2,1)S(1)} %get-tuple-element.90.refs_0_, bf16[64,1536]{1,0:T(8,128)(2,1)S(1)} %collective-permute-done.13.refs_1_, bf16[128,1536]{1,0:T(8,128)(2,1)S(1)} %collective-permute-done.14.refs_2_, ...), custom_call_target="tpu_custom_call", output_to_operand_aliasing={{0}: (5, {}), {1}: (6, {})} | custom-call | flops 1811939328 | bytes 11796480 | tf_op jit(solution)/shard_map/gate_up/pallas_call | solution.py:106
  57.4 0.7 copy-done.6
  58.1 1.0 copy-done.7
  59.1 5.8 %gate_up.6 = (f32[256,1152]{1,0:T(8,128)S(1)}, f32[256,1152]{1,0:T(8,128)S(1)}) custom-call(bf16[64,1536]{1,0:T(8,128)(2,1)S(1)} %get-tuple-element.98.refs_0_, bf16[64,1536]{1,0:T(8,128)(2,1)S(1)} %collective-permute-done.8.refs_1_, bf16[128,1536]{1,0:T(8,128)(2,1)S(1)} %copy-done.7, ...), custom_call_target="tpu_custom_call", output_to_operand_aliasing={{0}: (5, {}), {1}: (6, {})} | custom-call | flops 1811939328 | bytes 11796480 | tf_op jit(solution)/shard_map/gate_up/pallas_call | solution.py:106
  64.9 0.7 copy-done.4
  65.7 1.0 copy-done.5
  66.7 4.9 %gate_up.7.hidden_ref = bf16[256,1152]{1,0:T(8,128)(2,1)S(1)} custom-call(bf16[64,1536]{1,0:T(8,128)(2,1)S(1)} %get-tuple-element.106.refs_0_, bf16[64,1536]{1,0:T(8,128)(2,1)S(1)} %collective-permute-done.3.refs_1_, bf16[128,1536]{1,0:T(8,128)(2,1)S(1)} %copy-done.5, bf16[1152,6144]{1,0:T(8,128)(2,1)S(1)} %bitcast.4, bf16[1152,6144]{1,0:T(8,128)(2,1)} %refs_4_.7, ...), custom_call_target="tpu_custom_call" | custom-call | flops 1811939328 | bytes 11796480 | tf_op jit(solution)/shard_map/gate_up/pallas_call | solution.py:106
  71.6 1.9 %down.7 = (bf16[128,1536]{1,0:T(8,128)(2,1)S(1)}, bf16[128,1536]{1,0:T(8,128)(2,1)S(1)}) custom-call(bf16[256,1152]{1,0:T(8,128)(2,1)S(1)} %gate_up.7.hidden_ref, bf16[1152,6144]{1,0:T(8,128)(2,1)S(1)} %bitcast.2), custom_call_target="tpu_custom_call" | custom-call | flops 905969664 | bytes 4915200 | tf_op jit(solution)/shard_map/down/pallas_call | solution.py:138
  73.5 0.6 collective-permute-start.35
  74.1 1.9 %down.6 = (bf16[128,1536]{1,0:T(8,128)(2,1)S(1)}, bf16[128,1536]{1,0:T(8,128)(2,1)S(1)}) custom-call(bf16[256,1152]{1,0:T(8,128)(2,1)S(1)} %gate_up.7.hidden_ref, bf16[1152,6144]{1,0:T(8,128)(2,1)S(1)} %bitcast.2), custom_call_target="tpu_custom_call" | custom-call | flops 905969664 | bytes 4915200 | tf_op jit(solution)/shard_map/down/pallas_call | solution.py:138
  76.1 1.9 %down.5 = (bf16[128,1536]{1,0:T(8,128)(2,1)S(1)}, bf16[128,1536]{1,0:T(8,128)(2,1)S(1)}) custom-call(bf16[256,1152]{1,0:T(8,128)(2,1)S(1)} %gate_up.7.hidden_ref, bf16[1152,6144]{1,0:T(8,128)(2,1)S(1)} %bitcast.2), custom_call_target="tpu_custom_call" | custom-call | flops 905969664 | bytes 4915200 | tf_op jit(solution)/shard_map/down/pallas_call | solution.py:138
  78.0 0.6 collective-permute-start.25
  78.5 1.9 %down.4 = (bf16[128,1536]{1,0:T(8,128)(2,1)S(1)}, bf16[128,1536]{1,0:T(8,128)(2,1)S(1)}) custom-call(bf16[256,1152]{1,0:T(8,128)(2,1)S(1)} %gate_up.7.hidden_ref, bf16[1152,6144]{1,0:T(8,128)(2,1)S(1)} %bitcast.2), custom_call_target="tpu_custom_call" | custom-call | flops 905969664 | bytes 4915200 | tf_op jit(solution)/shard_map/down/pallas_call | solution.py:138
  80.6 1.6 %collective-permute-start.36 = (bf16[64,1536]{1,0:T(8,128)(2,1)S(1)}, bf16[64,1536]{1,0:T(8,128)(2,1)S(1)}, u32[]{:S(2)}, u32[]{:S(2)}) collective-permute-start(bf16[64,1536]{1,0:T(8,128)(2,1)S(1)} %slice.115), channel_id=1, source_target_pairs={{0,2},{1,3},{2,0},{3,1},{4,6},{5,7},{6,4},{7,5},{8,10},{9,11},{10,... | collective-permute-start | bytes 589832 | tf_op jit(solution)/shard_map/ppermute | solution.py:198
  82.4 0.6 collective-permute-start.31
  83.0 1.6 %collective-permute-start.26 = (bf16[64,1536]{1,0:T(8,128)(2,1)S(1)}, bf16[64,1536]{1,0:T(8,128)(2,1)S(1)}, u32[]{:S(2)}, u32[]{:S(2)}) collective-permute-start(bf16[64,1536]{1,0:T(8,128)(2,1)S(1)} %slice.103), channel_id=1, source_target_pairs={{0,2},{1,3},{2,0},{3,1},{4,6},{5,7},{6,4},{7,5},{8,10},{9,11},{10,... | collective-permute-start | bytes 589832 | tf_op jit(solution)/shard_map/ppermute | solution.py:198
  84.8 0.6 collective-permute-start.21
  85.3 3.1 %collective-permute-done.36 = bf16[64,1536]{1,0:T(8,128)(2,1)S(1)} collective-permute-done((bf16[64,1536]{1,0:T(8,128)(2,1)S(1)}, bf16[64,1536]{1,0:T(8,128)(2,1)S(1)}, u32[]{:S(2)}, u32[]{:S(2)}) %collective-permute-start.36) | collective-permute-done | bytes 196640 | tf_op jit(solution)/shard_map/ppermute | solution.py:198
  88.5 0.6 collective-permute-start.37
  89.1 1.5 %collective-permute-start.38 = (bf16[16,1536]{1,0:T(8,128)(2,1)S(1)}, bf16[16,1536]{1,0:T(8,128)(2,1)S(1)}, u32[]{:S(2)}, u32[]{:S(2)}) collective-permute-start(bf16[16,1536]{1,0:T(8,128)(2,1)S(1)} %get-tuple-element.66), channel_id=1, source_target_pairs={{0,8},{1,9},{2,10},{3,11},{4,12},{5,13},{6,14},{7,15},{8,0},{9,1},... | collective-permute-start | bytes 147464 | tf_op jit(solution)/shard_map/ppermute | solution.py:193
  90.6 2.1 %collective-permute-done.31 = bf16[64,1536]{1,0:T(8,128)(2,1)S(1)} collective-permute-done((bf16[64,1536]{1,0:T(8,128)(2,1)S(1)}, bf16[64,1536]{1,0:T(8,128)(2,1)S(1)}, u32[]{:S(2)}, u32[]{:S(2)}) %collective-permute-start.31) | collective-permute-done | bytes 196640 | tf_op jit(solution)/shard_map/ppermute | solution.py:198
  92.6 0.6 collective-permute-start.39
  93.3 3.6 %collective-permute-done.26 = bf16[64,1536]{1,0:T(8,128)(2,1)S(1)} collective-permute-done((bf16[64,1536]{1,0:T(8,128)(2,1)S(1)}, bf16[64,1536]{1,0:T(8,128)(2,1)S(1)}, u32[]{:S(2)}, u32[]{:S(2)}) %collective-permute-start.26) | collective-permute-done | bytes 196640 | tf_op jit(solution)/shard_map/ppermute | solution.py:198
  96.8 0.6 collective-permute-start.32
  97.4 3.2 %collective-permute-done.21 = bf16[64,1536]{1,0:T(8,128)(2,1)S(1)} collective-permute-done((bf16[64,1536]{1,0:T(8,128)(2,1)S(1)}, bf16[64,1536]{1,0:T(8,128)(2,1)S(1)}, u32[]{:S(2)}, u32[]{:S(2)}) %collective-permute-start.21) | collective-permute-done | bytes 196640 | tf_op jit(solution)/shard_map/ppermute | solution.py:198
  100.6 1.7 %collective-permute-start.33 = (bf16[16,1536]{1,0:T(8,128)(2,1)S(1)}, bf16[16,1536]{1,0:T(8,128)(2,1)S(1)}, u32[]{:S(2)}, u32[]{:S(2)}) collective-permute-start(bf16[16,1536]{1,0:T(8,128)(2,1)S(1)} %get-tuple-element.70), channel_id=1, source_target_pairs={{0,8},{1,9},{2,10},{3,11},{4,12},{5,13},{6,14},{7,15},{8,0},{9,1},... | collective-permute-start | bytes 147464 | tf_op jit(solution)/shard_map/ppermute | solution.py:193
  102.5 3.8 %collective-permute-start.27 = (bf16[16,1536]{1,0:T(8,128)(2,1)S(1)}, bf16[16,1536]{1,0:T(8,128)(2,1)S(1)}, u32[]{:S(2)}, u32[]{:S(2)}) collective-permute-start(bf16[16,1536]{1,0:T(8,128)(2,1)S(1)} %get-tuple-element.75), channel_id=1, source_target_pairs={{0,12},{1,13},{2,14},{3,15},{4,0},{5,1},{6,2},{7,3},{8,4},{9,5},{1... | collective-permute-start | bytes 147464 | tf_op jit(solution)/shard_map/ppermute | solution.py:193
  106.4 0.5 collective-permute-start.29
  107.2 3.1 %collective-permute-start.22 = (bf16[16,1536]{1,0:T(8,128)(2,1)S(1)}, bf16[16,1536]{1,0:T(8,128)(2,1)S(1)}, u32[]{:S(2)}, u32[]{:S(2)}) collective-permute-start(bf16[16,1536]{1,0:T(8,128)(2,1)S(1)} %get-tuple-element.79), channel_id=1, source_target_pairs={{0,12},{1,13},{2,14},{3,15},{4,0},{5,1},{6,2},{7,3},{8,4},{9,5},{1... | collective-permute-start | bytes 147464 | tf_op jit(solution)/shard_map/ppermute | solution.py:193
  110.3 1.1 collective-permute-start.23
  111.5 1.3 %collective-permute-done.28.refs_6_ = bf16[16,1536]{1,0:T(8,128)(2,1)S(1)} collective-permute-done((bf16[16,1536]{1,0:T(8,128)(2,1)S(1)}, bf16[16,1536]{1,0:T(8,128)(2,1)S(1)}, u32[]{:S(2)}, u32[]{:S(2)}) %collective-permute-start.28) | collective-permute-done | bytes 49184 | tf_op jit(solution)/shard_map/ppermute | solution.py:193
  113.1 2.2 %collective-permute-done.23.refs_2_ = bf16[16,1536]{1,0:T(8,128)(2,1)S(1)} collective-permute-done((bf16[16,1536]{1,0:T(8,128)(2,1)S(1)}, bf16[16,1536]{1,0:T(8,128)(2,1)S(1)}, u32[]{:S(2)}, u32[]{:S(2)}) %collective-permute-start.23) | collective-permute-done | bytes 49184 | tf_op jit(solution)/shard_map/ppermute | solution.py:193
  115.3 2.0 %collective-permute-done.24.refs_3_ = bf16[16,1536]{1,0:T(8,128)(2,1)S(1)} collective-permute-done((bf16[16,1536]{1,0:T(8,128)(2,1)S(1)}, bf16[16,1536]{1,0:T(8,128)(2,1)S(1)}, u32[]{:S(2)}, u32[]{:S(2)}) %collective-permute-start.24) | collective-permute-done | bytes 49184 | tf_op jit(solution)/shard_map/ppermute | solution.py:193
  117.3 1.3 %mix.1 = bf16[24,6144]{1,0:T(8,128)(2,1)} custom-call(s32[24,2]{1,0:T(8,128)S(1)} %copy.13.ids_ref, f32[24,2]{1,0:T(8,128)S(1)} %copy.14.logits_ref, bf16[24,6144]{1,0:T(8,128)(2,1)S(1)} %copy-done.3, bf16[16,1536]{1,0:T(8,128)(2,1)S(1)} %get-tuple-element.80.refs_0_, bf16[16,1536]{1,0:T(8,128)(2,1)S(1)} %collective-permute-done.22.refs_1_, ...), custom_call_target="tpu_custom_call" | custom-call | tf_op jit(solution)/shard_map/mix/pallas_call | solution.py:180
  (100 shorter events, 2.5 us)
Async XLA Ops:
  0.8 1.0 copy-start.2
  1.7 0.7 copy-start.8
  3.1 8.7 %collective-permute-start.15 = (bf16[16,1536]{1,0:T(8,128)(2,1)S(1)}, bf16[16,1536]{1,0:T(8,128)(2,1)S(1)}, u32[]{:S(2)}, u32[]{:S(2)}) collective-permute-start(bf16[16,1536]{1,0:T(8,128)(2,1)S(1)} %get-tuple-element.48), channel_id=1, source_target_pairs={{0,4},{1,5},{2,6},{3,7},{4,8},{5,9},{6,10},{7,11},{8,12},{9,13},{1... | collective-permute-start | bytes 147464 | tf_op jit(solution)/shard_map/ppermute | solution.py:193
  6.1 8.4 %collective-permute-start.16 = (bf16[16,1536]{1,0:T(8,128)(2,1)S(1)}, bf16[16,1536]{1,0:T(8,128)(2,1)S(1)}, u32[]{:S(2)}, u32[]{:S(2)}) collective-permute-start(bf16[16,1536]{1,0:T(8,128)(2,1)S(1)} %get-tuple-element.49), channel_id=1, source_target_pairs={{0,8},{1,9},{2,10},{3,11},{4,12},{5,13},{6,14},{7,15},{8,0},{9,1},... | collective-permute-start | bytes 147464 | tf_op jit(solution)/shard_map/ppermute | solution.py:193
  8.7 6.5 %collective-permute-start.17 = (bf16[16,1536]{1,0:T(8,128)(2,1)S(1)}, bf16[16,1536]{1,0:T(8,128)(2,1)S(1)}, u32[]{:S(2)}, u32[]{:S(2)}) collective-permute-start(bf16[16,1536]{1,0:T(8,128)(2,1)S(1)} %get-tuple-element.50), channel_id=1, source_target_pairs={{0,12},{1,13},{2,14},{3,15},{4,0},{5,1},{6,2},{7,3},{8,4},{9,5},{1... | collective-permute-start | bytes 147464 | tf_op jit(solution)/shard_map/ppermute | solution.py:193
  10.1 6.7 %collective-permute-start.10 = (bf16[16,1536]{1,0:T(8,128)(2,1)S(1)}, bf16[16,1536]{1,0:T(8,128)(2,1)S(1)}, u32[]{:S(2)}, u32[]{:S(2)}) collective-permute-start(bf16[16,1536]{1,0:T(8,128)(2,1)S(1)} %get-tuple-element.44), channel_id=1, source_target_pairs={{0,4},{1,5},{2,6},{3,7},{4,8},{5,9},{6,10},{7,11},{8,12},{9,13},{1... | collective-permute-start | bytes 147464 | tf_op jit(solution)/shard_map/ppermute | solution.py:193
  10.8 9.0 %collective-permute-start.11 = (bf16[16,1536]{1,0:T(8,128)(2,1)S(1)}, bf16[16,1536]{1,0:T(8,128)(2,1)S(1)}, u32[]{:S(2)}, u32[]{:S(2)}) collective-permute-start(bf16[16,1536]{1,0:T(8,128)(2,1)S(1)} %get-tuple-element.45), channel_id=1, source_target_pairs={{0,8},{1,9},{2,10},{3,11},{4,12},{5,13},{6,14},{7,15},{8,0},{9,1},... | collective-permute-start | bytes 147464 | tf_op jit(solution)/shard_map/ppermute | solution.py:193
  11.7 8.1 %collective-permute-start.12 = (bf16[16,1536]{1,0:T(8,128)(2,1)S(1)}, bf16[16,1536]{1,0:T(8,128)(2,1)S(1)}, u32[]{:S(2)}, u32[]{:S(2)}) collective-permute-start(bf16[16,1536]{1,0:T(8,128)(2,1)S(1)} %get-tuple-element.46), channel_id=1, source_target_pairs={{0,12},{1,13},{2,14},{3,15},{4,0},{5,1},{6,2},{7,3},{8,4},{9,5},{1... | collective-permute-start | bytes 147464 | tf_op jit(solution)/shard_map/ppermute | solution.py:193
  14.6 6.7 %collective-permute-start.5 = (bf16[16,1536]{1,0:T(8,128)(2,1)S(1)}, bf16[16,1536]{1,0:T(8,128)(2,1)S(1)}, u32[]{:S(2)}, u32[]{:S(2)}) collective-permute-start(bf16[16,1536]{1,0:T(8,128)(2,1)S(1)} %get-tuple-element.40), channel_id=1, source_target_pairs={{0,4},{1,5},{2,6},{3,7},{4,8},{5,9},{6,10},{7,11},{8,12},{9,13},{1... | collective-permute-start | bytes 147464 | tf_op jit(solution)/shard_map/ppermute | solution.py:193
  15.2 8.6 %collective-permute-start.6 = (bf16[16,1536]{1,0:T(8,128)(2,1)S(1)}, bf16[16,1536]{1,0:T(8,128)(2,1)S(1)}, u32[]{:S(2)}, u32[]{:S(2)}) collective-permute-start(bf16[16,1536]{1,0:T(8,128)(2,1)S(1)} %get-tuple-element.41), channel_id=1, source_target_pairs={{0,8},{1,9},{2,10},{3,11},{4,12},{5,13},{6,14},{7,15},{8,0},{9,1},... | collective-permute-start | bytes 147464 | tf_op jit(solution)/shard_map/ppermute | solution.py:193
  16.8 8.6 %collective-permute-start.7 = (bf16[16,1536]{1,0:T(8,128)(2,1)S(1)}, bf16[16,1536]{1,0:T(8,128)(2,1)S(1)}, u32[]{:S(2)}, u32[]{:S(2)}) collective-permute-start(bf16[16,1536]{1,0:T(8,128)(2,1)S(1)} %get-tuple-element.42), channel_id=1, source_target_pairs={{0,12},{1,13},{2,14},{3,15},{4,0},{5,1},{6,2},{7,3},{8,4},{9,5},{1... | collective-permute-start | bytes 147464 | tf_op jit(solution)/shard_map/ppermute | solution.py:193
  19.7 6.2 %collective-permute-start = (bf16[16,1536]{1,0:T(8,128)(2,1)S(1)}, bf16[16,1536]{1,0:T(8,128)(2,1)S(1)}, u32[]{:S(2)}, u32[]{:S(2)}) collective-permute-start(bf16[16,1536]{1,0:T(8,128)(2,1)S(1)} %get-tuple-element.36), channel_id=1, source_target_pairs={{0,4},{1,5},{2,6},{3,7},{4,8},{5,9},{6,10},{7,11},{8,12},{9,13},{1... | collective-permute-start | bytes 147464 | tf_op jit(solution)/shard_map/ppermute | solution.py:193
  19.8 8.4 %collective-permute-start.1 = (bf16[16,1536]{1,0:T(8,128)(2,1)S(1)}, bf16[16,1536]{1,0:T(8,128)(2,1)S(1)}, u32[]{:S(2)}, u32[]{:S(2)}) collective-permute-start(bf16[16,1536]{1,0:T(8,128)(2,1)S(1)} %get-tuple-element.37), channel_id=1, source_target_pairs={{0,8},{1,9},{2,10},{3,11},{4,12},{5,13},{6,14},{7,15},{8,0},{9,1},... | collective-permute-start | bytes 147464 | tf_op jit(solution)/shard_map/ppermute | solution.py:193
  21.3 7.6 %collective-permute-start.2 = (bf16[16,1536]{1,0:T(8,128)(2,1)S(1)}, bf16[16,1536]{1,0:T(8,128)(2,1)S(1)}, u32[]{:S(2)}, u32[]{:S(2)}) collective-permute-start(bf16[16,1536]{1,0:T(8,128)(2,1)S(1)} %get-tuple-element.38), channel_id=1, source_target_pairs={{0,12},{1,13},{2,14},{3,15},{4,0},{5,1},{6,2},{7,3},{8,4},{9,5},{1... | collective-permute-start | bytes 147464 | tf_op jit(solution)/shard_map/ppermute | solution.py:193
  23.8 7.9 %collective-permute-start.18 = (bf16[64,1536]{1,0:T(8,128)(2,1)S(1)}, bf16[64,1536]{1,0:T(8,128)(2,1)S(1)}, u32[]{:S(2)}, u32[]{:S(2)}) collective-permute-start(bf16[64,1536]{1,0:T(8,128)(2,1)S(1)} %get-tuple-element.82.refs_0_), channel_id=1, source_target_pairs={{0,2},{1,3},{2,0},{3,1},{4,6},{5,7},{6,4},{7,5},{8,10},{9,11},{10,... | collective-permute-start | bytes 589832 | tf_op jit(solution)/shard_map/ppermute | solution.py:198
  25.4 10.4 %collective-permute-start.13 = (bf16[64,1536]{1,0:T(8,128)(2,1)S(1)}, bf16[64,1536]{1,0:T(8,128)(2,1)S(1)}, u32[]{:S(2)}, u32[]{:S(2)}) collective-permute-start(bf16[64,1536]{1,0:T(8,128)(2,1)S(1)} %get-tuple-element.90.refs_0_), channel_id=1, source_target_pairs={{0,2},{1,3},{2,0},{3,1},{4,6},{5,7},{6,4},{7,5},{8,10},{9,11},{10,... | collective-permute-start | bytes 589832 | tf_op jit(solution)/shard_map/ppermute | solution.py:198
  26.0 12.0 %collective-permute-start.8 = (bf16[64,1536]{1,0:T(8,128)(2,1)S(1)}, bf16[64,1536]{1,0:T(8,128)(2,1)S(1)}, u32[]{:S(2)}, u32[]{:S(2)}) collective-permute-start(bf16[64,1536]{1,0:T(8,128)(2,1)S(1)} %get-tuple-element.98.refs_0_), channel_id=1, source_target_pairs={{0,2},{1,3},{2,0},{3,1},{4,6},{5,7},{6,4},{7,5},{8,10},{9,11},{10,... | collective-permute-start | bytes 589832 | tf_op jit(solution)/shard_map/ppermute | solution.py:198
  29.4 10.6 %collective-permute-start.3 = (bf16[64,1536]{1,0:T(8,128)(2,1)S(1)}, bf16[64,1536]{1,0:T(8,128)(2,1)S(1)}, u32[]{:S(2)}, u32[]{:S(2)}) collective-permute-start(bf16[64,1536]{1,0:T(8,128)(2,1)S(1)} %get-tuple-element.106.refs_0_), channel_id=1, source_target_pairs={{0,2},{1,3},{2,0},{3,1},{4,6},{5,7},{6,4},{7,5},{8,10},{9,11},{10,... | collective-permute-start | bytes 589832 | tf_op jit(solution)/shard_map/ppermute | solution.py:198
  31.7 9.0 %collective-permute-start.19 = (bf16[128,1536]{1,0:T(8,128)(2,1)S(1)}, bf16[128,1536]{1,0:T(8,128)(2,1)S(1)}, u32[]{:S(2)}, u32[]{:S(2)}) collective-permute-start(bf16[128,1536]{1,0:T(8,128)(2,1)S(1)} %constant_dynamic-update-slice_fusion.31), channel_id=1, source_target_pairs={{0,1},{1,0},{2,3},{3,2},{4,5},{5,4},{6,7},{7,6},{8,9},{9,8},{10,11... | collective-permute-start | bytes 1179656 | tf_op jit(solution)/shard_map/ppermute | solution.py:198
  35.8 15.5 %collective-permute-start.14 = (bf16[128,1536]{1,0:T(8,128)(2,1)S(1)}, bf16[128,1536]{1,0:T(8,128)(2,1)S(1)}, u32[]{:S(2)}, u32[]{:S(2)}) collective-permute-start(bf16[128,1536]{1,0:T(8,128)(2,1)S(1)} %constant_dynamic-update-slice_fusion.22), channel_id=1, source_target_pairs={{0,1},{1,0},{2,3},{3,2},{4,5},{5,4},{6,7},{7,6},{8,9},{9,8},{10,11... | collective-permute-start | bytes 1179656 | tf_op jit(solution)/shard_map/ppermute | solution.py:198
  38.0 19.4 %collective-permute-start.9 = (bf16[128,1536]{1,0:T(8,128)(2,1)S(1)}, bf16[128,1536]{1,0:T(8,128)(2,1)S(1)}, u32[]{:S(2)}, u32[]{:S(2)}) collective-permute-start(bf16[128,1536]{1,0:T(8,128)(2,1)S(1)} %constant_dynamic-update-slice_fusion.13), channel_id=1, source_target_pairs={{0,1},{1,0},{2,3},{3,2},{4,5},{5,4},{6,7},{7,6},{8,9},{9,8},{10,11... | collective-permute-start | bytes 1179656 | tf_op jit(solution)/shard_map/ppermute | solution.py:198
  40.7 24.2 %collective-permute-start.4 = (bf16[128,1536]{1,0:T(8,128)(2,1)}, bf16[128,1536]{1,0:T(8,128)(2,1)S(1)}, u32[]{:S(2)}, u32[]{:S(2)}) collective-permute-start(bf16[128,1536]{1,0:T(8,128)(2,1)} %constant_dynamic-update-slice_fusion.4), channel_id=1, source_target_pairs={{0,1},{1,0},{2,3},{3,2},{4,5},{5,4},{6,7},{7,6},{8,9},{9,8},{10,11... | collective-permute-start | bytes 1179656 | tf_op jit(solution)/shard_map/ppermute | solution.py:198
  40.8 5.0 %copy-start = (bf16[1152,6144]{1,0:T(8,128)(2,1)S(1)}, bf16[1152,6144]{1,0:T(8,128)(2,1)}, u32[]{:S(2)}) copy-start(bf16[1152,6144]{1,0:T(8,128)(2,1)} %refs_3_.7) | copy-start | bytes 42467332
  45.8 6.1 %copy-start.1 = (bf16[1152,6144]{1,0:T(8,128)(2,1)S(1)}, bf16[1152,6144]{1,0:T(8,128)(2,1)}, u32[]{:S(2)}) copy-start(bf16[1152,6144]{1,0:T(8,128)(2,1)} %refs_3_.7) | copy-start | bytes 42467332
  51.9 13.8 %slice-start.4 = ((s8[14155776]{0:T(1024)(128)(4,1)}), s8[4194304]{0:T(1024)(128)(4,1)S(1)}, s32[]{:S(2)}) async-start(s8[14155776]{0:T(1024)(128)(4,1)} %bitcast.3), calls=%async_computation.4 | async-start | bytes 8388608
  51.9 13.8 %slice-start.5 = ((s8[14155776]{0:T(1024)(128)(4,1)}), s8[4194304]{0:T(1024)(128)(4,1)S(1)}, s32[]{:S(2)}) async-start(s8[14155776]{0:T(1024)(128)(4,1)} %bitcast.3), calls=%async_computation.5 | async-start | bytes 8388608
  57.4 0.8 copy-start.6
  58.1 1.0 copy-start.7
  59.1 6.5 %slice-start.6 = ((s8[14155776]{0:T(1024)(128)(4,1)}), s8[4194304]{0:T(1024)(128)(4,1)S(1)}, s32[]{:S(2)}) async-start(s8[14155776]{0:T(1024)(128)(4,1)} %bitcast.3), calls=%async_computation.6 | async-start | bytes 8388608
  59.1 6.5 %slice-start.7 = ((s8[14155776]{0:T(1024)(128)(4,1)}), s8[1572864]{0:T(1024)(128)(4,1)S(1)}, s32[]{:S(2)}) async-start(s8[14155776]{0:T(1024)(128)(4,1)} %bitcast.3), calls=%async_computation.7 | async-start | bytes 3145728
  59.1 12.5 %slice-start = ((s8[14155776]{0:T(1024)(128)(4,1)}), s8[4194304]{0:T(1024)(128)(4,1)S(1)}, s32[]{:S(2)}) async-start(s8[14155776]{0:T(1024)(128)(4,1)} %bitcast.1), calls=%async_computation | async-start | bytes 8388608
  59.1 12.5 %slice-start.1 = ((s8[14155776]{0:T(1024)(128)(4,1)}), s8[4194304]{0:T(1024)(128)(4,1)S(1)}, s32[]{:S(2)}) async-start(s8[14155776]{0:T(1024)(128)(4,1)} %bitcast.1), calls=%async_computation.1 | async-start | bytes 8388608
  64.9 0.7 copy-start.4
  65.7 1.0 copy-start.5
  66.7 4.9 %slice-start.2 = ((s8[14155776]{0:T(1024)(128)(4,1)}), s8[4194304]{0:T(1024)(128)(4,1)S(1)}, s32[]{:S(2)}) async-start(s8[14155776]{0:T(1024)(128)(4,1)} %bitcast.1), calls=%async_computation.2 | async-start | bytes 8388608
  66.7 4.9 %slice-start.3 = ((s8[14155776]{0:T(1024)(128)(4,1)}), s8[1572864]{0:T(1024)(128)(4,1)S(1)}, s32[]{:S(2)}) async-start(s8[14155776]{0:T(1024)(128)(4,1)} %bitcast.1), calls=%async_computation.3 | async-start | bytes 3145728
  73.5 7.0 %collective-permute-start.35 = (bf16[128,1536]{1,0:T(8,128)(2,1)S(1)}, bf16[128,1536]{1,0:T(8,128)(2,1)S(1)}, u32[]{:S(2)}, u32[]{:S(2)}) collective-permute-start(bf16[128,1536]{1,0:T(8,128)(2,1)S(1)} %get-tuple-element.64), channel_id=1, source_target_pairs={{0,1},{1,0},{2,3},{3,2},{4,5},{5,4},{6,7},{7,6},{8,9},{9,8},{10,11... | collective-permute-start | bytes 1179656 | tf_op jit(solution)/shard_map/ppermute | solution.py:198
  76.0 6.2 %collective-permute-start.30 = (bf16[128,1536]{1,0:T(8,128)(2,1)S(1)}, bf16[128,1536]{1,0:T(8,128)(2,1)S(1)}, u32[]{:S(2)}, u32[]{:S(2)}) collective-permute-start(bf16[128,1536]{1,0:T(8,128)(2,1)S(1)} %get-tuple-element.62), channel_id=1, source_target_pairs={{0,1},{1,0},{2,3},{3,2},{4,5},{5,4},{6,7},{7,6},{8,9},{9,8},{10,11... | collective-permute-start | bytes 1179656 | tf_op jit(solution)/shard_map/ppermute | solution.py:198
  78.0 4.9 %collective-permute-start.25 = (bf16[128,1536]{1,0:T(8,128)(2,1)S(1)}, bf16[128,1536]{1,0:T(8,128)(2,1)S(1)}, u32[]{:S(2)}, u32[]{:S(2)}) collective-permute-start(bf16[128,1536]{1,0:T(8,128)(2,1)S(1)} %get-tuple-element.60), channel_id=1, source_target_pairs={{0,1},{1,0},{2,3},{3,2},{4,5},{5,4},{6,7},{7,6},{8,9},{9,8},{10,11... | collective-permute-start | bytes 1179656 | tf_op jit(solution)/shard_map/ppermute | solution.py:198
  80.4 4.2 %collective-permute-start.20 = (bf16[128,1536]{1,0:T(8,128)(2,1)S(1)}, bf16[128,1536]{1,0:T(8,128)(2,1)S(1)}, u32[]{:S(2)}, u32[]{:S(2)}) collective-permute-start(bf16[128,1536]{1,0:T(8,128)(2,1)S(1)} %get-tuple-element.58), channel_id=1, source_target_pairs={{0,1},{1,0},{2,3},{3,2},{4,5},{5,4},{6,7},{7,6},{8,9},{9,8},{10,11... | collective-permute-start | bytes 1179656 | tf_op jit(solution)/shard_map/ppermute | solution.py:198
  80.6 7.8 %collective-permute-start.36 = (bf16[64,1536]{1,0:T(8,128)(2,1)S(1)}, bf16[64,1536]{1,0:T(8,128)(2,1)S(1)}, u32[]{:S(2)}, u32[]{:S(2)}) collective-permute-start(bf16[64,1536]{1,0:T(8,128)(2,1)S(1)} %slice.115), channel_id=1, source_target_pairs={{0,2},{1,3},{2,0},{3,1},{4,6},{5,7},{6,4},{7,5},{8,10},{9,11},{10,... | collective-permute-start | bytes 589832 | tf_op jit(solution)/shard_map/ppermute | solution.py:198
  82.4 10.3 %collective-permute-start.31 = (bf16[64,1536]{1,0:T(8,128)(2,1)S(1)}, bf16[64,1536]{1,0:T(8,128)(2,1)S(1)}, u32[]{:S(2)}, u32[]{:S(2)}) collective-permute-start(bf16[64,1536]{1,0:T(8,128)(2,1)S(1)} %slice.109), channel_id=1, source_target_pairs={{0,2},{1,3},{2,0},{3,1},{4,6},{5,7},{6,4},{7,5},{8,10},{9,11},{10,... | collective-permute-start | bytes 589832 | tf_op jit(solution)/shard_map/ppermute | solution.py:198
  83.0 13.8 %collective-permute-start.26 = (bf16[64,1536]{1,0:T(8,128)(2,1)S(1)}, bf16[64,1536]{1,0:T(8,128)(2,1)S(1)}, u32[]{:S(2)}, u32[]{:S(2)}) collective-permute-start(bf16[64,1536]{1,0:T(8,128)(2,1)S(1)} %slice.103), channel_id=1, source_target_pairs={{0,2},{1,3},{2,0},{3,1},{4,6},{5,7},{6,4},{7,5},{8,10},{9,11},{10,... | collective-permute-start | bytes 589832 | tf_op jit(solution)/shard_map/ppermute | solution.py:198
  84.8 15.9 %collective-permute-start.21 = (bf16[64,1536]{1,0:T(8,128)(2,1)S(1)}, bf16[64,1536]{1,0:T(8,128)(2,1)S(1)}, u32[]{:S(2)}, u32[]{:S(2)}) collective-permute-start(bf16[64,1536]{1,0:T(8,128)(2,1)S(1)} %slice.97), channel_id=1, source_target_pairs={{0,2},{1,3},{2,0},{3,1},{4,6},{5,7},{6,4},{7,5},{8,10},{9,11},{10,... | collective-permute-start | bytes 589832 | tf_op jit(solution)/shard_map/ppermute | solution.py:198
  88.5 13.9 %collective-permute-start.37 = (bf16[16,1536]{1,0:T(8,128)(2,1)S(1)}, bf16[16,1536]{1,0:T(8,128)(2,1)S(1)}, u32[]{:S(2)}, u32[]{:S(2)}) collective-permute-start(bf16[16,1536]{1,0:T(8,128)(2,1)S(1)} %get-tuple-element.67), channel_id=1, source_target_pairs={{0,12},{1,13},{2,14},{3,15},{4,0},{5,1},{6,2},{7,3},{8,4},{9,5},{1... | collective-permute-start | bytes 147464 | tf_op jit(solution)/shard_map/ppermute | solution.py:193
  89.1 13.4 %collective-permute-start.38 = (bf16[16,1536]{1,0:T(8,128)(2,1)S(1)}, bf16[16,1536]{1,0:T(8,128)(2,1)S(1)}, u32[]{:S(2)}, u32[]{:S(2)}) collective-permute-start(bf16[16,1536]{1,0:T(8,128)(2,1)S(1)} %get-tuple-element.66), channel_id=1, source_target_pairs={{0,8},{1,9},{2,10},{3,11},{4,12},{5,13},{6,14},{7,15},{8,0},{9,1},... | collective-permute-start | bytes 147464 | tf_op jit(solution)/shard_map/ppermute | solution.py:193
  92.6 13.7 %collective-permute-start.39 = (bf16[16,1536]{1,0:T(8,128)(2,1)S(1)}, bf16[16,1536]{1,0:T(8,128)(2,1)S(1)}, u32[]{:S(2)}, u32[]{:S(2)}) collective-permute-start(bf16[16,1536]{1,0:T(8,128)(2,1)S(1)} %get-tuple-element.65), channel_id=1, source_target_pairs={{0,4},{1,5},{2,6},{3,7},{4,8},{5,9},{6,10},{7,11},{8,12},{9,13},{1... | collective-permute-start | bytes 147464 | tf_op jit(solution)/shard_map/ppermute | solution.py:193
  93.2 18.2 %copy-start.9 = (f32[24,2]{0,1:T(2,128)S(1)}, f32[24,2]{0,1:T(2,128)}, u32[]{:S(2)}) copy-start(f32[24,2]{0,1:T(2,128)} %param.9) | copy-start | bytes 580
  93.2 24.0 %copy-start.3 = (bf16[24,6144]{1,0:T(8,128)(2,1)S(1)}, bf16[24,6144]{1,0:T(8,128)(2,1)}, u32[]{:S(2)}) copy-start(bf16[24,6144]{1,0:T(8,128)(2,1)} %act_ref.3) | copy-start | bytes 884740
  96.8 9.6 %collective-permute-start.32 = (bf16[16,1536]{1,0:T(8,128)(2,1)S(1)}, bf16[16,1536]{1,0:T(8,128)(2,1)S(1)}, u32[]{:S(2)}, u32[]{:S(2)}) collective-permute-start(bf16[16,1536]{1,0:T(8,128)(2,1)S(1)} %get-tuple-element.71), channel_id=1, source_target_pairs={{0,12},{1,13},{2,14},{3,15},{4,0},{5,1},{6,2},{7,3},{8,4},{9,5},{1... | collective-permute-start | bytes 147464 | tf_op jit(solution)/shard_map/ppermute | solution.py:193
  100.6 6.5 %collective-permute-start.33 = (bf16[16,1536]{1,0:T(8,128)(2,1)S(1)}, bf16[16,1536]{1,0:T(8,128)(2,1)S(1)}, u32[]{:S(2)}, u32[]{:S(2)}) collective-permute-start(bf16[16,1536]{1,0:T(8,128)(2,1)S(1)} %get-tuple-element.70), channel_id=1, source_target_pairs={{0,8},{1,9},{2,10},{3,11},{4,12},{5,13},{6,14},{7,15},{8,0},{9,1},... | collective-permute-start | bytes 147464 | tf_op jit(solution)/shard_map/ppermute | solution.py:193
  102.4 7.9 %collective-permute-start.34 = (bf16[16,1536]{1,0:T(8,128)(2,1)S(1)}, bf16[16,1536]{1,0:T(8,128)(2,1)S(1)}, u32[]{:S(2)}, u32[]{:S(2)}) collective-permute-start(bf16[16,1536]{1,0:T(8,128)(2,1)S(1)} %get-tuple-element.69), channel_id=1, source_target_pairs={{0,4},{1,5},{2,6},{3,7},{4,8},{5,9},{6,10},{7,11},{8,12},{9,13},{1... | collective-permute-start | bytes 147464 | tf_op jit(solution)/shard_map/ppermute | solution.py:193
  102.5 8.9 %collective-permute-start.27 = (bf16[16,1536]{1,0:T(8,128)(2,1)S(1)}, bf16[16,1536]{1,0:T(8,128)(2,1)S(1)}, u32[]{:S(2)}, u32[]{:S(2)}) collective-permute-start(bf16[16,1536]{1,0:T(8,128)(2,1)S(1)} %get-tuple-element.75), channel_id=1, source_target_pairs={{0,12},{1,13},{2,14},{3,15},{4,0},{5,1},{6,2},{7,3},{8,4},{9,5},{1... | collective-permute-start | bytes 147464 | tf_op jit(solution)/shard_map/ppermute | solution.py:193
  106.3 6.4 %collective-permute-start.28 = (bf16[16,1536]{1,0:T(8,128)(2,1)S(1)}, bf16[16,1536]{1,0:T(8,128)(2,1)S(1)}, u32[]{:S(2)}, u32[]{:S(2)}) collective-permute-start(bf16[16,1536]{1,0:T(8,128)(2,1)S(1)} %get-tuple-element.74), channel_id=1, source_target_pairs={{0,8},{1,9},{2,10},{3,11},{4,12},{5,13},{6,14},{7,15},{8,0},{9,1},... | collective-permute-start | bytes 147464 | tf_op jit(solution)/shard_map/ppermute | solution.py:193
  106.4 6.3 %collective-permute-start.29 = (bf16[16,1536]{1,0:T(8,128)(2,1)S(1)}, bf16[16,1536]{1,0:T(8,128)(2,1)S(1)}, u32[]{:S(2)}, u32[]{:S(2)}) collective-permute-start(bf16[16,1536]{1,0:T(8,128)(2,1)S(1)} %get-tuple-element.73), channel_id=1, source_target_pairs={{0,4},{1,5},{2,6},{3,7},{4,8},{5,9},{6,10},{7,11},{8,12},{9,13},{1... | collective-permute-start | bytes 147464 | tf_op jit(solution)/shard_map/ppermute | solution.py:193
  107.2 5.9 %collective-permute-start.22 = (bf16[16,1536]{1,0:T(8,128)(2,1)S(1)}, bf16[16,1536]{1,0:T(8,128)(2,1)S(1)}, u32[]{:S(2)}, u32[]{:S(2)}) collective-permute-start(bf16[16,1536]{1,0:T(8,128)(2,1)S(1)} %get-tuple-element.79), channel_id=1, source_target_pairs={{0,12},{1,13},{2,14},{3,15},{4,0},{5,1},{6,2},{7,3},{8,4},{9,5},{1... | collective-permute-start | bytes 147464 | tf_op jit(solution)/shard_map/ppermute | solution.py:193
  110.3 5.0 %collective-permute-start.23 = (bf16[16,1536]{1,0:T(8,128)(2,1)S(1)}, bf16[16,1536]{1,0:T(8,128)(2,1)S(1)}, u32[]{:S(2)}, u32[]{:S(2)}) collective-permute-start(bf16[16,1536]{1,0:T(8,128)(2,1)S(1)} %get-tuple-element.78), channel_id=1, source_target_pairs={{0,8},{1,9},{2,10},{3,11},{4,12},{5,13},{6,14},{7,15},{8,0},{9,1},... | collective-permute-start | bytes 147464 | tf_op jit(solution)/shard_map/ppermute | solution.py:193
  111.4 5.9 %collective-permute-start.24 = (bf16[16,1536]{1,0:T(8,128)(2,1)S(1)}, bf16[16,1536]{1,0:T(8,128)(2,1)S(1)}, u32[]{:S(2)}, u32[]{:S(2)}) collective-permute-start(bf16[16,1536]{1,0:T(8,128)(2,1)S(1)} %get-tuple-element.77), channel_id=1, source_target_pairs={{0,4},{1,5},{2,6},{3,7},{4,8},{5,9},{6,10},{7,11},{8,12},{9,13},{1... | collective-permute-start | bytes 147464 | tf_op jit(solution)/shard_map/ppermute | solution.py:193

commit v2 on v0

v2 whole, which is shorter than its diff:
```python
import functools

import jax
import jax.numpy as jnp
from jax import lax
from jax.experimental import pallas as pl
from jax.experimental.pallas import tpu as pltpu
from jax.sharding import PartitionSpec as P

EXPERTS = 4
CAP = 16
BACK = 2
LANES = 128
MIB = 1 << 20


def norm_kernel(ids_ref, logits_ref, act_ref, gain_ref, out_ref):
    tokens, width = act_ref.shape
    values = act_ref[...].astype(jnp.float32)
    mean_sq = jnp.mean(values * values, axis=-1, keepdims=True)
    normed = (values * lax.rsqrt(mean_sq + 1e-06) * gain_ref[...]).astype(jnp.bfloat16)
    out_ref[:, :width] = normed
    ids = ids_ref[...]
    lane = lax.broadcasted_iota(jnp.int32, (tokens, LANES), 1)
    named = ((ids[:, 0:1] == lane) | (ids[:, 1:2] == lane)).astype(jnp.float32)
    square = (tokens, tokens)
    earlier = lax.broadcasted_iota(jnp.int32, square, 0) > lax.broadcasted_iota(
        jnp.int32, square, 1
    )
    rank = jnp.dot(earlier.astype(jnp.float32), named, preferred_element_type=jnp.float32)
    slots = [
        jnp.sum(jnp.where(ids[:, j : j + 1] == lane, rank, 0.0), axis=1, keepdims=True)
        for j in range(2)
    ]
    logits = logits_ref[...]
    lead = logits[:, 0:1] - logits[:, 1:2]
    high = lead.astype(jnp.bfloat16).astype(jnp.float32)
    middle = (lead - high).astype(jnp.bfloat16).astype(jnp.float32)
    low = lead - high - middle
    notes = [ids[:, 0:1].astype(jnp.float32), ids[:, 1:2].astype(jnp.float32)]
    notes += slots + [high, middle, low]
    extra = jnp.zeros((tokens, LANES), jnp.float32)
    for j, note in enumerate(notes):
        extra = jnp.where(lane == j, note, extra)
    out_ref[:, width:] = extra.astype(jnp.bfloat16)


def norm(ids, logits, activations, gain):
    tokens, width = activations.shape
    return pl.pallas_call(
        norm_kernel,
        out_shape=jax.ShapeDtypeStruct((tokens, width + LANES), jnp.bfloat16),
        compiler_params=pltpu.CompilerParams(vmem_limit_bytes=16 * MIB),
        name="norm",
    )(ids, logits, activations, gain.reshape(1, width))


def placement(notes, plane, senders):
    tokens = notes.shape[0]
    notes = notes.astype(jnp.float32)
    here = plane.astype(jnp.float32)
    first, second = notes[:, 0:1] == here, notes[:, 1:2] == here
    slot = jnp.where(first, notes[:, 2:3], jnp.where(second, notes[:, 3:4], float(CAP)))
    shape = (tokens, senders * CAP)
    row = lax.broadcasted_iota(jnp.int32, shape, 0)
    lane = lax.broadcasted_iota(jnp.int32, shape, 1)
    per = tokens // senders
    match = (row // per == lane // CAP) & (slot == (lane % CAP).astype(jnp.float32))
    lead = notes[:, 4:5] + notes[:, 5:6] + notes[:, 6:7]
    weight = jax.nn.sigmoid(jnp.where(first, lead, -lead))
    return match.astype(jnp.float32).astype(jnp.bfloat16), jnp.where(first | second, weight, 0.0)


def gate_up_kernel(group, tok, rows_ref, gate_w, up_w, hidden_ref, held):
    plane = lax.axis_index("expert") // group
    width = gate_w.shape[1]
    senders = 8
    step = 1024

    @pl.when(pl.program_id(0) == 0)
    def _():
        for b in range(rows_ref.shape[0] // (senders * tok)):
            span = pl.ds(b * senders * tok, senders * tok)
            pick, _ = placement(rows_ref[span, width:], plane, senders)
            for c in range(width // step):
                held[pl.ds(b * senders * CAP, senders * CAP), c * step : (c + 1) * step] = (
                    lax.dot_general(
                        pick,
                        rows_ref[span, c * step : (c + 1) * step],
                        (((0,), (0,)), ((), ())),
                        preferred_element_type=jnp.float32,
                    ).astype(jnp.bfloat16)
                )

    dims = (((1,), (1,)), ((), ()))
    gate = lax.dot_general(held[...], gate_w[...], dims, preferred_element_type=jnp.float32)
    upper = lax.dot_general(held[...], up_w[...], dims, preferred_element_type=jnp.float32)
    hidden_ref[...] = (jax.nn.silu(gate) * upper).astype(jnp.bfloat16)


def gate_up(group, tok, rows, w_gate, w_up):
    hidden, width = w_gate.shape
    slots = rows.shape[0] // tok * CAP
    block = 128 if hidden % 128 == 0 else hidden
    weight_spec = pl.BlockSpec((block, width), lambda h: (h, 0))
    return pl.pallas_call(
        functools.partial(gate_up_kernel, group, tok),
        grid=(hidden // block,),
        in_specs=[pl.BlockSpec(rows.shape, lambda h: (0, 0)), weight_spec, weight_spec],
        out_specs=pl.BlockSpec((slots, block), lambda h: (0, h)),
        out_shape=jax.ShapeDtypeStruct((slots, hidden), jnp.bfloat16),
        scratch_shapes=[pltpu.VMEM((slots, width), jnp.bfloat16)],
        compiler_params=pltpu.CompilerParams(
            vmem_limit_bytes=(56 if slots > 256 else 32) * MIB
        ),
        cost_estimate=pl.CostEstimate(
            flops=4 * slots * hidden * width,
            bytes_accessed=4 * hidden * width + 2 * rows.size,
            transcendentals=0,
        ),
        name="gate_up",
    )(rows, w_gate, w_up)


def down_kernel(group, tok, hidden_ref, notes_ref, w_ref, out_ref):
    plane = lax.axis_index("expert") // group
    out = jnp.dot(hidden_ref[...], w_ref[...], preferred_element_type=jnp.float32)
    out = out.astype(jnp.bfloat16)
    senders = 8
    for b in range(notes_ref.shape[0] // (senders * tok)):
        span = pl.ds(b * senders * tok, senders * tok)
        place, weight = placement(notes_ref[span, :], plane, senders)
        rows = jnp.dot(
            place,
            out[b * senders * CAP : (b + 1) * senders * CAP],
            preferred_element_type=jnp.float32,
        )
        out_ref[span, :] = (rows * weight).astype(jnp.bfloat16)


def down(group, tok, k, hidden, rows, w_down):
    slots, depth = hidden.shape
    width = w_down.shape[1]
    part = width // BACK
    tokens = rows.shape[0]
    block = 512
    steps = part // block
    return pl.pallas_call(
        functools.partial(down_kernel, group, tok),
        grid=(steps,),
        in_specs=[
            pl.BlockSpec((slots, depth), lambda c: (0, 0)),
            pl.BlockSpec((tokens, LANES), lambda c: (0, width // LANES)),
            pl.BlockSpec((depth, block), lambda c: (0, k * steps + c)),
        ],
        out_specs=pl.BlockSpec((tokens, block), lambda c: (0, c)),
        out_shape=jax.ShapeDtypeStruct((tokens, part), jnp.bfloat16),
        compiler_params=pltpu.CompilerParams(vmem_limit_bytes=32 * MIB),
        cost_estimate=pl.CostEstimate(
            flops=2 * slots * depth * part,
            bytes_accessed=2 * (depth * part + slots * depth + tokens * part),
            transcendentals=0,
        ),
        name="down",
    )(hidden, rows, w_down)


def on_device(activations, expert_ids, route_logits, norm_gain, w_gate, w_up, w_down):
    group = lax.axis_size("expert") // EXPERTS
    tok = activations.shape[0]
    own = norm(expert_ids, route_logits, activations, norm_gain)
    rows = lax.all_gather(own, "expert", axis=0, tiled=True)
    hidden = gate_up(group, tok, rows, w_gate, w_up)
    summed = [
        lax.psum_scatter(
            down(group, tok, k, hidden, rows, w_down), "expert", scatter_dimension=0, tiled=True
        )
        for k in range(BACK)
    ]
    total = jnp.concatenate(summed, axis=1).astype(jnp.float32)
    return (activations.astype(jnp.float32) + total).astype(jnp.bfloat16)


def solution(mesh):
    in_specs = (
        P(("parts", "expert"), None),
        P(("parts", "expert"), None),
        P(("parts", "expert"), None),
        P(),
        P("expert", None),
        P("expert", None),
        P("expert", None),
    )
    out_specs = P(("parts", "expert"), None)
    return jax.shard_map(
        on_device, mesh=mesh, in_specs=in_specs, out_specs=out_specs, check_vma=False
    )
```

time: 191 us -> 242 us (1.27)
  the two profiles are of different devices: /device:TPU:13 before, /device:TPU:0 now
where the time goes in v2:
time: 242 us; the launch traced here: 241 us
  waiting for transfers between devices  171 us (71%)
  Pallas kernels  31.9 us (13%)
  local copies, waits for them, and re-layouts  23.3 us (10%)
  between operations  13.1 us (5%)
    reduce_scatter x2, waiting for transfers between devices, on_device(): lax.psum_scatter(down(group, tok, k, hidden, rows, w_down), 'expert', sca...  114 us
    all_gather x1, waiting for transfers between devices, on_device(): rows = lax.all_gather(own, 'expert', axis=0, tiled=True)  56.7 us
    unnamed x18, local copies, waits for them, and re-layouts  23.3 us
    pallas_call x1, Pallas kernels, gate_up(): pl.pallas_call(functools.partial(gate_up_kernel, group, tok), grid=(hidde...  19 us
    pallas_call x2, Pallas kernels, down(): pl.pallas_call(functools.partial(down_kernel, group, tok), grid=(steps,),...  11.9 us
  transfers between devices with their start and end apart: 3, of which 3 were waited for; matrix products, arithmetic and copies ran while one was open for 0% of the time, Pallas kernels for 2%

profile of v2, /device:TPU:0, one launch (start us, length us, event | category | flops | bytes accessed | tf_op | source)
XLA Modules:
  0.0 241.1 jit_solution(9223347403248630769)
XLA Ops:
  6.5 0.0 all-gather.2.cloned.1.call-start
  6.5 0.8 copy.8.ids_ref
  7.3 0.8 copy.9.logits_ref
  8.1 0.0 copy-start.5
  8.1 1.0 copy-done.5
  9.0 0.0 copy-start.7
  9.0 0.7 copy-done.7
  9.8 1.0 norm.1
  10.7 0.0 all-gather.2.cloned.1.call-update
  10.8 0.0 reduce-scatter.3.cloned.1.call-start
  10.8 56.7 %all-gather.2.cloned.1.call-done.rows_ref.notes_ref = bf16[384,6272]{1,0:T(8,128)(2,1)} async-done(((bf16[24,6272]{1,0:T(8,128)(2,1)}), bf16[384,6272]{1,0:T(8,128)(2,1)}) %all-gather.2.cloned.1.call-update) | async-done | bytes 4816912 | tf_op jit(solution)/shard_map/all_gather | solution.py:172
  67.6 0.0 copy-start.2
  67.6 2.4 copy-done.2
  69.9 0.0 copy-start.4
  69.9 5.0 %copy-done.4 = bf16[1152,6144]{1,0:T(8,128)(2,1)S(1)} copy-done((bf16[1152,6144]{1,0:T(8,128)(2,1)S(1)}, bf16[1152,6144]{1,0:T(8,128)(2,1)}, u32[]{:S(2)}) %copy-start.4) | copy-done | bytes 14155800
  75.0 19.0 %gate_up.1.hidden_ref = bf16[256,1152]{1,0:T(8,128)(2,1)S(1)} custom-call(bf16[384,6272]{1,0:T(8,128)(2,1)S(1)} %copy-done.2, bf16[1152,6144]{1,0:T(8,128)(2,1)S(1)} %copy-done.4, bf16[1152,6144]{1,0:T(8,128)(2,1)} %up_w.1), custom_call_target="tpu_custom_call" | custom-call | flops 7247757312 | bytes 33128448 | tf_op jit(solution)/shard_map/gate_up/pallas_call | solution.py:106
  94.0 0.0 copy-start
  94.0 5.0 %copy-done = bf16[1152,6144]{1,0:T(8,128)(2,1)S(1)} copy-done((bf16[1152,6144]{1,0:T(8,128)(2,1)S(1)}, bf16[1152,6144]{1,0:T(8,128)(2,1)}, u32[]{:S(2)}) %copy-start) | copy-done | bytes 14155800
  99.0 5.9 %down.2 = bf16[384,3072]{1,0:T(8,128)(2,1)} custom-call(bf16[256,1152]{1,0:T(8,128)(2,1)S(1)} %gate_up.1.hidden_ref, bf16[384,6272]{1,0:T(8,128)(2,1)S(1)} %copy-done.2, bf16[1152,6144]{1,0:T(8,128)(2,1)S(1)} %copy-done), custom_call_target="tpu_custom_call" | custom-call | flops 1811939328 | bytes 10027008 | tf_op jit(solution)/shard_map/down/pallas_call | solution.py:148
  104.9 0.0 copy-start.6
  104.9 0.0 reduce-scatter.3.cloned.1.call-update
  105.0 0.0 reduce-scatter.5.cloned.1.call-start
  105.0 0.0 copy-start.1
  105.0 5.1 %copy-done.1 = bf16[1152,6144]{1,0:T(8,128)(2,1)S(1)} copy-done((bf16[1152,6144]{1,0:T(8,128)(2,1)S(1)}, bf16[1152,6144]{1,0:T(8,128)(2,1)}, u32[]{:S(2)}) %copy-start.1) | copy-done | bytes 14155800
  110.2 0.0 copy-start.3
  110.2 2.5 %copy-done.3 = bf16[384,6272]{1,0:T(8,128)(2,1)S(1)} copy-done((bf16[384,6272]{1,0:T(8,128)(2,1)S(1)}, bf16[384,6272]{1,0:T(8,128)(2,1)}, u32[]{:S(2)}) %copy-start.3) | copy-done | bytes 4816920
  112.7 5.9 %down.3 = bf16[384,3072]{1,0:T(8,128)(2,1)} custom-call(bf16[256,1152]{1,0:T(8,128)(2,1)S(1)} %gate_up.1.hidden_ref, bf16[384,6272]{1,0:T(8,128)(2,1)S(1)} %copy-done.3, bf16[1152,6144]{1,0:T(8,128)(2,1)S(1)} %copy-done.1), custom_call_target="tpu_custom_call" | custom-call | flops 1811939328 | bytes 10027008 | tf_op jit(solution)/shard_map/down/pallas_call | solution.py:148
  118.6 0.0 reduce-scatter.5.cloned.1.call-update
  118.6 47.9 %reduce-scatter.3.cloned.1.call-done = bf16[24,3072]{1,0:T(8,128)(2,1)} async-done(((bf16[384,3072]{1,0:T(8,128)(2,1)}), bf16[24,3072]{1,0:T(8,128)(2,1)}) %reduce-scatter.3.cloned.1.call-update) | async-done | bytes 147472 | tf_op jit(solution)/shard_map/reduce_scatter | solution.py:175
  166.6 66.2 %reduce-scatter.5.cloned.1.call-done = bf16[24,3072]{1,0:T(8,128)(2,1)} async-done(((bf16[384,3072]{1,0:T(8,128)(2,1)}), bf16[24,3072]{1,0:T(8,128)(2,1)}) %reduce-scatter.5.cloned.1.call-update) | async-done | bytes 147472 | tf_op jit(solution)/shard_map/reduce_scatter | solution.py:175
  232.8 0.0 copy-done.6
  232.8 1.8 add_convert_fusion
Async XLA Ops:
  6.5 61.0 %all-gather.2.cloned.1.call-start = ((), (), s32[]{:S(2)}) async-start(), calls=%async_computation.2 | async-start | bytes 5117952 | tf_op jit(solution)/shard_map/all_gather | solution.py:172
  8.1 1.0 copy-start.5
  9.0 0.7 copy-start.7
  10.8 155.8 %reduce-scatter.3.cloned.1.call-start = ((), (), s32[]{:S(2)}) async-start(), calls=%async_computation.3 | async-start | bytes 2506752 | tf_op jit(solution)/shard_map/reduce_scatter | solution.py:175
  67.6 2.4 copy-start.2
  69.9 5.0 %copy-start.4 = (bf16[1152,6144]{1,0:T(8,128)(2,1)S(1)}, bf16[1152,6144]{1,0:T(8,128)(2,1)}, u32[]{:S(2)}) copy-start(bf16[1152,6144]{1,0:T(8,128)(2,1)} %gate_w.1) | copy-start | bytes 42467332
  94.0 5.0 %copy-start = (bf16[1152,6144]{1,0:T(8,128)(2,1)S(1)}, bf16[1152,6144]{1,0:T(8,128)(2,1)}, u32[]{:S(2)}) copy-start(bf16[1152,6144]{1,0:T(8,128)(2,1)} %w_ref.3) | copy-start | bytes 42467332
  104.9 127.9 %copy-start.6 = (bf16[24,6144]{1,0:T(8,128)(2,1)S(1)}, bf16[24,6144]{1,0:T(8,128)(2,1)}, u32[]{:S(2)}) copy-start(bf16[24,6144]{1,0:T(8,128)(2,1)} %act_ref.1) | copy-start | bytes 884740
  105.0 127.9 %reduce-scatter.5.cloned.1.call-start = ((), (), s32[]{:S(2)}) async-start(), calls=%async_computation.4 | async-start | bytes 2506752 | tf_op jit(solution)/shard_map/reduce_scatter | solution.py:175
  105.0 5.2 %copy-start.1 = (bf16[1152,6144]{1,0:T(8,128)(2,1)S(1)}, bf16[1152,6144]{1,0:T(8,128)(2,1)}, u32[]{:S(2)}) copy-start(bf16[1152,6144]{1,0:T(8,128)(2,1)} %w_ref.3) | copy-start | bytes 42467332
  110.2 2.5 %copy-start.3 = (bf16[384,6272]{1,0:T(8,128)(2,1)S(1)}, bf16[384,6272]{1,0:T(8,128)(2,1)}, u32[]{:S(2)}) copy-start(bf16[384,6272]{1,0:T(8,128)(2,1)} %all-gather.2.cloned.1.call-done.rows_ref.notes_ref) | copy-start | bytes 14450692
Sparse Core Ops, SparseCore 0:
  10.9 56.6 all-gather.1
  105.1 61.4 reduce-scatter.2
  170.8 61.9 reduce-scatter.4

commit v3 on v1

v3 whole, which is shorter than its diff:
```python
import functools

import jax
import jax.numpy as jnp
from jax import lax
from jax.experimental import pallas as pl
from jax.experimental.pallas import tpu as pltpu
from jax.sharding import PartitionSpec as P

EXPERTS = 4
CAP = 16
CHUNKS = 2
BLOCK = 512
MIB = 1 << 20
SMALL = pltpu.CompilerParams(vmem_limit_bytes=16 * MIB)
LARGE = pltpu.CompilerParams(vmem_limit_bytes=52 * MIB)


def choices(ids, plane):
    tokens = ids.shape[1]
    line = lax.broadcasted_iota(jnp.int32, (EXPERTS * CAP, tokens), 0)
    expert = lax.rem(line // CAP + plane, EXPERTS)
    slot = (line % CAP).astype(jnp.float32)
    first = ids[0:1, :] == expert
    second = ids[1:2, :] == expert
    named = (first | second).astype(jnp.float32)
    square = (tokens, tokens)
    earlier = lax.broadcasted_iota(jnp.int32, square, 0) < lax.broadcasted_iota(
        jnp.int32, square, 1
    )
    rank = jnp.dot(named, earlier.astype(jnp.float32), preferred_element_type=jnp.float32)
    here = rank == slot
    return first & here, second & here


def pack_kernel(group, ids_ref, act_ref, gain_ref, own_ref, *out_refs):
    plane = lax.axis_index("expert") // group
    values = act_ref[...].astype(jnp.float32)
    mean_sq = jnp.mean(values * values, axis=-1, keepdims=True)
    normed = (values * lax.rsqrt(mean_sq + 1e-06) * gain_ref[...]).astype(jnp.bfloat16)
    first, second = choices(ids_ref[...], plane)
    pick = (first | second).astype(jnp.float32).astype(jnp.bfloat16)
    others = EXPERTS - 1
    width = out_refs[0].shape[1]
    for k in range(CHUNKS):
        columns = slice(k * width, (k + 1) * width)
        rows = jnp.dot(pick, normed[:, columns], preferred_element_type=jnp.float32)
        rows = rows.astype(jnp.bfloat16)
        own_ref[:, columns] = rows[:CAP]
        for s in range(others):
            out_refs[k * others + s][...] = rows[(s + 1) * CAP : (s + 2) * CAP]


def pack(group, ids, activations, gain):
    width = activations.shape[1]
    part = jax.ShapeDtypeStruct((CAP, width // CHUNKS), jnp.bfloat16)
    whole = jax.ShapeDtypeStruct((CAP, width), jnp.bfloat16)
    return pl.pallas_call(
        functools.partial(pack_kernel, group),
        out_shape=[whole] + [part] * (CHUNKS * (EXPERTS - 1)),
        compiler_params=SMALL,
        name="norm_and_pack",
    )(ids, activations, gain.reshape(1, width))


def gate_up_kernel(count, begin, end, *refs):
    pieces, refs = refs[:count], refs[count:]
    gate_w, up_w, refs = refs[0], refs[1], refs[2:]
    if not begin:
        gate_in, up_in, refs = refs[0], refs[1], refs[2:]
    if end:
        hidden_ref, gate_sum, up_sum = refs
    else:
        gate_sum, up_sum = refs
    step = pl.program_id(0)

    @pl.when(step == 0)
    def _():
        if begin:
            gate_sum[...] = jnp.zeros_like(gate_sum)
            up_sum[...] = jnp.zeros_like(up_sum)
        else:
            gate_sum[...] = gate_in[...]
            up_sum[...] = up_in[...]

    rows = jnp.concatenate([p[...] for p in pieces], axis=0).T
    gate_sum[...] += jnp.dot(gate_w[...], rows, preferred_element_type=jnp.float32)
    up_sum[...] += jnp.dot(up_w[...], rows, preferred_element_type=jnp.float32)
    if end:

        @pl.when(step == pl.num_programs(0) - 1)
        def _():
            hidden = (jax.nn.silu(gate_sum[...]) * up_sum[...]).astype(jnp.bfloat16)
            hidden_ref[...] = hidden.T


def gate_up(k, pieces, w_gate, w_up, totals):
    begin, end = k == 0, k == CHUNKS - 1
    hidden, width = w_gate.shape
    part = width // CHUNKS
    steps = part // BLOCK
    rows = sum(p.shape[0] for p in pieces)

    def columns(array):
        offset = k * steps if array.shape[1] == width else 0
        return lambda c: (0, offset + c)

    total = jax.ShapeDtypeStruct((hidden, rows), jnp.float32)
    total_spec = pl.BlockSpec((hidden, rows), lambda c: (0, 0))
    in_specs = [pl.BlockSpec((p.shape[0], BLOCK), columns(p)) for p in pieces]
    in_specs += [pl.BlockSpec((hidden, BLOCK), columns(w_gate))] * 2
    in_specs += [total_spec] * len(totals)
    if end:
        out_shape = [jax.ShapeDtypeStruct((rows, hidden), jnp.bfloat16)]
        out_specs = [pl.BlockSpec((rows, hidden), lambda c: (0, 0))]
        scratch = [pltpu.VMEM((hidden, rows), jnp.float32)] * 2
    else:
        out_shape, out_specs, scratch = [total] * 2, [total_spec] * 2, []
    return pl.pallas_call(
        functools.partial(gate_up_kernel, len(pieces), begin, end),
        grid=(steps,),
        in_specs=in_specs,
        out_specs=out_specs,
        out_shape=out_shape,
        scratch_shapes=scratch,
        compiler_params=LARGE,
        cost_estimate=pl.CostEstimate(
            flops=4 * rows * hidden * part,
            bytes_accessed=4 * hidden * part + 8 * rows * hidden,
            transcendentals=0,
        ),
        name="gate_up",
    )(*pieces, w_gate, w_up, *totals)


def down_kernel(hidden_ref, w_ref, keep_ref, send_ref):
    out = jnp.dot(hidden_ref[...], w_ref[...], preferred_element_type=jnp.float32)
    out = out.astype(jnp.bfloat16)
    half = keep_ref.shape[0]
    keep_ref[...] = out[:half]
    send_ref[...] = out[half:]


def down(k, hidden, w_down):
    rows, depth = hidden.shape
    part = w_down.shape[1] // CHUNKS
    steps = part // BLOCK
    half = pl.BlockSpec((rows // 2, BLOCK), lambda c: (0, c))
    return pl.pallas_call(
        down_kernel,
        grid=(steps,),
        in_specs=[
            pl.BlockSpec((rows, depth), lambda c: (0, 0)),
            pl.BlockSpec((depth, BLOCK), lambda c: (0, k * steps + c)),
        ],
        out_specs=[half, half],
        out_shape=[jax.ShapeDtypeStruct((rows // 2, part), jnp.bfloat16)] * 2,
        compiler_params=LARGE,
        cost_estimate=pl.CostEstimate(
            flops=2 * rows * depth * part,
            bytes_accessed=2 * (depth * part + rows * depth + rows * part),
            transcendentals=0,
        ),
        name="down",
    )(hidden, w_down)


def mix_kernel(group, ids_ref, logits_ref, act_ref, arrived_ref, *refs):
    pieces, out_ref = refs[:-1], refs[-1]
    plane = lax.axis_index("expert") // group
    first, second = choices(ids_ref[...], plane)
    lead = logits_ref[0:1, :] - logits_ref[1:2, :]
    weight = jnp.where(first, jax.nn.sigmoid(lead), 0.0)
    weight = (weight + jnp.where(second, jax.nn.sigmoid(-lead), 0.0)).T
    high = weight.astype(jnp.bfloat16)
    rest = weight - high.astype(jnp.float32)
    middle = rest.astype(jnp.bfloat16)
    low = (rest - middle.astype(jnp.float32)).astype(jnp.bfloat16)
    part = pieces[0].shape[1]
    for k in range(CHUNKS):
        columns = slice(k * part, (k + 1) * part)
        blocks = [p[...] for p in pieces[k * EXPERTS : (k + 1) * EXPERTS]]
        own = blocks[0].astype(jnp.float32) + arrived_ref[:, columns].astype(jnp.float32)
        rows = jnp.concatenate([own.astype(jnp.bfloat16)] + blocks[1:], axis=0)
        total = act_ref[:, columns].astype(jnp.float32)
        for term in (low, middle, high):
            total = total + jnp.dot(term, rows, preferred_element_type=jnp.float32)
        out_ref[:, columns] = total.astype(jnp.bfloat16)


def mix(group, ids, logits, activations, arrived, pieces):
    return pl.pallas_call(
        functools.partial(mix_kernel, group),
        out_shape=jax.ShapeDtypeStruct(activations.shape, jnp.bfloat16),
        compiler_params=SMALL,
        name="mix",
    )(ids, logits, activations, arrived, *pieces)


def on_device(activations, expert_ids, route_logits, norm_gain, w_gate, w_up, w_down):
    devices = lax.axis_size("expert")
    group = devices // EXPERTS
    others = EXPERTS - 1
    width = activations.shape[1]
    part = width // CHUNKS
    far = group // 2

    def shift(x, s):
        return lax.ppermute(
            x, "expert", [(i, (i + s * group) % devices) for i in range(devices)]
        )

    def swap(x, bit):
        return lax.ppermute(x, "expert", [(i, i ^ bit) for i in range(devices)])

    ids = expert_ids.T
    own, *packed = pack(group, ids, activations, norm_gain)
    far_own = swap(own, far)
    totals = []
    gathered = []
    for k in range(CHUNKS):
        sends = packed[k * others : (k + 1) * others]
        if gathered:
            sends, gathered = lax.optimization_barrier((sends, gathered))
        gathered = [shift(sends[s], s + 1) for s in range(others)]
        block = jnp.concatenate(gathered, axis=0)
        pieces = [own, block, far_own, swap(block, far)]
        bit = far // 2
        while bit:
            columns = slice(k * part, (k + 1) * part)
            block = [p[:, columns] if p.shape[1] == width else p for p in pieces]
            pieces.append(swap(jnp.concatenate(block, axis=0), bit))
            bit //= 2
        totals = gate_up(k, pieces, w_gate, w_up, totals)
    hidden = totals[0]
    returned, back_own = [], []
    for k in range(CHUNKS):
        keep, send = down(k, hidden, w_down)
        bit = 1
        while bit < far:
            total = keep.astype(jnp.float32) + swap(send, bit).astype(jnp.float32)
            total = total.astype(jnp.bfloat16)
            keep, send = total[: total.shape[0] // 2], total[total.shape[0] // 2 :]
            bit *= 2
        half = total.shape[0] // 2
        back_own.append(total[half : half + CAP])
        block = total[CAP:half].astype(jnp.float32)
        block = block + swap(total[half + CAP :], far).astype(jnp.float32)
        block = block.astype(jnp.bfloat16)
        returned.append(total[:CAP])
        returned += [shift(block[s * CAP : (s + 1) * CAP], -1 - s) for s in range(others)]
    arrived = swap(jnp.concatenate(back_own, axis=1), far)
    return mix(group, ids, route_logits.T, activations, arrived, returned)


def solution(mesh):
    in_specs = (
        P(("parts", "expert"), None),
        P(("parts", "expert"), None),
        P(("parts", "expert"), None),
        P(),
        P("expert", None),
        P("expert", None),
        P("expert", None),
    )
    out_specs = P(("parts", "expert"), None)
    return jax.shard_map(
        on_device, mesh=mesh, in_specs=in_specs, out_specs=out_specs, check_vma=False
    )
```

time: 119 us -> 105 us (0.88)
  starting transfers between devices: 43.7 us -> 31.7 us
  local copies, waits for them, and re-layouts: 15.1 us -> 3.56 us
  waiting for transfers between devices: 27.7 us -> 32.7 us
  Pallas kernels: 31.1 us -> 36 us
    ppermute x24 -> x12, starting transfers between devices: 33.6 us -> 22.6 us  [shift(): lax.ppermute(x, 'expert', [(i, (i + s * group) % devices) for i in range(...]
    unnamed x52 -> x22, local copies, waits for them, and re-layouts: 14.2 us -> 3.41 us
    ppermute x24 -> x12, waiting for transfers between devices: 5.98 us -> 14.8 us  [shift(): lax.ppermute(x, 'expert', [(i, (i + s * group) % devices) for i in range(...]
    pallas_call x4 -> x2, Pallas kernels: 7.53 us -> 13.8 us  [down(): pl.pallas_call(down_kernel, grid=(steps,), in_specs=[pl.BlockSpec((rows,...]
    ppermute x16 -> x10, waiting for transfers between devices: 21.7 us -> 17.9 us  [swap(): return lax.ppermute(x, 'expert', [(i, i ^ bit) for i in range(devices)])]
    pallas_call x4 -> x2, Pallas kernels: 21.7 us -> 20.2 us  [gate_up(): pl.pallas_call(functools.partial(gate_up_kernel, len(pieces), begin, end)...]
    ppermute x16 -> x10, starting transfers between devices: 10.1 us -> 9.04 us  [swap(): return lax.ppermute(x, 'expert', [(i, i ^ bit) for i in range(devices)])]
  transfers between devices with their start and end apart: 40 -> 22, of which waited for: 13 -> 11; matrix products, arithmetic and copies ran while one was open for 3% -> 1% of each run, Pallas kernels for 19% -> 16%
where the time goes in v3:
time: 105 us
  Pallas kernels  36 us (34%)
  waiting for transfers between devices  32.7 us (31%)
  starting transfers between devices  31.7 us (30%)
  local copies, waits for them, and re-layouts  3.56 us (3%)
    ppermute x12, starting transfers between devices, shift(): lax.ppermute(x, 'expert', [(i, (i + s * group) % devices) for i in range(...  22.6 us
    pallas_call x2, Pallas kernels, gate_up(): pl.pallas_call(functools.partial(gate_up_kernel, len(pieces), begin, end)...  20.2 us
    ppermute x10, waiting for transfers between devices, swap(): return lax.ppermute(x, 'expert', [(i, i ^ bit) for i in range(devices)])  17.9 us
    ppermute x12, waiting for transfers between devices, shift(): lax.ppermute(x, 'expert', [(i, (i + s * group) % devices) for i in range(...  14.8 us
    pallas_call x2, Pallas kernels, down(): pl.pallas_call(down_kernel, grid=(steps,), in_specs=[pl.BlockSpec((rows,...  13.8 us
    ppermute x10, starting transfers between devices, swap(): return lax.ppermute(x, 'expert', [(i, i ^ bit) for i in range(devices)])  9.04 us
    unnamed x22, local copies, waits for them, and re-layouts  3.41 us
  transfers between devices with their start and end apart: 22, of which 11 were waited for; matrix products, arithmetic and copies ran while one was open for 1% of the time, Pallas kernels for 16%

profile of v3, /device:TPU:0, one launch (start us, length us, event | category | flops | bytes accessed | tf_op | source)
XLA Modules:
  0.0 104.7 jit_solution(2888499757485519496)
XLA Ops:
  0.0 1.0 copy-done
  1.0 0.7 copy-done.2
  1.7 0.7 copy-done.3
  2.4 0.5 norm_and_pack.1
  2.9 3.1 %collective-permute-start = (bf16[16,3072]{1,0:T(8,128)(2,1)S(1)}, bf16[16,3072]{1,0:T(8,128)(2,1)S(1)}, u32[]{:S(2)}, u32[]{:S(2)}) collective-permute-start(bf16[16,3072]{1,0:T(8,128)(2,1)S(1)} %get-tuple-element.25), channel_id=1, source_target_pairs={{0,4},{1,5},{2,6},{3,7},{4,8},{5,9},{6,10},{7,11},{8,12},{9,13},{1... | collective-permute-start | bytes 294920 | tf_op jit(solution)/shard_map/ppermute | solution.py:209
  6.0 2.6 %collective-permute-start.1 = (bf16[16,3072]{1,0:T(8,128)(2,1)S(1)}, bf16[16,3072]{1,0:T(8,128)(2,1)S(1)}, u32[]{:S(2)}, u32[]{:S(2)}) collective-permute-start(bf16[16,3072]{1,0:T(8,128)(2,1)S(1)} %get-tuple-element.26), channel_id=1, source_target_pairs={{0,8},{1,9},{2,10},{3,11},{4,12},{5,13},{6,14},{7,15},{8,0},{9,1},... | collective-permute-start | bytes 294920 | tf_op jit(solution)/shard_map/ppermute | solution.py:209
  8.6 1.3 %collective-permute-start.2 = (bf16[16,3072]{1,0:T(8,128)(2,1)S(1)}, bf16[16,3072]{1,0:T(8,128)(2,1)S(1)}, u32[]{:S(2)}, u32[]{:S(2)}) collective-permute-start(bf16[16,3072]{1,0:T(8,128)(2,1)S(1)} %get-tuple-element.27), channel_id=1, source_target_pairs={{0,12},{1,13},{2,14},{3,15},{4,0},{5,1},{6,2},{7,3},{8,4},{9,5},{1... | collective-permute-start | bytes 294920 | tf_op jit(solution)/shard_map/ppermute | solution.py:209
  9.9 1.5 %collective-permute-start.6 = (bf16[16,6144]{1,0:T(8,128)(2,1)S(1)}, bf16[16,6144]{1,0:T(8,128)(2,1)S(1)}, u32[]{:S(2)}, u32[]{:S(2)}) collective-permute-start(bf16[16,6144]{1,0:T(8,128)(2,1)S(1)} %get-tuple-element.21.refs_0_), channel_id=1, source_target_pairs={{0,2},{1,3},{2,0},{3,1},{4,6},{5,7},{6,4},{7,5},{8,10},{9,11},{10,... | collective-permute-start | bytes 589832 | tf_op jit(solution)/shard_map/ppermute | solution.py:214
  11.5 0.2 collective-permute-done
  11.7 3.5 %collective-permute-done.1 = bf16[16,3072]{1,0:T(8,128)(2,1)S(1)} collective-permute-done((bf16[16,3072]{1,0:T(8,128)(2,1)S(1)}, bf16[16,3072]{1,0:T(8,128)(2,1)S(1)}, u32[]{:S(2)}, u32[]{:S(2)}) %collective-permute-start.1) | collective-permute-done | bytes 98336 | tf_op jit(solution)/shard_map/ppermute | solution.py:209
  15.2 0.0 collective-permute-done.2
  15.2 2.5 %collective-permute-start.3 = (bf16[16,3072]{1,0:T(8,128)(2,1)S(1)}, bf16[16,3072]{1,0:T(8,128)(2,1)S(1)}, u32[]{:S(2)}, u32[]{:S(2)}) collective-permute-start(bf16[16,3072]{1,0:T(8,128)(2,1)S(1)} %get-tuple-element.28), channel_id=1, source_target_pairs={{0,4},{1,5},{2,6},{3,7},{4,8},{5,9},{6,10},{7,11},{8,12},{9,13},{1... | collective-permute-start | bytes 294920 | tf_op jit(solution)/shard_map/ppermute | solution.py:209
  17.7 1.6 %collective-permute-start.4 = (bf16[16,3072]{1,0:T(8,128)(2,1)S(1)}, bf16[16,3072]{1,0:T(8,128)(2,1)S(1)}, u32[]{:S(2)}, u32[]{:S(2)}) collective-permute-start(bf16[16,3072]{1,0:T(8,128)(2,1)S(1)} %get-tuple-element.29), channel_id=1, source_target_pairs={{0,8},{1,9},{2,10},{3,11},{4,12},{5,13},{6,14},{7,15},{8,0},{9,1},... | collective-permute-start | bytes 294920 | tf_op jit(solution)/shard_map/ppermute | solution.py:209
  19.4 0.7 collective-permute-start.5
  20.2 1.6 %collective-permute-start.9 = (bf16[48,3072]{1,0:T(8,128)(2,1)S(1)}, bf16[48,3072]{1,0:T(8,128)(2,1)S(1)}, u32[]{:S(2)}, u32[]{:S(2)}) collective-permute-start(bf16[48,3072]{1,0:T(8,128)(2,1)S(1)} %get-tuple-element.52.refs_1_), channel_id=1, source_target_pairs={{0,2},{1,3},{2,0},{3,1},{4,6},{5,7},{6,4},{7,5},{8,10},{9,11},{10,... | collective-permute-start | bytes 884744 | tf_op jit(solution)/shard_map/ppermute | solution.py:214
  21.8 0.9 collective-permute-done.3
  22.7 3.2 %collective-permute-done.4 = bf16[16,3072]{1,0:T(8,128)(2,1)S(1)} collective-permute-done((bf16[16,3072]{1,0:T(8,128)(2,1)S(1)}, bf16[16,3072]{1,0:T(8,128)(2,1)S(1)}, u32[]{:S(2)}, u32[]{:S(2)}) %collective-permute-start.4) | collective-permute-done | bytes 98336 | tf_op jit(solution)/shard_map/ppermute | solution.py:209
  25.9 0.0 collective-permute-done.5
  26.0 1.6 %collective-permute-start.7 = (bf16[48,3072]{1,0:T(8,128)(2,1)S(1)}, bf16[48,3072]{1,0:T(8,128)(2,1)S(1)}, u32[]{:S(2)}, u32[]{:S(2)}) collective-permute-start(bf16[48,3072]{1,0:T(8,128)(2,1)S(1)} %get-tuple-element.58.refs_1_), channel_id=1, source_target_pairs={{0,2},{1,3},{2,0},{3,1},{4,6},{5,7},{6,4},{7,5},{8,10},{9,11},{10,... | collective-permute-start | bytes 884744 | tf_op jit(solution)/shard_map/ppermute | solution.py:214
  27.6 0.0 collective-permute-done.6.refs_2_
  27.6 1.0 collective-permute-done.9.refs_3_
  28.6 0.1 collective-permute-start.10
  28.7 6.2 %collective-permute-done.7.refs_3_ = bf16[48,3072]{1,0:T(8,128)(2,1)S(1)} collective-permute-done((bf16[48,3072]{1,0:T(8,128)(2,1)S(1)}, bf16[48,3072]{1,0:T(8,128)(2,1)S(1)}, u32[]{:S(2)}, u32[]{:S(2)}) %collective-permute-start.7) | collective-permute-done | bytes 294944 | tf_op jit(solution)/shard_map/ppermute | solution.py:214
  34.9 0.1 collective-permute-start.8
  35.0 0.0 collective-permute-done.10.refs_4_
  35.0 10.3 %gate_up.2 = (f32[1152,256]{1,0:T(8,128)}, f32[1152,256]{1,0:T(8,128)}) custom-call(bf16[16,6144]{1,0:T(8,128)(2,1)S(1)} %get-tuple-element.21.refs_0_, bf16[48,3072]{1,0:T(8,128)(2,1)S(1)} %get-tuple-element.52.refs_1_, bf16[16,6144]{1,0:T(8,128)(2,1)S(1)} %collective-permute-done.6.refs_2_, bf16[48,3072]{1,0:T(8,128)(2,1)S(1)} %collective-permute-done.9.refs_3_, ...), custom_call_target="tpu_custom_call" | custom-call | flops 3623878656 | bytes 16515072 | tf_op jit(solution)/shard_map/gate_up/pallas_call | solution.py:119
  45.3 0.0 collective-permute-done.8.refs_4_
  45.3 0.9 copy-done.6
  46.2 10.0 %gate_up.3.hidden_ref = bf16[256,1152]{1,0:T(8,128)(2,1)S(1)} custom-call(bf16[16,6144]{1,0:T(8,128)(2,1)S(1)} %get-tuple-element.21.refs_0_, bf16[48,3072]{1,0:T(8,128)(2,1)S(1)} %get-tuple-element.58.refs_1_, bf16[16,6144]{1,0:T(8,128)(2,1)S(1)} %collective-permute-done.6.refs_2_, bf16[48,3072]{1,0:T(8,128)(2,1)S(1)} %collective-permute-done.7.refs_3_, ...), custom_call_target="tpu_custom_call" | custom-call | flops 3623878656 | bytes 16515072 | tf_op jit(solution)/shard_map/gate_up/pallas_call | solution.py:119
  56.2 6.9 %down.2 = (bf16[128,3072]{1,0:T(8,128)(2,1)S(1)}, bf16[128,3072]{1,0:T(8,128)(2,1)}) custom-call(bf16[256,1152]{1,0:T(8,128)(2,1)S(1)} %gate_up.3.hidden_ref, bf16[1152,6144]{1,0:T(8,128)(2,1)} %w_ref.3), custom_call_target="tpu_custom_call" | custom-call | flops 1811939328 | bytes 9240576 | tf_op jit(solution)/shard_map/down/pallas_call | solution.py:149
  63.1 0.5 collective-permute-start.11
  63.6 6.9 %down.3 = (bf16[128,3072]{1,0:T(8,128)(2,1)S(1)}, bf16[128,3072]{1,0:T(8,128)(2,1)}) custom-call(bf16[256,1152]{1,0:T(8,128)(2,1)S(1)} %gate_up.3.hidden_ref, bf16[1152,6144]{1,0:T(8,128)(2,1)} %w_ref.3), custom_call_target="tpu_custom_call" | custom-call | flops 1811939328 | bytes 9240576 | tf_op jit(solution)/shard_map/down/pallas_call | solution.py:149
  70.5 0.1 collective-permute-start.12
  70.5 0.0 collective-permute-done.11
  70.5 0.2 add_convert_fusion.1
  70.8 2.2 %collective-permute-done.12 = bf16[128,3072]{1,0:T(8,128)(2,1)S(1)} collective-permute-done((bf16[128,3072]{1,0:T(8,128)(2,1)}, bf16[128,3072]{1,0:T(8,128)(2,1)S(1)}, u32[]{:S(2)}, u32[]{:S(2)}) %collective-permute-start.12) | collective-permute-done | bytes 786464 | tf_op jit(solution)/shard_map/ppermute | solution.py:214
  73.0 0.2 add_convert_fusion
  73.2 1.6 %collective-permute-start.18 = (bf16[48,3072]{1,0:T(8,128)(2,1)S(1)}, bf16[48,3072]{1,0:T(8,128)(2,1)S(1)}, u32[]{:S(2)}, u32[]{:S(2)}) collective-permute-start(bf16[48,3072]{1,0:T(8,128)(2,1)S(1)} %slice.84), channel_id=1, source_target_pairs={{0,2},{1,3},{2,0},{3,1},{4,6},{5,7},{6,4},{7,5},{8,10},{9,11},{10,... | collective-permute-start | bytes 884744 | tf_op jit(solution)/shard_map/ppermute | solution.py:214
  74.8 0.5 collective-permute-start.14
  75.3 0.0 copy-start.1
  75.3 0.0 copy-start.4
  75.3 0.0 copy-start.5
  75.3 1.6 %collective-permute-start.13 = (bf16[16,6144]{1,0:T(8,128)(2,1)S(1)}, bf16[16,6144]{1,0:T(8,128)(2,1)S(1)}, u32[]{:S(2)}, u32[]{:S(2)}) collective-permute-start(bf16[16,6144]{1,0:T(8,128)(2,1)S(1)} %pad_maximum_fusion), channel_id=1, source_target_pairs={{0,2},{1,3},{2,0},{3,1},{4,6},{5,7},{6,4},{7,5},{8,10},{9,11},{10,... | collective-permute-start | bytes 589832 | tf_op jit(solution)/shard_map/ppermute | solution.py:214
  76.9 6.2 %collective-permute-done.18 = bf16[48,3072]{1,0:T(8,128)(2,1)S(1)} collective-permute-done((bf16[48,3072]{1,0:T(8,128)(2,1)S(1)}, bf16[48,3072]{1,0:T(8,128)(2,1)S(1)}, u32[]{:S(2)}, u32[]{:S(2)}) %collective-permute-start.18) | collective-permute-done | bytes 294944 | tf_op jit(solution)/shard_map/ppermute | solution.py:214
  83.1 0.1 add_convert_fusion.2
  83.2 3.1 %collective-permute-start.19 = (bf16[16,3072]{1,0:T(8,128)(2,1)S(1)}, bf16[16,3072]{1,0:T(8,128)(2,1)S(1)}, u32[]{:S(2)}, u32[]{:S(2)}) collective-permute-start(bf16[16,3072]{1,0:T(8,128)(2,1)S(1)} %get-tuple-element.43), channel_id=1, source_target_pairs={{0,12},{1,13},{2,14},{3,15},{4,0},{5,1},{6,2},{7,3},{8,4},{9,5},{1... | collective-permute-start | bytes 294920 | tf_op jit(solution)/shard_map/ppermute | solution.py:209
  86.3 1.1 %collective-permute-start.20 = (bf16[16,3072]{1,0:T(8,128)(2,1)S(1)}, bf16[16,3072]{1,0:T(8,128)(2,1)S(1)}, u32[]{:S(2)}, u32[]{:S(2)}) collective-permute-start(bf16[16,3072]{1,0:T(8,128)(2,1)S(1)} %get-tuple-element.42), channel_id=1, source_target_pairs={{0,8},{1,9},{2,10},{3,11},{4,12},{5,13},{6,14},{7,15},{8,0},{9,1},... | collective-permute-start | bytes 294920 | tf_op jit(solution)/shard_map/ppermute | solution.py:209
  87.3 0.0 collective-permute-start.21
  87.3 2.1 %collective-permute-done.14 = bf16[48,3072]{1,0:T(8,128)(2,1)S(1)} collective-permute-done((bf16[48,3072]{1,0:T(8,128)(2,1)S(1)}, bf16[48,3072]{1,0:T(8,128)(2,1)S(1)}, u32[]{:S(2)}, u32[]{:S(2)}) %collective-permute-start.14) | collective-permute-done | bytes 294944 | tf_op jit(solution)/shard_map/ppermute | solution.py:214
  89.4 0.1 add_convert_fusion.3
  89.5 3.1 %collective-permute-start.15 = (bf16[16,3072]{1,0:T(8,128)(2,1)S(1)}, bf16[16,3072]{1,0:T(8,128)(2,1)S(1)}, u32[]{:S(2)}, u32[]{:S(2)}) collective-permute-start(bf16[16,3072]{1,0:T(8,128)(2,1)S(1)} %get-tuple-element.46), channel_id=1, source_target_pairs={{0,12},{1,13},{2,14},{3,15},{4,0},{5,1},{6,2},{7,3},{8,4},{9,5},{1... | collective-permute-start | bytes 294920 | tf_op jit(solution)/shard_map/ppermute | solution.py:209
  92.6 0.3 collective-permute-done.13.arrived_ref
  92.9 1.6 %collective-permute-start.16 = (bf16[16,3072]{1,0:T(8,128)(2,1)S(1)}, bf16[16,3072]{1,0:T(8,128)(2,1)S(1)}, u32[]{:S(2)}, u32[]{:S(2)}) collective-permute-start(bf16[16,3072]{1,0:T(8,128)(2,1)S(1)} %get-tuple-element.45), channel_id=1, source_target_pairs={{0,8},{1,9},{2,10},{3,11},{4,12},{5,13},{6,14},{7,15},{8,0},{9,1},... | collective-permute-start | bytes 294920 | tf_op jit(solution)/shard_map/ppermute | solution.py:209
  94.4 0.0 collective-permute-done.19.refs_5_
  94.4 2.0 %collective-permute-start.17 = (bf16[16,3072]{1,0:T(8,128)(2,1)S(1)}, bf16[16,3072]{1,0:T(8,128)(2,1)S(1)}, u32[]{:S(2)}, u32[]{:S(2)}) collective-permute-start(bf16[16,3072]{1,0:T(8,128)(2,1)S(1)} %get-tuple-element.44), channel_id=1, source_target_pairs={{0,4},{1,5},{2,6},{3,7},{4,8},{5,9},{6,10},{7,11},{8,12},{9,13},{1... | collective-permute-start | bytes 294920 | tf_op jit(solution)/shard_map/ppermute | solution.py:209
  96.4 0.0 collective-permute-done.20.refs_6_
  96.4 0.0 collective-permute-done.21.refs_7_
  96.4 0.0 collective-permute-done.15.refs_1_
  96.4 6.9 %collective-permute-done.16.refs_2_ = bf16[16,3072]{1,0:T(8,128)(2,1)S(1)} collective-permute-done((bf16[16,3072]{1,0:T(8,128)(2,1)S(1)}, bf16[16,3072]{1,0:T(8,128)(2,1)S(1)}, u32[]{:S(2)}, u32[]{:S(2)}) %collective-permute-start.16) | collective-permute-done | bytes 98336 | tf_op jit(solution)/shard_map/ppermute | solution.py:209
  103.3 0.0 collective-permute-done.17.refs_3_
  103.3 0.0 copy-done.1
  103.3 0.0 copy-done.4
  103.3 0.0 copy-done.5
  103.3 1.4 %mix.1 = bf16[24,6144]{1,0:T(8,128)(2,1)} custom-call(s32[2,24]{1,0:T(2,128)S(1)} %bitcast.5, f32[2,24]{1,0:T(2,128)S(1)} %bitcast.6, bf16[24,6144]{1,0:T(8,128)(2,1)S(1)} %copy-done.1, bf16[16,6144]{1,0:T(8,128)(2,1)S(1)} %collective-permute-done.13.arrived_ref, bf16[16,3072]{1,0:T(8,128)(2,1)S(1)} %get-tuple-element.39.refs_0_, ...), custom_call_target="tpu_custom_call" | custom-call | tf_op jit(solution)/shard_map/mix/pallas_call | solution.py:192
  (21 shorter events, 0.3 us)
Async XLA Ops:
  0.0 1.0 copy-start
  1.0 0.7 copy-start.2
  1.7 0.7 copy-start.3
  2.9 8.7 %collective-permute-start = (bf16[16,3072]{1,0:T(8,128)(2,1)S(1)}, bf16[16,3072]{1,0:T(8,128)(2,1)S(1)}, u32[]{:S(2)}, u32[]{:S(2)}) collective-permute-start(bf16[16,3072]{1,0:T(8,128)(2,1)S(1)} %get-tuple-element.25), channel_id=1, source_target_pairs={{0,4},{1,5},{2,6},{3,7},{4,8},{5,9},{6,10},{7,11},{8,12},{9,13},{1... | collective-permute-start | bytes 294920 | tf_op jit(solution)/shard_map/ppermute | solution.py:209
  6.0 9.2 %collective-permute-start.1 = (bf16[16,3072]{1,0:T(8,128)(2,1)S(1)}, bf16[16,3072]{1,0:T(8,128)(2,1)S(1)}, u32[]{:S(2)}, u32[]{:S(2)}) collective-permute-start(bf16[16,3072]{1,0:T(8,128)(2,1)S(1)} %get-tuple-element.26), channel_id=1, source_target_pairs={{0,8},{1,9},{2,10},{3,11},{4,12},{5,13},{6,14},{7,15},{8,0},{9,1},... | collective-permute-start | bytes 294920 | tf_op jit(solution)/shard_map/ppermute | solution.py:209
  8.6 6.6 %collective-permute-start.2 = (bf16[16,3072]{1,0:T(8,128)(2,1)S(1)}, bf16[16,3072]{1,0:T(8,128)(2,1)S(1)}, u32[]{:S(2)}, u32[]{:S(2)}) collective-permute-start(bf16[16,3072]{1,0:T(8,128)(2,1)S(1)} %get-tuple-element.27), channel_id=1, source_target_pairs={{0,12},{1,13},{2,14},{3,15},{4,0},{5,1},{6,2},{7,3},{8,4},{9,5},{1... | collective-permute-start | bytes 294920 | tf_op jit(solution)/shard_map/ppermute | solution.py:209
  9.9 17.7 %collective-permute-start.6 = (bf16[16,6144]{1,0:T(8,128)(2,1)S(1)}, bf16[16,6144]{1,0:T(8,128)(2,1)S(1)}, u32[]{:S(2)}, u32[]{:S(2)}) collective-permute-start(bf16[16,6144]{1,0:T(8,128)(2,1)S(1)} %get-tuple-element.21.refs_0_), channel_id=1, source_target_pairs={{0,2},{1,3},{2,0},{3,1},{4,6},{5,7},{6,4},{7,5},{8,10},{9,11},{10,... | collective-permute-start | bytes 589832 | tf_op jit(solution)/shard_map/ppermute | solution.py:214
  15.2 7.5 %collective-permute-start.3 = (bf16[16,3072]{1,0:T(8,128)(2,1)S(1)}, bf16[16,3072]{1,0:T(8,128)(2,1)S(1)}, u32[]{:S(2)}, u32[]{:S(2)}) collective-permute-start(bf16[16,3072]{1,0:T(8,128)(2,1)S(1)} %get-tuple-element.28), channel_id=1, source_target_pairs={{0,4},{1,5},{2,6},{3,7},{4,8},{5,9},{6,10},{7,11},{8,12},{9,13},{1... | collective-permute-start | bytes 294920 | tf_op jit(solution)/shard_map/ppermute | solution.py:209
  17.7 8.2 %collective-permute-start.4 = (bf16[16,3072]{1,0:T(8,128)(2,1)S(1)}, bf16[16,3072]{1,0:T(8,128)(2,1)S(1)}, u32[]{:S(2)}, u32[]{:S(2)}) collective-permute-start(bf16[16,3072]{1,0:T(8,128)(2,1)S(1)} %get-tuple-element.29), channel_id=1, source_target_pairs={{0,8},{1,9},{2,10},{3,11},{4,12},{5,13},{6,14},{7,15},{8,0},{9,1},... | collective-permute-start | bytes 294920 | tf_op jit(solution)/shard_map/ppermute | solution.py:209
  19.4 6.6 %collective-permute-start.5 = (bf16[16,3072]{1,0:T(8,128)(2,1)S(1)}, bf16[16,3072]{1,0:T(8,128)(2,1)S(1)}, u32[]{:S(2)}, u32[]{:S(2)}) collective-permute-start(bf16[16,3072]{1,0:T(8,128)(2,1)S(1)} %get-tuple-element.30), channel_id=1, source_target_pairs={{0,12},{1,13},{2,14},{3,15},{4,0},{5,1},{6,2},{7,3},{8,4},{9,5},{1... | collective-permute-start | bytes 294920 | tf_op jit(solution)/shard_map/ppermute | solution.py:209
  20.2 8.4 %collective-permute-start.9 = (bf16[48,3072]{1,0:T(8,128)(2,1)S(1)}, bf16[48,3072]{1,0:T(8,128)(2,1)S(1)}, u32[]{:S(2)}, u32[]{:S(2)}) collective-permute-start(bf16[48,3072]{1,0:T(8,128)(2,1)S(1)} %get-tuple-element.52.refs_1_), channel_id=1, source_target_pairs={{0,2},{1,3},{2,0},{3,1},{4,6},{5,7},{6,4},{7,5},{8,10},{9,11},{10,... | collective-permute-start | bytes 884744 | tf_op jit(solution)/shard_map/ppermute | solution.py:214
  26.0 8.9 %collective-permute-start.7 = (bf16[48,3072]{1,0:T(8,128)(2,1)S(1)}, bf16[48,3072]{1,0:T(8,128)(2,1)S(1)}, u32[]{:S(2)}, u32[]{:S(2)}) collective-permute-start(bf16[48,3072]{1,0:T(8,128)(2,1)S(1)} %get-tuple-element.58.refs_1_), channel_id=1, source_target_pairs={{0,2},{1,3},{2,0},{3,1},{4,6},{5,7},{6,4},{7,5},{8,10},{9,11},{10,... | collective-permute-start | bytes 884744 | tf_op jit(solution)/shard_map/ppermute | solution.py:214
  28.6 6.4 %collective-permute-start.10 = (bf16[128,3072]{1,0:T(8,128)(2,1)S(1)}, bf16[128,3072]{1,0:T(8,128)(2,1)S(1)}, u32[]{:S(2)}, u32[]{:S(2)}) collective-permute-start(bf16[128,3072]{1,0:T(8,128)(2,1)S(1)} %constant_dynamic-update-slice_fusion.10), channel_id=1, source_target_pairs={{0,1},{1,0},{2,3},{3,2},{4,5},{5,4},{6,7},{7,6},{8,9},{9,8},{10,11... | collective-permute-start | bytes 2359304 | tf_op jit(solution)/shard_map/ppermute | solution.py:214
  34.9 10.4 %collective-permute-start.8 = (bf16[128,3072]{1,0:T(8,128)(2,1)S(1)}, bf16[128,3072]{1,0:T(8,128)(2,1)S(1)}, u32[]{:S(2)}, u32[]{:S(2)}) collective-permute-start(bf16[128,3072]{1,0:T(8,128)(2,1)S(1)} %constant_dynamic-update-slice_fusion.3), channel_id=1, source_target_pairs={{0,1},{1,0},{2,3},{3,2},{4,5},{5,4},{6,7},{7,6},{8,9},{9,8},{10,11... | collective-permute-start | bytes 2359304 | tf_op jit(solution)/shard_map/ppermute | solution.py:214
  45.3 0.9 copy-start.6
  63.1 7.4 %collective-permute-start.11 = (bf16[128,3072]{1,0:T(8,128)(2,1)}, bf16[128,3072]{1,0:T(8,128)(2,1)S(1)}, u32[]{:S(2)}, u32[]{:S(2)}) collective-permute-start(bf16[128,3072]{1,0:T(8,128)(2,1)} %get-tuple-element.34), channel_id=1, source_target_pairs={{0,1},{1,0},{2,3},{3,2},{4,5},{5,4},{6,7},{7,6},{8,9},{9,8},{10,11... | collective-permute-start | bytes 2359304 | tf_op jit(solution)/shard_map/ppermute | solution.py:214
  70.5 2.5 %collective-permute-start.12 = (bf16[128,3072]{1,0:T(8,128)(2,1)}, bf16[128,3072]{1,0:T(8,128)(2,1)S(1)}, u32[]{:S(2)}, u32[]{:S(2)}) collective-permute-start(bf16[128,3072]{1,0:T(8,128)(2,1)} %get-tuple-element.36), channel_id=1, source_target_pairs={{0,1},{1,0},{2,3},{3,2},{4,5},{5,4},{6,7},{7,6},{8,9},{9,8},{10,11... | collective-permute-start | bytes 2359304 | tf_op jit(solution)/shard_map/ppermute | solution.py:214
  73.2 9.9 %collective-permute-start.18 = (bf16[48,3072]{1,0:T(8,128)(2,1)S(1)}, bf16[48,3072]{1,0:T(8,128)(2,1)S(1)}, u32[]{:S(2)}, u32[]{:S(2)}) collective-permute-start(bf16[48,3072]{1,0:T(8,128)(2,1)S(1)} %slice.84), channel_id=1, source_target_pairs={{0,2},{1,3},{2,0},{3,1},{4,6},{5,7},{6,4},{7,5},{8,10},{9,11},{10,... | collective-permute-start | bytes 884744 | tf_op jit(solution)/shard_map/ppermute | solution.py:214
  74.8 14.6 %collective-permute-start.14 = (bf16[48,3072]{1,0:T(8,128)(2,1)S(1)}, bf16[48,3072]{1,0:T(8,128)(2,1)S(1)}, u32[]{:S(2)}, u32[]{:S(2)}) collective-permute-start(bf16[48,3072]{1,0:T(8,128)(2,1)S(1)} %slice.78), channel_id=1, source_target_pairs={{0,2},{1,3},{2,0},{3,1},{4,6},{5,7},{6,4},{7,5},{8,10},{9,11},{10,... | collective-permute-start | bytes 884744 | tf_op jit(solution)/shard_map/ppermute | solution.py:214
  75.3 28.0 %copy-start.1 = (bf16[24,6144]{1,0:T(8,128)(2,1)S(1)}, bf16[24,6144]{1,0:T(8,128)(2,1)}, u32[]{:S(2)}) copy-start(bf16[24,6144]{1,0:T(8,128)(2,1)} %act_ref.3) | copy-start | bytes 884740
  75.3 28.0 %copy-start.4 = (s32[24,2]{0,1:T(2,128)S(1)}, s32[24,2]{0,1:T(2,128)}, u32[]{:S(2)}) copy-start(s32[24,2]{0,1:T(2,128)} %param.8) | copy-start | bytes 580
  75.3 28.0 %copy-start.5 = (f32[24,2]{0,1:T(2,128)S(1)}, f32[24,2]{0,1:T(2,128)}, u32[]{:S(2)}) copy-start(f32[24,2]{0,1:T(2,128)} %param.9) | copy-start | bytes 580
  75.3 17.5 %collective-permute-start.13 = (bf16[16,6144]{1,0:T(8,128)(2,1)S(1)}, bf16[16,6144]{1,0:T(8,128)(2,1)S(1)}, u32[]{:S(2)}, u32[]{:S(2)}) collective-permute-start(bf16[16,6144]{1,0:T(8,128)(2,1)S(1)} %pad_maximum_fusion), channel_id=1, source_target_pairs={{0,2},{1,3},{2,0},{3,1},{4,6},{5,7},{6,4},{7,5},{8,10},{9,11},{10,... | collective-permute-start | bytes 589832 | tf_op jit(solution)/shard_map/ppermute | solution.py:214
  83.2 11.2 %collective-permute-start.19 = (bf16[16,3072]{1,0:T(8,128)(2,1)S(1)}, bf16[16,3072]{1,0:T(8,128)(2,1)S(1)}, u32[]{:S(2)}, u32[]{:S(2)}) collective-permute-start(bf16[16,3072]{1,0:T(8,128)(2,1)S(1)} %get-tuple-element.43), channel_id=1, source_target_pairs={{0,12},{1,13},{2,14},{3,15},{4,0},{5,1},{6,2},{7,3},{8,4},{9,5},{1... | collective-permute-start | bytes 294920 | tf_op jit(solution)/shard_map/ppermute | solution.py:209
  86.3 10.1 %collective-permute-start.20 = (bf16[16,3072]{1,0:T(8,128)(2,1)S(1)}, bf16[16,3072]{1,0:T(8,128)(2,1)S(1)}, u32[]{:S(2)}, u32[]{:S(2)}) collective-permute-start(bf16[16,3072]{1,0:T(8,128)(2,1)S(1)} %get-tuple-element.42), channel_id=1, source_target_pairs={{0,8},{1,9},{2,10},{3,11},{4,12},{5,13},{6,14},{7,15},{8,0},{9,1},... | collective-permute-start | bytes 294920 | tf_op jit(solution)/shard_map/ppermute | solution.py:209
  87.3 9.1 %collective-permute-start.21 = (bf16[16,3072]{1,0:T(8,128)(2,1)S(1)}, bf16[16,3072]{1,0:T(8,128)(2,1)S(1)}, u32[]{:S(2)}, u32[]{:S(2)}) collective-permute-start(bf16[16,3072]{1,0:T(8,128)(2,1)S(1)} %get-tuple-element.41), channel_id=1, source_target_pairs={{0,4},{1,5},{2,6},{3,7},{4,8},{5,9},{6,10},{7,11},{8,12},{9,13},{1... | collective-permute-start | bytes 294920 | tf_op jit(solution)/shard_map/ppermute | solution.py:209
  89.5 6.9 %collective-permute-start.15 = (bf16[16,3072]{1,0:T(8,128)(2,1)S(1)}, bf16[16,3072]{1,0:T(8,128)(2,1)S(1)}, u32[]{:S(2)}, u32[]{:S(2)}) collective-permute-start(bf16[16,3072]{1,0:T(8,128)(2,1)S(1)} %get-tuple-element.46), channel_id=1, source_target_pairs={{0,12},{1,13},{2,14},{3,15},{4,0},{5,1},{6,2},{7,3},{8,4},{9,5},{1... | collective-permute-start | bytes 294920 | tf_op jit(solution)/shard_map/ppermute | solution.py:209
  92.9 10.4 %collective-permute-start.16 = (bf16[16,3072]{1,0:T(8,128)(2,1)S(1)}, bf16[16,3072]{1,0:T(8,128)(2,1)S(1)}, u32[]{:S(2)}, u32[]{:S(2)}) collective-permute-start(bf16[16,3072]{1,0:T(8,128)(2,1)S(1)} %get-tuple-element.45), channel_id=1, source_target_pairs={{0,8},{1,9},{2,10},{3,11},{4,12},{5,13},{6,14},{7,15},{8,0},{9,1},... | collective-permute-start | bytes 294920 | tf_op jit(solution)/shard_map/ppermute | solution.py:209
  94.4 8.8 %collective-permute-start.17 = (bf16[16,3072]{1,0:T(8,128)(2,1)S(1)}, bf16[16,3072]{1,0:T(8,128)(2,1)S(1)}, u32[]{:S(2)}, u32[]{:S(2)}) collective-permute-start(bf16[16,3072]{1,0:T(8,128)(2,1)S(1)} %get-tuple-element.44), channel_id=1, source_target_pairs={{0,4},{1,5},{2,6},{3,7},{4,8},{5,9},{6,10},{7,11},{8,12},{9,13},{1... | collective-permute-start | bytes 294920 | tf_op jit(solution)/shard_map/ppermute | solution.py:209

commit v4 on v3

--- a/solution.py
+++ b/solution.py
@@ -9,11 +9,17 @@
 
 EXPERTS = 4
 CAP = 16
-CHUNKS = 2
 BLOCK = 512
+FORTH = (7, 5)
+BACK = (5, 7)
 MIB = 1 << 20
 SMALL = pltpu.CompilerParams(vmem_limit_bytes=16 * MIB)
 LARGE = pltpu.CompilerParams(vmem_limit_bytes=52 * MIB)
+
+
+def spans(width, shares):
+    unit = width // sum(shares)
+    return [(sum(shares[:k]) * unit, n * unit) for k, n in enumerate(shares)]
 
 
 def choices(ids, plane):
@@ -41,9 +47,8 @@
     first, second = choices(ids_ref[...], plane)
     pick = (first | second).astype(jnp.float32).astype(jnp.bfloat16)
     others = EXPERTS - 1
-    width = out_refs[0].shape[1]
-    for k in range(CHUNKS):
-        columns = slice(k * width, (k + 1) * width)
+    for k, (at, part) in enumerate(spans(act_ref.shape[1], FORTH)):
+        columns = slice(at, at + part)
         rows = jnp.dot(pick, normed[:, columns], preferred_element_type=jnp.float32)
         rows = rows.astype(jnp.bfloat16)
         own_ref[:, columns] = rows[:CAP]
@@ -53,74 +58,87 @@
 
 def pack(group, ids, activations, gain):
     width = activations.shape[1]
-    part = jax.ShapeDtypeStruct((CAP, width // CHUNKS), jnp.bfloat16)
-    whole = jax.ShapeDtypeStruct((CAP, width), jnp.bfloat16)
+    shapes = [width]
+    for _, part in spans(width, FORTH):
+        shapes += [part] * (EXPERTS - 1)
     return pl.pallas_call(
         functools.partial(pack_kernel, group),
-        out_shape=[whole] + [part] * (CHUNKS * (EXPERTS - 1)),
-        compiler_params=SMALL,
+        out_shape=[jax.ShapeDtypeStruct((CAP, n), jnp.bfloat16) for n in shapes],
+        compiler_params=LARGE,
         name="norm_and_pack",
     )(ids, activations, gain.reshape(1, width))
 
 
-def gate_up_kernel(count, begin, end, *refs):
+def fetches(weights, at, held, sems):
+    return [
+        [
+            pltpu.make_async_copy(
+                w.at[:, at + c * BLOCK : at + (c + 1) * BLOCK], held.at[j, c], sems.at[j, c]
+            )
+            for c in range(held.shape[1])
+        ]
+        for j, w in enumerate(weights)
+    ]
+
+
+def gate_up_kernel(count, at, begin, end, *refs):
     pieces, refs = refs[:count], refs[count:]
-    gate_w, up_w, refs = refs[0], refs[1], refs[2:]
+    weights, refs = refs[:2], refs[2:]
+    held, turned, sems, refs = *refs[-3:], refs[:-3]
     if not begin:
-        gate_in, up_in, refs = refs[0], refs[1], refs[2:]
+        before, refs = refs[:2], refs[2:]
     if end:
-        hidden_ref, gate_sum, up_sum = refs
-    else:
-        gate_sum, up_sum = refs
-    step = pl.program_id(0)
-
-    @pl.when(step == 0)
-    def _():
-        if begin:
-            gate_sum[...] = jnp.zeros_like(gate_sum)
-            up_sum[...] = jnp.zeros_like(up_sum)
-        else:
-            gate_sum[...] = gate_in[...]
-            up_sum[...] = up_in[...]
-
-    rows = jnp.concatenate([p[...] for p in pieces], axis=0).T
-    gate_sum[...] += jnp.dot(gate_w[...], rows, preferred_element_type=jnp.float32)
-    up_sum[...] += jnp.dot(up_w[...], rows, preferred_element_type=jnp.float32)
+        hidden_ref, refs = refs[0], refs[1:]
+    sums = refs
+    steps, _, block = held.shape[1:]
+    for pair in zip(*fetches(weights, at, held, sems)):
+        for copy in pair:
+            copy.start()
+    for j in range(2):
+        sums[j][...] = jnp.zeros_like(sums[j]) if begin else before[j][...]
+    wide = steps * block
+
+    @pl.loop(0, steps)
+    def _(c):
+        parts = []
+        for p in pieces:
+            first = at if p.shape[1] > wide else 0
+            parts.append(p[:, pl.ds(pl.multiple_of(first + c * block, block), block)])
+        turned[c] = jnp.concatenate(parts, axis=0).T
+
+    @pl.loop(0, steps)
+    def _(c):
+        for j in range(2):
+            pltpu.make_async_copy(held.at[j, c], held.at[j, c], sems.at[j, c]).wait()
+        for j in range(2):
+            sums[j][...] += jnp.dot(held[j, c], turned[c], preferred_element_type=jnp.float32)
+
     if end:
-
-        @pl.when(step == pl.num_programs(0) - 1)
-        def _():
-            hidden = (jax.nn.silu(gate_sum[...]) * up_sum[...]).astype(jnp.bfloat16)
-            hidden_ref[...] = hidden.T
-
-
-def gate_up(k, pieces, w_gate, w_up, totals):
-    begin, end = k == 0, k == CHUNKS - 1
+        hidden = (jax.nn.silu(sums[0][...]) * sums[1][...]).astype(jnp.bfloat16)
+        hidden_ref[...] = hidden.T
+
+
+def gate_up(at, part, pieces, w_gate, w_up, totals):
     hidden, width = w_gate.shape
-    part = width // CHUNKS
+    begin, end = at == 0, at + part == width
     steps = part // BLOCK
     rows = sum(p.shape[0] for p in pieces)
-
-    def columns(array):
-        offset = k * steps if array.shape[1] == width else 0
-        return lambda c: (0, offset + c)
-
     total = jax.ShapeDtypeStruct((hidden, rows), jnp.float32)
-    total_spec = pl.BlockSpec((hidden, rows), lambda c: (0, 0))
-    in_specs = [pl.BlockSpec((p.shape[0], BLOCK), columns(p)) for p in pieces]
-    in_specs += [pl.BlockSpec((hidden, BLOCK), columns(w_gate))] * 2
-    in_specs += [total_spec] * len(totals)
+    in_specs = [pl.BlockSpec(memory_space=pltpu.VMEM)] * len(pieces)
+    in_specs += [pl.BlockSpec(memory_space=pl.ANY)] * 2
+    in_specs += [pl.BlockSpec(memory_space=pltpu.VMEM)] * len(totals)
+    out_shape, scratch = [total] * 2, []
     if end:
         out_shape = [jax.ShapeDtypeStruct((rows, hidden), jnp.bfloat16)]
-        out_specs = [pl.BlockSpec((rows, hidden), lambda c: (0, 0))]
         scratch = [pltpu.VMEM((hidden, rows), jnp.float32)] * 2
-    else:
-        out_shape, out_specs, scratch = [total] * 2, [total_spec] * 2, []
-    return pl.pallas_call(
-        functools.partial(gate_up_kernel, len(pieces), begin, end),
-        grid=(steps,),
+    scratch += [
+        pltpu.VMEM((2, steps, hidden, BLOCK), jnp.bfloat16),
+        pltpu.VMEM((steps, BLOCK, rows), jnp.bfloat16),
+        pltpu.SemaphoreType.DMA((2, steps)),
+    ]
+    return pl.pallas_call(
+        functools.partial(gate_up_kernel, len(pieces), at, begin, end),
         in_specs=in_specs,
-        out_specs=out_specs,
         out_shape=out_shape,
         scratch_shapes=scratch,
         compiler_params=LARGE,
@@ -133,28 +151,33 @@
     )(*pieces, w_gate, w_up, *totals)
 
 
-def down_kernel(hidden_ref, w_ref, keep_ref, send_ref):
-    out = jnp.dot(hidden_ref[...], w_ref[...], preferred_element_type=jnp.float32)
-    out = out.astype(jnp.bfloat16)
+def down_kernel(at, hidden_ref, w_ref, keep_ref, send_ref, held, sems):
+    steps, _, block = held.shape[1:]
+    for copy in fetches([w_ref], at, held, sems)[0]:
+        copy.start()
     half = keep_ref.shape[0]
-    keep_ref[...] = out[:half]
-    send_ref[...] = out[half:]
-
-
-def down(k, hidden, w_down):
+
+    @pl.loop(0, steps)
+    def _(c):
+        pltpu.make_async_copy(held.at[0, c], held.at[0, c], sems.at[0, c]).wait()
+        out = jnp.dot(hidden_ref[...], held[0, c], preferred_element_type=jnp.float32)
+        out = out.astype(jnp.bfloat16)
+        columns = pl.ds(pl.multiple_of(c * block, block), block)
+        keep_ref[:, columns] = out[:half]
+        send_ref[:, columns] = out[half:]
+
+
+def down(at, part, hidden, w_down):
     rows, depth = hidden.shape
-    part = w_down.shape[1] // CHUNKS
     steps = part // BLOCK
-    half = pl.BlockSpec((rows // 2, BLOCK), lambda c: (0, c))
-    return pl.pallas_call(
-        down_kernel,
-        grid=(steps,),
-        in_specs=[
-            pl.BlockSpec((rows, depth), lambda c: (0, 0)),
-            pl.BlockSpec((depth, BLOCK), lambda c: (0, k * steps + c)),
+    return pl.pallas_call(
+        functools.partial(down_kernel, at),
+        in_specs=[pl.BlockSpec(memory_space=pltpu.VMEM), pl.BlockSpec(memory_space=pl.ANY)],
+        out_shape=[jax.ShapeDtypeStruct((rows // 2, part), jnp.bfloat16)] * 2,
+        scratch_shapes=[
+            pltpu.VMEM((1, steps, depth, BLOCK), jnp.bfloat16),
+            pltpu.SemaphoreType.DMA((1, steps)),
         ],
-        out_specs=[half, half],
-        out_shape=[jax.ShapeDtypeStruct((rows // 2, part), jnp.bfloat16)] * 2,
         compiler_params=LARGE,
         cost_estimate=pl.CostEstimate(
             flops=2 * rows * depth * part,
@@ -176,9 +199,8 @@
     rest = weight - high.astype(jnp.float32)
     middle = rest.astype(jnp.bfloat16)
     low = (rest - middle.astype(jnp.float32)).astype(jnp.bfloat16)
-    part = pieces[0].shape[1]
-    for k in range(CHUNKS):
-        columns = slice(k * part, (k + 1) * part)
+    for k, (at, part) in enumerate(spans(act_ref.shape[1], BACK)):
+        columns = slice(at, at + part)
         blocks = [p[...] for p in pieces[k * EXPERTS : (k + 1) * EXPERTS]]
         own = blocks[0].astype(jnp.float32) + arrived_ref[:, columns].astype(jnp.float32)
         rows = jnp.concatenate([own.astype(jnp.bfloat16)] + blocks[1:], axis=0)
@@ -202,7 +224,6 @@
     group = devices // EXPERTS
     others = EXPERTS - 1
     width = activations.shape[1]
-    part = width // CHUNKS
     far = group // 2
 
     def shift(x, s):
@@ -217,25 +238,23 @@
     own, *packed = pack(group, ids, activations, norm_gain)
     far_own = swap(own, far)
     totals = []
-    gathered = []
-    for k in range(CHUNKS):
+    for k, (at, part) in enumerate(spans(width, FORTH)):
         sends = packed[k * others : (k + 1) * others]
-        if gathered:
-            sends, gathered = lax.optimization_barrier((sends, gathered))
-        gathered = [shift(sends[s], s + 1) for s in range(others)]
-        block = jnp.concatenate(gathered, axis=0)
+        block = jnp.concatenate([shift(sends[s], s + 1) for s in range(others)], axis=0)
         pieces = [own, block, far_own, swap(block, far)]
         bit = far // 2
         while bit:
-            columns = slice(k * part, (k + 1) * part)
-            block = [p[:, columns] if p.shape[1] == width else p for p in pieces]
-            pieces.append(swap(jnp.concatenate(block, axis=0), bit))
+            block = [p[:, at : at + part] if p.shape[1] == width else p for p in pieces]
+            block = jnp.concatenate(block, axis=0)
+            if totals:
+                block, totals = lax.optimization_barrier((block, totals))
+            pieces.append(swap(block, bit))
             bit //= 2
-        totals = gate_up(k, pieces, w_gate, w_up, totals)
+        totals = gate_up(at, part, pieces, w_gate, w_up, totals)
     hidden = totals[0]
     returned, back_own = [], []
-    for k in range(CHUNKS):
-        keep, send = down(k, hidden, w_down)
+    for at, part in spans(width, BACK):
+        keep, send = down(at, part, hidden, w_down)
         bit = 1
         while bit < far:
             total = keep.astype(jnp.float32) + swap(send, bit).astype(jnp.float32)

time: 105 us -> 109 us (1.038)
  waiting for transfers between devices: 32.7 us -> 48.3 us
  Pallas kernels: 36 us -> 27.9 us
  starting transfers between devices: 31.7 us -> 27.9 us
    ppermute x10, waiting for transfers between devices: 17.9 us -> 29 us  [swap(): return lax.ppermute(x, 'expert', [(i, i ^ bit) for i in range(devices)])]
    pallas_call x5, Pallas kernels: 34.6 us -> 26.5 us  [the longest x2 16.3 us: gate_up(): pl.pallas_call(functools.partial(gate_up_kernel, len(pieces), at, begin,...]
    ppermute x12, waiting for transfers between devices: 14.8 us -> 19.3 us  [shift(): lax.ppermute(x, 'expert', [(i, (i + s * group) % devices) for i in range(...]
    ppermute x12, starting transfers between devices: 22.6 us -> 19.6 us  [shift(): lax.ppermute(x, 'expert', [(i, (i + s * group) % devices) for i in range(...]
    unnamed x22 -> x24, local copies, waits for them, and re-layouts: 3.41 us -> 3.35 us
  transfers between devices with their start and end apart: 22 -> 22, of which waited for: 11 -> 9; matrix products, arithmetic and copies ran while one was open for 1% -> 1% of each run, Pallas kernels for 16% -> 5%
where the time goes in v4:
time: 109 us; the launch traced here: 108 us
  waiting for transfers between devices  48.3 us (44%)
  Pallas kernels  27.9 us (26%)
  starting transfers between devices  27.9 us (26%)
  local copies, waits for them, and re-layouts  3.5 us (3%)
    ppermute x10, waiting for transfers between devices, swap(): return lax.ppermute(x, 'expert', [(i, i ^ bit) for i in range(devices)])  29 us
    ppermute x12, starting transfers between devices, shift(): lax.ppermute(x, 'expert', [(i, (i + s * group) % devices) for i in range(...  19.6 us
    ppermute x12, waiting for transfers between devices, shift(): lax.ppermute(x, 'expert', [(i, (i + s * group) % devices) for i in range(...  19.3 us
    pallas_call x2, Pallas kernels, gate_up(): pl.pallas_call(functools.partial(gate_up_kernel, len(pieces), at, begin,...  16.3 us
    pallas_call x2, Pallas kernels, down(): pl.pallas_call(functools.partial(down_kernel, at), in_specs=[pl.BlockSpec...  9.65 us
    ppermute x10, starting transfers between devices, swap(): return lax.ppermute(x, 'expert', [(i, i ^ bit) for i in range(devices)])  8.35 us
    unnamed x24, local copies, waits for them, and re-layouts  3.35 us
  transfers between devices with their start and end apart: 22, of which 9 were waited for; matrix products, arithmetic and copies ran while one was open for 1% of the time, Pallas kernels for 5%

profile of v4, /device:TPU:0, one launch (start us, length us, event | category | flops | bytes accessed | tf_op | source)
XLA Modules:
  0.0 108.4 jit_solution(8082845984626226065)
XLA Ops:
  0.0 1.0 copy-done
  1.0 0.7 copy-done.2
  1.7 0.7 copy-done.3
  2.4 0.5 norm_and_pack.1
  2.9 3.1 %collective-permute-start.5 = (bf16[16,3584]{1,0:T(8,128)(2,1)S(1)}, bf16[16,3584]{1,0:T(8,128)(2,1)S(1)}, u32[]{:S(2)}, u32[]{:S(2)}) collective-permute-start(bf16[16,3584]{1,0:T(8,128)(2,1)S(1)} %get-tuple-element.25), channel_id=1, source_target_pairs={{0,4},{1,5},{2,6},{3,7},{4,8},{5,9},{6,10},{7,11},{8,12},{9,13},{1... | collective-permute-start | bytes 344072 | tf_op jit(solution)/shard_map/ppermute | solution.py:230
  6.0 2.6 %collective-permute-start.6 = (bf16[16,3584]{1,0:T(8,128)(2,1)S(1)}, bf16[16,3584]{1,0:T(8,128)(2,1)S(1)}, u32[]{:S(2)}, u32[]{:S(2)}) collective-permute-start(bf16[16,3584]{1,0:T(8,128)(2,1)S(1)} %get-tuple-element.26), channel_id=1, source_target_pairs={{0,8},{1,9},{2,10},{3,11},{4,12},{5,13},{6,14},{7,15},{8,0},{9,1},... | collective-permute-start | bytes 344072 | tf_op jit(solution)/shard_map/ppermute | solution.py:230
  8.6 1.3 %collective-permute-start.7 = (bf16[16,3584]{1,0:T(8,128)(2,1)S(1)}, bf16[16,3584]{1,0:T(8,128)(2,1)S(1)}, u32[]{:S(2)}, u32[]{:S(2)}) collective-permute-start(bf16[16,3584]{1,0:T(8,128)(2,1)S(1)} %get-tuple-element.27), channel_id=1, source_target_pairs={{0,12},{1,13},{2,14},{3,15},{4,0},{5,1},{6,2},{7,3},{8,4},{9,5},{1... | collective-permute-start | bytes 344072 | tf_op jit(solution)/shard_map/ppermute | solution.py:230
  9.9 1.5 %collective-permute-start.3 = (bf16[16,6144]{1,0:T(8,128)(2,1)S(1)}, bf16[16,6144]{1,0:T(8,128)(2,1)S(1)}, u32[]{:S(2)}, u32[]{:S(2)}) collective-permute-start(bf16[16,6144]{1,0:T(8,128)(2,1)S(1)} %get-tuple-element.21.refs_0_), channel_id=1, source_target_pairs={{0,2},{1,3},{2,0},{3,1},{4,6},{5,7},{6,4},{7,5},{8,10},{9,11},{10,... | collective-permute-start | bytes 589832 | tf_op jit(solution)/shard_map/ppermute | solution.py:235
  11.4 0.7 collective-permute-start
  12.1 5.8 %collective-permute-done = bf16[16,2560]{1,0:T(8,128)(2,1)S(1)} collective-permute-done((bf16[16,2560]{1,0:T(8,128)(2,1)S(1)}, bf16[16,2560]{1,0:T(8,128)(2,1)S(1)}, u32[]{:S(2)}, u32[]{:S(2)}) %collective-permute-start) | collective-permute-done | bytes 81952 | tf_op jit(solution)/shard_map/ppermute | solution.py:230
  18.0 3.6 %collective-permute-start.1 = (bf16[16,2560]{1,0:T(8,128)(2,1)S(1)}, bf16[16,2560]{1,0:T(8,128)(2,1)S(1)}, u32[]{:S(2)}, u32[]{:S(2)}) collective-permute-start(bf16[16,2560]{1,0:T(8,128)(2,1)S(1)} %get-tuple-element.23), channel_id=1, source_target_pairs={{0,8},{1,9},{2,10},{3,11},{4,12},{5,13},{6,14},{7,15},{8,0},{9,1},... | collective-permute-start | bytes 245768 | tf_op jit(solution)/shard_map/ppermute | solution.py:230
  21.6 3.3 %collective-permute-done.1 = bf16[16,2560]{1,0:T(8,128)(2,1)S(1)} collective-permute-done((bf16[16,2560]{1,0:T(8,128)(2,1)S(1)}, bf16[16,2560]{1,0:T(8,128)(2,1)S(1)}, u32[]{:S(2)}, u32[]{:S(2)}) %collective-permute-start.1) | collective-permute-done | bytes 81952 | tf_op jit(solution)/shard_map/ppermute | solution.py:230
  24.9 0.4 collective-permute-start.2
  25.3 4.0 %collective-permute-done.2 = bf16[16,2560]{1,0:T(8,128)(2,1)S(1)} collective-permute-done((bf16[16,2560]{1,0:T(8,128)(2,1)S(1)}, bf16[16,2560]{1,0:T(8,128)(2,1)S(1)}, u32[]{:S(2)}, u32[]{:S(2)}) %collective-permute-start.2) | collective-permute-done | bytes 81952 | tf_op jit(solution)/shard_map/ppermute | solution.py:230
  29.3 1.6 %collective-permute-start.4 = (bf16[48,2560]{1,0:T(8,128)(2,1)S(1)}, bf16[48,2560]{1,0:T(8,128)(2,1)S(1)}, u32[]{:S(2)}, u32[]{:S(2)}) collective-permute-start(bf16[48,2560]{1,0:T(8,128)(2,1)S(1)} %get-tuple-element.54.refs_1_), channel_id=1, source_target_pairs={{0,2},{1,3},{2,0},{3,1},{4,6},{5,7},{6,4},{7,5},{8,10},{9,11},{10,... | collective-permute-start | bytes 737288 | tf_op jit(solution)/shard_map/ppermute | solution.py:235
  30.9 0.0 collective-permute-done.5
  31.0 0.0 collective-permute-done.6
  31.0 0.0 collective-permute-done.7
  31.0 0.6 collective-permute-start.8
  31.6 0.0 collective-permute-done.3.refs_2_
  31.6 9.3 %collective-permute-done.8.refs_3_ = bf16[48,3584]{1,0:T(8,128)(2,1)S(1)} collective-permute-done((bf16[48,3584]{1,0:T(8,128)(2,1)S(1)}, bf16[48,3584]{1,0:T(8,128)(2,1)S(1)}, u32[]{:S(2)}, u32[]{:S(2)}) %collective-permute-start.8) | collective-permute-done | bytes 344096 | tf_op jit(solution)/shard_map/ppermute | solution.py:235
  40.9 0.1 collective-permute-start.9
  41.0 0.0 collective-permute-done.4.refs_3_
  41.1 2.4 %collective-permute-done.9.refs_4_ = bf16[128,3584]{1,0:T(8,128)(2,1)S(1)} collective-permute-done((bf16[128,3584]{1,0:T(8,128)(2,1)S(1)}, bf16[128,3584]{1,0:T(8,128)(2,1)S(1)}, u32[]{:S(2)}, u32[]{:S(2)}) %collective-permute-start.9) | collective-permute-done | bytes 917536 | tf_op jit(solution)/shard_map/ppermute | solution.py:235
  43.5 8.6 %gate_up.2 = (f32[1152,256]{1,0:T(8,128)}, f32[1152,256]{1,0:T(8,128)}) custom-call(bf16[16,6144]{1,0:T(8,128)(2,1)S(1)} %get-tuple-element.21.refs_0_, bf16[48,3584]{1,0:T(8,128)(2,1)S(1)} %get-tuple-element.48.refs_1_, bf16[16,6144]{1,0:T(8,128)(2,1)S(1)} %collective-permute-done.3.refs_2_, bf16[48,3584]{1,0:T(8,128)(2,1)S(1)} %collective-permute-done.8.refs_3_, ...), custom_call_target="tpu_custom_call" | custom-call | flops 4227858432 | bytes 18874368 | tf_op jit(solution)/shard_map/gate_up/pallas_call | solution.py:139
  52.1 0.2 collective-permute-start.10
  52.3 2.0 %collective-permute-done.10.refs_4_ = bf16[128,2560]{1,0:T(8,128)(2,1)S(1)} collective-permute-done((bf16[128,2560]{1,0:T(8,128)(2,1)S(1)}, bf16[128,2560]{1,0:T(8,128)(2,1)S(1)}, u32[]{:S(2)}, u32[]{:S(2)}) %collective-permute-start.10) | collective-permute-done | bytes 655392 | tf_op jit(solution)/shard_map/ppermute | solution.py:235
  54.3 0.8 copy-done.6
  55.1 7.7 %gate_up.3.hidden_ref = bf16[256,1152]{1,0:T(8,128)(2,1)S(1)} custom-call(bf16[16,6144]{1,0:T(8,128)(2,1)S(1)} %get-tuple-element.21.refs_0_, bf16[48,2560]{1,0:T(8,128)(2,1)S(1)} %get-tuple-element.54.refs_1_, bf16[16,6144]{1,0:T(8,128)(2,1)S(1)} %collective-permute-done.3.refs_2_, bf16[48,2560]{1,0:T(8,128)(2,1)S(1)} %collective-permute-done.4.refs_3_, ...), custom_call_target="tpu_custom_call" | custom-call | flops 3019898880 | bytes 14155776 | tf_op jit(solution)/shard_map/gate_up/pallas_call | solution.py:139
  62.8 3.8 %down.2 = (bf16[128,2560]{1,0:T(8,128)(2,1)S(1)}, bf16[128,2560]{1,0:T(8,128)(2,1)S(1)}) custom-call(bf16[256,1152]{1,0:T(8,128)(2,1)S(1)} %gate_up.3.hidden_ref, bf16[1152,6144]{1,0:T(8,128)(2,1)} %w_ref.3), custom_call_target="tpu_custom_call" | custom-call | flops 1509949440 | bytes 7798784 | tf_op jit(solution)/shard_map/down/pallas_call | solution.py:173
  66.6 0.2 collective-permute-start.11
  66.8 5.8 %down.3 = (bf16[128,3584]{1,0:T(8,128)(2,1)S(1)}, bf16[128,3584]{1,0:T(8,128)(2,1)}) custom-call(bf16[256,1152]{1,0:T(8,128)(2,1)S(1)} %gate_up.3.hidden_ref, bf16[1152,6144]{1,0:T(8,128)(2,1)} %w_ref.3), custom_call_target="tpu_custom_call" | custom-call | flops 2113929216 | bytes 10682368 | tf_op jit(solution)/shard_map/down/pallas_call | solution.py:173
  72.7 0.4 collective-permute-start.12
  73.1 0.0 collective-permute-done.11
  73.1 0.2 add_convert_fusion.1
  73.3 1.6 %collective-permute-start.14 = (bf16[48,2560]{1,0:T(8,128)(2,1)S(1)}, bf16[48,2560]{1,0:T(8,128)(2,1)S(1)}, u32[]{:S(2)}, u32[]{:S(2)}) collective-permute-start(bf16[48,2560]{1,0:T(8,128)(2,1)S(1)} %slice.78), channel_id=1, source_target_pairs={{0,2},{1,3},{2,0},{3,1},{4,6},{5,7},{6,4},{7,5},{8,10},{9,11},{10,... | collective-permute-start | bytes 737288 | tf_op jit(solution)/shard_map/ppermute | solution.py:235
  74.9 6.5 %collective-permute-done.14 = bf16[48,2560]{1,0:T(8,128)(2,1)S(1)} collective-permute-done((bf16[48,2560]{1,0:T(8,128)(2,1)S(1)}, bf16[48,2560]{1,0:T(8,128)(2,1)S(1)}, u32[]{:S(2)}, u32[]{:S(2)}) %collective-permute-start.14) | collective-permute-done | bytes 245792 | tf_op jit(solution)/shard_map/ppermute | solution.py:235
  81.3 0.1 add_convert_fusion.3
  81.4 3.0 %collective-permute-start.15 = (bf16[16,2560]{1,0:T(8,128)(2,1)S(1)}, bf16[16,2560]{1,0:T(8,128)(2,1)S(1)}, u32[]{:S(2)}, u32[]{:S(2)}) collective-permute-start(bf16[16,2560]{1,0:T(8,128)(2,1)S(1)} %get-tuple-element.46), channel_id=1, source_target_pairs={{0,12},{1,13},{2,14},{3,15},{4,0},{5,1},{6,2},{7,3},{8,4},{9,5},{1... | collective-permute-start | bytes 245768 | tf_op jit(solution)/shard_map/ppermute | solution.py:230
  84.4 0.0 collective-permute-start.16
  84.4 0.0 collective-permute-done.12
  84.4 0.2 add_convert_fusion
  84.7 0.0 copy-start.1
  84.7 0.0 copy-start.4
  84.7 0.0 copy-start.5
  84.7 1.6 %collective-permute-start.18 = (bf16[48,3584]{1,0:T(8,128)(2,1)S(1)}, bf16[48,3584]{1,0:T(8,128)(2,1)S(1)}, u32[]{:S(2)}, u32[]{:S(2)}) collective-permute-start(bf16[48,3584]{1,0:T(8,128)(2,1)S(1)} %slice.84), channel_id=1, source_target_pairs={{0,2},{1,3},{2,0},{3,1},{4,6},{5,7},{6,4},{7,5},{8,10},{9,11},{10,... | collective-permute-start | bytes 1032200 | tf_op jit(solution)/shard_map/ppermute | solution.py:235
  86.3 0.6 collective-permute-start.13
  86.9 8.9 %collective-permute-done.18 = bf16[48,3584]{1,0:T(8,128)(2,1)S(1)} collective-permute-done((bf16[48,3584]{1,0:T(8,128)(2,1)S(1)}, bf16[48,3584]{1,0:T(8,128)(2,1)S(1)}, u32[]{:S(2)}, u32[]{:S(2)}) %collective-permute-start.18) | collective-permute-done | bytes 344096 | tf_op jit(solution)/shard_map/ppermute | solution.py:235
  95.8 0.1 add_convert_fusion.2
  95.9 1.3 %collective-permute-start.19 = (bf16[16,3584]{1,0:T(8,128)(2,1)S(1)}, bf16[16,3584]{1,0:T(8,128)(2,1)S(1)}, u32[]{:S(2)}, u32[]{:S(2)}) collective-permute-start(bf16[16,3584]{1,0:T(8,128)(2,1)S(1)} %get-tuple-element.43), channel_id=1, source_target_pairs={{0,12},{1,13},{2,14},{3,15},{4,0},{5,1},{6,2},{7,3},{8,4},{9,5},{1... | collective-permute-start | bytes 344072 | tf_op jit(solution)/shard_map/ppermute | solution.py:230
  97.2 1.5 %collective-permute-start.20 = (bf16[16,3584]{1,0:T(8,128)(2,1)S(1)}, bf16[16,3584]{1,0:T(8,128)(2,1)S(1)}, u32[]{:S(2)}, u32[]{:S(2)}) collective-permute-start(bf16[16,3584]{1,0:T(8,128)(2,1)S(1)} %get-tuple-element.42), channel_id=1, source_target_pairs={{0,8},{1,9},{2,10},{3,11},{4,12},{5,13},{6,14},{7,15},{8,0},{9,1},... | collective-permute-start | bytes 344072 | tf_op jit(solution)/shard_map/ppermute | solution.py:230
  98.8 0.0 collective-permute-done.15.refs_1_
  98.8 1.9 %collective-permute-start.21 = (bf16[16,3584]{1,0:T(8,128)(2,1)S(1)}, bf16[16,3584]{1,0:T(8,128)(2,1)S(1)}, u32[]{:S(2)}, u32[]{:S(2)}) collective-permute-start(bf16[16,3584]{1,0:T(8,128)(2,1)S(1)} %get-tuple-element.41), channel_id=1, source_target_pairs={{0,4},{1,5},{2,6},{3,7},{4,8},{5,9},{6,10},{7,11},{8,12},{9,13},{1... | collective-permute-start | bytes 344072 | tf_op jit(solution)/shard_map/ppermute | solution.py:230
  100.7 0.0 collective-permute-done.16.refs_2_
  100.7 0.1 collective-permute-start.17
  100.8 6.2 %collective-permute-done.17.refs_3_ = bf16[16,2560]{1,0:T(8,128)(2,1)S(1)} collective-permute-done((bf16[16,2560]{1,0:T(8,128)(2,1)S(1)}, bf16[16,2560]{1,0:T(8,128)(2,1)S(1)}, u32[]{:S(2)}, u32[]{:S(2)}) %collective-permute-start.17) | collective-permute-done | bytes 81952 | tf_op jit(solution)/shard_map/ppermute | solution.py:230
  107.0 0.0 collective-permute-done.13.arrived_ref
  107.0 0.0 collective-permute-done.19.refs_5_
  107.0 0.0 collective-permute-done.20.refs_6_
  107.0 0.0 collective-permute-done.21.refs_7_
  107.0 0.0 copy-done.1
  107.0 0.0 copy-done.4
  107.0 0.0 copy-done.5
  107.0 1.4 %mix.1 = bf16[24,6144]{1,0:T(8,128)(2,1)} custom-call(s32[2,24]{1,0:T(2,128)S(1)} %bitcast.5, f32[2,24]{1,0:T(2,128)S(1)} %bitcast.6, bf16[24,6144]{1,0:T(8,128)(2,1)S(1)} %copy-done.1, bf16[16,6144]{1,0:T(8,128)(2,1)S(1)} %collective-permute-done.13.arrived_ref, bf16[16,2560]{1,0:T(8,128)(2,1)S(1)} %get-tuple-element.39.refs_0_, ...), custom_call_target="tpu_custom_call" | custom-call | tf_op jit(solution)/shard_map/mix/pallas_call | solution.py:214
  (23 shorter events, 0.3 us)
Async XLA Ops:
  0.0 1.0 copy-start
  1.0 0.7 copy-start.2
  1.7 0.7 copy-start.3
  2.9 28.0 %collective-permute-start.5 = (bf16[16,3584]{1,0:T(8,128)(2,1)S(1)}, bf16[16,3584]{1,0:T(8,128)(2,1)S(1)}, u32[]{:S(2)}, u32[]{:S(2)}) collective-permute-start(bf16[16,3584]{1,0:T(8,128)(2,1)S(1)} %get-tuple-element.25), channel_id=1, source_target_pairs={{0,4},{1,5},{2,6},{3,7},{4,8},{5,9},{6,10},{7,11},{8,12},{9,13},{1... | collective-permute-start | bytes 344072 | tf_op jit(solution)/shard_map/ppermute | solution.py:230
  6.0 25.0 %collective-permute-start.6 = (bf16[16,3584]{1,0:T(8,128)(2,1)S(1)}, bf16[16,3584]{1,0:T(8,128)(2,1)S(1)}, u32[]{:S(2)}, u32[]{:S(2)}) collective-permute-start(bf16[16,3584]{1,0:T(8,128)(2,1)S(1)} %get-tuple-element.26), channel_id=1, source_target_pairs={{0,8},{1,9},{2,10},{3,11},{4,12},{5,13},{6,14},{7,15},{8,0},{9,1},... | collective-permute-start | bytes 344072 | tf_op jit(solution)/shard_map/ppermute | solution.py:230
  8.6 22.4 %collective-permute-start.7 = (bf16[16,3584]{1,0:T(8,128)(2,1)S(1)}, bf16[16,3584]{1,0:T(8,128)(2,1)S(1)}, u32[]{:S(2)}, u32[]{:S(2)}) collective-permute-start(bf16[16,3584]{1,0:T(8,128)(2,1)S(1)} %get-tuple-element.27), channel_id=1, source_target_pairs={{0,12},{1,13},{2,14},{3,15},{4,0},{5,1},{6,2},{7,3},{8,4},{9,5},{1... | collective-permute-start | bytes 344072 | tf_op jit(solution)/shard_map/ppermute | solution.py:230
  9.9 21.7 %collective-permute-start.3 = (bf16[16,6144]{1,0:T(8,128)(2,1)S(1)}, bf16[16,6144]{1,0:T(8,128)(2,1)S(1)}, u32[]{:S(2)}, u32[]{:S(2)}) collective-permute-start(bf16[16,6144]{1,0:T(8,128)(2,1)S(1)} %get-tuple-element.21.refs_0_), channel_id=1, source_target_pairs={{0,2},{1,3},{2,0},{3,1},{4,6},{5,7},{6,4},{7,5},{8,10},{9,11},{10,... | collective-permute-start | bytes 589832 | tf_op jit(solution)/shard_map/ppermute | solution.py:235
  11.4 6.5 %collective-permute-start = (bf16[16,2560]{1,0:T(8,128)(2,1)S(1)}, bf16[16,2560]{1,0:T(8,128)(2,1)S(1)}, u32[]{:S(2)}, u32[]{:S(2)}) collective-permute-start(bf16[16,2560]{1,0:T(8,128)(2,1)S(1)} %get-tuple-element.22), channel_id=1, source_target_pairs={{0,4},{1,5},{2,6},{3,7},{4,8},{5,9},{6,10},{7,11},{8,12},{9,13},{1... | collective-permute-start | bytes 245768 | tf_op jit(solution)/shard_map/ppermute | solution.py:230
  18.0 6.9 %collective-permute-start.1 = (bf16[16,2560]{1,0:T(8,128)(2,1)S(1)}, bf16[16,2560]{1,0:T(8,128)(2,1)S(1)}, u32[]{:S(2)}, u32[]{:S(2)}) collective-permute-start(bf16[16,2560]{1,0:T(8,128)(2,1)S(1)} %get-tuple-element.23), channel_id=1, source_target_pairs={{0,8},{1,9},{2,10},{3,11},{4,12},{5,13},{6,14},{7,15},{8,0},{9,1},... | collective-permute-start | bytes 245768 | tf_op jit(solution)/shard_map/ppermute | solution.py:230
  24.9 4.4 %collective-permute-start.2 = (bf16[16,2560]{1,0:T(8,128)(2,1)S(1)}, bf16[16,2560]{1,0:T(8,128)(2,1)S(1)}, u32[]{:S(2)}, u32[]{:S(2)}) collective-permute-start(bf16[16,2560]{1,0:T(8,128)(2,1)S(1)} %get-tuple-element.24), channel_id=1, source_target_pairs={{0,12},{1,13},{2,14},{3,15},{4,0},{5,1},{6,2},{7,3},{8,4},{9,5},{1... | collective-permute-start | bytes 245768 | tf_op jit(solution)/shard_map/ppermute | solution.py:230
  29.3 11.7 %collective-permute-start.4 = (bf16[48,2560]{1,0:T(8,128)(2,1)S(1)}, bf16[48,2560]{1,0:T(8,128)(2,1)S(1)}, u32[]{:S(2)}, u32[]{:S(2)}) collective-permute-start(bf16[48,2560]{1,0:T(8,128)(2,1)S(1)} %get-tuple-element.54.refs_1_), channel_id=1, source_target_pairs={{0,2},{1,3},{2,0},{3,1},{4,6},{5,7},{6,4},{7,5},{8,10},{9,11},{10,... | collective-permute-start | bytes 737288 | tf_op jit(solution)/shard_map/ppermute | solution.py:235
  31.0 9.9 %collective-permute-start.8 = (bf16[48,3584]{1,0:T(8,128)(2,1)S(1)}, bf16[48,3584]{1,0:T(8,128)(2,1)S(1)}, u32[]{:S(2)}, u32[]{:S(2)}) collective-permute-start(bf16[48,3584]{1,0:T(8,128)(2,1)S(1)} %get-tuple-element.48.refs_1_), channel_id=1, source_target_pairs={{0,2},{1,3},{2,0},{3,1},{4,6},{5,7},{6,4},{7,5},{8,10},{9,11},{10,... | collective-permute-start | bytes 1032200 | tf_op jit(solution)/shard_map/ppermute | solution.py:235
  40.9 2.5 %collective-permute-start.9 = (bf16[128,3584]{1,0:T(8,128)(2,1)S(1)}, bf16[128,3584]{1,0:T(8,128)(2,1)S(1)}, u32[]{:S(2)}, u32[]{:S(2)}) collective-permute-start(bf16[128,3584]{1,0:T(8,128)(2,1)S(1)} %constant_dynamic-update-slice_fusion.10), channel_id=1, source_target_pairs={{0,1},{1,0},{2,3},{3,2},{4,5},{5,4},{6,7},{7,6},{8,9},{9,8},{10,11... | collective-permute-start | bytes 2752520 | tf_op jit(solution)/shard_map/ppermute | solution.py:235
  52.1 2.2 %collective-permute-start.10 = (bf16[128,2560]{1,0:T(8,128)(2,1)S(1)}, bf16[128,2560]{1,0:T(8,128)(2,1)S(1)}, u32[]{:S(2)}, u32[]{:S(2)}) collective-permute-start(bf16[128,2560]{1,0:T(8,128)(2,1)S(1)} %constant_dynamic-update-slice_fusion.3), channel_id=1, source_target_pairs={{0,1},{1,0},{2,3},{3,2},{4,5},{5,4},{6,7},{7,6},{8,9},{9,8},{10,11... | collective-permute-start | bytes 1966088 | tf_op jit(solution)/shard_map/ppermute | solution.py:235
  54.3 0.8 copy-start.6
  66.6 6.5 %collective-permute-start.11 = (bf16[128,2560]{1,0:T(8,128)(2,1)S(1)}, bf16[128,2560]{1,0:T(8,128)(2,1)S(1)}, u32[]{:S(2)}, u32[]{:S(2)}) collective-permute-start(bf16[128,2560]{1,0:T(8,128)(2,1)S(1)} %get-tuple-element.34), channel_id=1, source_target_pairs={{0,1},{1,0},{2,3},{3,2},{4,5},{5,4},{6,7},{7,6},{8,9},{9,8},{10,11... | collective-permute-start | bytes 1966088 | tf_op jit(solution)/shard_map/ppermute | solution.py:235
  72.7 11.8 %collective-permute-start.12 = (bf16[128,3584]{1,0:T(8,128)(2,1)}, bf16[128,3584]{1,0:T(8,128)(2,1)S(1)}, u32[]{:S(2)}, u32[]{:S(2)}) collective-permute-start(bf16[128,3584]{1,0:T(8,128)(2,1)} %get-tuple-element.36), channel_id=1, source_target_pairs={{0,1},{1,0},{2,3},{3,2},{4,5},{5,4},{6,7},{7,6},{8,9},{9,8},{10,11... | collective-permute-start | bytes 2752520 | tf_op jit(solution)/shard_map/ppermute | solution.py:235
  73.3 8.1 %collective-permute-start.14 = (bf16[48,2560]{1,0:T(8,128)(2,1)S(1)}, bf16[48,2560]{1,0:T(8,128)(2,1)S(1)}, u32[]{:S(2)}, u32[]{:S(2)}) collective-permute-start(bf16[48,2560]{1,0:T(8,128)(2,1)S(1)} %slice.78), channel_id=1, source_target_pairs={{0,2},{1,3},{2,0},{3,1},{4,6},{5,7},{6,4},{7,5},{8,10},{9,11},{10,... | collective-permute-start | bytes 737288 | tf_op jit(solution)/shard_map/ppermute | solution.py:235
  81.4 17.4 %collective-permute-start.15 = (bf16[16,2560]{1,0:T(8,128)(2,1)S(1)}, bf16[16,2560]{1,0:T(8,128)(2,1)S(1)}, u32[]{:S(2)}, u32[]{:S(2)}) collective-permute-start(bf16[16,2560]{1,0:T(8,128)(2,1)S(1)} %get-tuple-element.46), channel_id=1, source_target_pairs={{0,12},{1,13},{2,14},{3,15},{4,0},{5,1},{6,2},{7,3},{8,4},{9,5},{1... | collective-permute-start | bytes 245768 | tf_op jit(solution)/shard_map/ppermute | solution.py:230
  84.4 16.3 %collective-permute-start.16 = (bf16[16,2560]{1,0:T(8,128)(2,1)S(1)}, bf16[16,2560]{1,0:T(8,128)(2,1)S(1)}, u32[]{:S(2)}, u32[]{:S(2)}) collective-permute-start(bf16[16,2560]{1,0:T(8,128)(2,1)S(1)} %get-tuple-element.45), channel_id=1, source_target_pairs={{0,8},{1,9},{2,10},{3,11},{4,12},{5,13},{6,14},{7,15},{8,0},{9,1},... | collective-permute-start | bytes 245768 | tf_op jit(solution)/shard_map/ppermute | solution.py:230
  84.7 22.4 %copy-start.1 = (bf16[24,6144]{1,0:T(8,128)(2,1)S(1)}, bf16[24,6144]{1,0:T(8,128)(2,1)}, u32[]{:S(2)}) copy-start(bf16[24,6144]{1,0:T(8,128)(2,1)} %act_ref.3) | copy-start | bytes 884740
  84.7 22.4 %copy-start.4 = (s32[24,2]{0,1:T(2,128)S(1)}, s32[24,2]{0,1:T(2,128)}, u32[]{:S(2)}) copy-start(s32[24,2]{0,1:T(2,128)} %param.8) | copy-start | bytes 580
  84.7 22.4 %copy-start.5 = (f32[24,2]{0,1:T(2,128)S(1)}, f32[24,2]{0,1:T(2,128)}, u32[]{:S(2)}) copy-start(f32[24,2]{0,1:T(2,128)} %param.9) | copy-start | bytes 580
  84.7 11.1 %collective-permute-start.18 = (bf16[48,3584]{1,0:T(8,128)(2,1)S(1)}, bf16[48,3584]{1,0:T(8,128)(2,1)S(1)}, u32[]{:S(2)}, u32[]{:S(2)}) collective-permute-start(bf16[48,3584]{1,0:T(8,128)(2,1)S(1)} %slice.84), channel_id=1, source_target_pairs={{0,2},{1,3},{2,0},{3,1},{4,6},{5,7},{6,4},{7,5},{8,10},{9,11},{10,... | collective-permute-start | bytes 1032200 | tf_op jit(solution)/shard_map/ppermute | solution.py:235
  86.3 20.6 %collective-permute-start.13 = (bf16[16,6144]{1,0:T(8,128)(2,1)S(1)}, bf16[16,6144]{1,0:T(8,128)(2,1)S(1)}, u32[]{:S(2)}, u32[]{:S(2)}) collective-permute-start(bf16[16,6144]{1,0:T(8,128)(2,1)S(1)} %pad_maximum_fusion), channel_id=1, source_target_pairs={{0,2},{1,3},{2,0},{3,1},{4,6},{5,7},{6,4},{7,5},{8,10},{9,11},{10,... | collective-permute-start | bytes 589832 | tf_op jit(solution)/shard_map/ppermute | solution.py:235
  95.9 11.0 %collective-permute-start.19 = (bf16[16,3584]{1,0:T(8,128)(2,1)S(1)}, bf16[16,3584]{1,0:T(8,128)(2,1)S(1)}, u32[]{:S(2)}, u32[]{:S(2)}) collective-permute-start(bf16[16,3584]{1,0:T(8,128)(2,1)S(1)} %get-tuple-element.43), channel_id=1, source_target_pairs={{0,12},{1,13},{2,14},{3,15},{4,0},{5,1},{6,2},{7,3},{8,4},{9,5},{1... | collective-permute-start | bytes 344072 | tf_op jit(solution)/shard_map/ppermute | solution.py:230
  97.2 9.7 %collective-permute-start.20 = (bf16[16,3584]{1,0:T(8,128)(2,1)S(1)}, bf16[16,3584]{1,0:T(8,128)(2,1)S(1)}, u32[]{:S(2)}, u32[]{:S(2)}) collective-permute-start(bf16[16,3584]{1,0:T(8,128)(2,1)S(1)} %get-tuple-element.42), channel_id=1, source_target_pairs={{0,8},{1,9},{2,10},{3,11},{4,12},{5,13},{6,14},{7,15},{8,0},{9,1},... | collective-permute-start | bytes 344072 | tf_op jit(solution)/shard_map/ppermute | solution.py:230
  98.8 8.2 %collective-permute-start.21 = (bf16[16,3584]{1,0:T(8,128)(2,1)S(1)}, bf16[16,3584]{1,0:T(8,128)(2,1)S(1)}, u32[]{:S(2)}, u32[]{:S(2)}) collective-permute-start(bf16[16,3584]{1,0:T(8,128)(2,1)S(1)} %get-tuple-element.41), channel_id=1, source_target_pairs={{0,4},{1,5},{2,6},{3,7},{4,8},{5,9},{6,10},{7,11},{8,12},{9,13},{1... | collective-permute-start | bytes 344072 | tf_op jit(solution)/shard_map/ppermute | solution.py:230
  100.7 6.2 %collective-permute-start.17 = (bf16[16,2560]{1,0:T(8,128)(2,1)S(1)}, bf16[16,2560]{1,0:T(8,128)(2,1)S(1)}, u32[]{:S(2)}, u32[]{:S(2)}) collective-permute-start(bf16[16,2560]{1,0:T(8,128)(2,1)S(1)} %get-tuple-element.44), channel_id=1, source_target_pairs={{0,4},{1,5},{2,6},{3,7},{4,8},{5,9},{6,10},{7,11},{8,12},{9,13},{1... | collective-permute-start | bytes 245768 | tf_op jit(solution)/shard_map/ppermute | solution.py:230

commit v5 on v4

v5 whole, which is shorter than its diff:
```python
import functools

import jax
import jax.numpy as jnp
from jax import lax
from jax.experimental import pallas as pl
from jax.experimental.pallas import tpu as pltpu
from jax.sharding import PartitionSpec as P

EXPERTS = 4
CAP = 16
CHUNKS = 2
BLOCK = 1024
FETCH_ROWS = 144
MIB = 1 << 20
LIMIT = pltpu.CompilerParams(vmem_limit_bytes=16 * MIB)
VMEM = pl.BlockSpec(memory_space=pltpu.VMEM)
ANY = pl.BlockSpec(memory_space=pl.ANY)


def choices(ids):
    tokens = ids.shape[1]
    line = lax.broadcasted_iota(jnp.int32, (EXPERTS * CAP, tokens), 0)
    expert = line // CAP
    slot = (line % CAP).astype(jnp.float32)
    first = ids[0:1, :] == expert
    second = ids[1:2, :] == expert
    named = (first | second).astype(jnp.float32)
    square = (tokens, tokens)
    earlier = lax.broadcasted_iota(jnp.int32, square, 0) < lax.broadcasted_iota(
        jnp.int32, square, 1
    )
    rank = jnp.dot(named, earlier.astype(jnp.float32), preferred_element_type=jnp.float32)
    here = rank == slot
    return first & here, second & here


def pack_kernel(ids_ref, act_ref, gain_ref, *out_refs):
    values = act_ref[...].astype(jnp.float32)
    mean_sq = jnp.mean(values * values, axis=-1, keepdims=True)
    normed = (values * lax.rsqrt(mean_sq + 1e-06) * gain_ref[...]).astype(jnp.bfloat16)
    first, second = choices(ids_ref[...])
    pick = (first | second).astype(jnp.float32).astype(jnp.bfloat16)
    width = out_refs[0].shape[1]
    for k in range(CHUNKS):
        columns = slice(k * width, (k + 1) * width)
        rows = jnp.dot(pick, normed[:, columns], preferred_element_type=jnp.float32)
        out_refs[k][...] = rows.astype(jnp.bfloat16)


def pack(ids, activations, gain):
    width = activations.shape[1]
    part = jax.ShapeDtypeStruct((EXPERTS * CAP, width // CHUNKS), jnp.bfloat16)
    return pl.pallas_call(
        pack_kernel,
        out_shape=[part] * CHUNKS,
        compiler_params=LIMIT,
        name="norm_and_pack",
    )(ids, activations, gain.reshape(1, width))


def fetch_kernel(count, at, *refs):
    weights, held, sems = refs[:count], refs[count + 1 : -1], refs[-1]
    copies = []
    for j in range(count):
        part = held[j].shape[1]
        for b in range(sems.shape[1]):
            rows = pl.ds(b * FETCH_ROWS, FETCH_ROWS)
            copies.append(
                pltpu.make_async_copy(
                    weights[j].at[rows, at : at + part], held[j].at[rows], sems.at[j, b]
                )
            )
    for copy in copies:
        copy.start()
    for copy in copies:
        copy.wait()


def fetch(weights, at, part, after):
    count = len(weights)
    rows = weights[0].shape[0]
    held = pltpu.VMEM((rows, part), jnp.bfloat16)
    return pl.pallas_call(
        functools.partial(fetch_kernel, count, at),
        in_specs=[ANY] * (count + 1),
        out_specs=[VMEM] * count,
        out_shape=[held] * count,
        scratch_shapes=[pltpu.SemaphoreType.DMA((count, rows // FETCH_ROWS))],
        compiler_params=LIMIT,
        cost_estimate=pl.CostEstimate(
            flops=0, bytes_accessed=4 * count * rows * part, transcendentals=0
        ),
        name="fetch",
    )(*[pltpu.with_memory_space_constraint(w, pltpu.HBM) for w in weights], after)


def gate_up_kernel(count, begin, end, *refs):
    pieces, refs = refs[:count], refs[count:]
    weights, refs = refs[:2], refs[2:]
    turned, refs = refs[-1], refs[:-1]
    if not begin:
        before, refs = refs[:2], refs[2:]
    if end:
        hidden_ref, refs = refs[0], refs[1:]
    sums = refs
    steps, block, _ = turned.shape

    @pl.loop(0, steps)
    def _(c):
        columns = pl.ds(pl.multiple_of(c * block, block), block)
        turned[c] = jnp.concatenate([p[:, columns] for p in pieces], axis=0).T

    for j in range(2):
        sums[j][...] = jnp.zeros_like(sums[j]) if begin else before[j][...]

    @pl.loop(0, steps)
    def _(c):
        columns = pl.ds(pl.multiple_of(c * block, block), block)
        for j in range(2):
            sums[j][...] += jnp.dot(
                weights[j][:, columns], turned[c], preferred_element_type=jnp.float32
            )

    if end:
        hidden = (jax.nn.silu(sums[0][...]) * sums[1][...]).astype(jnp.bfloat16)
        hidden_ref[...] = hidden.T


def gate_up(k, pieces, weights, totals):
    hidden, part = weights[0].shape
    begin, end = k == 0, k == CHUNKS - 1
    rows = sum(p.shape[0] for p in pieces)
    total = jax.ShapeDtypeStruct((hidden, rows), jnp.float32)
    out_shape, scratch = [total] * 2, []
    if end:
        out_shape = [jax.ShapeDtypeStruct((rows, hidden), jnp.bfloat16)]
        scratch = [pltpu.VMEM((hidden, rows), jnp.float32)] * 2
    scratch.append(pltpu.VMEM((part // BLOCK, BLOCK, rows), jnp.bfloat16))
    weights = [pltpu.with_memory_space_constraint(w, pltpu.VMEM) for w in weights]
    return pl.pallas_call(
        functools.partial(gate_up_kernel, len(pieces), begin, end),
        in_specs=[VMEM] * (len(pieces) + 2 + len(totals)),
        out_shape=out_shape,
        scratch_shapes=scratch,
        compiler_params=LIMIT,
        cost_estimate=pl.CostEstimate(
            flops=4 * rows * hidden * part,
            bytes_accessed=4 * hidden * part + 8 * rows * hidden,
            transcendentals=0,
        ),
        name="gate_up",
    )(*pieces, *weights, *totals)


def down_kernel(at, hidden_ref, w_ref, keep_ref, send_ref):
    half, part = keep_ref.shape
    block = BLOCK // 2

    @pl.loop(0, part // block)
    def _(c):
        columns = pl.ds(pl.multiple_of(at + c * block, block), block)
        out = jnp.dot(hidden_ref[...], w_ref[:, columns], preferred_element_type=jnp.float32)
        out = out.astype(jnp.bfloat16)
        columns = pl.ds(pl.multiple_of(c * block, block), block)
        keep_ref[:, columns] = out[:half]
        send_ref[:, columns] = out[half:]


def down(at, part, hidden, w_down):
    rows, depth = hidden.shape
    return pl.pallas_call(
        functools.partial(down_kernel, at),
        in_specs=[VMEM, VMEM],
        out_shape=[jax.ShapeDtypeStruct((rows // 2, part), jnp.bfloat16)] * 2,
        compiler_params=LIMIT,
        cost_estimate=pl.CostEstimate(
            flops=2 * rows * depth * part,
            bytes_accessed=2 * (depth * part + rows * depth + rows * part),
            transcendentals=0,
        ),
        name="down",
    )(hidden, pltpu.with_memory_space_constraint(w_down, pltpu.VMEM))


def mix_kernel(ids_ref, logits_ref, act_ref, *refs):
    pieces, out_ref = refs[:-1], refs[-1]
    first, second = choices(ids_ref[...])
    lead = logits_ref[0:1, :] - logits_ref[1:2, :]
    weight = jnp.where(first, jax.nn.sigmoid(lead), 0.0)
    weight = (weight + jnp.where(second, jax.nn.sigmoid(-lead), 0.0)).T
    high = weight.astype(jnp.bfloat16)
    rest = weight - high.astype(jnp.float32)
    middle = rest.astype(jnp.bfloat16)
    low = (rest - middle.astype(jnp.float32)).astype(jnp.bfloat16)
    part = pieces[0].shape[1]
    for k, piece in enumerate(pieces):
        columns = slice(k * part, (k + 1) * part)
        total = act_ref[:, columns].astype(jnp.float32)
        for term in (low, middle, high):
            total = total + jnp.dot(term, piece[...], preferred_element_type=jnp.float32)
        out_ref[:, columns] = total.astype(jnp.bfloat16)


def mix(ids, logits, activations, pieces):
    return pl.pallas_call(
        mix_kernel,
        out_shape=jax.ShapeDtypeStruct(activations.shape, jnp.bfloat16),
        compiler_params=LIMIT,
        name="mix",
    )(ids, logits, activations, *pieces)


def on_device(activations, expert_ids, route_logits, norm_gain, w_gate, w_up, w_down):
    devices = lax.axis_size("expert")
    group = devices // EXPERTS
    width = activations.shape[1]
    part = width // CHUNKS
    planes = [[g + e * group for e in range(EXPERTS)] for g in range(group)]

    def across(x):
        return lax.all_to_all(
            x, "expert", split_axis=0, concat_axis=0, tiled=True, axis_index_groups=planes
        )

    def swap(x, bit):
        return lax.ppermute(x, "expert", [(i, i ^ bit) for i in range(devices)])

    ids = expert_ids.T
    packed = pack(ids, activations, norm_gain)
    gate_up_w = [fetch([w_gate, w_up], k * part, part, packed[0]) for k in range(CHUNKS)]
    gathered = [across(p) for p in packed]
    totals = []
    for k in range(CHUNKS):
        block = gathered[k]
        if k:
            block, _ = lax.optimization_barrier((block, gathered[k - 1]))
        pieces = [block]
        bit = group // 2
        while bit:
            if bit == 1 and totals:
                block, totals = lax.optimization_barrier((block, totals))
            pieces.append(swap(block, bit))
            block = jnp.concatenate([block, pieces[-1]], axis=0)
            bit //= 2
        totals = gate_up(k, pieces, gate_up_w[k], totals)
        if k == CHUNKS - 2:
            (down_w,) = fetch([w_down], 0, width, totals[0])
    hidden = totals[0]
    returned = []
    for k in range(CHUNKS):
        keep, send = down(k * part, part, hidden, down_w)
        bit = 1
        while True:
            total = keep.astype(jnp.float32) + swap(send, bit).astype(jnp.float32)
            total = total.astype(jnp.bfloat16)
            bit *= 2
            if bit == group:
                break
            keep, send = total[: total.shape[0] // 2], total[total.shape[0] // 2 :]
        returned.append(across(total))
    return mix(ids, route_logits.T, activations, returned)


def solution(mesh):
    in_specs = (
        P(("parts", "expert"), None),
        P(("parts", "expert"), None),
        P(("parts", "expert"), None),
        P(),
        P("expert", None),
        P("expert", None),
        P("expert", None),
    )
    out_specs = P(("parts", "expert"), None)
    return jax.shard_map(
        on_device, mesh=mesh, in_specs=in_specs, out_specs=out_specs, check_vma=False
    )
```

time: 109 us -> 116 us (1.064)
  blocking collectives: 0 us -> 30.9 us
  starting transfers between devices: 27.9 us -> 11.8 us
  waiting for transfers between devices: 48.3 us -> 34.5 us
  Pallas kernels: 27.9 us -> 34.3 us
    all_to_all x0 -> x2, blocking collectives: none -> 30.9 us  [across(): lax.all_to_all(x, 'expert', split_axis=0, concat_axis=0, tiled=True, axis...]
    ppermute x12 -> x0, starting transfers between devices: 19.6 us -> none  [shift(): lax.ppermute(x, 'expert', [(i, (i + s * group) % devices) for i in range(...]
    ppermute x12 -> x0, waiting for transfers between devices: 19.3 us -> none  [shift(): lax.ppermute(x, 'expert', [(i, (i + s * group) % devices) for i in range(...]
    all_to_all x0 -> x2, waiting for transfers between devices: none -> 13.8 us  [across(): lax.all_to_all(x, 'expert', split_axis=0, concat_axis=0, tiled=True, axis...]
    ppermute x10 -> x8, waiting for transfers between devices: 29 us -> 20.7 us  [swap(): return lax.ppermute(x, 'expert', [(i, i ^ bit) for i in range(devices)])]
    all_to_all x0 -> x2, starting transfers between devices: none -> 7.81 us  [across(): lax.all_to_all(x, 'expert', split_axis=0, concat_axis=0, tiled=True, axis...]
    pallas_call x6 -> x9, Pallas kernels: 27.9 us -> 34.3 us  [the longest x3 15.5 us: fetch(): pl.pallas_call(functools.partial(fetch_kernel, count, at), in_specs=[ANY]...]
    ppermute x10 -> x8, starting transfers between devices: 8.35 us -> 4.01 us  [swap(): return lax.ppermute(x, 'expert', [(i, i ^ bit) for i in range(devices)])]
  transfers between devices with their start and end apart: 22 -> 10, of which waited for: 9 -> 7; matrix products, arithmetic and copies ran while one was open for 1% -> 1% of each run, Pallas kernels for 5% -> 16%
where the time goes in v5:
time: 116 us
  waiting for transfers between devices  34.5 us (30%)
  Pallas kernels  34.3 us (30%)
  blocking collectives  30.9 us (27%)
  starting transfers between devices  11.8 us (10%)
  local copies, waits for them, and re-layouts  2.44 us (2%)
  other arithmetic  1.41 us (1%)
    all_to_all x2, blocking collectives, across(): lax.all_to_all(x, 'expert', split_axis=0, concat_axis=0, tiled=True, axis...  30.9 us
    ppermute x8, waiting for transfers between devices, swap(): return lax.ppermute(x, 'expert', [(i, i ^ bit) for i in range(devices)])  20.7 us
    pallas_call x3, Pallas kernels, fetch(): pl.pallas_call(functools.partial(fetch_kernel, count, at), in_specs=[ANY]...  15.5 us
    all_to_all x2, waiting for transfers between devices, across(): lax.all_to_all(x, 'expert', split_axis=0, concat_axis=0, tiled=True, axis...  13.8 us
    pallas_call x2, Pallas kernels, gate_up(): pl.pallas_call(functools.partial(gate_up_kernel, len(pieces), begin, end)...  10 us
    all_to_all x2, starting transfers between devices, across(): lax.all_to_all(x, 'expert', split_axis=0, concat_axis=0, tiled=True, axis...  7.81 us
    pallas_call x2, Pallas kernels, down(): pl.pallas_call(functools.partial(down_kernel, at), in_specs=[VMEM, VMEM],...  6.13 us
    ppermute x8, starting transfers between devices, swap(): return lax.ppermute(x, 'expert', [(i, i ^ bit) for i in range(devices)])  4.01 us
  transfers between devices with their start and end apart: 10, of which 7 were waited for; matrix products, arithmetic and copies ran while one was open for 1% of the time, Pallas kernels for 16%

profile of v5, /device:TPU:0, one launch (start us, length us, event | category | flops | bytes accessed | tf_op | source)
XLA Modules:
  0.0 115.5 jit_solution(6914131839205422888)
XLA Ops:
  0.0 0.0 copy-start
  0.0 1.0 copy-done
  1.0 0.0 copy-start.2
  1.0 0.7 copy-done.2
  1.7 0.0 copy-start.3
  1.7 0.7 copy-done.3
  2.4 1.3 %norm_and_pack.1 = (bf16[64,3072]{1,0:T(8,128)(2,1)S(1)}, bf16[64,3072]{1,0:T(8,128)(2,1)}) custom-call(s32[2,24]{1,0:T(2,128)S(1)} %bitcast.21, bf16[24,6144]{1,0:T(8,128)(2,1)S(1)} %copy-done, f32[1,6144]{1,0:T(1,128)S(1)} %bitcast.20), custom_call_target="tpu_custom_call" | custom-call | tf_op jit(solution)/shard_map/norm_and_pack/pallas_call | solution.py:54
  3.6 17.8 %all_to_all.45 = bf16[4,16,3072]{2,1,0:T(8,128)(2,1)S(1)} all-to-all(bf16[4,16,3072]{2,1,0:T(8,128)(2,1)S(1)} %bitcast.11), channel_id=1, replica_groups={{0,4,8,12},{1,5,9,13},{2,6,10,14},{3,7,11,15},{16,20,24,28},{17,21,25,2..., dimensions={0} | all-to-all | bytes 786432 | tf_op jit(solution)/shard_map/all_to_all | solution.py:222
  21.4 1.5 %collective-permute-start.1 = (bf16[64,3072]{1,0:T(8,128)(2,1)S(1)}, bf16[64,3072]{1,0:T(8,128)(2,1)S(1)}, u32[]{:S(2)}, u32[]{:S(2)}) collective-permute-start(bf16[64,3072]{1,0:T(8,128)(2,1)S(1)} %bitcast.15), channel_id=1, source_target_pairs={{0,2},{1,3},{2,0},{3,1},{4,6},{5,7},{6,4},{7,5},{8,10},{9,11},{10,... | collective-permute-start | bytes 1179656 | tf_op jit(solution)/shard_map/ppermute | solution.py:227
  23.0 3.5 %all-to-all-start = ((bf16[4,16,3072]{2,1,0:T(8,128)(2,1)}), bf16[4,16,3072]{2,1,0:T(8,128)(2,1)S(1)}, u32[]{:S(2)}, u32[]{:S(2)}) async-start(bf16[4,16,3072]{2,1,0:T(8,128)(2,1)} %bitcast.3), calls=%async_computation | async-start | bytes 786432 | tf_op jit(solution)/shard_map/all_to_all | solution.py:222
  26.4 4.7 %collective-permute-done.1.refs_1_ = bf16[64,3072]{1,0:T(8,128)(2,1)S(1)} collective-permute-done((bf16[64,3072]{1,0:T(8,128)(2,1)S(1)}, bf16[64,3072]{1,0:T(8,128)(2,1)S(1)}, u32[]{:S(2)}, u32[]{:S(2)}) %collective-permute-start.1) | collective-permute-done | bytes 393248 | tf_op jit(solution)/shard_map/ppermute | solution.py:227
  31.2 0.1 pad_maximum_fusion.1
  31.2 0.1 collective-permute-start.2
  31.3 5.6 %all-to-all-done = bf16[4,16,3072]{2,1,0:T(8,128)(2,1)S(1)} async-done(((bf16[4,16,3072]{2,1,0:T(8,128)(2,1)}), bf16[4,16,3072]{2,1,0:T(8,128)(2,1)S(1)}, u32[]{:S(2)}, u32[]{:S(2)}) %all-to-all-start) | async-done | bytes 393248 | tf_op jit(solution)/shard_map/all_to_all | solution.py:222
  36.9 0.5 collective-permute-start
  37.4 5.2 %fetch.3 = (bf16[1152,3072]{1,0:T(8,128)(2,1)S(1)}, bf16[1152,3072]{1,0:T(8,128)(2,1)S(1)}) custom-call(bf16[1152,6144]{1,0:T(8,128)(2,1)} %refs_0_.4, bf16[1152,6144]{1,0:T(8,128)(2,1)} %refs_1_.3, bf16[64,3072]{1,0:T(8,128)(2,1)S(1)} %get-tuple-element.22.refs_2_), custom_call_target="tpu_custom_call" | custom-call | bytes 28311552 | tf_op jit(solution)/shard_map/fetch/pallas_call | solution.py:84
  42.6 2.5 %collective-permute-done.refs_1_ = bf16[64,3072]{1,0:T(8,128)(2,1)S(1)} collective-permute-done((bf16[64,3072]{1,0:T(8,128)(2,1)S(1)}, bf16[64,3072]{1,0:T(8,128)(2,1)S(1)}, u32[]{:S(2)}, u32[]{:S(2)}) %collective-permute-start) | collective-permute-done | bytes 393248 | tf_op jit(solution)/shard_map/ppermute | solution.py:227
  45.2 0.1 pad_maximum_fusion
  45.2 0.0 collective-permute-done.2.refs_2_
  45.2 4.9 %gate_up.2 = (f32[1152,256]{1,0:T(8,128)S(1)}, f32[1152,256]{1,0:T(8,128)S(1)}) custom-call(bf16[64,3072]{1,0:T(8,128)(2,1)S(1)} %bitcast.17, bf16[64,3072]{1,0:T(8,128)(2,1)S(1)} %collective-permute-done.1.refs_1_, bf16[128,3072]{1,0:T(8,128)(2,1)S(1)} %collective-permute-done.2.refs_2_, bf16[1152,3072]{1,0:T(8,128)(2,1)S(1)} %get-tuple-element.24.refs_3_, ...), custom_call_target="tpu_custom_call" | custom-call | flops 3623878656 | bytes 16515072 | tf_op jit(solution)/shard_map/gate_up/pallas_call | solution.py:141
  50.1 0.1 collective-permute-start.3
  50.2 5.2 %fetch.4 = (bf16[1152,3072]{1,0:T(8,128)(2,1)S(1)}, bf16[1152,3072]{1,0:T(8,128)(2,1)S(1)}) custom-call(bf16[1152,6144]{1,0:T(8,128)(2,1)} %refs_0_.4, bf16[1152,6144]{1,0:T(8,128)(2,1)} %refs_1_.3, bf16[64,3072]{1,0:T(8,128)(2,1)S(1)} %get-tuple-element.22.refs_2_), custom_call_target="tpu_custom_call" | custom-call | bytes 28311552 | tf_op jit(solution)/shard_map/fetch/pallas_call | solution.py:84
  55.4 5.2 %fetch.5.w_ref = bf16[1152,6144]{1,0:T(8,128)(2,1)S(1)} custom-call(bf16[1152,6144]{1,0:T(8,128)(2,1)} %refs_0_.5, f32[1152,256]{1,0:T(8,128)S(1)} %get-tuple-element.31.refs_5_.refs_1_), custom_call_target="tpu_custom_call" | custom-call | bytes 28311552 | tf_op jit(solution)/shard_map/fetch/pallas_call | solution.py:84
  60.6 0.0 collective-permute-done.3.refs_2_
  60.6 5.1 %gate_up.3.hidden_ref = bf16[256,1152]{1,0:T(8,128)(2,1)S(1)} custom-call(bf16[64,3072]{1,0:T(8,128)(2,1)S(1)} %bitcast.14, bf16[64,3072]{1,0:T(8,128)(2,1)S(1)} %collective-permute-done.refs_1_, bf16[128,3072]{1,0:T(8,128)(2,1)S(1)} %collective-permute-done.3.refs_2_, bf16[1152,3072]{1,0:T(8,128)(2,1)S(1)} %get-tuple-element.29.refs_3_, ...), custom_call_target="tpu_custom_call" | custom-call | flops 3623878656 | bytes 16515072 | tf_op jit(solution)/shard_map/gate_up/pallas_call | solution.py:141
  65.7 3.1 %down.3 = (bf16[128,3072]{1,0:T(8,128)(2,1)S(1)}, bf16[128,3072]{1,0:T(8,128)(2,1)S(1)}) custom-call(bf16[256,1152]{1,0:T(8,128)(2,1)S(1)} %gate_up.3.hidden_ref, bf16[1152,6144]{1,0:T(8,128)(2,1)S(1)} %fetch.5.w_ref), custom_call_target="tpu_custom_call" | custom-call | flops 1811939328 | bytes 9240576 | tf_op jit(solution)/shard_map/down/pallas_call | solution.py:172
  68.8 0.6 collective-permute-start.6
  69.4 3.1 %down.2 = (bf16[128,3072]{1,0:T(8,128)(2,1)S(1)}, bf16[128,3072]{1,0:T(8,128)(2,1)S(1)}) custom-call(bf16[256,1152]{1,0:T(8,128)(2,1)S(1)} %gate_up.3.hidden_ref, bf16[1152,6144]{1,0:T(8,128)(2,1)S(1)} %fetch.5.w_ref), custom_call_target="tpu_custom_call" | custom-call | flops 1811939328 | bytes 9240576 | tf_op jit(solution)/shard_map/down/pallas_call | solution.py:172
  72.4 0.1 collective-permute-start.4
  72.5 0.0 collective-permute-done.6
  72.5 0.2 add_convert_fusion
  72.8 0.6 collective-permute-start.7
  73.4 1.4 %collective-permute-done.4 = bf16[128,3072]{1,0:T(8,128)(2,1)S(1)} collective-permute-done((bf16[128,3072]{1,0:T(8,128)(2,1)S(1)}, bf16[128,3072]{1,0:T(8,128)(2,1)S(1)}, u32[]{:S(2)}, u32[]{:S(2)}) %collective-permute-start.4) | collective-permute-done | bytes 786464 | tf_op jit(solution)/shard_map/ppermute | solution.py:227
  74.8 0.2 add_convert_fusion.1
  75.0 0.6 collective-permute-start.5
  75.6 9.1 %collective-permute-done.7 = bf16[64,3072]{1,0:T(8,128)(2,1)S(1)} collective-permute-done((bf16[64,3072]{1,0:T(8,128)(2,1)S(1)}, bf16[64,3072]{1,0:T(8,128)(2,1)S(1)}, u32[]{:S(2)}, u32[]{:S(2)}) %collective-permute-start.7) | collective-permute-done | bytes 393248 | tf_op jit(solution)/shard_map/ppermute | solution.py:227
  84.7 0.8 add_convert_fusion.2
  85.6 0.0 copy-start.1
  85.6 0.0 copy-start.4
  85.6 0.0 copy-start.5
  85.6 4.4 %all-to-all-start.3 = ((bf16[4,16,3072]{2,1,0:T(8,128)(2,1)}), bf16[4,16,3072]{2,1,0:T(8,128)(2,1)S(1)}, u32[]{:S(2)}, u32[]{:S(2)}) async-start(bf16[4,16,3072]{2,1,0:T(8,128)(2,1)} %bitcast.9), calls=%async_computation.3 | async-start | bytes 786432 | tf_op jit(solution)/shard_map/all_to_all | solution.py:222
  89.9 2.8 %collective-permute-done.5 = bf16[64,3072]{1,0:T(8,128)(2,1)S(1)} collective-permute-done((bf16[64,3072]{1,0:T(8,128)(2,1)S(1)}, bf16[64,3072]{1,0:T(8,128)(2,1)S(1)}, u32[]{:S(2)}, u32[]{:S(2)}) %collective-permute-start.5) | collective-permute-done | bytes 393248 | tf_op jit(solution)/shard_map/ppermute | solution.py:227
  92.8 0.1 add_convert_fusion.3
  92.9 8.2 %all-to-all-done.3 = bf16[4,16,3072]{2,1,0:T(8,128)(2,1)S(1)} async-done(((bf16[4,16,3072]{2,1,0:T(8,128)(2,1)}), bf16[4,16,3072]{2,1,0:T(8,128)(2,1)S(1)}, u32[]{:S(2)}, u32[]{:S(2)}) %all-to-all-start.3) | async-done | bytes 393248 | tf_op jit(solution)/shard_map/all_to_all | solution.py:222
  101.0 13.1 %all_to_all.46 = bf16[4,16,3072]{2,1,0:T(8,128)(2,1)S(1)} all-to-all(bf16[4,16,3072]{2,1,0:T(8,128)(2,1)S(1)} %bitcast.24), channel_id=1, replica_groups={{0,4,8,12},{1,5,9,13},{2,6,10,14},{3,7,11,15},{16,20,24,28},{17,21,25,2..., dimensions={0} | all-to-all | bytes 786432 | tf_op jit(solution)/shard_map/all_to_all | solution.py:222
  114.1 0.0 copy-done.1
  114.1 0.0 copy-done.4
  114.1 0.0 copy-done.5
  114.2 1.4 %mix.1 = bf16[24,6144]{1,0:T(8,128)(2,1)} custom-call(s32[2,24]{1,0:T(2,128)S(1)} %bitcast.22, f32[2,24]{1,0:T(2,128)S(1)} %bitcast.23, bf16[24,6144]{1,0:T(8,128)(2,1)S(1)} %copy-done.1, bf16[64,3072]{1,0:T(8,128)(2,1)S(1)} %bitcast.19, bf16[64,3072]{1,0:T(8,128)(2,1)S(1)} %bitcast.18), custom_call_target="tpu_custom_call" | custom-call | tf_op jit(solution)/shard_map/mix/pallas_call | solution.py:206
  (2 shorter events, 0.1 us)
Async XLA Ops:
  0.0 1.0 copy-start
  1.0 0.7 copy-start.2
  1.7 0.7 copy-start.3
  21.4 9.7 %collective-permute-start.1 = (bf16[64,3072]{1,0:T(8,128)(2,1)S(1)}, bf16[64,3072]{1,0:T(8,128)(2,1)S(1)}, u32[]{:S(2)}, u32[]{:S(2)}) collective-permute-start(bf16[64,3072]{1,0:T(8,128)(2,1)S(1)} %bitcast.15), channel_id=1, source_target_pairs={{0,2},{1,3},{2,0},{3,1},{4,6},{5,7},{6,4},{7,5},{8,10},{9,11},{10,... | collective-permute-start | bytes 1179656 | tf_op jit(solution)/shard_map/ppermute | solution.py:227
  23.0 14.0 %all-to-all-start = ((bf16[4,16,3072]{2,1,0:T(8,128)(2,1)}), bf16[4,16,3072]{2,1,0:T(8,128)(2,1)S(1)}, u32[]{:S(2)}, u32[]{:S(2)}) async-start(bf16[4,16,3072]{2,1,0:T(8,128)(2,1)} %bitcast.3), calls=%async_computation | async-start | bytes 786432 | tf_op jit(solution)/shard_map/all_to_all | solution.py:222
  31.2 14.0 %collective-permute-start.2 = (bf16[128,3072]{1,0:T(8,128)(2,1)S(1)}, bf16[128,3072]{1,0:T(8,128)(2,1)S(1)}, u32[]{:S(2)}, u32[]{:S(2)}) collective-permute-start(bf16[128,3072]{1,0:T(8,128)(2,1)S(1)} %pad_maximum_fusion.1), channel_id=1, source_target_pairs={{0,1},{1,0},{2,3},{3,2},{4,5},{5,4},{6,7},{7,6},{8,9},{9,8},{10,11... | collective-permute-start | bytes 2359304 | tf_op jit(solution)/shard_map/ppermute | solution.py:227
  36.9 8.2 %collective-permute-start = (bf16[64,3072]{1,0:T(8,128)(2,1)S(1)}, bf16[64,3072]{1,0:T(8,128)(2,1)S(1)}, u32[]{:S(2)}, u32[]{:S(2)}) collective-permute-start(bf16[64,3072]{1,0:T(8,128)(2,1)S(1)} %bitcast.12), channel_id=1, source_target_pairs={{0,2},{1,3},{2,0},{3,1},{4,6},{5,7},{6,4},{7,5},{8,10},{9,11},{10,... | collective-permute-start | bytes 1179656 | tf_op jit(solution)/shard_map/ppermute | solution.py:227
  50.1 10.4 %collective-permute-start.3 = (bf16[128,3072]{1,0:T(8,128)(2,1)S(1)}, bf16[128,3072]{1,0:T(8,128)(2,1)S(1)}, u32[]{:S(2)}, u32[]{:S(2)}) collective-permute-start(bf16[128,3072]{1,0:T(8,128)(2,1)S(1)} %pad_maximum_fusion), channel_id=1, source_target_pairs={{0,1},{1,0},{2,3},{3,2},{4,5},{5,4},{6,7},{7,6},{8,9},{9,8},{10,11... | collective-permute-start | bytes 2359304 | tf_op jit(solution)/shard_map/ppermute | solution.py:227
  68.8 3.7 %collective-permute-start.6 = (bf16[128,3072]{1,0:T(8,128)(2,1)S(1)}, bf16[128,3072]{1,0:T(8,128)(2,1)S(1)}, u32[]{:S(2)}, u32[]{:S(2)}) collective-permute-start(bf16[128,3072]{1,0:T(8,128)(2,1)S(1)} %get-tuple-element.36), channel_id=1, source_target_pairs={{0,1},{1,0},{2,3},{3,2},{4,5},{5,4},{6,7},{7,6},{8,9},{9,8},{10,11... | collective-permute-start | bytes 2359304 | tf_op jit(solution)/shard_map/ppermute | solution.py:227
  72.4 2.4 %collective-permute-start.4 = (bf16[128,3072]{1,0:T(8,128)(2,1)S(1)}, bf16[128,3072]{1,0:T(8,128)(2,1)S(1)}, u32[]{:S(2)}, u32[]{:S(2)}) collective-permute-start(bf16[128,3072]{1,0:T(8,128)(2,1)S(1)} %get-tuple-element.34), channel_id=1, source_target_pairs={{0,1},{1,0},{2,3},{3,2},{4,5},{5,4},{6,7},{7,6},{8,9},{9,8},{10,11... | collective-permute-start | bytes 2359304 | tf_op jit(solution)/shard_map/ppermute | solution.py:227
  72.8 12.0 %collective-permute-start.7 = (bf16[64,3072]{1,0:T(8,128)(2,1)S(1)}, bf16[64,3072]{1,0:T(8,128)(2,1)S(1)}, u32[]{:S(2)}, u32[]{:S(2)}) collective-permute-start(bf16[64,3072]{1,0:T(8,128)(2,1)S(1)} %slice.19), channel_id=1, source_target_pairs={{0,2},{1,3},{2,0},{3,1},{4,6},{5,7},{6,4},{7,5},{8,10},{9,11},{10,... | collective-permute-start | bytes 1179656 | tf_op jit(solution)/shard_map/ppermute | solution.py:227
  75.0 17.7 %collective-permute-start.5 = (bf16[64,3072]{1,0:T(8,128)(2,1)S(1)}, bf16[64,3072]{1,0:T(8,128)(2,1)S(1)}, u32[]{:S(2)}, u32[]{:S(2)}) collective-permute-start(bf16[64,3072]{1,0:T(8,128)(2,1)S(1)} %slice.17), channel_id=1, source_target_pairs={{0,2},{1,3},{2,0},{3,1},{4,6},{5,7},{6,4},{7,5},{8,10},{9,11},{10,... | collective-permute-start | bytes 1179656 | tf_op jit(solution)/shard_map/ppermute | solution.py:227
  85.6 28.6 %copy-start.1 = (bf16[24,6144]{1,0:T(8,128)(2,1)S(1)}, bf16[24,6144]{1,0:T(8,128)(2,1)}, u32[]{:S(2)}) copy-start(bf16[24,6144]{1,0:T(8,128)(2,1)} %act_ref.3) | copy-start | bytes 884740
  85.6 28.6 %copy-start.4 = (s32[24,2]{0,1:T(2,128)S(1)}, s32[24,2]{0,1:T(2,128)}, u32[]{:S(2)}) copy-start(s32[24,2]{0,1:T(2,128)} %param.8) | copy-start | bytes 580
  85.6 28.6 %copy-start.5 = (f32[24,2]{0,1:T(2,128)S(1)}, f32[24,2]{0,1:T(2,128)}, u32[]{:S(2)}) copy-start(f32[24,2]{0,1:T(2,128)} %param.9) | copy-start | bytes 580
  85.6 15.5 %all-to-all-start.3 = ((bf16[4,16,3072]{2,1,0:T(8,128)(2,1)}), bf16[4,16,3072]{2,1,0:T(8,128)(2,1)S(1)}, u32[]{:S(2)}, u32[]{:S(2)}) async-start(bf16[4,16,3072]{2,1,0:T(8,128)(2,1)} %bitcast.9), calls=%async_computation.3 | async-start | bytes 786432 | tf_op jit(solution)/shard_map/all_to_all | solution.py:222

commit v6 on v5

v6 whole, which is shorter than its diff:
```python
import functools

import jax
import jax.numpy as jnp
from jax import lax
from jax.experimental import pallas as pl
from jax.experimental.pallas import tpu as pltpu
from jax.sharding import PartitionSpec as P

EXPERTS = 4
CAP = 16
HALVES = 2
BLOCK = 1024
FETCH_ROWS = 144
MIB = 1 << 20
LIMIT = pltpu.CompilerParams(vmem_limit_bytes=16 * MIB)
VMEM = pl.BlockSpec(memory_space=pltpu.VMEM)
ANY = pl.BlockSpec(memory_space=pl.ANY)


def choices(ids, plane):
    tokens = ids.shape[1]
    line = lax.broadcasted_iota(jnp.int32, (EXPERTS * CAP, tokens), 0)
    expert = lax.rem(line // CAP + plane, EXPERTS)
    slot = (line % CAP).astype(jnp.float32)
    first = ids[0:1, :] == expert
    second = ids[1:2, :] == expert
    named = (first | second).astype(jnp.float32)
    square = (tokens, tokens)
    earlier = lax.broadcasted_iota(jnp.int32, square, 0) < lax.broadcasted_iota(
        jnp.int32, square, 1
    )
    rank = jnp.dot(named, earlier.astype(jnp.float32), preferred_element_type=jnp.float32)
    here = rank == slot
    return first & here, second & here


def pack_kernel(group, ids_ref, act_ref, gain_ref, *out_refs):
    plane = lax.axis_index("expert") // group
    values = act_ref[...].astype(jnp.float32)
    mean_sq = jnp.mean(values * values, axis=-1, keepdims=True)
    normed = (values * lax.rsqrt(mean_sq + 1e-06) * gain_ref[...]).astype(jnp.bfloat16)
    first, second = choices(ids_ref[...], plane)
    pick = (first | second).astype(jnp.float32).astype(jnp.bfloat16)
    rows = jnp.dot(pick, normed, preferred_element_type=jnp.float32).astype(jnp.bfloat16)
    for s, out_ref in zip((0, 1, 3), out_refs):
        out_ref[...] = rows[s * CAP : (s + 1) * CAP]
    part = out_refs[-1].shape[1]
    for k, out_ref in enumerate(out_refs[3:]):
        out_ref[...] = rows[2 * CAP : 3 * CAP, k * part : (k + 1) * part]


def pack(group, ids, activations, gain):
    width = activations.shape[1]
    widths = [width] * 3 + [width // HALVES] * HALVES
    return pl.pallas_call(
        functools.partial(pack_kernel, group),
        out_shape=[jax.ShapeDtypeStruct((CAP, n), jnp.bfloat16) for n in widths],
        compiler_params=LIMIT,
        name="norm_and_pack",
    )(ids, activations, gain.reshape(1, width))


def fetches(weights, at, held, sems):
    copies = []
    for j, w in enumerate(weights):
        part = held[j].shape[1]
        for b in range(sems.shape[1]):
            rows = pl.ds(b * FETCH_ROWS, FETCH_ROWS)
            copies.append(
                pltpu.make_async_copy(w.at[rows, at : at + part], held[j].at[rows], sems.at[j, b])
            )
    return copies


def fetch_kernel(at, w_ref, after_ref, held_ref, sems):
    copies = fetches([w_ref], at, [held_ref], sems)
    for copy in copies:
        copy.start()
    for copy in copies:
        copy.wait()


def fetch(w, at, part, after):
    rows = w.shape[0]
    return pl.pallas_call(
        functools.partial(fetch_kernel, at),
        in_specs=[ANY, ANY],
        out_specs=VMEM,
        out_shape=pltpu.VMEM((rows, part), jnp.bfloat16),
        scratch_shapes=[pltpu.SemaphoreType.DMA((1, rows // FETCH_ROWS))],
        compiler_params=LIMIT,
        cost_estimate=pl.CostEstimate(flops=0, bytes_accessed=4 * rows * part, transcendentals=0),
        name="fetch",
    )(pltpu.with_memory_space_constraint(w, pltpu.HBM), after)


def gate_up_kernel(count, ahead, at, begin, end, *refs):
    pieces, refs = refs[:count], refs[count:]
    weights, later, refs = refs[:2], refs[2 : 2 + ahead], refs[2 + ahead :]
    if not begin:
        before, refs = refs[:2], refs[2:]
    held, refs = refs[:ahead], refs[ahead:]
    turned, sems, refs = *refs[-2:], refs[:-2]
    if end:
        hidden_ref, refs = refs[0], refs[1:]
    sums = refs
    steps, block, _ = turned.shape
    copies = fetches(later, 0 if end else steps * block, held, sems)
    for copy in copies:
        copy.start()

    @pl.loop(0, steps)
    def _(c):
        parts = []
        for p in pieces:
            first = at if p.shape[1] > steps * block else 0
            parts.append(p[:, pl.ds(pl.multiple_of(first + c * block, block), block)])
        turned[c] = jnp.concatenate(parts, axis=0).T

    for j in range(2):
        sums[j][...] = jnp.zeros_like(sums[j]) if begin else before[j][...]

    @pl.loop(0, steps)
    def _(c):
        columns = pl.ds(pl.multiple_of(c * block, block), block)
        for j in range(2):
            sums[j][...] += jnp.dot(
                weights[j][:, columns], turned[c], preferred_element_type=jnp.float32
            )

    if end:
        hidden = (jax.nn.silu(sums[0][...]) * sums[1][...]).astype(jnp.bfloat16)
        hidden_ref[...] = hidden.T
    for copy in copies:
        copy.wait()


def gate_up(k, pieces, weights, later, totals):
    hidden, part = weights[0].shape
    begin, end = k == 0, k == HALVES - 1
    rows = sum(p.shape[0] for p in pieces)
    total = jax.ShapeDtypeStruct((hidden, rows), jnp.float32)
    width = later[0].shape[1] if end else part
    out_shape = [pltpu.VMEM((hidden, width), jnp.bfloat16)] * len(later)
    out_specs = [VMEM] * len(later)
    scratch = []
    if end:
        out_shape.append(jax.ShapeDtypeStruct((rows, hidden), jnp.bfloat16))
        scratch += [pltpu.VMEM((hidden, rows), jnp.float32)] * 2
    else:
        out_shape += [total] * 2
    out_specs += [VMEM] * (len(out_shape) - len(later))
    scratch.append(pltpu.VMEM((part // BLOCK, BLOCK, rows), jnp.bfloat16))
    scratch.append(pltpu.SemaphoreType.DMA((len(later), hidden // FETCH_ROWS)))
    weights = [pltpu.with_memory_space_constraint(w, pltpu.VMEM) for w in weights]
    later = [pltpu.with_memory_space_constraint(w, pltpu.HBM) for w in later]
    out = pl.pallas_call(
        functools.partial(gate_up_kernel, len(pieces), len(later), k * part, begin, end),
        in_specs=[VMEM] * (len(pieces) + 2) + [ANY] * len(later) + [VMEM] * len(totals),
        out_specs=out_specs,
        out_shape=out_shape,
        scratch_shapes=scratch,
        compiler_params=LIMIT,
        cost_estimate=pl.CostEstimate(
            flops=4 * rows * hidden * part,
            bytes_accessed=4 * hidden * part + 8 * rows * hidden,
            transcendentals=0,
        ),
        name="gate_up",
    )(*pieces, *weights, *later, *totals)
    return out[: len(later)], out[len(later) :]


def down_kernel(at, hidden_ref, w_ref, keep_ref, send_ref):
    half, part = keep_ref.shape
    first = 3 * half // 4
    block = BLOCK // 2

    @pl.loop(0, part // block)
    def _(c):
        columns = pl.ds(pl.multiple_of(at + c * block, block), block)
        out = jnp.dot(hidden_ref[...], w_ref[:, columns], preferred_element_type=jnp.float32)
        out = out.astype(jnp.bfloat16)
        columns = pl.ds(pl.multiple_of(c * block, block), block)
        for j, ref in enumerate((keep_ref, send_ref)):
            ref[:first, columns] = out[j * first : (j + 1) * first]
            far_rows = out[2 * first :]
            ref[first:, columns] = far_rows[j * (half - first) : (j + 1) * (half - first)]


def down(at, part, hidden, w_down):
    rows, depth = hidden.shape
    return pl.pallas_call(
        functools.partial(down_kernel, at),
        in_specs=[VMEM, VMEM],
        out_shape=[jax.ShapeDtypeStruct((rows // 2, part), jnp.bfloat16)] * 2,
        compiler_params=LIMIT,
        cost_estimate=pl.CostEstimate(
            flops=2 * rows * depth * part,
            bytes_accessed=2 * (depth * part + rows * depth + rows * part),
            transcendentals=0,
        ),
        name="down",
    )(hidden, pltpu.with_memory_space_constraint(w_down, pltpu.VMEM))


def mix_kernel(group, ids_ref, logits_ref, act_ref, arrived, near, last, *refs):
    out_ref, kept, middle_rows = refs[-1], refs[:HALVES], refs[HALVES:-1]
    plane = lax.axis_index("expert") // group
    first, second = choices(ids_ref[...], plane)
    lead = logits_ref[0:1, :] - logits_ref[1:2, :]
    weight = jnp.where(first, jax.nn.sigmoid(lead), 0.0)
    weight = (weight + jnp.where(second, jax.nn.sigmoid(-lead), 0.0)).T
    high = weight.astype(jnp.bfloat16)
    rest = weight - high.astype(jnp.float32)
    middle = rest.astype(jnp.bfloat16)
    low = (rest - middle.astype(jnp.float32)).astype(jnp.bfloat16)
    part = kept[0].shape[1]
    for k in range(HALVES):
        columns = slice(k * part, (k + 1) * part)
        own = kept[k][...].astype(jnp.float32) + arrived[:, columns].astype(jnp.float32)
        blocks = [own.astype(jnp.bfloat16), near[:, columns], middle_rows[k][...]]
        rows = jnp.concatenate(blocks + [last[:, columns]], axis=0)
        total = act_ref[:, columns].astype(jnp.float32)
        for term in (low, middle, high):
            total = total + jnp.dot(term, rows, preferred_element_type=jnp.float32)
        out_ref[:, columns] = total.astype(jnp.bfloat16)


def mix(group, ids, logits, activations, pieces):
    return pl.pallas_call(
        functools.partial(mix_kernel, group),
        out_shape=jax.ShapeDtypeStruct(activations.shape, jnp.bfloat16),
        compiler_params=LIMIT,
        name="mix",
    )(ids, logits, activations, *pieces)


def added(mine, arrived):
    total = mine.astype(jnp.float32) + arrived.astype(jnp.float32)
    return total.astype(jnp.bfloat16)


def on_device(activations, expert_ids, route_logits, norm_gain, w_gate, w_up, w_down):
    devices = lax.axis_size("expert")
    group = devices // EXPERTS
    far = group // 2
    width = activations.shape[1]
    part = width // HALVES

    def shift(x, s):
        return lax.ppermute(
            x, "expert", [(i, (i + s * group) % devices) for i in range(devices)]
        )

    def swap(x, bit):
        return lax.ppermute(x, "expert", [(i, i ^ bit) for i in range(devices)])

    def after(x, *others):
        return lax.optimization_barrier((x, *others))[0]

    def spread(block):
        pieces, bit = [], far // 2
        while bit:
            pieces.append(swap(block, bit))
            block = jnp.concatenate([block, pieces[-1]], axis=0)
            bit //= 2
        return pieces

    ids = expert_ids.T
    own, *sends = pack(group, ids, activations, norm_gain)
    far_own = swap(own, far)
    arrivals = [shift(sends[0], 1), shift(sends[1], 3)]
    for j in range(HALVES):
        arrivals.append(shift(after(sends[2 + j], arrivals[j]), 2))
    now = [fetch(w_gate, 0, part, own), fetch(w_up, 0, part, arrivals[1])]
    passed = [swap(after(arrivals[0], far_own), far)]
    for j in range(1, len(arrivals)):
        passed.append(swap(after(arrivals[j], arrivals[j - 1]), far))
    head = [own, *arrivals[:2], far_own, *passed[:2]]
    head += spread(after(jnp.concatenate(head, axis=0), *now, *arrivals[2:]))
    totals = []
    for k in range(HALVES):
        tail = [arrivals[2 + k], passed[2 + k]]
        tail += spread(jnp.concatenate(tail, axis=0))
        later = [w_down] if k == HALVES - 1 else [w_gate, w_up]
        now, totals = gate_up(k, head + tail, now, later, totals)
    hidden, (down_w,) = totals[0], now
    held = []
    for k in range(HALVES):
        keep, send = down(k * part, part, hidden, down_w)
        bit = 1
        while bit < far:
            total = added(keep, swap(send, bit))
            bit *= 2
            if bit < far:
                count = total.shape[0] // 8
                groups = [total[: 3 * count], total[3 * count : 6 * count]]
                groups += [total[6 * count : 7 * count], total[7 * count :]]
                keep = jnp.concatenate(groups[0::2], axis=0)
                send = jnp.concatenate(groups[1::2], axis=0)
        held.append([total[j * CAP : (j + 1) * CAP] for j in range(2 * EXPERTS)])
    crossed = [swap(h[7], far) for h in held]
    middle = [shift(added(h[6], x), -2) for h, x in zip(held, crossed)]
    mine = [jnp.concatenate([h[j] for h in held], axis=1) for j in range(6)]
    crossed.append(swap(after(mine[4], crossed[0]), far))
    crossed.append(swap(after(mine[5], crossed[1]), far))
    near = shift(added(mine[1], crossed[2]), -1)
    last = shift(added(mine[2], crossed[3]), -3)
    arrived = swap(after(mine[3], crossed[2]), far)
    pieces = [arrived, near, last, *[h[0] for h in held], *middle]
    return mix(group, ids, route_logits.T, activations, pieces)


def solution(mesh):
    in_specs = (
        P(("parts", "expert"), None),
        P(("parts", "expert"), None),
        P(("parts", "expert"), None),
        P(),
        P("expert", None),
        P("expert", None),
        P("expert", None),
    )
    out_specs = P(("parts", "expert"), None)
    return jax.shard_map(
        on_device, mesh=mesh, in_specs=in_specs, out_specs=out_specs, check_vma=False
    )
```

time: 116 us -> 86.6 us (0.75)
  blocking collectives: 30.9 us -> 0 us
  starting transfers between devices: 11.8 us -> 33.2 us
  Pallas kernels: 34.3 us -> 24.7 us
  waiting for transfers between devices: 34.5 us -> 25.1 us
    all_to_all x2 -> x0, blocking collectives: 30.9 us -> none  [across(): lax.all_to_all(x, 'expert', split_axis=0, concat_axis=0, tiled=True, axis...]
    ppermute x0 -> x8, starting transfers between devices: none -> 19.1 us  [shift(): lax.ppermute(x, 'expert', [(i, (i + s * group) % devices) for i in range(...]
    all_to_all x2 -> x0, waiting for transfers between devices: 13.8 us -> none  [across(): lax.all_to_all(x, 'expert', split_axis=0, concat_axis=0, tiled=True, axis...]
    ppermute x8 -> x15, starting transfers between devices: 4.01 us -> 14.1 us  [swap(): return lax.ppermute(x, 'expert', [(i, i ^ bit) for i in range(devices)])]
    pallas_call x7 -> x6, Pallas kernels: 28.2 us -> 18.5 us  [the longest x2 10.4 us: gate_up(): pl.pallas_call(functools.partial(gate_up_kernel, len(pieces), len(later),...]
    ppermute x0 -> x8, waiting for transfers between devices: none -> 9.16 us  [shift(): lax.ppermute(x, 'expert', [(i, (i + s * group) % devices) for i in range(...]
    all_to_all x2 -> x0, starting transfers between devices: 7.81 us -> none  [across(): lax.all_to_all(x, 'expert', split_axis=0, concat_axis=0, tiled=True, axis...]
    ppermute x8 -> x15, waiting for transfers between devices: 20.7 us -> 15.9 us  [swap(): return lax.ppermute(x, 'expert', [(i, i ^ bit) for i in range(devices)])]
  transfers between devices with their start and end apart: 10 -> 23, of which waited for: 7 -> 8; matrix products, arithmetic and copies ran while one was open for 1% -> 1% of each run, Pallas kernels for 16% -> 17%
where the time goes in v6:
time: 86.6 us; the launch traced here: 86.4 us
  starting transfers between devices  33.2 us (38%)
  waiting for transfers between devices  25.1 us (29%)
  Pallas kernels  24.7 us (29%)
  local copies, waits for them, and re-layouts  2.58 us (3%)
    ppermute x8, starting transfers between devices, shift(): lax.ppermute(x, 'expert', [(i, (i + s * group) % devices) for i in range(...  19.1 us
    ppermute x15, waiting for transfers between devices, swap(): return lax.ppermute(x, 'expert', [(i, i ^ bit) for i in range(devices)])  15.9 us
    ppermute x15, starting transfers between devices, swap(): return lax.ppermute(x, 'expert', [(i, i ^ bit) for i in range(devices)])  14.1 us
    pallas_call x2, Pallas kernels, gate_up(): pl.pallas_call(functools.partial(gate_up_kernel, len(pieces), len(later),...  10.4 us
    ppermute x8, waiting for transfers between devices, shift(): lax.ppermute(x, 'expert', [(i, (i + s * group) % devices) for i in range(...  9.16 us
    pallas_call x2, Pallas kernels, fetch(): pl.pallas_call(functools.partial(fetch_kernel, at), in_specs=[ANY, ANY],...  6.19 us
    pallas_call x2, Pallas kernels, down(): pl.pallas_call(functools.partial(down_kernel, at), in_specs=[VMEM, VMEM],...  6.13 us
    unnamed x17, local copies, waits for them, and re-layouts  2.47 us
  transfers between devices with their start and end apart: 23, of which 8 were waited for; matrix products, arithmetic and copies ran while one was open for 1% of the time, Pallas kernels for 17%

profile of v6, /device:TPU:0, one launch (start us, length us, event | category | flops | bytes accessed | tf_op | source)
XLA Modules:
  0.0 86.4 jit_solution(11287632504670045899)
XLA Ops:
  0.0 1.0 %copy-done = bf16[24,6144]{1,0:T(8,128)(2,1)S(1)} copy-done((bf16[24,6144]{1,0:T(8,128)(2,1)S(1)}, bf16[24,6144]{1,0:T(8,128)(2,1)}, u32[]{:S(2)}) %copy-start) | copy-done | bytes 294936
  1.0 0.7 copy-done.2
  1.7 0.7 copy-done.3
  2.4 0.5 norm_and_pack.1
  2.9 3.1 %collective-permute-start = (bf16[16,6144]{1,0:T(8,128)(2,1)S(1)}, bf16[16,6144]{1,0:T(8,128)(2,1)S(1)}, u32[]{:S(2)}, u32[]{:S(2)}) collective-permute-start(bf16[16,6144]{1,0:T(8,128)(2,1)S(1)} %get-tuple-element.31), channel_id=1, source_target_pairs={{0,4},{1,5},{2,6},{3,7},{4,8},{5,9},{6,10},{7,11},{8,12},{9,13},{1... | collective-permute-start | bytes 589832 | tf_op jit(solution)/shard_map/ppermute | solution.py:253
  6.0 2.1 %collective-permute-start.1 = (bf16[16,6144]{1,0:T(8,128)(2,1)S(1)}, bf16[16,6144]{1,0:T(8,128)(2,1)S(1)}, u32[]{:S(2)}, u32[]{:S(2)}) collective-permute-start(bf16[16,6144]{1,0:T(8,128)(2,1)S(1)} %get-tuple-element.32), channel_id=1, source_target_pairs={{0,12},{1,13},{2,14},{3,15},{4,0},{5,1},{6,2},{7,3},{8,4},{9,5},{1... | collective-permute-start | bytes 589832 | tf_op jit(solution)/shard_map/ppermute | solution.py:253
  8.1 1.7 %collective-permute-start.2 = (bf16[16,6144]{1,0:T(8,128)(2,1)S(1)}, bf16[16,6144]{1,0:T(8,128)(2,1)S(1)}, u32[]{:S(2)}, u32[]{:S(2)}) collective-permute-start(bf16[16,6144]{1,0:T(8,128)(2,1)S(1)} %get-tuple-element.30.after_ref.refs_0_), channel_id=1, source_target_pairs={{0,2},{1,3},{2,0},{3,1},{4,6},{5,7},{6,4},{7,5},{8,10},{9,11},{10,... | collective-permute-start | bytes 589832 | tf_op jit(solution)/shard_map/ppermute | solution.py:258
  9.8 3.1 %fetch.2.refs_10_ = bf16[1152,3072]{1,0:T(8,128)(2,1)S(1)} custom-call(bf16[1152,6144]{1,0:T(8,128)(2,1)} %refs_12_.2, bf16[16,6144]{1,0:T(8,128)(2,1)S(1)} %get-tuple-element.30.after_ref.refs_0_), custom_call_target="tpu_custom_call" | custom-call | bytes 14155776 | tf_op jit(solution)/shard_map/fetch/pallas_call | solution.py:86
  12.9 0.9 %collective-permute-done.refs_1_ = bf16[16,6144]{1,0:T(8,128)(2,1)S(1)} collective-permute-done((bf16[16,6144]{1,0:T(8,128)(2,1)S(1)}, bf16[16,6144]{1,0:T(8,128)(2,1)S(1)}, u32[]{:S(2)}, u32[]{:S(2)}) %collective-permute-start) | collective-permute-done | bytes 196640 | tf_op jit(solution)/shard_map/ppermute | solution.py:253
  13.8 5.1 %collective-permute-start.5 = (bf16[16,3072]{1,0:T(8,128)(2,1)S(1)}, bf16[16,3072]{1,0:T(8,128)(2,1)S(1)}, u32[]{:S(2)}, u32[]{:S(2)}) collective-permute-start(bf16[16,3072]{1,0:T(8,128)(2,1)S(1)} %get-tuple-element.36), channel_id=1, source_target_pairs={{0,8},{1,9},{2,10},{3,11},{4,12},{5,13},{6,14},{7,15},{8,0},{9,1},... | collective-permute-start | bytes 294920 | tf_op jit(solution)/shard_map/ppermute | solution.py:253
  18.9 0.0 collective-permute-done.1.after_ref.refs_2_
  18.9 0.0 collective-permute-start.6
  18.9 1.5 %collective-permute-start.4 = (bf16[16,6144]{1,0:T(8,128)(2,1)S(1)}, bf16[16,6144]{1,0:T(8,128)(2,1)S(1)}, u32[]{:S(2)}, u32[]{:S(2)}) collective-permute-start(bf16[16,6144]{1,0:T(8,128)(2,1)S(1)} %collective-permute-done.1.after_ref.refs_2_), channel_id=1, source_target_pairs={{0,2},{1,3},{2,0},{3,1},{4,6},{5,7},{6,4},{7,5},{8,10},{9,11},{10,... | collective-permute-start | bytes 589832 | tf_op jit(solution)/shard_map/ppermute | solution.py:258
  20.5 0.0 collective-permute-done.2.refs_3_
  20.5 0.5 collective-permute-start.3
  21.0 3.1 %fetch.3.refs_11_ = bf16[1152,3072]{1,0:T(8,128)(2,1)S(1)} custom-call(bf16[1152,6144]{1,0:T(8,128)(2,1)} %refs_13_.1, bf16[16,6144]{1,0:T(8,128)(2,1)S(1)} %collective-permute-done.1.after_ref.refs_2_), custom_call_target="tpu_custom_call" | custom-call | bytes 14155776 | tf_op jit(solution)/shard_map/fetch/pallas_call | solution.py:86
  24.1 3.6 %collective-permute-done.3.refs_4_ = bf16[16,6144]{1,0:T(8,128)(2,1)S(1)} collective-permute-done((bf16[16,6144]{1,0:T(8,128)(2,1)S(1)}, bf16[16,6144]{1,0:T(8,128)(2,1)S(1)}, u32[]{:S(2)}, u32[]{:S(2)}) %collective-permute-start.3) | collective-permute-done | bytes 196640 | tf_op jit(solution)/shard_map/ppermute | solution.py:258
  27.8 0.0 collective-permute-done.4.refs_5_
  27.8 0.0 collective-permute-done.5.refs_7_
  27.8 0.0 collective-permute-done.6.refs_7_
  27.8 0.1 collective-permute-start.7
  27.9 1.7 %collective-permute-start.10 = (bf16[16,3072]{1,0:T(8,128)(2,1)S(1)}, bf16[16,3072]{1,0:T(8,128)(2,1)S(1)}, u32[]{:S(2)}, u32[]{:S(2)}) collective-permute-start(bf16[16,3072]{1,0:T(8,128)(2,1)S(1)} %collective-permute-done.5.refs_7_), channel_id=1, source_target_pairs={{0,2},{1,3},{2,0},{3,1},{4,6},{5,7},{6,4},{7,5},{8,10},{9,11},{10,... | collective-permute-start | bytes 294920 | tf_op jit(solution)/shard_map/ppermute | solution.py:258
  29.6 0.4 collective-permute-start.8
  30.0 3.6 %collective-permute-done.10.refs_8_ = bf16[16,3072]{1,0:T(8,128)(2,1)S(1)} collective-permute-done((bf16[16,3072]{1,0:T(8,128)(2,1)S(1)}, bf16[16,3072]{1,0:T(8,128)(2,1)S(1)}, u32[]{:S(2)}, u32[]{:S(2)}) %collective-permute-start.10) | collective-permute-done | bytes 98336 | tf_op jit(solution)/shard_map/ppermute | solution.py:258
  33.6 0.1 collective-permute-start.11
  33.7 1.6 %collective-permute-done.8.refs_8_ = bf16[16,3072]{1,0:T(8,128)(2,1)S(1)} collective-permute-done((bf16[16,3072]{1,0:T(8,128)(2,1)S(1)}, bf16[16,3072]{1,0:T(8,128)(2,1)S(1)}, u32[]{:S(2)}, u32[]{:S(2)}) %collective-permute-start.8) | collective-permute-done | bytes 98336 | tf_op jit(solution)/shard_map/ppermute | solution.py:258
  35.2 0.1 collective-permute-start.9
  35.3 0.0 collective-permute-done.11.refs_9_
  35.3 0.0 collective-permute-done.7.refs_6_
  35.3 5.2 %gate_up.2 = (bf16[1152,3072]{1,0:T(8,128)(2,1)S(1)}, bf16[1152,3072]{1,0:T(8,128)(2,1)S(1)}, f32[1152,256]{1,0:T(8,128)S(1)}, f32[1152,256]{1,0:T(8,128)S(1)}) custom-call(bf16[16,6144]{1,0:T(8,128)(2,1)S(1)} %get-tuple-element.30.after_ref.refs_0_, bf16[16,6144]{1,0:T(8,128)(2,1)S(1)} %collective-permute-done.refs_1_, ...), custom_call_target="tpu_custom_call" | custom-call | flops 3623878656 | bytes 16515072 | tf_op jit(solution)/shard_map/gate_up/pallas_call | solution.py:158
  40.5 0.0 collective-permute-done.9.refs_9_
  40.5 5.2 %gate_up.3 = (bf16[1152,6144]{1,0:T(8,128)(2,1)S(1)}, bf16[256,1152]{1,0:T(8,128)(2,1)S(1)}) custom-call(bf16[16,6144]{1,0:T(8,128)(2,1)S(1)} %get-tuple-element.30.after_ref.refs_0_, bf16[16,6144]{1,0:T(8,128)(2,1)S(1)} %collective-permute-done.refs_1_, bf16[16,6144]{1,0:T(8,128)(2,1)S(1)} %collective-permute-done.1.after_ref.refs_2_, ...), custom_call_target="tpu_custom_call" | custom-call | flops 3623878656 | bytes 16515072 | tf_op jit(solution)/shard_map/gate_up/pallas_call | solution.py:158
  45.8 3.1 %down.3 = (bf16[128,3072]{1,0:T(8,128)(2,1)S(1)}, bf16[128,3072]{1,0:T(8,128)(2,1)S(1)}) custom-call(bf16[256,1152]{1,0:T(8,128)(2,1)S(1)} %get-tuple-element.46.hidden_ref, bf16[1152,6144]{1,0:T(8,128)(2,1)S(1)} %get-tuple-element.47.w_ref), custom_call_target="tpu_custom_call" | custom-call | flops 1811939328 | bytes 9240576 | tf_op jit(solution)/shard_map/down/pallas_call | solution.py:194
  48.9 0.6 collective-permute-start.13
  49.4 3.1 %down.2 = (bf16[128,3072]{1,0:T(8,128)(2,1)S(1)}, bf16[128,3072]{1,0:T(8,128)(2,1)S(1)}) custom-call(bf16[256,1152]{1,0:T(8,128)(2,1)S(1)} %get-tuple-element.46.hidden_ref, bf16[1152,6144]{1,0:T(8,128)(2,1)S(1)} %get-tuple-element.47.w_ref), custom_call_target="tpu_custom_call" | custom-call | flops 1811939328 | bytes 9240576 | tf_op jit(solution)/shard_map/down/pallas_call | solution.py:194
  52.5 0.1 collective-permute-start.12
  52.6 0.0 collective-permute-done.13
  52.6 0.2 add_convert_fusion
  52.8 1.7 %collective-permute-start.18 = (bf16[16,3072]{1,0:T(8,128)(2,1)S(1)}, bf16[16,3072]{1,0:T(8,128)(2,1)S(1)}, u32[]{:S(2)}, u32[]{:S(2)}) collective-permute-start(bf16[16,3072]{1,0:T(8,128)(2,1)S(1)} %get-tuple-element.56), channel_id=1, source_target_pairs={{0,2},{1,3},{2,0},{3,1},{4,6},{5,7},{6,4},{7,5},{8,10},{9,11},{10,... | collective-permute-start | bytes 294920 | tf_op jit(solution)/shard_map/ppermute | solution.py:258
  54.5 0.3 collective-permute-done.12
  54.9 0.2 add_convert_fusion.1
  55.1 1.7 %collective-permute-start.14 = (bf16[16,3072]{1,0:T(8,128)(2,1)S(1)}, bf16[16,3072]{1,0:T(8,128)(2,1)S(1)}, u32[]{:S(2)}, u32[]{:S(2)}) collective-permute-start(bf16[16,3072]{1,0:T(8,128)(2,1)S(1)} %get-tuple-element.66), channel_id=1, source_target_pairs={{0,2},{1,3},{2,0},{3,1},{4,6},{5,7},{6,4},{7,5},{8,10},{9,11},{10,... | collective-permute-start | bytes 294920 | tf_op jit(solution)/shard_map/ppermute | solution.py:258
  56.8 0.0 copy-start.1
  56.8 0.0 copy-start.4
  56.9 0.0 copy-start.5
  56.9 3.3 %collective-permute-done.14 = bf16[16,3072]{1,0:T(8,128)(2,1)S(1)} collective-permute-done((bf16[16,3072]{1,0:T(8,128)(2,1)S(1)}, bf16[16,3072]{1,0:T(8,128)(2,1)S(1)}, u32[]{:S(2)}, u32[]{:S(2)}) %collective-permute-start.14) | collective-permute-done | bytes 98336 | tf_op jit(solution)/shard_map/ppermute | solution.py:258
  60.2 1.6 %collective-permute-start.15 = (bf16[16,6144]{1,0:T(8,128)(2,1)S(1)}, bf16[16,6144]{1,0:T(8,128)(2,1)S(1)}, u32[]{:S(2)}, u32[]{:S(2)}) collective-permute-start(bf16[16,6144]{1,0:T(8,128)(2,1)S(1)} %pad_maximum_fusion.3), channel_id=1, source_target_pairs={{0,2},{1,3},{2,0},{3,1},{4,6},{5,7},{6,4},{7,5},{8,10},{9,11},{10,... | collective-permute-start | bytes 589832 | tf_op jit(solution)/shard_map/ppermute | solution.py:258
  61.8 0.0 collective-permute-done.18
  61.9 1.8 %collective-permute-start.22 = (bf16[16,3072]{1,0:T(8,128)(2,1)S(1)}, bf16[16,3072]{1,0:T(8,128)(2,1)S(1)}, u32[]{:S(2)}, u32[]{:S(2)}) collective-permute-start(bf16[16,3072]{1,0:T(8,128)(2,1)S(1)} %add_convert_fusion.4), channel_id=1, source_target_pairs={{0,8},{1,9},{2,10},{3,11},{4,12},{5,13},{6,14},{7,15},{8,0},{9,1},... | collective-permute-start | bytes 294920 | tf_op jit(solution)/shard_map/ppermute | solution.py:253
  63.7 0.5 collective-permute-start.19
  64.2 3.5 %collective-permute-done.15 = bf16[16,6144]{1,0:T(8,128)(2,1)S(1)} collective-permute-done((bf16[16,6144]{1,0:T(8,128)(2,1)S(1)}, bf16[16,6144]{1,0:T(8,128)(2,1)S(1)}, u32[]{:S(2)}, u32[]{:S(2)}) %collective-permute-start.15) | collective-permute-done | bytes 196640 | tf_op jit(solution)/shard_map/ppermute | solution.py:258
  67.7 1.9 %collective-permute-start.16 = (bf16[16,6144]{1,0:T(8,128)(2,1)S(1)}, bf16[16,6144]{1,0:T(8,128)(2,1)S(1)}, u32[]{:S(2)}, u32[]{:S(2)}) collective-permute-start(bf16[16,6144]{1,0:T(8,128)(2,1)S(1)} %pad_maximum_fusion.2), channel_id=1, source_target_pairs={{0,2},{1,3},{2,0},{3,1},{4,6},{5,7},{6,4},{7,5},{8,10},{9,11},{10,... | collective-permute-start | bytes 589832 | tf_op jit(solution)/shard_map/ppermute | solution.py:258
  69.7 0.1 add_convert_fusion.3
  69.7 3.9 %collective-permute-start.17 = (bf16[16,6144]{1,0:T(8,128)(2,1)S(1)}, bf16[16,6144]{1,0:T(8,128)(2,1)S(1)}, u32[]{:S(2)}, u32[]{:S(2)}) collective-permute-start(bf16[16,6144]{1,0:T(8,128)(2,1)S(1)} %add_convert_fusion.3), channel_id=1, source_target_pairs={{0,12},{1,13},{2,14},{3,15},{4,0},{5,1},{6,2},{7,3},{8,4},{9,5},{1... | collective-permute-start | bytes 589832 | tf_op jit(solution)/shard_map/ppermute | solution.py:253
  73.7 0.0 collective-permute-done.19
  73.7 0.6 collective-permute-start.20
  74.3 2.4 %collective-permute-start.21 = (bf16[16,3072]{1,0:T(8,128)(2,1)S(1)}, bf16[16,3072]{1,0:T(8,128)(2,1)S(1)}, u32[]{:S(2)}, u32[]{:S(2)}) collective-permute-start(bf16[16,3072]{1,0:T(8,128)(2,1)S(1)} %add_convert_fusion.5), channel_id=1, source_target_pairs={{0,8},{1,9},{2,10},{3,11},{4,12},{5,13},{6,14},{7,15},{8,0},{9,1},... | collective-permute-start | bytes 294920 | tf_op jit(solution)/shard_map/ppermute | solution.py:253
  76.8 0.0 collective-permute-done.22.refs_3_
  76.8 8.2 %collective-permute-done.21.refs_2_ = bf16[16,3072]{1,0:T(8,128)(2,1)S(1)} collective-permute-done((bf16[16,3072]{1,0:T(8,128)(2,1)S(1)}, bf16[16,3072]{1,0:T(8,128)(2,1)S(1)}, u32[]{:S(2)}, u32[]{:S(2)}) %collective-permute-start.21) | collective-permute-done | bytes 98336 | tf_op jit(solution)/shard_map/ppermute | solution.py:253
  85.0 0.0 collective-permute-done.16.arrived
  85.0 0.0 collective-permute-done.17.near
  85.0 0.0 collective-permute-done.20.last
  85.0 0.0 copy-done.1
  85.0 1.4 %mix.1 = bf16[24,6144]{1,0:T(8,128)(2,1)} custom-call(s32[2,24]{1,0:T(2,128)S(1)} %bitcast.5, f32[2,24]{1,0:T(2,128)S(1)} %bitcast.6, bf16[24,6144]{1,0:T(8,128)(2,1)S(1)} %copy-done.1, bf16[16,6144]{1,0:T(8,128)(2,1)S(1)} %collective-permute-done.16.arrived, bf16[16,6144]{1,0:T(8,128)(2,1)S(1)} %collective-permute-done.17.near, ...), custom_call_target="tpu_custom_call" | custom-call | tf_op jit(solution)/shard_map/mix/pallas_call | solution.py:232
  (21 shorter events, 0.4 us)
Async XLA Ops:
  0.0 1.0 %copy-start = (bf16[24,6144]{1,0:T(8,128)(2,1)S(1)}, bf16[24,6144]{1,0:T(8,128)(2,1)}, u32[]{:S(2)}) copy-start(bf16[24,6144]{1,0:T(8,128)(2,1)} %act_ref.3) | copy-start | bytes 884740
  1.0 0.7 copy-start.2
  1.7 0.7 copy-start.3
  2.9 10.9 %collective-permute-start = (bf16[16,6144]{1,0:T(8,128)(2,1)S(1)}, bf16[16,6144]{1,0:T(8,128)(2,1)S(1)}, u32[]{:S(2)}, u32[]{:S(2)}) collective-permute-start(bf16[16,6144]{1,0:T(8,128)(2,1)S(1)} %get-tuple-element.31), channel_id=1, source_target_pairs={{0,4},{1,5},{2,6},{3,7},{4,8},{5,9},{6,10},{7,11},{8,12},{9,13},{1... | collective-permute-start | bytes 589832 | tf_op jit(solution)/shard_map/ppermute | solution.py:253
  6.0 12.9 %collective-permute-start.1 = (bf16[16,6144]{1,0:T(8,128)(2,1)S(1)}, bf16[16,6144]{1,0:T(8,128)(2,1)S(1)}, u32[]{:S(2)}, u32[]{:S(2)}) collective-permute-start(bf16[16,6144]{1,0:T(8,128)(2,1)S(1)} %get-tuple-element.32), channel_id=1, source_target_pairs={{0,12},{1,13},{2,14},{3,15},{4,0},{5,1},{6,2},{7,3},{8,4},{9,5},{1... | collective-permute-start | bytes 589832 | tf_op jit(solution)/shard_map/ppermute | solution.py:253
  8.1 12.4 %collective-permute-start.2 = (bf16[16,6144]{1,0:T(8,128)(2,1)S(1)}, bf16[16,6144]{1,0:T(8,128)(2,1)S(1)}, u32[]{:S(2)}, u32[]{:S(2)}) collective-permute-start(bf16[16,6144]{1,0:T(8,128)(2,1)S(1)} %get-tuple-element.30.after_ref.refs_0_), channel_id=1, source_target_pairs={{0,2},{1,3},{2,0},{3,1},{4,6},{5,7},{6,4},{7,5},{8,10},{9,11},{10,... | collective-permute-start | bytes 589832 | tf_op jit(solution)/shard_map/ppermute | solution.py:258
  13.8 14.0 %collective-permute-start.5 = (bf16[16,3072]{1,0:T(8,128)(2,1)S(1)}, bf16[16,3072]{1,0:T(8,128)(2,1)S(1)}, u32[]{:S(2)}, u32[]{:S(2)}) collective-permute-start(bf16[16,3072]{1,0:T(8,128)(2,1)S(1)} %get-tuple-element.36), channel_id=1, source_target_pairs={{0,8},{1,9},{2,10},{3,11},{4,12},{5,13},{6,14},{7,15},{8,0},{9,1},... | collective-permute-start | bytes 294920 | tf_op jit(solution)/shard_map/ppermute | solution.py:253
  18.9 8.9 %collective-permute-start.6 = (bf16[16,3072]{1,0:T(8,128)(2,1)S(1)}, bf16[16,3072]{1,0:T(8,128)(2,1)S(1)}, u32[]{:S(2)}, u32[]{:S(2)}) collective-permute-start(bf16[16,3072]{1,0:T(8,128)(2,1)S(1)} %get-tuple-element.38), channel_id=1, source_target_pairs={{0,8},{1,9},{2,10},{3,11},{4,12},{5,13},{6,14},{7,15},{8,0},{9,1},... | collective-permute-start | bytes 294920 | tf_op jit(solution)/shard_map/ppermute | solution.py:253
  18.9 8.8 %collective-permute-start.4 = (bf16[16,6144]{1,0:T(8,128)(2,1)S(1)}, bf16[16,6144]{1,0:T(8,128)(2,1)S(1)}, u32[]{:S(2)}, u32[]{:S(2)}) collective-permute-start(bf16[16,6144]{1,0:T(8,128)(2,1)S(1)} %collective-permute-done.1.after_ref.refs_2_), channel_id=1, source_target_pairs={{0,2},{1,3},{2,0},{3,1},{4,6},{5,7},{6,4},{7,5},{8,10},{9,11},{10,... | collective-permute-start | bytes 589832 | tf_op jit(solution)/shard_map/ppermute | solution.py:258
  20.5 7.3 %collective-permute-start.3 = (bf16[16,6144]{1,0:T(8,128)(2,1)S(1)}, bf16[16,6144]{1,0:T(8,128)(2,1)S(1)}, u32[]{:S(2)}, u32[]{:S(2)}) collective-permute-start(bf16[16,6144]{1,0:T(8,128)(2,1)S(1)} %collective-permute-done.refs_1_), channel_id=1, source_target_pairs={{0,2},{1,3},{2,0},{3,1},{4,6},{5,7},{6,4},{7,5},{8,10},{9,11},{10,... | collective-permute-start | bytes 589832 | tf_op jit(solution)/shard_map/ppermute | solution.py:258
  27.8 7.5 %collective-permute-start.7 = (bf16[96,6144]{1,0:T(8,128)(2,1)S(1)}, bf16[96,6144]{1,0:T(8,128)(2,1)S(1)}, u32[]{:S(2)}, u32[]{:S(2)}) collective-permute-start(bf16[96,6144]{1,0:T(8,128)(2,1)S(1)} %constant_dynamic-update-slice_fusion), channel_id=1, source_target_pairs={{0,1},{1,0},{2,3},{3,2},{4,5},{5,4},{6,7},{7,6},{8,9},{9,8},{10,11... | collective-permute-start | bytes 3538952 | tf_op jit(solution)/shard_map/ppermute | solution.py:258
  27.9 5.7 %collective-permute-start.10 = (bf16[16,3072]{1,0:T(8,128)(2,1)S(1)}, bf16[16,3072]{1,0:T(8,128)(2,1)S(1)}, u32[]{:S(2)}, u32[]{:S(2)}) collective-permute-start(bf16[16,3072]{1,0:T(8,128)(2,1)S(1)} %collective-permute-done.5.refs_7_), channel_id=1, source_target_pairs={{0,2},{1,3},{2,0},{3,1},{4,6},{5,7},{6,4},{7,5},{8,10},{9,11},{10,... | collective-permute-start | bytes 294920 | tf_op jit(solution)/shard_map/ppermute | solution.py:258
  29.6 5.6 %collective-permute-start.8 = (bf16[16,3072]{1,0:T(8,128)(2,1)S(1)}, bf16[16,3072]{1,0:T(8,128)(2,1)S(1)}, u32[]{:S(2)}, u32[]{:S(2)}) collective-permute-start(bf16[16,3072]{1,0:T(8,128)(2,1)S(1)} %collective-permute-done.6.refs_7_), channel_id=1, source_target_pairs={{0,2},{1,3},{2,0},{3,1},{4,6},{5,7},{6,4},{7,5},{8,10},{9,11},{10,... | collective-permute-start | bytes 294920 | tf_op jit(solution)/shard_map/ppermute | solution.py:258
  33.6 1.7 %collective-permute-start.11 = (bf16[32,3072]{1,0:T(8,128)(2,1)S(1)}, bf16[32,3072]{1,0:T(8,128)(2,1)S(1)}, u32[]{:S(2)}, u32[]{:S(2)}) collective-permute-start(bf16[32,3072]{1,0:T(8,128)(2,1)S(1)} %pad_maximum_fusion.1), channel_id=1, source_target_pairs={{0,1},{1,0},{2,3},{3,2},{4,5},{5,4},{6,7},{7,6},{8,9},{9,8},{10,11... | collective-permute-start | bytes 589832 | tf_op jit(solution)/shard_map/ppermute | solution.py:258
  35.2 5.3 %collective-permute-start.9 = (bf16[32,3072]{1,0:T(8,128)(2,1)S(1)}, bf16[32,3072]{1,0:T(8,128)(2,1)S(1)}, u32[]{:S(2)}, u32[]{:S(2)}) collective-permute-start(bf16[32,3072]{1,0:T(8,128)(2,1)S(1)} %pad_maximum_fusion), channel_id=1, source_target_pairs={{0,1},{1,0},{2,3},{3,2},{4,5},{5,4},{6,7},{7,6},{8,9},{9,8},{10,11... | collective-permute-start | bytes 589832 | tf_op jit(solution)/shard_map/ppermute | solution.py:258
  48.9 3.7 %collective-permute-start.13 = (bf16[128,3072]{1,0:T(8,128)(2,1)S(1)}, bf16[128,3072]{1,0:T(8,128)(2,1)S(1)}, u32[]{:S(2)}, u32[]{:S(2)}) collective-permute-start(bf16[128,3072]{1,0:T(8,128)(2,1)S(1)} %get-tuple-element.51), channel_id=1, source_target_pairs={{0,1},{1,0},{2,3},{3,2},{4,5},{5,4},{6,7},{7,6},{8,9},{9,8},{10,11... | collective-permute-start | bytes 2359304 | tf_op jit(solution)/shard_map/ppermute | solution.py:258
  52.5 2.4 %collective-permute-start.12 = (bf16[128,3072]{1,0:T(8,128)(2,1)S(1)}, bf16[128,3072]{1,0:T(8,128)(2,1)S(1)}, u32[]{:S(2)}, u32[]{:S(2)}) collective-permute-start(bf16[128,3072]{1,0:T(8,128)(2,1)S(1)} %get-tuple-element.49), channel_id=1, source_target_pairs={{0,1},{1,0},{2,3},{3,2},{4,5},{5,4},{6,7},{7,6},{8,9},{9,8},{10,11... | collective-permute-start | bytes 2359304 | tf_op jit(solution)/shard_map/ppermute | solution.py:258
  52.8 9.0 %collective-permute-start.18 = (bf16[16,3072]{1,0:T(8,128)(2,1)S(1)}, bf16[16,3072]{1,0:T(8,128)(2,1)S(1)}, u32[]{:S(2)}, u32[]{:S(2)}) collective-permute-start(bf16[16,3072]{1,0:T(8,128)(2,1)S(1)} %get-tuple-element.56), channel_id=1, source_target_pairs={{0,2},{1,3},{2,0},{3,1},{4,6},{5,7},{6,4},{7,5},{8,10},{9,11},{10,... | collective-permute-start | bytes 294920 | tf_op jit(solution)/shard_map/ppermute | solution.py:258
  55.1 5.1 %collective-permute-start.14 = (bf16[16,3072]{1,0:T(8,128)(2,1)S(1)}, bf16[16,3072]{1,0:T(8,128)(2,1)S(1)}, u32[]{:S(2)}, u32[]{:S(2)}) collective-permute-start(bf16[16,3072]{1,0:T(8,128)(2,1)S(1)} %get-tuple-element.66), channel_id=1, source_target_pairs={{0,2},{1,3},{2,0},{3,1},{4,6},{5,7},{6,4},{7,5},{8,10},{9,11},{10,... | collective-permute-start | bytes 294920 | tf_op jit(solution)/shard_map/ppermute | solution.py:258
  56.8 28.2 %copy-start.1 = (bf16[24,6144]{1,0:T(8,128)(2,1)S(1)}, bf16[24,6144]{1,0:T(8,128)(2,1)}, u32[]{:S(2)}) copy-start(bf16[24,6144]{1,0:T(8,128)(2,1)} %act_ref.3) | copy-start | bytes 884740
  56.8 28.2 %copy-start.4 = (s32[24,2]{0,1:T(2,128)S(1)}, s32[24,2]{0,1:T(2,128)}, u32[]{:S(2)}) copy-start(s32[24,2]{0,1:T(2,128)} %param.8) | copy-start | bytes 580
  56.9 28.2 %copy-start.5 = (f32[24,2]{0,1:T(2,128)S(1)}, f32[24,2]{0,1:T(2,128)}, u32[]{:S(2)}) copy-start(f32[24,2]{0,1:T(2,128)} %param.9) | copy-start | bytes 580
  60.2 7.5 %collective-permute-start.15 = (bf16[16,6144]{1,0:T(8,128)(2,1)S(1)}, bf16[16,6144]{1,0:T(8,128)(2,1)S(1)}, u32[]{:S(2)}, u32[]{:S(2)}) collective-permute-start(bf16[16,6144]{1,0:T(8,128)(2,1)S(1)} %pad_maximum_fusion.3), channel_id=1, source_target_pairs={{0,2},{1,3},{2,0},{3,1},{4,6},{5,7},{6,4},{7,5},{8,10},{9,11},{10,... | collective-permute-start | bytes 589832 | tf_op jit(solution)/shard_map/ppermute | solution.py:258
  61.9 14.9 %collective-permute-start.22 = (bf16[16,3072]{1,0:T(8,128)(2,1)S(1)}, bf16[16,3072]{1,0:T(8,128)(2,1)S(1)}, u32[]{:S(2)}, u32[]{:S(2)}) collective-permute-start(bf16[16,3072]{1,0:T(8,128)(2,1)S(1)} %add_convert_fusion.4), channel_id=1, source_target_pairs={{0,8},{1,9},{2,10},{3,11},{4,12},{5,13},{6,14},{7,15},{8,0},{9,1},... | collective-permute-start | bytes 294920 | tf_op jit(solution)/shard_map/ppermute | solution.py:253
  63.7 10.0 %collective-permute-start.19 = (bf16[16,6144]{1,0:T(8,128)(2,1)S(1)}, bf16[16,6144]{1,0:T(8,128)(2,1)S(1)}, u32[]{:S(2)}, u32[]{:S(2)}) collective-permute-start(bf16[16,6144]{1,0:T(8,128)(2,1)S(1)} %pad_maximum_fusion.4), channel_id=1, source_target_pairs={{0,2},{1,3},{2,0},{3,1},{4,6},{5,7},{6,4},{7,5},{8,10},{9,11},{10,... | collective-permute-start | bytes 589832 | tf_op jit(solution)/shard_map/ppermute | solution.py:258
  67.7 17.3 %collective-permute-start.16 = (bf16[16,6144]{1,0:T(8,128)(2,1)S(1)}, bf16[16,6144]{1,0:T(8,128)(2,1)S(1)}, u32[]{:S(2)}, u32[]{:S(2)}) collective-permute-start(bf16[16,6144]{1,0:T(8,128)(2,1)S(1)} %pad_maximum_fusion.2), channel_id=1, source_target_pairs={{0,2},{1,3},{2,0},{3,1},{4,6},{5,7},{6,4},{7,5},{8,10},{9,11},{10,... | collective-permute-start | bytes 589832 | tf_op jit(solution)/shard_map/ppermute | solution.py:258
  69.7 15.3 %collective-permute-start.17 = (bf16[16,6144]{1,0:T(8,128)(2,1)S(1)}, bf16[16,6144]{1,0:T(8,128)(2,1)S(1)}, u32[]{:S(2)}, u32[]{:S(2)}) collective-permute-start(bf16[16,6144]{1,0:T(8,128)(2,1)S(1)} %add_convert_fusion.3), channel_id=1, source_target_pairs={{0,12},{1,13},{2,14},{3,15},{4,0},{5,1},{6,2},{7,3},{8,4},{9,5},{1... | collective-permute-start | bytes 589832 | tf_op jit(solution)/shard_map/ppermute | solution.py:253
  73.7 11.3 %collective-permute-start.20 = (bf16[16,6144]{1,0:T(8,128)(2,1)S(1)}, bf16[16,6144]{1,0:T(8,128)(2,1)S(1)}, u32[]{:S(2)}, u32[]{:S(2)}) collective-permute-start(bf16[16,6144]{1,0:T(8,128)(2,1)S(1)} %add_convert_fusion.2), channel_id=1, source_target_pairs={{0,4},{1,5},{2,6},{3,7},{4,8},{5,9},{6,10},{7,11},{8,12},{9,13},{1... | collective-permute-start | bytes 589832 | tf_op jit(solution)/shard_map/ppermute | solution.py:253
  74.3 10.7 %collective-permute-start.21 = (bf16[16,3072]{1,0:T(8,128)(2,1)S(1)}, bf16[16,3072]{1,0:T(8,128)(2,1)S(1)}, u32[]{:S(2)}, u32[]{:S(2)}) collective-permute-start(bf16[16,3072]{1,0:T(8,128)(2,1)S(1)} %add_convert_fusion.5), channel_id=1, source_target_pairs={{0,8},{1,9},{2,10},{3,11},{4,12},{5,13},{6,14},{7,15},{8,0},{9,1},... | collective-permute-start | bytes 294920 | tf_op jit(solution)/shard_map/ppermute | solution.py:253

commit v7 on v6

--- a/solution.py
+++ b/solution.py
@@ -53,12 +53,16 @@
 def pack(group, ids, activations, gain):
     width = activations.shape[1]
     widths = [width] * 3 + [width // HALVES] * HALVES
+    operands = [ids, activations, gain.reshape(1, width)]
     return pl.pallas_call(
         functools.partial(pack_kernel, group),
+        grid=(1,),
+        in_specs=[pl.BlockSpec(x.shape, lambda i: (0, 0)) for x in operands],
+        out_specs=[pl.BlockSpec((CAP, n), lambda i: (0, 0)) for n in widths],
         out_shape=[jax.ShapeDtypeStruct((CAP, n), jnp.bfloat16) for n in widths],
         compiler_params=LIMIT,
         name="norm_and_pack",
-    )(ids, activations, gain.reshape(1, width))
+    )(*[pltpu.with_memory_space_constraint(x, pltpu.HBM) for x in operands])
 
 
 def fetches(weights, at, held, sems):
@@ -272,14 +276,14 @@
     own, *sends = pack(group, ids, activations, norm_gain)
     far_own = swap(own, far)
     arrivals = [shift(sends[0], 1), shift(sends[1], 3)]
+    now = [fetch(w_gate, 0, part, own), fetch(w_up, 0, part, own)]
     for j in range(HALVES):
-        arrivals.append(shift(after(sends[2 + j], arrivals[j]), 2))
-    now = [fetch(w_gate, 0, part, own), fetch(w_up, 0, part, arrivals[1])]
-    passed = [swap(after(arrivals[0], far_own), far)]
-    for j in range(1, len(arrivals)):
+        arrivals.append(shift(after(sends[2 + j], arrivals[1], now[1]), 2))
+    passed = [swap(after(arrivals[0], far_own), far), swap(arrivals[1], far)]
+    for j in range(2, len(arrivals)):
         passed.append(swap(after(arrivals[j], arrivals[j - 1]), far))
     head = [own, *arrivals[:2], far_own, *passed[:2]]
-    head += spread(after(jnp.concatenate(head, axis=0), *now, *arrivals[2:]))
+    head += spread(after(jnp.concatenate(head, axis=0), *now, passed[2], arrivals[3]))
     totals = []
     for k in range(HALVES):
         tail = [arrivals[2 + k], passed[2 + k]]
@@ -304,9 +308,9 @@
     crossed = [swap(h[7], far) for h in held]
     middle = [shift(added(h[6], x), -2) for h, x in zip(held, crossed)]
     mine = [jnp.concatenate([h[j] for h in held], axis=1) for j in range(6)]
-    crossed.append(swap(after(mine[4], crossed[0]), far))
-    crossed.append(swap(after(mine[5], crossed[1]), far))
-    near = shift(added(mine[1], crossed[2]), -1)
+    crossed.append(swap(mine[4], far))
+    crossed.append(swap(mine[5], far))
+    near = shift(after(added(mine[1], crossed[2]), crossed[1]), -1)
     last = shift(added(mine[2], crossed[3]), -3)
     arrived = swap(after(mine[3], crossed[2]), far)
     pieces = [arrived, near, last, *[h[0] for h in held], *middle]

time: 86.6 us -> 81.9 us (0.946)
  starting transfers between devices: 33.2 us -> 26.6 us
  waiting for transfers between devices: 25.1 us -> 28.4 us
  local copies, waits for them, and re-layouts: 2.58 us -> 0.2 us
  Pallas kernels: 24.7 us -> 25.6 us
    ppermute x8, starting transfers between devices: 19.1 us -> 12.2 us  [shift(): lax.ppermute(x, 'expert', [(i, (i + s * group) % devices) for i in range(...]
    ppermute x8, waiting for transfers between devices: 9.16 us -> 14.5 us  [shift(): lax.ppermute(x, 'expert', [(i, (i + s * group) % devices) for i in range(...]
    unnamed x17 -> x11, local copies, waits for them, and re-layouts: 2.47 us -> 0.09 us
    ppermute x15, waiting for transfers between devices: 15.9 us -> 13.9 us  [swap(): return lax.ppermute(x, 'expert', [(i, i ^ bit) for i in range(devices)])]
    pallas_call x1, Pallas kernels: 0.52 us -> 1.48 us  [pack(): pl.pallas_call(functools.partial(pack_kernel, group), grid=(1,), in_specs...]
  transfers between devices with their start and end apart: 23 -> 23, of which waited for: 8 -> 8; matrix products, arithmetic and copies ran while one was open for 1% -> 1% of each run, Pallas kernels for 17% -> 18%
where the time goes in v7:
time: 81.9 us; the launch traced here: 81.7 us
  waiting for transfers between devices  28.4 us (35%)
  starting transfers between devices  26.6 us (32%)
  Pallas kernels  25.6 us (31%)
    ppermute x8, waiting for transfers between devices, shift(): lax.ppermute(x, 'expert', [(i, (i + s * group) % devices) for i in range(...  14.5 us
    ppermute x15, starting transfers between devices, swap(): return lax.ppermute(x, 'expert', [(i, i ^ bit) for i in range(devices)])  14.5 us
    ppermute x15, waiting for transfers between devices, swap(): return lax.ppermute(x, 'expert', [(i, i ^ bit) for i in range(devices)])  13.9 us
    ppermute x8, starting transfers between devices, shift(): lax.ppermute(x, 'expert', [(i, (i + s * group) % devices) for i in range(...  12.2 us
    pallas_call x2, Pallas kernels, gate_up(): pl.pallas_call(functools.partial(gate_up_kernel, len(pieces), len(later),...  10.4 us
    pallas_call x2, Pallas kernels, fetch(): pl.pallas_call(functools.partial(fetch_kernel, at), in_specs=[ANY, ANY],...  6.19 us
    pallas_call x2, Pallas kernels, down(): pl.pallas_call(functools.partial(down_kernel, at), in_specs=[VMEM, VMEM],...  6.13 us
  transfers between devices with their start and end apart: 23, of which 8 were waited for; matrix products, arithmetic and copies ran while one was open for 1% of the time, Pallas kernels for 18%

profile of v7, /device:TPU:0, one launch (start us, length us, event | category | flops | bytes accessed | tf_op | source)
XLA Modules:
  0.0 81.7 jit_solution(13296285605857594184)
XLA Ops:
  0.0 1.5 %norm_and_pack.1 = (bf16[16,6144]{1,0:T(8,128)(2,1)S(1)}, bf16[16,6144]{1,0:T(8,128)(2,1)S(1)}, bf16[16,6144]{1,0:T(8,128)(2,1)S(1)}, bf16[16,3072]{1,0:T(8,128)(2,1)S(1)}, bf16[16,3072]{1,0:T(8,128)(2,1)S(1)}) custom-call(s32[2,24]{1,0:T(2,128)} %bitcast.3, bf16[24,6144]{1,0:T(8,128)(2,1)} %act_ref.3, f32[1,6144]{1,0:T(1,128)} %bitcast.6), custom_call_target="tpu_custom_call" | custom-call | tf_op jit(solution)/shard_map/norm_and_pack/pallas_call | solution.py:57
  1.5 3.1 %collective-permute-start = (bf16[16,6144]{1,0:T(8,128)(2,1)S(1)}, bf16[16,6144]{1,0:T(8,128)(2,1)S(1)}, u32[]{:S(2)}, u32[]{:S(2)}) collective-permute-start(bf16[16,6144]{1,0:T(8,128)(2,1)S(1)} %get-tuple-element.29), channel_id=1, source_target_pairs={{0,4},{1,5},{2,6},{3,7},{4,8},{5,9},{6,10},{7,11},{8,12},{9,13},{1... | collective-permute-start | bytes 589832 | tf_op jit(solution)/shard_map/ppermute | solution.py:257
  4.6 2.1 %collective-permute-start.1 = (bf16[16,6144]{1,0:T(8,128)(2,1)S(1)}, bf16[16,6144]{1,0:T(8,128)(2,1)S(1)}, u32[]{:S(2)}, u32[]{:S(2)}) collective-permute-start(bf16[16,6144]{1,0:T(8,128)(2,1)S(1)} %get-tuple-element.30), channel_id=1, source_target_pairs={{0,12},{1,13},{2,14},{3,15},{4,0},{5,1},{6,2},{7,3},{8,4},{9,5},{1... | collective-permute-start | bytes 589832 | tf_op jit(solution)/shard_map/ppermute | solution.py:257
  6.7 1.7 %collective-permute-start.2 = (bf16[16,6144]{1,0:T(8,128)(2,1)S(1)}, bf16[16,6144]{1,0:T(8,128)(2,1)S(1)}, u32[]{:S(2)}, u32[]{:S(2)}) collective-permute-start(bf16[16,6144]{1,0:T(8,128)(2,1)S(1)} %get-tuple-element.28.after_ref.refs_0_), channel_id=1, source_target_pairs={{0,2},{1,3},{2,0},{3,1},{4,6},{5,7},{6,4},{7,5},{8,10},{9,11},{10,... | collective-permute-start | bytes 589832 | tf_op jit(solution)/shard_map/ppermute | solution.py:262
  8.3 3.1 %fetch.3.refs_11_ = bf16[1152,3072]{1,0:T(8,128)(2,1)S(1)} custom-call(bf16[1152,6144]{1,0:T(8,128)(2,1)} %refs_13_.1, bf16[16,6144]{1,0:T(8,128)(2,1)S(1)} %get-tuple-element.28.after_ref.refs_0_), custom_call_target="tpu_custom_call" | custom-call | bytes 14155776 | tf_op jit(solution)/shard_map/fetch/pallas_call | solution.py:90
  11.4 3.1 %fetch.2.refs_10_ = bf16[1152,3072]{1,0:T(8,128)(2,1)S(1)} custom-call(bf16[1152,6144]{1,0:T(8,128)(2,1)} %refs_12_.2, bf16[16,6144]{1,0:T(8,128)(2,1)S(1)} %get-tuple-element.28.after_ref.refs_0_), custom_call_target="tpu_custom_call" | custom-call | bytes 14155776 | tf_op jit(solution)/shard_map/fetch/pallas_call | solution.py:90
  14.5 0.0 collective-permute-done.refs_1_
  14.6 0.0 collective-permute-done.2.refs_3_
  14.6 0.4 collective-permute-start.3
  15.0 0.1 collective-permute-done.1.refs_2_
  15.1 2.8 %collective-permute-start.5 = (bf16[16,3072]{1,0:T(8,128)(2,1)S(1)}, bf16[16,3072]{1,0:T(8,128)(2,1)S(1)}, u32[]{:S(2)}, u32[]{:S(2)}) collective-permute-start(bf16[16,3072]{1,0:T(8,128)(2,1)S(1)} %get-tuple-element.33), channel_id=1, source_target_pairs={{0,8},{1,9},{2,10},{3,11},{4,12},{5,13},{6,14},{7,15},{8,0},{9,1},... | collective-permute-start | bytes 294920 | tf_op jit(solution)/shard_map/ppermute | solution.py:257
  18.0 0.1 collective-permute-start.7
  18.1 1.5 %collective-permute-start.4 = (bf16[16,6144]{1,0:T(8,128)(2,1)S(1)}, bf16[16,6144]{1,0:T(8,128)(2,1)S(1)}, u32[]{:S(2)}, u32[]{:S(2)}) collective-permute-start(bf16[16,6144]{1,0:T(8,128)(2,1)S(1)} %collective-permute-done.1.refs_2_), channel_id=1, source_target_pairs={{0,2},{1,3},{2,0},{3,1},{4,6},{5,7},{6,4},{7,5},{8,10},{9,11},{10,... | collective-permute-start | bytes 589832 | tf_op jit(solution)/shard_map/ppermute | solution.py:262
  19.7 5.8 %collective-permute-done.5.refs_7_ = bf16[16,3072]{1,0:T(8,128)(2,1)S(1)} collective-permute-done((bf16[16,3072]{1,0:T(8,128)(2,1)S(1)}, bf16[16,3072]{1,0:T(8,128)(2,1)S(1)}, u32[]{:S(2)}, u32[]{:S(2)}) %collective-permute-start.5) | collective-permute-done | bytes 98336 | tf_op jit(solution)/shard_map/ppermute | solution.py:257
  25.4 1.5 %collective-permute-start.6 = (bf16[16,3072]{1,0:T(8,128)(2,1)S(1)}, bf16[16,3072]{1,0:T(8,128)(2,1)S(1)}, u32[]{:S(2)}, u32[]{:S(2)}) collective-permute-start(bf16[16,3072]{1,0:T(8,128)(2,1)S(1)} %collective-permute-done.5.refs_7_), channel_id=1, source_target_pairs={{0,2},{1,3},{2,0},{3,1},{4,6},{5,7},{6,4},{7,5},{8,10},{9,11},{10,... | collective-permute-start | bytes 294920 | tf_op jit(solution)/shard_map/ppermute | solution.py:262
  26.9 0.0 collective-permute-done.3.refs_4_
  26.9 0.0 collective-permute-done.4.refs_5_
  27.0 0.0 collective-permute-done.7.refs_7_
  27.0 3.0 %collective-permute-done.6.refs_8_ = bf16[16,3072]{1,0:T(8,128)(2,1)S(1)} collective-permute-done((bf16[16,3072]{1,0:T(8,128)(2,1)S(1)}, bf16[16,3072]{1,0:T(8,128)(2,1)S(1)}, u32[]{:S(2)}, u32[]{:S(2)}) %collective-permute-start.6) | collective-permute-done | bytes 98336 | tf_op jit(solution)/shard_map/ppermute | solution.py:262
  30.0 0.0 collective-permute-start.8
  30.0 1.5 %collective-permute-start.9 = (bf16[16,3072]{1,0:T(8,128)(2,1)S(1)}, bf16[16,3072]{1,0:T(8,128)(2,1)S(1)}, u32[]{:S(2)}, u32[]{:S(2)}) collective-permute-start(bf16[16,3072]{1,0:T(8,128)(2,1)S(1)} %collective-permute-done.7.refs_7_), channel_id=1, source_target_pairs={{0,2},{1,3},{2,0},{3,1},{4,6},{5,7},{6,4},{7,5},{8,10},{9,11},{10,... | collective-permute-start | bytes 294920 | tf_op jit(solution)/shard_map/ppermute | solution.py:262
  31.6 0.3 collective-permute-start.11
  31.8 3.4 %collective-permute-done.9.refs_8_ = bf16[16,3072]{1,0:T(8,128)(2,1)S(1)} collective-permute-done((bf16[16,3072]{1,0:T(8,128)(2,1)S(1)}, bf16[16,3072]{1,0:T(8,128)(2,1)S(1)}, u32[]{:S(2)}, u32[]{:S(2)}) %collective-permute-start.9) | collective-permute-done | bytes 98336 | tf_op jit(solution)/shard_map/ppermute | solution.py:262
  35.3 0.1 collective-permute-start.10
  35.3 0.0 collective-permute-done.11.refs_9_
  35.3 0.0 collective-permute-done.8.refs_6_
  35.4 5.2 %gate_up.2 = (bf16[1152,3072]{1,0:T(8,128)(2,1)S(1)}, bf16[1152,3072]{1,0:T(8,128)(2,1)S(1)}, f32[1152,256]{1,0:T(8,128)S(1)}, f32[1152,256]{1,0:T(8,128)S(1)}) custom-call(bf16[16,6144]{1,0:T(8,128)(2,1)S(1)} %get-tuple-element.28.after_ref.refs_0_, bf16[16,6144]{1,0:T(8,128)(2,1)S(1)} %collective-permute-done.refs_1_, ...), custom_call_target="tpu_custom_call" | custom-call | flops 3623878656 | bytes 16515072 | tf_op jit(solution)/shard_map/gate_up/pallas_call | solution.py:162
  40.6 0.0 collective-permute-done.10.refs_9_
  40.6 5.3 %gate_up.3 = (bf16[1152,6144]{1,0:T(8,128)(2,1)S(1)}, bf16[256,1152]{1,0:T(8,128)(2,1)S(1)}) custom-call(bf16[16,6144]{1,0:T(8,128)(2,1)S(1)} %get-tuple-element.28.after_ref.refs_0_, bf16[16,6144]{1,0:T(8,128)(2,1)S(1)} %collective-permute-done.refs_1_, bf16[16,6144]{1,0:T(8,128)(2,1)S(1)} %collective-permute-done.1.refs_2_, ...), custom_call_target="tpu_custom_call" | custom-call | flops 3623878656 | bytes 16515072 | tf_op jit(solution)/shard_map/gate_up/pallas_call | solution.py:162
  45.8 3.1 %down.3 = (bf16[128,3072]{1,0:T(8,128)(2,1)S(1)}, bf16[128,3072]{1,0:T(8,128)(2,1)S(1)}) custom-call(bf16[256,1152]{1,0:T(8,128)(2,1)S(1)} %get-tuple-element.43.hidden_ref, bf16[1152,6144]{1,0:T(8,128)(2,1)S(1)} %get-tuple-element.44.w_ref), custom_call_target="tpu_custom_call" | custom-call | flops 1811939328 | bytes 9240576 | tf_op jit(solution)/shard_map/down/pallas_call | solution.py:198
  48.9 0.5 collective-permute-start.13
  49.4 3.1 %down.2 = (bf16[128,3072]{1,0:T(8,128)(2,1)S(1)}, bf16[128,3072]{1,0:T(8,128)(2,1)S(1)}) custom-call(bf16[256,1152]{1,0:T(8,128)(2,1)S(1)} %get-tuple-element.43.hidden_ref, bf16[1152,6144]{1,0:T(8,128)(2,1)S(1)} %get-tuple-element.44.w_ref), custom_call_target="tpu_custom_call" | custom-call | flops 1811939328 | bytes 9240576 | tf_op jit(solution)/shard_map/down/pallas_call | solution.py:198
  52.5 0.1 collective-permute-start.12
  52.6 0.0 collective-permute-done.13
  52.6 0.2 add_convert_fusion
  52.9 1.6 %collective-permute-start.16 = (bf16[16,3072]{1,0:T(8,128)(2,1)S(1)}, bf16[16,3072]{1,0:T(8,128)(2,1)S(1)}, u32[]{:S(2)}, u32[]{:S(2)}) collective-permute-start(bf16[16,3072]{1,0:T(8,128)(2,1)S(1)} %get-tuple-element.61), channel_id=1, source_target_pairs={{0,2},{1,3},{2,0},{3,1},{4,6},{5,7},{6,4},{7,5},{8,10},{9,11},{10,... | collective-permute-start | bytes 294920 | tf_op jit(solution)/shard_map/ppermute | solution.py:262
  54.4 0.4 collective-permute-done.12
  54.9 0.2 add_convert_fusion.1
  55.1 1.6 %collective-permute-start.20 = (bf16[16,3072]{1,0:T(8,128)(2,1)S(1)}, bf16[16,3072]{1,0:T(8,128)(2,1)S(1)}, u32[]{:S(2)}, u32[]{:S(2)}) collective-permute-start(bf16[16,3072]{1,0:T(8,128)(2,1)S(1)} %get-tuple-element.51), channel_id=1, source_target_pairs={{0,2},{1,3},{2,0},{3,1},{4,6},{5,7},{6,4},{7,5},{8,10},{9,11},{10,... | collective-permute-start | bytes 294920 | tf_op jit(solution)/shard_map/ppermute | solution.py:262
  56.7 0.6 collective-permute-start.14
  57.3 0.0 copy-start
  57.3 0.0 copy-start.1
  57.3 0.0 copy-start.2
  57.3 1.6 %collective-permute-start.18 = (bf16[16,6144]{1,0:T(8,128)(2,1)S(1)}, bf16[16,6144]{1,0:T(8,128)(2,1)S(1)}, u32[]{:S(2)}, u32[]{:S(2)}) collective-permute-start(bf16[16,6144]{1,0:T(8,128)(2,1)S(1)} %pad_maximum_fusion.4), channel_id=1, source_target_pairs={{0,2},{1,3},{2,0},{3,1},{4,6},{5,7},{6,4},{7,5},{8,10},{9,11},{10,... | collective-permute-start | bytes 589832 | tf_op jit(solution)/shard_map/ppermute | solution.py:262
  58.9 0.0 collective-permute-done.16
  59.0 0.1 collective-permute-start.22
  59.0 6.0 %collective-permute-done.14 = bf16[16,6144]{1,0:T(8,128)(2,1)S(1)} collective-permute-done((bf16[16,6144]{1,0:T(8,128)(2,1)S(1)}, bf16[16,6144]{1,0:T(8,128)(2,1)S(1)}, u32[]{:S(2)}, u32[]{:S(2)}) %collective-permute-start.14) | collective-permute-done | bytes 196640 | tf_op jit(solution)/shard_map/ppermute | solution.py:262
  65.1 1.6 %collective-permute-start.15 = (bf16[16,6144]{1,0:T(8,128)(2,1)S(1)}, bf16[16,6144]{1,0:T(8,128)(2,1)S(1)}, u32[]{:S(2)}, u32[]{:S(2)}) collective-permute-start(bf16[16,6144]{1,0:T(8,128)(2,1)S(1)} %pad_maximum_fusion.2), channel_id=1, source_target_pairs={{0,2},{1,3},{2,0},{3,1},{4,6},{5,7},{6,4},{7,5},{8,10},{9,11},{10,... | collective-permute-start | bytes 589832 | tf_op jit(solution)/shard_map/ppermute | solution.py:262
  66.6 1.6 %collective-permute-start.17 = (bf16[16,6144]{1,0:T(8,128)(2,1)S(1)}, bf16[16,6144]{1,0:T(8,128)(2,1)S(1)}, u32[]{:S(2)}, u32[]{:S(2)}) collective-permute-start(bf16[16,6144]{1,0:T(8,128)(2,1)S(1)} %add_convert_fusion.3), channel_id=1, source_target_pairs={{0,12},{1,13},{2,14},{3,15},{4,0},{5,1},{6,2},{7,3},{8,4},{9,5},{1... | collective-permute-start | bytes 589832 | tf_op jit(solution)/shard_map/ppermute | solution.py:257
  68.2 1.0 %collective-permute-done.18 = bf16[16,6144]{1,0:T(8,128)(2,1)S(1)} collective-permute-done((bf16[16,6144]{1,0:T(8,128)(2,1)S(1)}, bf16[16,6144]{1,0:T(8,128)(2,1)S(1)}, u32[]{:S(2)}, u32[]{:S(2)}) %collective-permute-start.18) | collective-permute-done | bytes 196640 | tf_op jit(solution)/shard_map/ppermute | solution.py:262
  69.3 0.1 collective-permute-start.19
  69.4 0.0 collective-permute-done.20
  69.4 2.3 %collective-permute-start.21 = (bf16[16,3072]{1,0:T(8,128)(2,1)S(1)}, bf16[16,3072]{1,0:T(8,128)(2,1)S(1)}, u32[]{:S(2)}, u32[]{:S(2)}) collective-permute-start(bf16[16,3072]{1,0:T(8,128)(2,1)S(1)} %add_convert_fusion.5), channel_id=1, source_target_pairs={{0,8},{1,9},{2,10},{3,11},{4,12},{5,13},{6,14},{7,15},{8,0},{9,1},... | collective-permute-start | bytes 294920 | tf_op jit(solution)/shard_map/ppermute | solution.py:257
  71.7 0.0 collective-permute-done.22.refs_3_
  71.7 8.6 %collective-permute-done.21.refs_2_ = bf16[16,3072]{1,0:T(8,128)(2,1)S(1)} collective-permute-done((bf16[16,3072]{1,0:T(8,128)(2,1)S(1)}, bf16[16,3072]{1,0:T(8,128)(2,1)S(1)}, u32[]{:S(2)}, u32[]{:S(2)}) %collective-permute-start.21) | collective-permute-done | bytes 98336 | tf_op jit(solution)/shard_map/ppermute | solution.py:257
  80.3 0.0 collective-permute-done.15.arrived
  80.3 0.0 collective-permute-done.17.near
  80.3 0.0 collective-permute-done.19.last
  80.3 0.0 copy-done
  80.4 0.0 copy-done.1
  80.4 0.0 copy-done.2
  80.4 1.4 %mix.1 = bf16[24,6144]{1,0:T(8,128)(2,1)} custom-call(s32[2,24]{1,0:T(2,128)S(1)} %bitcast.4, f32[2,24]{1,0:T(2,128)S(1)} %bitcast.5, bf16[24,6144]{1,0:T(8,128)(2,1)S(1)} %copy-done, bf16[16,6144]{1,0:T(8,128)(2,1)S(1)} %collective-permute-done.15.arrived, bf16[16,6144]{1,0:T(8,128)(2,1)S(1)} %collective-permute-done.17.near, ...), custom_call_target="tpu_custom_call" | custom-call | tf_op jit(solution)/shard_map/mix/pallas_call | solution.py:236
  (17 shorter events, 0.4 us)
Async XLA Ops:
  1.5 13.1 %collective-permute-start = (bf16[16,6144]{1,0:T(8,128)(2,1)S(1)}, bf16[16,6144]{1,0:T(8,128)(2,1)S(1)}, u32[]{:S(2)}, u32[]{:S(2)}) collective-permute-start(bf16[16,6144]{1,0:T(8,128)(2,1)S(1)} %get-tuple-element.29), channel_id=1, source_target_pairs={{0,4},{1,5},{2,6},{3,7},{4,8},{5,9},{6,10},{7,11},{8,12},{9,13},{1... | collective-permute-start | bytes 589832 | tf_op jit(solution)/shard_map/ppermute | solution.py:257
  4.6 10.6 %collective-permute-start.1 = (bf16[16,6144]{1,0:T(8,128)(2,1)S(1)}, bf16[16,6144]{1,0:T(8,128)(2,1)S(1)}, u32[]{:S(2)}, u32[]{:S(2)}) collective-permute-start(bf16[16,6144]{1,0:T(8,128)(2,1)S(1)} %get-tuple-element.30), channel_id=1, source_target_pairs={{0,12},{1,13},{2,14},{3,15},{4,0},{5,1},{6,2},{7,3},{8,4},{9,5},{1... | collective-permute-start | bytes 589832 | tf_op jit(solution)/shard_map/ppermute | solution.py:257
  6.7 7.9 %collective-permute-start.2 = (bf16[16,6144]{1,0:T(8,128)(2,1)S(1)}, bf16[16,6144]{1,0:T(8,128)(2,1)S(1)}, u32[]{:S(2)}, u32[]{:S(2)}) collective-permute-start(bf16[16,6144]{1,0:T(8,128)(2,1)S(1)} %get-tuple-element.28.after_ref.refs_0_), channel_id=1, source_target_pairs={{0,2},{1,3},{2,0},{3,1},{4,6},{5,7},{6,4},{7,5},{8,10},{9,11},{10,... | collective-permute-start | bytes 589832 | tf_op jit(solution)/shard_map/ppermute | solution.py:262
  14.6 12.3 %collective-permute-start.3 = (bf16[16,6144]{1,0:T(8,128)(2,1)S(1)}, bf16[16,6144]{1,0:T(8,128)(2,1)S(1)}, u32[]{:S(2)}, u32[]{:S(2)}) collective-permute-start(bf16[16,6144]{1,0:T(8,128)(2,1)S(1)} %collective-permute-done.refs_1_), channel_id=1, source_target_pairs={{0,2},{1,3},{2,0},{3,1},{4,6},{5,7},{6,4},{7,5},{8,10},{9,11},{10,... | collective-permute-start | bytes 589832 | tf_op jit(solution)/shard_map/ppermute | solution.py:262
  15.1 10.3 %collective-permute-start.5 = (bf16[16,3072]{1,0:T(8,128)(2,1)S(1)}, bf16[16,3072]{1,0:T(8,128)(2,1)S(1)}, u32[]{:S(2)}, u32[]{:S(2)}) collective-permute-start(bf16[16,3072]{1,0:T(8,128)(2,1)S(1)} %get-tuple-element.33), channel_id=1, source_target_pairs={{0,8},{1,9},{2,10},{3,11},{4,12},{5,13},{6,14},{7,15},{8,0},{9,1},... | collective-permute-start | bytes 294920 | tf_op jit(solution)/shard_map/ppermute | solution.py:257
  18.0 9.0 %collective-permute-start.7 = (bf16[16,3072]{1,0:T(8,128)(2,1)S(1)}, bf16[16,3072]{1,0:T(8,128)(2,1)S(1)}, u32[]{:S(2)}, u32[]{:S(2)}) collective-permute-start(bf16[16,3072]{1,0:T(8,128)(2,1)S(1)} %get-tuple-element.36), channel_id=1, source_target_pairs={{0,8},{1,9},{2,10},{3,11},{4,12},{5,13},{6,14},{7,15},{8,0},{9,1},... | collective-permute-start | bytes 294920 | tf_op jit(solution)/shard_map/ppermute | solution.py:257
  18.1 8.9 %collective-permute-start.4 = (bf16[16,6144]{1,0:T(8,128)(2,1)S(1)}, bf16[16,6144]{1,0:T(8,128)(2,1)S(1)}, u32[]{:S(2)}, u32[]{:S(2)}) collective-permute-start(bf16[16,6144]{1,0:T(8,128)(2,1)S(1)} %collective-permute-done.1.refs_2_), channel_id=1, source_target_pairs={{0,2},{1,3},{2,0},{3,1},{4,6},{5,7},{6,4},{7,5},{8,10},{9,11},{10,... | collective-permute-start | bytes 589832 | tf_op jit(solution)/shard_map/ppermute | solution.py:262
  25.4 4.6 %collective-permute-start.6 = (bf16[16,3072]{1,0:T(8,128)(2,1)S(1)}, bf16[16,3072]{1,0:T(8,128)(2,1)S(1)}, u32[]{:S(2)}, u32[]{:S(2)}) collective-permute-start(bf16[16,3072]{1,0:T(8,128)(2,1)S(1)} %collective-permute-done.5.refs_7_), channel_id=1, source_target_pairs={{0,2},{1,3},{2,0},{3,1},{4,6},{5,7},{6,4},{7,5},{8,10},{9,11},{10,... | collective-permute-start | bytes 294920 | tf_op jit(solution)/shard_map/ppermute | solution.py:262
  30.0 5.3 %collective-permute-start.8 = (bf16[96,6144]{1,0:T(8,128)(2,1)S(1)}, bf16[96,6144]{1,0:T(8,128)(2,1)S(1)}, u32[]{:S(2)}, u32[]{:S(2)}) collective-permute-start(bf16[96,6144]{1,0:T(8,128)(2,1)S(1)} %constant_dynamic-update-slice_fusion), channel_id=1, source_target_pairs={{0,1},{1,0},{2,3},{3,2},{4,5},{5,4},{6,7},{7,6},{8,9},{9,8},{10,11... | collective-permute-start | bytes 3538952 | tf_op jit(solution)/shard_map/ppermute | solution.py:262
  30.0 5.2 %collective-permute-start.9 = (bf16[16,3072]{1,0:T(8,128)(2,1)S(1)}, bf16[16,3072]{1,0:T(8,128)(2,1)S(1)}, u32[]{:S(2)}, u32[]{:S(2)}) collective-permute-start(bf16[16,3072]{1,0:T(8,128)(2,1)S(1)} %collective-permute-done.7.refs_7_), channel_id=1, source_target_pairs={{0,2},{1,3},{2,0},{3,1},{4,6},{5,7},{6,4},{7,5},{8,10},{9,11},{10,... | collective-permute-start | bytes 294920 | tf_op jit(solution)/shard_map/ppermute | solution.py:262
  31.6 3.8 %collective-permute-start.11 = (bf16[32,3072]{1,0:T(8,128)(2,1)S(1)}, bf16[32,3072]{1,0:T(8,128)(2,1)S(1)}, u32[]{:S(2)}, u32[]{:S(2)}) collective-permute-start(bf16[32,3072]{1,0:T(8,128)(2,1)S(1)} %pad_maximum_fusion.1), channel_id=1, source_target_pairs={{0,1},{1,0},{2,3},{3,2},{4,5},{5,4},{6,7},{7,6},{8,9},{9,8},{10,11... | collective-permute-start | bytes 589832 | tf_op jit(solution)/shard_map/ppermute | solution.py:262
  35.3 5.3 %collective-permute-start.10 = (bf16[32,3072]{1,0:T(8,128)(2,1)S(1)}, bf16[32,3072]{1,0:T(8,128)(2,1)S(1)}, u32[]{:S(2)}, u32[]{:S(2)}) collective-permute-start(bf16[32,3072]{1,0:T(8,128)(2,1)S(1)} %pad_maximum_fusion), channel_id=1, source_target_pairs={{0,1},{1,0},{2,3},{3,2},{4,5},{5,4},{6,7},{7,6},{8,9},{9,8},{10,11... | collective-permute-start | bytes 589832 | tf_op jit(solution)/shard_map/ppermute | solution.py:262
  48.9 3.7 %collective-permute-start.13 = (bf16[128,3072]{1,0:T(8,128)(2,1)S(1)}, bf16[128,3072]{1,0:T(8,128)(2,1)S(1)}, u32[]{:S(2)}, u32[]{:S(2)}) collective-permute-start(bf16[128,3072]{1,0:T(8,128)(2,1)S(1)} %get-tuple-element.48), channel_id=1, source_target_pairs={{0,1},{1,0},{2,3},{3,2},{4,5},{5,4},{6,7},{7,6},{8,9},{9,8},{10,11... | collective-permute-start | bytes 2359304 | tf_op jit(solution)/shard_map/ppermute | solution.py:262
  52.5 2.4 %collective-permute-start.12 = (bf16[128,3072]{1,0:T(8,128)(2,1)S(1)}, bf16[128,3072]{1,0:T(8,128)(2,1)S(1)}, u32[]{:S(2)}, u32[]{:S(2)}) collective-permute-start(bf16[128,3072]{1,0:T(8,128)(2,1)S(1)} %get-tuple-element.46), channel_id=1, source_target_pairs={{0,1},{1,0},{2,3},{3,2},{4,5},{5,4},{6,7},{7,6},{8,9},{9,8},{10,11... | collective-permute-start | bytes 2359304 | tf_op jit(solution)/shard_map/ppermute | solution.py:262
  52.9 6.1 %collective-permute-start.16 = (bf16[16,3072]{1,0:T(8,128)(2,1)S(1)}, bf16[16,3072]{1,0:T(8,128)(2,1)S(1)}, u32[]{:S(2)}, u32[]{:S(2)}) collective-permute-start(bf16[16,3072]{1,0:T(8,128)(2,1)S(1)} %get-tuple-element.61), channel_id=1, source_target_pairs={{0,2},{1,3},{2,0},{3,1},{4,6},{5,7},{6,4},{7,5},{8,10},{9,11},{10,... | collective-permute-start | bytes 294920 | tf_op jit(solution)/shard_map/ppermute | solution.py:262
  55.1 14.3 %collective-permute-start.20 = (bf16[16,3072]{1,0:T(8,128)(2,1)S(1)}, bf16[16,3072]{1,0:T(8,128)(2,1)S(1)}, u32[]{:S(2)}, u32[]{:S(2)}) collective-permute-start(bf16[16,3072]{1,0:T(8,128)(2,1)S(1)} %get-tuple-element.51), channel_id=1, source_target_pairs={{0,2},{1,3},{2,0},{3,1},{4,6},{5,7},{6,4},{7,5},{8,10},{9,11},{10,... | collective-permute-start | bytes 294920 | tf_op jit(solution)/shard_map/ppermute | solution.py:262
  56.7 8.3 %collective-permute-start.14 = (bf16[16,6144]{1,0:T(8,128)(2,1)S(1)}, bf16[16,6144]{1,0:T(8,128)(2,1)S(1)}, u32[]{:S(2)}, u32[]{:S(2)}) collective-permute-start(bf16[16,6144]{1,0:T(8,128)(2,1)S(1)} %pad_maximum_fusion.3), channel_id=1, source_target_pairs={{0,2},{1,3},{2,0},{3,1},{4,6},{5,7},{6,4},{7,5},{8,10},{9,11},{10,... | collective-permute-start | bytes 589832 | tf_op jit(solution)/shard_map/ppermute | solution.py:262
  57.3 23.1 %copy-start = (bf16[24,6144]{1,0:T(8,128)(2,1)S(1)}, bf16[24,6144]{1,0:T(8,128)(2,1)}, u32[]{:S(2)}) copy-start(bf16[24,6144]{1,0:T(8,128)(2,1)} %act_ref.3) | copy-start | bytes 884740
  57.3 23.0 %copy-start.1 = (s32[24,2]{0,1:T(2,128)S(1)}, s32[24,2]{0,1:T(2,128)}, u32[]{:S(2)}) copy-start(s32[24,2]{0,1:T(2,128)} %param.8) | copy-start | bytes 580
  57.3 23.0 %copy-start.2 = (f32[24,2]{0,1:T(2,128)S(1)}, f32[24,2]{0,1:T(2,128)}, u32[]{:S(2)}) copy-start(f32[24,2]{0,1:T(2,128)} %param.9) | copy-start | bytes 580
  57.3 11.9 %collective-permute-start.18 = (bf16[16,6144]{1,0:T(8,128)(2,1)S(1)}, bf16[16,6144]{1,0:T(8,128)(2,1)S(1)}, u32[]{:S(2)}, u32[]{:S(2)}) collective-permute-start(bf16[16,6144]{1,0:T(8,128)(2,1)S(1)} %pad_maximum_fusion.4), channel_id=1, source_target_pairs={{0,2},{1,3},{2,0},{3,1},{4,6},{5,7},{6,4},{7,5},{8,10},{9,11},{10,... | collective-permute-start | bytes 589832 | tf_op jit(solution)/shard_map/ppermute | solution.py:262
  59.0 12.8 %collective-permute-start.22 = (bf16[16,3072]{1,0:T(8,128)(2,1)S(1)}, bf16[16,3072]{1,0:T(8,128)(2,1)S(1)}, u32[]{:S(2)}, u32[]{:S(2)}) collective-permute-start(bf16[16,3072]{1,0:T(8,128)(2,1)S(1)} %add_convert_fusion.4), channel_id=1, source_target_pairs={{0,8},{1,9},{2,10},{3,11},{4,12},{5,13},{6,14},{7,15},{8,0},{9,1},... | collective-permute-start | bytes 294920 | tf_op jit(solution)/shard_map/ppermute | solution.py:257
  65.1 15.3 %collective-permute-start.15 = (bf16[16,6144]{1,0:T(8,128)(2,1)S(1)}, bf16[16,6144]{1,0:T(8,128)(2,1)S(1)}, u32[]{:S(2)}, u32[]{:S(2)}) collective-permute-start(bf16[16,6144]{1,0:T(8,128)(2,1)S(1)} %pad_maximum_fusion.2), channel_id=1, source_target_pairs={{0,2},{1,3},{2,0},{3,1},{4,6},{5,7},{6,4},{7,5},{8,10},{9,11},{10,... | collective-permute-start | bytes 589832 | tf_op jit(solution)/shard_map/ppermute | solution.py:262
  66.6 13.7 %collective-permute-start.17 = (bf16[16,6144]{1,0:T(8,128)(2,1)S(1)}, bf16[16,6144]{1,0:T(8,128)(2,1)S(1)}, u32[]{:S(2)}, u32[]{:S(2)}) collective-permute-start(bf16[16,6144]{1,0:T(8,128)(2,1)S(1)} %add_convert_fusion.3), channel_id=1, source_target_pairs={{0,12},{1,13},{2,14},{3,15},{4,0},{5,1},{6,2},{7,3},{8,4},{9,5},{1... | collective-permute-start | bytes 589832 | tf_op jit(solution)/shard_map/ppermute | solution.py:257
  69.3 11.1 %collective-permute-start.19 = (bf16[16,6144]{1,0:T(8,128)(2,1)S(1)}, bf16[16,6144]{1,0:T(8,128)(2,1)S(1)}, u32[]{:S(2)}, u32[]{:S(2)}) collective-permute-start(bf16[16,6144]{1,0:T(8,128)(2,1)S(1)} %add_convert_fusion.2), channel_id=1, source_target_pairs={{0,4},{1,5},{2,6},{3,7},{4,8},{5,9},{6,10},{7,11},{8,12},{9,13},{1... | collective-permute-start | bytes 589832 | tf_op jit(solution)/shard_map/ppermute | solution.py:257
  69.4 10.9 %collective-permute-start.21 = (bf16[16,3072]{1,0:T(8,128)(2,1)S(1)}, bf16[16,3072]{1,0:T(8,128)(2,1)S(1)}, u32[]{:S(2)}, u32[]{:S(2)}) collective-permute-start(bf16[16,3072]{1,0:T(8,128)(2,1)S(1)} %add_convert_fusion.5), channel_id=1, source_target_pairs={{0,8},{1,9},{2,10},{3,11},{4,12},{5,13},{6,14},{7,15},{8,0},{9,1},... | collective-permute-start | bytes 294920 | tf_op jit(solution)/shard_map/ppermute | solution.py:257

commit v8 on v7

--- a/solution.py
+++ b/solution.py
@@ -43,16 +43,16 @@
     first, second = choices(ids_ref[...], plane)
     pick = (first | second).astype(jnp.float32).astype(jnp.bfloat16)
     rows = jnp.dot(pick, normed, preferred_element_type=jnp.float32).astype(jnp.bfloat16)
-    for s, out_ref in zip((0, 1, 3), out_refs):
-        out_ref[...] = rows[s * CAP : (s + 1) * CAP]
+    out_refs[0][...] = rows[:CAP]
     part = out_refs[-1].shape[1]
-    for k, out_ref in enumerate(out_refs[3:]):
-        out_ref[...] = rows[2 * CAP : 3 * CAP, k * part : (k + 1) * part]
+    for j, out_ref in enumerate(out_refs[1:]):
+        k, s = j // (EXPERTS - 1), j % (EXPERTS - 1) + 1
+        out_ref[...] = rows[s * CAP : (s + 1) * CAP, k * part : (k + 1) * part]
 
 
 def pack(group, ids, activations, gain):
     width = activations.shape[1]
-    widths = [width] * 3 + [width // HALVES] * HALVES
+    widths = [width] + [width // HALVES] * (HALVES * (EXPERTS - 1))
     operands = [ids, activations, gain.reshape(1, width)]
     return pl.pallas_call(
         functools.partial(pack_kernel, group),
@@ -178,7 +178,6 @@
 
 def down_kernel(at, hidden_ref, w_ref, keep_ref, send_ref):
     half, part = keep_ref.shape
-    first = 3 * half // 4
     block = BLOCK // 2
 
     @pl.loop(0, part // block)
@@ -187,10 +186,8 @@
         out = jnp.dot(hidden_ref[...], w_ref[:, columns], preferred_element_type=jnp.float32)
         out = out.astype(jnp.bfloat16)
         columns = pl.ds(pl.multiple_of(c * block, block), block)
-        for j, ref in enumerate((keep_ref, send_ref)):
-            ref[:first, columns] = out[j * first : (j + 1) * first]
-            far_rows = out[2 * first :]
-            ref[first:, columns] = far_rows[j * (half - first) : (j + 1) * (half - first)]
+        keep_ref[:, columns] = out[:half]
+        send_ref[:, columns] = out[half:]
 
 
 def down(at, part, hidden, w_down):
@@ -264,32 +261,35 @@
     def after(x, *others):
         return lax.optimization_barrier((x, *others))[0]
 
-    def spread(block):
-        pieces, bit = [], far // 2
-        while bit:
-            pieces.append(swap(block, bit))
-            block = jnp.concatenate([block, pieces[-1]], axis=0)
-            bit //= 2
-        return pieces
-
+    others = EXPERTS - 1
     ids = expert_ids.T
     own, *sends = pack(group, ids, activations, norm_gain)
     far_own = swap(own, far)
-    arrivals = [shift(sends[0], 1), shift(sends[1], 3)]
-    now = [fetch(w_gate, 0, part, own), fetch(w_up, 0, part, own)]
-    for j in range(HALVES):
-        arrivals.append(shift(after(sends[2 + j], arrivals[1], now[1]), 2))
-    passed = [swap(after(arrivals[0], far_own), far), swap(arrivals[1], far)]
-    for j in range(2, len(arrivals)):
-        passed.append(swap(after(arrivals[j], arrivals[j - 1]), far))
-    head = [own, *arrivals[:2], far_own, *passed[:2]]
-    head += spread(after(jnp.concatenate(head, axis=0), *now, passed[2], arrivals[3]))
+    now = [fetch(w, 0, part, own) for w in (w_gate, w_up)]
+    blocks, earlier = [], []
+    for k in range(HALVES):
+        arrivals = []
+        for s in range(others):
+            x = sends[k * others + s]
+            arrivals.append(shift(after(x, *earlier, *now) if k else x, s + 1))
+        earlier = arrivals
+        blocks.append(jnp.concatenate(arrivals, axis=0))
     totals = []
     for k in range(HALVES):
-        tail = [arrivals[2 + k], passed[2 + k]]
-        tail += spread(jnp.concatenate(tail, axis=0))
+        columns = slice(k * part, (k + 1) * part)
+        far_block = swap(blocks[k], far)
+        if totals:
+            far_block, totals = lax.optimization_barrier((far_block, totals))
+        pieces = [own[:, columns], blocks[k], far_own[:, columns], far_block]
+        bit = far // 2
+        while bit:
+            pieces.append(swap(jnp.concatenate(pieces, axis=0), bit))
+            bit //= 2
+        pieces[0], pieces[2] = own, far_own
+        if k < HALVES - 1:
+            pieces[1] = after(pieces[1], blocks[k + 1])
         later = [w_down] if k == HALVES - 1 else [w_gate, w_up]
-        now, totals = gate_up(k, head + tail, now, later, totals)
+        now, totals = gate_up(k, pieces, now, later, totals)
     hidden, (down_w,) = totals[0], now
     held = []
     for k in range(HALVES):
@@ -297,22 +297,19 @@
         bit = 1
         while bit < far:
             total = added(keep, swap(send, bit))
+            keep, send = total[: total.shape[0] // 2], total[total.shape[0] // 2 :]
             bit *= 2
-            if bit < far:
-                count = total.shape[0] // 8
-                groups = [total[: 3 * count], total[3 * count : 6 * count]]
-                groups += [total[6 * count : 7 * count], total[7 * count :]]
-                keep = jnp.concatenate(groups[0::2], axis=0)
-                send = jnp.concatenate(groups[1::2], axis=0)
         held.append([total[j * CAP : (j + 1) * CAP] for j in range(2 * EXPERTS)])
-    crossed = [swap(h[7], far) for h in held]
-    middle = [shift(added(h[6], x), -2) for h, x in zip(held, crossed)]
-    mine = [jnp.concatenate([h[j] for h in held], axis=1) for j in range(6)]
-    crossed.append(swap(mine[4], far))
-    crossed.append(swap(mine[5], far))
-    near = shift(after(added(mine[1], crossed[2]), crossed[1]), -1)
-    last = shift(added(mine[2], crossed[3]), -3)
-    arrived = swap(after(mine[3], crossed[2]), far)
+    crossed = [swap(h[6], far) for h in held]
+    middle = [shift(added(h[2], x), -2) for h, x in zip(held, crossed)]
+    mine = [jnp.concatenate([h[j] for h in held], axis=1) for j in range(2 * EXPERTS)]
+    back = {}
+    for s, ready in ((1, []), (3, middle[:1]), (0, middle)):
+        crossed.append(swap(after(mine[EXPERTS + s], *crossed, *ready), far))
+        back[s] = crossed[-1]
+    near = shift(added(mine[1], back[1]), -1)
+    last = shift(added(mine[3], back[3]), -3)
+    arrived = back[0]
     pieces = [arrived, near, last, *[h[0] for h in held], *middle]
     return mix(group, ids, route_logits.T, activations, pieces)
 

time: 81.9 us -> 81.5 us (level)
    ppermute x8 -> x10, starting transfers between devices: 12.2 us -> 15.7 us  [shift(): lax.ppermute(x, 'expert', [(i, (i + s * group) % devices) for i in range(...]
    ppermute x15 -> x12, starting transfers between devices: 14.5 us -> 11.4 us  [swap(): return lax.ppermute(x, 'expert', [(i, i ^ bit) for i in range(devices)])]
    ppermute x15 -> x12, waiting for transfers between devices: 13.9 us -> 11.5 us  [swap(): return lax.ppermute(x, 'expert', [(i, i ^ bit) for i in range(devices)])]
    ppermute x8 -> x10, waiting for transfers between devices: 14.5 us -> 16.2 us  [shift(): lax.ppermute(x, 'expert', [(i, (i + s * group) % devices) for i in range(...]
  transfers between devices with their start and end apart: 23 -> 22, of which waited for: 8 -> 13; matrix products, arithmetic and copies ran while one was open for 1% -> 1% of each run, Pallas kernels for 18% -> 18%
where the time goes in v8:
time: 81.5 us; the launch traced here: 81.4 us
  waiting for transfers between devices  27.6 us (34%)
  starting transfers between devices  27 us (33%)
  Pallas kernels  25.6 us (31%)
    ppermute x10, waiting for transfers between devices, shift(): lax.ppermute(x, 'expert', [(i, (i + s * group) % devices) for i in range(...  16.2 us
    ppermute x10, starting transfers between devices, shift(): lax.ppermute(x, 'expert', [(i, (i + s * group) % devices) for i in range(...  15.7 us
    ppermute x12, waiting for transfers between devices, swap(): return lax.ppermute(x, 'expert', [(i, i ^ bit) for i in range(devices)])  11.5 us
    ppermute x12, starting transfers between devices, swap(): return lax.ppermute(x, 'expert', [(i, i ^ bit) for i in range(devices)])  11.4 us
    pallas_call x2, Pallas kernels, gate_up(): pl.pallas_call(functools.partial(gate_up_kernel, len(pieces), len(later),...  10.4 us
    pallas_call x2, Pallas kernels, fetch(): pl.pallas_call(functools.partial(fetch_kernel, at), in_specs=[ANY, ANY],...  6.19 us
    pallas_call x2, Pallas kernels, down(): pl.pallas_call(functools.partial(down_kernel, at), in_specs=[VMEM, VMEM],...  6.13 us
  transfers between devices with their start and end apart: 22, of which 13 were waited for; matrix products, arithmetic and copies ran while one was open for 1% of the time, Pallas kernels for 18%

profile of v8, /device:TPU:0, one launch (start us, length us, event | category | flops | bytes accessed | tf_op | source)
XLA Modules:
  0.0 81.4 jit_solution(1567273022083566632)
XLA Ops:
  0.0 1.5 %norm_and_pack.1 = (bf16[16,6144]{1,0:T(8,128)(2,1)S(1)}, bf16[16,3072]{1,0:T(8,128)(2,1)S(1)}, bf16[16,3072]{1,0:T(8,128)(2,1)S(1)}, bf16[16,3072]{1,0:T(8,128)...) custom-call(s32[2,24]{1,0:T(2,128)} %bitcast.3, ...), custom_call_target="tpu_custom_call" | custom-call | tf_op jit(solution)/shard_map/norm_and_pack/pallas_call | solution.py:57
  1.5 3.1 %collective-permute-start = (bf16[16,3072]{1,0:T(8,128)(2,1)S(1)}, bf16[16,3072]{1,0:T(8,128)(2,1)S(1)}, u32[]{:S(2)}, u32[]{:S(2)}) collective-permute-start(bf16[16,3072]{1,0:T(8,128)(2,1)S(1)} %get-tuple-element.34), channel_id=1, source_target_pairs={{0,4},{1,5},{2,6},{3,7},{4,8},{5,9},{6,10},{7,11},{8,12},{9,13},{1... | collective-permute-start | bytes 294920 | tf_op jit(solution)/shard_map/ppermute | solution.py:254
  4.6 2.6 %collective-permute-start.1 = (bf16[16,3072]{1,0:T(8,128)(2,1)S(1)}, bf16[16,3072]{1,0:T(8,128)(2,1)S(1)}, u32[]{:S(2)}, u32[]{:S(2)}) collective-permute-start(bf16[16,3072]{1,0:T(8,128)(2,1)S(1)} %get-tuple-element.35), channel_id=1, source_target_pairs={{0,8},{1,9},{2,10},{3,11},{4,12},{5,13},{6,14},{7,15},{8,0},{9,1},... | collective-permute-start | bytes 294920 | tf_op jit(solution)/shard_map/ppermute | solution.py:254
  7.2 1.3 %collective-permute-start.2 = (bf16[16,3072]{1,0:T(8,128)(2,1)S(1)}, bf16[16,3072]{1,0:T(8,128)(2,1)S(1)}, u32[]{:S(2)}, u32[]{:S(2)}) collective-permute-start(bf16[16,3072]{1,0:T(8,128)(2,1)S(1)} %get-tuple-element.36), channel_id=1, source_target_pairs={{0,12},{1,13},{2,14},{3,15},{4,0},{5,1},{6,2},{7,3},{8,4},{9,5},{1... | collective-permute-start | bytes 294920 | tf_op jit(solution)/shard_map/ppermute | solution.py:254
  8.5 1.5 %collective-permute-start.6 = (bf16[16,6144]{1,0:T(8,128)(2,1)S(1)}, bf16[16,6144]{1,0:T(8,128)(2,1)S(1)}, u32[]{:S(2)}, u32[]{:S(2)}) collective-permute-start(bf16[16,6144]{1,0:T(8,128)(2,1)S(1)} %get-tuple-element.32.after_ref.refs_0_), channel_id=1, source_target_pairs={{0,2},{1,3},{2,0},{3,1},{4,6},{5,7},{6,4},{7,5},{8,10},{9,11},{10,... | collective-permute-start | bytes 589832 | tf_op jit(solution)/shard_map/ppermute | solution.py:259
  10.0 3.1 %fetch.2.refs_5_ = bf16[1152,3072]{1,0:T(8,128)(2,1)S(1)} custom-call(bf16[1152,6144]{1,0:T(8,128)(2,1)} %refs_7_.2, bf16[16,6144]{1,0:T(8,128)(2,1)S(1)} %get-tuple-element.32.after_ref.refs_0_), custom_call_target="tpu_custom_call" | custom-call | bytes 14155776 | tf_op jit(solution)/shard_map/fetch/pallas_call | solution.py:90
  13.1 3.1 %fetch.3.refs_6_ = bf16[1152,3072]{1,0:T(8,128)(2,1)S(1)} custom-call(bf16[1152,6144]{1,0:T(8,128)(2,1)} %refs_8_.1, bf16[16,6144]{1,0:T(8,128)(2,1)S(1)} %get-tuple-element.32.after_ref.refs_0_), custom_call_target="tpu_custom_call" | custom-call | bytes 14155776 | tf_op jit(solution)/shard_map/fetch/pallas_call | solution.py:90
  16.2 0.0 collective-permute-done
  16.3 0.0 collective-permute-done.1
  16.3 0.0 collective-permute-done.2
  16.3 0.7 collective-permute-start.3
  17.0 0.9 %collective-permute-start.4 = (bf16[16,3072]{1,0:T(8,128)(2,1)S(1)}, bf16[16,3072]{1,0:T(8,128)(2,1)S(1)}, u32[]{:S(2)}, u32[]{:S(2)}) collective-permute-start(bf16[16,3072]{1,0:T(8,128)(2,1)S(1)} %get-tuple-element.39), channel_id=1, source_target_pairs={{0,8},{1,9},{2,10},{3,11},{4,12},{5,13},{6,14},{7,15},{8,0},{9,1},... | collective-permute-start | bytes 294920 | tf_op jit(solution)/shard_map/ppermute | solution.py:254
  17.9 2.2 %collective-permute-start.5 = (bf16[16,3072]{1,0:T(8,128)(2,1)S(1)}, bf16[16,3072]{1,0:T(8,128)(2,1)S(1)}, u32[]{:S(2)}, u32[]{:S(2)}) collective-permute-start(bf16[16,3072]{1,0:T(8,128)(2,1)S(1)} %get-tuple-element.41), channel_id=1, source_target_pairs={{0,12},{1,13},{2,14},{3,15},{4,0},{5,1},{6,2},{7,3},{8,4},{9,5},{1... | collective-permute-start | bytes 294920 | tf_op jit(solution)/shard_map/ppermute | solution.py:254
  20.2 0.6 collective-permute-start.8
  20.8 3.0 %collective-permute-done.3 = bf16[16,3072]{1,0:T(8,128)(2,1)S(1)} collective-permute-done((bf16[16,3072]{1,0:T(8,128)(2,1)S(1)}, bf16[16,3072]{1,0:T(8,128)(2,1)S(1)}, u32[]{:S(2)}, u32[]{:S(2)}) %collective-permute-start.3) | collective-permute-done | bytes 98336 | tf_op jit(solution)/shard_map/ppermute | solution.py:254
  23.8 2.0 %collective-permute-done.4 = bf16[16,3072]{1,0:T(8,128)(2,1)S(1)} collective-permute-done((bf16[16,3072]{1,0:T(8,128)(2,1)S(1)}, bf16[16,3072]{1,0:T(8,128)(2,1)S(1)}, u32[]{:S(2)}, u32[]{:S(2)}) %collective-permute-start.4) | collective-permute-done | bytes 98336 | tf_op jit(solution)/shard_map/ppermute | solution.py:254
  25.9 0.0 collective-permute-done.5
  25.9 0.0 collective-permute-done.6.refs_2_
  25.9 1.4 %collective-permute-done.8.refs_3_ = bf16[48,3072]{1,0:T(8,128)(2,1)S(1)} collective-permute-done((bf16[48,3072]{1,0:T(8,128)(2,1)S(1)}, bf16[48,3072]{1,0:T(8,128)(2,1)S(1)}, u32[]{:S(2)}, u32[]{:S(2)}) %collective-permute-start.8) | collective-permute-done | bytes 294944 | tf_op jit(solution)/shard_map/ppermute | solution.py:259
  27.4 0.1 collective-permute-start.9
  27.5 1.4 %collective-permute-start.7 = (bf16[48,3072]{1,0:T(8,128)(2,1)S(1)}, bf16[48,3072]{1,0:T(8,128)(2,1)S(1)}, u32[]{:S(2)}, u32[]{:S(2)}) collective-permute-start(bf16[48,3072]{1,0:T(8,128)(2,1)S(1)} %get-tuple-element.78.refs_1_), channel_id=1, source_target_pairs={{0,2},{1,3},{2,0},{3,1},{4,6},{5,7},{6,4},{7,5},{8,10},{9,11},{10,... | collective-permute-start | bytes 884744 | tf_op jit(solution)/shard_map/ppermute | solution.py:259
  28.9 0.9 %collective-permute-done.9.refs_4_ = bf16[128,3072]{1,0:T(8,128)(2,1)S(1)} collective-permute-done((bf16[128,3072]{1,0:T(8,128)(2,1)S(1)}, bf16[128,3072]{1,0:T(8,128)(2,1)S(1)}, u32[]{:S(2)}, u32[]{:S(2)}) %collective-permute-start.9) | collective-permute-done | bytes 786464 | tf_op jit(solution)/shard_map/ppermute | solution.py:259
  29.7 5.2 %gate_up.2 = (bf16[1152,3072]{1,0:T(8,128)(2,1)S(1)}, bf16[1152,3072]{1,0:T(8,128)(2,1)S(1)}, f32[1152,256]{1,0:T(8,128)S(1)}, f32[1152,256]{1,0:T(8,128)S(1)}) custom-call(bf16[16,6144]{1,0:T(8,128)(2,1)S(1)} %get-tuple-element.32.after_ref.refs_0_, bf16[48,3072]{1,0:T(8,128)(2,1)S(1)} %get-tuple-element.42.refs_1_, ...), custom_call_target="tpu_custom_call" | custom-call | flops 3623878656 | bytes 16515072 | tf_op jit(solution)/shard_map/gate_up/pallas_call | solution.py:162
  34.9 2.0 %collective-permute-done.7.refs_3_ = bf16[48,3072]{1,0:T(8,128)(2,1)S(1)} collective-permute-done((bf16[48,3072]{1,0:T(8,128)(2,1)S(1)}, bf16[48,3072]{1,0:T(8,128)(2,1)S(1)}, u32[]{:S(2)}, u32[]{:S(2)}) %collective-permute-start.7) | collective-permute-done | bytes 294944 | tf_op jit(solution)/shard_map/ppermute | solution.py:259
  36.9 0.1 collective-permute-start.10
  37.0 2.3 %collective-permute-done.10.refs_4_ = bf16[128,3072]{1,0:T(8,128)(2,1)S(1)} collective-permute-done((bf16[128,3072]{1,0:T(8,128)(2,1)S(1)}, bf16[128,3072]{1,0:T(8,128)(2,1)S(1)}, u32[]{:S(2)}, u32[]{:S(2)}) %collective-permute-start.10) | collective-permute-done | bytes 786464 | tf_op jit(solution)/shard_map/ppermute | solution.py:259
  39.3 5.2 %gate_up.3 = (bf16[1152,6144]{1,0:T(8,128)(2,1)S(1)}, bf16[256,1152]{1,0:T(8,128)(2,1)S(1)}) custom-call(bf16[16,6144]{1,0:T(8,128)(2,1)S(1)} %get-tuple-element.32.after_ref.refs_0_, bf16[48,3072]{1,0:T(8,128)(2,1)S(1)} %get-tuple-element.78.refs_1_, bf16[16,6144]{1,0:T(8,128)(2,1)S(1)} %collective-permute-done.6.refs_2_, ...), custom_call_target="tpu_custom_call" | custom-call | flops 3623878656 | bytes 16515072 | tf_op jit(solution)/shard_map/gate_up/pallas_call | solution.py:162
  44.5 3.1 %down.2 = (bf16[128,3072]{1,0:T(8,128)(2,1)S(1)}, bf16[128,3072]{1,0:T(8,128)(2,1)S(1)}) custom-call(bf16[256,1152]{1,0:T(8,128)(2,1)S(1)} %get-tuple-element.50.hidden_ref, bf16[1152,6144]{1,0:T(8,128)(2,1)S(1)} %get-tuple-element.51.w_ref), custom_call_target="tpu_custom_call" | custom-call | flops 1811939328 | bytes 9240576 | tf_op jit(solution)/shard_map/down/pallas_call | solution.py:195
  47.6 0.2 collective-permute-start.11
  47.8 3.1 %down.3 = (bf16[128,3072]{1,0:T(8,128)(2,1)S(1)}, bf16[128,3072]{1,0:T(8,128)(2,1)S(1)}) custom-call(bf16[256,1152]{1,0:T(8,128)(2,1)S(1)} %get-tuple-element.50.hidden_ref, bf16[1152,6144]{1,0:T(8,128)(2,1)S(1)} %get-tuple-element.51.w_ref), custom_call_target="tpu_custom_call" | custom-call | flops 1811939328 | bytes 9240576 | tf_op jit(solution)/shard_map/down/pallas_call | solution.py:195
  50.9 0.0 copy-start
  50.9 0.0 copy-start.1
  50.9 0.0 copy-start.2
  50.9 0.4 collective-permute-start.12
  51.3 0.0 collective-permute-done.11
  51.3 0.2 add_convert_fusion.1
  51.6 1.4 %collective-permute-start.13 = (bf16[16,3072]{1,0:T(8,128)(2,1)S(1)}, bf16[16,3072]{1,0:T(8,128)(2,1)S(1)}, u32[]{:S(2)}, u32[]{:S(2)}) collective-permute-start(bf16[16,3072]{1,0:T(8,128)(2,1)S(1)} %get-tuple-element.71), channel_id=1, source_target_pairs={{0,2},{1,3},{2,0},{3,1},{4,6},{5,7},{6,4},{7,5},{8,10},{9,11},{10,... | collective-permute-start | bytes 294920 | tf_op jit(solution)/shard_map/ppermute | solution.py:259
  53.0 0.3 collective-permute-done.12
  53.2 0.2 add_convert_fusion
  53.5 1.4 %collective-permute-start.14 = (bf16[16,3072]{1,0:T(8,128)(2,1)S(1)}, bf16[16,3072]{1,0:T(8,128)(2,1)S(1)}, u32[]{:S(2)}, u32[]{:S(2)}) collective-permute-start(bf16[16,3072]{1,0:T(8,128)(2,1)S(1)} %get-tuple-element.64), channel_id=1, source_target_pairs={{0,2},{1,3},{2,0},{3,1},{4,6},{5,7},{6,4},{7,5},{8,10},{9,11},{10,... | collective-permute-start | bytes 294920 | tf_op jit(solution)/shard_map/ppermute | solution.py:259
  55.0 1.5 %collective-permute-done.13 = bf16[16,3072]{1,0:T(8,128)(2,1)S(1)} collective-permute-done((bf16[16,3072]{1,0:T(8,128)(2,1)S(1)}, bf16[16,3072]{1,0:T(8,128)(2,1)S(1)}, u32[]{:S(2)}, u32[]{:S(2)}) %collective-permute-start.13) | collective-permute-done | bytes 98336 | tf_op jit(solution)/shard_map/ppermute | solution.py:259
  56.5 1.8 %collective-permute-start.16 = (bf16[16,3072]{1,0:T(8,128)(2,1)S(1)}, bf16[16,3072]{1,0:T(8,128)(2,1)S(1)}, u32[]{:S(2)}, u32[]{:S(2)}) collective-permute-start(bf16[16,3072]{1,0:T(8,128)(2,1)S(1)} %add_convert_fusion.5), channel_id=1, source_target_pairs={{0,8},{1,9},{2,10},{3,11},{4,12},{5,13},{6,14},{7,15},{8,0},{9,1},... | collective-permute-start | bytes 294920 | tf_op jit(solution)/shard_map/ppermute | solution.py:254
  58.3 0.3 collective-permute-done.14
  58.6 1.3 %collective-permute-start.15 = (bf16[16,6144]{1,0:T(8,128)(2,1)S(1)}, bf16[16,6144]{1,0:T(8,128)(2,1)S(1)}, u32[]{:S(2)}, u32[]{:S(2)}) collective-permute-start(bf16[16,6144]{1,0:T(8,128)(2,1)S(1)} %pad_maximum_fusion.1), channel_id=1, source_target_pairs={{0,2},{1,3},{2,0},{3,1},{4,6},{5,7},{6,4},{7,5},{8,10},{9,11},{10,... | collective-permute-start | bytes 589832 | tf_op jit(solution)/shard_map/ppermute | solution.py:259
  60.0 1.0 %collective-permute-start.18 = (bf16[16,3072]{1,0:T(8,128)(2,1)S(1)}, bf16[16,3072]{1,0:T(8,128)(2,1)S(1)}, u32[]{:S(2)}, u32[]{:S(2)}) collective-permute-start(bf16[16,3072]{1,0:T(8,128)(2,1)S(1)} %add_convert_fusion.4), channel_id=1, source_target_pairs={{0,8},{1,9},{2,10},{3,11},{4,12},{5,13},{6,14},{7,15},{8,0},{9,1},... | collective-permute-start | bytes 294920 | tf_op jit(solution)/shard_map/ppermute | solution.py:254
  61.0 5.5 %collective-permute-done.16.refs_2_ = bf16[16,3072]{1,0:T(8,128)(2,1)S(1)} collective-permute-done((bf16[16,3072]{1,0:T(8,128)(2,1)S(1)}, bf16[16,3072]{1,0:T(8,128)(2,1)S(1)}, u32[]{:S(2)}, u32[]{:S(2)}) %collective-permute-start.16) | collective-permute-done | bytes 98336 | tf_op jit(solution)/shard_map/ppermute | solution.py:254
  66.4 0.0 collective-permute-done.15
  66.4 1.1 %collective-permute-start.17 = (bf16[16,6144]{1,0:T(8,128)(2,1)S(1)}, bf16[16,6144]{1,0:T(8,128)(2,1)S(1)}, u32[]{:S(2)}, u32[]{:S(2)}) collective-permute-start(bf16[16,6144]{1,0:T(8,128)(2,1)S(1)} %pad_maximum_fusion.2), channel_id=1, source_target_pairs={{0,2},{1,3},{2,0},{3,1},{4,6},{5,7},{6,4},{7,5},{8,10},{9,11},{10,... | collective-permute-start | bytes 589832 | tf_op jit(solution)/shard_map/ppermute | solution.py:259
  67.6 2.0 %collective-permute-start.20 = (bf16[16,6144]{1,0:T(8,128)(2,1)S(1)}, bf16[16,6144]{1,0:T(8,128)(2,1)S(1)}, u32[]{:S(2)}, u32[]{:S(2)}) collective-permute-start(bf16[16,6144]{1,0:T(8,128)(2,1)S(1)} %add_convert_fusion.3), channel_id=1, source_target_pairs={{0,12},{1,13},{2,14},{3,15},{4,0},{5,1},{6,2},{7,3},{8,4},{9,5},{1... | collective-permute-start | bytes 589832 | tf_op jit(solution)/shard_map/ppermute | solution.py:254
  69.6 2.8 %collective-permute-done.17 = bf16[16,6144]{1,0:T(8,128)(2,1)S(1)} collective-permute-done((bf16[16,6144]{1,0:T(8,128)(2,1)S(1)}, bf16[16,6144]{1,0:T(8,128)(2,1)S(1)}, u32[]{:S(2)}, u32[]{:S(2)}) %collective-permute-start.17) | collective-permute-done | bytes 196640 | tf_op jit(solution)/shard_map/ppermute | solution.py:259
  72.4 0.1 add_convert_fusion.2
  72.5 0.1 collective-permute-start.21
  72.5 0.0 collective-permute-done.18.refs_3_
  72.5 1.8 %collective-permute-start.19 = (bf16[16,6144]{1,0:T(8,128)(2,1)S(1)}, bf16[16,6144]{1,0:T(8,128)(2,1)S(1)}, u32[]{:S(2)}, u32[]{:S(2)}) collective-permute-start(bf16[16,6144]{1,0:T(8,128)(2,1)S(1)} %pad_maximum_fusion), channel_id=1, source_target_pairs={{0,2},{1,3},{2,0},{3,1},{4,6},{5,7},{6,4},{7,5},{8,10},{9,11},{10,... | collective-permute-start | bytes 589832 | tf_op jit(solution)/shard_map/ppermute | solution.py:259
  74.3 1.1 %collective-permute-done.20.near = bf16[16,6144]{1,0:T(8,128)(2,1)S(1)} collective-permute-done((bf16[16,6144]{1,0:T(8,128)(2,1)S(1)}, bf16[16,6144]{1,0:T(8,128)(2,1)S(1)}, u32[]{:S(2)}, u32[]{:S(2)}) %collective-permute-start.20) | collective-permute-done | bytes 196640 | tf_op jit(solution)/shard_map/ppermute | solution.py:254
  75.4 4.6 %collective-permute-done.21.last = bf16[16,6144]{1,0:T(8,128)(2,1)S(1)} collective-permute-done((bf16[16,6144]{1,0:T(8,128)(2,1)S(1)}, bf16[16,6144]{1,0:T(8,128)(2,1)S(1)}, u32[]{:S(2)}, u32[]{:S(2)}) %collective-permute-start.21) | collective-permute-done | bytes 196640 | tf_op jit(solution)/shard_map/ppermute | solution.py:254
  80.0 0.0 collective-permute-done.19.arrived
  80.0 0.0 copy-done
  80.0 0.0 copy-done.1
  80.0 0.0 copy-done.2
  80.0 1.4 %mix.1 = bf16[24,6144]{1,0:T(8,128)(2,1)} custom-call(s32[2,24]{1,0:T(2,128)S(1)} %bitcast.4, f32[2,24]{1,0:T(2,128)S(1)} %bitcast.5, bf16[24,6144]{1,0:T(8,128)(2,1)S(1)} %copy-done, bf16[16,6144]{1,0:T(8,128)(2,1)S(1)} %collective-permute-done.19.arrived, bf16[16,6144]{1,0:T(8,128)(2,1)S(1)} %collective-permute-done.20.near, ...), custom_call_target="tpu_custom_call" | custom-call | tf_op jit(solution)/shard_map/mix/pallas_call | solution.py:233
  (18 shorter events, 0.4 us)
Async XLA Ops:
  1.5 14.8 %collective-permute-start = (bf16[16,3072]{1,0:T(8,128)(2,1)S(1)}, bf16[16,3072]{1,0:T(8,128)(2,1)S(1)}, u32[]{:S(2)}, u32[]{:S(2)}) collective-permute-start(bf16[16,3072]{1,0:T(8,128)(2,1)S(1)} %get-tuple-element.34), channel_id=1, source_target_pairs={{0,4},{1,5},{2,6},{3,7},{4,8},{5,9},{6,10},{7,11},{8,12},{9,13},{1... | collective-permute-start | bytes 294920 | tf_op jit(solution)/shard_map/ppermute | solution.py:254
  4.6 11.7 %collective-permute-start.1 = (bf16[16,3072]{1,0:T(8,128)(2,1)S(1)}, bf16[16,3072]{1,0:T(8,128)(2,1)S(1)}, u32[]{:S(2)}, u32[]{:S(2)}) collective-permute-start(bf16[16,3072]{1,0:T(8,128)(2,1)S(1)} %get-tuple-element.35), channel_id=1, source_target_pairs={{0,8},{1,9},{2,10},{3,11},{4,12},{5,13},{6,14},{7,15},{8,0},{9,1},... | collective-permute-start | bytes 294920 | tf_op jit(solution)/shard_map/ppermute | solution.py:254
  7.2 9.1 %collective-permute-start.2 = (bf16[16,3072]{1,0:T(8,128)(2,1)S(1)}, bf16[16,3072]{1,0:T(8,128)(2,1)S(1)}, u32[]{:S(2)}, u32[]{:S(2)}) collective-permute-start(bf16[16,3072]{1,0:T(8,128)(2,1)S(1)} %get-tuple-element.36), channel_id=1, source_target_pairs={{0,12},{1,13},{2,14},{3,15},{4,0},{5,1},{6,2},{7,3},{8,4},{9,5},{1... | collective-permute-start | bytes 294920 | tf_op jit(solution)/shard_map/ppermute | solution.py:254
  8.5 17.4 %collective-permute-start.6 = (bf16[16,6144]{1,0:T(8,128)(2,1)S(1)}, bf16[16,6144]{1,0:T(8,128)(2,1)S(1)}, u32[]{:S(2)}, u32[]{:S(2)}) collective-permute-start(bf16[16,6144]{1,0:T(8,128)(2,1)S(1)} %get-tuple-element.32.after_ref.refs_0_), channel_id=1, source_target_pairs={{0,2},{1,3},{2,0},{3,1},{4,6},{5,7},{6,4},{7,5},{8,10},{9,11},{10,... | collective-permute-start | bytes 589832 | tf_op jit(solution)/shard_map/ppermute | solution.py:259
  16.3 7.5 %collective-permute-start.3 = (bf16[16,3072]{1,0:T(8,128)(2,1)S(1)}, bf16[16,3072]{1,0:T(8,128)(2,1)S(1)}, u32[]{:S(2)}, u32[]{:S(2)}) collective-permute-start(bf16[16,3072]{1,0:T(8,128)(2,1)S(1)} %get-tuple-element.37), channel_id=1, source_target_pairs={{0,4},{1,5},{2,6},{3,7},{4,8},{5,9},{6,10},{7,11},{8,12},{9,13},{1... | collective-permute-start | bytes 294920 | tf_op jit(solution)/shard_map/ppermute | solution.py:254
  17.0 8.8 %collective-permute-start.4 = (bf16[16,3072]{1,0:T(8,128)(2,1)S(1)}, bf16[16,3072]{1,0:T(8,128)(2,1)S(1)}, u32[]{:S(2)}, u32[]{:S(2)}) collective-permute-start(bf16[16,3072]{1,0:T(8,128)(2,1)S(1)} %get-tuple-element.39), channel_id=1, source_target_pairs={{0,8},{1,9},{2,10},{3,11},{4,12},{5,13},{6,14},{7,15},{8,0},{9,1},... | collective-permute-start | bytes 294920 | tf_op jit(solution)/shard_map/ppermute | solution.py:254
  17.9 7.9 %collective-permute-start.5 = (bf16[16,3072]{1,0:T(8,128)(2,1)S(1)}, bf16[16,3072]{1,0:T(8,128)(2,1)S(1)}, u32[]{:S(2)}, u32[]{:S(2)}) collective-permute-start(bf16[16,3072]{1,0:T(8,128)(2,1)S(1)} %get-tuple-element.41), channel_id=1, source_target_pairs={{0,12},{1,13},{2,14},{3,15},{4,0},{5,1},{6,2},{7,3},{8,4},{9,5},{1... | collective-permute-start | bytes 294920 | tf_op jit(solution)/shard_map/ppermute | solution.py:254
  20.2 7.1 %collective-permute-start.8 = (bf16[48,3072]{1,0:T(8,128)(2,1)S(1)}, bf16[48,3072]{1,0:T(8,128)(2,1)S(1)}, u32[]{:S(2)}, u32[]{:S(2)}) collective-permute-start(bf16[48,3072]{1,0:T(8,128)(2,1)S(1)} %get-tuple-element.42.refs_1_), channel_id=1, source_target_pairs={{0,2},{1,3},{2,0},{3,1},{4,6},{5,7},{6,4},{7,5},{8,10},{9,11},{10,... | collective-permute-start | bytes 884744 | tf_op jit(solution)/shard_map/ppermute | solution.py:259
  27.4 2.4 %collective-permute-start.9 = (bf16[128,3072]{1,0:T(8,128)(2,1)S(1)}, bf16[128,3072]{1,0:T(8,128)(2,1)S(1)}, u32[]{:S(2)}, u32[]{:S(2)}) collective-permute-start(bf16[128,3072]{1,0:T(8,128)(2,1)S(1)} %constant_dynamic-update-slice_fusion.6), channel_id=1, source_target_pairs={{0,1},{1,0},{2,3},{3,2},{4,5},{5,4},{6,7},{7,6},{8,9},{9,8},{10,11... | collective-permute-start | bytes 2359304 | tf_op jit(solution)/shard_map/ppermute | solution.py:259
  27.5 9.4 %collective-permute-start.7 = (bf16[48,3072]{1,0:T(8,128)(2,1)S(1)}, bf16[48,3072]{1,0:T(8,128)(2,1)S(1)}, u32[]{:S(2)}, u32[]{:S(2)}) collective-permute-start(bf16[48,3072]{1,0:T(8,128)(2,1)S(1)} %get-tuple-element.78.refs_1_), channel_id=1, source_target_pairs={{0,2},{1,3},{2,0},{3,1},{4,6},{5,7},{6,4},{7,5},{8,10},{9,11},{10,... | collective-permute-start | bytes 884744 | tf_op jit(solution)/shard_map/ppermute | solution.py:259
  36.9 2.4 %collective-permute-start.10 = (bf16[128,3072]{1,0:T(8,128)(2,1)S(1)}, bf16[128,3072]{1,0:T(8,128)(2,1)S(1)}, u32[]{:S(2)}, u32[]{:S(2)}) collective-permute-start(bf16[128,3072]{1,0:T(8,128)(2,1)S(1)} %constant_dynamic-update-slice_fusion.10), channel_id=1, source_target_pairs={{0,1},{1,0},{2,3},{3,2},{4,5},{5,4},{6,7},{7,6},{8,9},{9,8},{10,11... | collective-permute-start | bytes 2359304 | tf_op jit(solution)/shard_map/ppermute | solution.py:259
  47.6 3.8 %collective-permute-start.11 = (bf16[128,3072]{1,0:T(8,128)(2,1)S(1)}, bf16[128,3072]{1,0:T(8,128)(2,1)S(1)}, u32[]{:S(2)}, u32[]{:S(2)}) collective-permute-start(bf16[128,3072]{1,0:T(8,128)(2,1)S(1)} %get-tuple-element.53), channel_id=1, source_target_pairs={{0,1},{1,0},{2,3},{3,2},{4,5},{5,4},{6,7},{7,6},{8,9},{9,8},{10,11... | collective-permute-start | bytes 2359304 | tf_op jit(solution)/shard_map/ppermute | solution.py:259
  50.9 29.1 %copy-start = (bf16[24,6144]{1,0:T(8,128)(2,1)S(1)}, bf16[24,6144]{1,0:T(8,128)(2,1)}, u32[]{:S(2)}) copy-start(bf16[24,6144]{1,0:T(8,128)(2,1)} %act_ref.3) | copy-start | bytes 884740
  50.9 29.1 %copy-start.1 = (s32[24,2]{0,1:T(2,128)S(1)}, s32[24,2]{0,1:T(2,128)}, u32[]{:S(2)}) copy-start(s32[24,2]{0,1:T(2,128)} %param.8) | copy-start | bytes 580
  50.9 29.1 %copy-start.2 = (f32[24,2]{0,1:T(2,128)S(1)}, f32[24,2]{0,1:T(2,128)}, u32[]{:S(2)}) copy-start(f32[24,2]{0,1:T(2,128)} %param.9) | copy-start | bytes 580
  50.9 2.4 %collective-permute-start.12 = (bf16[128,3072]{1,0:T(8,128)(2,1)S(1)}, bf16[128,3072]{1,0:T(8,128)(2,1)S(1)}, u32[]{:S(2)}, u32[]{:S(2)}) collective-permute-start(bf16[128,3072]{1,0:T(8,128)(2,1)S(1)} %get-tuple-element.55), channel_id=1, source_target_pairs={{0,1},{1,0},{2,3},{3,2},{4,5},{5,4},{6,7},{7,6},{8,9},{9,8},{10,11... | collective-permute-start | bytes 2359304 | tf_op jit(solution)/shard_map/ppermute | solution.py:259
  51.6 4.9 %collective-permute-start.13 = (bf16[16,3072]{1,0:T(8,128)(2,1)S(1)}, bf16[16,3072]{1,0:T(8,128)(2,1)S(1)}, u32[]{:S(2)}, u32[]{:S(2)}) collective-permute-start(bf16[16,3072]{1,0:T(8,128)(2,1)S(1)} %get-tuple-element.71), channel_id=1, source_target_pairs={{0,2},{1,3},{2,0},{3,1},{4,6},{5,7},{6,4},{7,5},{8,10},{9,11},{10,... | collective-permute-start | bytes 294920 | tf_op jit(solution)/shard_map/ppermute | solution.py:259
  53.5 5.1 %collective-permute-start.14 = (bf16[16,3072]{1,0:T(8,128)(2,1)S(1)}, bf16[16,3072]{1,0:T(8,128)(2,1)S(1)}, u32[]{:S(2)}, u32[]{:S(2)}) collective-permute-start(bf16[16,3072]{1,0:T(8,128)(2,1)S(1)} %get-tuple-element.64), channel_id=1, source_target_pairs={{0,2},{1,3},{2,0},{3,1},{4,6},{5,7},{6,4},{7,5},{8,10},{9,11},{10,... | collective-permute-start | bytes 294920 | tf_op jit(solution)/shard_map/ppermute | solution.py:259
  56.5 9.9 %collective-permute-start.16 = (bf16[16,3072]{1,0:T(8,128)(2,1)S(1)}, bf16[16,3072]{1,0:T(8,128)(2,1)S(1)}, u32[]{:S(2)}, u32[]{:S(2)}) collective-permute-start(bf16[16,3072]{1,0:T(8,128)(2,1)S(1)} %add_convert_fusion.5), channel_id=1, source_target_pairs={{0,8},{1,9},{2,10},{3,11},{4,12},{5,13},{6,14},{7,15},{8,0},{9,1},... | collective-permute-start | bytes 294920 | tf_op jit(solution)/shard_map/ppermute | solution.py:254
  58.6 7.8 %collective-permute-start.15 = (bf16[16,6144]{1,0:T(8,128)(2,1)S(1)}, bf16[16,6144]{1,0:T(8,128)(2,1)S(1)}, u32[]{:S(2)}, u32[]{:S(2)}) collective-permute-start(bf16[16,6144]{1,0:T(8,128)(2,1)S(1)} %pad_maximum_fusion.1), channel_id=1, source_target_pairs={{0,2},{1,3},{2,0},{3,1},{4,6},{5,7},{6,4},{7,5},{8,10},{9,11},{10,... | collective-permute-start | bytes 589832 | tf_op jit(solution)/shard_map/ppermute | solution.py:259
  60.0 12.5 %collective-permute-start.18 = (bf16[16,3072]{1,0:T(8,128)(2,1)S(1)}, bf16[16,3072]{1,0:T(8,128)(2,1)S(1)}, u32[]{:S(2)}, u32[]{:S(2)}) collective-permute-start(bf16[16,3072]{1,0:T(8,128)(2,1)S(1)} %add_convert_fusion.4), channel_id=1, source_target_pairs={{0,8},{1,9},{2,10},{3,11},{4,12},{5,13},{6,14},{7,15},{8,0},{9,1},... | collective-permute-start | bytes 294920 | tf_op jit(solution)/shard_map/ppermute | solution.py:254
  66.4 6.0 %collective-permute-start.17 = (bf16[16,6144]{1,0:T(8,128)(2,1)S(1)}, bf16[16,6144]{1,0:T(8,128)(2,1)S(1)}, u32[]{:S(2)}, u32[]{:S(2)}) collective-permute-start(bf16[16,6144]{1,0:T(8,128)(2,1)S(1)} %pad_maximum_fusion.2), channel_id=1, source_target_pairs={{0,2},{1,3},{2,0},{3,1},{4,6},{5,7},{6,4},{7,5},{8,10},{9,11},{10,... | collective-permute-start | bytes 589832 | tf_op jit(solution)/shard_map/ppermute | solution.py:259
  67.6 7.8 %collective-permute-start.20 = (bf16[16,6144]{1,0:T(8,128)(2,1)S(1)}, bf16[16,6144]{1,0:T(8,128)(2,1)S(1)}, u32[]{:S(2)}, u32[]{:S(2)}) collective-permute-start(bf16[16,6144]{1,0:T(8,128)(2,1)S(1)} %add_convert_fusion.3), channel_id=1, source_target_pairs={{0,12},{1,13},{2,14},{3,15},{4,0},{5,1},{6,2},{7,3},{8,4},{9,5},{1... | collective-permute-start | bytes 589832 | tf_op jit(solution)/shard_map/ppermute | solution.py:254
  72.5 7.5 %collective-permute-start.21 = (bf16[16,6144]{1,0:T(8,128)(2,1)S(1)}, bf16[16,6144]{1,0:T(8,128)(2,1)S(1)}, u32[]{:S(2)}, u32[]{:S(2)}) collective-permute-start(bf16[16,6144]{1,0:T(8,128)(2,1)S(1)} %add_convert_fusion.2), channel_id=1, source_target_pairs={{0,4},{1,5},{2,6},{3,7},{4,8},{5,9},{6,10},{7,11},{8,12},{9,13},{1... | collective-permute-start | bytes 589832 | tf_op jit(solution)/shard_map/ppermute | solution.py:254
  72.5 7.4 %collective-permute-start.19 = (bf16[16,6144]{1,0:T(8,128)(2,1)S(1)}, bf16[16,6144]{1,0:T(8,128)(2,1)S(1)}, u32[]{:S(2)}, u32[]{:S(2)}) collective-permute-start(bf16[16,6144]{1,0:T(8,128)(2,1)S(1)} %pad_maximum_fusion), channel_id=1, source_target_pairs={{0,2},{1,3},{2,0},{3,1},{4,6},{5,7},{6,4},{7,5},{8,10},{9,11},{10,... | collective-permute-start | bytes 589832 | tf_op jit(solution)/shard_map/ppermute | solution.py:259

commit v9 on v8

--- a/solution.py
+++ b/solution.py
@@ -13,7 +13,8 @@
 BLOCK = 1024
 FETCH_ROWS = 144
 MIB = 1 << 20
-LIMIT = pltpu.CompilerParams(vmem_limit_bytes=16 * MIB)
+LIMIT = pltpu.CompilerParams(vmem_limit_bytes=10 * MIB)
+WIDE = pltpu.CompilerParams(vmem_limit_bytes=32 * MIB)
 VMEM = pl.BlockSpec(memory_space=pltpu.VMEM)
 ANY = pl.BlockSpec(memory_space=pl.ANY)
 
@@ -99,7 +100,7 @@
     )(pltpu.with_memory_space_constraint(w, pltpu.HBM), after)
 
 
-def gate_up_kernel(count, ahead, at, begin, end, *refs):
+def gate_up_kernel(count, ahead, at, ahead_at, begin, end, *refs):
     pieces, refs = refs[:count], refs[count:]
     weights, later, refs = refs[:2], refs[2 : 2 + ahead], refs[2 + ahead :]
     if not begin:
@@ -109,30 +110,19 @@
     if end:
         hidden_ref, refs = refs[0], refs[1:]
     sums = refs
-    steps, block, _ = turned.shape
-    copies = fetches(later, 0 if end else steps * block, held, sems)
+    part, rows = turned.shape
+    copies = fetches(later, ahead_at, held, sems)
     for copy in copies:
         copy.start()
-
-    @pl.loop(0, steps)
-    def _(c):
+    for c in range(0, part, BLOCK):
         parts = []
         for p in pieces:
-            first = at if p.shape[1] > steps * block else 0
-            parts.append(p[:, pl.ds(pl.multiple_of(first + c * block, block), block)])
-        turned[c] = jnp.concatenate(parts, axis=0).T
-
+            first = c + (at if p.shape[1] > part else 0)
+            parts.append(p[:, first : first + BLOCK])
+        turned[c : c + BLOCK, :] = jnp.concatenate(parts, axis=0).T
     for j in range(2):
-        sums[j][...] = jnp.zeros_like(sums[j]) if begin else before[j][...]
-
-    @pl.loop(0, steps)
-    def _(c):
-        columns = pl.ds(pl.multiple_of(c * block, block), block)
-        for j in range(2):
-            sums[j][...] += jnp.dot(
-                weights[j][:, columns], turned[c], preferred_element_type=jnp.float32
-            )
-
+        total = jnp.dot(weights[j][...], turned[...], preferred_element_type=jnp.float32)
+        sums[j][...] = total if begin else total + before[j][...]
     if end:
         hidden = (jax.nn.silu(sums[0][...]) * sums[1][...]).astype(jnp.bfloat16)
         hidden_ref[...] = hidden.T
@@ -145,8 +135,7 @@
     begin, end = k == 0, k == HALVES - 1
     rows = sum(p.shape[0] for p in pieces)
     total = jax.ShapeDtypeStruct((hidden, rows), jnp.float32)
-    width = later[0].shape[1] if end else part
-    out_shape = [pltpu.VMEM((hidden, width), jnp.bfloat16)] * len(later)
+    out_shape = [pltpu.VMEM((hidden, part), jnp.bfloat16)] * len(later)
     out_specs = [VMEM] * len(later)
     scratch = []
     if end:
@@ -155,17 +144,19 @@
     else:
         out_shape += [total] * 2
     out_specs += [VMEM] * (len(out_shape) - len(later))
-    scratch.append(pltpu.VMEM((part // BLOCK, BLOCK, rows), jnp.bfloat16))
+    scratch.append(pltpu.VMEM((part, rows), jnp.bfloat16))
     scratch.append(pltpu.SemaphoreType.DMA((len(later), hidden // FETCH_ROWS)))
     weights = [pltpu.with_memory_space_constraint(w, pltpu.VMEM) for w in weights]
     later = [pltpu.with_memory_space_constraint(w, pltpu.HBM) for w in later]
     out = pl.pallas_call(
-        functools.partial(gate_up_kernel, len(pieces), len(later), k * part, begin, end),
+        functools.partial(
+            gate_up_kernel, len(pieces), len(later), k * part, 0 if end else part, begin, end
+        ),
         in_specs=[VMEM] * (len(pieces) + 2) + [ANY] * len(later) + [VMEM] * len(totals),
         out_specs=out_specs,
         out_shape=out_shape,
         scratch_shapes=scratch,
-        compiler_params=LIMIT,
+        compiler_params=LIMIT if rows <= 256 else WIDE,
         cost_estimate=pl.CostEstimate(
             flops=4 * rows * hidden * part,
             bytes_accessed=4 * hidden * part + 8 * rows * hidden,
@@ -176,34 +167,46 @@
     return out[: len(later)], out[len(later) :]
 
 
-def down_kernel(at, hidden_ref, w_ref, keep_ref, send_ref):
+def down_kernel(ahead, hidden_ref, w_ref, *refs):
+    later, held, refs = refs[:ahead], refs[ahead : 2 * ahead], refs[2 * ahead :]
+    keep_ref, send_ref, sems = refs
     half, part = keep_ref.shape
-    block = BLOCK // 2
-
-    @pl.loop(0, part // block)
-    def _(c):
-        columns = pl.ds(pl.multiple_of(at + c * block, block), block)
+    copies = fetches(later, part, held, sems)
+    for copy in copies:
+        copy.start()
+    for c in range(0, part, BLOCK):
+        columns = slice(c, c + BLOCK)
         out = jnp.dot(hidden_ref[...], w_ref[:, columns], preferred_element_type=jnp.float32)
         out = out.astype(jnp.bfloat16)
-        columns = pl.ds(pl.multiple_of(c * block, block), block)
         keep_ref[:, columns] = out[:half]
         send_ref[:, columns] = out[half:]
-
-
-def down(at, part, hidden, w_down):
+    for copy in copies:
+        copy.wait()
+
+
+def down(hidden, w_down, later):
     rows, depth = hidden.shape
-    return pl.pallas_call(
-        functools.partial(down_kernel, at),
-        in_specs=[VMEM, VMEM],
-        out_shape=[jax.ShapeDtypeStruct((rows // 2, part), jnp.bfloat16)] * 2,
-        compiler_params=LIMIT,
+    part = w_down.shape[1]
+    ahead = len(later)
+    out_shape = [pltpu.VMEM((depth, part), jnp.bfloat16)] * ahead
+    out_shape += [jax.ShapeDtypeStruct((rows // 2, part), jnp.bfloat16)] * 2
+    w_down = pltpu.with_memory_space_constraint(w_down, pltpu.VMEM)
+    later = [pltpu.with_memory_space_constraint(w, pltpu.HBM) for w in later]
+    out = pl.pallas_call(
+        functools.partial(down_kernel, ahead),
+        in_specs=[VMEM, VMEM] + [ANY] * ahead,
+        out_specs=[VMEM] * (ahead + 2),
+        out_shape=out_shape,
+        scratch_shapes=[pltpu.SemaphoreType.DMA((max(ahead, 1), depth // FETCH_ROWS))],
+        compiler_params=LIMIT if rows <= 256 else WIDE,
         cost_estimate=pl.CostEstimate(
             flops=2 * rows * depth * part,
             bytes_accessed=2 * (depth * part + rows * depth + rows * part),
             transcendentals=0,
         ),
         name="down",
-    )(hidden, pltpu.with_memory_space_constraint(w_down, pltpu.VMEM))
+    )(hidden, w_down, *later)
+    return out[:ahead], out[ahead:]
 
 
 def mix_kernel(group, ids_ref, logits_ref, act_ref, arrived, near, last, *refs):
@@ -213,19 +216,20 @@
     lead = logits_ref[0:1, :] - logits_ref[1:2, :]
     weight = jnp.where(first, jax.nn.sigmoid(lead), 0.0)
     weight = (weight + jnp.where(second, jax.nn.sigmoid(-lead), 0.0)).T
-    high = weight.astype(jnp.bfloat16)
-    rest = weight - high.astype(jnp.float32)
-    middle = rest.astype(jnp.bfloat16)
-    low = (rest - middle.astype(jnp.float32)).astype(jnp.bfloat16)
+    tokens = weight.shape[0]
+    high = weight.astype(jnp.bfloat16).astype(jnp.float32)
+    middle = (weight - high).astype(jnp.bfloat16).astype(jnp.float32)
+    terms = jnp.concatenate([weight - high - middle, middle, high], axis=0).astype(jnp.bfloat16)
     part = kept[0].shape[1]
     for k in range(HALVES):
         columns = slice(k * part, (k + 1) * part)
         own = kept[k][...].astype(jnp.float32) + arrived[:, columns].astype(jnp.float32)
         blocks = [own.astype(jnp.bfloat16), near[:, columns], middle_rows[k][...]]
         rows = jnp.concatenate(blocks + [last[:, columns]], axis=0)
+        sums = jnp.dot(terms, rows, preferred_element_type=jnp.float32)
         total = act_ref[:, columns].astype(jnp.float32)
-        for term in (low, middle, high):
-            total = total + jnp.dot(term, rows, preferred_element_type=jnp.float32)
+        for j in range(3):
+            total = total + sums[j * tokens : (j + 1) * tokens]
         out_ref[:, columns] = total.astype(jnp.bfloat16)
 
 
@@ -290,10 +294,11 @@
             pieces[1] = after(pieces[1], blocks[k + 1])
         later = [w_down] if k == HALVES - 1 else [w_gate, w_up]
         now, totals = gate_up(k, pieces, now, later, totals)
-    hidden, (down_w,) = totals[0], now
+    hidden = totals[0]
     held = []
     for k in range(HALVES):
-        keep, send = down(k * part, part, hidden, down_w)
+        later = [w_down] if k < HALVES - 1 else []
+        now, (keep, send) = down(hidden, now[0], later)
         bit = 1
         while bit < far:
             total = added(keep, swap(send, bit))
@@ -304,7 +309,7 @@
     middle = [shift(added(h[2], x), -2) for h, x in zip(held, crossed)]
     mine = [jnp.concatenate([h[j] for h in held], axis=1) for j in range(2 * EXPERTS)]
     back = {}
-    for s, ready in ((1, []), (3, middle[:1]), (0, middle)):
+    for s, ready in ((1, []), (3, []), (0, middle)):
         crossed.append(swap(after(mine[EXPERTS + s], *crossed, *ready), far))
         back[s] = crossed[-1]
     near = shift(added(mine[1], back[1]), -1)

time: 81.5 us -> 87.2 us (1.070)
  Pallas kernels: 25.6 us -> 31.8 us
    pallas_call x2, Pallas kernels: 10.4 us -> 15.5 us  [gate_up(): pl.pallas_call(functools.partial(gate_up_kernel, len(pieces), len(later),...]
    ppermute x10, waiting for transfers between devices: 16.2 us -> 11.6 us  [shift(): lax.ppermute(x, 'expert', [(i, (i + s * group) % devices) for i in range(...]
    ppermute x12, waiting for transfers between devices: 11.5 us -> 15.5 us  [swap(): return lax.ppermute(x, 'expert', [(i, i ^ bit) for i in range(devices)])]
    ppermute x12, starting transfers between devices: 11.4 us -> 10 us  [swap(): return lax.ppermute(x, 'expert', [(i, i ^ bit) for i in range(devices)])]
    ppermute x10, starting transfers between devices: 15.7 us -> 16.9 us  [shift(): lax.ppermute(x, 'expert', [(i, (i + s * group) % devices) for i in range(...]
    pallas_call x2, Pallas kernels: 6.13 us -> 7.32 us  [down(): pl.pallas_call(functools.partial(down_kernel, ahead), in_specs=[VMEM, VME...]
  transfers between devices with their start and end apart: 22 -> 22, of which waited for: 13 -> 11; matrix products, arithmetic and copies ran while one was open for 1% -> 1% of each run, Pallas kernels for 18% -> 20%
where the time goes in v9:
time: 87.2 us; the launch traced here: 87 us
  Pallas kernels  31.8 us (36%)
  waiting for transfers between devices  27.2 us (31%)
  starting transfers between devices  27 us (31%)
    ppermute x10, starting transfers between devices, shift(): lax.ppermute(x, 'expert', [(i, (i + s * group) % devices) for i in range(...  16.9 us
    ppermute x12, waiting for transfers between devices, swap(): return lax.ppermute(x, 'expert', [(i, i ^ bit) for i in range(devices)])  15.5 us
    pallas_call x2, Pallas kernels, gate_up(): pl.pallas_call(functools.partial(gate_up_kernel, len(pieces), len(later),...  15.5 us
    ppermute x10, waiting for transfers between devices, shift(): lax.ppermute(x, 'expert', [(i, (i + s * group) % devices) for i in range(...  11.6 us
    ppermute x12, starting transfers between devices, swap(): return lax.ppermute(x, 'expert', [(i, i ^ bit) for i in range(devices)])  10 us
    pallas_call x2, Pallas kernels, down(): pl.pallas_call(functools.partial(down_kernel, ahead), in_specs=[VMEM, VME...  7.32 us
    pallas_call x2, Pallas kernels, fetch(): pl.pallas_call(functools.partial(fetch_kernel, at), in_specs=[ANY, ANY],...  6.19 us
  transfers between devices with their start and end apart: 22, of which 11 were waited for; matrix products, arithmetic and copies ran while one was open for 1% of the time, Pallas kernels for 20%

profile of v9, /device:TPU:0, one launch (start us, length us, event | category | flops | bytes accessed | tf_op | source)
XLA Modules:
  0.0 87.0 jit_solution(13508943491081175914)
XLA Ops:
  0.0 1.5 %norm_and_pack.1 = (bf16[16,6144]{1,0:T(8,128)(2,1)S(1)}, bf16[16,3072]{1,0:T(8,128)(2,1)S(1)}, bf16[16,3072]{1,0:T(8,128)(2,1)S(1)}, bf16[16,3072]{1,0:T(8,128)...) custom-call(s32[2,24]{1,0:T(2,128)} %bitcast.3, ...), custom_call_target="tpu_custom_call" | custom-call | tf_op jit(solution)/shard_map/norm_and_pack/pallas_call | solution.py:58
  1.5 3.1 %collective-permute-start = (bf16[16,3072]{1,0:T(8,128)(2,1)S(1)}, bf16[16,3072]{1,0:T(8,128)(2,1)S(1)}, u32[]{:S(2)}, u32[]{:S(2)}) collective-permute-start(bf16[16,3072]{1,0:T(8,128)(2,1)S(1)} %get-tuple-element.35), channel_id=1, source_target_pairs={{0,4},{1,5},{2,6},{3,7},{4,8},{5,9},{6,10},{7,11},{8,12},{9,13},{1... | collective-permute-start | bytes 294920 | tf_op jit(solution)/shard_map/ppermute | solution.py:258
  4.6 2.6 %collective-permute-start.1 = (bf16[16,3072]{1,0:T(8,128)(2,1)S(1)}, bf16[16,3072]{1,0:T(8,128)(2,1)S(1)}, u32[]{:S(2)}, u32[]{:S(2)}) collective-permute-start(bf16[16,3072]{1,0:T(8,128)(2,1)S(1)} %get-tuple-element.36), channel_id=1, source_target_pairs={{0,8},{1,9},{2,10},{3,11},{4,12},{5,13},{6,14},{7,15},{8,0},{9,1},... | collective-permute-start | bytes 294920 | tf_op jit(solution)/shard_map/ppermute | solution.py:258
  7.2 1.3 %collective-permute-start.2 = (bf16[16,3072]{1,0:T(8,128)(2,1)S(1)}, bf16[16,3072]{1,0:T(8,128)(2,1)S(1)}, u32[]{:S(2)}, u32[]{:S(2)}) collective-permute-start(bf16[16,3072]{1,0:T(8,128)(2,1)S(1)} %get-tuple-element.37), channel_id=1, source_target_pairs={{0,12},{1,13},{2,14},{3,15},{4,0},{5,1},{6,2},{7,3},{8,4},{9,5},{1... | collective-permute-start | bytes 294920 | tf_op jit(solution)/shard_map/ppermute | solution.py:258
  8.5 1.5 %collective-permute-start.6 = (bf16[16,6144]{1,0:T(8,128)(2,1)S(1)}, bf16[16,6144]{1,0:T(8,128)(2,1)S(1)}, u32[]{:S(2)}, u32[]{:S(2)}) collective-permute-start(bf16[16,6144]{1,0:T(8,128)(2,1)S(1)} %get-tuple-element.33.after_ref.refs_0_), channel_id=1, source_target_pairs={{0,2},{1,3},{2,0},{3,1},{4,6},{5,7},{6,4},{7,5},{8,10},{9,11},{10,... | collective-permute-start | bytes 589832 | tf_op jit(solution)/shard_map/ppermute | solution.py:263
  10.0 3.1 %fetch.2.refs_5_ = bf16[1152,3072]{1,0:T(8,128)(2,1)S(1)} custom-call(bf16[1152,6144]{1,0:T(8,128)(2,1)} %refs_7_.2, bf16[16,6144]{1,0:T(8,128)(2,1)S(1)} %get-tuple-element.33.after_ref.refs_0_), custom_call_target="tpu_custom_call" | custom-call | bytes 14155776 | tf_op jit(solution)/shard_map/fetch/pallas_call | solution.py:91
  13.1 3.1 %fetch.3.refs_6_ = bf16[1152,3072]{1,0:T(8,128)(2,1)S(1)} custom-call(bf16[1152,6144]{1,0:T(8,128)(2,1)} %refs_8_.1, bf16[16,6144]{1,0:T(8,128)(2,1)S(1)} %get-tuple-element.33.after_ref.refs_0_), custom_call_target="tpu_custom_call" | custom-call | bytes 14155776 | tf_op jit(solution)/shard_map/fetch/pallas_call | solution.py:91
  16.2 0.0 collective-permute-done
  16.3 0.0 collective-permute-done.1
  16.3 0.0 collective-permute-done.2
  16.3 0.7 collective-permute-start.3
  17.0 0.9 %collective-permute-start.4 = (bf16[16,3072]{1,0:T(8,128)(2,1)S(1)}, bf16[16,3072]{1,0:T(8,128)(2,1)S(1)}, u32[]{:S(2)}, u32[]{:S(2)}) collective-permute-start(bf16[16,3072]{1,0:T(8,128)(2,1)S(1)} %get-tuple-element.40), channel_id=1, source_target_pairs={{0,8},{1,9},{2,10},{3,11},{4,12},{5,13},{6,14},{7,15},{8,0},{9,1},... | collective-permute-start | bytes 294920 | tf_op jit(solution)/shard_map/ppermute | solution.py:258
  17.9 2.2 %collective-permute-start.5 = (bf16[16,3072]{1,0:T(8,128)(2,1)S(1)}, bf16[16,3072]{1,0:T(8,128)(2,1)S(1)}, u32[]{:S(2)}, u32[]{:S(2)}) collective-permute-start(bf16[16,3072]{1,0:T(8,128)(2,1)S(1)} %get-tuple-element.42), channel_id=1, source_target_pairs={{0,12},{1,13},{2,14},{3,15},{4,0},{5,1},{6,2},{7,3},{8,4},{9,5},{1... | collective-permute-start | bytes 294920 | tf_op jit(solution)/shard_map/ppermute | solution.py:258
  20.2 0.6 collective-permute-start.8
  20.8 3.0 %collective-permute-done.3 = bf16[16,3072]{1,0:T(8,128)(2,1)S(1)} collective-permute-done((bf16[16,3072]{1,0:T(8,128)(2,1)S(1)}, bf16[16,3072]{1,0:T(8,128)(2,1)S(1)}, u32[]{:S(2)}, u32[]{:S(2)}) %collective-permute-start.3) | collective-permute-done | bytes 98336 | tf_op jit(solution)/shard_map/ppermute | solution.py:258
  23.8 2.0 %collective-permute-done.4 = bf16[16,3072]{1,0:T(8,128)(2,1)S(1)} collective-permute-done((bf16[16,3072]{1,0:T(8,128)(2,1)S(1)}, bf16[16,3072]{1,0:T(8,128)(2,1)S(1)}, u32[]{:S(2)}, u32[]{:S(2)}) %collective-permute-start.4) | collective-permute-done | bytes 98336 | tf_op jit(solution)/shard_map/ppermute | solution.py:258
  25.9 0.0 collective-permute-done.5
  25.9 0.0 collective-permute-done.6.refs_2_
  25.9 1.4 %collective-permute-done.8.refs_3_ = bf16[48,3072]{1,0:T(8,128)(2,1)S(1)} collective-permute-done((bf16[48,3072]{1,0:T(8,128)(2,1)S(1)}, bf16[48,3072]{1,0:T(8,128)(2,1)S(1)}, u32[]{:S(2)}, u32[]{:S(2)}) %collective-permute-start.8) | collective-permute-done | bytes 294944 | tf_op jit(solution)/shard_map/ppermute | solution.py:263
  27.4 0.1 collective-permute-start.9
  27.5 1.4 %collective-permute-start.7 = (bf16[48,3072]{1,0:T(8,128)(2,1)S(1)}, bf16[48,3072]{1,0:T(8,128)(2,1)S(1)}, u32[]{:S(2)}, u32[]{:S(2)}) collective-permute-start(bf16[48,3072]{1,0:T(8,128)(2,1)S(1)} %get-tuple-element.80.refs_1_), channel_id=1, source_target_pairs={{0,2},{1,3},{2,0},{3,1},{4,6},{5,7},{6,4},{7,5},{8,10},{9,11},{10,... | collective-permute-start | bytes 884744 | tf_op jit(solution)/shard_map/ppermute | solution.py:263
  28.9 0.9 collective-permute-done.9.refs_4_
  29.7 8.8 %gate_up.2 = (bf16[1152,3072]{1,0:T(8,128)(2,1)S(1)}, bf16[1152,3072]{1,0:T(8,128)(2,1)S(1)}, f32[1152,256]{1,0:T(8,128)S(1)}, f32[1152,256]{1,0:T(8,128)S(1)}) custom-call(bf16[16,6144]{1,0:T(8,128)(2,1)S(1)} %get-tuple-element.33.after_ref.refs_0_, bf16[48,3072]{1,0:T(8,128)(2,1)S(1)} %get-tuple-element.43.refs_1_, ...), custom_call_target="tpu_custom_call" | custom-call | flops 3623878656 | bytes 16515072 | tf_op jit(solution)/shard_map/gate_up/pallas_call | solution.py:151
  38.5 0.0 collective-permute-done.7.refs_3_
  38.6 0.2 collective-permute-start.10
  38.8 2.1 %collective-permute-done.10.refs_4_ = bf16[128,3072]{1,0:T(8,128)(2,1)S(1)} collective-permute-done((bf16[128,3072]{1,0:T(8,128)(2,1)S(1)}, bf16[128,3072]{1,0:T(8,128)(2,1)S(1)}, u32[]{:S(2)}, u32[]{:S(2)}) %collective-permute-start.10) | collective-permute-done | bytes 786464 | tf_op jit(solution)/shard_map/ppermute | solution.py:263
  40.9 6.7 %gate_up.3 = (bf16[1152,3072]{1,0:T(8,128)(2,1)S(1)}, bf16[256,1152]{1,0:T(8,128)(2,1)S(1)}) custom-call(bf16[16,6144]{1,0:T(8,128)(2,1)S(1)} %get-tuple-element.33.after_ref.refs_0_, bf16[48,3072]{1,0:T(8,128)(2,1)S(1)} %get-tuple-element.80.refs_1_, bf16[16,6144]{1,0:T(8,128)(2,1)S(1)} %collective-permute-done.6.refs_2_, ...), custom_call_target="tpu_custom_call" | custom-call | flops 3623878656 | bytes 16515072 | tf_op jit(solution)/shard_map/gate_up/pallas_call | solution.py:151
  47.6 5.1 %down.2 = (bf16[1152,3072]{1,0:T(8,128)(2,1)S(1)}, bf16[128,3072]{1,0:T(8,128)(2,1)S(1)}, bf16[128,3072]{1,0:T(8,128)(2,1)S(1)}) custom-call(bf16[256,1152]{1,0:T(8,128)(2,1)S(1)} %get-tuple-element.51.hidden_ref, bf16[1152,3072]{1,0:T(8,128)(2,1)S(1)} %get-tuple-element.52.w_ref, bf16[1152,6144]{1,0:T(8,128)(2,1)} %refs_0_.1), custom_call_target="tpu_custom_call" | custom-call | flops 1811939328 | bytes 9240576 | tf_op jit(solution)/shard_map/down/pallas_call | solution.py:195
  52.7 0.2 collective-permute-start.11
  52.9 2.3 %down.3 = (bf16[128,3072]{1,0:T(8,128)(2,1)S(1)}, bf16[128,3072]{1,0:T(8,128)(2,1)S(1)}) custom-call(bf16[256,1152]{1,0:T(8,128)(2,1)S(1)} %get-tuple-element.51.hidden_ref, bf16[1152,3072]{1,0:T(8,128)(2,1)S(1)} %get-tuple-element.55.w_ref), custom_call_target="tpu_custom_call" | custom-call | flops 1811939328 | bytes 9240576 | tf_op jit(solution)/shard_map/down/pallas_call | solution.py:195
  55.2 0.0 copy-start
  55.2 0.0 copy-start.1
  55.2 0.0 copy-start.2
  55.2 0.4 collective-permute-start.12
  55.6 0.0 collective-permute-done.11
  55.6 0.2 add_convert_fusion.1
  55.9 1.7 %collective-permute-done.12 = bf16[128,3072]{1,0:T(8,128)(2,1)S(1)} collective-permute-done((bf16[128,3072]{1,0:T(8,128)(2,1)S(1)}, bf16[128,3072]{1,0:T(8,128)(2,1)S(1)}, u32[]{:S(2)}, u32[]{:S(2)}) %collective-permute-start.12) | collective-permute-done | bytes 786464 | tf_op jit(solution)/shard_map/ppermute | solution.py:263
  57.5 0.2 add_convert_fusion
  57.8 1.4 %collective-permute-start.13 = (bf16[16,3072]{1,0:T(8,128)(2,1)S(1)}, bf16[16,3072]{1,0:T(8,128)(2,1)S(1)}, u32[]{:S(2)}, u32[]{:S(2)}) collective-permute-start(bf16[16,3072]{1,0:T(8,128)(2,1)S(1)} %get-tuple-element.73), channel_id=1, source_target_pairs={{0,2},{1,3},{2,0},{3,1},{4,6},{5,7},{6,4},{7,5},{8,10},{9,11},{10,... | collective-permute-start | bytes 294920 | tf_op jit(solution)/shard_map/ppermute | solution.py:263
  59.2 0.7 collective-permute-start.14
  60.0 3.5 %collective-permute-done.13 = bf16[16,3072]{1,0:T(8,128)(2,1)S(1)} collective-permute-done((bf16[16,3072]{1,0:T(8,128)(2,1)S(1)}, bf16[16,3072]{1,0:T(8,128)(2,1)S(1)}, u32[]{:S(2)}, u32[]{:S(2)}) %collective-permute-start.13) | collective-permute-done | bytes 98336 | tf_op jit(solution)/shard_map/ppermute | solution.py:263
  63.5 1.6 %collective-permute-done.14 = bf16[16,3072]{1,0:T(8,128)(2,1)S(1)} collective-permute-done((bf16[16,3072]{1,0:T(8,128)(2,1)S(1)}, bf16[16,3072]{1,0:T(8,128)(2,1)S(1)}, u32[]{:S(2)}, u32[]{:S(2)}) %collective-permute-start.14) | collective-permute-done | bytes 98336 | tf_op jit(solution)/shard_map/ppermute | solution.py:263
  65.0 1.4 %collective-permute-start.15 = (bf16[16,6144]{1,0:T(8,128)(2,1)S(1)}, bf16[16,6144]{1,0:T(8,128)(2,1)S(1)}, u32[]{:S(2)}, u32[]{:S(2)}) collective-permute-start(bf16[16,6144]{1,0:T(8,128)(2,1)S(1)} %pad_maximum_fusion.1), channel_id=1, source_target_pairs={{0,2},{1,3},{2,0},{3,1},{4,6},{5,7},{6,4},{7,5},{8,10},{9,11},{10,... | collective-permute-start | bytes 589832 | tf_op jit(solution)/shard_map/ppermute | solution.py:263
  66.4 1.0 %collective-permute-start.18 = (bf16[16,3072]{1,0:T(8,128)(2,1)S(1)}, bf16[16,3072]{1,0:T(8,128)(2,1)S(1)}, u32[]{:S(2)}, u32[]{:S(2)}) collective-permute-start(bf16[16,3072]{1,0:T(8,128)(2,1)S(1)} %add_convert_fusion.4), channel_id=1, source_target_pairs={{0,8},{1,9},{2,10},{3,11},{4,12},{5,13},{6,14},{7,15},{8,0},{9,1},... | collective-permute-start | bytes 294920 | tf_op jit(solution)/shard_map/ppermute | solution.py:258
  67.4 2.1 %collective-permute-start.17 = (bf16[16,3072]{1,0:T(8,128)(2,1)S(1)}, bf16[16,3072]{1,0:T(8,128)(2,1)S(1)}, u32[]{:S(2)}, u32[]{:S(2)}) collective-permute-start(bf16[16,3072]{1,0:T(8,128)(2,1)S(1)} %add_convert_fusion.5), channel_id=1, source_target_pairs={{0,8},{1,9},{2,10},{3,11},{4,12},{5,13},{6,14},{7,15},{8,0},{9,1},... | collective-permute-start | bytes 294920 | tf_op jit(solution)/shard_map/ppermute | solution.py:258
  69.5 1.9 %collective-permute-done.15 = bf16[16,6144]{1,0:T(8,128)(2,1)S(1)} collective-permute-done((bf16[16,6144]{1,0:T(8,128)(2,1)S(1)}, bf16[16,6144]{1,0:T(8,128)(2,1)S(1)}, u32[]{:S(2)}, u32[]{:S(2)}) %collective-permute-start.15) | collective-permute-done | bytes 196640 | tf_op jit(solution)/shard_map/ppermute | solution.py:263
  71.4 1.3 %collective-permute-start.16 = (bf16[16,6144]{1,0:T(8,128)(2,1)S(1)}, bf16[16,6144]{1,0:T(8,128)(2,1)S(1)}, u32[]{:S(2)}, u32[]{:S(2)}) collective-permute-start(bf16[16,6144]{1,0:T(8,128)(2,1)S(1)} %pad_maximum_fusion.2), channel_id=1, source_target_pairs={{0,2},{1,3},{2,0},{3,1},{4,6},{5,7},{6,4},{7,5},{8,10},{9,11},{10,... | collective-permute-start | bytes 589832 | tf_op jit(solution)/shard_map/ppermute | solution.py:263
  72.8 1.8 %collective-permute-start.20 = (bf16[16,6144]{1,0:T(8,128)(2,1)S(1)}, bf16[16,6144]{1,0:T(8,128)(2,1)S(1)}, u32[]{:S(2)}, u32[]{:S(2)}) collective-permute-start(bf16[16,6144]{1,0:T(8,128)(2,1)S(1)} %add_convert_fusion.3), channel_id=1, source_target_pairs={{0,12},{1,13},{2,14},{3,15},{4,0},{5,1},{6,2},{7,3},{8,4},{9,5},{1... | collective-permute-start | bytes 589832 | tf_op jit(solution)/shard_map/ppermute | solution.py:258
  74.6 2.5 %collective-permute-done.16 = bf16[16,6144]{1,0:T(8,128)(2,1)S(1)} collective-permute-done((bf16[16,6144]{1,0:T(8,128)(2,1)S(1)}, bf16[16,6144]{1,0:T(8,128)(2,1)S(1)}, u32[]{:S(2)}, u32[]{:S(2)}) %collective-permute-start.16) | collective-permute-done | bytes 196640 | tf_op jit(solution)/shard_map/ppermute | solution.py:263
  77.1 1.2 %collective-permute-start.21 = (bf16[16,6144]{1,0:T(8,128)(2,1)S(1)}, bf16[16,6144]{1,0:T(8,128)(2,1)S(1)}, u32[]{:S(2)}, u32[]{:S(2)}) collective-permute-start(bf16[16,6144]{1,0:T(8,128)(2,1)S(1)} %add_convert_fusion.2), channel_id=1, source_target_pairs={{0,4},{1,5},{2,6},{3,7},{4,8},{5,9},{6,10},{7,11},{8,12},{9,13},{1... | collective-permute-start | bytes 589832 | tf_op jit(solution)/shard_map/ppermute | solution.py:258
  78.3 0.0 collective-permute-done.18.refs_3_
  78.3 0.0 collective-permute-done.17.refs_2_
  78.3 0.8 collective-permute-start.19
  79.1 6.6 %collective-permute-done.20.near = bf16[16,6144]{1,0:T(8,128)(2,1)S(1)} collective-permute-done((bf16[16,6144]{1,0:T(8,128)(2,1)S(1)}, bf16[16,6144]{1,0:T(8,128)(2,1)S(1)}, u32[]{:S(2)}, u32[]{:S(2)}) %collective-permute-start.20) | collective-permute-done | bytes 196640 | tf_op jit(solution)/shard_map/ppermute | solution.py:258
  85.7 0.0 collective-permute-done.21.last
  85.7 0.0 collective-permute-done.19.arrived
  85.7 0.0 copy-done
  85.7 0.0 copy-done.1
  85.7 0.0 copy-done.2
  85.7 1.3 %mix.1 = bf16[24,6144]{1,0:T(8,128)(2,1)} custom-call(s32[2,24]{1,0:T(2,128)S(1)} %bitcast.4, f32[2,24]{1,0:T(2,128)S(1)} %bitcast.5, bf16[24,6144]{1,0:T(8,128)(2,1)S(1)} %copy-done, bf16[16,6144]{1,0:T(8,128)(2,1)S(1)} %collective-permute-done.19.arrived, bf16[16,6144]{1,0:T(8,128)(2,1)S(1)} %collective-permute-done.20.near, ...), custom_call_target="tpu_custom_call" | custom-call | tf_op jit(solution)/shard_map/mix/pallas_call | solution.py:237
  (19 shorter events, 0.4 us)
Async XLA Ops:
  1.5 14.8 %collective-permute-start = (bf16[16,3072]{1,0:T(8,128)(2,1)S(1)}, bf16[16,3072]{1,0:T(8,128)(2,1)S(1)}, u32[]{:S(2)}, u32[]{:S(2)}) collective-permute-start(bf16[16,3072]{1,0:T(8,128)(2,1)S(1)} %get-tuple-element.35), channel_id=1, source_target_pairs={{0,4},{1,5},{2,6},{3,7},{4,8},{5,9},{6,10},{7,11},{8,12},{9,13},{1... | collective-permute-start | bytes 294920 | tf_op jit(solution)/shard_map/ppermute | solution.py:258
  4.6 11.7 %collective-permute-start.1 = (bf16[16,3072]{1,0:T(8,128)(2,1)S(1)}, bf16[16,3072]{1,0:T(8,128)(2,1)S(1)}, u32[]{:S(2)}, u32[]{:S(2)}) collective-permute-start(bf16[16,3072]{1,0:T(8,128)(2,1)S(1)} %get-tuple-element.36), channel_id=1, source_target_pairs={{0,8},{1,9},{2,10},{3,11},{4,12},{5,13},{6,14},{7,15},{8,0},{9,1},... | collective-permute-start | bytes 294920 | tf_op jit(solution)/shard_map/ppermute | solution.py:258
  7.2 9.1 %collective-permute-start.2 = (bf16[16,3072]{1,0:T(8,128)(2,1)S(1)}, bf16[16,3072]{1,0:T(8,128)(2,1)S(1)}, u32[]{:S(2)}, u32[]{:S(2)}) collective-permute-start(bf16[16,3072]{1,0:T(8,128)(2,1)S(1)} %get-tuple-element.37), channel_id=1, source_target_pairs={{0,12},{1,13},{2,14},{3,15},{4,0},{5,1},{6,2},{7,3},{8,4},{9,5},{1... | collective-permute-start | bytes 294920 | tf_op jit(solution)/shard_map/ppermute | solution.py:258
  8.5 17.4 %collective-permute-start.6 = (bf16[16,6144]{1,0:T(8,128)(2,1)S(1)}, bf16[16,6144]{1,0:T(8,128)(2,1)S(1)}, u32[]{:S(2)}, u32[]{:S(2)}) collective-permute-start(bf16[16,6144]{1,0:T(8,128)(2,1)S(1)} %get-tuple-element.33.after_ref.refs_0_), channel_id=1, source_target_pairs={{0,2},{1,3},{2,0},{3,1},{4,6},{5,7},{6,4},{7,5},{8,10},{9,11},{10,... | collective-permute-start | bytes 589832 | tf_op jit(solution)/shard_map/ppermute | solution.py:263
  16.3 7.5 %collective-permute-start.3 = (bf16[16,3072]{1,0:T(8,128)(2,1)S(1)}, bf16[16,3072]{1,0:T(8,128)(2,1)S(1)}, u32[]{:S(2)}, u32[]{:S(2)}) collective-permute-start(bf16[16,3072]{1,0:T(8,128)(2,1)S(1)} %get-tuple-element.38), channel_id=1, source_target_pairs={{0,4},{1,5},{2,6},{3,7},{4,8},{5,9},{6,10},{7,11},{8,12},{9,13},{1... | collective-permute-start | bytes 294920 | tf_op jit(solution)/shard_map/ppermute | solution.py:258
  17.0 8.8 %collective-permute-start.4 = (bf16[16,3072]{1,0:T(8,128)(2,1)S(1)}, bf16[16,3072]{1,0:T(8,128)(2,1)S(1)}, u32[]{:S(2)}, u32[]{:S(2)}) collective-permute-start(bf16[16,3072]{1,0:T(8,128)(2,1)S(1)} %get-tuple-element.40), channel_id=1, source_target_pairs={{0,8},{1,9},{2,10},{3,11},{4,12},{5,13},{6,14},{7,15},{8,0},{9,1},... | collective-permute-start | bytes 294920 | tf_op jit(solution)/shard_map/ppermute | solution.py:258
  17.9 7.9 %collective-permute-start.5 = (bf16[16,3072]{1,0:T(8,128)(2,1)S(1)}, bf16[16,3072]{1,0:T(8,128)(2,1)S(1)}, u32[]{:S(2)}, u32[]{:S(2)}) collective-permute-start(bf16[16,3072]{1,0:T(8,128)(2,1)S(1)} %get-tuple-element.42), channel_id=1, source_target_pairs={{0,12},{1,13},{2,14},{3,15},{4,0},{5,1},{6,2},{7,3},{8,4},{9,5},{1... | collective-permute-start | bytes 294920 | tf_op jit(solution)/shard_map/ppermute | solution.py:258
  20.2 7.1 %collective-permute-start.8 = (bf16[48,3072]{1,0:T(8,128)(2,1)S(1)}, bf16[48,3072]{1,0:T(8,128)(2,1)S(1)}, u32[]{:S(2)}, u32[]{:S(2)}) collective-permute-start(bf16[48,3072]{1,0:T(8,128)(2,1)S(1)} %get-tuple-element.43.refs_1_), channel_id=1, source_target_pairs={{0,2},{1,3},{2,0},{3,1},{4,6},{5,7},{6,4},{7,5},{8,10},{9,11},{10,... | collective-permute-start | bytes 884744 | tf_op jit(solution)/shard_map/ppermute | solution.py:263
  27.4 2.4 %collective-permute-start.9 = (bf16[128,3072]{1,0:T(8,128)(2,1)S(1)}, bf16[128,3072]{1,0:T(8,128)(2,1)S(1)}, u32[]{:S(2)}, u32[]{:S(2)}) collective-permute-start(bf16[128,3072]{1,0:T(8,128)(2,1)S(1)} %constant_dynamic-update-slice_fusion.6), channel_id=1, source_target_pairs={{0,1},{1,0},{2,3},{3,2},{4,5},{5,4},{6,7},{7,6},{8,9},{9,8},{10,11... | collective-permute-start | bytes 2359304 | tf_op jit(solution)/shard_map/ppermute | solution.py:263
  27.5 11.1 %collective-permute-start.7 = (bf16[48,3072]{1,0:T(8,128)(2,1)S(1)}, bf16[48,3072]{1,0:T(8,128)(2,1)S(1)}, u32[]{:S(2)}, u32[]{:S(2)}) collective-permute-start(bf16[48,3072]{1,0:T(8,128)(2,1)S(1)} %get-tuple-element.80.refs_1_), channel_id=1, source_target_pairs={{0,2},{1,3},{2,0},{3,1},{4,6},{5,7},{6,4},{7,5},{8,10},{9,11},{10,... | collective-permute-start | bytes 884744 | tf_op jit(solution)/shard_map/ppermute | solution.py:263
  38.6 2.4 %collective-permute-start.10 = (bf16[128,3072]{1,0:T(8,128)(2,1)S(1)}, bf16[128,3072]{1,0:T(8,128)(2,1)S(1)}, u32[]{:S(2)}, u32[]{:S(2)}) collective-permute-start(bf16[128,3072]{1,0:T(8,128)(2,1)S(1)} %constant_dynamic-update-slice_fusion.10), channel_id=1, source_target_pairs={{0,1},{1,0},{2,3},{3,2},{4,5},{5,4},{6,7},{7,6},{8,9},{9,8},{10,11... | collective-permute-start | bytes 2359304 | tf_op jit(solution)/shard_map/ppermute | solution.py:263
  52.7 3.0 %collective-permute-start.11 = (bf16[128,3072]{1,0:T(8,128)(2,1)S(1)}, bf16[128,3072]{1,0:T(8,128)(2,1)S(1)}, u32[]{:S(2)}, u32[]{:S(2)}) collective-permute-start(bf16[128,3072]{1,0:T(8,128)(2,1)S(1)} %get-tuple-element.54), channel_id=1, source_target_pairs={{0,1},{1,0},{2,3},{3,2},{4,5},{5,4},{6,7},{7,6},{8,9},{9,8},{10,11... | collective-permute-start | bytes 2359304 | tf_op jit(solution)/shard_map/ppermute | solution.py:263
  55.2 30.6 %copy-start = (bf16[24,6144]{1,0:T(8,128)(2,1)S(1)}, bf16[24,6144]{1,0:T(8,128)(2,1)}, u32[]{:S(2)}) copy-start(bf16[24,6144]{1,0:T(8,128)(2,1)} %act_ref.3) | copy-start | bytes 884740
  55.2 30.5 %copy-start.1 = (s32[24,2]{0,1:T(2,128)S(1)}, s32[24,2]{0,1:T(2,128)}, u32[]{:S(2)}) copy-start(s32[24,2]{0,1:T(2,128)} %param.8) | copy-start | bytes 580
  55.2 30.5 %copy-start.2 = (f32[24,2]{0,1:T(2,128)S(1)}, f32[24,2]{0,1:T(2,128)}, u32[]{:S(2)}) copy-start(f32[24,2]{0,1:T(2,128)} %param.9) | copy-start | bytes 580
  55.2 2.4 %collective-permute-start.12 = (bf16[128,3072]{1,0:T(8,128)(2,1)S(1)}, bf16[128,3072]{1,0:T(8,128)(2,1)S(1)}, u32[]{:S(2)}, u32[]{:S(2)}) collective-permute-start(bf16[128,3072]{1,0:T(8,128)(2,1)S(1)} %get-tuple-element.57), channel_id=1, source_target_pairs={{0,1},{1,0},{2,3},{3,2},{4,5},{5,4},{6,7},{7,6},{8,9},{9,8},{10,11... | collective-permute-start | bytes 2359304 | tf_op jit(solution)/shard_map/ppermute | solution.py:263
  57.8 5.7 %collective-permute-start.13 = (bf16[16,3072]{1,0:T(8,128)(2,1)S(1)}, bf16[16,3072]{1,0:T(8,128)(2,1)S(1)}, u32[]{:S(2)}, u32[]{:S(2)}) collective-permute-start(bf16[16,3072]{1,0:T(8,128)(2,1)S(1)} %get-tuple-element.73), channel_id=1, source_target_pairs={{0,2},{1,3},{2,0},{3,1},{4,6},{5,7},{6,4},{7,5},{8,10},{9,11},{10,... | collective-permute-start | bytes 294920 | tf_op jit(solution)/shard_map/ppermute | solution.py:263
  59.2 5.8 %collective-permute-start.14 = (bf16[16,3072]{1,0:T(8,128)(2,1)S(1)}, bf16[16,3072]{1,0:T(8,128)(2,1)S(1)}, u32[]{:S(2)}, u32[]{:S(2)}) collective-permute-start(bf16[16,3072]{1,0:T(8,128)(2,1)S(1)} %get-tuple-element.66), channel_id=1, source_target_pairs={{0,2},{1,3},{2,0},{3,1},{4,6},{5,7},{6,4},{7,5},{8,10},{9,11},{10,... | collective-permute-start | bytes 294920 | tf_op jit(solution)/shard_map/ppermute | solution.py:263
  65.0 6.4 %collective-permute-start.15 = (bf16[16,6144]{1,0:T(8,128)(2,1)S(1)}, bf16[16,6144]{1,0:T(8,128)(2,1)S(1)}, u32[]{:S(2)}, u32[]{:S(2)}) collective-permute-start(bf16[16,6144]{1,0:T(8,128)(2,1)S(1)} %pad_maximum_fusion.1), channel_id=1, source_target_pairs={{0,2},{1,3},{2,0},{3,1},{4,6},{5,7},{6,4},{7,5},{8,10},{9,11},{10,... | collective-permute-start | bytes 589832 | tf_op jit(solution)/shard_map/ppermute | solution.py:263
  66.4 11.9 %collective-permute-start.18 = (bf16[16,3072]{1,0:T(8,128)(2,1)S(1)}, bf16[16,3072]{1,0:T(8,128)(2,1)S(1)}, u32[]{:S(2)}, u32[]{:S(2)}) collective-permute-start(bf16[16,3072]{1,0:T(8,128)(2,1)S(1)} %add_convert_fusion.4), channel_id=1, source_target_pairs={{0,8},{1,9},{2,10},{3,11},{4,12},{5,13},{6,14},{7,15},{8,0},{9,1},... | collective-permute-start | bytes 294920 | tf_op jit(solution)/shard_map/ppermute | solution.py:258
  67.4 10.9 %collective-permute-start.17 = (bf16[16,3072]{1,0:T(8,128)(2,1)S(1)}, bf16[16,3072]{1,0:T(8,128)(2,1)S(1)}, u32[]{:S(2)}, u32[]{:S(2)}) collective-permute-start(bf16[16,3072]{1,0:T(8,128)(2,1)S(1)} %add_convert_fusion.5), channel_id=1, source_target_pairs={{0,8},{1,9},{2,10},{3,11},{4,12},{5,13},{6,14},{7,15},{8,0},{9,1},... | collective-permute-start | bytes 294920 | tf_op jit(solution)/shard_map/ppermute | solution.py:258
  71.4 5.7 %collective-permute-start.16 = (bf16[16,6144]{1,0:T(8,128)(2,1)S(1)}, bf16[16,6144]{1,0:T(8,128)(2,1)S(1)}, u32[]{:S(2)}, u32[]{:S(2)}) collective-permute-start(bf16[16,6144]{1,0:T(8,128)(2,1)S(1)} %pad_maximum_fusion.2), channel_id=1, source_target_pairs={{0,2},{1,3},{2,0},{3,1},{4,6},{5,7},{6,4},{7,5},{8,10},{9,11},{10,... | collective-permute-start | bytes 589832 | tf_op jit(solution)/shard_map/ppermute | solution.py:263
  72.8 12.9 %collective-permute-start.20 = (bf16[16,6144]{1,0:T(8,128)(2,1)S(1)}, bf16[16,6144]{1,0:T(8,128)(2,1)S(1)}, u32[]{:S(2)}, u32[]{:S(2)}) collective-permute-start(bf16[16,6144]{1,0:T(8,128)(2,1)S(1)} %add_convert_fusion.3), channel_id=1, source_target_pairs={{0,12},{1,13},{2,14},{3,15},{4,0},{5,1},{6,2},{7,3},{8,4},{9,5},{1... | collective-permute-start | bytes 589832 | tf_op jit(solution)/shard_map/ppermute | solution.py:258
  77.1 8.6 %collective-permute-start.21 = (bf16[16,6144]{1,0:T(8,128)(2,1)S(1)}, bf16[16,6144]{1,0:T(8,128)(2,1)S(1)}, u32[]{:S(2)}, u32[]{:S(2)}) collective-permute-start(bf16[16,6144]{1,0:T(8,128)(2,1)S(1)} %add_convert_fusion.2), channel_id=1, source_target_pairs={{0,4},{1,5},{2,6},{3,7},{4,8},{5,9},{6,10},{7,11},{8,12},{9,13},{1... | collective-permute-start | bytes 589832 | tf_op jit(solution)/shard_map/ppermute | solution.py:258
  78.3 7.4 %collective-permute-start.19 = (bf16[16,6144]{1,0:T(8,128)(2,1)S(1)}, bf16[16,6144]{1,0:T(8,128)(2,1)S(1)}, u32[]{:S(2)}, u32[]{:S(2)}) collective-permute-start(bf16[16,6144]{1,0:T(8,128)(2,1)S(1)} %pad_maximum_fusion), channel_id=1, source_target_pairs={{0,2},{1,3},{2,0},{3,1},{4,6},{5,7},{6,4},{7,5},{8,10},{9,11},{10,... | collective-permute-start | bytes 589832 | tf_op jit(solution)/shard_map/ppermute | solution.py:263

commit v10 on v9

--- a/solution.py
+++ b/solution.py
@@ -100,6 +100,24 @@
     )(pltpu.with_memory_space_constraint(w, pltpu.HBM), after)
 
 
+def relay_kernel(count, *refs):
+    for x_ref, out_ref in zip(refs[:count], refs[count + 1 :]):
+        out_ref[...] = x_ref[...]
+
+
+def relay(arrays, after):
+    count = len(arrays)
+    return pl.pallas_call(
+        functools.partial(relay_kernel, count),
+        in_specs=[VMEM] * count + [ANY],
+        out_specs=[VMEM] * count,
+        out_shape=[jax.ShapeDtypeStruct(x.shape, x.dtype) for x in arrays],
+        compiler_params=LIMIT,
+        cost_estimate=pl.CostEstimate(flops=0, bytes_accessed=16 * MIB, transcendentals=0),
+        name="relay",
+    )(*arrays, after)
+
+
 def gate_up_kernel(count, ahead, at, ahead_at, begin, end, *refs):
     pieces, refs = refs[:count], refs[count:]
     weights, later, refs = refs[:2], refs[2 : 2 + ahead], refs[2 + ahead :]
@@ -114,12 +132,15 @@
     copies = fetches(later, ahead_at, held, sems)
     for copy in copies:
         copy.start()
-    for c in range(0, part, BLOCK):
+
+    @pl.loop(0, part // BLOCK)
+    def _(c):
         parts = []
         for p in pieces:
-            first = c + (at if p.shape[1] > part else 0)
-            parts.append(p[:, first : first + BLOCK])
-        turned[c : c + BLOCK, :] = jnp.concatenate(parts, axis=0).T
+            first = c * BLOCK + (at if p.shape[1] > part else 0)
+            parts.append(p[:, pl.ds(pl.multiple_of(first, BLOCK), BLOCK)])
+        turned[pl.ds(pl.multiple_of(c * BLOCK, BLOCK), BLOCK), :] = jnp.concatenate(parts, axis=0).T
+
     for j in range(2):
         total = jnp.dot(weights[j][...], turned[...], preferred_element_type=jnp.float32)
         sums[j][...] = total if begin else total + before[j][...]
@@ -149,9 +170,7 @@
     weights = [pltpu.with_memory_space_constraint(w, pltpu.VMEM) for w in weights]
     later = [pltpu.with_memory_space_constraint(w, pltpu.HBM) for w in later]
     out = pl.pallas_call(
-        functools.partial(
-            gate_up_kernel, len(pieces), len(later), k * part, 0 if end else part, begin, end
-        ),
+        functools.partial(gate_up_kernel, len(pieces), len(later), k * part, part, begin, end),
         in_specs=[VMEM] * (len(pieces) + 2) + [ANY] * len(later) + [VMEM] * len(totals),
         out_specs=out_specs,
         out_shape=out_shape,
@@ -171,15 +190,18 @@
     later, held, refs = refs[:ahead], refs[ahead : 2 * ahead], refs[2 * ahead :]
     keep_ref, send_ref, sems = refs
     half, part = keep_ref.shape
-    copies = fetches(later, part, held, sems)
+    copies = fetches(later, 0, held, sems)
     for copy in copies:
         copy.start()
-    for c in range(0, part, BLOCK):
-        columns = slice(c, c + BLOCK)
+
+    @pl.loop(0, part // BLOCK)
+    def _(c):
+        columns = pl.ds(pl.multiple_of(c * BLOCK, BLOCK), BLOCK)
         out = jnp.dot(hidden_ref[...], w_ref[:, columns], preferred_element_type=jnp.float32)
         out = out.astype(jnp.bfloat16)
         keep_ref[:, columns] = out[:half]
         send_ref[:, columns] = out[half:]
+
     for copy in copies:
         copy.wait()
 
@@ -270,13 +292,12 @@
     own, *sends = pack(group, ids, activations, norm_gain)
     far_own = swap(own, far)
     now = [fetch(w, 0, part, own) for w in (w_gate, w_up)]
-    blocks, earlier = [], []
+    blocks = []
     for k in range(HALVES):
-        arrivals = []
-        for s in range(others):
-            x = sends[k * others + s]
-            arrivals.append(shift(after(x, *earlier, *now) if k else x, s + 1))
-        earlier = arrivals
+        x = sends[k * others : (k + 1) * others]
+        if k:
+            x = relay(after(x, *now, far_own), blocks[-1])
+        arrivals = [shift(x[s], s + 1) for s in range(others)]
         blocks.append(jnp.concatenate(arrivals, axis=0))
     totals = []
     for k in range(HALVES):
@@ -296,24 +317,24 @@
         now, totals = gate_up(k, pieces, now, later, totals)
     hidden = totals[0]
     held = []
-    for k in range(HALVES):
-        later = [w_down] if k < HALVES - 1 else []
+    for k in reversed(range(HALVES)):
+        later = [w_down] if k else []
         now, (keep, send) = down(hidden, now[0], later)
         bit = 1
         while bit < far:
             total = added(keep, swap(send, bit))
             keep, send = total[: total.shape[0] // 2], total[total.shape[0] // 2 :]
             bit *= 2
-        held.append([total[j * CAP : (j + 1) * CAP] for j in range(2 * EXPERTS)])
+        held.insert(0, [total[j * CAP : (j + 1) * CAP] for j in range(2 * EXPERTS)])
     crossed = [swap(h[6], far) for h in held]
     middle = [shift(added(h[2], x), -2) for h, x in zip(held, crossed)]
     mine = [jnp.concatenate([h[j] for h in held], axis=1) for j in range(2 * EXPERTS)]
     back = {}
-    for s, ready in ((1, []), (3, []), (0, middle)):
-        crossed.append(swap(after(mine[EXPERTS + s], *crossed, *ready), far))
-        back[s] = crossed[-1]
-    near = shift(added(mine[1], back[1]), -1)
-    last = shift(added(mine[3], back[3]), -3)
+    back[1] = swap(after(mine[EXPERTS + 1], crossed[0]), far)
+    back[3] = swap(after(mine[EXPERTS + 3], *crossed), far)
+    back[0] = swap(after(mine[EXPERTS], back[1], back[3]), far)
+    near = shift(after(added(mine[1], back[1]), middle[0]), -1)
+    last = shift(after(added(mine[3], back[3]), middle[1]), -3)
     arrived = back[0]
     pieces = [arrived, near, last, *[h[0] for h in held], *middle]
     return mix(group, ids, route_logits.T, activations, pieces)

time: 87.2 us -> 76.9 us (0.88)
  Pallas kernels: 31.8 us -> 24.5 us
  waiting for transfers between devices: 27.2 us -> 24.6 us
    pallas_call x2, Pallas kernels: 15.5 us -> 9.82 us  [gate_up(): pl.pallas_call(functools.partial(gate_up_kernel, len(pieces), len(later),...]
    ppermute x12, waiting for transfers between devices: 15.5 us -> 13.2 us  [swap(): return lax.ppermute(x, 'expert', [(i, i ^ bit) for i in range(devices)])]
    pallas_call x2, Pallas kernels: 7.32 us -> 5.7 us  [down(): pl.pallas_call(functools.partial(down_kernel, ahead), in_specs=[VMEM, VME...]
  transfers between devices with their start and end apart: 22 -> 22, of which waited for: 11 -> 14; matrix products, arithmetic and copies ran while one was open for 1% -> 1% of each run, Pallas kernels for 20% -> 18%
where the time goes in v10:
time: 76.9 us; the launch traced here: 76.8 us
  starting transfers between devices  26.5 us (34%)
  waiting for transfers between devices  24.6 us (32%)
  Pallas kernels  24.5 us (32%)
    ppermute x10, starting transfers between devices, shift(): lax.ppermute(x, 'expert', [(i, (i + s * group) % devices) for i in range(...  16.5 us
    ppermute x12, waiting for transfers between devices, swap(): return lax.ppermute(x, 'expert', [(i, i ^ bit) for i in range(devices)])  13.2 us
    ppermute x10, waiting for transfers between devices, shift(): lax.ppermute(x, 'expert', [(i, (i + s * group) % devices) for i in range(...  11.4 us
    ppermute x12, starting transfers between devices, swap(): return lax.ppermute(x, 'expert', [(i, i ^ bit) for i in range(devices)])  10 us
    pallas_call x2, Pallas kernels, gate_up(): pl.pallas_call(functools.partial(gate_up_kernel, len(pieces), len(later),...  9.82 us
    pallas_call x2, Pallas kernels, fetch(): pl.pallas_call(functools.partial(fetch_kernel, at), in_specs=[ANY, ANY],...  6.19 us
    pallas_call x2, Pallas kernels, down(): pl.pallas_call(functools.partial(down_kernel, ahead), in_specs=[VMEM, VME...  5.7 us
  transfers between devices with their start and end apart: 22, of which 14 were waited for; matrix products, arithmetic and copies ran while one was open for 1% of the time, Pallas kernels for 18%

profile of v10, /device:TPU:0, one launch (start us, length us, event | category | flops | bytes accessed | tf_op | source)
XLA Modules:
  0.0 76.8 jit_solution(418934338333205368)
XLA Ops:
  0.0 1.5 %norm_and_pack.1 = (bf16[16,6144]{1,0:T(8,128)(2,1)S(1)}, bf16[16,3072]{1,0:T(8,128)(2,1)S(1)}, bf16[16,3072]{1,0:T(8,128)(2,1)S(1)}, bf16[16,3072]{1,0:T(8,128)...) custom-call(s32[2,24]{1,0:T(2,128)} %bitcast.3, ...), custom_call_target="tpu_custom_call" | custom-call | tf_op jit(solution)/shard_map/norm_and_pack/pallas_call | solution.py:58
  1.5 3.1 %collective-permute-start.1 = (bf16[16,3072]{1,0:T(8,128)(2,1)S(1)}, bf16[16,3072]{1,0:T(8,128)(2,1)S(1)}, u32[]{:S(2)}, u32[]{:S(2)}) collective-permute-start(bf16[16,3072]{1,0:T(8,128)(2,1)S(1)} %get-tuple-element.45), channel_id=1, source_target_pairs={{0,4},{1,5},{2,6},{3,7},{4,8},{5,9},{6,10},{7,11},{8,12},{9,13},{1... | collective-permute-start | bytes 294920 | tf_op jit(solution)/shard_map/ppermute | solution.py:280
  4.6 2.6 %collective-permute-start.2 = (bf16[16,3072]{1,0:T(8,128)(2,1)S(1)}, bf16[16,3072]{1,0:T(8,128)(2,1)S(1)}, u32[]{:S(2)}, u32[]{:S(2)}) collective-permute-start(bf16[16,3072]{1,0:T(8,128)(2,1)S(1)} %get-tuple-element.46), channel_id=1, source_target_pairs={{0,8},{1,9},{2,10},{3,11},{4,12},{5,13},{6,14},{7,15},{8,0},{9,1},... | collective-permute-start | bytes 294920 | tf_op jit(solution)/shard_map/ppermute | solution.py:280
  7.2 1.3 %collective-permute-start.3 = (bf16[16,3072]{1,0:T(8,128)(2,1)S(1)}, bf16[16,3072]{1,0:T(8,128)(2,1)S(1)}, u32[]{:S(2)}, u32[]{:S(2)}) collective-permute-start(bf16[16,3072]{1,0:T(8,128)(2,1)S(1)} %get-tuple-element.47), channel_id=1, source_target_pairs={{0,12},{1,13},{2,14},{3,15},{4,0},{5,1},{6,2},{7,3},{8,4},{9,5},{1... | collective-permute-start | bytes 294920 | tf_op jit(solution)/shard_map/ppermute | solution.py:280
  8.5 1.5 %collective-permute-start = (bf16[16,6144]{1,0:T(8,128)(2,1)S(1)}, bf16[16,6144]{1,0:T(8,128)(2,1)S(1)}, u32[]{:S(2)}, u32[]{:S(2)}) collective-permute-start(bf16[16,6144]{1,0:T(8,128)(2,1)S(1)} %get-tuple-element.38.after_ref.refs_0_), channel_id=1, source_target_pairs={{0,2},{1,3},{2,0},{3,1},{4,6},{5,7},{6,4},{7,5},{8,10},{9,11},{10,... | collective-permute-start | bytes 589832 | tf_op jit(solution)/shard_map/ppermute | solution.py:285
  10.0 3.1 %fetch.2.refs_5_ = bf16[1152,3072]{1,0:T(8,128)(2,1)S(1)} custom-call(bf16[1152,6144]{1,0:T(8,128)(2,1)} %refs_7_.2, bf16[16,6144]{1,0:T(8,128)(2,1)S(1)} %get-tuple-element.38.after_ref.refs_0_), custom_call_target="tpu_custom_call" | custom-call | bytes 14155776 | tf_op jit(solution)/shard_map/fetch/pallas_call | solution.py:91
  13.1 3.1 %fetch.3.refs_6_ = bf16[1152,3072]{1,0:T(8,128)(2,1)S(1)} custom-call(bf16[1152,6144]{1,0:T(8,128)(2,1)} %refs_8_.1, bf16[16,6144]{1,0:T(8,128)(2,1)S(1)} %get-tuple-element.38.after_ref.refs_0_), custom_call_target="tpu_custom_call" | custom-call | bytes 14155776 | tf_op jit(solution)/shard_map/fetch/pallas_call | solution.py:91
  16.2 0.0 collective-permute-done.1
  16.3 0.0 collective-permute-done.2
  16.3 0.0 collective-permute-done.3
  16.3 0.0 collective-permute-done.refs_2_
  16.4 0.7 collective-permute-start.4
  17.1 0.8 %collective-permute-start.8 = (bf16[48,3072]{1,0:T(8,128)(2,1)S(1)}, bf16[48,3072]{1,0:T(8,128)(2,1)S(1)}, u32[]{:S(2)}, u32[]{:S(2)}) collective-permute-start(bf16[48,3072]{1,0:T(8,128)(2,1)S(1)} %get-tuple-element.51.refs_3_.refs_1_), channel_id=1, source_target_pairs={{0,2},{1,3},{2,0},{3,1},{4,6},{5,7},{6,4},{7,5},{8,10},{9,11},{10,... | collective-permute-start | bytes 884744 | tf_op jit(solution)/shard_map/ppermute | solution.py:285
  18.0 1.7 %collective-permute-start.5 = (bf16[16,3072]{1,0:T(8,128)(2,1)S(1)}, bf16[16,3072]{1,0:T(8,128)(2,1)S(1)}, u32[]{:S(2)}, u32[]{:S(2)}) collective-permute-start(bf16[16,3072]{1,0:T(8,128)(2,1)S(1)} %get-tuple-element.49), channel_id=1, source_target_pairs={{0,8},{1,9},{2,10},{3,11},{4,12},{5,13},{6,14},{7,15},{8,0},{9,1},... | collective-permute-start | bytes 294920 | tf_op jit(solution)/shard_map/ppermute | solution.py:280
  19.6 1.2 %collective-permute-start.6 = (bf16[16,3072]{1,0:T(8,128)(2,1)S(1)}, bf16[16,3072]{1,0:T(8,128)(2,1)S(1)}, u32[]{:S(2)}, u32[]{:S(2)}) collective-permute-start(bf16[16,3072]{1,0:T(8,128)(2,1)S(1)} %get-tuple-element.50), channel_id=1, source_target_pairs={{0,12},{1,13},{2,14},{3,15},{4,0},{5,1},{6,2},{7,3},{8,4},{9,5},{1... | collective-permute-start | bytes 294920 | tf_op jit(solution)/shard_map/ppermute | solution.py:280
  20.8 2.9 %collective-permute-done.4 = bf16[16,3072]{1,0:T(8,128)(2,1)S(1)} collective-permute-done((bf16[16,3072]{1,0:T(8,128)(2,1)S(1)}, bf16[16,3072]{1,0:T(8,128)(2,1)S(1)}, u32[]{:S(2)}, u32[]{:S(2)}) %collective-permute-start.4) | collective-permute-done | bytes 98336 | tf_op jit(solution)/shard_map/ppermute | solution.py:280
  23.7 2.5 %collective-permute-done.5 = bf16[16,3072]{1,0:T(8,128)(2,1)S(1)} collective-permute-done((bf16[16,3072]{1,0:T(8,128)(2,1)S(1)}, bf16[16,3072]{1,0:T(8,128)(2,1)S(1)}, u32[]{:S(2)}, u32[]{:S(2)}) %collective-permute-start.5) | collective-permute-done | bytes 98336 | tf_op jit(solution)/shard_map/ppermute | solution.py:280
  26.2 0.0 collective-permute-done.6
  26.3 0.0 collective-permute-done.8.refs_3_
  26.3 0.1 collective-permute-start.9
  26.4 1.0 %collective-permute-start.7 = (bf16[48,3072]{1,0:T(8,128)(2,1)S(1)}, bf16[48,3072]{1,0:T(8,128)(2,1)S(1)}, u32[]{:S(2)}, u32[]{:S(2)}) collective-permute-start(bf16[48,3072]{1,0:T(8,128)(2,1)S(1)} %get-tuple-element.90.refs_1_), channel_id=1, source_target_pairs={{0,2},{1,3},{2,0},{3,1},{4,6},{5,7},{6,4},{7,5},{8,10},{9,11},{10,... | collective-permute-start | bytes 884744 | tf_op jit(solution)/shard_map/ppermute | solution.py:285
  27.4 1.2 %collective-permute-done.9.refs_4_ = bf16[128,3072]{1,0:T(8,128)(2,1)S(1)} collective-permute-done((bf16[128,3072]{1,0:T(8,128)(2,1)S(1)}, bf16[128,3072]{1,0:T(8,128)(2,1)S(1)}, u32[]{:S(2)}, u32[]{:S(2)}) %collective-permute-start.9) | collective-permute-done | bytes 786464 | tf_op jit(solution)/shard_map/ppermute | solution.py:285
  28.6 5.2 %gate_up.2 = (bf16[1152,3072]{1,0:T(8,128)(2,1)S(1)}, bf16[1152,3072]{1,0:T(8,128)(2,1)S(1)}, f32[1152,256]{1,0:T(8,128)S(1)}, f32[1152,256]{1,0:T(8,128)S(1)}) custom-call(bf16[16,6144]{1,0:T(8,128)(2,1)S(1)} %get-tuple-element.38.after_ref.refs_0_, bf16[48,3072]{1,0:T(8,128)(2,1)S(1)} %get-tuple-element.51.refs_3_.refs_1_, ...), custom_call_target="tpu_custom_call" | custom-call | flops 3623878656 | bytes 16515072 | tf_op jit(solution)/shard_map/gate_up/pallas_call | solution.py:172
  33.8 2.0 %collective-permute-done.7.refs_3_ = bf16[48,3072]{1,0:T(8,128)(2,1)S(1)} collective-permute-done((bf16[48,3072]{1,0:T(8,128)(2,1)S(1)}, bf16[48,3072]{1,0:T(8,128)(2,1)S(1)}, u32[]{:S(2)}, u32[]{:S(2)}) %collective-permute-start.7) | collective-permute-done | bytes 294944 | tf_op jit(solution)/shard_map/ppermute | solution.py:285
  35.8 0.1 collective-permute-start.10
  35.9 2.3 %collective-permute-done.10.refs_4_ = bf16[128,3072]{1,0:T(8,128)(2,1)S(1)} collective-permute-done((bf16[128,3072]{1,0:T(8,128)(2,1)S(1)}, bf16[128,3072]{1,0:T(8,128)(2,1)S(1)}, u32[]{:S(2)}, u32[]{:S(2)}) %collective-permute-start.10) | collective-permute-done | bytes 786464 | tf_op jit(solution)/shard_map/ppermute | solution.py:285
  38.2 4.6 %gate_up.3 = (bf16[1152,3072]{1,0:T(8,128)(2,1)S(1)}, bf16[256,1152]{1,0:T(8,128)(2,1)S(1)}) custom-call(bf16[16,6144]{1,0:T(8,128)(2,1)S(1)} %get-tuple-element.38.after_ref.refs_0_, bf16[48,3072]{1,0:T(8,128)(2,1)S(1)} %get-tuple-element.90.refs_1_, bf16[16,6144]{1,0:T(8,128)(2,1)S(1)} %collective-permute-done.refs_2_, ...), custom_call_target="tpu_custom_call" | custom-call | flops 3623878656 | bytes 16515072 | tf_op jit(solution)/shard_map/gate_up/pallas_call | solution.py:172
  42.8 3.1 %down.2 = (bf16[1152,3072]{1,0:T(8,128)(2,1)S(1)}, bf16[128,3072]{1,0:T(8,128)(2,1)S(1)}, bf16[128,3072]{1,0:T(8,128)(2,1)S(1)}) custom-call(bf16[256,1152]{1,0:T(8,128)(2,1)S(1)} %get-tuple-element.59.hidden_ref, bf16[1152,3072]{1,0:T(8,128)(2,1)S(1)} %get-tuple-element.60.w_ref, bf16[1152,6144]{1,0:T(8,128)(2,1)} %refs_0_.1), custom_call_target="tpu_custom_call" | custom-call | flops 1811939328 | bytes 9240576 | tf_op jit(solution)/shard_map/down/pallas_call | solution.py:217
  45.9 0.2 collective-permute-start.12
  46.1 2.6 %down.3 = (bf16[128,3072]{1,0:T(8,128)(2,1)S(1)}, bf16[128,3072]{1,0:T(8,128)(2,1)S(1)}) custom-call(bf16[256,1152]{1,0:T(8,128)(2,1)S(1)} %get-tuple-element.59.hidden_ref, bf16[1152,3072]{1,0:T(8,128)(2,1)S(1)} %get-tuple-element.61.w_ref), custom_call_target="tpu_custom_call" | custom-call | flops 1811939328 | bytes 9240576 | tf_op jit(solution)/shard_map/down/pallas_call | solution.py:217
  48.7 0.0 copy-start
  48.8 0.0 copy-start.1
  48.8 0.0 copy-start.2
  48.8 0.4 collective-permute-start.11
  49.2 0.0 collective-permute-done.12
  49.2 0.2 add_convert_fusion
  49.5 1.0 %collective-permute-start.15 = (bf16[16,3072]{1,0:T(8,128)(2,1)S(1)}, bf16[16,3072]{1,0:T(8,128)(2,1)S(1)}, u32[]{:S(2)}, u32[]{:S(2)}) collective-permute-start(bf16[16,3072]{1,0:T(8,128)(2,1)S(1)} %get-tuple-element.74), channel_id=1, source_target_pairs={{0,2},{1,3},{2,0},{3,1},{4,6},{5,7},{6,4},{7,5},{8,10},{9,11},{10,... | collective-permute-start | bytes 294920 | tf_op jit(solution)/shard_map/ppermute | solution.py:285
  50.5 0.6 collective-permute-done.11
  51.1 0.2 add_convert_fusion.1
  51.4 1.0 %collective-permute-start.13 = (bf16[16,3072]{1,0:T(8,128)(2,1)S(1)}, bf16[16,3072]{1,0:T(8,128)(2,1)S(1)}, u32[]{:S(2)}, u32[]{:S(2)}) collective-permute-start(bf16[16,3072]{1,0:T(8,128)(2,1)S(1)} %get-tuple-element.82), channel_id=1, source_target_pairs={{0,2},{1,3},{2,0},{3,1},{4,6},{5,7},{6,4},{7,5},{8,10},{9,11},{10,... | collective-permute-start | bytes 294920 | tf_op jit(solution)/shard_map/ppermute | solution.py:285
  52.5 1.9 %collective-permute-done.15 = bf16[16,3072]{1,0:T(8,128)(2,1)S(1)} collective-permute-done((bf16[16,3072]{1,0:T(8,128)(2,1)S(1)}, bf16[16,3072]{1,0:T(8,128)(2,1)S(1)}, u32[]{:S(2)}, u32[]{:S(2)}) %collective-permute-start.15) | collective-permute-done | bytes 98336 | tf_op jit(solution)/shard_map/ppermute | solution.py:285
  54.4 1.5 %collective-permute-start.20 = (bf16[16,3072]{1,0:T(8,128)(2,1)S(1)}, bf16[16,3072]{1,0:T(8,128)(2,1)S(1)}, u32[]{:S(2)}, u32[]{:S(2)}) collective-permute-start(bf16[16,3072]{1,0:T(8,128)(2,1)S(1)} %add_convert_fusion.4), channel_id=1, source_target_pairs={{0,8},{1,9},{2,10},{3,11},{4,12},{5,13},{6,14},{7,15},{8,0},{9,1},... | collective-permute-start | bytes 294920 | tf_op jit(solution)/shard_map/ppermute | solution.py:280
  55.9 0.7 collective-permute-done.13
  56.5 1.0 %collective-permute-start.16 = (bf16[16,6144]{1,0:T(8,128)(2,1)S(1)}, bf16[16,6144]{1,0:T(8,128)(2,1)S(1)}, u32[]{:S(2)}, u32[]{:S(2)}) collective-permute-start(bf16[16,6144]{1,0:T(8,128)(2,1)S(1)} %get-tuple-element.67), channel_id=1, source_target_pairs={{0,2},{1,3},{2,0},{3,1},{4,6},{5,7},{6,4},{7,5},{8,10},{9,11},{10,... | collective-permute-start | bytes 589832 | tf_op jit(solution)/shard_map/ppermute | solution.py:285
  57.5 1.2 %collective-permute-start.18 = (bf16[16,3072]{1,0:T(8,128)(2,1)S(1)}, bf16[16,3072]{1,0:T(8,128)(2,1)S(1)}, u32[]{:S(2)}, u32[]{:S(2)}) collective-permute-start(bf16[16,3072]{1,0:T(8,128)(2,1)S(1)} %add_convert_fusion.5), channel_id=1, source_target_pairs={{0,8},{1,9},{2,10},{3,11},{4,12},{5,13},{6,14},{7,15},{8,0},{9,1},... | collective-permute-start | bytes 294920 | tf_op jit(solution)/shard_map/ppermute | solution.py:280
  58.7 1.4 %collective-permute-start.14 = (bf16[16,6144]{1,0:T(8,128)(2,1)S(1)}, bf16[16,6144]{1,0:T(8,128)(2,1)S(1)}, u32[]{:S(2)}, u32[]{:S(2)}) collective-permute-start(bf16[16,6144]{1,0:T(8,128)(2,1)S(1)} %get-tuple-element.66), channel_id=1, source_target_pairs={{0,2},{1,3},{2,0},{3,1},{4,6},{5,7},{6,4},{7,5},{8,10},{9,11},{10,... | collective-permute-start | bytes 589832 | tf_op jit(solution)/shard_map/ppermute | solution.py:285
  60.1 4.3 %collective-permute-done.16 = bf16[16,6144]{1,0:T(8,128)(2,1)S(1)} collective-permute-done((bf16[16,6144]{1,0:T(8,128)(2,1)S(1)}, bf16[16,6144]{1,0:T(8,128)(2,1)S(1)}, u32[]{:S(2)}, u32[]{:S(2)}) %collective-permute-start.16) | collective-permute-done | bytes 196640 | tf_op jit(solution)/shard_map/ppermute | solution.py:285
  64.4 0.4 collective-permute-done.20.refs_3_
  64.8 2.1 %collective-permute-start.21 = (bf16[16,6144]{1,0:T(8,128)(2,1)S(1)}, bf16[16,6144]{1,0:T(8,128)(2,1)S(1)}, u32[]{:S(2)}, u32[]{:S(2)}) collective-permute-start(bf16[16,6144]{1,0:T(8,128)(2,1)S(1)} %add_convert_fusion.2), channel_id=1, source_target_pairs={{0,4},{1,5},{2,6},{3,7},{4,8},{5,9},{6,10},{7,11},{8,12},{9,13},{1... | collective-permute-start | bytes 589832 | tf_op jit(solution)/shard_map/ppermute | solution.py:280
  66.9 0.2 collective-permute-done.14
  67.2 1.3 %collective-permute-done.18.refs_2_ = bf16[16,3072]{1,0:T(8,128)(2,1)S(1)} collective-permute-done((bf16[16,3072]{1,0:T(8,128)(2,1)S(1)}, bf16[16,3072]{1,0:T(8,128)(2,1)S(1)}, u32[]{:S(2)}, u32[]{:S(2)}) %collective-permute-start.18) | collective-permute-done | bytes 98336 | tf_op jit(solution)/shard_map/ppermute | solution.py:280
  68.4 1.2 %collective-permute-start.19 = (bf16[16,6144]{1,0:T(8,128)(2,1)S(1)}, bf16[16,6144]{1,0:T(8,128)(2,1)S(1)}, u32[]{:S(2)}, u32[]{:S(2)}) collective-permute-start(bf16[16,6144]{1,0:T(8,128)(2,1)S(1)} %add_convert_fusion.3), channel_id=1, source_target_pairs={{0,12},{1,13},{2,14},{3,15},{4,0},{5,1},{6,2},{7,3},{8,4},{9,5},{1... | collective-permute-start | bytes 589832 | tf_op jit(solution)/shard_map/ppermute | solution.py:280
  69.6 1.4 %collective-permute-start.17 = (bf16[16,6144]{1,0:T(8,128)(2,1)S(1)}, bf16[16,6144]{1,0:T(8,128)(2,1)S(1)}, u32[]{:S(2)}, u32[]{:S(2)}) collective-permute-start(bf16[16,6144]{1,0:T(8,128)(2,1)S(1)} %pad_maximum_fusion), channel_id=1, source_target_pairs={{0,2},{1,3},{2,0},{3,1},{4,6},{5,7},{6,4},{7,5},{8,10},{9,11},{10,... | collective-permute-start | bytes 589832 | tf_op jit(solution)/shard_map/ppermute | solution.py:285
  71.1 2.6 %collective-permute-done.21.last = bf16[16,6144]{1,0:T(8,128)(2,1)S(1)} collective-permute-done((bf16[16,6144]{1,0:T(8,128)(2,1)S(1)}, bf16[16,6144]{1,0:T(8,128)(2,1)S(1)}, u32[]{:S(2)}, u32[]{:S(2)}) %collective-permute-start.21) | collective-permute-done | bytes 196640 | tf_op jit(solution)/shard_map/ppermute | solution.py:280
  73.7 1.8 %collective-permute-done.19.near = bf16[16,6144]{1,0:T(8,128)(2,1)S(1)} collective-permute-done((bf16[16,6144]{1,0:T(8,128)(2,1)S(1)}, bf16[16,6144]{1,0:T(8,128)(2,1)S(1)}, u32[]{:S(2)}, u32[]{:S(2)}) %collective-permute-start.19) | collective-permute-done | bytes 196640 | tf_op jit(solution)/shard_map/ppermute | solution.py:280
  75.5 0.0 collective-permute-done.17.arrived
  75.5 0.0 copy-done
  75.5 0.0 copy-done.1
  75.5 0.0 copy-done.2
  75.5 1.3 %mix.1 = bf16[24,6144]{1,0:T(8,128)(2,1)} custom-call(s32[2,24]{1,0:T(2,128)S(1)} %bitcast.4, f32[2,24]{1,0:T(2,128)S(1)} %bitcast.5, bf16[24,6144]{1,0:T(8,128)(2,1)S(1)} %copy-done, bf16[16,6144]{1,0:T(8,128)(2,1)S(1)} %collective-permute-done.17.arrived, bf16[16,6144]{1,0:T(8,128)(2,1)S(1)} %collective-permute-done.19.near, ...), custom_call_target="tpu_custom_call" | custom-call | tf_op jit(solution)/shard_map/mix/pallas_call | solution.py:259
  (19 shorter events, 0.5 us)
Async XLA Ops:
  1.5 14.8 %collective-permute-start.1 = (bf16[16,3072]{1,0:T(8,128)(2,1)S(1)}, bf16[16,3072]{1,0:T(8,128)(2,1)S(1)}, u32[]{:S(2)}, u32[]{:S(2)}) collective-permute-start(bf16[16,3072]{1,0:T(8,128)(2,1)S(1)} %get-tuple-element.45), channel_id=1, source_target_pairs={{0,4},{1,5},{2,6},{3,7},{4,8},{5,9},{6,10},{7,11},{8,12},{9,13},{1... | collective-permute-start | bytes 294920 | tf_op jit(solution)/shard_map/ppermute | solution.py:280
  4.6 11.7 %collective-permute-start.2 = (bf16[16,3072]{1,0:T(8,128)(2,1)S(1)}, bf16[16,3072]{1,0:T(8,128)(2,1)S(1)}, u32[]{:S(2)}, u32[]{:S(2)}) collective-permute-start(bf16[16,3072]{1,0:T(8,128)(2,1)S(1)} %get-tuple-element.46), channel_id=1, source_target_pairs={{0,8},{1,9},{2,10},{3,11},{4,12},{5,13},{6,14},{7,15},{8,0},{9,1},... | collective-permute-start | bytes 294920 | tf_op jit(solution)/shard_map/ppermute | solution.py:280
  7.2 9.2 %collective-permute-start.3 = (bf16[16,3072]{1,0:T(8,128)(2,1)S(1)}, bf16[16,3072]{1,0:T(8,128)(2,1)S(1)}, u32[]{:S(2)}, u32[]{:S(2)}) collective-permute-start(bf16[16,3072]{1,0:T(8,128)(2,1)S(1)} %get-tuple-element.47), channel_id=1, source_target_pairs={{0,12},{1,13},{2,14},{3,15},{4,0},{5,1},{6,2},{7,3},{8,4},{9,5},{1... | collective-permute-start | bytes 294920 | tf_op jit(solution)/shard_map/ppermute | solution.py:280
  8.5 7.8 %collective-permute-start = (bf16[16,6144]{1,0:T(8,128)(2,1)S(1)}, bf16[16,6144]{1,0:T(8,128)(2,1)S(1)}, u32[]{:S(2)}, u32[]{:S(2)}) collective-permute-start(bf16[16,6144]{1,0:T(8,128)(2,1)S(1)} %get-tuple-element.38.after_ref.refs_0_), channel_id=1, source_target_pairs={{0,2},{1,3},{2,0},{3,1},{4,6},{5,7},{6,4},{7,5},{8,10},{9,11},{10,... | collective-permute-start | bytes 589832 | tf_op jit(solution)/shard_map/ppermute | solution.py:285
  16.4 7.3 %collective-permute-start.4 = (bf16[16,3072]{1,0:T(8,128)(2,1)S(1)}, bf16[16,3072]{1,0:T(8,128)(2,1)S(1)}, u32[]{:S(2)}, u32[]{:S(2)}) collective-permute-start(bf16[16,3072]{1,0:T(8,128)(2,1)S(1)} %get-tuple-element.48), channel_id=1, source_target_pairs={{0,4},{1,5},{2,6},{3,7},{4,8},{5,9},{6,10},{7,11},{8,12},{9,13},{1... | collective-permute-start | bytes 294920 | tf_op jit(solution)/shard_map/ppermute | solution.py:280
  17.1 9.1 %collective-permute-start.8 = (bf16[48,3072]{1,0:T(8,128)(2,1)S(1)}, bf16[48,3072]{1,0:T(8,128)(2,1)S(1)}, u32[]{:S(2)}, u32[]{:S(2)}) collective-permute-start(bf16[48,3072]{1,0:T(8,128)(2,1)S(1)} %get-tuple-element.51.refs_3_.refs_1_), channel_id=1, source_target_pairs={{0,2},{1,3},{2,0},{3,1},{4,6},{5,7},{6,4},{7,5},{8,10},{9,11},{10,... | collective-permute-start | bytes 884744 | tf_op jit(solution)/shard_map/ppermute | solution.py:285
  18.0 8.2 %collective-permute-start.5 = (bf16[16,3072]{1,0:T(8,128)(2,1)S(1)}, bf16[16,3072]{1,0:T(8,128)(2,1)S(1)}, u32[]{:S(2)}, u32[]{:S(2)}) collective-permute-start(bf16[16,3072]{1,0:T(8,128)(2,1)S(1)} %get-tuple-element.49), channel_id=1, source_target_pairs={{0,8},{1,9},{2,10},{3,11},{4,12},{5,13},{6,14},{7,15},{8,0},{9,1},... | collective-permute-start | bytes 294920 | tf_op jit(solution)/shard_map/ppermute | solution.py:280
  19.6 6.6 %collective-permute-start.6 = (bf16[16,3072]{1,0:T(8,128)(2,1)S(1)}, bf16[16,3072]{1,0:T(8,128)(2,1)S(1)}, u32[]{:S(2)}, u32[]{:S(2)}) collective-permute-start(bf16[16,3072]{1,0:T(8,128)(2,1)S(1)} %get-tuple-element.50), channel_id=1, source_target_pairs={{0,12},{1,13},{2,14},{3,15},{4,0},{5,1},{6,2},{7,3},{8,4},{9,5},{1... | collective-permute-start | bytes 294920 | tf_op jit(solution)/shard_map/ppermute | solution.py:280
  26.3 2.4 %collective-permute-start.9 = (bf16[128,3072]{1,0:T(8,128)(2,1)S(1)}, bf16[128,3072]{1,0:T(8,128)(2,1)S(1)}, u32[]{:S(2)}, u32[]{:S(2)}) collective-permute-start(bf16[128,3072]{1,0:T(8,128)(2,1)S(1)} %constant_dynamic-update-slice_fusion.6), channel_id=1, source_target_pairs={{0,1},{1,0},{2,3},{3,2},{4,5},{5,4},{6,7},{7,6},{8,9},{9,8},{10,11... | collective-permute-start | bytes 2359304 | tf_op jit(solution)/shard_map/ppermute | solution.py:285
  26.4 9.4 %collective-permute-start.7 = (bf16[48,3072]{1,0:T(8,128)(2,1)S(1)}, bf16[48,3072]{1,0:T(8,128)(2,1)S(1)}, u32[]{:S(2)}, u32[]{:S(2)}) collective-permute-start(bf16[48,3072]{1,0:T(8,128)(2,1)S(1)} %get-tuple-element.90.refs_1_), channel_id=1, source_target_pairs={{0,2},{1,3},{2,0},{3,1},{4,6},{5,7},{6,4},{7,5},{8,10},{9,11},{10,... | collective-permute-start | bytes 884744 | tf_op jit(solution)/shard_map/ppermute | solution.py:285
  35.8 2.4 %collective-permute-start.10 = (bf16[128,3072]{1,0:T(8,128)(2,1)S(1)}, bf16[128,3072]{1,0:T(8,128)(2,1)S(1)}, u32[]{:S(2)}, u32[]{:S(2)}) collective-permute-start(bf16[128,3072]{1,0:T(8,128)(2,1)S(1)} %constant_dynamic-update-slice_fusion.10), channel_id=1, source_target_pairs={{0,1},{1,0},{2,3},{3,2},{4,5},{5,4},{6,7},{7,6},{8,9},{9,8},{10,11... | collective-permute-start | bytes 2359304 | tf_op jit(solution)/shard_map/ppermute | solution.py:285
  45.9 3.3 %collective-permute-start.12 = (bf16[128,3072]{1,0:T(8,128)(2,1)S(1)}, bf16[128,3072]{1,0:T(8,128)(2,1)S(1)}, u32[]{:S(2)}, u32[]{:S(2)}) collective-permute-start(bf16[128,3072]{1,0:T(8,128)(2,1)S(1)} %get-tuple-element.65), channel_id=1, source_target_pairs={{0,1},{1,0},{2,3},{3,2},{4,5},{5,4},{6,7},{7,6},{8,9},{9,8},{10,11... | collective-permute-start | bytes 2359304 | tf_op jit(solution)/shard_map/ppermute | solution.py:285
  48.7 26.7 %copy-start = (bf16[24,6144]{1,0:T(8,128)(2,1)S(1)}, bf16[24,6144]{1,0:T(8,128)(2,1)}, u32[]{:S(2)}) copy-start(bf16[24,6144]{1,0:T(8,128)(2,1)} %act_ref.3) | copy-start | bytes 884740
  48.8 26.7 %copy-start.1 = (s32[24,2]{0,1:T(2,128)S(1)}, s32[24,2]{0,1:T(2,128)}, u32[]{:S(2)}) copy-start(s32[24,2]{0,1:T(2,128)} %param.8) | copy-start | bytes 580
  48.8 26.7 %copy-start.2 = (f32[24,2]{0,1:T(2,128)S(1)}, f32[24,2]{0,1:T(2,128)}, u32[]{:S(2)}) copy-start(f32[24,2]{0,1:T(2,128)} %param.9) | copy-start | bytes 580
  48.8 2.4 %collective-permute-start.11 = (bf16[128,3072]{1,0:T(8,128)(2,1)S(1)}, bf16[128,3072]{1,0:T(8,128)(2,1)S(1)}, u32[]{:S(2)}, u32[]{:S(2)}) collective-permute-start(bf16[128,3072]{1,0:T(8,128)(2,1)S(1)} %get-tuple-element.63), channel_id=1, source_target_pairs={{0,1},{1,0},{2,3},{3,2},{4,5},{5,4},{6,7},{7,6},{8,9},{9,8},{10,11... | collective-permute-start | bytes 2359304 | tf_op jit(solution)/shard_map/ppermute | solution.py:285
  49.5 4.9 %collective-permute-start.15 = (bf16[16,3072]{1,0:T(8,128)(2,1)S(1)}, bf16[16,3072]{1,0:T(8,128)(2,1)S(1)}, u32[]{:S(2)}, u32[]{:S(2)}) collective-permute-start(bf16[16,3072]{1,0:T(8,128)(2,1)S(1)} %get-tuple-element.74), channel_id=1, source_target_pairs={{0,2},{1,3},{2,0},{3,1},{4,6},{5,7},{6,4},{7,5},{8,10},{9,11},{10,... | collective-permute-start | bytes 294920 | tf_op jit(solution)/shard_map/ppermute | solution.py:285
  51.4 5.1 %collective-permute-start.13 = (bf16[16,3072]{1,0:T(8,128)(2,1)S(1)}, bf16[16,3072]{1,0:T(8,128)(2,1)S(1)}, u32[]{:S(2)}, u32[]{:S(2)}) collective-permute-start(bf16[16,3072]{1,0:T(8,128)(2,1)S(1)} %get-tuple-element.82), channel_id=1, source_target_pairs={{0,2},{1,3},{2,0},{3,1},{4,6},{5,7},{6,4},{7,5},{8,10},{9,11},{10,... | collective-permute-start | bytes 294920 | tf_op jit(solution)/shard_map/ppermute | solution.py:285
  54.4 10.4 %collective-permute-start.20 = (bf16[16,3072]{1,0:T(8,128)(2,1)S(1)}, bf16[16,3072]{1,0:T(8,128)(2,1)S(1)}, u32[]{:S(2)}, u32[]{:S(2)}) collective-permute-start(bf16[16,3072]{1,0:T(8,128)(2,1)S(1)} %add_convert_fusion.4), channel_id=1, source_target_pairs={{0,8},{1,9},{2,10},{3,11},{4,12},{5,13},{6,14},{7,15},{8,0},{9,1},... | collective-permute-start | bytes 294920 | tf_op jit(solution)/shard_map/ppermute | solution.py:280
  56.5 7.8 %collective-permute-start.16 = (bf16[16,6144]{1,0:T(8,128)(2,1)S(1)}, bf16[16,6144]{1,0:T(8,128)(2,1)S(1)}, u32[]{:S(2)}, u32[]{:S(2)}) collective-permute-start(bf16[16,6144]{1,0:T(8,128)(2,1)S(1)} %get-tuple-element.67), channel_id=1, source_target_pairs={{0,2},{1,3},{2,0},{3,1},{4,6},{5,7},{6,4},{7,5},{8,10},{9,11},{10,... | collective-permute-start | bytes 589832 | tf_op jit(solution)/shard_map/ppermute | solution.py:285
  57.5 10.9 %collective-permute-start.18 = (bf16[16,3072]{1,0:T(8,128)(2,1)S(1)}, bf16[16,3072]{1,0:T(8,128)(2,1)S(1)}, u32[]{:S(2)}, u32[]{:S(2)}) collective-permute-start(bf16[16,3072]{1,0:T(8,128)(2,1)S(1)} %add_convert_fusion.5), channel_id=1, source_target_pairs={{0,8},{1,9},{2,10},{3,11},{4,12},{5,13},{6,14},{7,15},{8,0},{9,1},... | collective-permute-start | bytes 294920 | tf_op jit(solution)/shard_map/ppermute | solution.py:280
  58.7 8.4 %collective-permute-start.14 = (bf16[16,6144]{1,0:T(8,128)(2,1)S(1)}, bf16[16,6144]{1,0:T(8,128)(2,1)S(1)}, u32[]{:S(2)}, u32[]{:S(2)}) collective-permute-start(bf16[16,6144]{1,0:T(8,128)(2,1)S(1)} %get-tuple-element.66), channel_id=1, source_target_pairs={{0,2},{1,3},{2,0},{3,1},{4,6},{5,7},{6,4},{7,5},{8,10},{9,11},{10,... | collective-permute-start | bytes 589832 | tf_op jit(solution)/shard_map/ppermute | solution.py:285
  64.8 8.8 %collective-permute-start.21 = (bf16[16,6144]{1,0:T(8,128)(2,1)S(1)}, bf16[16,6144]{1,0:T(8,128)(2,1)S(1)}, u32[]{:S(2)}, u32[]{:S(2)}) collective-permute-start(bf16[16,6144]{1,0:T(8,128)(2,1)S(1)} %add_convert_fusion.2), channel_id=1, source_target_pairs={{0,4},{1,5},{2,6},{3,7},{4,8},{5,9},{6,10},{7,11},{8,12},{9,13},{1... | collective-permute-start | bytes 589832 | tf_op jit(solution)/shard_map/ppermute | solution.py:280
  68.4 7.0 %collective-permute-start.19 = (bf16[16,6144]{1,0:T(8,128)(2,1)S(1)}, bf16[16,6144]{1,0:T(8,128)(2,1)S(1)}, u32[]{:S(2)}, u32[]{:S(2)}) collective-permute-start(bf16[16,6144]{1,0:T(8,128)(2,1)S(1)} %add_convert_fusion.3), channel_id=1, source_target_pairs={{0,12},{1,13},{2,14},{3,15},{4,0},{5,1},{6,2},{7,3},{8,4},{9,5},{1... | collective-permute-start | bytes 589832 | tf_op jit(solution)/shard_map/ppermute | solution.py:280
  69.6 5.8 %collective-permute-start.17 = (bf16[16,6144]{1,0:T(8,128)(2,1)S(1)}, bf16[16,6144]{1,0:T(8,128)(2,1)S(1)}, u32[]{:S(2)}, u32[]{:S(2)}) collective-permute-start(bf16[16,6144]{1,0:T(8,128)(2,1)S(1)} %pad_maximum_fusion), channel_id=1, source_target_pairs={{0,2},{1,3},{2,0},{3,1},{4,6},{5,7},{6,4},{7,5},{8,10},{9,11},{10,... | collective-permute-start | bytes 589832 | tf_op jit(solution)/shard_map/ppermute | solution.py:285

commit v11 on v10

--- a/solution.py
+++ b/solution.py
@@ -10,13 +10,21 @@
 EXPERTS = 4
 CAP = 16
 HALVES = 2
-BLOCK = 1024
+ORDER = (2, 1, 3)
+FORTH = (7, 5)
+BLOCK = 512
+WIDE_BLOCK = 1024
 FETCH_ROWS = 144
 MIB = 1 << 20
 LIMIT = pltpu.CompilerParams(vmem_limit_bytes=10 * MIB)
 WIDE = pltpu.CompilerParams(vmem_limit_bytes=32 * MIB)
 VMEM = pl.BlockSpec(memory_space=pltpu.VMEM)
 ANY = pl.BlockSpec(memory_space=pl.ANY)
+
+
+def spans(width):
+    unit = width // sum(FORTH)
+    return [(sum(FORTH[:k]) * unit, n * unit) for k, n in enumerate(FORTH)]
 
 
 def choices(ids, plane):
@@ -45,15 +53,15 @@
     pick = (first | second).astype(jnp.float32).astype(jnp.bfloat16)
     rows = jnp.dot(pick, normed, preferred_element_type=jnp.float32).astype(jnp.bfloat16)
     out_refs[0][...] = rows[:CAP]
-    part = out_refs[-1].shape[1]
     for j, out_ref in enumerate(out_refs[1:]):
         k, s = j // (EXPERTS - 1), j % (EXPERTS - 1) + 1
-        out_ref[...] = rows[s * CAP : (s + 1) * CAP, k * part : (k + 1) * part]
+        at, part = spans(rows.shape[1])[k]
+        out_ref[...] = rows[s * CAP : (s + 1) * CAP, at : at + part]
 
 
 def pack(group, ids, activations, gain):
     width = activations.shape[1]
-    widths = [width] + [width // HALVES] * (HALVES * (EXPERTS - 1))
+    widths = [width] + [part for _, part in spans(width) for _ in range(EXPERTS - 1)]
     operands = [ids, activations, gain.reshape(1, width)]
     return pl.pallas_call(
         functools.partial(pack_kernel, group),
@@ -151,12 +159,13 @@
         copy.wait()
 
 
-def gate_up(k, pieces, weights, later, totals):
+def gate_up(k, pieces, weights, later, ahead, totals):
     hidden, part = weights[0].shape
     begin, end = k == 0, k == HALVES - 1
+    width = later[0].shape[1]
     rows = sum(p.shape[0] for p in pieces)
     total = jax.ShapeDtypeStruct((hidden, rows), jnp.float32)
-    out_shape = [pltpu.VMEM((hidden, part), jnp.bfloat16)] * len(later)
+    out_shape = [pltpu.VMEM((hidden, ahead[1]), jnp.bfloat16)] * len(later)
     out_specs = [VMEM] * len(later)
     scratch = []
     if end:
@@ -170,7 +179,9 @@
     weights = [pltpu.with_memory_space_constraint(w, pltpu.VMEM) for w in weights]
     later = [pltpu.with_memory_space_constraint(w, pltpu.HBM) for w in later]
     out = pl.pallas_call(
-        functools.partial(gate_up_kernel, len(pieces), len(later), k * part, part, begin, end),
+        functools.partial(
+            gate_up_kernel, len(pieces), len(later), spans(width)[k][0], ahead[0], begin, end
+        ),
         in_specs=[VMEM] * (len(pieces) + 2) + [ANY] * len(later) + [VMEM] * len(totals),
         out_specs=out_specs,
         out_shape=out_shape,
@@ -190,13 +201,13 @@
     later, held, refs = refs[:ahead], refs[ahead : 2 * ahead], refs[2 * ahead :]
     keep_ref, send_ref, sems = refs
     half, part = keep_ref.shape
-    copies = fetches(later, 0, held, sems)
+    copies = fetches(later, part, held, sems)
     for copy in copies:
         copy.start()
 
-    @pl.loop(0, part // BLOCK)
+    @pl.loop(0, part // WIDE_BLOCK)
     def _(c):
-        columns = pl.ds(pl.multiple_of(c * BLOCK, BLOCK), BLOCK)
+        columns = pl.ds(pl.multiple_of(c * WIDE_BLOCK, WIDE_BLOCK), WIDE_BLOCK)
         out = jnp.dot(hidden_ref[...], w_ref[:, columns], preferred_element_type=jnp.float32)
         out = out.astype(jnp.bfloat16)
         keep_ref[:, columns] = out[:half]
@@ -291,17 +302,18 @@
     ids = expert_ids.T
     own, *sends = pack(group, ids, activations, norm_gain)
     far_own = swap(own, far)
-    now = [fetch(w, 0, part, own) for w in (w_gate, w_up)]
+    now = [fetch(w, 0, spans(width)[0][1], own) for w in (w_gate, w_up)]
     blocks = []
     for k in range(HALVES):
         x = sends[k * others : (k + 1) * others]
         if k:
             x = relay(after(x, *now, far_own), blocks[-1])
-        arrivals = [shift(x[s], s + 1) for s in range(others)]
+        arrivals = [shift(x[s - 1], s) for s in ORDER]
         blocks.append(jnp.concatenate(arrivals, axis=0))
     totals = []
     for k in range(HALVES):
-        columns = slice(k * part, (k + 1) * part)
+        at, size = spans(width)[k]
+        columns = slice(at, at + size)
         far_block = swap(blocks[k], far)
         if totals:
             far_block, totals = lax.optimization_barrier((far_block, totals))
@@ -313,28 +325,31 @@
         pieces[0], pieces[2] = own, far_own
         if k < HALVES - 1:
             pieces[1] = after(pieces[1], blocks[k + 1])
-        later = [w_down] if k == HALVES - 1 else [w_gate, w_up]
-        now, totals = gate_up(k, pieces, now, later, totals)
+        later, ahead = [w_gate, w_up], (size, width - size)
+        if k == HALVES - 1:
+            later, ahead = [w_down], (0, part)
+        now, totals = gate_up(k, pieces, now, later, ahead, totals)
     hidden = totals[0]
     held = []
-    for k in reversed(range(HALVES)):
-        later = [w_down] if k else []
+    for k in range(HALVES):
+        later = [w_down] if k == 0 else []
         now, (keep, send) = down(hidden, now[0], later)
         bit = 1
         while bit < far:
             total = added(keep, swap(send, bit))
             keep, send = total[: total.shape[0] // 2], total[total.shape[0] // 2 :]
             bit *= 2
-        held.insert(0, [total[j * CAP : (j + 1) * CAP] for j in range(2 * EXPERTS)])
-    crossed = [swap(h[6], far) for h in held]
-    middle = [shift(added(h[2], x), -2) for h, x in zip(held, crossed)]
+        held.append([total[j * CAP : (j + 1) * CAP] for j in range(2 * EXPERTS)])
+    place = {s: 1 + j for j, s in enumerate(ORDER)}
+    crossed = [swap(h[EXPERTS + place[2]], far) for h in held]
+    middle = [shift(added(h[place[2]], x), -2) for h, x in zip(held, crossed)]
     mine = [jnp.concatenate([h[j] for h in held], axis=1) for j in range(2 * EXPERTS)]
     back = {}
-    back[1] = swap(after(mine[EXPERTS + 1], crossed[0]), far)
-    back[3] = swap(after(mine[EXPERTS + 3], *crossed), far)
+    back[1] = swap(after(mine[EXPERTS + place[1]], crossed[0]), far)
+    back[3] = swap(after(mine[EXPERTS + place[3]], *crossed), far)
     back[0] = swap(after(mine[EXPERTS], back[1], back[3]), far)
-    near = shift(after(added(mine[1], back[1]), middle[0]), -1)
-    last = shift(after(added(mine[3], back[3]), middle[1]), -3)
+    near = shift(after(added(mine[place[1]], back[1]), middle[1]), -1)
+    last = shift(after(added(mine[place[3]], back[3]), middle[0]), -3)
     arrived = back[0]
     pieces = [arrived, near, last, *[h[0] for h in held], *middle]
     return mix(group, ids, route_logits.T, activations, pieces)

time: 76.9 us -> 75.8 us (0.986)
  waiting for transfers between devices: 24.6 us -> 21.3 us
  starting transfers between devices: 26.5 us -> 28.2 us
    ppermute x10, waiting for transfers between devices: 11.4 us -> 8.21 us  [shift(): lax.ppermute(x, 'expert', [(i, (i + s * group) % devices) for i in range(...]
    ppermute x10, starting transfers between devices: 16.5 us -> 19.7 us  [shift(): lax.ppermute(x, 'expert', [(i, (i + s * group) % devices) for i in range(...]
    ppermute x12, starting transfers between devices: 10 us -> 8.55 us  [swap(): return lax.ppermute(x, 'expert', [(i, i ^ bit) for i in range(devices)])]
  transfers between devices with their start and end apart: 22 -> 22, of which waited for: 14 -> 12; matrix products, arithmetic and copies ran while one was open for 1% -> 1% of each run, Pallas kernels for 18% -> 20%
where the time goes in v11:
time: 75.8 us; the launch traced here: 75.6 us
  starting transfers between devices  28.2 us (37%)
  Pallas kernels  25 us (33%)
  waiting for transfers between devices  21.3 us (28%)
    ppermute x10, starting transfers between devices, shift(): lax.ppermute(x, 'expert', [(i, (i + s * group) % devices) for i in range(...  19.7 us
    ppermute x12, waiting for transfers between devices, swap(): return lax.ppermute(x, 'expert', [(i, i ^ bit) for i in range(devices)])  13.1 us
    pallas_call x2, Pallas kernels, gate_up(): pl.pallas_call(functools.partial(gate_up_kernel, len(pieces), len(later),...  9.57 us
    ppermute x12, starting transfers between devices, swap(): return lax.ppermute(x, 'expert', [(i, i ^ bit) for i in range(devices)])  8.55 us
    ppermute x10, waiting for transfers between devices, shift(): lax.ppermute(x, 'expert', [(i, (i + s * group) % devices) for i in range(...  8.21 us
    pallas_call x2, Pallas kernels, fetch(): pl.pallas_call(functools.partial(fetch_kernel, at), in_specs=[ANY, ANY],...  6.88 us
    pallas_call x2, Pallas kernels, down(): pl.pallas_call(functools.partial(down_kernel, ahead), in_specs=[VMEM, VME...  5.75 us
  transfers between devices with their start and end apart: 22, of which 12 were waited for; matrix products, arithmetic and copies ran while one was open for 1% of the time, Pallas kernels for 20%

profile of v11, /device:TPU:0, one launch (start us, length us, event | category | flops | bytes accessed | tf_op | source)
XLA Modules:
  0.0 75.6 jit_solution(1078273665153788626)
XLA Ops:
  0.0 1.5 %norm_and_pack.1 = (bf16[16,6144]{1,0:T(8,128)(2,1)S(1)}, bf16[16,3584]{1,0:T(8,128)(2,1)S(1)}, bf16[16,3584]{1,0:T(8,128)(2,1)S(1)}, bf16[16,3584]{1,0:T(8,128)...) custom-call(s32[2,24]{1,0:T(2,128)} %bitcast.3, ...), custom_call_target="tpu_custom_call" | custom-call | tf_op jit(solution)/shard_map/norm_and_pack/pallas_call | solution.py:66
  1.5 4.1 %collective-permute-start.1 = (bf16[16,3584]{1,0:T(8,128)(2,1)S(1)}, bf16[16,3584]{1,0:T(8,128)(2,1)S(1)}, u32[]{:S(2)}, u32[]{:S(2)}) collective-permute-start(bf16[16,3584]{1,0:T(8,128)(2,1)S(1)} %get-tuple-element.45), channel_id=1, source_target_pairs={{0,8},{1,9},{2,10},{3,11},{4,12},{5,13},{6,14},{7,15},{8,0},{9,1},... | collective-permute-start | bytes 344072 | tf_op jit(solution)/shard_map/ppermute | solution.py:291
  5.6 1.6 %collective-permute-start.2 = (bf16[16,3584]{1,0:T(8,128)(2,1)S(1)}, bf16[16,3584]{1,0:T(8,128)(2,1)S(1)}, u32[]{:S(2)}, u32[]{:S(2)}) collective-permute-start(bf16[16,3584]{1,0:T(8,128)(2,1)S(1)} %get-tuple-element.46), channel_id=1, source_target_pairs={{0,4},{1,5},{2,6},{3,7},{4,8},{5,9},{6,10},{7,11},{8,12},{9,13},{1... | collective-permute-start | bytes 344072 | tf_op jit(solution)/shard_map/ppermute | solution.py:291
  7.2 2.2 %collective-permute-start.3 = (bf16[16,3584]{1,0:T(8,128)(2,1)S(1)}, bf16[16,3584]{1,0:T(8,128)(2,1)S(1)}, u32[]{:S(2)}, u32[]{:S(2)}) collective-permute-start(bf16[16,3584]{1,0:T(8,128)(2,1)S(1)} %get-tuple-element.47), channel_id=1, source_target_pairs={{0,12},{1,13},{2,14},{3,15},{4,0},{5,1},{6,2},{7,3},{8,4},{9,5},{1... | collective-permute-start | bytes 344072 | tf_op jit(solution)/shard_map/ppermute | solution.py:291
  9.4 1.5 %collective-permute-start = (bf16[16,6144]{1,0:T(8,128)(2,1)S(1)}, bf16[16,6144]{1,0:T(8,128)(2,1)S(1)}, u32[]{:S(2)}, u32[]{:S(2)}) collective-permute-start(bf16[16,6144]{1,0:T(8,128)(2,1)S(1)} %get-tuple-element.38.after_ref.refs_0_), channel_id=1, source_target_pairs={{0,2},{1,3},{2,0},{3,1},{4,6},{5,7},{6,4},{7,5},{8,10},{9,11},{10,... | collective-permute-start | bytes 589832 | tf_op jit(solution)/shard_map/ppermute | solution.py:296
  11.0 3.4 %fetch.3.refs_6_ = bf16[1152,3584]{1,0:T(8,128)(2,1)S(1)} custom-call(bf16[1152,6144]{1,0:T(8,128)(2,1)} %refs_8_.1, bf16[16,6144]{1,0:T(8,128)(2,1)S(1)} %get-tuple-element.38.after_ref.refs_0_), custom_call_target="tpu_custom_call" | custom-call | bytes 16515072 | tf_op jit(solution)/shard_map/fetch/pallas_call | solution.py:99
  14.4 3.4 %fetch.2.refs_5_ = bf16[1152,3584]{1,0:T(8,128)(2,1)S(1)} custom-call(bf16[1152,6144]{1,0:T(8,128)(2,1)} %refs_7_.2, bf16[16,6144]{1,0:T(8,128)(2,1)S(1)} %get-tuple-element.38.after_ref.refs_0_), custom_call_target="tpu_custom_call" | custom-call | bytes 16515072 | tf_op jit(solution)/shard_map/fetch/pallas_call | solution.py:99
  17.9 0.0 collective-permute-done.1
  17.9 0.0 collective-permute-done.2
  17.9 0.0 collective-permute-done.3
  18.0 0.6 collective-permute-start.8
  18.5 0.0 collective-permute-done.refs_2_
  18.6 1.9 %collective-permute-start.4 = (bf16[16,2560]{1,0:T(8,128)(2,1)S(1)}, bf16[16,2560]{1,0:T(8,128)(2,1)S(1)}, u32[]{:S(2)}, u32[]{:S(2)}) collective-permute-start(bf16[16,2560]{1,0:T(8,128)(2,1)S(1)} %get-tuple-element.48), channel_id=1, source_target_pairs={{0,8},{1,9},{2,10},{3,11},{4,12},{5,13},{6,14},{7,15},{8,0},{9,1},... | collective-permute-start | bytes 245768 | tf_op jit(solution)/shard_map/ppermute | solution.py:291
  20.5 0.0 collective-permute-start.5
  20.5 3.8 %collective-permute-start.6 = (bf16[16,2560]{1,0:T(8,128)(2,1)S(1)}, bf16[16,2560]{1,0:T(8,128)(2,1)S(1)}, u32[]{:S(2)}, u32[]{:S(2)}) collective-permute-start(bf16[16,2560]{1,0:T(8,128)(2,1)S(1)} %get-tuple-element.50), channel_id=1, source_target_pairs={{0,12},{1,13},{2,14},{3,15},{4,0},{5,1},{6,2},{7,3},{8,4},{9,5},{1... | collective-permute-start | bytes 245768 | tf_op jit(solution)/shard_map/ppermute | solution.py:291
  24.3 1.8 %collective-permute-done.4 = bf16[16,2560]{1,0:T(8,128)(2,1)S(1)} collective-permute-done((bf16[16,2560]{1,0:T(8,128)(2,1)S(1)}, bf16[16,2560]{1,0:T(8,128)(2,1)S(1)}, u32[]{:S(2)}, u32[]{:S(2)}) %collective-permute-start.4) | collective-permute-done | bytes 81952 | tf_op jit(solution)/shard_map/ppermute | solution.py:291
  26.2 0.9 %collective-permute-done.5 = bf16[16,2560]{1,0:T(8,128)(2,1)S(1)} collective-permute-done((bf16[16,2560]{1,0:T(8,128)(2,1)S(1)}, bf16[16,2560]{1,0:T(8,128)(2,1)S(1)}, u32[]{:S(2)}, u32[]{:S(2)}) %collective-permute-start.5) | collective-permute-done | bytes 81952 | tf_op jit(solution)/shard_map/ppermute | solution.py:291
  27.1 0.0 collective-permute-done.8.refs_3_
  27.2 0.1 collective-permute-start.9
  27.3 0.0 collective-permute-done.6
  27.3 1.1 %collective-permute-start.7 = (bf16[48,2560]{1,0:T(8,128)(2,1)S(1)}, bf16[48,2560]{1,0:T(8,128)(2,1)S(1)}, u32[]{:S(2)}, u32[]{:S(2)}) collective-permute-start(bf16[48,2560]{1,0:T(8,128)(2,1)S(1)} %get-tuple-element.92.refs_1_), channel_id=1, source_target_pairs={{0,2},{1,3},{2,0},{3,1},{4,6},{5,7},{6,4},{7,5},{8,10},{9,11},{10,... | collective-permute-start | bytes 737288 | tf_op jit(solution)/shard_map/ppermute | solution.py:296
  28.4 1.3 %collective-permute-done.9.refs_4_ = bf16[128,3584]{1,0:T(8,128)(2,1)S(1)} collective-permute-done((bf16[128,3584]{1,0:T(8,128)(2,1)S(1)}, bf16[128,3584]{1,0:T(8,128)(2,1)S(1)}, u32[]{:S(2)}, u32[]{:S(2)}) %collective-permute-start.9) | collective-permute-done | bytes 917536 | tf_op jit(solution)/shard_map/ppermute | solution.py:296
  29.7 5.5 %gate_up.2 = (bf16[1152,2560]{1,0:T(8,128)(2,1)S(1)}, bf16[1152,2560]{1,0:T(8,128)(2,1)S(1)}, f32[1152,256]{1,0:T(8,128)S(1)}, f32[1152,256]{1,0:T(8,128)S(1)}) custom-call(bf16[16,6144]{1,0:T(8,128)(2,1)S(1)} %get-tuple-element.38.after_ref.refs_0_, bf16[48,3584]{1,0:T(8,128)(2,1)S(1)} %get-tuple-element.51.refs_3_.refs_1_, ...), custom_call_target="tpu_custom_call" | custom-call | flops 4227858432 | bytes 18874368 | tf_op jit(solution)/shard_map/gate_up/pallas_call | solution.py:181
  35.2 0.5 collective-permute-done.7.refs_3_
  35.7 0.1 collective-permute-start.10
  35.8 2.1 %collective-permute-done.10.refs_4_ = bf16[128,2560]{1,0:T(8,128)(2,1)S(1)} collective-permute-done((bf16[128,2560]{1,0:T(8,128)(2,1)S(1)}, bf16[128,2560]{1,0:T(8,128)(2,1)S(1)}, u32[]{:S(2)}, u32[]{:S(2)}) %collective-permute-start.10) | collective-permute-done | bytes 655392 | tf_op jit(solution)/shard_map/ppermute | solution.py:296
  37.9 4.1 %gate_up.3 = (bf16[1152,3072]{1,0:T(8,128)(2,1)S(1)}, bf16[256,1152]{1,0:T(8,128)(2,1)S(1)}) custom-call(bf16[16,6144]{1,0:T(8,128)(2,1)S(1)} %get-tuple-element.38.after_ref.refs_0_, bf16[48,2560]{1,0:T(8,128)(2,1)S(1)} %get-tuple-element.92.refs_1_, bf16[16,6144]{1,0:T(8,128)(2,1)S(1)} %collective-permute-done.refs_2_, ...), custom_call_target="tpu_custom_call" | custom-call | flops 3019898880 | bytes 14155776 | tf_op jit(solution)/shard_map/gate_up/pallas_call | solution.py:181
  42.0 3.1 %down.2 = (bf16[1152,3072]{1,0:T(8,128)(2,1)S(1)}, bf16[128,3072]{1,0:T(8,128)(2,1)S(1)}, bf16[128,3072]{1,0:T(8,128)(2,1)S(1)}) custom-call(bf16[256,1152]{1,0:T(8,128)(2,1)S(1)} %get-tuple-element.59.hidden_ref, bf16[1152,3072]{1,0:T(8,128)(2,1)S(1)} %get-tuple-element.60.w_ref, bf16[1152,6144]{1,0:T(8,128)(2,1)} %refs_0_.1), custom_call_target="tpu_custom_call" | custom-call | flops 1811939328 | bytes 9240576 | tf_op jit(solution)/shard_map/down/pallas_call | solution.py:228
  45.1 0.2 collective-permute-start.11
  45.3 2.7 %down.3 = (bf16[128,3072]{1,0:T(8,128)(2,1)S(1)}, bf16[128,3072]{1,0:T(8,128)(2,1)S(1)}) custom-call(bf16[256,1152]{1,0:T(8,128)(2,1)S(1)} %get-tuple-element.59.hidden_ref, bf16[1152,3072]{1,0:T(8,128)(2,1)S(1)} %get-tuple-element.63.w_ref), custom_call_target="tpu_custom_call" | custom-call | flops 1811939328 | bytes 9240576 | tf_op jit(solution)/shard_map/down/pallas_call | solution.py:228
  47.9 0.0 copy-start
  48.0 0.0 copy-start.1
  48.0 0.0 copy-start.2
  48.0 0.4 collective-permute-start.12
  48.4 0.0 collective-permute-done.11
  48.4 0.2 add_convert_fusion.1
  48.7 1.0 %collective-permute-start.13 = (bf16[16,3072]{1,0:T(8,128)(2,1)S(1)}, bf16[16,3072]{1,0:T(8,128)(2,1)S(1)}, u32[]{:S(2)}, u32[]{:S(2)}) collective-permute-start(bf16[16,3072]{1,0:T(8,128)(2,1)S(1)} %get-tuple-element.82), channel_id=1, source_target_pairs={{0,2},{1,3},{2,0},{3,1},{4,6},{5,7},{6,4},{7,5},{8,10},{9,11},{10,... | collective-permute-start | bytes 294920 | tf_op jit(solution)/shard_map/ppermute | solution.py:296
  49.6 0.7 collective-permute-done.12
  50.3 0.2 add_convert_fusion
  50.6 1.0 %collective-permute-start.15 = (bf16[16,3072]{1,0:T(8,128)(2,1)S(1)}, bf16[16,3072]{1,0:T(8,128)(2,1)S(1)}, u32[]{:S(2)}, u32[]{:S(2)}) collective-permute-start(bf16[16,3072]{1,0:T(8,128)(2,1)S(1)} %get-tuple-element.74), channel_id=1, source_target_pairs={{0,2},{1,3},{2,0},{3,1},{4,6},{5,7},{6,4},{7,5},{8,10},{9,11},{10,... | collective-permute-start | bytes 294920 | tf_op jit(solution)/shard_map/ppermute | solution.py:296
  51.6 2.0 %collective-permute-done.13 = bf16[16,3072]{1,0:T(8,128)(2,1)S(1)} collective-permute-done((bf16[16,3072]{1,0:T(8,128)(2,1)S(1)}, bf16[16,3072]{1,0:T(8,128)(2,1)S(1)}, u32[]{:S(2)}, u32[]{:S(2)}) %collective-permute-start.13) | collective-permute-done | bytes 98336 | tf_op jit(solution)/shard_map/ppermute | solution.py:296
  53.6 1.8 %collective-permute-start.20 = (bf16[16,3072]{1,0:T(8,128)(2,1)S(1)}, bf16[16,3072]{1,0:T(8,128)(2,1)S(1)}, u32[]{:S(2)}, u32[]{:S(2)}) collective-permute-start(bf16[16,3072]{1,0:T(8,128)(2,1)S(1)} %add_convert_fusion.4), channel_id=1, source_target_pairs={{0,8},{1,9},{2,10},{3,11},{4,12},{5,13},{6,14},{7,15},{8,0},{9,1},... | collective-permute-start | bytes 294920 | tf_op jit(solution)/shard_map/ppermute | solution.py:291
  55.4 0.4 collective-permute-done.15
  55.7 1.2 %collective-permute-start.16 = (bf16[16,6144]{1,0:T(8,128)(2,1)S(1)}, bf16[16,6144]{1,0:T(8,128)(2,1)S(1)}, u32[]{:S(2)}, u32[]{:S(2)}) collective-permute-start(bf16[16,6144]{1,0:T(8,128)(2,1)S(1)} %get-tuple-element.67), channel_id=1, source_target_pairs={{0,2},{1,3},{2,0},{3,1},{4,6},{5,7},{6,4},{7,5},{8,10},{9,11},{10,... | collective-permute-start | bytes 589832 | tf_op jit(solution)/shard_map/ppermute | solution.py:296
  56.9 2.1 %collective-permute-start.18 = (bf16[16,3072]{1,0:T(8,128)(2,1)S(1)}, bf16[16,3072]{1,0:T(8,128)(2,1)S(1)}, u32[]{:S(2)}, u32[]{:S(2)}) collective-permute-start(bf16[16,3072]{1,0:T(8,128)(2,1)S(1)} %add_convert_fusion.5), channel_id=1, source_target_pairs={{0,8},{1,9},{2,10},{3,11},{4,12},{5,13},{6,14},{7,15},{8,0},{9,1},... | collective-permute-start | bytes 294920 | tf_op jit(solution)/shard_map/ppermute | solution.py:291
  59.0 0.5 collective-permute-start.14
  59.6 4.0 %collective-permute-done.16 = bf16[16,6144]{1,0:T(8,128)(2,1)S(1)} collective-permute-done((bf16[16,6144]{1,0:T(8,128)(2,1)S(1)}, bf16[16,6144]{1,0:T(8,128)(2,1)S(1)}, u32[]{:S(2)}, u32[]{:S(2)}) %collective-permute-start.16) | collective-permute-done | bytes 196640 | tf_op jit(solution)/shard_map/ppermute | solution.py:296
  63.5 0.1 add_convert_fusion.2
  63.6 0.0 collective-permute-done.20.refs_2_
  63.6 0.5 collective-permute-start.21
  64.1 2.2 %collective-permute-done.14 = bf16[16,6144]{1,0:T(8,128)(2,1)S(1)} collective-permute-done((bf16[16,6144]{1,0:T(8,128)(2,1)S(1)}, bf16[16,6144]{1,0:T(8,128)(2,1)S(1)}, u32[]{:S(2)}, u32[]{:S(2)}) %collective-permute-start.14) | collective-permute-done | bytes 196640 | tf_op jit(solution)/shard_map/ppermute | solution.py:296
  66.4 0.0 collective-permute-done.18.refs_3_
  66.4 1.0 %collective-permute-start.17 = (bf16[16,6144]{1,0:T(8,128)(2,1)S(1)}, bf16[16,6144]{1,0:T(8,128)(2,1)S(1)}, u32[]{:S(2)}, u32[]{:S(2)}) collective-permute-start(bf16[16,6144]{1,0:T(8,128)(2,1)S(1)} %pad_maximum_fusion), channel_id=1, source_target_pairs={{0,2},{1,3},{2,0},{3,1},{4,6},{5,7},{6,4},{7,5},{8,10},{9,11},{10,... | collective-permute-start | bytes 589832 | tf_op jit(solution)/shard_map/ppermute | solution.py:296
  67.3 1.6 %collective-permute-start.19 = (bf16[16,6144]{1,0:T(8,128)(2,1)S(1)}, bf16[16,6144]{1,0:T(8,128)(2,1)S(1)}, u32[]{:S(2)}, u32[]{:S(2)}) collective-permute-start(bf16[16,6144]{1,0:T(8,128)(2,1)S(1)} %add_convert_fusion.3), channel_id=1, source_target_pairs={{0,12},{1,13},{2,14},{3,15},{4,0},{5,1},{6,2},{7,3},{8,4},{9,5},{1... | collective-permute-start | bytes 589832 | tf_op jit(solution)/shard_map/ppermute | solution.py:291
  68.9 3.3 %collective-permute-done.21.last = bf16[16,6144]{1,0:T(8,128)(2,1)S(1)} collective-permute-done((bf16[16,6144]{1,0:T(8,128)(2,1)S(1)}, bf16[16,6144]{1,0:T(8,128)(2,1)S(1)}, u32[]{:S(2)}, u32[]{:S(2)}) %collective-permute-start.21) | collective-permute-done | bytes 196640 | tf_op jit(solution)/shard_map/ppermute | solution.py:291
  72.2 0.0 collective-permute-done.17.arrived
  72.2 2.1 %collective-permute-done.19.near = bf16[16,6144]{1,0:T(8,128)(2,1)S(1)} collective-permute-done((bf16[16,6144]{1,0:T(8,128)(2,1)S(1)}, bf16[16,6144]{1,0:T(8,128)(2,1)S(1)}, u32[]{:S(2)}, u32[]{:S(2)}) %collective-permute-start.19) | collective-permute-done | bytes 196640 | tf_op jit(solution)/shard_map/ppermute | solution.py:291
  74.3 0.0 copy-done
  74.3 0.0 copy-done.1
  74.3 0.0 copy-done.2
  74.3 1.3 %mix.1 = bf16[24,6144]{1,0:T(8,128)(2,1)} custom-call(s32[2,24]{1,0:T(2,128)S(1)} %bitcast.4, f32[2,24]{1,0:T(2,128)S(1)} %bitcast.5, bf16[24,6144]{1,0:T(8,128)(2,1)S(1)} %copy-done, bf16[16,6144]{1,0:T(8,128)(2,1)S(1)} %collective-permute-done.17.arrived, bf16[16,6144]{1,0:T(8,128)(2,1)S(1)} %collective-permute-done.19.near, ...), custom_call_target="tpu_custom_call" | custom-call | tf_op jit(solution)/shard_map/mix/pallas_call | solution.py:270
  (20 shorter events, 0.4 us)
Async XLA Ops:
  1.5 16.4 %collective-permute-start.1 = (bf16[16,3584]{1,0:T(8,128)(2,1)S(1)}, bf16[16,3584]{1,0:T(8,128)(2,1)S(1)}, u32[]{:S(2)}, u32[]{:S(2)}) collective-permute-start(bf16[16,3584]{1,0:T(8,128)(2,1)S(1)} %get-tuple-element.45), channel_id=1, source_target_pairs={{0,8},{1,9},{2,10},{3,11},{4,12},{5,13},{6,14},{7,15},{8,0},{9,1},... | collective-permute-start | bytes 344072 | tf_op jit(solution)/shard_map/ppermute | solution.py:291
  5.6 12.3 %collective-permute-start.2 = (bf16[16,3584]{1,0:T(8,128)(2,1)S(1)}, bf16[16,3584]{1,0:T(8,128)(2,1)S(1)}, u32[]{:S(2)}, u32[]{:S(2)}) collective-permute-start(bf16[16,3584]{1,0:T(8,128)(2,1)S(1)} %get-tuple-element.46), channel_id=1, source_target_pairs={{0,4},{1,5},{2,6},{3,7},{4,8},{5,9},{6,10},{7,11},{8,12},{9,13},{1... | collective-permute-start | bytes 344072 | tf_op jit(solution)/shard_map/ppermute | solution.py:291
  7.2 10.8 %collective-permute-start.3 = (bf16[16,3584]{1,0:T(8,128)(2,1)S(1)}, bf16[16,3584]{1,0:T(8,128)(2,1)S(1)}, u32[]{:S(2)}, u32[]{:S(2)}) collective-permute-start(bf16[16,3584]{1,0:T(8,128)(2,1)S(1)} %get-tuple-element.47), channel_id=1, source_target_pairs={{0,12},{1,13},{2,14},{3,15},{4,0},{5,1},{6,2},{7,3},{8,4},{9,5},{1... | collective-permute-start | bytes 344072 | tf_op jit(solution)/shard_map/ppermute | solution.py:291
  9.4 9.1 %collective-permute-start = (bf16[16,6144]{1,0:T(8,128)(2,1)S(1)}, bf16[16,6144]{1,0:T(8,128)(2,1)S(1)}, u32[]{:S(2)}, u32[]{:S(2)}) collective-permute-start(bf16[16,6144]{1,0:T(8,128)(2,1)S(1)} %get-tuple-element.38.after_ref.refs_0_), channel_id=1, source_target_pairs={{0,2},{1,3},{2,0},{3,1},{4,6},{5,7},{6,4},{7,5},{8,10},{9,11},{10,... | collective-permute-start | bytes 589832 | tf_op jit(solution)/shard_map/ppermute | solution.py:296
  18.0 9.2 %collective-permute-start.8 = (bf16[48,3584]{1,0:T(8,128)(2,1)S(1)}, bf16[48,3584]{1,0:T(8,128)(2,1)S(1)}, u32[]{:S(2)}, u32[]{:S(2)}) collective-permute-start(bf16[48,3584]{1,0:T(8,128)(2,1)S(1)} %get-tuple-element.51.refs_3_.refs_1_), channel_id=1, source_target_pairs={{0,2},{1,3},{2,0},{3,1},{4,6},{5,7},{6,4},{7,5},{8,10},{9,11},{10,... | collective-permute-start | bytes 1032200 | tf_op jit(solution)/shard_map/ppermute | solution.py:296
  18.6 7.6 %collective-permute-start.4 = (bf16[16,2560]{1,0:T(8,128)(2,1)S(1)}, bf16[16,2560]{1,0:T(8,128)(2,1)S(1)}, u32[]{:S(2)}, u32[]{:S(2)}) collective-permute-start(bf16[16,2560]{1,0:T(8,128)(2,1)S(1)} %get-tuple-element.48), channel_id=1, source_target_pairs={{0,8},{1,9},{2,10},{3,11},{4,12},{5,13},{6,14},{7,15},{8,0},{9,1},... | collective-permute-start | bytes 245768 | tf_op jit(solution)/shard_map/ppermute | solution.py:291
  20.5 6.6 %collective-permute-start.5 = (bf16[16,2560]{1,0:T(8,128)(2,1)S(1)}, bf16[16,2560]{1,0:T(8,128)(2,1)S(1)}, u32[]{:S(2)}, u32[]{:S(2)}) collective-permute-start(bf16[16,2560]{1,0:T(8,128)(2,1)S(1)} %get-tuple-element.49), channel_id=1, source_target_pairs={{0,4},{1,5},{2,6},{3,7},{4,8},{5,9},{6,10},{7,11},{8,12},{9,13},{1... | collective-permute-start | bytes 245768 | tf_op jit(solution)/shard_map/ppermute | solution.py:291
  20.5 6.8 %collective-permute-start.6 = (bf16[16,2560]{1,0:T(8,128)(2,1)S(1)}, bf16[16,2560]{1,0:T(8,128)(2,1)S(1)}, u32[]{:S(2)}, u32[]{:S(2)}) collective-permute-start(bf16[16,2560]{1,0:T(8,128)(2,1)S(1)} %get-tuple-element.50), channel_id=1, source_target_pairs={{0,12},{1,13},{2,14},{3,15},{4,0},{5,1},{6,2},{7,3},{8,4},{9,5},{1... | collective-permute-start | bytes 245768 | tf_op jit(solution)/shard_map/ppermute | solution.py:291
  27.2 2.5 %collective-permute-start.9 = (bf16[128,3584]{1,0:T(8,128)(2,1)S(1)}, bf16[128,3584]{1,0:T(8,128)(2,1)S(1)}, u32[]{:S(2)}, u32[]{:S(2)}) collective-permute-start(bf16[128,3584]{1,0:T(8,128)(2,1)S(1)} %constant_dynamic-update-slice_fusion.6), channel_id=1, source_target_pairs={{0,1},{1,0},{2,3},{3,2},{4,5},{5,4},{6,7},{7,6},{8,9},{9,8},{10,11... | collective-permute-start | bytes 2752520 | tf_op jit(solution)/shard_map/ppermute | solution.py:296
  27.3 8.4 %collective-permute-start.7 = (bf16[48,2560]{1,0:T(8,128)(2,1)S(1)}, bf16[48,2560]{1,0:T(8,128)(2,1)S(1)}, u32[]{:S(2)}, u32[]{:S(2)}) collective-permute-start(bf16[48,2560]{1,0:T(8,128)(2,1)S(1)} %get-tuple-element.92.refs_1_), channel_id=1, source_target_pairs={{0,2},{1,3},{2,0},{3,1},{4,6},{5,7},{6,4},{7,5},{8,10},{9,11},{10,... | collective-permute-start | bytes 737288 | tf_op jit(solution)/shard_map/ppermute | solution.py:296
  35.7 2.2 %collective-permute-start.10 = (bf16[128,2560]{1,0:T(8,128)(2,1)S(1)}, bf16[128,2560]{1,0:T(8,128)(2,1)S(1)}, u32[]{:S(2)}, u32[]{:S(2)}) collective-permute-start(bf16[128,2560]{1,0:T(8,128)(2,1)S(1)} %constant_dynamic-update-slice_fusion.10), channel_id=1, source_target_pairs={{0,1},{1,0},{2,3},{3,2},{4,5},{5,4},{6,7},{7,6},{8,9},{9,8},{10,11... | collective-permute-start | bytes 1966088 | tf_op jit(solution)/shard_map/ppermute | solution.py:296
  45.1 3.3 %collective-permute-start.11 = (bf16[128,3072]{1,0:T(8,128)(2,1)S(1)}, bf16[128,3072]{1,0:T(8,128)(2,1)S(1)}, u32[]{:S(2)}, u32[]{:S(2)}) collective-permute-start(bf16[128,3072]{1,0:T(8,128)(2,1)S(1)} %get-tuple-element.62), channel_id=1, source_target_pairs={{0,1},{1,0},{2,3},{3,2},{4,5},{5,4},{6,7},{7,6},{8,9},{9,8},{10,11... | collective-permute-start | bytes 2359304 | tf_op jit(solution)/shard_map/ppermute | solution.py:296
  47.9 26.4 %copy-start = (bf16[24,6144]{1,0:T(8,128)(2,1)S(1)}, bf16[24,6144]{1,0:T(8,128)(2,1)}, u32[]{:S(2)}) copy-start(bf16[24,6144]{1,0:T(8,128)(2,1)} %act_ref.3) | copy-start | bytes 884740
  48.0 26.4 %copy-start.1 = (s32[24,2]{0,1:T(2,128)S(1)}, s32[24,2]{0,1:T(2,128)}, u32[]{:S(2)}) copy-start(s32[24,2]{0,1:T(2,128)} %param.8) | copy-start | bytes 580
  48.0 26.3 %copy-start.2 = (f32[24,2]{0,1:T(2,128)S(1)}, f32[24,2]{0,1:T(2,128)}, u32[]{:S(2)}) copy-start(f32[24,2]{0,1:T(2,128)} %param.9) | copy-start | bytes 580
  48.0 2.4 %collective-permute-start.12 = (bf16[128,3072]{1,0:T(8,128)(2,1)S(1)}, bf16[128,3072]{1,0:T(8,128)(2,1)S(1)}, u32[]{:S(2)}, u32[]{:S(2)}) collective-permute-start(bf16[128,3072]{1,0:T(8,128)(2,1)S(1)} %get-tuple-element.65), channel_id=1, source_target_pairs={{0,1},{1,0},{2,3},{3,2},{4,5},{5,4},{6,7},{7,6},{8,9},{9,8},{10,11... | collective-permute-start | bytes 2359304 | tf_op jit(solution)/shard_map/ppermute | solution.py:296
  48.7 4.9 %collective-permute-start.13 = (bf16[16,3072]{1,0:T(8,128)(2,1)S(1)}, bf16[16,3072]{1,0:T(8,128)(2,1)S(1)}, u32[]{:S(2)}, u32[]{:S(2)}) collective-permute-start(bf16[16,3072]{1,0:T(8,128)(2,1)S(1)} %get-tuple-element.82), channel_id=1, source_target_pairs={{0,2},{1,3},{2,0},{3,1},{4,6},{5,7},{6,4},{7,5},{8,10},{9,11},{10,... | collective-permute-start | bytes 294920 | tf_op jit(solution)/shard_map/ppermute | solution.py:296
  50.6 5.1 %collective-permute-start.15 = (bf16[16,3072]{1,0:T(8,128)(2,1)S(1)}, bf16[16,3072]{1,0:T(8,128)(2,1)S(1)}, u32[]{:S(2)}, u32[]{:S(2)}) collective-permute-start(bf16[16,3072]{1,0:T(8,128)(2,1)S(1)} %get-tuple-element.74), channel_id=1, source_target_pairs={{0,2},{1,3},{2,0},{3,1},{4,6},{5,7},{6,4},{7,5},{8,10},{9,11},{10,... | collective-permute-start | bytes 294920 | tf_op jit(solution)/shard_map/ppermute | solution.py:296
  53.6 10.0 %collective-permute-start.20 = (bf16[16,3072]{1,0:T(8,128)(2,1)S(1)}, bf16[16,3072]{1,0:T(8,128)(2,1)S(1)}, u32[]{:S(2)}, u32[]{:S(2)}) collective-permute-start(bf16[16,3072]{1,0:T(8,128)(2,1)S(1)} %add_convert_fusion.4), channel_id=1, source_target_pairs={{0,8},{1,9},{2,10},{3,11},{4,12},{5,13},{6,14},{7,15},{8,0},{9,1},... | collective-permute-start | bytes 294920 | tf_op jit(solution)/shard_map/ppermute | solution.py:291
  55.7 7.8 %collective-permute-start.16 = (bf16[16,6144]{1,0:T(8,128)(2,1)S(1)}, bf16[16,6144]{1,0:T(8,128)(2,1)S(1)}, u32[]{:S(2)}, u32[]{:S(2)}) collective-permute-start(bf16[16,6144]{1,0:T(8,128)(2,1)S(1)} %get-tuple-element.67), channel_id=1, source_target_pairs={{0,2},{1,3},{2,0},{3,1},{4,6},{5,7},{6,4},{7,5},{8,10},{9,11},{10,... | collective-permute-start | bytes 589832 | tf_op jit(solution)/shard_map/ppermute | solution.py:296
  56.9 9.4 %collective-permute-start.18 = (bf16[16,3072]{1,0:T(8,128)(2,1)S(1)}, bf16[16,3072]{1,0:T(8,128)(2,1)S(1)}, u32[]{:S(2)}, u32[]{:S(2)}) collective-permute-start(bf16[16,3072]{1,0:T(8,128)(2,1)S(1)} %add_convert_fusion.5), channel_id=1, source_target_pairs={{0,8},{1,9},{2,10},{3,11},{4,12},{5,13},{6,14},{7,15},{8,0},{9,1},... | collective-permute-start | bytes 294920 | tf_op jit(solution)/shard_map/ppermute | solution.py:291
  59.0 7.3 %collective-permute-start.14 = (bf16[16,6144]{1,0:T(8,128)(2,1)S(1)}, bf16[16,6144]{1,0:T(8,128)(2,1)S(1)}, u32[]{:S(2)}, u32[]{:S(2)}) collective-permute-start(bf16[16,6144]{1,0:T(8,128)(2,1)S(1)} %get-tuple-element.66), channel_id=1, source_target_pairs={{0,2},{1,3},{2,0},{3,1},{4,6},{5,7},{6,4},{7,5},{8,10},{9,11},{10,... | collective-permute-start | bytes 589832 | tf_op jit(solution)/shard_map/ppermute | solution.py:296
  63.6 8.6 %collective-permute-start.21 = (bf16[16,6144]{1,0:T(8,128)(2,1)S(1)}, bf16[16,6144]{1,0:T(8,128)(2,1)S(1)}, u32[]{:S(2)}, u32[]{:S(2)}) collective-permute-start(bf16[16,6144]{1,0:T(8,128)(2,1)S(1)} %add_convert_fusion.2), channel_id=1, source_target_pairs={{0,4},{1,5},{2,6},{3,7},{4,8},{5,9},{6,10},{7,11},{8,12},{9,13},{1... | collective-permute-start | bytes 589832 | tf_op jit(solution)/shard_map/ppermute | solution.py:291
  66.4 5.9 %collective-permute-start.17 = (bf16[16,6144]{1,0:T(8,128)(2,1)S(1)}, bf16[16,6144]{1,0:T(8,128)(2,1)S(1)}, u32[]{:S(2)}, u32[]{:S(2)}) collective-permute-start(bf16[16,6144]{1,0:T(8,128)(2,1)S(1)} %pad_maximum_fusion), channel_id=1, source_target_pairs={{0,2},{1,3},{2,0},{3,1},{4,6},{5,7},{6,4},{7,5},{8,10},{9,11},{10,... | collective-permute-start | bytes 589832 | tf_op jit(solution)/shard_map/ppermute | solution.py:296
  67.3 7.0 %collective-permute-start.19 = (bf16[16,6144]{1,0:T(8,128)(2,1)S(1)}, bf16[16,6144]{1,0:T(8,128)(2,1)S(1)}, u32[]{:S(2)}, u32[]{:S(2)}) collective-permute-start(bf16[16,6144]{1,0:T(8,128)(2,1)S(1)} %add_convert_fusion.3), channel_id=1, source_target_pairs={{0,12},{1,13},{2,14},{3,15},{4,0},{5,1},{6,2},{7,3},{8,4},{9,5},{1... | collective-permute-start | bytes 589832 | tf_op jit(solution)/shard_map/ppermute | solution.py:291

commit v12 on v11

--- a/solution.py
+++ b/solution.py
@@ -10,10 +10,10 @@
 EXPERTS = 4
 CAP = 16
 HALVES = 2
-ORDER = (2, 1, 3)
+ORDER = (2, 3, 1)
 FORTH = (7, 5)
+BACK = (1, 1)
 BLOCK = 512
-WIDE_BLOCK = 1024
 FETCH_ROWS = 144
 MIB = 1 << 20
 LIMIT = pltpu.CompilerParams(vmem_limit_bytes=10 * MIB)
@@ -22,9 +22,9 @@
 ANY = pl.BlockSpec(memory_space=pl.ANY)
 
 
-def spans(width):
-    unit = width // sum(FORTH)
-    return [(sum(FORTH[:k]) * unit, n * unit) for k, n in enumerate(FORTH)]
+def spans(width, shares=FORTH):
+    unit = width // sum(shares)
+    return [(sum(shares[:k]) * unit, n * unit) for k, n in enumerate(shares)]
 
 
 def choices(ids, plane):
@@ -201,13 +201,14 @@
     later, held, refs = refs[:ahead], refs[ahead : 2 * ahead], refs[2 * ahead :]
     keep_ref, send_ref, sems = refs
     half, part = keep_ref.shape
+    block = part // 2
     copies = fetches(later, part, held, sems)
     for copy in copies:
         copy.start()
 
-    @pl.loop(0, part // WIDE_BLOCK)
+    @pl.loop(0, 2)
     def _(c):
-        columns = pl.ds(pl.multiple_of(c * WIDE_BLOCK, WIDE_BLOCK), WIDE_BLOCK)
+        columns = pl.ds(pl.multiple_of(c * block, block), block)
         out = jnp.dot(hidden_ref[...], w_ref[:, columns], preferred_element_type=jnp.float32)
         out = out.astype(jnp.bfloat16)
         keep_ref[:, columns] = out[:half]
@@ -221,7 +222,7 @@
     rows, depth = hidden.shape
     part = w_down.shape[1]
     ahead = len(later)
-    out_shape = [pltpu.VMEM((depth, part), jnp.bfloat16)] * ahead
+    out_shape = [pltpu.VMEM((depth, w.shape[1] - part), jnp.bfloat16) for w in later]
     out_shape += [jax.ShapeDtypeStruct((rows // 2, part), jnp.bfloat16)] * 2
     w_down = pltpu.with_memory_space_constraint(w_down, pltpu.VMEM)
     later = [pltpu.with_memory_space_constraint(w, pltpu.HBM) for w in later]
@@ -253,9 +254,8 @@
     high = weight.astype(jnp.bfloat16).astype(jnp.float32)
     middle = (weight - high).astype(jnp.bfloat16).astype(jnp.float32)
     terms = jnp.concatenate([weight - high - middle, middle, high], axis=0).astype(jnp.bfloat16)
-    part = kept[0].shape[1]
-    for k in range(HALVES):
-        columns = slice(k * part, (k + 1) * part)
+    for k, (at, part) in enumerate(spans(act_ref.shape[1], BACK)):
+        columns = slice(at, at + part)
         own = kept[k][...].astype(jnp.float32) + arrived[:, columns].astype(jnp.float32)
         blocks = [own.astype(jnp.bfloat16), near[:, columns], middle_rows[k][...]]
         rows = jnp.concatenate(blocks + [last[:, columns]], axis=0)
@@ -302,12 +302,13 @@
     ids = expert_ids.T
     own, *sends = pack(group, ids, activations, norm_gain)
     far_own = swap(own, far)
-    now = [fetch(w, 0, spans(width)[0][1], own) for w in (w_gate, w_up)]
+    now = [fetch(w_gate, 0, spans(width)[0][1], own)]
     blocks = []
     for k in range(HALVES):
         x = sends[k * others : (k + 1) * others]
         if k:
             x = relay(after(x, *now, far_own), blocks[-1])
+            now.append(fetch(w_up, 0, spans(width)[0][1], x[0]))
         arrivals = [shift(x[s - 1], s) for s in ORDER]
         blocks.append(jnp.concatenate(arrivals, axis=0))
     totals = []
@@ -327,7 +328,7 @@
             pieces[1] = after(pieces[1], blocks[k + 1])
         later, ahead = [w_gate, w_up], (size, width - size)
         if k == HALVES - 1:
-            later, ahead = [w_down], (0, part)
+            later, ahead = [w_down], spans(width, BACK)[0]
         now, totals = gate_up(k, pieces, now, later, ahead, totals)
     hidden = totals[0]
     held = []
@@ -345,8 +346,8 @@
     middle = [shift(added(h[place[2]], x), -2) for h, x in zip(held, crossed)]
     mine = [jnp.concatenate([h[j] for h in held], axis=1) for j in range(2 * EXPERTS)]
     back = {}
-    back[1] = swap(after(mine[EXPERTS + place[1]], crossed[0]), far)
-    back[3] = swap(after(mine[EXPERTS + place[3]], *crossed), far)
+    back[1] = swap(after(mine[EXPERTS + place[1]], crossed[1]), far)
+    back[3] = swap(after(mine[EXPERTS + place[3]], crossed[0]), far)
     back[0] = swap(after(mine[EXPERTS], back[1], back[3]), far)
     near = shift(after(added(mine[place[1]], back[1]), middle[1]), -1)
     last = shift(after(added(mine[place[3]], back[3]), middle[0]), -3)

time: 75.8 us -> 78.4 us (1.034)
  waiting for transfers between devices: 21.3 us -> 23.6 us
    ppermute x10, waiting for transfers between devices: 8.21 us -> 11.6 us  [shift(): lax.ppermute(x, 'expert', [(i, (i + s * group) % devices) for i in range(...]
    ppermute x12, waiting for transfers between devices: 13.1 us -> 12 us  [swap(): return lax.ppermute(x, 'expert', [(i, i ^ bit) for i in range(devices)])]
    ppermute x10, starting transfers between devices: 19.7 us -> 20.5 us  [shift(): lax.ppermute(x, 'expert', [(i, (i + s * group) % devices) for i in range(...]
  transfers between devices with their start and end apart: 22 -> 22, of which waited for: 12 -> 13; matrix products, arithmetic and copies ran while one was open for 1% -> 1% of each run, Pallas kernels for 20% -> 19%
where the time goes in v12:
time: 78.4 us; the launch traced here: 78.3 us
  starting transfers between devices  28.8 us (37%)
  Pallas kernels  24.8 us (32%)
  waiting for transfers between devices  23.6 us (30%)
    ppermute x10, starting transfers between devices, shift(): lax.ppermute(x, 'expert', [(i, (i + s * group) % devices) for i in range(...  20.5 us
    ppermute x12, waiting for transfers between devices, swap(): return lax.ppermute(x, 'expert', [(i, i ^ bit) for i in range(devices)])  12 us
    ppermute x10, waiting for transfers between devices, shift(): lax.ppermute(x, 'expert', [(i, (i + s * group) % devices) for i in range(...  11.6 us
    pallas_call x2, Pallas kernels, gate_up(): pl.pallas_call(functools.partial(gate_up_kernel, len(pieces), len(later),...  9.57 us
    ppermute x12, starting transfers between devices, swap(): return lax.ppermute(x, 'expert', [(i, i ^ bit) for i in range(devices)])  8.23 us
    pallas_call x2, Pallas kernels, fetch(): pl.pallas_call(functools.partial(fetch_kernel, at), in_specs=[ANY, ANY],...  6.88 us
    pallas_call x2, Pallas kernels, down(): pl.pallas_call(functools.partial(down_kernel, ahead), in_specs=[VMEM, VME...  5.58 us
  transfers between devices with their start and end apart: 22, of which 13 were waited for; matrix products, arithmetic and copies ran while one was open for 1% of the time, Pallas kernels for 19%

profile of v12, /device:TPU:0, one launch (start us, length us, event | category | flops | bytes accessed | tf_op | source)
XLA Modules:
  0.0 78.3 jit_solution(2520823524684019035)
XLA Ops:
  0.0 1.5 %norm_and_pack.1 = (bf16[16,6144]{1,0:T(8,128)(2,1)S(1)}, bf16[16,3584]{1,0:T(8,128)(2,1)S(1)}, bf16[16,3584]{1,0:T(8,128)(2,1)S(1)}, bf16[16,3584]{1,0:T(8,128)...) custom-call(s32[2,24]{1,0:T(2,128)} %bitcast.3, ...), custom_call_target="tpu_custom_call" | custom-call | tf_op jit(solution)/shard_map/norm_and_pack/pallas_call | solution.py:66
  1.5 4.1 %collective-permute-start.1 = (bf16[16,3584]{1,0:T(8,128)(2,1)S(1)}, bf16[16,3584]{1,0:T(8,128)(2,1)S(1)}, u32[]{:S(2)}, u32[]{:S(2)}) collective-permute-start(bf16[16,3584]{1,0:T(8,128)(2,1)S(1)} %get-tuple-element.45), channel_id=1, source_target_pairs={{0,8},{1,9},{2,10},{3,11},{4,12},{5,13},{6,14},{7,15},{8,0},{9,1},... | collective-permute-start | bytes 344072 | tf_op jit(solution)/shard_map/ppermute | solution.py:291
  5.6 1.3 %collective-permute-start.2 = (bf16[16,3584]{1,0:T(8,128)(2,1)S(1)}, bf16[16,3584]{1,0:T(8,128)(2,1)S(1)}, u32[]{:S(2)}, u32[]{:S(2)}) collective-permute-start(bf16[16,3584]{1,0:T(8,128)(2,1)S(1)} %get-tuple-element.46), channel_id=1, source_target_pairs={{0,12},{1,13},{2,14},{3,15},{4,0},{5,1},{6,2},{7,3},{8,4},{9,5},{1... | collective-permute-start | bytes 344072 | tf_op jit(solution)/shard_map/ppermute | solution.py:291
  6.9 0.7 collective-permute-start.3
  7.6 1.5 %collective-permute-start = (bf16[16,6144]{1,0:T(8,128)(2,1)S(1)}, bf16[16,6144]{1,0:T(8,128)(2,1)S(1)}, u32[]{:S(2)}, u32[]{:S(2)}) collective-permute-start(bf16[16,6144]{1,0:T(8,128)(2,1)S(1)} %get-tuple-element.38.after_ref.refs_0_), channel_id=1, source_target_pairs={{0,2},{1,3},{2,0},{3,1},{4,6},{5,7},{6,4},{7,5},{8,10},{9,11},{10,... | collective-permute-start | bytes 589832 | tf_op jit(solution)/shard_map/ppermute | solution.py:296
  9.2 3.4 %fetch.2.refs_5_ = bf16[1152,3584]{1,0:T(8,128)(2,1)S(1)} custom-call(bf16[1152,6144]{1,0:T(8,128)(2,1)} %refs_7_.2, bf16[16,6144]{1,0:T(8,128)(2,1)S(1)} %get-tuple-element.38.after_ref.refs_0_), custom_call_target="tpu_custom_call" | custom-call | bytes 16515072 | tf_op jit(solution)/shard_map/fetch/pallas_call | solution.py:99
  12.6 0.2 collective-permute-done.1
  12.9 0.0 collective-permute-done.2
  12.9 1.9 %collective-permute-done.3 = bf16[16,3584]{1,0:T(8,128)(2,1)S(1)} collective-permute-done((bf16[16,3584]{1,0:T(8,128)(2,1)S(1)}, bf16[16,3584]{1,0:T(8,128)(2,1)S(1)}, u32[]{:S(2)}, u32[]{:S(2)}) %collective-permute-start.3) | collective-permute-done | bytes 114720 | tf_op jit(solution)/shard_map/ppermute | solution.py:291
  14.8 1.7 %collective-permute-start.8 = (bf16[48,3584]{1,0:T(8,128)(2,1)S(1)}, bf16[48,3584]{1,0:T(8,128)(2,1)S(1)}, u32[]{:S(2)}, u32[]{:S(2)}) collective-permute-start(bf16[48,3584]{1,0:T(8,128)(2,1)S(1)} %get-tuple-element.51.refs_3_.refs_1_), channel_id=1, source_target_pairs={{0,2},{1,3},{2,0},{3,1},{4,6},{5,7},{6,4},{7,5},{8,10},{9,11},{10,... | collective-permute-start | bytes 1032200 | tf_op jit(solution)/shard_map/ppermute | solution.py:296
  16.5 0.0 collective-permute-done.refs_2_
  16.5 4.0 %collective-permute-start.4 = (bf16[16,2560]{1,0:T(8,128)(2,1)S(1)}, bf16[16,2560]{1,0:T(8,128)(2,1)S(1)}, u32[]{:S(2)}, u32[]{:S(2)}) collective-permute-start(bf16[16,2560]{1,0:T(8,128)(2,1)S(1)} %get-tuple-element.48), channel_id=1, source_target_pairs={{0,8},{1,9},{2,10},{3,11},{4,12},{5,13},{6,14},{7,15},{8,0},{9,1},... | collective-permute-start | bytes 245768 | tf_op jit(solution)/shard_map/ppermute | solution.py:291
  20.5 0.0 collective-permute-start.6
  20.5 3.4 %fetch.3.refs_6_ = bf16[1152,3584]{1,0:T(8,128)(2,1)S(1)} custom-call(bf16[1152,6144]{1,0:T(8,128)(2,1)} %refs_8_.1, bf16[16,2560]{1,0:T(8,128)(2,1)S(1)} %get-tuple-element.50.after_ref), custom_call_target="tpu_custom_call" | custom-call | bytes 16515072 | tf_op jit(solution)/shard_map/fetch/pallas_call | solution.py:99
  24.0 3.9 %collective-permute-start.5 = (bf16[16,2560]{1,0:T(8,128)(2,1)S(1)}, bf16[16,2560]{1,0:T(8,128)(2,1)S(1)}, u32[]{:S(2)}, u32[]{:S(2)}) collective-permute-start(bf16[16,2560]{1,0:T(8,128)(2,1)S(1)} %get-tuple-element.49), channel_id=1, source_target_pairs={{0,12},{1,13},{2,14},{3,15},{4,0},{5,1},{6,2},{7,3},{8,4},{9,5},{1... | collective-permute-start | bytes 245768 | tf_op jit(solution)/shard_map/ppermute | solution.py:291
  27.8 0.0 collective-permute-done.4
  27.9 2.0 %collective-permute-done.5 = bf16[16,2560]{1,0:T(8,128)(2,1)S(1)} collective-permute-done((bf16[16,2560]{1,0:T(8,128)(2,1)S(1)}, bf16[16,2560]{1,0:T(8,128)(2,1)S(1)}, u32[]{:S(2)}, u32[]{:S(2)}) %collective-permute-start.5) | collective-permute-done | bytes 81952 | tf_op jit(solution)/shard_map/ppermute | solution.py:291
  29.9 0.0 collective-permute-done.8.refs_3_
  30.0 0.1 collective-permute-start.9
  30.0 0.0 collective-permute-done.6
  30.1 0.6 collective-permute-start.7
  30.6 1.9 %collective-permute-done.9.refs_4_ = bf16[128,3584]{1,0:T(8,128)(2,1)S(1)} collective-permute-done((bf16[128,3584]{1,0:T(8,128)(2,1)S(1)}, bf16[128,3584]{1,0:T(8,128)(2,1)S(1)}, u32[]{:S(2)}, u32[]{:S(2)}) %collective-permute-start.9) | collective-permute-done | bytes 917536 | tf_op jit(solution)/shard_map/ppermute | solution.py:296
  32.5 5.5 %gate_up.2 = (bf16[1152,2560]{1,0:T(8,128)(2,1)S(1)}, bf16[1152,2560]{1,0:T(8,128)(2,1)S(1)}, f32[1152,256]{1,0:T(8,128)S(1)}, f32[1152,256]{1,0:T(8,128)S(1)}) custom-call(bf16[16,6144]{1,0:T(8,128)(2,1)S(1)} %get-tuple-element.38.after_ref.refs_0_, bf16[48,3584]{1,0:T(8,128)(2,1)S(1)} %get-tuple-element.51.refs_3_.refs_1_, ...), custom_call_target="tpu_custom_call" | custom-call | flops 4227858432 | bytes 18874368 | tf_op jit(solution)/shard_map/gate_up/pallas_call | solution.py:181
  38.0 0.5 collective-permute-done.7.refs_3_
  38.5 0.1 collective-permute-start.10
  38.6 2.1 %collective-permute-done.10.refs_4_ = bf16[128,2560]{1,0:T(8,128)(2,1)S(1)} collective-permute-done((bf16[128,2560]{1,0:T(8,128)(2,1)S(1)}, bf16[128,2560]{1,0:T(8,128)(2,1)S(1)}, u32[]{:S(2)}, u32[]{:S(2)}) %collective-permute-start.10) | collective-permute-done | bytes 655392 | tf_op jit(solution)/shard_map/ppermute | solution.py:296
  40.7 4.1 %gate_up.3 = (bf16[1152,3072]{1,0:T(8,128)(2,1)S(1)}, bf16[256,1152]{1,0:T(8,128)(2,1)S(1)}) custom-call(bf16[16,6144]{1,0:T(8,128)(2,1)S(1)} %get-tuple-element.38.after_ref.refs_0_, bf16[48,2560]{1,0:T(8,128)(2,1)S(1)} %get-tuple-element.92.refs_1_, bf16[16,6144]{1,0:T(8,128)(2,1)S(1)} %collective-permute-done.refs_2_, ...), custom_call_target="tpu_custom_call" | custom-call | flops 3019898880 | bytes 14155776 | tf_op jit(solution)/shard_map/gate_up/pallas_call | solution.py:181
  44.7 3.1 %down.2 = (bf16[1152,3072]{1,0:T(8,128)(2,1)S(1)}, bf16[128,3072]{1,0:T(8,128)(2,1)S(1)}, bf16[128,3072]{1,0:T(8,128)(2,1)S(1)}) custom-call(bf16[256,1152]{1,0:T(8,128)(2,1)S(1)} %get-tuple-element.59.hidden_ref, bf16[1152,3072]{1,0:T(8,128)(2,1)S(1)} %get-tuple-element.60.w_ref, bf16[1152,6144]{1,0:T(8,128)(2,1)} %refs_0_.1), custom_call_target="tpu_custom_call" | custom-call | flops 1811939328 | bytes 9240576 | tf_op jit(solution)/shard_map/down/pallas_call | solution.py:229
  47.9 0.2 collective-permute-start.11
  48.1 2.5 %down.3 = (bf16[128,3072]{1,0:T(8,128)(2,1)S(1)}, bf16[128,3072]{1,0:T(8,128)(2,1)S(1)}) custom-call(bf16[256,1152]{1,0:T(8,128)(2,1)S(1)} %get-tuple-element.59.hidden_ref, bf16[1152,3072]{1,0:T(8,128)(2,1)S(1)} %get-tuple-element.63.w_ref), custom_call_target="tpu_custom_call" | custom-call | flops 1811939328 | bytes 9240576 | tf_op jit(solution)/shard_map/down/pallas_call | solution.py:229
  50.6 0.0 copy-start
  50.6 0.0 copy-start.1
  50.6 0.0 copy-start.2
  50.6 0.4 collective-permute-start.12
  51.0 0.0 collective-permute-done.11
  51.0 0.2 add_convert_fusion.1
  51.3 0.6 collective-permute-start.15
  51.9 1.1 %collective-permute-done.12 = bf16[128,3072]{1,0:T(8,128)(2,1)S(1)} collective-permute-done((bf16[128,3072]{1,0:T(8,128)(2,1)S(1)}, bf16[128,3072]{1,0:T(8,128)(2,1)S(1)}, u32[]{:S(2)}, u32[]{:S(2)}) %collective-permute-start.12) | collective-permute-done | bytes 786464 | tf_op jit(solution)/shard_map/ppermute | solution.py:296
  52.9 0.2 add_convert_fusion
  53.2 0.6 collective-permute-start.13
  53.8 2.4 %collective-permute-done.15 = bf16[16,3072]{1,0:T(8,128)(2,1)S(1)} collective-permute-done((bf16[16,3072]{1,0:T(8,128)(2,1)S(1)}, bf16[16,3072]{1,0:T(8,128)(2,1)S(1)}, u32[]{:S(2)}, u32[]{:S(2)}) %collective-permute-start.15) | collective-permute-done | bytes 98336 | tf_op jit(solution)/shard_map/ppermute | solution.py:296
  56.2 1.0 %collective-permute-start.20 = (bf16[16,3072]{1,0:T(8,128)(2,1)S(1)}, bf16[16,3072]{1,0:T(8,128)(2,1)S(1)}, u32[]{:S(2)}, u32[]{:S(2)}) collective-permute-start(bf16[16,3072]{1,0:T(8,128)(2,1)S(1)} %add_convert_fusion.4), channel_id=1, source_target_pairs={{0,8},{1,9},{2,10},{3,11},{4,12},{5,13},{6,14},{7,15},{8,0},{9,1},... | collective-permute-start | bytes 294920 | tf_op jit(solution)/shard_map/ppermute | solution.py:291
  57.2 0.5 collective-permute-start.16
  57.7 0.6 collective-permute-done.13
  58.4 1.4 %collective-permute-start.18 = (bf16[16,3072]{1,0:T(8,128)(2,1)S(1)}, bf16[16,3072]{1,0:T(8,128)(2,1)S(1)}, u32[]{:S(2)}, u32[]{:S(2)}) collective-permute-start(bf16[16,3072]{1,0:T(8,128)(2,1)S(1)} %add_convert_fusion.5), channel_id=1, source_target_pairs={{0,8},{1,9},{2,10},{3,11},{4,12},{5,13},{6,14},{7,15},{8,0},{9,1},... | collective-permute-start | bytes 294920 | tf_op jit(solution)/shard_map/ppermute | solution.py:291
  59.8 1.5 %collective-permute-start.14 = (bf16[16,6144]{1,0:T(8,128)(2,1)S(1)}, bf16[16,6144]{1,0:T(8,128)(2,1)S(1)}, u32[]{:S(2)}, u32[]{:S(2)}) collective-permute-start(bf16[16,6144]{1,0:T(8,128)(2,1)S(1)} %get-tuple-element.66), channel_id=1, source_target_pairs={{0,2},{1,3},{2,0},{3,1},{4,6},{5,7},{6,4},{7,5},{8,10},{9,11},{10,... | collective-permute-start | bytes 589832 | tf_op jit(solution)/shard_map/ppermute | solution.py:296
  61.3 3.5 %collective-permute-done.16 = bf16[16,6144]{1,0:T(8,128)(2,1)S(1)} collective-permute-done((bf16[16,6144]{1,0:T(8,128)(2,1)S(1)}, bf16[16,6144]{1,0:T(8,128)(2,1)S(1)}, u32[]{:S(2)}, u32[]{:S(2)}) %collective-permute-start.16) | collective-permute-done | bytes 196640 | tf_op jit(solution)/shard_map/ppermute | solution.py:296
  64.9 2.0 %collective-permute-done.20.refs_2_ = bf16[16,3072]{1,0:T(8,128)(2,1)S(1)} collective-permute-done((bf16[16,3072]{1,0:T(8,128)(2,1)S(1)}, bf16[16,3072]{1,0:T(8,128)(2,1)S(1)}, u32[]{:S(2)}, u32[]{:S(2)}) %collective-permute-start.20) | collective-permute-done | bytes 98336 | tf_op jit(solution)/shard_map/ppermute | solution.py:291
  66.9 1.9 %collective-permute-start.21 = (bf16[16,6144]{1,0:T(8,128)(2,1)S(1)}, bf16[16,6144]{1,0:T(8,128)(2,1)S(1)}, u32[]{:S(2)}, u32[]{:S(2)}) collective-permute-start(bf16[16,6144]{1,0:T(8,128)(2,1)S(1)} %add_convert_fusion.2), channel_id=1, source_target_pairs={{0,4},{1,5},{2,6},{3,7},{4,8},{5,9},{6,10},{7,11},{8,12},{9,13},{1... | collective-permute-start | bytes 589832 | tf_op jit(solution)/shard_map/ppermute | solution.py:291
  68.8 0.0 collective-permute-done.14
  68.8 0.0 collective-permute-done.18.refs_3_
  68.8 2.2 %collective-permute-start.19 = (bf16[16,6144]{1,0:T(8,128)(2,1)S(1)}, bf16[16,6144]{1,0:T(8,128)(2,1)S(1)}, u32[]{:S(2)}, u32[]{:S(2)}) collective-permute-start(bf16[16,6144]{1,0:T(8,128)(2,1)S(1)} %add_convert_fusion.3), channel_id=1, source_target_pairs={{0,12},{1,13},{2,14},{3,15},{4,0},{5,1},{6,2},{7,3},{8,4},{9,5},{1... | collective-permute-start | bytes 589832 | tf_op jit(solution)/shard_map/ppermute | solution.py:291
  71.0 0.5 collective-permute-start.17
  71.6 3.5 %collective-permute-done.21.last = bf16[16,6144]{1,0:T(8,128)(2,1)S(1)} collective-permute-done((bf16[16,6144]{1,0:T(8,128)(2,1)S(1)}, bf16[16,6144]{1,0:T(8,128)(2,1)S(1)}, u32[]{:S(2)}, u32[]{:S(2)}) %collective-permute-start.21) | collective-permute-done | bytes 196640 | tf_op jit(solution)/shard_map/ppermute | solution.py:291
  75.0 1.9 %collective-permute-done.19.near = bf16[16,6144]{1,0:T(8,128)(2,1)S(1)} collective-permute-done((bf16[16,6144]{1,0:T(8,128)(2,1)S(1)}, bf16[16,6144]{1,0:T(8,128)(2,1)S(1)}, u32[]{:S(2)}, u32[]{:S(2)}) %collective-permute-start.19) | collective-permute-done | bytes 196640 | tf_op jit(solution)/shard_map/ppermute | solution.py:291
  77.0 0.0 collective-permute-done.17.arrived
  77.0 0.0 copy-done
  77.0 0.0 copy-done.1
  77.0 0.0 copy-done.2
  77.0 1.3 %mix.1 = bf16[24,6144]{1,0:T(8,128)(2,1)} custom-call(s32[2,24]{1,0:T(2,128)S(1)} %bitcast.4, f32[2,24]{1,0:T(2,128)S(1)} %bitcast.5, bf16[24,6144]{1,0:T(8,128)(2,1)S(1)} %copy-done, bf16[16,6144]{1,0:T(8,128)(2,1)S(1)} %collective-permute-done.17.arrived, bf16[16,6144]{1,0:T(8,128)(2,1)S(1)} %collective-permute-done.19.near, ...), custom_call_target="tpu_custom_call" | custom-call | tf_op jit(solution)/shard_map/mix/pallas_call | solution.py:270
  (21 shorter events, 0.5 us)
Async XLA Ops:
  1.5 11.4 %collective-permute-start.1 = (bf16[16,3584]{1,0:T(8,128)(2,1)S(1)}, bf16[16,3584]{1,0:T(8,128)(2,1)S(1)}, u32[]{:S(2)}, u32[]{:S(2)}) collective-permute-start(bf16[16,3584]{1,0:T(8,128)(2,1)S(1)} %get-tuple-element.45), channel_id=1, source_target_pairs={{0,8},{1,9},{2,10},{3,11},{4,12},{5,13},{6,14},{7,15},{8,0},{9,1},... | collective-permute-start | bytes 344072 | tf_op jit(solution)/shard_map/ppermute | solution.py:291
  5.6 7.3 %collective-permute-start.2 = (bf16[16,3584]{1,0:T(8,128)(2,1)S(1)}, bf16[16,3584]{1,0:T(8,128)(2,1)S(1)}, u32[]{:S(2)}, u32[]{:S(2)}) collective-permute-start(bf16[16,3584]{1,0:T(8,128)(2,1)S(1)} %get-tuple-element.46), channel_id=1, source_target_pairs={{0,12},{1,13},{2,14},{3,15},{4,0},{5,1},{6,2},{7,3},{8,4},{9,5},{1... | collective-permute-start | bytes 344072 | tf_op jit(solution)/shard_map/ppermute | solution.py:291
  6.9 7.9 %collective-permute-start.3 = (bf16[16,3584]{1,0:T(8,128)(2,1)S(1)}, bf16[16,3584]{1,0:T(8,128)(2,1)S(1)}, u32[]{:S(2)}, u32[]{:S(2)}) collective-permute-start(bf16[16,3584]{1,0:T(8,128)(2,1)S(1)} %get-tuple-element.47), channel_id=1, source_target_pairs={{0,4},{1,5},{2,6},{3,7},{4,8},{5,9},{6,10},{7,11},{8,12},{9,13},{1... | collective-permute-start | bytes 344072 | tf_op jit(solution)/shard_map/ppermute | solution.py:291
  7.6 8.9 %collective-permute-start = (bf16[16,6144]{1,0:T(8,128)(2,1)S(1)}, bf16[16,6144]{1,0:T(8,128)(2,1)S(1)}, u32[]{:S(2)}, u32[]{:S(2)}) collective-permute-start(bf16[16,6144]{1,0:T(8,128)(2,1)S(1)} %get-tuple-element.38.after_ref.refs_0_), channel_id=1, source_target_pairs={{0,2},{1,3},{2,0},{3,1},{4,6},{5,7},{6,4},{7,5},{8,10},{9,11},{10,... | collective-permute-start | bytes 589832 | tf_op jit(solution)/shard_map/ppermute | solution.py:296
  14.8 15.1 %collective-permute-start.8 = (bf16[48,3584]{1,0:T(8,128)(2,1)S(1)}, bf16[48,3584]{1,0:T(8,128)(2,1)S(1)}, u32[]{:S(2)}, u32[]{:S(2)}) collective-permute-start(bf16[48,3584]{1,0:T(8,128)(2,1)S(1)} %get-tuple-element.51.refs_3_.refs_1_), channel_id=1, source_target_pairs={{0,2},{1,3},{2,0},{3,1},{4,6},{5,7},{6,4},{7,5},{8,10},{9,11},{10,... | collective-permute-start | bytes 1032200 | tf_op jit(solution)/shard_map/ppermute | solution.py:296
  16.5 11.3 %collective-permute-start.4 = (bf16[16,2560]{1,0:T(8,128)(2,1)S(1)}, bf16[16,2560]{1,0:T(8,128)(2,1)S(1)}, u32[]{:S(2)}, u32[]{:S(2)}) collective-permute-start(bf16[16,2560]{1,0:T(8,128)(2,1)S(1)} %get-tuple-element.48), channel_id=1, source_target_pairs={{0,8},{1,9},{2,10},{3,11},{4,12},{5,13},{6,14},{7,15},{8,0},{9,1},... | collective-permute-start | bytes 245768 | tf_op jit(solution)/shard_map/ppermute | solution.py:291
  20.5 9.5 %collective-permute-start.6 = (bf16[16,2560]{1,0:T(8,128)(2,1)S(1)}, bf16[16,2560]{1,0:T(8,128)(2,1)S(1)}, u32[]{:S(2)}, u32[]{:S(2)}) collective-permute-start(bf16[16,2560]{1,0:T(8,128)(2,1)S(1)} %get-tuple-element.50.after_ref), channel_id=1, source_target_pairs={{0,4},{1,5},{2,6},{3,7},{4,8},{5,9},{6,10},{7,11},{8,12},{9,13},{1... | collective-permute-start | bytes 245768 | tf_op jit(solution)/shard_map/ppermute | solution.py:291
  24.0 5.9 %collective-permute-start.5 = (bf16[16,2560]{1,0:T(8,128)(2,1)S(1)}, bf16[16,2560]{1,0:T(8,128)(2,1)S(1)}, u32[]{:S(2)}, u32[]{:S(2)}) collective-permute-start(bf16[16,2560]{1,0:T(8,128)(2,1)S(1)} %get-tuple-element.49), channel_id=1, source_target_pairs={{0,12},{1,13},{2,14},{3,15},{4,0},{5,1},{6,2},{7,3},{8,4},{9,5},{1... | collective-permute-start | bytes 245768 | tf_op jit(solution)/shard_map/ppermute | solution.py:291
  30.0 2.5 %collective-permute-start.9 = (bf16[128,3584]{1,0:T(8,128)(2,1)S(1)}, bf16[128,3584]{1,0:T(8,128)(2,1)S(1)}, u32[]{:S(2)}, u32[]{:S(2)}) collective-permute-start(bf16[128,3584]{1,0:T(8,128)(2,1)S(1)} %constant_dynamic-update-slice_fusion.6), channel_id=1, source_target_pairs={{0,1},{1,0},{2,3},{3,2},{4,5},{5,4},{6,7},{7,6},{8,9},{9,8},{10,11... | collective-permute-start | bytes 2752520 | tf_op jit(solution)/shard_map/ppermute | solution.py:296
  30.1 8.4 %collective-permute-start.7 = (bf16[48,2560]{1,0:T(8,128)(2,1)S(1)}, bf16[48,2560]{1,0:T(8,128)(2,1)S(1)}, u32[]{:S(2)}, u32[]{:S(2)}) collective-permute-start(bf16[48,2560]{1,0:T(8,128)(2,1)S(1)} %get-tuple-element.92.refs_1_), channel_id=1, source_target_pairs={{0,2},{1,3},{2,0},{3,1},{4,6},{5,7},{6,4},{7,5},{8,10},{9,11},{10,... | collective-permute-start | bytes 737288 | tf_op jit(solution)/shard_map/ppermute | solution.py:296
  38.5 2.2 %collective-permute-start.10 = (bf16[128,2560]{1,0:T(8,128)(2,1)S(1)}, bf16[128,2560]{1,0:T(8,128)(2,1)S(1)}, u32[]{:S(2)}, u32[]{:S(2)}) collective-permute-start(bf16[128,2560]{1,0:T(8,128)(2,1)S(1)} %constant_dynamic-update-slice_fusion.10), channel_id=1, source_target_pairs={{0,1},{1,0},{2,3},{3,2},{4,5},{5,4},{6,7},{7,6},{8,9},{9,8},{10,11... | collective-permute-start | bytes 1966088 | tf_op jit(solution)/shard_map/ppermute | solution.py:296
  47.9 3.2 %collective-permute-start.11 = (bf16[128,3072]{1,0:T(8,128)(2,1)S(1)}, bf16[128,3072]{1,0:T(8,128)(2,1)S(1)}, u32[]{:S(2)}, u32[]{:S(2)}) collective-permute-start(bf16[128,3072]{1,0:T(8,128)(2,1)S(1)} %get-tuple-element.62), channel_id=1, source_target_pairs={{0,1},{1,0},{2,3},{3,2},{4,5},{5,4},{6,7},{7,6},{8,9},{9,8},{10,11... | collective-permute-start | bytes 2359304 | tf_op jit(solution)/shard_map/ppermute | solution.py:296
  50.6 26.4 %copy-start = (bf16[24,6144]{1,0:T(8,128)(2,1)S(1)}, bf16[24,6144]{1,0:T(8,128)(2,1)}, u32[]{:S(2)}) copy-start(bf16[24,6144]{1,0:T(8,128)(2,1)} %act_ref.3) | copy-start | bytes 884740
  50.6 26.4 %copy-start.1 = (s32[24,2]{0,1:T(2,128)S(1)}, s32[24,2]{0,1:T(2,128)}, u32[]{:S(2)}) copy-start(s32[24,2]{0,1:T(2,128)} %param.8) | copy-start | bytes 580
  50.6 26.4 %copy-start.2 = (f32[24,2]{0,1:T(2,128)S(1)}, f32[24,2]{0,1:T(2,128)}, u32[]{:S(2)}) copy-start(f32[24,2]{0,1:T(2,128)} %param.9) | copy-start | bytes 580
  50.6 2.4 %collective-permute-start.12 = (bf16[128,3072]{1,0:T(8,128)(2,1)S(1)}, bf16[128,3072]{1,0:T(8,128)(2,1)S(1)}, u32[]{:S(2)}, u32[]{:S(2)}) collective-permute-start(bf16[128,3072]{1,0:T(8,128)(2,1)S(1)} %get-tuple-element.65), channel_id=1, source_target_pairs={{0,1},{1,0},{2,3},{3,2},{4,5},{5,4},{6,7},{7,6},{8,9},{9,8},{10,11... | collective-permute-start | bytes 2359304 | tf_op jit(solution)/shard_map/ppermute | solution.py:296
  51.3 4.9 %collective-permute-start.15 = (bf16[16,3072]{1,0:T(8,128)(2,1)S(1)}, bf16[16,3072]{1,0:T(8,128)(2,1)S(1)}, u32[]{:S(2)}, u32[]{:S(2)}) collective-permute-start(bf16[16,3072]{1,0:T(8,128)(2,1)S(1)} %get-tuple-element.81), channel_id=1, source_target_pairs={{0,2},{1,3},{2,0},{3,1},{4,6},{5,7},{6,4},{7,5},{8,10},{9,11},{10,... | collective-permute-start | bytes 294920 | tf_op jit(solution)/shard_map/ppermute | solution.py:296
  53.2 5.1 %collective-permute-start.13 = (bf16[16,3072]{1,0:T(8,128)(2,1)S(1)}, bf16[16,3072]{1,0:T(8,128)(2,1)S(1)}, u32[]{:S(2)}, u32[]{:S(2)}) collective-permute-start(bf16[16,3072]{1,0:T(8,128)(2,1)S(1)} %get-tuple-element.75), channel_id=1, source_target_pairs={{0,2},{1,3},{2,0},{3,1},{4,6},{5,7},{6,4},{7,5},{8,10},{9,11},{10,... | collective-permute-start | bytes 294920 | tf_op jit(solution)/shard_map/ppermute | solution.py:296
  56.2 10.6 %collective-permute-start.20 = (bf16[16,3072]{1,0:T(8,128)(2,1)S(1)}, bf16[16,3072]{1,0:T(8,128)(2,1)S(1)}, u32[]{:S(2)}, u32[]{:S(2)}) collective-permute-start(bf16[16,3072]{1,0:T(8,128)(2,1)S(1)} %add_convert_fusion.4), channel_id=1, source_target_pairs={{0,8},{1,9},{2,10},{3,11},{4,12},{5,13},{6,14},{7,15},{8,0},{9,1},... | collective-permute-start | bytes 294920 | tf_op jit(solution)/shard_map/ppermute | solution.py:291
  57.2 7.7 %collective-permute-start.16 = (bf16[16,6144]{1,0:T(8,128)(2,1)S(1)}, bf16[16,6144]{1,0:T(8,128)(2,1)S(1)}, u32[]{:S(2)}, u32[]{:S(2)}) collective-permute-start(bf16[16,6144]{1,0:T(8,128)(2,1)S(1)} %get-tuple-element.67), channel_id=1, source_target_pairs={{0,2},{1,3},{2,0},{3,1},{4,6},{5,7},{6,4},{7,5},{8,10},{9,11},{10,... | collective-permute-start | bytes 589832 | tf_op jit(solution)/shard_map/ppermute | solution.py:296
  58.4 10.5 %collective-permute-start.18 = (bf16[16,3072]{1,0:T(8,128)(2,1)S(1)}, bf16[16,3072]{1,0:T(8,128)(2,1)S(1)}, u32[]{:S(2)}, u32[]{:S(2)}) collective-permute-start(bf16[16,3072]{1,0:T(8,128)(2,1)S(1)} %add_convert_fusion.5), channel_id=1, source_target_pairs={{0,8},{1,9},{2,10},{3,11},{4,12},{5,13},{6,14},{7,15},{8,0},{9,1},... | collective-permute-start | bytes 294920 | tf_op jit(solution)/shard_map/ppermute | solution.py:291
  59.8 9.0 %collective-permute-start.14 = (bf16[16,6144]{1,0:T(8,128)(2,1)S(1)}, bf16[16,6144]{1,0:T(8,128)(2,1)S(1)}, u32[]{:S(2)}, u32[]{:S(2)}) collective-permute-start(bf16[16,6144]{1,0:T(8,128)(2,1)S(1)} %get-tuple-element.66), channel_id=1, source_target_pairs={{0,2},{1,3},{2,0},{3,1},{4,6},{5,7},{6,4},{7,5},{8,10},{9,11},{10,... | collective-permute-start | bytes 589832 | tf_op jit(solution)/shard_map/ppermute | solution.py:296
  66.9 8.2 %collective-permute-start.21 = (bf16[16,6144]{1,0:T(8,128)(2,1)S(1)}, bf16[16,6144]{1,0:T(8,128)(2,1)S(1)}, u32[]{:S(2)}, u32[]{:S(2)}) collective-permute-start(bf16[16,6144]{1,0:T(8,128)(2,1)S(1)} %add_convert_fusion.2), channel_id=1, source_target_pairs={{0,4},{1,5},{2,6},{3,7},{4,8},{5,9},{6,10},{7,11},{8,12},{9,13},{1... | collective-permute-start | bytes 589832 | tf_op jit(solution)/shard_map/ppermute | solution.py:291
  68.8 8.1 %collective-permute-start.19 = (bf16[16,6144]{1,0:T(8,128)(2,1)S(1)}, bf16[16,6144]{1,0:T(8,128)(2,1)S(1)}, u32[]{:S(2)}, u32[]{:S(2)}) collective-permute-start(bf16[16,6144]{1,0:T(8,128)(2,1)S(1)} %add_convert_fusion.3), channel_id=1, source_target_pairs={{0,12},{1,13},{2,14},{3,15},{4,0},{5,1},{6,2},{7,3},{8,4},{9,5},{1... | collective-permute-start | bytes 589832 | tf_op jit(solution)/shard_map/ppermute | solution.py:291
  71.0 5.9 %collective-permute-start.17 = (bf16[16,6144]{1,0:T(8,128)(2,1)S(1)}, bf16[16,6144]{1,0:T(8,128)(2,1)S(1)}, u32[]{:S(2)}, u32[]{:S(2)}) collective-permute-start(bf16[16,6144]{1,0:T(8,128)(2,1)S(1)} %pad_maximum_fusion), channel_id=1, source_target_pairs={{0,2},{1,3},{2,0},{3,1},{4,6},{5,7},{6,4},{7,5},{8,10},{9,11},{10,... | collective-permute-start | bytes 589832 | tf_op jit(solution)/shard_map/ppermute | solution.py:296

commit v13 on v12

--- a/solution.py
+++ b/solution.py
@@ -10,10 +10,11 @@
 EXPERTS = 4
 CAP = 16
 HALVES = 2
-ORDER = (2, 3, 1)
+ORDER = (2, 1, 3)
 FORTH = (7, 5)
 BACK = (1, 1)
 BLOCK = 512
+AHEAD = 8
 FETCH_ROWS = 144
 MIB = 1 << 20
 LIMIT = pltpu.CompilerParams(vmem_limit_bytes=10 * MIB)
@@ -197,38 +198,43 @@
     return out[: len(later)], out[len(later) :]
 
 
-def down_kernel(ahead, hidden_ref, w_ref, *refs):
+def down_kernel(ahead, segments, hidden_ref, *refs):
+    weights, refs = refs[: len(segments)], refs[len(segments) :]
     later, held, refs = refs[:ahead], refs[ahead : 2 * ahead], refs[2 * ahead :]
     keep_ref, send_ref, sems = refs
     half, part = keep_ref.shape
-    block = part // 2
-    copies = fetches(later, part, held, sems)
+    copies = fetches(later, AHEAD * BLOCK, held, sems)
     for copy in copies:
         copy.start()
-
-    @pl.loop(0, 2)
-    def _(c):
-        columns = pl.ds(pl.multiple_of(c * block, block), block)
-        out = jnp.dot(hidden_ref[...], w_ref[:, columns], preferred_element_type=jnp.float32)
-        out = out.astype(jnp.bfloat16)
-        keep_ref[:, columns] = out[:half]
-        send_ref[:, columns] = out[half:]
-
+    done = 0
+    for w_ref, (first, size) in zip(weights, segments):
+        block = size // 2
+
+        @pl.loop(0, 2)
+        def _(c, first=first, done=done, block=block, w_ref=w_ref):
+            columns = pl.ds(pl.multiple_of(first + c * block, BLOCK), block)
+            out = jnp.dot(hidden_ref[...], w_ref[:, columns], preferred_element_type=jnp.float32)
+            out = out.astype(jnp.bfloat16)
+            columns = pl.ds(pl.multiple_of(done + c * block, BLOCK), block)
+            keep_ref[:, columns] = out[:half]
+            send_ref[:, columns] = out[half:]
+
+        done += size
     for copy in copies:
         copy.wait()
 
 
-def down(hidden, w_down, later):
+def down(hidden, weights, segments, later):
     rows, depth = hidden.shape
-    part = w_down.shape[1]
+    part = sum(size for _, size in segments)
     ahead = len(later)
-    out_shape = [pltpu.VMEM((depth, w.shape[1] - part), jnp.bfloat16) for w in later]
+    out_shape = [pltpu.VMEM((depth, w.shape[1] - AHEAD * BLOCK), jnp.bfloat16) for w in later]
     out_shape += [jax.ShapeDtypeStruct((rows // 2, part), jnp.bfloat16)] * 2
-    w_down = pltpu.with_memory_space_constraint(w_down, pltpu.VMEM)
+    weights = [pltpu.with_memory_space_constraint(w, pltpu.VMEM) for w in weights]
     later = [pltpu.with_memory_space_constraint(w, pltpu.HBM) for w in later]
     out = pl.pallas_call(
-        functools.partial(down_kernel, ahead),
-        in_specs=[VMEM, VMEM] + [ANY] * ahead,
+        functools.partial(down_kernel, ahead, segments),
+        in_specs=[VMEM] * (1 + len(weights)) + [ANY] * ahead,
         out_specs=[VMEM] * (ahead + 2),
         out_shape=out_shape,
         scratch_shapes=[pltpu.SemaphoreType.DMA((max(ahead, 1), depth // FETCH_ROWS))],
@@ -239,7 +245,7 @@
             transcendentals=0,
         ),
         name="down",
-    )(hidden, w_down, *later)
+    )(hidden, *weights, *later)
     return out[:ahead], out[ahead:]
 
 
@@ -302,13 +308,12 @@
     ids = expert_ids.T
     own, *sends = pack(group, ids, activations, norm_gain)
     far_own = swap(own, far)
-    now = [fetch(w_gate, 0, spans(width)[0][1], own)]
+    now = [fetch(w, 0, spans(width)[0][1], own) for w in (w_gate, w_up)]
     blocks = []
     for k in range(HALVES):
         x = sends[k * others : (k + 1) * others]
         if k:
             x = relay(after(x, *now, far_own), blocks[-1])
-            now.append(fetch(w_up, 0, spans(width)[0][1], x[0]))
         arrivals = [shift(x[s - 1], s) for s in ORDER]
         blocks.append(jnp.concatenate(arrivals, axis=0))
     totals = []
@@ -328,13 +333,17 @@
             pieces[1] = after(pieces[1], blocks[k + 1])
         later, ahead = [w_gate, w_up], (size, width - size)
         if k == HALVES - 1:
-            later, ahead = [w_down], spans(width, BACK)[0]
+            later, ahead = [w_down], (0, AHEAD * BLOCK)
         now, totals = gate_up(k, pieces, now, later, ahead, totals)
     hidden = totals[0]
     held = []
-    for k in range(HALVES):
-        later = [w_down] if k == 0 else []
-        now, (keep, send) = down(hidden, now[0], later)
+    early = AHEAD * BLOCK
+    for k, (at, size) in enumerate(spans(width, BACK)):
+        if k == 0:
+            rest, (keep, send) = down(hidden, now, [(at, size)], [w_down])
+        else:
+            segments = [(at, early - at), (0, width - early)]
+            _, (keep, send) = down(hidden, [*now, *rest], segments, [])
         bit = 1
         while bit < far:
             total = added(keep, swap(send, bit))

time: 78.4 us -> 75.9 us (0.968)
  waiting for transfers between devices: 23.6 us -> 21.6 us
    ppermute x10, waiting for transfers between devices: 11.6 us -> 9.07 us  [shift(): lax.ppermute(x, 'expert', [(i, (i + s * group) % devices) for i in range(...]
    ppermute x10, starting transfers between devices: 20.5 us -> 18 us  [shift(): lax.ppermute(x, 'expert', [(i, (i + s * group) % devices) for i in range(...]
    ppermute x12, starting transfers between devices: 8.23 us -> 10.5 us  [swap(): return lax.ppermute(x, 'expert', [(i, i ^ bit) for i in range(devices)])]
  transfers between devices with their start and end apart: 22 -> 22, of which waited for: 13 -> 12; matrix products, arithmetic and copies ran while one was open for 1% -> 1% of each run, Pallas kernels for 19% -> 20%
where the time goes in v13:
time: 75.9 us; the launch traced here: 75.8 us
  starting transfers between devices  28.5 us (38%)
  Pallas kernels  24.6 us (32%)
  waiting for transfers between devices  21.6 us (28%)
    ppermute x10, starting transfers between devices, shift(): lax.ppermute(x, 'expert', [(i, (i + s * group) % devices) for i in range(...  18 us
    ppermute x12, waiting for transfers between devices, swap(): return lax.ppermute(x, 'expert', [(i, i ^ bit) for i in range(devices)])  12.5 us
    ppermute x12, starting transfers between devices, swap(): return lax.ppermute(x, 'expert', [(i, i ^ bit) for i in range(devices)])  10.5 us
    pallas_call x2, Pallas kernels, gate_up(): pl.pallas_call(functools.partial(gate_up_kernel, len(pieces), len(later),...  9.62 us
    ppermute x10, waiting for transfers between devices, shift(): lax.ppermute(x, 'expert', [(i, (i + s * group) % devices) for i in range(...  9.07 us
    pallas_call x2, Pallas kernels, fetch(): pl.pallas_call(functools.partial(fetch_kernel, at), in_specs=[ANY, ANY],...  6.88 us
    pallas_call x2, Pallas kernels, down(): pl.pallas_call(functools.partial(down_kernel, ahead, segments), in_specs=...  5.29 us
  transfers between devices with their start and end apart: 22, of which 12 were waited for; matrix products, arithmetic and copies ran while one was open for 1% of the time, Pallas kernels for 20%

profile of v13, /device:TPU:0, one launch (start us, length us, event | category | flops | bytes accessed | tf_op | source)
XLA Modules:
  0.0 75.8 jit_solution(7341964841860082371)
XLA Ops:
  0.0 1.5 %norm_and_pack.1 = (bf16[16,6144]{1,0:T(8,128)(2,1)S(1)}, bf16[16,3584]{1,0:T(8,128)(2,1)S(1)}, bf16[16,3584]{1,0:T(8,128)(2,1)S(1)}, bf16[16,3584]{1,0:T(8,128)...) custom-call(s32[2,24]{1,0:T(2,128)} %bitcast.3, ...), custom_call_target="tpu_custom_call" | custom-call | tf_op jit(solution)/shard_map/norm_and_pack/pallas_call | solution.py:67
  1.5 4.1 %collective-permute-start.1 = (bf16[16,3584]{1,0:T(8,128)(2,1)S(1)}, bf16[16,3584]{1,0:T(8,128)(2,1)S(1)}, u32[]{:S(2)}, u32[]{:S(2)}) collective-permute-start(bf16[16,3584]{1,0:T(8,128)(2,1)S(1)} %get-tuple-element.45), channel_id=1, source_target_pairs={{0,8},{1,9},{2,10},{3,11},{4,12},{5,13},{6,14},{7,15},{8,0},{9,1},... | collective-permute-start | bytes 344072 | tf_op jit(solution)/shard_map/ppermute | solution.py:297
  5.6 1.6 %collective-permute-start.2 = (bf16[16,3584]{1,0:T(8,128)(2,1)S(1)}, bf16[16,3584]{1,0:T(8,128)(2,1)S(1)}, u32[]{:S(2)}, u32[]{:S(2)}) collective-permute-start(bf16[16,3584]{1,0:T(8,128)(2,1)S(1)} %get-tuple-element.46), channel_id=1, source_target_pairs={{0,4},{1,5},{2,6},{3,7},{4,8},{5,9},{6,10},{7,11},{8,12},{9,13},{1... | collective-permute-start | bytes 344072 | tf_op jit(solution)/shard_map/ppermute | solution.py:297
  7.2 2.2 %collective-permute-start.3 = (bf16[16,3584]{1,0:T(8,128)(2,1)S(1)}, bf16[16,3584]{1,0:T(8,128)(2,1)S(1)}, u32[]{:S(2)}, u32[]{:S(2)}) collective-permute-start(bf16[16,3584]{1,0:T(8,128)(2,1)S(1)} %get-tuple-element.47), channel_id=1, source_target_pairs={{0,12},{1,13},{2,14},{3,15},{4,0},{5,1},{6,2},{7,3},{8,4},{9,5},{1... | collective-permute-start | bytes 344072 | tf_op jit(solution)/shard_map/ppermute | solution.py:297
  9.4 1.5 %collective-permute-start = (bf16[16,6144]{1,0:T(8,128)(2,1)S(1)}, bf16[16,6144]{1,0:T(8,128)(2,1)S(1)}, u32[]{:S(2)}, u32[]{:S(2)}) collective-permute-start(bf16[16,6144]{1,0:T(8,128)(2,1)S(1)} %get-tuple-element.38.after_ref.refs_0_), channel_id=1, source_target_pairs={{0,2},{1,3},{2,0},{3,1},{4,6},{5,7},{6,4},{7,5},{8,10},{9,11},{10,... | collective-permute-start | bytes 589832 | tf_op jit(solution)/shard_map/ppermute | solution.py:302
  11.0 3.4 %fetch.3.refs_6_ = bf16[1152,3584]{1,0:T(8,128)(2,1)S(1)} custom-call(bf16[1152,6144]{1,0:T(8,128)(2,1)} %refs_8_.1, bf16[16,6144]{1,0:T(8,128)(2,1)S(1)} %get-tuple-element.38.after_ref.refs_0_), custom_call_target="tpu_custom_call" | custom-call | bytes 16515072 | tf_op jit(solution)/shard_map/fetch/pallas_call | solution.py:100
  14.4 3.4 %fetch.2.refs_5_ = bf16[1152,3584]{1,0:T(8,128)(2,1)S(1)} custom-call(bf16[1152,6144]{1,0:T(8,128)(2,1)} %refs_7_.2, bf16[16,6144]{1,0:T(8,128)(2,1)S(1)} %get-tuple-element.38.after_ref.refs_0_), custom_call_target="tpu_custom_call" | custom-call | bytes 16515072 | tf_op jit(solution)/shard_map/fetch/pallas_call | solution.py:100
  17.9 0.0 collective-permute-done.1
  17.9 0.0 collective-permute-done.2
  17.9 0.0 collective-permute-done.3
  18.0 0.6 collective-permute-start.8
  18.5 0.0 collective-permute-done.refs_2_
  18.6 1.9 %collective-permute-start.4 = (bf16[16,2560]{1,0:T(8,128)(2,1)S(1)}, bf16[16,2560]{1,0:T(8,128)(2,1)S(1)}, u32[]{:S(2)}, u32[]{:S(2)}) collective-permute-start(bf16[16,2560]{1,0:T(8,128)(2,1)S(1)} %get-tuple-element.48), channel_id=1, source_target_pairs={{0,8},{1,9},{2,10},{3,11},{4,12},{5,13},{6,14},{7,15},{8,0},{9,1},... | collective-permute-start | bytes 245768 | tf_op jit(solution)/shard_map/ppermute | solution.py:297
  20.5 0.0 collective-permute-start.5
  20.5 3.8 %collective-permute-start.6 = (bf16[16,2560]{1,0:T(8,128)(2,1)S(1)}, bf16[16,2560]{1,0:T(8,128)(2,1)S(1)}, u32[]{:S(2)}, u32[]{:S(2)}) collective-permute-start(bf16[16,2560]{1,0:T(8,128)(2,1)S(1)} %get-tuple-element.50), channel_id=1, source_target_pairs={{0,12},{1,13},{2,14},{3,15},{4,0},{5,1},{6,2},{7,3},{8,4},{9,5},{1... | collective-permute-start | bytes 245768 | tf_op jit(solution)/shard_map/ppermute | solution.py:297
  24.3 1.8 %collective-permute-done.4 = bf16[16,2560]{1,0:T(8,128)(2,1)S(1)} collective-permute-done((bf16[16,2560]{1,0:T(8,128)(2,1)S(1)}, bf16[16,2560]{1,0:T(8,128)(2,1)S(1)}, u32[]{:S(2)}, u32[]{:S(2)}) %collective-permute-start.4) | collective-permute-done | bytes 81952 | tf_op jit(solution)/shard_map/ppermute | solution.py:297
  26.2 0.9 %collective-permute-done.5 = bf16[16,2560]{1,0:T(8,128)(2,1)S(1)} collective-permute-done((bf16[16,2560]{1,0:T(8,128)(2,1)S(1)}, bf16[16,2560]{1,0:T(8,128)(2,1)S(1)}, u32[]{:S(2)}, u32[]{:S(2)}) %collective-permute-start.5) | collective-permute-done | bytes 81952 | tf_op jit(solution)/shard_map/ppermute | solution.py:297
  27.1 0.0 collective-permute-done.8.refs_3_
  27.2 0.1 collective-permute-start.9
  27.3 0.0 collective-permute-done.6
  27.3 1.1 %collective-permute-start.7 = (bf16[48,2560]{1,0:T(8,128)(2,1)S(1)}, bf16[48,2560]{1,0:T(8,128)(2,1)S(1)}, u32[]{:S(2)}, u32[]{:S(2)}) collective-permute-start(bf16[48,2560]{1,0:T(8,128)(2,1)S(1)} %get-tuple-element.92.refs_1_), channel_id=1, source_target_pairs={{0,2},{1,3},{2,0},{3,1},{4,6},{5,7},{6,4},{7,5},{8,10},{9,11},{10,... | collective-permute-start | bytes 737288 | tf_op jit(solution)/shard_map/ppermute | solution.py:302
  28.4 1.3 %collective-permute-done.9.refs_4_ = bf16[128,3584]{1,0:T(8,128)(2,1)S(1)} collective-permute-done((bf16[128,3584]{1,0:T(8,128)(2,1)S(1)}, bf16[128,3584]{1,0:T(8,128)(2,1)S(1)}, u32[]{:S(2)}, u32[]{:S(2)}) %collective-permute-start.9) | collective-permute-done | bytes 917536 | tf_op jit(solution)/shard_map/ppermute | solution.py:302
  29.7 5.5 %gate_up.2 = (bf16[1152,2560]{1,0:T(8,128)(2,1)S(1)}, bf16[1152,2560]{1,0:T(8,128)(2,1)S(1)}, f32[1152,256]{1,0:T(8,128)S(1)}, f32[1152,256]{1,0:T(8,128)S(1)}) custom-call(bf16[16,6144]{1,0:T(8,128)(2,1)S(1)} %get-tuple-element.38.after_ref.refs_0_, bf16[48,3584]{1,0:T(8,128)(2,1)S(1)} %get-tuple-element.51.refs_3_.refs_1_, ...), custom_call_target="tpu_custom_call" | custom-call | flops 4227858432 | bytes 18874368 | tf_op jit(solution)/shard_map/gate_up/pallas_call | solution.py:182
  35.2 0.5 collective-permute-done.7.refs_3_
  35.7 0.1 collective-permute-start.10
  35.8 2.1 %collective-permute-done.10.refs_4_ = bf16[128,2560]{1,0:T(8,128)(2,1)S(1)} collective-permute-done((bf16[128,2560]{1,0:T(8,128)(2,1)S(1)}, bf16[128,2560]{1,0:T(8,128)(2,1)S(1)}, u32[]{:S(2)}, u32[]{:S(2)}) %collective-permute-start.10) | collective-permute-done | bytes 655392 | tf_op jit(solution)/shard_map/ppermute | solution.py:302
  37.9 4.1 %gate_up.3 = (bf16[1152,4096]{1,0:T(8,128)(2,1)S(1)}, bf16[256,1152]{1,0:T(8,128)(2,1)S(1)}) custom-call(bf16[16,6144]{1,0:T(8,128)(2,1)S(1)} %get-tuple-element.38.after_ref.refs_0_, bf16[48,2560]{1,0:T(8,128)(2,1)S(1)} %get-tuple-element.92.refs_1_, bf16[16,6144]{1,0:T(8,128)(2,1)S(1)} %collective-permute-done.refs_2_, ...), custom_call_target="tpu_custom_call" | custom-call | flops 3019898880 | bytes 14155776 | tf_op jit(solution)/shard_map/gate_up/pallas_call | solution.py:182
  42.0 2.5 %down.2 = (bf16[1152,2048]{1,0:T(8,128)(2,1)S(1)}, bf16[128,3072]{1,0:T(8,128)(2,1)S(1)}, bf16[128,3072]{1,0:T(8,128)(2,1)S(1)}) custom-call(bf16[256,1152]{1,0:T(8,128)(2,1)S(1)} %get-tuple-element.59.hidden_ref, bf16[1152,4096]{1,0:T(8,128)(2,1)S(1)} %get-tuple-element.60.refs_0_, bf16[1152,6144]{1,0:T(8,128)(2,1)} %refs_1_.1), custom_call_target="tpu_custom_call" | custom-call | flops 1811939328 | bytes 9240576 | tf_op jit(solution)/shard_map/down/pallas_call | solution.py:235
  44.5 0.2 collective-permute-start.11
  44.7 2.8 %down.3 = (bf16[128,3072]{1,0:T(8,128)(2,1)S(1)}, bf16[128,3072]{1,0:T(8,128)(2,1)S(1)}) custom-call(bf16[256,1152]{1,0:T(8,128)(2,1)S(1)} %get-tuple-element.59.hidden_ref, bf16[1152,4096]{1,0:T(8,128)(2,1)S(1)} %get-tuple-element.60.refs_0_, bf16[1152,2048]{1,0:T(8,128)(2,1)S(1)} %get-tuple-element.63.refs_1_), custom_call_target="tpu_custom_call" | custom-call | flops 1811939328 | bytes 9240576 | tf_op jit(solution)/shard_map/down/pallas_call | solution.py:235
  47.5 0.4 collective-permute-start.12
  48.0 0.0 collective-permute-done.11
  48.0 0.0 copy-start
  48.0 0.0 copy-start.1
  48.0 0.0 copy-start.2
  48.0 0.2 add_convert_fusion.1
  48.2 1.0 %collective-permute-start.15 = (bf16[16,3072]{1,0:T(8,128)(2,1)S(1)}, bf16[16,3072]{1,0:T(8,128)(2,1)S(1)}, u32[]{:S(2)}, u32[]{:S(2)}) collective-permute-start(bf16[16,3072]{1,0:T(8,128)(2,1)S(1)} %get-tuple-element.81), channel_id=1, source_target_pairs={{0,2},{1,3},{2,0},{3,1},{4,6},{5,7},{6,4},{7,5},{8,10},{9,11},{10,... | collective-permute-start | bytes 294920 | tf_op jit(solution)/shard_map/ppermute | solution.py:302
  49.2 0.7 collective-permute-done.12
  49.9 0.2 add_convert_fusion
  50.1 1.0 %collective-permute-start.13 = (bf16[16,3072]{1,0:T(8,128)(2,1)S(1)}, bf16[16,3072]{1,0:T(8,128)(2,1)S(1)}, u32[]{:S(2)}, u32[]{:S(2)}) collective-permute-start(bf16[16,3072]{1,0:T(8,128)(2,1)S(1)} %get-tuple-element.75), channel_id=1, source_target_pairs={{0,2},{1,3},{2,0},{3,1},{4,6},{5,7},{6,4},{7,5},{8,10},{9,11},{10,... | collective-permute-start | bytes 294920 | tf_op jit(solution)/shard_map/ppermute | solution.py:302
  51.2 2.0 %collective-permute-done.15 = bf16[16,3072]{1,0:T(8,128)(2,1)S(1)} collective-permute-done((bf16[16,3072]{1,0:T(8,128)(2,1)S(1)}, bf16[16,3072]{1,0:T(8,128)(2,1)S(1)}, u32[]{:S(2)}, u32[]{:S(2)}) %collective-permute-start.15) | collective-permute-done | bytes 98336 | tf_op jit(solution)/shard_map/ppermute | solution.py:302
  53.2 1.8 %collective-permute-start.20 = (bf16[16,3072]{1,0:T(8,128)(2,1)S(1)}, bf16[16,3072]{1,0:T(8,128)(2,1)S(1)}, u32[]{:S(2)}, u32[]{:S(2)}) collective-permute-start(bf16[16,3072]{1,0:T(8,128)(2,1)S(1)} %add_convert_fusion.4), channel_id=1, source_target_pairs={{0,8},{1,9},{2,10},{3,11},{4,12},{5,13},{6,14},{7,15},{8,0},{9,1},... | collective-permute-start | bytes 294920 | tf_op jit(solution)/shard_map/ppermute | solution.py:297
  54.9 1.5 %collective-permute-start.16 = (bf16[16,6144]{1,0:T(8,128)(2,1)S(1)}, bf16[16,6144]{1,0:T(8,128)(2,1)S(1)}, u32[]{:S(2)}, u32[]{:S(2)}) collective-permute-start(bf16[16,6144]{1,0:T(8,128)(2,1)S(1)} %get-tuple-element.67), channel_id=1, source_target_pairs={{0,2},{1,3},{2,0},{3,1},{4,6},{5,7},{6,4},{7,5},{8,10},{9,11},{10,... | collective-permute-start | bytes 589832 | tf_op jit(solution)/shard_map/ppermute | solution.py:302
  56.5 0.0 collective-permute-done.13
  56.5 0.7 collective-permute-start.18
  57.2 1.4 %collective-permute-start.14 = (bf16[16,6144]{1,0:T(8,128)(2,1)S(1)}, bf16[16,6144]{1,0:T(8,128)(2,1)S(1)}, u32[]{:S(2)}, u32[]{:S(2)}) collective-permute-start(bf16[16,6144]{1,0:T(8,128)(2,1)S(1)} %get-tuple-element.66), channel_id=1, source_target_pairs={{0,2},{1,3},{2,0},{3,1},{4,6},{5,7},{6,4},{7,5},{8,10},{9,11},{10,... | collective-permute-start | bytes 589832 | tf_op jit(solution)/shard_map/ppermute | solution.py:302
  58.6 4.0 %collective-permute-done.16 = bf16[16,6144]{1,0:T(8,128)(2,1)S(1)} collective-permute-done((bf16[16,6144]{1,0:T(8,128)(2,1)S(1)}, bf16[16,6144]{1,0:T(8,128)(2,1)S(1)}, u32[]{:S(2)}, u32[]{:S(2)}) %collective-permute-start.16) | collective-permute-done | bytes 196640 | tf_op jit(solution)/shard_map/ppermute | solution.py:302
  62.6 0.1 add_convert_fusion.2
  62.7 0.3 collective-permute-done.20.refs_2_
  63.0 0.0 collective-permute-start.21
  63.0 2.0 %collective-permute-done.14 = bf16[16,6144]{1,0:T(8,128)(2,1)S(1)} collective-permute-done((bf16[16,6144]{1,0:T(8,128)(2,1)S(1)}, bf16[16,6144]{1,0:T(8,128)(2,1)S(1)}, u32[]{:S(2)}, u32[]{:S(2)}) %collective-permute-start.14) | collective-permute-done | bytes 196640 | tf_op jit(solution)/shard_map/ppermute | solution.py:302
  65.0 0.0 collective-permute-done.18.refs_3_
  65.0 1.6 %collective-permute-start.17 = (bf16[16,6144]{1,0:T(8,128)(2,1)S(1)}, bf16[16,6144]{1,0:T(8,128)(2,1)S(1)}, u32[]{:S(2)}, u32[]{:S(2)}) collective-permute-start(bf16[16,6144]{1,0:T(8,128)(2,1)S(1)} %pad_maximum_fusion), channel_id=1, source_target_pairs={{0,2},{1,3},{2,0},{3,1},{4,6},{5,7},{6,4},{7,5},{8,10},{9,11},{10,... | collective-permute-start | bytes 589832 | tf_op jit(solution)/shard_map/ppermute | solution.py:302
  66.6 1.9 %collective-permute-start.19 = (bf16[16,6144]{1,0:T(8,128)(2,1)S(1)}, bf16[16,6144]{1,0:T(8,128)(2,1)S(1)}, u32[]{:S(2)}, u32[]{:S(2)}) collective-permute-start(bf16[16,6144]{1,0:T(8,128)(2,1)S(1)} %add_convert_fusion.3), channel_id=1, source_target_pairs={{0,12},{1,13},{2,14},{3,15},{4,0},{5,1},{6,2},{7,3},{8,4},{9,5},{1... | collective-permute-start | bytes 589832 | tf_op jit(solution)/shard_map/ppermute | solution.py:297
  68.6 3.8 %collective-permute-done.21.last = bf16[16,6144]{1,0:T(8,128)(2,1)S(1)} collective-permute-done((bf16[16,6144]{1,0:T(8,128)(2,1)S(1)}, bf16[16,6144]{1,0:T(8,128)(2,1)S(1)}, u32[]{:S(2)}, u32[]{:S(2)}) %collective-permute-start.21) | collective-permute-done | bytes 196640 | tf_op jit(solution)/shard_map/ppermute | solution.py:297
  72.3 0.0 collective-permute-done.17.arrived
  72.3 2.1 %collective-permute-done.19.near = bf16[16,6144]{1,0:T(8,128)(2,1)S(1)} collective-permute-done((bf16[16,6144]{1,0:T(8,128)(2,1)S(1)}, bf16[16,6144]{1,0:T(8,128)(2,1)S(1)}, u32[]{:S(2)}, u32[]{:S(2)}) %collective-permute-start.19) | collective-permute-done | bytes 196640 | tf_op jit(solution)/shard_map/ppermute | solution.py:297
  74.5 0.0 copy-done
  74.5 0.0 copy-done.1
  74.5 0.0 copy-done.2
  74.5 1.3 %mix.1 = bf16[24,6144]{1,0:T(8,128)(2,1)} custom-call(s32[2,24]{1,0:T(2,128)S(1)} %bitcast.4, f32[2,24]{1,0:T(2,128)S(1)} %bitcast.5, bf16[24,6144]{1,0:T(8,128)(2,1)S(1)} %copy-done, bf16[16,6144]{1,0:T(8,128)(2,1)S(1)} %collective-permute-done.17.arrived, bf16[16,6144]{1,0:T(8,128)(2,1)S(1)} %collective-permute-done.19.near, ...), custom_call_target="tpu_custom_call" | custom-call | tf_op jit(solution)/shard_map/mix/pallas_call | solution.py:276
  (20 shorter events, 0.4 us)
Async XLA Ops:
  1.5 16.4 %collective-permute-start.1 = (bf16[16,3584]{1,0:T(8,128)(2,1)S(1)}, bf16[16,3584]{1,0:T(8,128)(2,1)S(1)}, u32[]{:S(2)}, u32[]{:S(2)}) collective-permute-start(bf16[16,3584]{1,0:T(8,128)(2,1)S(1)} %get-tuple-element.45), channel_id=1, source_target_pairs={{0,8},{1,9},{2,10},{3,11},{4,12},{5,13},{6,14},{7,15},{8,0},{9,1},... | collective-permute-start | bytes 344072 | tf_op jit(solution)/shard_map/ppermute | solution.py:297
  5.6 12.3 %collective-permute-start.2 = (bf16[16,3584]{1,0:T(8,128)(2,1)S(1)}, bf16[16,3584]{1,0:T(8,128)(2,1)S(1)}, u32[]{:S(2)}, u32[]{:S(2)}) collective-permute-start(bf16[16,3584]{1,0:T(8,128)(2,1)S(1)} %get-tuple-element.46), channel_id=1, source_target_pairs={{0,4},{1,5},{2,6},{3,7},{4,8},{5,9},{6,10},{7,11},{8,12},{9,13},{1... | collective-permute-start | bytes 344072 | tf_op jit(solution)/shard_map/ppermute | solution.py:297
  7.2 10.8 %collective-permute-start.3 = (bf16[16,3584]{1,0:T(8,128)(2,1)S(1)}, bf16[16,3584]{1,0:T(8,128)(2,1)S(1)}, u32[]{:S(2)}, u32[]{:S(2)}) collective-permute-start(bf16[16,3584]{1,0:T(8,128)(2,1)S(1)} %get-tuple-element.47), channel_id=1, source_target_pairs={{0,12},{1,13},{2,14},{3,15},{4,0},{5,1},{6,2},{7,3},{8,4},{9,5},{1... | collective-permute-start | bytes 344072 | tf_op jit(solution)/shard_map/ppermute | solution.py:297
  9.4 9.1 %collective-permute-start = (bf16[16,6144]{1,0:T(8,128)(2,1)S(1)}, bf16[16,6144]{1,0:T(8,128)(2,1)S(1)}, u32[]{:S(2)}, u32[]{:S(2)}) collective-permute-start(bf16[16,6144]{1,0:T(8,128)(2,1)S(1)} %get-tuple-element.38.after_ref.refs_0_), channel_id=1, source_target_pairs={{0,2},{1,3},{2,0},{3,1},{4,6},{5,7},{6,4},{7,5},{8,10},{9,11},{10,... | collective-permute-start | bytes 589832 | tf_op jit(solution)/shard_map/ppermute | solution.py:302
  18.0 9.2 %collective-permute-start.8 = (bf16[48,3584]{1,0:T(8,128)(2,1)S(1)}, bf16[48,3584]{1,0:T(8,128)(2,1)S(1)}, u32[]{:S(2)}, u32[]{:S(2)}) collective-permute-start(bf16[48,3584]{1,0:T(8,128)(2,1)S(1)} %get-tuple-element.51.refs_3_.refs_1_), channel_id=1, source_target_pairs={{0,2},{1,3},{2,0},{3,1},{4,6},{5,7},{6,4},{7,5},{8,10},{9,11},{10,... | collective-permute-start | bytes 1032200 | tf_op jit(solution)/shard_map/ppermute | solution.py:302
  18.6 7.6 %collective-permute-start.4 = (bf16[16,2560]{1,0:T(8,128)(2,1)S(1)}, bf16[16,2560]{1,0:T(8,128)(2,1)S(1)}, u32[]{:S(2)}, u32[]{:S(2)}) collective-permute-start(bf16[16,2560]{1,0:T(8,128)(2,1)S(1)} %get-tuple-element.48), channel_id=1, source_target_pairs={{0,8},{1,9},{2,10},{3,11},{4,12},{5,13},{6,14},{7,15},{8,0},{9,1},... | collective-permute-start | bytes 245768 | tf_op jit(solution)/shard_map/ppermute | solution.py:297
  20.5 6.6 %collective-permute-start.5 = (bf16[16,2560]{1,0:T(8,128)(2,1)S(1)}, bf16[16,2560]{1,0:T(8,128)(2,1)S(1)}, u32[]{:S(2)}, u32[]{:S(2)}) collective-permute-start(bf16[16,2560]{1,0:T(8,128)(2,1)S(1)} %get-tuple-element.49), channel_id=1, source_target_pairs={{0,4},{1,5},{2,6},{3,7},{4,8},{5,9},{6,10},{7,11},{8,12},{9,13},{1... | collective-permute-start | bytes 245768 | tf_op jit(solution)/shard_map/ppermute | solution.py:297
  20.5 6.8 %collective-permute-start.6 = (bf16[16,2560]{1,0:T(8,128)(2,1)S(1)}, bf16[16,2560]{1,0:T(8,128)(2,1)S(1)}, u32[]{:S(2)}, u32[]{:S(2)}) collective-permute-start(bf16[16,2560]{1,0:T(8,128)(2,1)S(1)} %get-tuple-element.50), channel_id=1, source_target_pairs={{0,12},{1,13},{2,14},{3,15},{4,0},{5,1},{6,2},{7,3},{8,4},{9,5},{1... | collective-permute-start | bytes 245768 | tf_op jit(solution)/shard_map/ppermute | solution.py:297
  27.2 2.5 %collective-permute-start.9 = (bf16[128,3584]{1,0:T(8,128)(2,1)S(1)}, bf16[128,3584]{1,0:T(8,128)(2,1)S(1)}, u32[]{:S(2)}, u32[]{:S(2)}) collective-permute-start(bf16[128,3584]{1,0:T(8,128)(2,1)S(1)} %constant_dynamic-update-slice_fusion.6), channel_id=1, source_target_pairs={{0,1},{1,0},{2,3},{3,2},{4,5},{5,4},{6,7},{7,6},{8,9},{9,8},{10,11... | collective-permute-start | bytes 2752520 | tf_op jit(solution)/shard_map/ppermute | solution.py:302
  27.3 8.4 %collective-permute-start.7 = (bf16[48,2560]{1,0:T(8,128)(2,1)S(1)}, bf16[48,2560]{1,0:T(8,128)(2,1)S(1)}, u32[]{:S(2)}, u32[]{:S(2)}) collective-permute-start(bf16[48,2560]{1,0:T(8,128)(2,1)S(1)} %get-tuple-element.92.refs_1_), channel_id=1, source_target_pairs={{0,2},{1,3},{2,0},{3,1},{4,6},{5,7},{6,4},{7,5},{8,10},{9,11},{10,... | collective-permute-start | bytes 737288 | tf_op jit(solution)/shard_map/ppermute | solution.py:302
  35.7 2.2 %collective-permute-start.10 = (bf16[128,2560]{1,0:T(8,128)(2,1)S(1)}, bf16[128,2560]{1,0:T(8,128)(2,1)S(1)}, u32[]{:S(2)}, u32[]{:S(2)}) collective-permute-start(bf16[128,2560]{1,0:T(8,128)(2,1)S(1)} %constant_dynamic-update-slice_fusion.10), channel_id=1, source_target_pairs={{0,1},{1,0},{2,3},{3,2},{4,5},{5,4},{6,7},{7,6},{8,9},{9,8},{10,11... | collective-permute-start | bytes 1966088 | tf_op jit(solution)/shard_map/ppermute | solution.py:302
  44.5 3.4 %collective-permute-start.11 = (bf16[128,3072]{1,0:T(8,128)(2,1)S(1)}, bf16[128,3072]{1,0:T(8,128)(2,1)S(1)}, u32[]{:S(2)}, u32[]{:S(2)}) collective-permute-start(bf16[128,3072]{1,0:T(8,128)(2,1)S(1)} %get-tuple-element.62), channel_id=1, source_target_pairs={{0,1},{1,0},{2,3},{3,2},{4,5},{5,4},{6,7},{7,6},{8,9},{9,8},{10,11... | collective-permute-start | bytes 2359304 | tf_op jit(solution)/shard_map/ppermute | solution.py:302
  47.5 2.4 %collective-permute-start.12 = (bf16[128,3072]{1,0:T(8,128)(2,1)S(1)}, bf16[128,3072]{1,0:T(8,128)(2,1)S(1)}, u32[]{:S(2)}, u32[]{:S(2)}) collective-permute-start(bf16[128,3072]{1,0:T(8,128)(2,1)S(1)} %get-tuple-element.65), channel_id=1, source_target_pairs={{0,1},{1,0},{2,3},{3,2},{4,5},{5,4},{6,7},{7,6},{8,9},{9,8},{10,11... | collective-permute-start | bytes 2359304 | tf_op jit(solution)/shard_map/ppermute | solution.py:302
  48.0 26.5 %copy-start = (bf16[24,6144]{1,0:T(8,128)(2,1)S(1)}, bf16[24,6144]{1,0:T(8,128)(2,1)}, u32[]{:S(2)}) copy-start(bf16[24,6144]{1,0:T(8,128)(2,1)} %act_ref.3) | copy-start | bytes 884740
  48.0 26.5 %copy-start.1 = (s32[24,2]{0,1:T(2,128)S(1)}, s32[24,2]{0,1:T(2,128)}, u32[]{:S(2)}) copy-start(s32[24,2]{0,1:T(2,128)} %param.8) | copy-start | bytes 580
  48.0 26.5 %copy-start.2 = (f32[24,2]{0,1:T(2,128)S(1)}, f32[24,2]{0,1:T(2,128)}, u32[]{:S(2)}) copy-start(f32[24,2]{0,1:T(2,128)} %param.9) | copy-start | bytes 580
  48.2 4.9 %collective-permute-start.15 = (bf16[16,3072]{1,0:T(8,128)(2,1)S(1)}, bf16[16,3072]{1,0:T(8,128)(2,1)S(1)}, u32[]{:S(2)}, u32[]{:S(2)}) collective-permute-start(bf16[16,3072]{1,0:T(8,128)(2,1)S(1)} %get-tuple-element.81), channel_id=1, source_target_pairs={{0,2},{1,3},{2,0},{3,1},{4,6},{5,7},{6,4},{7,5},{8,10},{9,11},{10,... | collective-permute-start | bytes 294920 | tf_op jit(solution)/shard_map/ppermute | solution.py:302
  50.1 6.3 %collective-permute-start.13 = (bf16[16,3072]{1,0:T(8,128)(2,1)S(1)}, bf16[16,3072]{1,0:T(8,128)(2,1)S(1)}, u32[]{:S(2)}, u32[]{:S(2)}) collective-permute-start(bf16[16,3072]{1,0:T(8,128)(2,1)S(1)} %get-tuple-element.75), channel_id=1, source_target_pairs={{0,2},{1,3},{2,0},{3,1},{4,6},{5,7},{6,4},{7,5},{8,10},{9,11},{10,... | collective-permute-start | bytes 294920 | tf_op jit(solution)/shard_map/ppermute | solution.py:302
  53.2 9.8 %collective-permute-start.20 = (bf16[16,3072]{1,0:T(8,128)(2,1)S(1)}, bf16[16,3072]{1,0:T(8,128)(2,1)S(1)}, u32[]{:S(2)}, u32[]{:S(2)}) collective-permute-start(bf16[16,3072]{1,0:T(8,128)(2,1)S(1)} %add_convert_fusion.4), channel_id=1, source_target_pairs={{0,8},{1,9},{2,10},{3,11},{4,12},{5,13},{6,14},{7,15},{8,0},{9,1},... | collective-permute-start | bytes 294920 | tf_op jit(solution)/shard_map/ppermute | solution.py:297
  54.9 7.7 %collective-permute-start.16 = (bf16[16,6144]{1,0:T(8,128)(2,1)S(1)}, bf16[16,6144]{1,0:T(8,128)(2,1)S(1)}, u32[]{:S(2)}, u32[]{:S(2)}) collective-permute-start(bf16[16,6144]{1,0:T(8,128)(2,1)S(1)} %get-tuple-element.67), channel_id=1, source_target_pairs={{0,2},{1,3},{2,0},{3,1},{4,6},{5,7},{6,4},{7,5},{8,10},{9,11},{10,... | collective-permute-start | bytes 589832 | tf_op jit(solution)/shard_map/ppermute | solution.py:302
  56.5 8.5 %collective-permute-start.18 = (bf16[16,3072]{1,0:T(8,128)(2,1)S(1)}, bf16[16,3072]{1,0:T(8,128)(2,1)S(1)}, u32[]{:S(2)}, u32[]{:S(2)}) collective-permute-start(bf16[16,3072]{1,0:T(8,128)(2,1)S(1)} %add_convert_fusion.5), channel_id=1, source_target_pairs={{0,8},{1,9},{2,10},{3,11},{4,12},{5,13},{6,14},{7,15},{8,0},{9,1},... | collective-permute-start | bytes 294920 | tf_op jit(solution)/shard_map/ppermute | solution.py:297
  57.2 7.8 %collective-permute-start.14 = (bf16[16,6144]{1,0:T(8,128)(2,1)S(1)}, bf16[16,6144]{1,0:T(8,128)(2,1)S(1)}, u32[]{:S(2)}, u32[]{:S(2)}) collective-permute-start(bf16[16,6144]{1,0:T(8,128)(2,1)S(1)} %get-tuple-element.66), channel_id=1, source_target_pairs={{0,2},{1,3},{2,0},{3,1},{4,6},{5,7},{6,4},{7,5},{8,10},{9,11},{10,... | collective-permute-start | bytes 589832 | tf_op jit(solution)/shard_map/ppermute | solution.py:302
  63.0 9.3 %collective-permute-start.21 = (bf16[16,6144]{1,0:T(8,128)(2,1)S(1)}, bf16[16,6144]{1,0:T(8,128)(2,1)S(1)}, u32[]{:S(2)}, u32[]{:S(2)}) collective-permute-start(bf16[16,6144]{1,0:T(8,128)(2,1)S(1)} %add_convert_fusion.2), channel_id=1, source_target_pairs={{0,4},{1,5},{2,6},{3,7},{4,8},{5,9},{6,10},{7,11},{8,12},{9,13},{1... | collective-permute-start | bytes 589832 | tf_op jit(solution)/shard_map/ppermute | solution.py:297
  65.0 7.3 %collective-permute-start.17 = (bf16[16,6144]{1,0:T(8,128)(2,1)S(1)}, bf16[16,6144]{1,0:T(8,128)(2,1)S(1)}, u32[]{:S(2)}, u32[]{:S(2)}) collective-permute-start(bf16[16,6144]{1,0:T(8,128)(2,1)S(1)} %pad_maximum_fusion), channel_id=1, source_target_pairs={{0,2},{1,3},{2,0},{3,1},{4,6},{5,7},{6,4},{7,5},{8,10},{9,11},{10,... | collective-permute-start | bytes 589832 | tf_op jit(solution)/shard_map/ppermute | solution.py:302
  66.6 7.8 %collective-permute-start.19 = (bf16[16,6144]{1,0:T(8,128)(2,1)S(1)}, bf16[16,6144]{1,0:T(8,128)(2,1)S(1)}, u32[]{:S(2)}, u32[]{:S(2)}) collective-permute-start(bf16[16,6144]{1,0:T(8,128)(2,1)S(1)} %add_convert_fusion.3), channel_id=1, source_target_pairs={{0,12},{1,13},{2,14},{3,15},{4,0},{5,1},{6,2},{7,3},{8,4},{9,5},{1... | collective-permute-start | bytes 589832 | tf_op jit(solution)/shard_map/ppermute | solution.py:297

commit v14 on v13

--- a/solution.py
+++ b/solution.py
@@ -10,7 +10,7 @@
 EXPERTS = 4
 CAP = 16
 HALVES = 2
-ORDER = (2, 1, 3)
+ORDER = (1, 2, 3)
 FORTH = (7, 5)
 BACK = (1, 1)
 BLOCK = 512
@@ -326,7 +326,11 @@
         pieces = [own[:, columns], blocks[k], far_own[:, columns], far_block]
         bit = far // 2
         while bit:
-            pieces.append(swap(jnp.concatenate(pieces, axis=0), bit))
+            if k and len(pieces) == EXPERTS:
+                early = swap(jnp.concatenate(pieces[:-1], axis=0), bit)
+                pieces += [early, swap(far_block, bit)]
+            else:
+                pieces.append(swap(jnp.concatenate(pieces, axis=0), bit))
             bit //= 2
         pieces[0], pieces[2] = own, far_own
         if k < HALVES - 1:

time: 75.9 us -> 75.6 us (level)
  starting transfers between devices: 28.5 us -> 27.3 us
  waiting for transfers between devices: 21.6 us -> 22.6 us
    ppermute x10, waiting for transfers between devices: 9.07 us -> 14.7 us  [shift(): lax.ppermute(x, 'expert', [(i, (i + s * group) % devices) for i in range(...]
    ppermute x12 -> x13, waiting for transfers between devices: 12.5 us -> 7.87 us  [swap(): return lax.ppermute(x, 'expert', [(i, i ^ bit) for i in range(devices)])]
    ppermute x12 -> x13, starting transfers between devices: 10.5 us -> 9.92 us  [swap(): return lax.ppermute(x, 'expert', [(i, i ^ bit) for i in range(devices)])]
  transfers between devices with their start and end apart: 22 -> 23, of which waited for: 12 -> 13; matrix products, arithmetic and copies ran while one was open for 1% -> 1% of each run, Pallas kernels for 20% -> 20%
where the time goes in v14:
time: 75.6 us; the launch traced here: 75.4 us
  starting transfers between devices  27.3 us (36%)
  Pallas kernels  24.5 us (32%)
  waiting for transfers between devices  22.6 us (30%)
    ppermute x10, starting transfers between devices, shift(): lax.ppermute(x, 'expert', [(i, (i + s * group) % devices) for i in range(...  17.4 us
    ppermute x10, waiting for transfers between devices, shift(): lax.ppermute(x, 'expert', [(i, (i + s * group) % devices) for i in range(...  14.7 us
    ppermute x13, starting transfers between devices, swap(): return lax.ppermute(x, 'expert', [(i, i ^ bit) for i in range(devices)])  9.92 us
    pallas_call x2, Pallas kernels, gate_up(): pl.pallas_call(functools.partial(gate_up_kernel, len(pieces), len(later),...  9.5 us
    ppermute x13, waiting for transfers between devices, swap(): return lax.ppermute(x, 'expert', [(i, i ^ bit) for i in range(devices)])  7.87 us
    pallas_call x2, Pallas kernels, fetch(): pl.pallas_call(functools.partial(fetch_kernel, at), in_specs=[ANY, ANY],...  6.88 us
    pallas_call x2, Pallas kernels, down(): pl.pallas_call(functools.partial(down_kernel, ahead, segments), in_specs=...  5.29 us
  transfers between devices with their start and end apart: 23, of which 13 were waited for; matrix products, arithmetic and copies ran while one was open for 1% of the time, Pallas kernels for 20%

profile of v14, /device:TPU:0, one launch (start us, length us, event | category | flops | bytes accessed | tf_op | source)
XLA Modules:
  0.0 75.4 jit_solution(843169821611950453)
XLA Ops:
  0.0 1.5 %norm_and_pack.1 = (bf16[16,6144]{1,0:T(8,128)(2,1)S(1)}, bf16[16,3584]{1,0:T(8,128)(2,1)S(1)}, bf16[16,3584]{1,0:T(8,128)(2,1)S(1)}, bf16[16,3584]{1,0:T(8,128)...) custom-call(s32[2,24]{1,0:T(2,128)} %bitcast.3, ...), custom_call_target="tpu_custom_call" | custom-call | tf_op jit(solution)/shard_map/norm_and_pack/pallas_call | solution.py:67
  1.5 3.1 %collective-permute-start.1 = (bf16[16,3584]{1,0:T(8,128)(2,1)S(1)}, bf16[16,3584]{1,0:T(8,128)(2,1)S(1)}, u32[]{:S(2)}, u32[]{:S(2)}) collective-permute-start(bf16[16,3584]{1,0:T(8,128)(2,1)S(1)} %get-tuple-element.45), channel_id=1, source_target_pairs={{0,4},{1,5},{2,6},{3,7},{4,8},{5,9},{6,10},{7,11},{8,12},{9,13},{1... | collective-permute-start | bytes 344072 | tf_op jit(solution)/shard_map/ppermute | solution.py:297
  4.6 2.6 %collective-permute-start.2 = (bf16[16,3584]{1,0:T(8,128)(2,1)S(1)}, bf16[16,3584]{1,0:T(8,128)(2,1)S(1)}, u32[]{:S(2)}, u32[]{:S(2)}) collective-permute-start(bf16[16,3584]{1,0:T(8,128)(2,1)S(1)} %get-tuple-element.46), channel_id=1, source_target_pairs={{0,8},{1,9},{2,10},{3,11},{4,12},{5,13},{6,14},{7,15},{8,0},{9,1},... | collective-permute-start | bytes 344072 | tf_op jit(solution)/shard_map/ppermute | solution.py:297
  7.2 1.3 %collective-permute-start.3 = (bf16[16,3584]{1,0:T(8,128)(2,1)S(1)}, bf16[16,3584]{1,0:T(8,128)(2,1)S(1)}, u32[]{:S(2)}, u32[]{:S(2)}) collective-permute-start(bf16[16,3584]{1,0:T(8,128)(2,1)S(1)} %get-tuple-element.47), channel_id=1, source_target_pairs={{0,12},{1,13},{2,14},{3,15},{4,0},{5,1},{6,2},{7,3},{8,4},{9,5},{1... | collective-permute-start | bytes 344072 | tf_op jit(solution)/shard_map/ppermute | solution.py:297
  8.5 1.5 %collective-permute-start = (bf16[16,6144]{1,0:T(8,128)(2,1)S(1)}, bf16[16,6144]{1,0:T(8,128)(2,1)S(1)}, u32[]{:S(2)}, u32[]{:S(2)}) collective-permute-start(bf16[16,6144]{1,0:T(8,128)(2,1)S(1)} %get-tuple-element.38.after_ref.refs_0_), channel_id=1, source_target_pairs={{0,2},{1,3},{2,0},{3,1},{4,6},{5,7},{6,4},{7,5},{8,10},{9,11},{10,... | collective-permute-start | bytes 589832 | tf_op jit(solution)/shard_map/ppermute | solution.py:302
  10.1 3.4 %fetch.3.refs_6_ = bf16[1152,3584]{1,0:T(8,128)(2,1)S(1)} custom-call(bf16[1152,6144]{1,0:T(8,128)(2,1)} %refs_8_.2, bf16[16,6144]{1,0:T(8,128)(2,1)S(1)} %get-tuple-element.38.after_ref.refs_0_), custom_call_target="tpu_custom_call" | custom-call | bytes 16515072 | tf_op jit(solution)/shard_map/fetch/pallas_call | solution.py:100
  13.5 3.4 %fetch.2.refs_5_ = bf16[1152,3584]{1,0:T(8,128)(2,1)S(1)} custom-call(bf16[1152,6144]{1,0:T(8,128)(2,1)} %refs_7_.1, bf16[16,6144]{1,0:T(8,128)(2,1)S(1)} %get-tuple-element.38.after_ref.refs_0_), custom_call_target="tpu_custom_call" | custom-call | bytes 16515072 | tf_op jit(solution)/shard_map/fetch/pallas_call | solution.py:100
  16.9 0.0 collective-permute-done.1
  17.0 0.0 collective-permute-done.2
  17.0 0.0 collective-permute-done.3
  17.1 0.6 collective-permute-start.8
  17.6 0.0 collective-permute-done.refs_2_
  17.6 1.8 %collective-permute-start.4 = (bf16[16,2560]{1,0:T(8,128)(2,1)S(1)}, bf16[16,2560]{1,0:T(8,128)(2,1)S(1)}, u32[]{:S(2)}, u32[]{:S(2)}) collective-permute-start(bf16[16,2560]{1,0:T(8,128)(2,1)S(1)} %get-tuple-element.48), channel_id=1, source_target_pairs={{0,4},{1,5},{2,6},{3,7},{4,8},{5,9},{6,10},{7,11},{8,12},{9,13},{1... | collective-permute-start | bytes 245768 | tf_op jit(solution)/shard_map/ppermute | solution.py:297
  19.4 1.6 %collective-permute-start.5 = (bf16[16,2560]{1,0:T(8,128)(2,1)S(1)}, bf16[16,2560]{1,0:T(8,128)(2,1)S(1)}, u32[]{:S(2)}, u32[]{:S(2)}) collective-permute-start(bf16[16,2560]{1,0:T(8,128)(2,1)S(1)} %get-tuple-element.49), channel_id=1, source_target_pairs={{0,8},{1,9},{2,10},{3,11},{4,12},{5,13},{6,14},{7,15},{8,0},{9,1},... | collective-permute-start | bytes 245768 | tf_op jit(solution)/shard_map/ppermute | solution.py:297
  21.0 0.8 %collective-permute-start.6 = (bf16[16,2560]{1,0:T(8,128)(2,1)S(1)}, bf16[16,2560]{1,0:T(8,128)(2,1)S(1)}, u32[]{:S(2)}, u32[]{:S(2)}) collective-permute-start(bf16[16,2560]{1,0:T(8,128)(2,1)S(1)} %get-tuple-element.50), channel_id=1, source_target_pairs={{0,12},{1,13},{2,14},{3,15},{4,0},{5,1},{6,2},{7,3},{8,4},{9,5},{1... | collective-permute-start | bytes 245768 | tf_op jit(solution)/shard_map/ppermute | solution.py:297
  21.9 2.6 %collective-permute-done.4 = bf16[16,2560]{1,0:T(8,128)(2,1)S(1)} collective-permute-done((bf16[16,2560]{1,0:T(8,128)(2,1)S(1)}, bf16[16,2560]{1,0:T(8,128)(2,1)S(1)}, u32[]{:S(2)}, u32[]{:S(2)}) %collective-permute-start.4) | collective-permute-done | bytes 81952 | tf_op jit(solution)/shard_map/ppermute | solution.py:297
  24.4 2.3 %collective-permute-done.5 = bf16[16,2560]{1,0:T(8,128)(2,1)S(1)} collective-permute-done((bf16[16,2560]{1,0:T(8,128)(2,1)S(1)}, bf16[16,2560]{1,0:T(8,128)(2,1)S(1)}, u32[]{:S(2)}, u32[]{:S(2)}) %collective-permute-start.5) | collective-permute-done | bytes 81952 | tf_op jit(solution)/shard_map/ppermute | solution.py:297
  26.8 0.0 collective-permute-done.8.refs_3_
  26.8 0.1 collective-permute-start.9
  26.9 0.0 collective-permute-done.6
  26.9 1.2 %collective-permute-start.7 = (bf16[48,2560]{1,0:T(8,128)(2,1)S(1)}, bf16[48,2560]{1,0:T(8,128)(2,1)S(1)}, u32[]{:S(2)}, u32[]{:S(2)}) collective-permute-start(bf16[48,2560]{1,0:T(8,128)(2,1)S(1)} %get-tuple-element.92.refs_1_), channel_id=1, source_target_pairs={{0,2},{1,3},{2,0},{3,1},{4,6},{5,7},{6,4},{7,5},{8,10},{9,11},{10,... | collective-permute-start | bytes 737288 | tf_op jit(solution)/shard_map/ppermute | solution.py:302
  28.2 0.2 collective-permute-start.10
  28.4 1.0 %collective-permute-done.9.refs_4_ = bf16[128,3584]{1,0:T(8,128)(2,1)S(1)} collective-permute-done((bf16[128,3584]{1,0:T(8,128)(2,1)S(1)}, bf16[128,3584]{1,0:T(8,128)(2,1)S(1)}, u32[]{:S(2)}, u32[]{:S(2)}) %collective-permute-start.9) | collective-permute-done | bytes 917536 | tf_op jit(solution)/shard_map/ppermute | solution.py:302
  29.4 5.5 %gate_up.2 = (bf16[1152,2560]{1,0:T(8,128)(2,1)S(1)}, bf16[1152,2560]{1,0:T(8,128)(2,1)S(1)}, f32[1152,256]{1,0:T(8,128)S(1)}, f32[1152,256]{1,0:T(8,128)S(1)}) custom-call(bf16[16,6144]{1,0:T(8,128)(2,1)S(1)} %get-tuple-element.38.after_ref.refs_0_, bf16[48,3584]{1,0:T(8,128)(2,1)S(1)} %get-tuple-element.51.refs_3_.refs_1_, ...), custom_call_target="tpu_custom_call" | custom-call | flops 4227858432 | bytes 18874368 | tf_op jit(solution)/shard_map/gate_up/pallas_call | solution.py:182
  34.9 0.5 collective-permute-done.7.refs_3_
  35.4 0.0 collective-permute-start.11
  35.4 0.0 collective-permute-done.10.refs_4_
  35.4 1.5 %collective-permute-done.11.refs_5_ = bf16[48,2560]{1,0:T(8,128)(2,1)S(1)} collective-permute-done((bf16[48,2560]{1,0:T(8,128)(2,1)S(1)}, bf16[48,2560]{1,0:T(8,128)(2,1)S(1)}, u32[]{:S(2)}, u32[]{:S(2)}) %collective-permute-start.11) | collective-permute-done | bytes 245792 | tf_op jit(solution)/shard_map/ppermute | solution.py:302
  36.9 4.0 %gate_up.3 = (bf16[1152,4096]{1,0:T(8,128)(2,1)S(1)}, bf16[256,1152]{1,0:T(8,128)(2,1)S(1)}) custom-call(bf16[16,6144]{1,0:T(8,128)(2,1)S(1)} %get-tuple-element.38.after_ref.refs_0_, bf16[48,2560]{1,0:T(8,128)(2,1)S(1)} %get-tuple-element.92.refs_1_, bf16[16,6144]{1,0:T(8,128)(2,1)S(1)} %collective-permute-done.refs_2_, ...), custom_call_target="tpu_custom_call" | custom-call | flops 3019898880 | bytes 14155776 | tf_op jit(solution)/shard_map/gate_up/pallas_call | solution.py:182
  40.9 2.5 %down.2 = (bf16[1152,2048]{1,0:T(8,128)(2,1)S(1)}, bf16[128,3072]{1,0:T(8,128)(2,1)S(1)}, bf16[128,3072]{1,0:T(8,128)(2,1)S(1)}) custom-call(bf16[256,1152]{1,0:T(8,128)(2,1)S(1)} %get-tuple-element.59.hidden_ref, bf16[1152,4096]{1,0:T(8,128)(2,1)S(1)} %get-tuple-element.60.refs_0_, bf16[1152,6144]{1,0:T(8,128)(2,1)} %refs_1_.1), custom_call_target="tpu_custom_call" | custom-call | flops 1811939328 | bytes 9240576 | tf_op jit(solution)/shard_map/down/pallas_call | solution.py:235
  43.4 0.2 collective-permute-start.12
  43.6 2.8 %down.3 = (bf16[128,3072]{1,0:T(8,128)(2,1)S(1)}, bf16[128,3072]{1,0:T(8,128)(2,1)S(1)}) custom-call(bf16[256,1152]{1,0:T(8,128)(2,1)S(1)} %get-tuple-element.59.hidden_ref, bf16[1152,4096]{1,0:T(8,128)(2,1)S(1)} %get-tuple-element.60.refs_0_, bf16[1152,2048]{1,0:T(8,128)(2,1)S(1)} %get-tuple-element.63.refs_1_), custom_call_target="tpu_custom_call" | custom-call | flops 1811939328 | bytes 9240576 | tf_op jit(solution)/shard_map/down/pallas_call | solution.py:235
  46.4 0.4 collective-permute-start.13
  46.8 0.0 collective-permute-done.12
  46.8 0.0 copy-start
  46.8 0.0 copy-start.1
  46.8 0.0 copy-start.2
  46.9 0.2 add_convert_fusion.1
  47.1 1.2 %collective-permute-start.16 = (bf16[16,3072]{1,0:T(8,128)(2,1)S(1)}, bf16[16,3072]{1,0:T(8,128)(2,1)S(1)}, u32[]{:S(2)}, u32[]{:S(2)}) collective-permute-start(bf16[16,3072]{1,0:T(8,128)(2,1)S(1)} %get-tuple-element.81), channel_id=1, source_target_pairs={{0,2},{1,3},{2,0},{3,1},{4,6},{5,7},{6,4},{7,5},{8,10},{9,11},{10,... | collective-permute-start | bytes 294920 | tf_op jit(solution)/shard_map/ppermute | solution.py:302
  48.3 0.4 collective-permute-done.13
  48.8 0.2 add_convert_fusion
  49.0 1.2 %collective-permute-start.14 = (bf16[16,3072]{1,0:T(8,128)(2,1)S(1)}, bf16[16,3072]{1,0:T(8,128)(2,1)S(1)}, u32[]{:S(2)}, u32[]{:S(2)}) collective-permute-start(bf16[16,3072]{1,0:T(8,128)(2,1)S(1)} %get-tuple-element.75), channel_id=1, source_target_pairs={{0,2},{1,3},{2,0},{3,1},{4,6},{5,7},{6,4},{7,5},{8,10},{9,11},{10,... | collective-permute-start | bytes 294920 | tf_op jit(solution)/shard_map/ppermute | solution.py:302
  50.3 1.7 %collective-permute-done.16 = bf16[16,3072]{1,0:T(8,128)(2,1)S(1)} collective-permute-done((bf16[16,3072]{1,0:T(8,128)(2,1)S(1)}, bf16[16,3072]{1,0:T(8,128)(2,1)S(1)}, u32[]{:S(2)}, u32[]{:S(2)}) %collective-permute-start.16) | collective-permute-done | bytes 98336 | tf_op jit(solution)/shard_map/ppermute | solution.py:302
  52.0 0.4 collective-permute-start.21
  52.4 1.2 %collective-permute-start.17 = (bf16[16,6144]{1,0:T(8,128)(2,1)S(1)}, bf16[16,6144]{1,0:T(8,128)(2,1)S(1)}, u32[]{:S(2)}, u32[]{:S(2)}) collective-permute-start(bf16[16,6144]{1,0:T(8,128)(2,1)S(1)} %get-tuple-element.67), channel_id=1, source_target_pairs={{0,2},{1,3},{2,0},{3,1},{4,6},{5,7},{6,4},{7,5},{8,10},{9,11},{10,... | collective-permute-start | bytes 589832 | tf_op jit(solution)/shard_map/ppermute | solution.py:302
  53.6 0.6 collective-permute-done.14
  54.2 2.1 %collective-permute-start.19 = (bf16[16,3072]{1,0:T(8,128)(2,1)S(1)}, bf16[16,3072]{1,0:T(8,128)(2,1)S(1)}, u32[]{:S(2)}, u32[]{:S(2)}) collective-permute-start(bf16[16,3072]{1,0:T(8,128)(2,1)S(1)} %add_convert_fusion.5), channel_id=1, source_target_pairs={{0,8},{1,9},{2,10},{3,11},{4,12},{5,13},{6,14},{7,15},{8,0},{9,1},... | collective-permute-start | bytes 294920 | tf_op jit(solution)/shard_map/ppermute | solution.py:297
  56.3 0.9 %collective-permute-start.15 = (bf16[16,6144]{1,0:T(8,128)(2,1)S(1)}, bf16[16,6144]{1,0:T(8,128)(2,1)S(1)}, u32[]{:S(2)}, u32[]{:S(2)}) collective-permute-start(bf16[16,6144]{1,0:T(8,128)(2,1)S(1)} %get-tuple-element.66), channel_id=1, source_target_pairs={{0,2},{1,3},{2,0},{3,1},{4,6},{5,7},{6,4},{7,5},{8,10},{9,11},{10,... | collective-permute-start | bytes 589832 | tf_op jit(solution)/shard_map/ppermute | solution.py:302
  57.1 2.1 %collective-permute-done.17 = bf16[16,6144]{1,0:T(8,128)(2,1)S(1)} collective-permute-done((bf16[16,6144]{1,0:T(8,128)(2,1)S(1)}, bf16[16,6144]{1,0:T(8,128)(2,1)S(1)}, u32[]{:S(2)}, u32[]{:S(2)}) %collective-permute-start.17) | collective-permute-done | bytes 196640 | tf_op jit(solution)/shard_map/ppermute | solution.py:302
  59.3 0.1 add_convert_fusion.2
  59.3 2.6 %collective-permute-done.21.refs_2_ = bf16[16,3072]{1,0:T(8,128)(2,1)S(1)} collective-permute-done((bf16[16,3072]{1,0:T(8,128)(2,1)S(1)}, bf16[16,3072]{1,0:T(8,128)(2,1)S(1)}, u32[]{:S(2)}, u32[]{:S(2)}) %collective-permute-start.21) | collective-permute-done | bytes 98336 | tf_op jit(solution)/shard_map/ppermute | solution.py:297
  62.0 1.1 %collective-permute-start.22 = (bf16[16,6144]{1,0:T(8,128)(2,1)S(1)}, bf16[16,6144]{1,0:T(8,128)(2,1)S(1)}, u32[]{:S(2)}, u32[]{:S(2)}) collective-permute-start(bf16[16,6144]{1,0:T(8,128)(2,1)S(1)} %add_convert_fusion.2), channel_id=1, source_target_pairs={{0,4},{1,5},{2,6},{3,7},{4,8},{5,9},{6,10},{7,11},{8,12},{9,13},{1... | collective-permute-start | bytes 589832 | tf_op jit(solution)/shard_map/ppermute | solution.py:297
  63.0 0.0 collective-permute-done.15
  63.1 2.3 %collective-permute-done.19.refs_3_ = bf16[16,3072]{1,0:T(8,128)(2,1)S(1)} collective-permute-done((bf16[16,3072]{1,0:T(8,128)(2,1)S(1)}, bf16[16,3072]{1,0:T(8,128)(2,1)S(1)}, u32[]{:S(2)}, u32[]{:S(2)}) %collective-permute-start.19) | collective-permute-done | bytes 98336 | tf_op jit(solution)/shard_map/ppermute | solution.py:297
  65.4 1.2 %collective-permute-start.18 = (bf16[16,6144]{1,0:T(8,128)(2,1)S(1)}, bf16[16,6144]{1,0:T(8,128)(2,1)S(1)}, u32[]{:S(2)}, u32[]{:S(2)}) collective-permute-start(bf16[16,6144]{1,0:T(8,128)(2,1)S(1)} %pad_maximum_fusion), channel_id=1, source_target_pairs={{0,2},{1,3},{2,0},{3,1},{4,6},{5,7},{6,4},{7,5},{8,10},{9,11},{10,... | collective-permute-start | bytes 589832 | tf_op jit(solution)/shard_map/ppermute | solution.py:302
  66.6 2.6 %collective-permute-start.20 = (bf16[16,6144]{1,0:T(8,128)(2,1)S(1)}, bf16[16,6144]{1,0:T(8,128)(2,1)S(1)}, u32[]{:S(2)}, u32[]{:S(2)}) collective-permute-start(bf16[16,6144]{1,0:T(8,128)(2,1)S(1)} %add_convert_fusion.3), channel_id=1, source_target_pairs={{0,12},{1,13},{2,14},{3,15},{4,0},{5,1},{6,2},{7,3},{8,4},{9,5},{1... | collective-permute-start | bytes 589832 | tf_op jit(solution)/shard_map/ppermute | solution.py:297
  69.2 2.3 %collective-permute-done.22.last = bf16[16,6144]{1,0:T(8,128)(2,1)S(1)} collective-permute-done((bf16[16,6144]{1,0:T(8,128)(2,1)S(1)}, bf16[16,6144]{1,0:T(8,128)(2,1)S(1)}, u32[]{:S(2)}, u32[]{:S(2)}) %collective-permute-start.22) | collective-permute-done | bytes 196640 | tf_op jit(solution)/shard_map/ppermute | solution.py:297
  71.5 0.0 collective-permute-done.18.arrived
  71.6 2.5 %collective-permute-done.20.near = bf16[16,6144]{1,0:T(8,128)(2,1)S(1)} collective-permute-done((bf16[16,6144]{1,0:T(8,128)(2,1)S(1)}, bf16[16,6144]{1,0:T(8,128)(2,1)S(1)}, u32[]{:S(2)}, u32[]{:S(2)}) %collective-permute-start.20) | collective-permute-done | bytes 196640 | tf_op jit(solution)/shard_map/ppermute | solution.py:297
  74.1 0.0 copy-done
  74.1 0.0 copy-done.1
  74.1 0.0 copy-done.2
  74.1 1.3 %mix.1 = bf16[24,6144]{1,0:T(8,128)(2,1)} custom-call(s32[2,24]{1,0:T(2,128)S(1)} %bitcast.4, f32[2,24]{1,0:T(2,128)S(1)} %bitcast.5, bf16[24,6144]{1,0:T(8,128)(2,1)S(1)} %copy-done, bf16[16,6144]{1,0:T(8,128)(2,1)S(1)} %collective-permute-done.18.arrived, bf16[16,6144]{1,0:T(8,128)(2,1)S(1)} %collective-permute-done.20.near, ...), custom_call_target="tpu_custom_call" | custom-call | tf_op jit(solution)/shard_map/mix/pallas_call | solution.py:276
  (19 shorter events, 0.4 us)
Async XLA Ops:
  1.5 15.5 %collective-permute-start.1 = (bf16[16,3584]{1,0:T(8,128)(2,1)S(1)}, bf16[16,3584]{1,0:T(8,128)(2,1)S(1)}, u32[]{:S(2)}, u32[]{:S(2)}) collective-permute-start(bf16[16,3584]{1,0:T(8,128)(2,1)S(1)} %get-tuple-element.45), channel_id=1, source_target_pairs={{0,4},{1,5},{2,6},{3,7},{4,8},{5,9},{6,10},{7,11},{8,12},{9,13},{1... | collective-permute-start | bytes 344072 | tf_op jit(solution)/shard_map/ppermute | solution.py:297
  4.6 12.4 %collective-permute-start.2 = (bf16[16,3584]{1,0:T(8,128)(2,1)S(1)}, bf16[16,3584]{1,0:T(8,128)(2,1)S(1)}, u32[]{:S(2)}, u32[]{:S(2)}) collective-permute-start(bf16[16,3584]{1,0:T(8,128)(2,1)S(1)} %get-tuple-element.46), channel_id=1, source_target_pairs={{0,8},{1,9},{2,10},{3,11},{4,12},{5,13},{6,14},{7,15},{8,0},{9,1},... | collective-permute-start | bytes 344072 | tf_op jit(solution)/shard_map/ppermute | solution.py:297
  7.2 9.9 %collective-permute-start.3 = (bf16[16,3584]{1,0:T(8,128)(2,1)S(1)}, bf16[16,3584]{1,0:T(8,128)(2,1)S(1)}, u32[]{:S(2)}, u32[]{:S(2)}) collective-permute-start(bf16[16,3584]{1,0:T(8,128)(2,1)S(1)} %get-tuple-element.47), channel_id=1, source_target_pairs={{0,12},{1,13},{2,14},{3,15},{4,0},{5,1},{6,2},{7,3},{8,4},{9,5},{1... | collective-permute-start | bytes 344072 | tf_op jit(solution)/shard_map/ppermute | solution.py:297
  8.5 9.1 %collective-permute-start = (bf16[16,6144]{1,0:T(8,128)(2,1)S(1)}, bf16[16,6144]{1,0:T(8,128)(2,1)S(1)}, u32[]{:S(2)}, u32[]{:S(2)}) collective-permute-start(bf16[16,6144]{1,0:T(8,128)(2,1)S(1)} %get-tuple-element.38.after_ref.refs_0_), channel_id=1, source_target_pairs={{0,2},{1,3},{2,0},{3,1},{4,6},{5,7},{6,4},{7,5},{8,10},{9,11},{10,... | collective-permute-start | bytes 589832 | tf_op jit(solution)/shard_map/ppermute | solution.py:302
  17.1 9.7 %collective-permute-start.8 = (bf16[48,3584]{1,0:T(8,128)(2,1)S(1)}, bf16[48,3584]{1,0:T(8,128)(2,1)S(1)}, u32[]{:S(2)}, u32[]{:S(2)}) collective-permute-start(bf16[48,3584]{1,0:T(8,128)(2,1)S(1)} %get-tuple-element.51.refs_3_.refs_1_), channel_id=1, source_target_pairs={{0,2},{1,3},{2,0},{3,1},{4,6},{5,7},{6,4},{7,5},{8,10},{9,11},{10,... | collective-permute-start | bytes 1032200 | tf_op jit(solution)/shard_map/ppermute | solution.py:302
  17.6 6.8 %collective-permute-start.4 = (bf16[16,2560]{1,0:T(8,128)(2,1)S(1)}, bf16[16,2560]{1,0:T(8,128)(2,1)S(1)}, u32[]{:S(2)}, u32[]{:S(2)}) collective-permute-start(bf16[16,2560]{1,0:T(8,128)(2,1)S(1)} %get-tuple-element.48), channel_id=1, source_target_pairs={{0,4},{1,5},{2,6},{3,7},{4,8},{5,9},{6,10},{7,11},{8,12},{9,13},{1... | collective-permute-start | bytes 245768 | tf_op jit(solution)/shard_map/ppermute | solution.py:297
  19.4 7.4 %collective-permute-start.5 = (bf16[16,2560]{1,0:T(8,128)(2,1)S(1)}, bf16[16,2560]{1,0:T(8,128)(2,1)S(1)}, u32[]{:S(2)}, u32[]{:S(2)}) collective-permute-start(bf16[16,2560]{1,0:T(8,128)(2,1)S(1)} %get-tuple-element.49), channel_id=1, source_target_pairs={{0,8},{1,9},{2,10},{3,11},{4,12},{5,13},{6,14},{7,15},{8,0},{9,1},... | collective-permute-start | bytes 245768 | tf_op jit(solution)/shard_map/ppermute | solution.py:297
  21.0 5.9 %collective-permute-start.6 = (bf16[16,2560]{1,0:T(8,128)(2,1)S(1)}, bf16[16,2560]{1,0:T(8,128)(2,1)S(1)}, u32[]{:S(2)}, u32[]{:S(2)}) collective-permute-start(bf16[16,2560]{1,0:T(8,128)(2,1)S(1)} %get-tuple-element.50), channel_id=1, source_target_pairs={{0,12},{1,13},{2,14},{3,15},{4,0},{5,1},{6,2},{7,3},{8,4},{9,5},{1... | collective-permute-start | bytes 245768 | tf_op jit(solution)/shard_map/ppermute | solution.py:297
  26.8 2.5 %collective-permute-start.9 = (bf16[128,3584]{1,0:T(8,128)(2,1)S(1)}, bf16[128,3584]{1,0:T(8,128)(2,1)S(1)}, u32[]{:S(2)}, u32[]{:S(2)}) collective-permute-start(bf16[128,3584]{1,0:T(8,128)(2,1)S(1)} %constant_dynamic-update-slice_fusion.6), channel_id=1, source_target_pairs={{0,1},{1,0},{2,3},{3,2},{4,5},{5,4},{6,7},{7,6},{8,9},{9,8},{10,11... | collective-permute-start | bytes 2752520 | tf_op jit(solution)/shard_map/ppermute | solution.py:302
  26.9 8.4 %collective-permute-start.7 = (bf16[48,2560]{1,0:T(8,128)(2,1)S(1)}, bf16[48,2560]{1,0:T(8,128)(2,1)S(1)}, u32[]{:S(2)}, u32[]{:S(2)}) collective-permute-start(bf16[48,2560]{1,0:T(8,128)(2,1)S(1)} %get-tuple-element.92.refs_1_), channel_id=1, source_target_pairs={{0,2},{1,3},{2,0},{3,1},{4,6},{5,7},{6,4},{7,5},{8,10},{9,11},{10,... | collective-permute-start | bytes 737288 | tf_op jit(solution)/shard_map/ppermute | solution.py:302
  28.2 7.2 %collective-permute-start.10 = (bf16[80,2560]{1,0:T(8,128)(2,1)S(1)}, bf16[80,2560]{1,0:T(8,128)(2,1)S(1)}, u32[]{:S(2)}, u32[]{:S(2)}) collective-permute-start(bf16[80,2560]{1,0:T(8,128)(2,1)S(1)} %slice_dynamic-update-slice_fusion.2), channel_id=1, source_target_pairs={{0,1},{1,0},{2,3},{3,2},{4,5},{5,4},{6,7},{7,6},{8,9},{9,8},{10,11... | collective-permute-start | bytes 1228808 | tf_op jit(solution)/shard_map/ppermute | solution.py:302
  35.4 1.5 %collective-permute-start.11 = (bf16[48,2560]{1,0:T(8,128)(2,1)S(1)}, bf16[48,2560]{1,0:T(8,128)(2,1)S(1)}, u32[]{:S(2)}, u32[]{:S(2)}) collective-permute-start(bf16[48,2560]{1,0:T(8,128)(2,1)S(1)} %collective-permute-done.7.refs_3_), channel_id=1, source_target_pairs={{0,1},{1,0},{2,3},{3,2},{4,5},{5,4},{6,7},{7,6},{8,9},{9,8},{10,11... | collective-permute-start | bytes 737288 | tf_op jit(solution)/shard_map/ppermute | solution.py:302
  43.4 3.4 %collective-permute-start.12 = (bf16[128,3072]{1,0:T(8,128)(2,1)S(1)}, bf16[128,3072]{1,0:T(8,128)(2,1)S(1)}, u32[]{:S(2)}, u32[]{:S(2)}) collective-permute-start(bf16[128,3072]{1,0:T(8,128)(2,1)S(1)} %get-tuple-element.62), channel_id=1, source_target_pairs={{0,1},{1,0},{2,3},{3,2},{4,5},{5,4},{6,7},{7,6},{8,9},{9,8},{10,11... | collective-permute-start | bytes 2359304 | tf_op jit(solution)/shard_map/ppermute | solution.py:302
  46.4 2.4 %collective-permute-start.13 = (bf16[128,3072]{1,0:T(8,128)(2,1)S(1)}, bf16[128,3072]{1,0:T(8,128)(2,1)S(1)}, u32[]{:S(2)}, u32[]{:S(2)}) collective-permute-start(bf16[128,3072]{1,0:T(8,128)(2,1)S(1)} %get-tuple-element.65), channel_id=1, source_target_pairs={{0,1},{1,0},{2,3},{3,2},{4,5},{5,4},{6,7},{7,6},{8,9},{9,8},{10,11... | collective-permute-start | bytes 2359304 | tf_op jit(solution)/shard_map/ppermute | solution.py:302
  46.8 27.3 %copy-start = (bf16[24,6144]{1,0:T(8,128)(2,1)S(1)}, bf16[24,6144]{1,0:T(8,128)(2,1)}, u32[]{:S(2)}) copy-start(bf16[24,6144]{1,0:T(8,128)(2,1)} %act_ref.3) | copy-start | bytes 884740
  46.8 27.3 %copy-start.1 = (s32[24,2]{0,1:T(2,128)S(1)}, s32[24,2]{0,1:T(2,128)}, u32[]{:S(2)}) copy-start(s32[24,2]{0,1:T(2,128)} %param.8) | copy-start | bytes 580
  46.8 27.3 %copy-start.2 = (f32[24,2]{0,1:T(2,128)S(1)}, f32[24,2]{0,1:T(2,128)}, u32[]{:S(2)}) copy-start(f32[24,2]{0,1:T(2,128)} %param.9) | copy-start | bytes 580
  47.1 4.9 %collective-permute-start.16 = (bf16[16,3072]{1,0:T(8,128)(2,1)S(1)}, bf16[16,3072]{1,0:T(8,128)(2,1)S(1)}, u32[]{:S(2)}, u32[]{:S(2)}) collective-permute-start(bf16[16,3072]{1,0:T(8,128)(2,1)S(1)} %get-tuple-element.81), channel_id=1, source_target_pairs={{0,2},{1,3},{2,0},{3,1},{4,6},{5,7},{6,4},{7,5},{8,10},{9,11},{10,... | collective-permute-start | bytes 294920 | tf_op jit(solution)/shard_map/ppermute | solution.py:302
  49.0 5.1 %collective-permute-start.14 = (bf16[16,3072]{1,0:T(8,128)(2,1)S(1)}, bf16[16,3072]{1,0:T(8,128)(2,1)S(1)}, u32[]{:S(2)}, u32[]{:S(2)}) collective-permute-start(bf16[16,3072]{1,0:T(8,128)(2,1)S(1)} %get-tuple-element.75), channel_id=1, source_target_pairs={{0,2},{1,3},{2,0},{3,1},{4,6},{5,7},{6,4},{7,5},{8,10},{9,11},{10,... | collective-permute-start | bytes 294920 | tf_op jit(solution)/shard_map/ppermute | solution.py:302
  52.0 9.9 %collective-permute-start.21 = (bf16[16,3072]{1,0:T(8,128)(2,1)S(1)}, bf16[16,3072]{1,0:T(8,128)(2,1)S(1)}, u32[]{:S(2)}, u32[]{:S(2)}) collective-permute-start(bf16[16,3072]{1,0:T(8,128)(2,1)S(1)} %add_convert_fusion.4), channel_id=1, source_target_pairs={{0,8},{1,9},{2,10},{3,11},{4,12},{5,13},{6,14},{7,15},{8,0},{9,1},... | collective-permute-start | bytes 294920 | tf_op jit(solution)/shard_map/ppermute | solution.py:297
  52.4 6.9 %collective-permute-start.17 = (bf16[16,6144]{1,0:T(8,128)(2,1)S(1)}, bf16[16,6144]{1,0:T(8,128)(2,1)S(1)}, u32[]{:S(2)}, u32[]{:S(2)}) collective-permute-start(bf16[16,6144]{1,0:T(8,128)(2,1)S(1)} %get-tuple-element.67), channel_id=1, source_target_pairs={{0,2},{1,3},{2,0},{3,1},{4,6},{5,7},{6,4},{7,5},{8,10},{9,11},{10,... | collective-permute-start | bytes 589832 | tf_op jit(solution)/shard_map/ppermute | solution.py:302
  54.2 11.3 %collective-permute-start.19 = (bf16[16,3072]{1,0:T(8,128)(2,1)S(1)}, bf16[16,3072]{1,0:T(8,128)(2,1)S(1)}, u32[]{:S(2)}, u32[]{:S(2)}) collective-permute-start(bf16[16,3072]{1,0:T(8,128)(2,1)S(1)} %add_convert_fusion.5), channel_id=1, source_target_pairs={{0,8},{1,9},{2,10},{3,11},{4,12},{5,13},{6,14},{7,15},{8,0},{9,1},... | collective-permute-start | bytes 294920 | tf_op jit(solution)/shard_map/ppermute | solution.py:297
  56.3 6.8 %collective-permute-start.15 = (bf16[16,6144]{1,0:T(8,128)(2,1)S(1)}, bf16[16,6144]{1,0:T(8,128)(2,1)S(1)}, u32[]{:S(2)}, u32[]{:S(2)}) collective-permute-start(bf16[16,6144]{1,0:T(8,128)(2,1)S(1)} %get-tuple-element.66), channel_id=1, source_target_pairs={{0,2},{1,3},{2,0},{3,1},{4,6},{5,7},{6,4},{7,5},{8,10},{9,11},{10,... | collective-permute-start | bytes 589832 | tf_op jit(solution)/shard_map/ppermute | solution.py:302
  62.0 9.6 %collective-permute-start.22 = (bf16[16,6144]{1,0:T(8,128)(2,1)S(1)}, bf16[16,6144]{1,0:T(8,128)(2,1)S(1)}, u32[]{:S(2)}, u32[]{:S(2)}) collective-permute-start(bf16[16,6144]{1,0:T(8,128)(2,1)S(1)} %add_convert_fusion.2), channel_id=1, source_target_pairs={{0,4},{1,5},{2,6},{3,7},{4,8},{5,9},{6,10},{7,11},{8,12},{9,13},{1... | collective-permute-start | bytes 589832 | tf_op jit(solution)/shard_map/ppermute | solution.py:297
  65.4 6.1 %collective-permute-start.18 = (bf16[16,6144]{1,0:T(8,128)(2,1)S(1)}, bf16[16,6144]{1,0:T(8,128)(2,1)S(1)}, u32[]{:S(2)}, u32[]{:S(2)}) collective-permute-start(bf16[16,6144]{1,0:T(8,128)(2,1)S(1)} %pad_maximum_fusion), channel_id=1, source_target_pairs={{0,2},{1,3},{2,0},{3,1},{4,6},{5,7},{6,4},{7,5},{8,10},{9,11},{10,... | collective-permute-start | bytes 589832 | tf_op jit(solution)/shard_map/ppermute | solution.py:302
  66.6 7.5 %collective-permute-start.20 = (bf16[16,6144]{1,0:T(8,128)(2,1)S(1)}, bf16[16,6144]{1,0:T(8,128)(2,1)S(1)}, u32[]{:S(2)}, u32[]{:S(2)}) collective-permute-start(bf16[16,6144]{1,0:T(8,128)(2,1)S(1)} %add_convert_fusion.3), channel_id=1, source_target_pairs={{0,12},{1,13},{2,14},{3,15},{4,0},{5,1},{6,2},{7,3},{8,4},{9,5},{1... | collective-permute-start | bytes 589832 | tf_op jit(solution)/shard_map/ppermute | solution.py:297

commit v15 on v14

--- a/solution.py
+++ b/solution.py
@@ -279,6 +279,23 @@
         compiler_params=LIMIT,
         name="mix",
     )(ids, logits, activations, *pieces)
+
+
+def fold_kernel(mine_ref, arrived_ref, out_ref):
+    total = mine_ref[...].astype(jnp.float32) + arrived_ref[...].astype(jnp.float32)
+    out_ref[...] = total.astype(jnp.bfloat16)
+
+
+def fold(mine, arrived):
+    return pl.pallas_call(
+        fold_kernel,
+        in_specs=[VMEM, VMEM],
+        out_specs=VMEM,
+        out_shape=jax.ShapeDtypeStruct(mine.shape, mine.dtype),
+        compiler_params=LIMIT,
+        cost_estimate=pl.CostEstimate(flops=0, bytes_accessed=16 * MIB, transcendentals=0),
+        name="fold",
+    )(mine, arrived)
 
 
 def added(mine, arrived):
@@ -359,11 +376,13 @@
     middle = [shift(added(h[place[2]], x), -2) for h, x in zip(held, crossed)]
     mine = [jnp.concatenate([h[j] for h in held], axis=1) for j in range(2 * EXPERTS)]
     back = {}
-    back[1] = swap(after(mine[EXPERTS + place[1]], crossed[1]), far)
     back[3] = swap(after(mine[EXPERTS + place[3]], crossed[0]), far)
-    back[0] = swap(after(mine[EXPERTS], back[1], back[3]), far)
-    near = shift(after(added(mine[place[1]], back[1]), middle[1]), -1)
-    last = shift(after(added(mine[place[3]], back[3]), middle[0]), -3)
+    back[1] = swap(after(mine[EXPERTS + place[1]], back[3]), far)
+    near_rows = fold(mine[place[1]], back[1])
+    last_rows = fold(mine[place[3]], back[3])
+    back[0] = swap(after(mine[EXPERTS], last_rows, *middle), far)
+    near = shift(near_rows, -1)
+    last = shift(last_rows, -3)
     arrived = back[0]
     pieces = [arrived, near, last, *[h[0] for h in held], *middle]
     return mix(group, ids, route_logits.T, activations, pieces)

time: 75.6 us -> 76.6 us (1.013)
  waiting for transfers between devices: 22.6 us -> 24 us
    ppermute x13, waiting for transfers between devices: 7.87 us -> 11.7 us  [swap(): return lax.ppermute(x, 'expert', [(i, i ^ bit) for i in range(devices)])]
    ppermute x10, waiting for transfers between devices: 14.7 us -> 12.3 us  [shift(): lax.ppermute(x, 'expert', [(i, (i + s * group) % devices) for i in range(...]
    ppermute x10, starting transfers between devices: 17.4 us -> 16.2 us  [shift(): lax.ppermute(x, 'expert', [(i, (i + s * group) % devices) for i in range(...]
  transfers between devices with their start and end apart: 23 -> 23, of which waited for: 13 -> 12; matrix products, arithmetic and copies ran while one was open for 1% -> 1% of each run, Pallas kernels for 20% -> 20%
where the time goes in v15:
time: 76.6 us; the launch traced here: 76.4 us
  starting transfers between devices  26.8 us (35%)
  Pallas kernels  24.6 us (32%)
  waiting for transfers between devices  24 us (31%)
    ppermute x10, starting transfers between devices, shift(): lax.ppermute(x, 'expert', [(i, (i + s * group) % devices) for i in range(...  16.2 us
    ppermute x10, waiting for transfers between devices, shift(): lax.ppermute(x, 'expert', [(i, (i + s * group) % devices) for i in range(...  12.3 us
    ppermute x13, waiting for transfers between devices, swap(): return lax.ppermute(x, 'expert', [(i, i ^ bit) for i in range(devices)])  11.7 us
    ppermute x13, starting transfers between devices, swap(): return lax.ppermute(x, 'expert', [(i, i ^ bit) for i in range(devices)])  10.5 us
    pallas_call x2, Pallas kernels, gate_up(): pl.pallas_call(functools.partial(gate_up_kernel, len(pieces), len(later),...  9.5 us
    pallas_call x2, Pallas kernels, fetch(): pl.pallas_call(functools.partial(fetch_kernel, at), in_specs=[ANY, ANY],...  6.88 us
    pallas_call x2, Pallas kernels, down(): pl.pallas_call(functools.partial(down_kernel, ahead, segments), in_specs=...  5.29 us
  transfers between devices with their start and end apart: 23, of which 12 were waited for; matrix products, arithmetic and copies ran while one was open for 1% of the time, Pallas kernels for 20%

profile of v15, /device:TPU:0, one launch (start us, length us, event | category | flops | bytes accessed | tf_op | source)
XLA Modules:
  0.0 76.4 jit_solution(285457389703145689)
XLA Ops:
  0.0 1.5 %norm_and_pack.1 = (bf16[16,6144]{1,0:T(8,128)(2,1)S(1)}, bf16[16,3584]{1,0:T(8,128)(2,1)S(1)}, bf16[16,3584]{1,0:T(8,128)(2,1)S(1)}, bf16[16,3584]{1,0:T(8,128)...) custom-call(s32[2,24]{1,0:T(2,128)} %bitcast.3, ...), custom_call_target="tpu_custom_call" | custom-call | tf_op jit(solution)/shard_map/norm_and_pack/pallas_call | solution.py:67
  1.5 3.1 %collective-permute-start.1 = (bf16[16,3584]{1,0:T(8,128)(2,1)S(1)}, bf16[16,3584]{1,0:T(8,128)(2,1)S(1)}, u32[]{:S(2)}, u32[]{:S(2)}) collective-permute-start(bf16[16,3584]{1,0:T(8,128)(2,1)S(1)} %get-tuple-element.43), channel_id=1, source_target_pairs={{0,4},{1,5},{2,6},{3,7},{4,8},{5,9},{6,10},{7,11},{8,12},{9,13},{1... | collective-permute-start | bytes 344072 | tf_op jit(solution)/shard_map/ppermute | solution.py:314
  4.6 2.6 %collective-permute-start.2 = (bf16[16,3584]{1,0:T(8,128)(2,1)S(1)}, bf16[16,3584]{1,0:T(8,128)(2,1)S(1)}, u32[]{:S(2)}, u32[]{:S(2)}) collective-permute-start(bf16[16,3584]{1,0:T(8,128)(2,1)S(1)} %get-tuple-element.44), channel_id=1, source_target_pairs={{0,8},{1,9},{2,10},{3,11},{4,12},{5,13},{6,14},{7,15},{8,0},{9,1},... | collective-permute-start | bytes 344072 | tf_op jit(solution)/shard_map/ppermute | solution.py:314
  7.2 1.3 %collective-permute-start.3 = (bf16[16,3584]{1,0:T(8,128)(2,1)S(1)}, bf16[16,3584]{1,0:T(8,128)(2,1)S(1)}, u32[]{:S(2)}, u32[]{:S(2)}) collective-permute-start(bf16[16,3584]{1,0:T(8,128)(2,1)S(1)} %get-tuple-element.45), channel_id=1, source_target_pairs={{0,12},{1,13},{2,14},{3,15},{4,0},{5,1},{6,2},{7,3},{8,4},{9,5},{1... | collective-permute-start | bytes 344072 | tf_op jit(solution)/shard_map/ppermute | solution.py:314
  8.5 1.5 %collective-permute-start = (bf16[16,6144]{1,0:T(8,128)(2,1)S(1)}, bf16[16,6144]{1,0:T(8,128)(2,1)S(1)}, u32[]{:S(2)}, u32[]{:S(2)}) collective-permute-start(bf16[16,6144]{1,0:T(8,128)(2,1)S(1)} %get-tuple-element.36.after_ref.refs_0_), channel_id=1, source_target_pairs={{0,2},{1,3},{2,0},{3,1},{4,6},{5,7},{6,4},{7,5},{8,10},{9,11},{10,... | collective-permute-start | bytes 589832 | tf_op jit(solution)/shard_map/ppermute | solution.py:319
  10.1 3.4 %fetch.3.refs_6_ = bf16[1152,3584]{1,0:T(8,128)(2,1)S(1)} custom-call(bf16[1152,6144]{1,0:T(8,128)(2,1)} %refs_8_.2, bf16[16,6144]{1,0:T(8,128)(2,1)S(1)} %get-tuple-element.36.after_ref.refs_0_), custom_call_target="tpu_custom_call" | custom-call | bytes 16515072 | tf_op jit(solution)/shard_map/fetch/pallas_call | solution.py:100
  13.5 3.4 %fetch.2.refs_5_ = bf16[1152,3584]{1,0:T(8,128)(2,1)S(1)} custom-call(bf16[1152,6144]{1,0:T(8,128)(2,1)} %refs_7_.1, bf16[16,6144]{1,0:T(8,128)(2,1)S(1)} %get-tuple-element.36.after_ref.refs_0_), custom_call_target="tpu_custom_call" | custom-call | bytes 16515072 | tf_op jit(solution)/shard_map/fetch/pallas_call | solution.py:100
  16.9 0.0 collective-permute-done.1
  17.0 0.0 collective-permute-done.2
  17.0 0.0 collective-permute-done.3
  17.1 0.6 collective-permute-start.8
  17.6 0.0 collective-permute-done.refs_2_
  17.6 1.8 %collective-permute-start.4 = (bf16[16,2560]{1,0:T(8,128)(2,1)S(1)}, bf16[16,2560]{1,0:T(8,128)(2,1)S(1)}, u32[]{:S(2)}, u32[]{:S(2)}) collective-permute-start(bf16[16,2560]{1,0:T(8,128)(2,1)S(1)} %get-tuple-element.46), channel_id=1, source_target_pairs={{0,4},{1,5},{2,6},{3,7},{4,8},{5,9},{6,10},{7,11},{8,12},{9,13},{1... | collective-permute-start | bytes 245768 | tf_op jit(solution)/shard_map/ppermute | solution.py:314
  19.4 1.6 %collective-permute-start.5 = (bf16[16,2560]{1,0:T(8,128)(2,1)S(1)}, bf16[16,2560]{1,0:T(8,128)(2,1)S(1)}, u32[]{:S(2)}, u32[]{:S(2)}) collective-permute-start(bf16[16,2560]{1,0:T(8,128)(2,1)S(1)} %get-tuple-element.47), channel_id=1, source_target_pairs={{0,8},{1,9},{2,10},{3,11},{4,12},{5,13},{6,14},{7,15},{8,0},{9,1},... | collective-permute-start | bytes 245768 | tf_op jit(solution)/shard_map/ppermute | solution.py:314
  21.0 0.8 %collective-permute-start.6 = (bf16[16,2560]{1,0:T(8,128)(2,1)S(1)}, bf16[16,2560]{1,0:T(8,128)(2,1)S(1)}, u32[]{:S(2)}, u32[]{:S(2)}) collective-permute-start(bf16[16,2560]{1,0:T(8,128)(2,1)S(1)} %get-tuple-element.48), channel_id=1, source_target_pairs={{0,12},{1,13},{2,14},{3,15},{4,0},{5,1},{6,2},{7,3},{8,4},{9,5},{1... | collective-permute-start | bytes 245768 | tf_op jit(solution)/shard_map/ppermute | solution.py:314
  21.9 2.6 %collective-permute-done.4 = bf16[16,2560]{1,0:T(8,128)(2,1)S(1)} collective-permute-done((bf16[16,2560]{1,0:T(8,128)(2,1)S(1)}, bf16[16,2560]{1,0:T(8,128)(2,1)S(1)}, u32[]{:S(2)}, u32[]{:S(2)}) %collective-permute-start.4) | collective-permute-done | bytes 81952 | tf_op jit(solution)/shard_map/ppermute | solution.py:314
  24.4 2.3 %collective-permute-done.5 = bf16[16,2560]{1,0:T(8,128)(2,1)S(1)} collective-permute-done((bf16[16,2560]{1,0:T(8,128)(2,1)S(1)}, bf16[16,2560]{1,0:T(8,128)(2,1)S(1)}, u32[]{:S(2)}, u32[]{:S(2)}) %collective-permute-start.5) | collective-permute-done | bytes 81952 | tf_op jit(solution)/shard_map/ppermute | solution.py:314
  26.8 0.0 collective-permute-done.8.refs_3_
  26.8 0.1 collective-permute-start.9
  26.9 0.0 collective-permute-done.6
  26.9 1.2 %collective-permute-start.7 = (bf16[48,2560]{1,0:T(8,128)(2,1)S(1)}, bf16[48,2560]{1,0:T(8,128)(2,1)S(1)}, u32[]{:S(2)}, u32[]{:S(2)}) collective-permute-start(bf16[48,2560]{1,0:T(8,128)(2,1)S(1)} %get-tuple-element.88.refs_1_), channel_id=1, source_target_pairs={{0,2},{1,3},{2,0},{3,1},{4,6},{5,7},{6,4},{7,5},{8,10},{9,11},{10,... | collective-permute-start | bytes 737288 | tf_op jit(solution)/shard_map/ppermute | solution.py:319
  28.2 0.2 collective-permute-start.10
  28.4 1.0 %collective-permute-done.9.refs_4_ = bf16[128,3584]{1,0:T(8,128)(2,1)S(1)} collective-permute-done((bf16[128,3584]{1,0:T(8,128)(2,1)S(1)}, bf16[128,3584]{1,0:T(8,128)(2,1)S(1)}, u32[]{:S(2)}, u32[]{:S(2)}) %collective-permute-start.9) | collective-permute-done | bytes 917536 | tf_op jit(solution)/shard_map/ppermute | solution.py:319
  29.4 5.5 %gate_up.2 = (bf16[1152,2560]{1,0:T(8,128)(2,1)S(1)}, bf16[1152,2560]{1,0:T(8,128)(2,1)S(1)}, f32[1152,256]{1,0:T(8,128)S(1)}, f32[1152,256]{1,0:T(8,128)S(1)}) custom-call(bf16[16,6144]{1,0:T(8,128)(2,1)S(1)} %get-tuple-element.36.after_ref.refs_0_, bf16[48,3584]{1,0:T(8,128)(2,1)S(1)} %get-tuple-element.49.refs_3_.refs_1_, ...), custom_call_target="tpu_custom_call" | custom-call | flops 4227858432 | bytes 18874368 | tf_op jit(solution)/shard_map/gate_up/pallas_call | solution.py:182
  34.9 0.5 collective-permute-done.7.refs_3_
  35.4 0.0 collective-permute-start.11
  35.4 0.0 collective-permute-done.10.refs_4_
  35.4 1.5 %collective-permute-done.11.refs_5_ = bf16[48,2560]{1,0:T(8,128)(2,1)S(1)} collective-permute-done((bf16[48,2560]{1,0:T(8,128)(2,1)S(1)}, bf16[48,2560]{1,0:T(8,128)(2,1)S(1)}, u32[]{:S(2)}, u32[]{:S(2)}) %collective-permute-start.11) | collective-permute-done | bytes 245792 | tf_op jit(solution)/shard_map/ppermute | solution.py:319
  36.9 4.0 %gate_up.3 = (bf16[1152,4096]{1,0:T(8,128)(2,1)S(1)}, bf16[256,1152]{1,0:T(8,128)(2,1)S(1)}) custom-call(bf16[16,6144]{1,0:T(8,128)(2,1)S(1)} %get-tuple-element.36.after_ref.refs_0_, bf16[48,2560]{1,0:T(8,128)(2,1)S(1)} %get-tuple-element.88.refs_1_, bf16[16,6144]{1,0:T(8,128)(2,1)S(1)} %collective-permute-done.refs_2_, ...), custom_call_target="tpu_custom_call" | custom-call | flops 3019898880 | bytes 14155776 | tf_op jit(solution)/shard_map/gate_up/pallas_call | solution.py:182
  40.9 2.5 %down.2 = (bf16[1152,2048]{1,0:T(8,128)(2,1)S(1)}, bf16[128,3072]{1,0:T(8,128)(2,1)S(1)}, bf16[128,3072]{1,0:T(8,128)(2,1)S(1)}) custom-call(bf16[256,1152]{1,0:T(8,128)(2,1)S(1)} %get-tuple-element.57.hidden_ref, bf16[1152,4096]{1,0:T(8,128)(2,1)S(1)} %get-tuple-element.58.refs_0_, bf16[1152,6144]{1,0:T(8,128)(2,1)} %refs_1_.1), custom_call_target="tpu_custom_call" | custom-call | flops 1811939328 | bytes 9240576 | tf_op jit(solution)/shard_map/down/pallas_call | solution.py:235
  43.4 0.2 collective-permute-start.12
  43.6 2.8 %down.3 = (bf16[128,3072]{1,0:T(8,128)(2,1)S(1)}, bf16[128,3072]{1,0:T(8,128)(2,1)S(1)}) custom-call(bf16[256,1152]{1,0:T(8,128)(2,1)S(1)} %get-tuple-element.57.hidden_ref, bf16[1152,4096]{1,0:T(8,128)(2,1)S(1)} %get-tuple-element.58.refs_0_, bf16[1152,2048]{1,0:T(8,128)(2,1)S(1)} %get-tuple-element.61.refs_1_), custom_call_target="tpu_custom_call" | custom-call | flops 1811939328 | bytes 9240576 | tf_op jit(solution)/shard_map/down/pallas_call | solution.py:235
  46.4 0.4 collective-permute-start.13
  46.8 0.0 collective-permute-done.12
  46.8 0.2 add_convert_fusion.1
  47.0 0.0 copy-start
  47.0 0.0 copy-start.1
  47.1 0.0 copy-start.2
  47.1 1.2 %collective-permute-start.14 = (bf16[16,3072]{1,0:T(8,128)(2,1)S(1)}, bf16[16,3072]{1,0:T(8,128)(2,1)S(1)}, u32[]{:S(2)}, u32[]{:S(2)}) collective-permute-start(bf16[16,3072]{1,0:T(8,128)(2,1)S(1)} %get-tuple-element.77), channel_id=1, source_target_pairs={{0,2},{1,3},{2,0},{3,1},{4,6},{5,7},{6,4},{7,5},{8,10},{9,11},{10,... | collective-permute-start | bytes 294920 | tf_op jit(solution)/shard_map/ppermute | solution.py:319
  48.3 0.4 collective-permute-done.13
  48.8 0.2 add_convert_fusion
  49.0 1.2 %collective-permute-start.17 = (bf16[16,3072]{1,0:T(8,128)(2,1)S(1)}, bf16[16,3072]{1,0:T(8,128)(2,1)S(1)}, u32[]{:S(2)}, u32[]{:S(2)}) collective-permute-start(bf16[16,3072]{1,0:T(8,128)(2,1)S(1)} %get-tuple-element.70), channel_id=1, source_target_pairs={{0,2},{1,3},{2,0},{3,1},{4,6},{5,7},{6,4},{7,5},{8,10},{9,11},{10,... | collective-permute-start | bytes 294920 | tf_op jit(solution)/shard_map/ppermute | solution.py:319
  50.3 1.7 %collective-permute-done.14 = bf16[16,3072]{1,0:T(8,128)(2,1)S(1)} collective-permute-done((bf16[16,3072]{1,0:T(8,128)(2,1)S(1)}, bf16[16,3072]{1,0:T(8,128)(2,1)S(1)}, u32[]{:S(2)}, u32[]{:S(2)}) %collective-permute-start.14) | collective-permute-done | bytes 98336 | tf_op jit(solution)/shard_map/ppermute | solution.py:319
  52.1 0.4 collective-permute-start.16
  52.4 1.2 %collective-permute-start.15 = (bf16[16,6144]{1,0:T(8,128)(2,1)S(1)}, bf16[16,6144]{1,0:T(8,128)(2,1)S(1)}, u32[]{:S(2)}, u32[]{:S(2)}) collective-permute-start(bf16[16,6144]{1,0:T(8,128)(2,1)S(1)} %pad_maximum_fusion.2), channel_id=1, source_target_pairs={{0,2},{1,3},{2,0},{3,1},{4,6},{5,7},{6,4},{7,5},{8,10},{9,11},{10,... | collective-permute-start | bytes 589832 | tf_op jit(solution)/shard_map/ppermute | solution.py:319
  53.6 0.5 collective-permute-done.17
  54.2 2.1 %collective-permute-start.18 = (bf16[16,3072]{1,0:T(8,128)(2,1)S(1)}, bf16[16,3072]{1,0:T(8,128)(2,1)S(1)}, u32[]{:S(2)}, u32[]{:S(2)}) collective-permute-start(bf16[16,3072]{1,0:T(8,128)(2,1)S(1)} %add_convert_fusion.2), channel_id=1, source_target_pairs={{0,8},{1,9},{2,10},{3,11},{4,12},{5,13},{6,14},{7,15},{8,0},{9,1},... | collective-permute-start | bytes 294920 | tf_op jit(solution)/shard_map/ppermute | solution.py:314
  56.3 2.0 %collective-permute-done.15.arrived_ref = bf16[16,6144]{1,0:T(8,128)(2,1)S(1)} collective-permute-done((bf16[16,6144]{1,0:T(8,128)(2,1)S(1)}, bf16[16,6144]{1,0:T(8,128)(2,1)S(1)}, u32[]{:S(2)}, u32[]{:S(2)}) %collective-permute-start.15) | collective-permute-done | bytes 196640 | tf_op jit(solution)/shard_map/ppermute | solution.py:319
  58.4 1.2 %collective-permute-start.20 = (bf16[16,6144]{1,0:T(8,128)(2,1)S(1)}, bf16[16,6144]{1,0:T(8,128)(2,1)S(1)}, u32[]{:S(2)}, u32[]{:S(2)}) collective-permute-start(bf16[16,6144]{1,0:T(8,128)(2,1)S(1)} %pad_maximum_fusion.4), channel_id=1, source_target_pairs={{0,2},{1,3},{2,0},{3,1},{4,6},{5,7},{6,4},{7,5},{8,10},{9,11},{10,... | collective-permute-start | bytes 589832 | tf_op jit(solution)/shard_map/ppermute | solution.py:319
  59.5 0.1 fold.2
  59.6 2.5 %collective-permute-start.22 = (bf16[16,6144]{1,0:T(8,128)(2,1)S(1)}, bf16[16,6144]{1,0:T(8,128)(2,1)S(1)}, u32[]{:S(2)}, u32[]{:S(2)}) collective-permute-start(bf16[16,6144]{1,0:T(8,128)(2,1)S(1)} %fold.2), channel_id=1, source_target_pairs={{0,4},{1,5},{2,6},{3,7},{4,8},{5,9},{6,10},{7,11},{8,12},{9,13},{1... | collective-permute-start | bytes 589832 | tf_op jit(solution)/shard_map/ppermute | solution.py:314
  62.0 0.0 collective-permute-done.16.refs_2_
  62.0 5.8 %collective-permute-done.18.refs_3_ = bf16[16,3072]{1,0:T(8,128)(2,1)S(1)} collective-permute-done((bf16[16,3072]{1,0:T(8,128)(2,1)S(1)}, bf16[16,3072]{1,0:T(8,128)(2,1)S(1)}, u32[]{:S(2)}, u32[]{:S(2)}) %collective-permute-start.18) | collective-permute-done | bytes 98336 | tf_op jit(solution)/shard_map/ppermute | solution.py:314
  67.8 1.5 %collective-permute-start.19 = (bf16[16,6144]{1,0:T(8,128)(2,1)S(1)}, bf16[16,6144]{1,0:T(8,128)(2,1)S(1)}, u32[]{:S(2)}, u32[]{:S(2)}) collective-permute-start(bf16[16,6144]{1,0:T(8,128)(2,1)S(1)} %pad_maximum_fusion), channel_id=1, source_target_pairs={{0,2},{1,3},{2,0},{3,1},{4,6},{5,7},{6,4},{7,5},{8,10},{9,11},{10,... | collective-permute-start | bytes 589832 | tf_op jit(solution)/shard_map/ppermute | solution.py:319
  69.3 0.0 collective-permute-done.20.arrived_ref
  69.3 0.1 fold.3
  69.4 0.1 collective-permute-start.21
  69.5 4.1 %collective-permute-done.19.arrived = bf16[16,6144]{1,0:T(8,128)(2,1)S(1)} collective-permute-done((bf16[16,6144]{1,0:T(8,128)(2,1)S(1)}, bf16[16,6144]{1,0:T(8,128)(2,1)S(1)}, u32[]{:S(2)}, u32[]{:S(2)}) %collective-permute-start.19) | collective-permute-done | bytes 196640 | tf_op jit(solution)/shard_map/ppermute | solution.py:319
  73.5 0.0 collective-permute-done.22.last
  73.5 1.6 %collective-permute-done.21.near = bf16[16,6144]{1,0:T(8,128)(2,1)S(1)} collective-permute-done((bf16[16,6144]{1,0:T(8,128)(2,1)S(1)}, bf16[16,6144]{1,0:T(8,128)(2,1)S(1)}, u32[]{:S(2)}, u32[]{:S(2)}) %collective-permute-start.21) | collective-permute-done | bytes 196640 | tf_op jit(solution)/shard_map/ppermute | solution.py:314
  75.1 0.0 copy-done
  75.1 0.0 copy-done.1
  75.1 0.0 copy-done.2
  75.1 1.3 %mix.1 = bf16[24,6144]{1,0:T(8,128)(2,1)} custom-call(s32[2,24]{1,0:T(2,128)S(1)} %bitcast.4, f32[2,24]{1,0:T(2,128)S(1)} %bitcast.5, bf16[24,6144]{1,0:T(8,128)(2,1)S(1)} %copy-done, bf16[16,6144]{1,0:T(8,128)(2,1)S(1)} %collective-permute-done.19.arrived, bf16[16,6144]{1,0:T(8,128)(2,1)S(1)} %collective-permute-done.21.near, ...), custom_call_target="tpu_custom_call" | custom-call | tf_op jit(solution)/shard_map/mix/pallas_call | solution.py:276
  (21 shorter events, 0.4 us)
Async XLA Ops:
  1.5 15.5 %collective-permute-start.1 = (bf16[16,3584]{1,0:T(8,128)(2,1)S(1)}, bf16[16,3584]{1,0:T(8,128)(2,1)S(1)}, u32[]{:S(2)}, u32[]{:S(2)}) collective-permute-start(bf16[16,3584]{1,0:T(8,128)(2,1)S(1)} %get-tuple-element.43), channel_id=1, source_target_pairs={{0,4},{1,5},{2,6},{3,7},{4,8},{5,9},{6,10},{7,11},{8,12},{9,13},{1... | collective-permute-start | bytes 344072 | tf_op jit(solution)/shard_map/ppermute | solution.py:314
  4.6 12.4 %collective-permute-start.2 = (bf16[16,3584]{1,0:T(8,128)(2,1)S(1)}, bf16[16,3584]{1,0:T(8,128)(2,1)S(1)}, u32[]{:S(2)}, u32[]{:S(2)}) collective-permute-start(bf16[16,3584]{1,0:T(8,128)(2,1)S(1)} %get-tuple-element.44), channel_id=1, source_target_pairs={{0,8},{1,9},{2,10},{3,11},{4,12},{5,13},{6,14},{7,15},{8,0},{9,1},... | collective-permute-start | bytes 344072 | tf_op jit(solution)/shard_map/ppermute | solution.py:314
  7.2 9.9 %collective-permute-start.3 = (bf16[16,3584]{1,0:T(8,128)(2,1)S(1)}, bf16[16,3584]{1,0:T(8,128)(2,1)S(1)}, u32[]{:S(2)}, u32[]{:S(2)}) collective-permute-start(bf16[16,3584]{1,0:T(8,128)(2,1)S(1)} %get-tuple-element.45), channel_id=1, source_target_pairs={{0,12},{1,13},{2,14},{3,15},{4,0},{5,1},{6,2},{7,3},{8,4},{9,5},{1... | collective-permute-start | bytes 344072 | tf_op jit(solution)/shard_map/ppermute | solution.py:314
  8.5 9.1 %collective-permute-start = (bf16[16,6144]{1,0:T(8,128)(2,1)S(1)}, bf16[16,6144]{1,0:T(8,128)(2,1)S(1)}, u32[]{:S(2)}, u32[]{:S(2)}) collective-permute-start(bf16[16,6144]{1,0:T(8,128)(2,1)S(1)} %get-tuple-element.36.after_ref.refs_0_), channel_id=1, source_target_pairs={{0,2},{1,3},{2,0},{3,1},{4,6},{5,7},{6,4},{7,5},{8,10},{9,11},{10,... | collective-permute-start | bytes 589832 | tf_op jit(solution)/shard_map/ppermute | solution.py:319
  17.1 9.7 %collective-permute-start.8 = (bf16[48,3584]{1,0:T(8,128)(2,1)S(1)}, bf16[48,3584]{1,0:T(8,128)(2,1)S(1)}, u32[]{:S(2)}, u32[]{:S(2)}) collective-permute-start(bf16[48,3584]{1,0:T(8,128)(2,1)S(1)} %get-tuple-element.49.refs_3_.refs_1_), channel_id=1, source_target_pairs={{0,2},{1,3},{2,0},{3,1},{4,6},{5,7},{6,4},{7,5},{8,10},{9,11},{10,... | collective-permute-start | bytes 1032200 | tf_op jit(solution)/shard_map/ppermute | solution.py:319
  17.6 6.8 %collective-permute-start.4 = (bf16[16,2560]{1,0:T(8,128)(2,1)S(1)}, bf16[16,2560]{1,0:T(8,128)(2,1)S(1)}, u32[]{:S(2)}, u32[]{:S(2)}) collective-permute-start(bf16[16,2560]{1,0:T(8,128)(2,1)S(1)} %get-tuple-element.46), channel_id=1, source_target_pairs={{0,4},{1,5},{2,6},{3,7},{4,8},{5,9},{6,10},{7,11},{8,12},{9,13},{1... | collective-permute-start | bytes 245768 | tf_op jit(solution)/shard_map/ppermute | solution.py:314
  19.4 7.4 %collective-permute-start.5 = (bf16[16,2560]{1,0:T(8,128)(2,1)S(1)}, bf16[16,2560]{1,0:T(8,128)(2,1)S(1)}, u32[]{:S(2)}, u32[]{:S(2)}) collective-permute-start(bf16[16,2560]{1,0:T(8,128)(2,1)S(1)} %get-tuple-element.47), channel_id=1, source_target_pairs={{0,8},{1,9},{2,10},{3,11},{4,12},{5,13},{6,14},{7,15},{8,0},{9,1},... | collective-permute-start | bytes 245768 | tf_op jit(solution)/shard_map/ppermute | solution.py:314
  21.0 5.9 %collective-permute-start.6 = (bf16[16,2560]{1,0:T(8,128)(2,1)S(1)}, bf16[16,2560]{1,0:T(8,128)(2,1)S(1)}, u32[]{:S(2)}, u32[]{:S(2)}) collective-permute-start(bf16[16,2560]{1,0:T(8,128)(2,1)S(1)} %get-tuple-element.48), channel_id=1, source_target_pairs={{0,12},{1,13},{2,14},{3,15},{4,0},{5,1},{6,2},{7,3},{8,4},{9,5},{1... | collective-permute-start | bytes 245768 | tf_op jit(solution)/shard_map/ppermute | solution.py:314
  26.8 2.5 %collective-permute-start.9 = (bf16[128,3584]{1,0:T(8,128)(2,1)S(1)}, bf16[128,3584]{1,0:T(8,128)(2,1)S(1)}, u32[]{:S(2)}, u32[]{:S(2)}) collective-permute-start(bf16[128,3584]{1,0:T(8,128)(2,1)S(1)} %constant_dynamic-update-slice_fusion.6), channel_id=1, source_target_pairs={{0,1},{1,0},{2,3},{3,2},{4,5},{5,4},{6,7},{7,6},{8,9},{9,8},{10,11... | collective-permute-start | bytes 2752520 | tf_op jit(solution)/shard_map/ppermute | solution.py:319
  26.9 8.4 %collective-permute-start.7 = (bf16[48,2560]{1,0:T(8,128)(2,1)S(1)}, bf16[48,2560]{1,0:T(8,128)(2,1)S(1)}, u32[]{:S(2)}, u32[]{:S(2)}) collective-permute-start(bf16[48,2560]{1,0:T(8,128)(2,1)S(1)} %get-tuple-element.88.refs_1_), channel_id=1, source_target_pairs={{0,2},{1,3},{2,0},{3,1},{4,6},{5,7},{6,4},{7,5},{8,10},{9,11},{10,... | collective-permute-start | bytes 737288 | tf_op jit(solution)/shard_map/ppermute | solution.py:319
  28.2 7.2 %collective-permute-start.10 = (bf16[80,2560]{1,0:T(8,128)(2,1)S(1)}, bf16[80,2560]{1,0:T(8,128)(2,1)S(1)}, u32[]{:S(2)}, u32[]{:S(2)}) collective-permute-start(bf16[80,2560]{1,0:T(8,128)(2,1)S(1)} %slice_dynamic-update-slice_fusion.2), channel_id=1, source_target_pairs={{0,1},{1,0},{2,3},{3,2},{4,5},{5,4},{6,7},{7,6},{8,9},{9,8},{10,11... | collective-permute-start | bytes 1228808 | tf_op jit(solution)/shard_map/ppermute | solution.py:319
  35.4 1.5 %collective-permute-start.11 = (bf16[48,2560]{1,0:T(8,128)(2,1)S(1)}, bf16[48,2560]{1,0:T(8,128)(2,1)S(1)}, u32[]{:S(2)}, u32[]{:S(2)}) collective-permute-start(bf16[48,2560]{1,0:T(8,128)(2,1)S(1)} %collective-permute-done.7.refs_3_), channel_id=1, source_target_pairs={{0,1},{1,0},{2,3},{3,2},{4,5},{5,4},{6,7},{7,6},{8,9},{9,8},{10,11... | collective-permute-start | bytes 737288 | tf_op jit(solution)/shard_map/ppermute | solution.py:319
  43.4 3.4 %collective-permute-start.12 = (bf16[128,3072]{1,0:T(8,128)(2,1)S(1)}, bf16[128,3072]{1,0:T(8,128)(2,1)S(1)}, u32[]{:S(2)}, u32[]{:S(2)}) collective-permute-start(bf16[128,3072]{1,0:T(8,128)(2,1)S(1)} %get-tuple-element.60), channel_id=1, source_target_pairs={{0,1},{1,0},{2,3},{3,2},{4,5},{5,4},{6,7},{7,6},{8,9},{9,8},{10,11... | collective-permute-start | bytes 2359304 | tf_op jit(solution)/shard_map/ppermute | solution.py:319
  46.4 2.4 %collective-permute-start.13 = (bf16[128,3072]{1,0:T(8,128)(2,1)S(1)}, bf16[128,3072]{1,0:T(8,128)(2,1)S(1)}, u32[]{:S(2)}, u32[]{:S(2)}) collective-permute-start(bf16[128,3072]{1,0:T(8,128)(2,1)S(1)} %get-tuple-element.63), channel_id=1, source_target_pairs={{0,1},{1,0},{2,3},{3,2},{4,5},{5,4},{6,7},{7,6},{8,9},{9,8},{10,11... | collective-permute-start | bytes 2359304 | tf_op jit(solution)/shard_map/ppermute | solution.py:319
  47.0 28.1 %copy-start = (bf16[24,6144]{1,0:T(8,128)(2,1)S(1)}, bf16[24,6144]{1,0:T(8,128)(2,1)}, u32[]{:S(2)}) copy-start(bf16[24,6144]{1,0:T(8,128)(2,1)} %act_ref.3) | copy-start | bytes 884740
  47.0 28.1 %copy-start.1 = (s32[24,2]{0,1:T(2,128)S(1)}, s32[24,2]{0,1:T(2,128)}, u32[]{:S(2)}) copy-start(s32[24,2]{0,1:T(2,128)} %param.8) | copy-start | bytes 580
  47.1 28.1 %copy-start.2 = (f32[24,2]{0,1:T(2,128)S(1)}, f32[24,2]{0,1:T(2,128)}, u32[]{:S(2)}) copy-start(f32[24,2]{0,1:T(2,128)} %param.9) | copy-start | bytes 580
  47.1 4.9 %collective-permute-start.14 = (bf16[16,3072]{1,0:T(8,128)(2,1)S(1)}, bf16[16,3072]{1,0:T(8,128)(2,1)S(1)}, u32[]{:S(2)}, u32[]{:S(2)}) collective-permute-start(bf16[16,3072]{1,0:T(8,128)(2,1)S(1)} %get-tuple-element.77), channel_id=1, source_target_pairs={{0,2},{1,3},{2,0},{3,1},{4,6},{5,7},{6,4},{7,5},{8,10},{9,11},{10,... | collective-permute-start | bytes 294920 | tf_op jit(solution)/shard_map/ppermute | solution.py:319
  49.0 5.1 %collective-permute-start.17 = (bf16[16,3072]{1,0:T(8,128)(2,1)S(1)}, bf16[16,3072]{1,0:T(8,128)(2,1)S(1)}, u32[]{:S(2)}, u32[]{:S(2)}) collective-permute-start(bf16[16,3072]{1,0:T(8,128)(2,1)S(1)} %get-tuple-element.70), channel_id=1, source_target_pairs={{0,2},{1,3},{2,0},{3,1},{4,6},{5,7},{6,4},{7,5},{8,10},{9,11},{10,... | collective-permute-start | bytes 294920 | tf_op jit(solution)/shard_map/ppermute | solution.py:319
  52.1 10.0 %collective-permute-start.16 = (bf16[16,3072]{1,0:T(8,128)(2,1)S(1)}, bf16[16,3072]{1,0:T(8,128)(2,1)S(1)}, u32[]{:S(2)}, u32[]{:S(2)}) collective-permute-start(bf16[16,3072]{1,0:T(8,128)(2,1)S(1)} %add_convert_fusion.3), channel_id=1, source_target_pairs={{0,8},{1,9},{2,10},{3,11},{4,12},{5,13},{6,14},{7,15},{8,0},{9,1},... | collective-permute-start | bytes 294920 | tf_op jit(solution)/shard_map/ppermute | solution.py:314
  52.4 5.9 %collective-permute-start.15 = (bf16[16,6144]{1,0:T(8,128)(2,1)S(1)}, bf16[16,6144]{1,0:T(8,128)(2,1)S(1)}, u32[]{:S(2)}, u32[]{:S(2)}) collective-permute-start(bf16[16,6144]{1,0:T(8,128)(2,1)S(1)} %pad_maximum_fusion.2), channel_id=1, source_target_pairs={{0,2},{1,3},{2,0},{3,1},{4,6},{5,7},{6,4},{7,5},{8,10},{9,11},{10,... | collective-permute-start | bytes 589832 | tf_op jit(solution)/shard_map/ppermute | solution.py:319
  54.2 13.7 %collective-permute-start.18 = (bf16[16,3072]{1,0:T(8,128)(2,1)S(1)}, bf16[16,3072]{1,0:T(8,128)(2,1)S(1)}, u32[]{:S(2)}, u32[]{:S(2)}) collective-permute-start(bf16[16,3072]{1,0:T(8,128)(2,1)S(1)} %add_convert_fusion.2), channel_id=1, source_target_pairs={{0,8},{1,9},{2,10},{3,11},{4,12},{5,13},{6,14},{7,15},{8,0},{9,1},... | collective-permute-start | bytes 294920 | tf_op jit(solution)/shard_map/ppermute | solution.py:314
  58.4 11.0 %collective-permute-start.20 = (bf16[16,6144]{1,0:T(8,128)(2,1)S(1)}, bf16[16,6144]{1,0:T(8,128)(2,1)S(1)}, u32[]{:S(2)}, u32[]{:S(2)}) collective-permute-start(bf16[16,6144]{1,0:T(8,128)(2,1)S(1)} %pad_maximum_fusion.4), channel_id=1, source_target_pairs={{0,2},{1,3},{2,0},{3,1},{4,6},{5,7},{6,4},{7,5},{8,10},{9,11},{10,... | collective-permute-start | bytes 589832 | tf_op jit(solution)/shard_map/ppermute | solution.py:319
  59.6 13.9 %collective-permute-start.22 = (bf16[16,6144]{1,0:T(8,128)(2,1)S(1)}, bf16[16,6144]{1,0:T(8,128)(2,1)S(1)}, u32[]{:S(2)}, u32[]{:S(2)}) collective-permute-start(bf16[16,6144]{1,0:T(8,128)(2,1)S(1)} %fold.2), channel_id=1, source_target_pairs={{0,4},{1,5},{2,6},{3,7},{4,8},{5,9},{6,10},{7,11},{8,12},{9,13},{1... | collective-permute-start | bytes 589832 | tf_op jit(solution)/shard_map/ppermute | solution.py:314
  67.8 5.7 %collective-permute-start.19 = (bf16[16,6144]{1,0:T(8,128)(2,1)S(1)}, bf16[16,6144]{1,0:T(8,128)(2,1)S(1)}, u32[]{:S(2)}, u32[]{:S(2)}) collective-permute-start(bf16[16,6144]{1,0:T(8,128)(2,1)S(1)} %pad_maximum_fusion), channel_id=1, source_target_pairs={{0,2},{1,3},{2,0},{3,1},{4,6},{5,7},{6,4},{7,5},{8,10},{9,11},{10,... | collective-permute-start | bytes 589832 | tf_op jit(solution)/shard_map/ppermute | solution.py:319
  69.4 5.7 %collective-permute-start.21 = (bf16[16,6144]{1,0:T(8,128)(2,1)S(1)}, bf16[16,6144]{1,0:T(8,128)(2,1)S(1)}, u32[]{:S(2)}, u32[]{:S(2)}) collective-permute-start(bf16[16,6144]{1,0:T(8,128)(2,1)S(1)} %fold.3), channel_id=1, source_target_pairs={{0,12},{1,13},{2,14},{3,15},{4,0},{5,1},{6,2},{7,3},{8,4},{9,5},{1... | collective-permute-start | bytes 589832 | tf_op jit(solution)/shard_map/ppermute | solution.py:314

commit v16 on v15

--- a/solution.py
+++ b/solution.py
@@ -249,8 +249,8 @@
     return out[:ahead], out[ahead:]
 
 
-def mix_kernel(group, ids_ref, logits_ref, act_ref, arrived, near, last, *refs):
-    out_ref, kept, middle_rows = refs[-1], refs[:HALVES], refs[HALVES:-1]
+def mix_kernel(group, ids_ref, logits_ref, act_ref, arrived, near, last, two, *refs):
+    kept, out_ref = refs[:-1], refs[-1]
     plane = lax.axis_index("expert") // group
     first, second = choices(ids_ref[...], plane)
     lead = logits_ref[0:1, :] - logits_ref[1:2, :]
@@ -263,7 +263,7 @@
     for k, (at, part) in enumerate(spans(act_ref.shape[1], BACK)):
         columns = slice(at, at + part)
         own = kept[k][...].astype(jnp.float32) + arrived[:, columns].astype(jnp.float32)
-        blocks = [own.astype(jnp.bfloat16), near[:, columns], middle_rows[k][...]]
+        blocks = [own.astype(jnp.bfloat16), near[:, columns], two[:, columns]]
         rows = jnp.concatenate(blocks + [last[:, columns]], axis=0)
         sums = jnp.dot(terms, rows, preferred_element_type=jnp.float32)
         total = act_ref[:, columns].astype(jnp.float32)
@@ -373,18 +373,19 @@
         held.append([total[j * CAP : (j + 1) * CAP] for j in range(2 * EXPERTS)])
     place = {s: 1 + j for j, s in enumerate(ORDER)}
     crossed = [swap(h[EXPERTS + place[2]], far) for h in held]
-    middle = [shift(added(h[place[2]], x), -2) for h, x in zip(held, crossed)]
+    two = [added(h[place[2]], x) for h, x in zip(held, crossed)]
+    middle = shift(jnp.concatenate(two, axis=1), -2)
     mine = [jnp.concatenate([h[j] for h in held], axis=1) for j in range(2 * EXPERTS)]
     back = {}
-    back[3] = swap(after(mine[EXPERTS + place[3]], crossed[0]), far)
+    back[3] = swap(after(mine[EXPERTS + place[3]], *crossed), far)
     back[1] = swap(after(mine[EXPERTS + place[1]], back[3]), far)
     near_rows = fold(mine[place[1]], back[1])
     last_rows = fold(mine[place[3]], back[3])
-    back[0] = swap(after(mine[EXPERTS], last_rows, *middle), far)
+    back[0] = swap(after(mine[EXPERTS], near_rows, middle), far)
     near = shift(near_rows, -1)
     last = shift(last_rows, -3)
     arrived = back[0]
-    pieces = [arrived, near, last, *[h[0] for h in held], *middle]
+    pieces = [arrived, near, last, middle, *[h[0] for h in held]]
     return mix(group, ids, route_logits.T, activations, pieces)
 
 

time: 76.6 us -> 79 us (1.031)
  waiting for transfers between devices: 24 us -> 27.7 us
  starting transfers between devices: 26.8 us -> 25.5 us
    ppermute x13, waiting for transfers between devices: 11.7 us -> 17.4 us  [swap(): return lax.ppermute(x, 'expert', [(i, i ^ bit) for i in range(devices)])]
    ppermute x10 -> x9, waiting for transfers between devices: 12.3 us -> 10.2 us  [shift(): lax.ppermute(x, 'expert', [(i, (i + s * group) % devices) for i in range(...]
    ppermute x10 -> x9, starting transfers between devices: 16.2 us -> 15.7 us  [shift(): lax.ppermute(x, 'expert', [(i, (i + s * group) % devices) for i in range(...]
  transfers between devices with their start and end apart: 23 -> 22, of which waited for: 12 -> 13; matrix products, arithmetic and copies ran while one was open for 1% -> 1% of each run, Pallas kernels for 20% -> 19%
where the time goes in v16:
time: 79 us; the launch traced here: 78.8 us
  waiting for transfers between devices  27.7 us (35%)
  starting transfers between devices  25.5 us (32%)
  Pallas kernels  24.6 us (31%)
    ppermute x13, waiting for transfers between devices, swap(): return lax.ppermute(x, 'expert', [(i, i ^ bit) for i in range(devices)])  17.4 us
    ppermute x9, starting transfers between devices, shift(): lax.ppermute(x, 'expert', [(i, (i + s * group) % devices) for i in range(...  15.7 us
    ppermute x9, waiting for transfers between devices, shift(): lax.ppermute(x, 'expert', [(i, (i + s * group) % devices) for i in range(...  10.2 us
    ppermute x13, starting transfers between devices, swap(): return lax.ppermute(x, 'expert', [(i, i ^ bit) for i in range(devices)])  9.85 us
    pallas_call x2, Pallas kernels, gate_up(): pl.pallas_call(functools.partial(gate_up_kernel, len(pieces), len(later),...  9.5 us
    pallas_call x2, Pallas kernels, fetch(): pl.pallas_call(functools.partial(fetch_kernel, at), in_specs=[ANY, ANY],...  6.88 us
    pallas_call x2, Pallas kernels, down(): pl.pallas_call(functools.partial(down_kernel, ahead, segments), in_specs=...  5.29 us
  transfers between devices with their start and end apart: 22, of which 13 were waited for; matrix products, arithmetic and copies ran while one was open for 1% of the time, Pallas kernels for 19%

profile of v16, /device:TPU:0, one launch (start us, length us, event | category | flops | bytes accessed | tf_op | source)
XLA Modules:
  0.0 78.8 jit_solution(79120442397397083)
XLA Ops:
  0.0 1.5 %norm_and_pack.1 = (bf16[16,6144]{1,0:T(8,128)(2,1)S(1)}, bf16[16,3584]{1,0:T(8,128)(2,1)S(1)}, bf16[16,3584]{1,0:T(8,128)(2,1)S(1)}, bf16[16,3584]{1,0:T(8,128)...) custom-call(s32[2,24]{1,0:T(2,128)} %bitcast.3, ...), custom_call_target="tpu_custom_call" | custom-call | tf_op jit(solution)/shard_map/norm_and_pack/pallas_call | solution.py:67
  1.5 3.1 %collective-permute-start.1 = (bf16[16,3584]{1,0:T(8,128)(2,1)S(1)}, bf16[16,3584]{1,0:T(8,128)(2,1)S(1)}, u32[]{:S(2)}, u32[]{:S(2)}) collective-permute-start(bf16[16,3584]{1,0:T(8,128)(2,1)S(1)} %get-tuple-element.43), channel_id=1, source_target_pairs={{0,4},{1,5},{2,6},{3,7},{4,8},{5,9},{6,10},{7,11},{8,12},{9,13},{1... | collective-permute-start | bytes 344072 | tf_op jit(solution)/shard_map/ppermute | solution.py:314
  4.6 2.6 %collective-permute-start.2 = (bf16[16,3584]{1,0:T(8,128)(2,1)S(1)}, bf16[16,3584]{1,0:T(8,128)(2,1)S(1)}, u32[]{:S(2)}, u32[]{:S(2)}) collective-permute-start(bf16[16,3584]{1,0:T(8,128)(2,1)S(1)} %get-tuple-element.44), channel_id=1, source_target_pairs={{0,8},{1,9},{2,10},{3,11},{4,12},{5,13},{6,14},{7,15},{8,0},{9,1},... | collective-permute-start | bytes 344072 | tf_op jit(solution)/shard_map/ppermute | solution.py:314
  7.2 1.3 %collective-permute-start.3 = (bf16[16,3584]{1,0:T(8,128)(2,1)S(1)}, bf16[16,3584]{1,0:T(8,128)(2,1)S(1)}, u32[]{:S(2)}, u32[]{:S(2)}) collective-permute-start(bf16[16,3584]{1,0:T(8,128)(2,1)S(1)} %get-tuple-element.45), channel_id=1, source_target_pairs={{0,12},{1,13},{2,14},{3,15},{4,0},{5,1},{6,2},{7,3},{8,4},{9,5},{1... | collective-permute-start | bytes 344072 | tf_op jit(solution)/shard_map/ppermute | solution.py:314
  8.5 1.5 %collective-permute-start = (bf16[16,6144]{1,0:T(8,128)(2,1)S(1)}, bf16[16,6144]{1,0:T(8,128)(2,1)S(1)}, u32[]{:S(2)}, u32[]{:S(2)}) collective-permute-start(bf16[16,6144]{1,0:T(8,128)(2,1)S(1)} %get-tuple-element.36.after_ref.refs_0_), channel_id=1, source_target_pairs={{0,2},{1,3},{2,0},{3,1},{4,6},{5,7},{6,4},{7,5},{8,10},{9,11},{10,... | collective-permute-start | bytes 589832 | tf_op jit(solution)/shard_map/ppermute | solution.py:319
  10.1 3.4 %fetch.3.refs_6_ = bf16[1152,3584]{1,0:T(8,128)(2,1)S(1)} custom-call(bf16[1152,6144]{1,0:T(8,128)(2,1)} %refs_8_.2, bf16[16,6144]{1,0:T(8,128)(2,1)S(1)} %get-tuple-element.36.after_ref.refs_0_), custom_call_target="tpu_custom_call" | custom-call | bytes 16515072 | tf_op jit(solution)/shard_map/fetch/pallas_call | solution.py:100
  13.5 3.4 %fetch.2.refs_5_ = bf16[1152,3584]{1,0:T(8,128)(2,1)S(1)} custom-call(bf16[1152,6144]{1,0:T(8,128)(2,1)} %refs_7_.1, bf16[16,6144]{1,0:T(8,128)(2,1)S(1)} %get-tuple-element.36.after_ref.refs_0_), custom_call_target="tpu_custom_call" | custom-call | bytes 16515072 | tf_op jit(solution)/shard_map/fetch/pallas_call | solution.py:100
  16.9 0.0 collective-permute-done.1
  17.0 0.0 collective-permute-done.2
  17.0 0.0 collective-permute-done.3
  17.1 0.6 collective-permute-start.8
  17.6 0.0 collective-permute-done.refs_2_
  17.6 1.8 %collective-permute-start.4 = (bf16[16,2560]{1,0:T(8,128)(2,1)S(1)}, bf16[16,2560]{1,0:T(8,128)(2,1)S(1)}, u32[]{:S(2)}, u32[]{:S(2)}) collective-permute-start(bf16[16,2560]{1,0:T(8,128)(2,1)S(1)} %get-tuple-element.46), channel_id=1, source_target_pairs={{0,4},{1,5},{2,6},{3,7},{4,8},{5,9},{6,10},{7,11},{8,12},{9,13},{1... | collective-permute-start | bytes 245768 | tf_op jit(solution)/shard_map/ppermute | solution.py:314
  19.4 1.6 %collective-permute-start.5 = (bf16[16,2560]{1,0:T(8,128)(2,1)S(1)}, bf16[16,2560]{1,0:T(8,128)(2,1)S(1)}, u32[]{:S(2)}, u32[]{:S(2)}) collective-permute-start(bf16[16,2560]{1,0:T(8,128)(2,1)S(1)} %get-tuple-element.47), channel_id=1, source_target_pairs={{0,8},{1,9},{2,10},{3,11},{4,12},{5,13},{6,14},{7,15},{8,0},{9,1},... | collective-permute-start | bytes 245768 | tf_op jit(solution)/shard_map/ppermute | solution.py:314
  21.0 0.8 %collective-permute-start.6 = (bf16[16,2560]{1,0:T(8,128)(2,1)S(1)}, bf16[16,2560]{1,0:T(8,128)(2,1)S(1)}, u32[]{:S(2)}, u32[]{:S(2)}) collective-permute-start(bf16[16,2560]{1,0:T(8,128)(2,1)S(1)} %get-tuple-element.48), channel_id=1, source_target_pairs={{0,12},{1,13},{2,14},{3,15},{4,0},{5,1},{6,2},{7,3},{8,4},{9,5},{1... | collective-permute-start | bytes 245768 | tf_op jit(solution)/shard_map/ppermute | solution.py:314
  21.9 2.6 %collective-permute-done.4 = bf16[16,2560]{1,0:T(8,128)(2,1)S(1)} collective-permute-done((bf16[16,2560]{1,0:T(8,128)(2,1)S(1)}, bf16[16,2560]{1,0:T(8,128)(2,1)S(1)}, u32[]{:S(2)}, u32[]{:S(2)}) %collective-permute-start.4) | collective-permute-done | bytes 81952 | tf_op jit(solution)/shard_map/ppermute | solution.py:314
  24.4 2.3 %collective-permute-done.5 = bf16[16,2560]{1,0:T(8,128)(2,1)S(1)} collective-permute-done((bf16[16,2560]{1,0:T(8,128)(2,1)S(1)}, bf16[16,2560]{1,0:T(8,128)(2,1)S(1)}, u32[]{:S(2)}, u32[]{:S(2)}) %collective-permute-start.5) | collective-permute-done | bytes 81952 | tf_op jit(solution)/shard_map/ppermute | solution.py:314
  26.8 0.0 collective-permute-done.8.refs_3_
  26.8 0.1 collective-permute-start.9
  26.9 0.0 collective-permute-done.6
  26.9 1.2 %collective-permute-start.7 = (bf16[48,2560]{1,0:T(8,128)(2,1)S(1)}, bf16[48,2560]{1,0:T(8,128)(2,1)S(1)}, u32[]{:S(2)}, u32[]{:S(2)}) collective-permute-start(bf16[48,2560]{1,0:T(8,128)(2,1)S(1)} %get-tuple-element.88.refs_1_), channel_id=1, source_target_pairs={{0,2},{1,3},{2,0},{3,1},{4,6},{5,7},{6,4},{7,5},{8,10},{9,11},{10,... | collective-permute-start | bytes 737288 | tf_op jit(solution)/shard_map/ppermute | solution.py:319
  28.2 0.2 collective-permute-start.10
  28.4 1.0 %collective-permute-done.9.refs_4_ = bf16[128,3584]{1,0:T(8,128)(2,1)S(1)} collective-permute-done((bf16[128,3584]{1,0:T(8,128)(2,1)S(1)}, bf16[128,3584]{1,0:T(8,128)(2,1)S(1)}, u32[]{:S(2)}, u32[]{:S(2)}) %collective-permute-start.9) | collective-permute-done | bytes 917536 | tf_op jit(solution)/shard_map/ppermute | solution.py:319
  29.4 5.5 %gate_up.2 = (bf16[1152,2560]{1,0:T(8,128)(2,1)S(1)}, bf16[1152,2560]{1,0:T(8,128)(2,1)S(1)}, f32[1152,256]{1,0:T(8,128)S(1)}, f32[1152,256]{1,0:T(8,128)S(1)}) custom-call(bf16[16,6144]{1,0:T(8,128)(2,1)S(1)} %get-tuple-element.36.after_ref.refs_0_, bf16[48,3584]{1,0:T(8,128)(2,1)S(1)} %get-tuple-element.49.refs_3_.refs_1_, ...), custom_call_target="tpu_custom_call" | custom-call | flops 4227858432 | bytes 18874368 | tf_op jit(solution)/shard_map/gate_up/pallas_call | solution.py:182
  34.9 0.5 collective-permute-done.7.refs_3_
  35.4 0.0 collective-permute-start.11
  35.4 0.0 collective-permute-done.10.refs_4_
  35.4 1.5 %collective-permute-done.11.refs_5_ = bf16[48,2560]{1,0:T(8,128)(2,1)S(1)} collective-permute-done((bf16[48,2560]{1,0:T(8,128)(2,1)S(1)}, bf16[48,2560]{1,0:T(8,128)(2,1)S(1)}, u32[]{:S(2)}, u32[]{:S(2)}) %collective-permute-start.11) | collective-permute-done | bytes 245792 | tf_op jit(solution)/shard_map/ppermute | solution.py:319
  36.9 4.0 %gate_up.3 = (bf16[1152,4096]{1,0:T(8,128)(2,1)S(1)}, bf16[256,1152]{1,0:T(8,128)(2,1)S(1)}) custom-call(bf16[16,6144]{1,0:T(8,128)(2,1)S(1)} %get-tuple-element.36.after_ref.refs_0_, bf16[48,2560]{1,0:T(8,128)(2,1)S(1)} %get-tuple-element.88.refs_1_, bf16[16,6144]{1,0:T(8,128)(2,1)S(1)} %collective-permute-done.refs_2_, ...), custom_call_target="tpu_custom_call" | custom-call | flops 3019898880 | bytes 14155776 | tf_op jit(solution)/shard_map/gate_up/pallas_call | solution.py:182
  40.9 2.5 %down.2 = (bf16[1152,2048]{1,0:T(8,128)(2,1)S(1)}, bf16[128,3072]{1,0:T(8,128)(2,1)S(1)}, bf16[128,3072]{1,0:T(8,128)(2,1)S(1)}) custom-call(bf16[256,1152]{1,0:T(8,128)(2,1)S(1)} %get-tuple-element.57.hidden_ref, bf16[1152,4096]{1,0:T(8,128)(2,1)S(1)} %get-tuple-element.58.refs_0_, bf16[1152,6144]{1,0:T(8,128)(2,1)} %refs_1_.1), custom_call_target="tpu_custom_call" | custom-call | flops 1811939328 | bytes 9240576 | tf_op jit(solution)/shard_map/down/pallas_call | solution.py:235
  43.4 0.2 collective-permute-start.12
  43.6 2.8 %down.3 = (bf16[128,3072]{1,0:T(8,128)(2,1)S(1)}, bf16[128,3072]{1,0:T(8,128)(2,1)S(1)}) custom-call(bf16[256,1152]{1,0:T(8,128)(2,1)S(1)} %get-tuple-element.57.hidden_ref, bf16[1152,4096]{1,0:T(8,128)(2,1)S(1)} %get-tuple-element.58.refs_0_, bf16[1152,2048]{1,0:T(8,128)(2,1)S(1)} %get-tuple-element.61.refs_1_), custom_call_target="tpu_custom_call" | custom-call | flops 1811939328 | bytes 9240576 | tf_op jit(solution)/shard_map/down/pallas_call | solution.py:235
  46.4 0.4 collective-permute-start.13
  46.8 0.0 collective-permute-done.12
  46.8 0.2 add_convert_fusion.1
  47.0 0.0 copy-start
  47.0 0.0 copy-start.1
  47.1 0.0 copy-start.2
  47.1 1.2 %collective-permute-start.14 = (bf16[16,3072]{1,0:T(8,128)(2,1)S(1)}, bf16[16,3072]{1,0:T(8,128)(2,1)S(1)}, u32[]{:S(2)}, u32[]{:S(2)}) collective-permute-start(bf16[16,3072]{1,0:T(8,128)(2,1)S(1)} %get-tuple-element.76), channel_id=1, source_target_pairs={{0,2},{1,3},{2,0},{3,1},{4,6},{5,7},{6,4},{7,5},{8,10},{9,11},{10,... | collective-permute-start | bytes 294920 | tf_op jit(solution)/shard_map/ppermute | solution.py:319
  48.3 0.4 collective-permute-done.13
  48.8 0.2 add_convert_fusion
  49.0 1.2 %collective-permute-start.15 = (bf16[16,3072]{1,0:T(8,128)(2,1)S(1)}, bf16[16,3072]{1,0:T(8,128)(2,1)S(1)}, u32[]{:S(2)}, u32[]{:S(2)}) collective-permute-start(bf16[16,3072]{1,0:T(8,128)(2,1)S(1)} %get-tuple-element.69), channel_id=1, source_target_pairs={{0,2},{1,3},{2,0},{3,1},{4,6},{5,7},{6,4},{7,5},{8,10},{9,11},{10,... | collective-permute-start | bytes 294920 | tf_op jit(solution)/shard_map/ppermute | solution.py:319
  50.3 1.7 %collective-permute-done.14 = bf16[16,3072]{1,0:T(8,128)(2,1)S(1)} collective-permute-done((bf16[16,3072]{1,0:T(8,128)(2,1)S(1)}, bf16[16,3072]{1,0:T(8,128)(2,1)S(1)}, u32[]{:S(2)}, u32[]{:S(2)}) %collective-permute-start.14) | collective-permute-done | bytes 98336 | tf_op jit(solution)/shard_map/ppermute | solution.py:319
  52.0 2.1 %collective-permute-done.15 = bf16[16,3072]{1,0:T(8,128)(2,1)S(1)} collective-permute-done((bf16[16,3072]{1,0:T(8,128)(2,1)S(1)}, bf16[16,3072]{1,0:T(8,128)(2,1)S(1)}, u32[]{:S(2)}, u32[]{:S(2)}) %collective-permute-start.15) | collective-permute-done | bytes 98336 | tf_op jit(solution)/shard_map/ppermute | solution.py:319
  54.1 1.2 %collective-permute-start.16 = (bf16[16,6144]{1,0:T(8,128)(2,1)S(1)}, bf16[16,6144]{1,0:T(8,128)(2,1)S(1)}, u32[]{:S(2)}, u32[]{:S(2)}) collective-permute-start(bf16[16,6144]{1,0:T(8,128)(2,1)S(1)} %pad_maximum_fusion.3), channel_id=1, source_target_pairs={{0,2},{1,3},{2,0},{3,1},{4,6},{5,7},{6,4},{7,5},{8,10},{9,11},{10,... | collective-permute-start | bytes 589832 | tf_op jit(solution)/shard_map/ppermute | solution.py:319
  55.4 0.4 collective-permute-start.18
  55.8 4.7 %collective-permute-done.16.arrived_ref = bf16[16,6144]{1,0:T(8,128)(2,1)S(1)} collective-permute-done((bf16[16,6144]{1,0:T(8,128)(2,1)S(1)}, bf16[16,6144]{1,0:T(8,128)(2,1)S(1)}, u32[]{:S(2)}, u32[]{:S(2)}) %collective-permute-start.16) | collective-permute-done | bytes 196640 | tf_op jit(solution)/shard_map/ppermute | solution.py:319
  60.5 1.2 %collective-permute-start.17 = (bf16[16,6144]{1,0:T(8,128)(2,1)S(1)}, bf16[16,6144]{1,0:T(8,128)(2,1)S(1)}, u32[]{:S(2)}, u32[]{:S(2)}) collective-permute-start(bf16[16,6144]{1,0:T(8,128)(2,1)S(1)} %pad_maximum_fusion.2), channel_id=1, source_target_pairs={{0,2},{1,3},{2,0},{3,1},{4,6},{5,7},{6,4},{7,5},{8,10},{9,11},{10,... | collective-permute-start | bytes 589832 | tf_op jit(solution)/shard_map/ppermute | solution.py:319
  61.7 0.1 fold.3
  61.7 1.4 %collective-permute-start.21 = (bf16[16,6144]{1,0:T(8,128)(2,1)S(1)}, bf16[16,6144]{1,0:T(8,128)(2,1)S(1)}, u32[]{:S(2)}, u32[]{:S(2)}) collective-permute-start(bf16[16,6144]{1,0:T(8,128)(2,1)S(1)} %fold.3), channel_id=1, source_target_pairs={{0,4},{1,5},{2,6},{3,7},{4,8},{5,9},{6,10},{7,11},{8,12},{9,13},{1... | collective-permute-start | bytes 589832 | tf_op jit(solution)/shard_map/ppermute | solution.py:314
  63.1 3.0 %collective-permute-done.17.arrived_ref = bf16[16,6144]{1,0:T(8,128)(2,1)S(1)} collective-permute-done((bf16[16,6144]{1,0:T(8,128)(2,1)S(1)}, bf16[16,6144]{1,0:T(8,128)(2,1)S(1)}, u32[]{:S(2)}, u32[]{:S(2)}) %collective-permute-start.17) | collective-permute-done | bytes 196640 | tf_op jit(solution)/shard_map/ppermute | solution.py:319
  66.2 0.1 fold.2
  66.2 2.7 %collective-permute-start.20 = (bf16[16,6144]{1,0:T(8,128)(2,1)S(1)}, bf16[16,6144]{1,0:T(8,128)(2,1)S(1)}, u32[]{:S(2)}, u32[]{:S(2)}) collective-permute-start(bf16[16,6144]{1,0:T(8,128)(2,1)S(1)} %fold.2), channel_id=1, source_target_pairs={{0,12},{1,13},{2,14},{3,15},{4,0},{5,1},{6,2},{7,3},{8,4},{9,5},{1... | collective-permute-start | bytes 589832 | tf_op jit(solution)/shard_map/ppermute | solution.py:314
  68.9 2.9 %collective-permute-done.18.two = bf16[16,6144]{1,0:T(8,128)(2,1)S(1)} collective-permute-done((bf16[16,6144]{1,0:T(8,128)(2,1)S(1)}, bf16[16,6144]{1,0:T(8,128)(2,1)S(1)}, u32[]{:S(2)}, u32[]{:S(2)}) %collective-permute-start.18) | collective-permute-done | bytes 196640 | tf_op jit(solution)/shard_map/ppermute | solution.py:314
  71.8 0.8 %collective-permute-start.19 = (bf16[16,6144]{1,0:T(8,128)(2,1)S(1)}, bf16[16,6144]{1,0:T(8,128)(2,1)S(1)}, u32[]{:S(2)}, u32[]{:S(2)}) collective-permute-start(bf16[16,6144]{1,0:T(8,128)(2,1)S(1)} %pad_maximum_fusion), channel_id=1, source_target_pairs={{0,2},{1,3},{2,0},{3,1},{4,6},{5,7},{6,4},{7,5},{8,10},{9,11},{10,... | collective-permute-start | bytes 589832 | tf_op jit(solution)/shard_map/ppermute | solution.py:319
  72.7 0.0 collective-permute-done.21.last
  72.7 2.4 %collective-permute-done.20.near = bf16[16,6144]{1,0:T(8,128)(2,1)S(1)} collective-permute-done((bf16[16,6144]{1,0:T(8,128)(2,1)S(1)}, bf16[16,6144]{1,0:T(8,128)(2,1)S(1)}, u32[]{:S(2)}, u32[]{:S(2)}) %collective-permute-start.20) | collective-permute-done | bytes 196640 | tf_op jit(solution)/shard_map/ppermute | solution.py:314
  75.1 2.4 %collective-permute-done.19.arrived = bf16[16,6144]{1,0:T(8,128)(2,1)S(1)} collective-permute-done((bf16[16,6144]{1,0:T(8,128)(2,1)S(1)}, bf16[16,6144]{1,0:T(8,128)(2,1)S(1)}, u32[]{:S(2)}, u32[]{:S(2)}) %collective-permute-start.19) | collective-permute-done | bytes 196640 | tf_op jit(solution)/shard_map/ppermute | solution.py:319
  77.5 0.0 copy-done
  77.5 0.0 copy-done.1
  77.5 0.0 copy-done.2
  77.5 1.3 %mix.1 = bf16[24,6144]{1,0:T(8,128)(2,1)} custom-call(s32[2,24]{1,0:T(2,128)S(1)} %bitcast.4, f32[2,24]{1,0:T(2,128)S(1)} %bitcast.5, bf16[24,6144]{1,0:T(8,128)(2,1)S(1)} %copy-done, bf16[16,6144]{1,0:T(8,128)(2,1)S(1)} %collective-permute-done.19.arrived, bf16[16,6144]{1,0:T(8,128)(2,1)S(1)} %collective-permute-done.20.near, ...), custom_call_target="tpu_custom_call" | custom-call | tf_op jit(solution)/shard_map/mix/pallas_call | solution.py:276
  (22 shorter events, 0.4 us)
Async XLA Ops:
  1.5 15.5 %collective-permute-start.1 = (bf16[16,3584]{1,0:T(8,128)(2,1)S(1)}, bf16[16,3584]{1,0:T(8,128)(2,1)S(1)}, u32[]{:S(2)}, u32[]{:S(2)}) collective-permute-start(bf16[16,3584]{1,0:T(8,128)(2,1)S(1)} %get-tuple-element.43), channel_id=1, source_target_pairs={{0,4},{1,5},{2,6},{3,7},{4,8},{5,9},{6,10},{7,11},{8,12},{9,13},{1... | collective-permute-start | bytes 344072 | tf_op jit(solution)/shard_map/ppermute | solution.py:314
  4.6 12.4 %collective-permute-start.2 = (bf16[16,3584]{1,0:T(8,128)(2,1)S(1)}, bf16[16,3584]{1,0:T(8,128)(2,1)S(1)}, u32[]{:S(2)}, u32[]{:S(2)}) collective-permute-start(bf16[16,3584]{1,0:T(8,128)(2,1)S(1)} %get-tuple-element.44), channel_id=1, source_target_pairs={{0,8},{1,9},{2,10},{3,11},{4,12},{5,13},{6,14},{7,15},{8,0},{9,1},... | collective-permute-start | bytes 344072 | tf_op jit(solution)/shard_map/ppermute | solution.py:314
  7.2 9.9 %collective-permute-start.3 = (bf16[16,3584]{1,0:T(8,128)(2,1)S(1)}, bf16[16,3584]{1,0:T(8,128)(2,1)S(1)}, u32[]{:S(2)}, u32[]{:S(2)}) collective-permute-start(bf16[16,3584]{1,0:T(8,128)(2,1)S(1)} %get-tuple-element.45), channel_id=1, source_target_pairs={{0,12},{1,13},{2,14},{3,15},{4,0},{5,1},{6,2},{7,3},{8,4},{9,5},{1... | collective-permute-start | bytes 344072 | tf_op jit(solution)/shard_map/ppermute | solution.py:314
  8.5 9.1 %collective-permute-start = (bf16[16,6144]{1,0:T(8,128)(2,1)S(1)}, bf16[16,6144]{1,0:T(8,128)(2,1)S(1)}, u32[]{:S(2)}, u32[]{:S(2)}) collective-permute-start(bf16[16,6144]{1,0:T(8,128)(2,1)S(1)} %get-tuple-element.36.after_ref.refs_0_), channel_id=1, source_target_pairs={{0,2},{1,3},{2,0},{3,1},{4,6},{5,7},{6,4},{7,5},{8,10},{9,11},{10,... | collective-permute-start | bytes 589832 | tf_op jit(solution)/shard_map/ppermute | solution.py:319
  17.1 9.7 %collective-permute-start.8 = (bf16[48,3584]{1,0:T(8,128)(2,1)S(1)}, bf16[48,3584]{1,0:T(8,128)(2,1)S(1)}, u32[]{:S(2)}, u32[]{:S(2)}) collective-permute-start(bf16[48,3584]{1,0:T(8,128)(2,1)S(1)} %get-tuple-element.49.refs_3_.refs_1_), channel_id=1, source_target_pairs={{0,2},{1,3},{2,0},{3,1},{4,6},{5,7},{6,4},{7,5},{8,10},{9,11},{10,... | collective-permute-start | bytes 1032200 | tf_op jit(solution)/shard_map/ppermute | solution.py:319
  17.6 6.8 %collective-permute-start.4 = (bf16[16,2560]{1,0:T(8,128)(2,1)S(1)}, bf16[16,2560]{1,0:T(8,128)(2,1)S(1)}, u32[]{:S(2)}, u32[]{:S(2)}) collective-permute-start(bf16[16,2560]{1,0:T(8,128)(2,1)S(1)} %get-tuple-element.46), channel_id=1, source_target_pairs={{0,4},{1,5},{2,6},{3,7},{4,8},{5,9},{6,10},{7,11},{8,12},{9,13},{1... | collective-permute-start | bytes 245768 | tf_op jit(solution)/shard_map/ppermute | solution.py:314
  19.4 7.4 %collective-permute-start.5 = (bf16[16,2560]{1,0:T(8,128)(2,1)S(1)}, bf16[16,2560]{1,0:T(8,128)(2,1)S(1)}, u32[]{:S(2)}, u32[]{:S(2)}) collective-permute-start(bf16[16,2560]{1,0:T(8,128)(2,1)S(1)} %get-tuple-element.47), channel_id=1, source_target_pairs={{0,8},{1,9},{2,10},{3,11},{4,12},{5,13},{6,14},{7,15},{8,0},{9,1},... | collective-permute-start | bytes 245768 | tf_op jit(solution)/shard_map/ppermute | solution.py:314
  21.0 5.9 %collective-permute-start.6 = (bf16[16,2560]{1,0:T(8,128)(2,1)S(1)}, bf16[16,2560]{1,0:T(8,128)(2,1)S(1)}, u32[]{:S(2)}, u32[]{:S(2)}) collective-permute-start(bf16[16,2560]{1,0:T(8,128)(2,1)S(1)} %get-tuple-element.48), channel_id=1, source_target_pairs={{0,12},{1,13},{2,14},{3,15},{4,0},{5,1},{6,2},{7,3},{8,4},{9,5},{1... | collective-permute-start | bytes 245768 | tf_op jit(solution)/shard_map/ppermute | solution.py:314
  26.8 2.5 %collective-permute-start.9 = (bf16[128,3584]{1,0:T(8,128)(2,1)S(1)}, bf16[128,3584]{1,0:T(8,128)(2,1)S(1)}, u32[]{:S(2)}, u32[]{:S(2)}) collective-permute-start(bf16[128,3584]{1,0:T(8,128)(2,1)S(1)} %constant_dynamic-update-slice_fusion.6), channel_id=1, source_target_pairs={{0,1},{1,0},{2,3},{3,2},{4,5},{5,4},{6,7},{7,6},{8,9},{9,8},{10,11... | collective-permute-start | bytes 2752520 | tf_op jit(solution)/shard_map/ppermute | solution.py:319
  26.9 8.4 %collective-permute-start.7 = (bf16[48,2560]{1,0:T(8,128)(2,1)S(1)}, bf16[48,2560]{1,0:T(8,128)(2,1)S(1)}, u32[]{:S(2)}, u32[]{:S(2)}) collective-permute-start(bf16[48,2560]{1,0:T(8,128)(2,1)S(1)} %get-tuple-element.88.refs_1_), channel_id=1, source_target_pairs={{0,2},{1,3},{2,0},{3,1},{4,6},{5,7},{6,4},{7,5},{8,10},{9,11},{10,... | collective-permute-start | bytes 737288 | tf_op jit(solution)/shard_map/ppermute | solution.py:319
  28.2 7.2 %collective-permute-start.10 = (bf16[80,2560]{1,0:T(8,128)(2,1)S(1)}, bf16[80,2560]{1,0:T(8,128)(2,1)S(1)}, u32[]{:S(2)}, u32[]{:S(2)}) collective-permute-start(bf16[80,2560]{1,0:T(8,128)(2,1)S(1)} %slice_dynamic-update-slice_fusion.2), channel_id=1, source_target_pairs={{0,1},{1,0},{2,3},{3,2},{4,5},{5,4},{6,7},{7,6},{8,9},{9,8},{10,11... | collective-permute-start | bytes 1228808 | tf_op jit(solution)/shard_map/ppermute | solution.py:319
  35.4 1.5 %collective-permute-start.11 = (bf16[48,2560]{1,0:T(8,128)(2,1)S(1)}, bf16[48,2560]{1,0:T(8,128)(2,1)S(1)}, u32[]{:S(2)}, u32[]{:S(2)}) collective-permute-start(bf16[48,2560]{1,0:T(8,128)(2,1)S(1)} %collective-permute-done.7.refs_3_), channel_id=1, source_target_pairs={{0,1},{1,0},{2,3},{3,2},{4,5},{5,4},{6,7},{7,6},{8,9},{9,8},{10,11... | collective-permute-start | bytes 737288 | tf_op jit(solution)/shard_map/ppermute | solution.py:319
  43.4 3.4 %collective-permute-start.12 = (bf16[128,3072]{1,0:T(8,128)(2,1)S(1)}, bf16[128,3072]{1,0:T(8,128)(2,1)S(1)}, u32[]{:S(2)}, u32[]{:S(2)}) collective-permute-start(bf16[128,3072]{1,0:T(8,128)(2,1)S(1)} %get-tuple-element.60), channel_id=1, source_target_pairs={{0,1},{1,0},{2,3},{3,2},{4,5},{5,4},{6,7},{7,6},{8,9},{9,8},{10,11... | collective-permute-start | bytes 2359304 | tf_op jit(solution)/shard_map/ppermute | solution.py:319
  46.4 2.4 %collective-permute-start.13 = (bf16[128,3072]{1,0:T(8,128)(2,1)S(1)}, bf16[128,3072]{1,0:T(8,128)(2,1)S(1)}, u32[]{:S(2)}, u32[]{:S(2)}) collective-permute-start(bf16[128,3072]{1,0:T(8,128)(2,1)S(1)} %get-tuple-element.63), channel_id=1, source_target_pairs={{0,1},{1,0},{2,3},{3,2},{4,5},{5,4},{6,7},{7,6},{8,9},{9,8},{10,11... | collective-permute-start | bytes 2359304 | tf_op jit(solution)/shard_map/ppermute | solution.py:319
  47.0 30.5 %copy-start = (bf16[24,6144]{1,0:T(8,128)(2,1)S(1)}, bf16[24,6144]{1,0:T(8,128)(2,1)}, u32[]{:S(2)}) copy-start(bf16[24,6144]{1,0:T(8,128)(2,1)} %act_ref.3) | copy-start | bytes 884740
  47.0 30.5 %copy-start.1 = (s32[24,2]{0,1:T(2,128)S(1)}, s32[24,2]{0,1:T(2,128)}, u32[]{:S(2)}) copy-start(s32[24,2]{0,1:T(2,128)} %param.8) | copy-start | bytes 580
  47.1 30.5 %copy-start.2 = (f32[24,2]{0,1:T(2,128)S(1)}, f32[24,2]{0,1:T(2,128)}, u32[]{:S(2)}) copy-start(f32[24,2]{0,1:T(2,128)} %param.9) | copy-start | bytes 580
  47.1 4.9 %collective-permute-start.14 = (bf16[16,3072]{1,0:T(8,128)(2,1)S(1)}, bf16[16,3072]{1,0:T(8,128)(2,1)S(1)}, u32[]{:S(2)}, u32[]{:S(2)}) collective-permute-start(bf16[16,3072]{1,0:T(8,128)(2,1)S(1)} %get-tuple-element.76), channel_id=1, source_target_pairs={{0,2},{1,3},{2,0},{3,1},{4,6},{5,7},{6,4},{7,5},{8,10},{9,11},{10,... | collective-permute-start | bytes 294920 | tf_op jit(solution)/shard_map/ppermute | solution.py:319
  49.0 5.1 %collective-permute-start.15 = (bf16[16,3072]{1,0:T(8,128)(2,1)S(1)}, bf16[16,3072]{1,0:T(8,128)(2,1)S(1)}, u32[]{:S(2)}, u32[]{:S(2)}) collective-permute-start(bf16[16,3072]{1,0:T(8,128)(2,1)S(1)} %get-tuple-element.69), channel_id=1, source_target_pairs={{0,2},{1,3},{2,0},{3,1},{4,6},{5,7},{6,4},{7,5},{8,10},{9,11},{10,... | collective-permute-start | bytes 294920 | tf_op jit(solution)/shard_map/ppermute | solution.py:319
  54.1 6.4 %collective-permute-start.16 = (bf16[16,6144]{1,0:T(8,128)(2,1)S(1)}, bf16[16,6144]{1,0:T(8,128)(2,1)S(1)}, u32[]{:S(2)}, u32[]{:S(2)}) collective-permute-start(bf16[16,6144]{1,0:T(8,128)(2,1)S(1)} %pad_maximum_fusion.3), channel_id=1, source_target_pairs={{0,2},{1,3},{2,0},{3,1},{4,6},{5,7},{6,4},{7,5},{8,10},{9,11},{10,... | collective-permute-start | bytes 589832 | tf_op jit(solution)/shard_map/ppermute | solution.py:319
  55.4 16.5 %collective-permute-start.18 = (bf16[16,6144]{1,0:T(8,128)(2,1)S(1)}, bf16[16,6144]{1,0:T(8,128)(2,1)S(1)}, u32[]{:S(2)}, u32[]{:S(2)}) collective-permute-start(bf16[16,6144]{1,0:T(8,128)(2,1)S(1)} %pad_maximum_fusion.4), channel_id=1, source_target_pairs={{0,8},{1,9},{2,10},{3,11},{4,12},{5,13},{6,14},{7,15},{8,0},{9,1},... | collective-permute-start | bytes 589832 | tf_op jit(solution)/shard_map/ppermute | solution.py:314
  60.5 5.7 %collective-permute-start.17 = (bf16[16,6144]{1,0:T(8,128)(2,1)S(1)}, bf16[16,6144]{1,0:T(8,128)(2,1)S(1)}, u32[]{:S(2)}, u32[]{:S(2)}) collective-permute-start(bf16[16,6144]{1,0:T(8,128)(2,1)S(1)} %pad_maximum_fusion.2), channel_id=1, source_target_pairs={{0,2},{1,3},{2,0},{3,1},{4,6},{5,7},{6,4},{7,5},{8,10},{9,11},{10,... | collective-permute-start | bytes 589832 | tf_op jit(solution)/shard_map/ppermute | solution.py:319
  61.7 11.0 %collective-permute-start.21 = (bf16[16,6144]{1,0:T(8,128)(2,1)S(1)}, bf16[16,6144]{1,0:T(8,128)(2,1)S(1)}, u32[]{:S(2)}, u32[]{:S(2)}) collective-permute-start(bf16[16,6144]{1,0:T(8,128)(2,1)S(1)} %fold.3), channel_id=1, source_target_pairs={{0,4},{1,5},{2,6},{3,7},{4,8},{5,9},{6,10},{7,11},{8,12},{9,13},{1... | collective-permute-start | bytes 589832 | tf_op jit(solution)/shard_map/ppermute | solution.py:314
  66.2 8.8 %collective-permute-start.20 = (bf16[16,6144]{1,0:T(8,128)(2,1)S(1)}, bf16[16,6144]{1,0:T(8,128)(2,1)S(1)}, u32[]{:S(2)}, u32[]{:S(2)}) collective-permute-start(bf16[16,6144]{1,0:T(8,128)(2,1)S(1)} %fold.2), channel_id=1, source_target_pairs={{0,12},{1,13},{2,14},{3,15},{4,0},{5,1},{6,2},{7,3},{8,4},{9,5},{1... | collective-permute-start | bytes 589832 | tf_op jit(solution)/shard_map/ppermute | solution.py:314
  71.8 5.7 %collective-permute-start.19 = (bf16[16,6144]{1,0:T(8,128)(2,1)S(1)}, bf16[16,6144]{1,0:T(8,128)(2,1)S(1)}, u32[]{:S(2)}, u32[]{:S(2)}) collective-permute-start(bf16[16,6144]{1,0:T(8,128)(2,1)S(1)} %pad_maximum_fusion), channel_id=1, source_target_pairs={{0,2},{1,3},{2,0},{3,1},{4,6},{5,7},{6,4},{7,5},{8,10},{9,11},{10,... | collective-permute-start | bytes 589832 | tf_op jit(solution)/shard_map/ppermute | solution.py:319

commit v17 on v14

--- a/solution.py
+++ b/solution.py
@@ -10,7 +10,7 @@
 EXPERTS = 4
 CAP = 16
 HALVES = 2
-ORDER = (1, 2, 3)
+ORDER = (1, 3, 2)
 FORTH = (7, 5)
 BACK = (1, 1)
 BLOCK = 512
@@ -249,17 +249,34 @@
     return out[:ahead], out[ahead:]
 
 
-def mix_kernel(group, ids_ref, logits_ref, act_ref, arrived, near, last, *refs):
-    out_ref, kept, middle_rows = refs[-1], refs[:HALVES], refs[HALVES:-1]
+def shares_kernel(group, ids_ref, logits_ref, after_ref, out_ref):
     plane = lax.axis_index("expert") // group
     first, second = choices(ids_ref[...], plane)
     lead = logits_ref[0:1, :] - logits_ref[1:2, :]
     weight = jnp.where(first, jax.nn.sigmoid(lead), 0.0)
     weight = (weight + jnp.where(second, jax.nn.sigmoid(-lead), 0.0)).T
-    tokens = weight.shape[0]
     high = weight.astype(jnp.bfloat16).astype(jnp.float32)
     middle = (weight - high).astype(jnp.bfloat16).astype(jnp.float32)
-    terms = jnp.concatenate([weight - high - middle, middle, high], axis=0).astype(jnp.bfloat16)
+    terms = jnp.concatenate([weight - high - middle, middle, high], axis=0)
+    out_ref[...] = terms
+
+
+def shares(group, ids, logits, after):
+    shape = (3 * ids.shape[1], EXPERTS * CAP)
+    return pl.pallas_call(
+        functools.partial(shares_kernel, group),
+        in_specs=[VMEM, VMEM, ANY],
+        out_specs=VMEM,
+        out_shape=jax.ShapeDtypeStruct(shape, jnp.float32),
+        compiler_params=LIMIT,
+        name="shares",
+    )(ids, logits, after)
+
+
+def mix_kernel(terms_ref, act_ref, arrived, near, last, *refs):
+    out_ref, kept, middle_rows = refs[-1], refs[:HALVES], refs[HALVES:-1]
+    tokens = act_ref.shape[0]
+    terms = terms_ref[...].astype(jnp.bfloat16)
     for k, (at, part) in enumerate(spans(act_ref.shape[1], BACK)):
         columns = slice(at, at + part)
         own = kept[k][...].astype(jnp.float32) + arrived[:, columns].astype(jnp.float32)
@@ -272,13 +289,13 @@
         out_ref[:, columns] = total.astype(jnp.bfloat16)
 
 
-def mix(group, ids, logits, activations, pieces):
+def mix(terms, activations, pieces):
     return pl.pallas_call(
-        functools.partial(mix_kernel, group),
+        mix_kernel,
         out_shape=jax.ShapeDtypeStruct(activations.shape, jnp.bfloat16),
         compiler_params=LIMIT,
         name="mix",
-    )(ids, logits, activations, *pieces)
+    )(terms, activations, *pieces)
 
 
 def added(mine, arrived):
@@ -366,7 +383,8 @@
     last = shift(after(added(mine[place[3]], back[3]), middle[0]), -3)
     arrived = back[0]
     pieces = [arrived, near, last, *[h[0] for h in held], *middle]
-    return mix(group, ids, route_logits.T, activations, pieces)
+    terms = shares(group, ids, route_logits.T, hidden)
+    return mix(terms, activations, pieces)
 
 
 def solution(mesh):

time: 75.6 us -> 73.8 us (0.976)
  waiting for transfers between devices: 22.6 us -> 20.8 us
    ppermute x10, waiting for transfers between devices: 14.7 us -> 12.8 us  [shift(): lax.ppermute(x, 'expert', [(i, (i + s * group) % devices) for i in range(...]
  transfers between devices with their start and end apart: 23 -> 23, of which waited for: 13 -> 15; matrix products, arithmetic and copies ran while one was open for 1% -> 1% of each run, Pallas kernels for 20% -> 21%
where the time goes in v17:
time: 73.8 us; the launch traced here: 73.6 us
  starting transfers between devices  27.3 us (37%)
  Pallas kernels  24.5 us (33%)
  waiting for transfers between devices  20.8 us (28%)
    ppermute x10, starting transfers between devices, shift(): lax.ppermute(x, 'expert', [(i, (i + s * group) % devices) for i in range(...  17 us
    ppermute x10, waiting for transfers between devices, shift(): lax.ppermute(x, 'expert', [(i, (i + s * group) % devices) for i in range(...  12.8 us
    ppermute x13, starting transfers between devices, swap(): return lax.ppermute(x, 'expert', [(i, i ^ bit) for i in range(devices)])  10.3 us
    pallas_call x2, Pallas kernels, gate_up(): pl.pallas_call(functools.partial(gate_up_kernel, len(pieces), len(later),...  9.5 us
    ppermute x13, waiting for transfers between devices, swap(): return lax.ppermute(x, 'expert', [(i, i ^ bit) for i in range(devices)])  7.96 us
    pallas_call x2, Pallas kernels, fetch(): pl.pallas_call(functools.partial(fetch_kernel, at), in_specs=[ANY, ANY],...  6.88 us
    pallas_call x2, Pallas kernels, down(): pl.pallas_call(functools.partial(down_kernel, ahead, segments), in_specs=...  5.29 us
    pallas_call x1, Pallas kernels, pack(): pl.pallas_call(functools.partial(pack_kernel, group), grid=(1,), in_specs...  1.48 us
  transfers between devices with their start and end apart: 23, of which 15 were waited for; matrix products, arithmetic and copies ran while one was open for 1% of the time, Pallas kernels for 21%

profile of v17, /device:TPU:0, one launch (start us, length us, event | category | flops | bytes accessed | tf_op | source)
XLA Modules:
  0.0 73.6 jit_solution(4457825628459706812)
XLA Ops:
  0.0 1.5 %norm_and_pack.1 = (bf16[16,6144]{1,0:T(8,128)(2,1)S(1)}, bf16[16,3584]{1,0:T(8,128)(2,1)S(1)}, bf16[16,3584]{1,0:T(8,128)(2,1)S(1)}, bf16[16,3584]{1,0:T(8,128)...) custom-call(s32[2,24]{1,0:T(2,128)} %bitcast.3, ...), custom_call_target="tpu_custom_call" | custom-call | tf_op jit(solution)/shard_map/norm_and_pack/pallas_call | solution.py:67
  1.5 3.1 %collective-permute-start.1 = (bf16[16,3584]{1,0:T(8,128)(2,1)S(1)}, bf16[16,3584]{1,0:T(8,128)(2,1)S(1)}, u32[]{:S(2)}, u32[]{:S(2)}) collective-permute-start(bf16[16,3584]{1,0:T(8,128)(2,1)S(1)} %get-tuple-element.45), channel_id=1, source_target_pairs={{0,4},{1,5},{2,6},{3,7},{4,8},{5,9},{6,10},{7,11},{8,12},{9,13},{1... | collective-permute-start | bytes 344072 | tf_op jit(solution)/shard_map/ppermute | solution.py:314
  4.6 2.1 %collective-permute-start.2 = (bf16[16,3584]{1,0:T(8,128)(2,1)S(1)}, bf16[16,3584]{1,0:T(8,128)(2,1)S(1)}, u32[]{:S(2)}, u32[]{:S(2)}) collective-permute-start(bf16[16,3584]{1,0:T(8,128)(2,1)S(1)} %get-tuple-element.46), channel_id=1, source_target_pairs={{0,12},{1,13},{2,14},{3,15},{4,0},{5,1},{6,2},{7,3},{8,4},{9,5},{1... | collective-permute-start | bytes 344072 | tf_op jit(solution)/shard_map/ppermute | solution.py:314
  6.7 0.9 %collective-permute-start.3 = (bf16[16,3584]{1,0:T(8,128)(2,1)S(1)}, bf16[16,3584]{1,0:T(8,128)(2,1)S(1)}, u32[]{:S(2)}, u32[]{:S(2)}) collective-permute-start(bf16[16,3584]{1,0:T(8,128)(2,1)S(1)} %get-tuple-element.47), channel_id=1, source_target_pairs={{0,8},{1,9},{2,10},{3,11},{4,12},{5,13},{6,14},{7,15},{8,0},{9,1},... | collective-permute-start | bytes 344072 | tf_op jit(solution)/shard_map/ppermute | solution.py:314
  7.6 1.5 %collective-permute-start = (bf16[16,6144]{1,0:T(8,128)(2,1)S(1)}, bf16[16,6144]{1,0:T(8,128)(2,1)S(1)}, u32[]{:S(2)}, u32[]{:S(2)}) collective-permute-start(bf16[16,6144]{1,0:T(8,128)(2,1)S(1)} %get-tuple-element.38.after_ref.refs_0_), channel_id=1, source_target_pairs={{0,2},{1,3},{2,0},{3,1},{4,6},{5,7},{6,4},{7,5},{8,10},{9,11},{10,... | collective-permute-start | bytes 589832 | tf_op jit(solution)/shard_map/ppermute | solution.py:319
  9.2 3.4 %fetch.3.refs_6_ = bf16[1152,3584]{1,0:T(8,128)(2,1)S(1)} custom-call(bf16[1152,6144]{1,0:T(8,128)(2,1)} %refs_8_.2, bf16[16,6144]{1,0:T(8,128)(2,1)S(1)} %get-tuple-element.38.after_ref.refs_0_), custom_call_target="tpu_custom_call" | custom-call | bytes 16515072 | tf_op jit(solution)/shard_map/fetch/pallas_call | solution.py:100
  12.6 3.4 %fetch.2.refs_5_ = bf16[1152,3584]{1,0:T(8,128)(2,1)S(1)} custom-call(bf16[1152,6144]{1,0:T(8,128)(2,1)} %refs_7_.1, bf16[16,6144]{1,0:T(8,128)(2,1)S(1)} %get-tuple-element.38.after_ref.refs_0_), custom_call_target="tpu_custom_call" | custom-call | bytes 16515072 | tf_op jit(solution)/shard_map/fetch/pallas_call | solution.py:100
  16.0 0.0 collective-permute-done.1
  16.1 0.0 collective-permute-done.2
  16.1 1.0 %collective-permute-done.3 = bf16[16,3584]{1,0:T(8,128)(2,1)S(1)} collective-permute-done((bf16[16,3584]{1,0:T(8,128)(2,1)S(1)}, bf16[16,3584]{1,0:T(8,128)(2,1)S(1)}, u32[]{:S(2)}, u32[]{:S(2)}) %collective-permute-start.3) | collective-permute-done | bytes 114720 | tf_op jit(solution)/shard_map/ppermute | solution.py:314
  17.1 1.6 %collective-permute-start.8 = (bf16[48,3584]{1,0:T(8,128)(2,1)S(1)}, bf16[48,3584]{1,0:T(8,128)(2,1)S(1)}, u32[]{:S(2)}, u32[]{:S(2)}) collective-permute-start(bf16[48,3584]{1,0:T(8,128)(2,1)S(1)} %get-tuple-element.51.refs_3_.refs_1_), channel_id=1, source_target_pairs={{0,2},{1,3},{2,0},{3,1},{4,6},{5,7},{6,4},{7,5},{8,10},{9,11},{10,... | collective-permute-start | bytes 1032200 | tf_op jit(solution)/shard_map/ppermute | solution.py:319
  18.7 0.0 collective-permute-done.refs_2_
  18.7 0.1 collective-permute-start.4
  18.8 3.8 %collective-permute-start.5 = (bf16[16,2560]{1,0:T(8,128)(2,1)S(1)}, bf16[16,2560]{1,0:T(8,128)(2,1)S(1)}, u32[]{:S(2)}, u32[]{:S(2)}) collective-permute-start(bf16[16,2560]{1,0:T(8,128)(2,1)S(1)} %get-tuple-element.49), channel_id=1, source_target_pairs={{0,12},{1,13},{2,14},{3,15},{4,0},{5,1},{6,2},{7,3},{8,4},{9,5},{1... | collective-permute-start | bytes 245768 | tf_op jit(solution)/shard_map/ppermute | solution.py:314
  22.6 0.0 collective-permute-start.6
  22.6 3.3 %collective-permute-done.4 = bf16[16,2560]{1,0:T(8,128)(2,1)S(1)} collective-permute-done((bf16[16,2560]{1,0:T(8,128)(2,1)S(1)}, bf16[16,2560]{1,0:T(8,128)(2,1)S(1)}, u32[]{:S(2)}, u32[]{:S(2)}) %collective-permute-start.4) | collective-permute-done | bytes 81952 | tf_op jit(solution)/shard_map/ppermute | solution.py:314
  26.0 0.0 collective-permute-done.5
  26.0 1.2 %collective-permute-done.8.refs_3_ = bf16[48,3584]{1,0:T(8,128)(2,1)S(1)} collective-permute-done((bf16[48,3584]{1,0:T(8,128)(2,1)S(1)}, bf16[48,3584]{1,0:T(8,128)(2,1)S(1)}, u32[]{:S(2)}, u32[]{:S(2)}) %collective-permute-start.8) | collective-permute-done | bytes 344096 | tf_op jit(solution)/shard_map/ppermute | solution.py:319
  27.2 0.1 collective-permute-start.9
  27.3 1.7 %collective-permute-done.6 = bf16[16,2560]{1,0:T(8,128)(2,1)S(1)} collective-permute-done((bf16[16,2560]{1,0:T(8,128)(2,1)S(1)}, bf16[16,2560]{1,0:T(8,128)(2,1)S(1)}, u32[]{:S(2)}, u32[]{:S(2)}) %collective-permute-start.6) | collective-permute-done | bytes 81952 | tf_op jit(solution)/shard_map/ppermute | solution.py:314
  29.0 0.6 collective-permute-start.7
  29.6 0.0 collective-permute-start.10
  29.7 0.1 collective-permute-done.9.refs_4_
  29.7 5.5 %gate_up.2 = (bf16[1152,2560]{1,0:T(8,128)(2,1)S(1)}, bf16[1152,2560]{1,0:T(8,128)(2,1)S(1)}, f32[1152,256]{1,0:T(8,128)S(1)}, f32[1152,256]{1,0:T(8,128)S(1)}) custom-call(bf16[16,6144]{1,0:T(8,128)(2,1)S(1)} %get-tuple-element.38.after_ref.refs_0_, bf16[48,3584]{1,0:T(8,128)(2,1)S(1)} %get-tuple-element.51.refs_3_.refs_1_, ...), custom_call_target="tpu_custom_call" | custom-call | flops 4227858432 | bytes 18874368 | tf_op jit(solution)/shard_map/gate_up/pallas_call | solution.py:182
  35.2 0.5 collective-permute-done.7.refs_3_
  35.7 0.0 collective-permute-start.11
  35.7 0.0 collective-permute-done.10.refs_4_
  35.7 1.5 %collective-permute-done.11.refs_5_ = bf16[48,2560]{1,0:T(8,128)(2,1)S(1)} collective-permute-done((bf16[48,2560]{1,0:T(8,128)(2,1)S(1)}, bf16[48,2560]{1,0:T(8,128)(2,1)S(1)}, u32[]{:S(2)}, u32[]{:S(2)}) %collective-permute-start.11) | collective-permute-done | bytes 245792 | tf_op jit(solution)/shard_map/ppermute | solution.py:319
  37.2 4.0 %gate_up.3 = (bf16[1152,4096]{1,0:T(8,128)(2,1)S(1)}, bf16[256,1152]{1,0:T(8,128)(2,1)S(1)}) custom-call(bf16[16,6144]{1,0:T(8,128)(2,1)S(1)} %get-tuple-element.38.after_ref.refs_0_, bf16[48,2560]{1,0:T(8,128)(2,1)S(1)} %get-tuple-element.92.refs_1_, bf16[16,6144]{1,0:T(8,128)(2,1)S(1)} %collective-permute-done.refs_2_, ...), custom_call_target="tpu_custom_call" | custom-call | flops 3019898880 | bytes 14155776 | tf_op jit(solution)/shard_map/gate_up/pallas_call | solution.py:182
  41.2 2.5 %down.2 = (bf16[1152,2048]{1,0:T(8,128)(2,1)S(1)}, bf16[128,3072]{1,0:T(8,128)(2,1)S(1)}, bf16[128,3072]{1,0:T(8,128)(2,1)S(1)}) custom-call(bf16[256,1152]{1,0:T(8,128)(2,1)S(1)} %get-tuple-element.59.after_ref.hidden_ref, bf16[1152,4096]{1,0:T(8,128)(2,1)S(1)} %get-tuple-element.60.refs_0_, bf16[1152,6144]{1,0:T(8,128)(2,1)} %refs_1_.1), custom_call_target="tpu_custom_call" | custom-call | flops 1811939328 | bytes 9240576 | tf_op jit(solution)/shard_map/down/pallas_call | solution.py:235
  43.8 0.2 collective-permute-start.12
  44.0 2.8 %down.3 = (bf16[128,3072]{1,0:T(8,128)(2,1)S(1)}, bf16[128,3072]{1,0:T(8,128)(2,1)S(1)}) custom-call(bf16[256,1152]{1,0:T(8,128)(2,1)S(1)} %get-tuple-element.59.after_ref.hidden_ref, bf16[1152,4096]{1,0:T(8,128)(2,1)S(1)} %get-tuple-element.60.refs_0_, bf16[1152,2048]{1,0:T(8,128)(2,1)S(1)} %get-tuple-element.63.refs_1_), custom_call_target="tpu_custom_call" | custom-call | flops 1811939328 | bytes 9240576 | tf_op jit(solution)/shard_map/down/pallas_call | solution.py:235
  46.8 0.4 collective-permute-start.13
  47.2 0.0 collective-permute-done.12
  47.2 0.0 copy-start.1
  47.2 0.0 copy-start.2
  47.2 0.2 add_convert_fusion.1
  47.4 0.0 copy-start
  47.5 1.5 %collective-permute-start.16 = (bf16[16,3072]{1,0:T(8,128)(2,1)S(1)}, bf16[16,3072]{1,0:T(8,128)(2,1)S(1)}, u32[]{:S(2)}, u32[]{:S(2)}) collective-permute-start(bf16[16,3072]{1,0:T(8,128)(2,1)S(1)} %get-tuple-element.81), channel_id=1, source_target_pairs={{0,2},{1,3},{2,0},{3,1},{4,6},{5,7},{6,4},{7,5},{8,10},{9,11},{10,... | collective-permute-start | bytes 294920 | tf_op jit(solution)/shard_map/ppermute | solution.py:319
  49.0 0.1 collective-permute-done.13
  49.1 0.2 add_convert_fusion
  49.4 1.5 %collective-permute-start.14 = (bf16[16,3072]{1,0:T(8,128)(2,1)S(1)}, bf16[16,3072]{1,0:T(8,128)(2,1)S(1)}, u32[]{:S(2)}, u32[]{:S(2)}) collective-permute-start(bf16[16,3072]{1,0:T(8,128)(2,1)S(1)} %get-tuple-element.75), channel_id=1, source_target_pairs={{0,2},{1,3},{2,0},{3,1},{4,6},{5,7},{6,4},{7,5},{8,10},{9,11},{10,... | collective-permute-start | bytes 294920 | tf_op jit(solution)/shard_map/ppermute | solution.py:319
  50.9 1.4 %collective-permute-done.16 = bf16[16,3072]{1,0:T(8,128)(2,1)S(1)} collective-permute-done((bf16[16,3072]{1,0:T(8,128)(2,1)S(1)}, bf16[16,3072]{1,0:T(8,128)(2,1)S(1)}, u32[]{:S(2)}, u32[]{:S(2)}) %collective-permute-start.16) | collective-permute-done | bytes 98336 | tf_op jit(solution)/shard_map/ppermute | solution.py:319
  52.4 0.7 collective-permute-start.21
  53.1 0.9 %collective-permute-start.17 = (bf16[16,6144]{1,0:T(8,128)(2,1)S(1)}, bf16[16,6144]{1,0:T(8,128)(2,1)S(1)}, u32[]{:S(2)}, u32[]{:S(2)}) collective-permute-start(bf16[16,6144]{1,0:T(8,128)(2,1)S(1)} %get-tuple-element.67), channel_id=1, source_target_pairs={{0,2},{1,3},{2,0},{3,1},{4,6},{5,7},{6,4},{7,5},{8,10},{9,11},{10,... | collective-permute-start | bytes 589832 | tf_op jit(solution)/shard_map/ppermute | solution.py:319
  54.0 0.5 collective-permute-done.14
  54.5 2.4 %collective-permute-start.19 = (bf16[16,3072]{1,0:T(8,128)(2,1)S(1)}, bf16[16,3072]{1,0:T(8,128)(2,1)S(1)}, u32[]{:S(2)}, u32[]{:S(2)}) collective-permute-start(bf16[16,3072]{1,0:T(8,128)(2,1)S(1)} %add_convert_fusion.5), channel_id=1, source_target_pairs={{0,8},{1,9},{2,10},{3,11},{4,12},{5,13},{6,14},{7,15},{8,0},{9,1},... | collective-permute-start | bytes 294920 | tf_op jit(solution)/shard_map/ppermute | solution.py:314
  56.9 0.6 collective-permute-start.15
  57.5 2.3 %collective-permute-done.17 = bf16[16,6144]{1,0:T(8,128)(2,1)S(1)} collective-permute-done((bf16[16,6144]{1,0:T(8,128)(2,1)S(1)}, bf16[16,6144]{1,0:T(8,128)(2,1)S(1)}, u32[]{:S(2)}, u32[]{:S(2)}) %collective-permute-start.17) | collective-permute-done | bytes 196640 | tf_op jit(solution)/shard_map/ppermute | solution.py:319
  59.9 1.5 %collective-permute-done.21.refs_2_ = bf16[16,3072]{1,0:T(8,128)(2,1)S(1)} collective-permute-done((bf16[16,3072]{1,0:T(8,128)(2,1)S(1)}, bf16[16,3072]{1,0:T(8,128)(2,1)S(1)}, u32[]{:S(2)}, u32[]{:S(2)}) %collective-permute-start.21) | collective-permute-done | bytes 98336 | tf_op jit(solution)/shard_map/ppermute | solution.py:314
  61.4 1.4 %collective-permute-start.22 = (bf16[16,6144]{1,0:T(8,128)(2,1)S(1)}, bf16[16,6144]{1,0:T(8,128)(2,1)S(1)}, u32[]{:S(2)}, u32[]{:S(2)}) collective-permute-start(bf16[16,6144]{1,0:T(8,128)(2,1)S(1)} %add_convert_fusion.2), channel_id=1, source_target_pairs={{0,4},{1,5},{2,6},{3,7},{4,8},{5,9},{6,10},{7,11},{8,12},{9,13},{1... | collective-permute-start | bytes 589832 | tf_op jit(solution)/shard_map/ppermute | solution.py:314
  62.8 0.4 collective-permute-done.15
  63.2 0.0 collective-permute-done.19.refs_3_
  63.2 1.3 %collective-permute-start.18 = (bf16[16,6144]{1,0:T(8,128)(2,1)S(1)}, bf16[16,6144]{1,0:T(8,128)(2,1)S(1)}, u32[]{:S(2)}, u32[]{:S(2)}) collective-permute-start(bf16[16,6144]{1,0:T(8,128)(2,1)S(1)} %pad_maximum_fusion), channel_id=1, source_target_pairs={{0,2},{1,3},{2,0},{3,1},{4,6},{5,7},{6,4},{7,5},{8,10},{9,11},{10,... | collective-permute-start | bytes 589832 | tf_op jit(solution)/shard_map/ppermute | solution.py:319
  64.5 2.5 %collective-permute-start.20 = (bf16[16,6144]{1,0:T(8,128)(2,1)S(1)}, bf16[16,6144]{1,0:T(8,128)(2,1)S(1)}, u32[]{:S(2)}, u32[]{:S(2)}) collective-permute-start(bf16[16,6144]{1,0:T(8,128)(2,1)S(1)} %add_convert_fusion.3), channel_id=1, source_target_pairs={{0,12},{1,13},{2,14},{3,15},{4,0},{5,1},{6,2},{7,3},{8,4},{9,5},{1... | collective-permute-start | bytes 589832 | tf_op jit(solution)/shard_map/ppermute | solution.py:314
  67.0 0.0 copy-done.1
  67.0 0.0 copy-done.2
  67.0 0.2 shares.1.terms_ref
  67.2 3.5 %collective-permute-done.22.last = bf16[16,6144]{1,0:T(8,128)(2,1)S(1)} collective-permute-done((bf16[16,6144]{1,0:T(8,128)(2,1)S(1)}, bf16[16,6144]{1,0:T(8,128)(2,1)S(1)}, u32[]{:S(2)}, u32[]{:S(2)}) %collective-permute-start.22) | collective-permute-done | bytes 196640 | tf_op jit(solution)/shard_map/ppermute | solution.py:314
  70.7 0.0 collective-permute-done.18.arrived
  70.7 1.8 %collective-permute-done.20.near = bf16[16,6144]{1,0:T(8,128)(2,1)S(1)} collective-permute-done((bf16[16,6144]{1,0:T(8,128)(2,1)S(1)}, bf16[16,6144]{1,0:T(8,128)(2,1)S(1)}, u32[]{:S(2)}, u32[]{:S(2)}) %collective-permute-start.20) | collective-permute-done | bytes 196640 | tf_op jit(solution)/shard_map/ppermute | solution.py:314
  72.5 0.0 copy-done
  72.5 1.1 %mix.1 = bf16[24,6144]{1,0:T(8,128)(2,1)} custom-call(f32[72,64]{1,0:T(8,128)S(1)} %shares.1.terms_ref, bf16[24,6144]{1,0:T(8,128)(2,1)S(1)} %copy-done, bf16[16,6144]{1,0:T(8,128)(2,1)S(1)} %collective-permute-done.18.arrived, bf16[16,6144]{1,0:T(8,128)(2,1)S(1)} %collective-permute-done.20.near, bf16[16,6144]{1,0:T(8,128)(2,1)S(1)} %collective-permute-done.22.last, ...), custom_call_target="tpu_custom_call" | custom-call | tf_op jit(solution)/shard_map/mix/pallas_call | solution.py:293
  (20 shorter events, 0.4 us)
Async XLA Ops:
  1.5 14.6 %collective-permute-start.1 = (bf16[16,3584]{1,0:T(8,128)(2,1)S(1)}, bf16[16,3584]{1,0:T(8,128)(2,1)S(1)}, u32[]{:S(2)}, u32[]{:S(2)}) collective-permute-start(bf16[16,3584]{1,0:T(8,128)(2,1)S(1)} %get-tuple-element.45), channel_id=1, source_target_pairs={{0,4},{1,5},{2,6},{3,7},{4,8},{5,9},{6,10},{7,11},{8,12},{9,13},{1... | collective-permute-start | bytes 344072 | tf_op jit(solution)/shard_map/ppermute | solution.py:314
  4.6 11.5 %collective-permute-start.2 = (bf16[16,3584]{1,0:T(8,128)(2,1)S(1)}, bf16[16,3584]{1,0:T(8,128)(2,1)S(1)}, u32[]{:S(2)}, u32[]{:S(2)}) collective-permute-start(bf16[16,3584]{1,0:T(8,128)(2,1)S(1)} %get-tuple-element.46), channel_id=1, source_target_pairs={{0,12},{1,13},{2,14},{3,15},{4,0},{5,1},{6,2},{7,3},{8,4},{9,5},{1... | collective-permute-start | bytes 344072 | tf_op jit(solution)/shard_map/ppermute | solution.py:314
  6.7 10.4 %collective-permute-start.3 = (bf16[16,3584]{1,0:T(8,128)(2,1)S(1)}, bf16[16,3584]{1,0:T(8,128)(2,1)S(1)}, u32[]{:S(2)}, u32[]{:S(2)}) collective-permute-start(bf16[16,3584]{1,0:T(8,128)(2,1)S(1)} %get-tuple-element.47), channel_id=1, source_target_pairs={{0,8},{1,9},{2,10},{3,11},{4,12},{5,13},{6,14},{7,15},{8,0},{9,1},... | collective-permute-start | bytes 344072 | tf_op jit(solution)/shard_map/ppermute | solution.py:314
  7.6 11.1 %collective-permute-start = (bf16[16,6144]{1,0:T(8,128)(2,1)S(1)}, bf16[16,6144]{1,0:T(8,128)(2,1)S(1)}, u32[]{:S(2)}, u32[]{:S(2)}) collective-permute-start(bf16[16,6144]{1,0:T(8,128)(2,1)S(1)} %get-tuple-element.38.after_ref.refs_0_), channel_id=1, source_target_pairs={{0,2},{1,3},{2,0},{3,1},{4,6},{5,7},{6,4},{7,5},{8,10},{9,11},{10,... | collective-permute-start | bytes 589832 | tf_op jit(solution)/shard_map/ppermute | solution.py:319
  17.1 10.0 %collective-permute-start.8 = (bf16[48,3584]{1,0:T(8,128)(2,1)S(1)}, bf16[48,3584]{1,0:T(8,128)(2,1)S(1)}, u32[]{:S(2)}, u32[]{:S(2)}) collective-permute-start(bf16[48,3584]{1,0:T(8,128)(2,1)S(1)} %get-tuple-element.51.refs_3_.refs_1_), channel_id=1, source_target_pairs={{0,2},{1,3},{2,0},{3,1},{4,6},{5,7},{6,4},{7,5},{8,10},{9,11},{10,... | collective-permute-start | bytes 1032200 | tf_op jit(solution)/shard_map/ppermute | solution.py:319
  18.7 7.2 %collective-permute-start.4 = (bf16[16,2560]{1,0:T(8,128)(2,1)S(1)}, bf16[16,2560]{1,0:T(8,128)(2,1)S(1)}, u32[]{:S(2)}, u32[]{:S(2)}) collective-permute-start(bf16[16,2560]{1,0:T(8,128)(2,1)S(1)} %get-tuple-element.48), channel_id=1, source_target_pairs={{0,4},{1,5},{2,6},{3,7},{4,8},{5,9},{6,10},{7,11},{8,12},{9,13},{1... | collective-permute-start | bytes 245768 | tf_op jit(solution)/shard_map/ppermute | solution.py:314
  18.8 7.2 %collective-permute-start.5 = (bf16[16,2560]{1,0:T(8,128)(2,1)S(1)}, bf16[16,2560]{1,0:T(8,128)(2,1)S(1)}, u32[]{:S(2)}, u32[]{:S(2)}) collective-permute-start(bf16[16,2560]{1,0:T(8,128)(2,1)S(1)} %get-tuple-element.49), channel_id=1, source_target_pairs={{0,12},{1,13},{2,14},{3,15},{4,0},{5,1},{6,2},{7,3},{8,4},{9,5},{1... | collective-permute-start | bytes 245768 | tf_op jit(solution)/shard_map/ppermute | solution.py:314
  22.6 6.3 %collective-permute-start.6 = (bf16[16,2560]{1,0:T(8,128)(2,1)S(1)}, bf16[16,2560]{1,0:T(8,128)(2,1)S(1)}, u32[]{:S(2)}, u32[]{:S(2)}) collective-permute-start(bf16[16,2560]{1,0:T(8,128)(2,1)S(1)} %get-tuple-element.50), channel_id=1, source_target_pairs={{0,8},{1,9},{2,10},{3,11},{4,12},{5,13},{6,14},{7,15},{8,0},{9,1},... | collective-permute-start | bytes 245768 | tf_op jit(solution)/shard_map/ppermute | solution.py:314
  27.2 2.5 %collective-permute-start.9 = (bf16[128,3584]{1,0:T(8,128)(2,1)S(1)}, bf16[128,3584]{1,0:T(8,128)(2,1)S(1)}, u32[]{:S(2)}, u32[]{:S(2)}) collective-permute-start(bf16[128,3584]{1,0:T(8,128)(2,1)S(1)} %constant_dynamic-update-slice_fusion.6), channel_id=1, source_target_pairs={{0,1},{1,0},{2,3},{3,2},{4,5},{5,4},{6,7},{7,6},{8,9},{9,8},{10,11... | collective-permute-start | bytes 2752520 | tf_op jit(solution)/shard_map/ppermute | solution.py:319
  29.0 6.7 %collective-permute-start.7 = (bf16[48,2560]{1,0:T(8,128)(2,1)S(1)}, bf16[48,2560]{1,0:T(8,128)(2,1)S(1)}, u32[]{:S(2)}, u32[]{:S(2)}) collective-permute-start(bf16[48,2560]{1,0:T(8,128)(2,1)S(1)} %get-tuple-element.92.refs_1_), channel_id=1, source_target_pairs={{0,2},{1,3},{2,0},{3,1},{4,6},{5,7},{6,4},{7,5},{8,10},{9,11},{10,... | collective-permute-start | bytes 737288 | tf_op jit(solution)/shard_map/ppermute | solution.py:319
  29.6 6.1 %collective-permute-start.10 = (bf16[80,2560]{1,0:T(8,128)(2,1)S(1)}, bf16[80,2560]{1,0:T(8,128)(2,1)S(1)}, u32[]{:S(2)}, u32[]{:S(2)}) collective-permute-start(bf16[80,2560]{1,0:T(8,128)(2,1)S(1)} %slice_dynamic-update-slice_fusion.2), channel_id=1, source_target_pairs={{0,1},{1,0},{2,3},{3,2},{4,5},{5,4},{6,7},{7,6},{8,9},{9,8},{10,11... | collective-permute-start | bytes 1228808 | tf_op jit(solution)/shard_map/ppermute | solution.py:319
  35.7 1.5 %collective-permute-start.11 = (bf16[48,2560]{1,0:T(8,128)(2,1)S(1)}, bf16[48,2560]{1,0:T(8,128)(2,1)S(1)}, u32[]{:S(2)}, u32[]{:S(2)}) collective-permute-start(bf16[48,2560]{1,0:T(8,128)(2,1)S(1)} %collective-permute-done.7.refs_3_), channel_id=1, source_target_pairs={{0,1},{1,0},{2,3},{3,2},{4,5},{5,4},{6,7},{7,6},{8,9},{9,8},{10,11... | collective-permute-start | bytes 737288 | tf_op jit(solution)/shard_map/ppermute | solution.py:319
  43.8 3.4 %collective-permute-start.12 = (bf16[128,3072]{1,0:T(8,128)(2,1)S(1)}, bf16[128,3072]{1,0:T(8,128)(2,1)S(1)}, u32[]{:S(2)}, u32[]{:S(2)}) collective-permute-start(bf16[128,3072]{1,0:T(8,128)(2,1)S(1)} %get-tuple-element.62), channel_id=1, source_target_pairs={{0,1},{1,0},{2,3},{3,2},{4,5},{5,4},{6,7},{7,6},{8,9},{9,8},{10,11... | collective-permute-start | bytes 2359304 | tf_op jit(solution)/shard_map/ppermute | solution.py:319
  46.8 2.4 %collective-permute-start.13 = (bf16[128,3072]{1,0:T(8,128)(2,1)S(1)}, bf16[128,3072]{1,0:T(8,128)(2,1)S(1)}, u32[]{:S(2)}, u32[]{:S(2)}) collective-permute-start(bf16[128,3072]{1,0:T(8,128)(2,1)S(1)} %get-tuple-element.65), channel_id=1, source_target_pairs={{0,1},{1,0},{2,3},{3,2},{4,5},{5,4},{6,7},{7,6},{8,9},{9,8},{10,11... | collective-permute-start | bytes 2359304 | tf_op jit(solution)/shard_map/ppermute | solution.py:319
  47.2 19.8 %copy-start.1 = (s32[24,2]{0,1:T(2,128)S(1)}, s32[24,2]{0,1:T(2,128)}, u32[]{:S(2)}) copy-start(s32[24,2]{0,1:T(2,128)} %param.8) | copy-start | bytes 580
  47.2 19.8 %copy-start.2 = (f32[24,2]{0,1:T(2,128)S(1)}, f32[24,2]{0,1:T(2,128)}, u32[]{:S(2)}) copy-start(f32[24,2]{0,1:T(2,128)} %param.9) | copy-start | bytes 580
  47.4 25.1 %copy-start = (bf16[24,6144]{1,0:T(8,128)(2,1)S(1)}, bf16[24,6144]{1,0:T(8,128)(2,1)}, u32[]{:S(2)}) copy-start(bf16[24,6144]{1,0:T(8,128)(2,1)} %act_ref.3) | copy-start | bytes 884740
  47.5 4.9 %collective-permute-start.16 = (bf16[16,3072]{1,0:T(8,128)(2,1)S(1)}, bf16[16,3072]{1,0:T(8,128)(2,1)S(1)}, u32[]{:S(2)}, u32[]{:S(2)}) collective-permute-start(bf16[16,3072]{1,0:T(8,128)(2,1)S(1)} %get-tuple-element.81), channel_id=1, source_target_pairs={{0,2},{1,3},{2,0},{3,1},{4,6},{5,7},{6,4},{7,5},{8,10},{9,11},{10,... | collective-permute-start | bytes 294920 | tf_op jit(solution)/shard_map/ppermute | solution.py:319
  49.4 5.1 %collective-permute-start.14 = (bf16[16,3072]{1,0:T(8,128)(2,1)S(1)}, bf16[16,3072]{1,0:T(8,128)(2,1)S(1)}, u32[]{:S(2)}, u32[]{:S(2)}) collective-permute-start(bf16[16,3072]{1,0:T(8,128)(2,1)S(1)} %get-tuple-element.75), channel_id=1, source_target_pairs={{0,2},{1,3},{2,0},{3,1},{4,6},{5,7},{6,4},{7,5},{8,10},{9,11},{10,... | collective-permute-start | bytes 294920 | tf_op jit(solution)/shard_map/ppermute | solution.py:319
  52.4 9.0 %collective-permute-start.21 = (bf16[16,3072]{1,0:T(8,128)(2,1)S(1)}, bf16[16,3072]{1,0:T(8,128)(2,1)S(1)}, u32[]{:S(2)}, u32[]{:S(2)}) collective-permute-start(bf16[16,3072]{1,0:T(8,128)(2,1)S(1)} %add_convert_fusion.4), channel_id=1, source_target_pairs={{0,8},{1,9},{2,10},{3,11},{4,12},{5,13},{6,14},{7,15},{8,0},{9,1},... | collective-permute-start | bytes 294920 | tf_op jit(solution)/shard_map/ppermute | solution.py:314
  53.1 6.7 %collective-permute-start.17 = (bf16[16,6144]{1,0:T(8,128)(2,1)S(1)}, bf16[16,6144]{1,0:T(8,128)(2,1)S(1)}, u32[]{:S(2)}, u32[]{:S(2)}) collective-permute-start(bf16[16,6144]{1,0:T(8,128)(2,1)S(1)} %get-tuple-element.67), channel_id=1, source_target_pairs={{0,2},{1,3},{2,0},{3,1},{4,6},{5,7},{6,4},{7,5},{8,10},{9,11},{10,... | collective-permute-start | bytes 589832 | tf_op jit(solution)/shard_map/ppermute | solution.py:319
  54.5 8.7 %collective-permute-start.19 = (bf16[16,3072]{1,0:T(8,128)(2,1)S(1)}, bf16[16,3072]{1,0:T(8,128)(2,1)S(1)}, u32[]{:S(2)}, u32[]{:S(2)}) collective-permute-start(bf16[16,3072]{1,0:T(8,128)(2,1)S(1)} %add_convert_fusion.5), channel_id=1, source_target_pairs={{0,8},{1,9},{2,10},{3,11},{4,12},{5,13},{6,14},{7,15},{8,0},{9,1},... | collective-permute-start | bytes 294920 | tf_op jit(solution)/shard_map/ppermute | solution.py:314
  56.9 6.2 %collective-permute-start.15 = (bf16[16,6144]{1,0:T(8,128)(2,1)S(1)}, bf16[16,6144]{1,0:T(8,128)(2,1)S(1)}, u32[]{:S(2)}, u32[]{:S(2)}) collective-permute-start(bf16[16,6144]{1,0:T(8,128)(2,1)S(1)} %get-tuple-element.66), channel_id=1, source_target_pairs={{0,2},{1,3},{2,0},{3,1},{4,6},{5,7},{6,4},{7,5},{8,10},{9,11},{10,... | collective-permute-start | bytes 589832 | tf_op jit(solution)/shard_map/ppermute | solution.py:319
  61.4 9.3 %collective-permute-start.22 = (bf16[16,6144]{1,0:T(8,128)(2,1)S(1)}, bf16[16,6144]{1,0:T(8,128)(2,1)S(1)}, u32[]{:S(2)}, u32[]{:S(2)}) collective-permute-start(bf16[16,6144]{1,0:T(8,128)(2,1)S(1)} %add_convert_fusion.2), channel_id=1, source_target_pairs={{0,4},{1,5},{2,6},{3,7},{4,8},{5,9},{6,10},{7,11},{8,12},{9,13},{1... | collective-permute-start | bytes 589832 | tf_op jit(solution)/shard_map/ppermute | solution.py:314
  63.2 7.5 %collective-permute-start.18 = (bf16[16,6144]{1,0:T(8,128)(2,1)S(1)}, bf16[16,6144]{1,0:T(8,128)(2,1)S(1)}, u32[]{:S(2)}, u32[]{:S(2)}) collective-permute-start(bf16[16,6144]{1,0:T(8,128)(2,1)S(1)} %pad_maximum_fusion), channel_id=1, source_target_pairs={{0,2},{1,3},{2,0},{3,1},{4,6},{5,7},{6,4},{7,5},{8,10},{9,11},{10,... | collective-permute-start | bytes 589832 | tf_op jit(solution)/shard_map/ppermute | solution.py:319
  64.5 8.0 %collective-permute-start.20 = (bf16[16,6144]{1,0:T(8,128)(2,1)S(1)}, bf16[16,6144]{1,0:T(8,128)(2,1)S(1)}, u32[]{:S(2)}, u32[]{:S(2)}) collective-permute-start(bf16[16,6144]{1,0:T(8,128)(2,1)S(1)} %add_convert_fusion.3), channel_id=1, source_target_pairs={{0,12},{1,13},{2,14},{3,15},{4,0},{5,1},{6,2},{7,3},{8,4},{9,5},{1... | collective-permute-start | bytes 589832 | tf_op jit(solution)/shard_map/ppermute | solution.py:314

commit v18 on v17

--- a/solution.py
+++ b/solution.py
@@ -208,9 +208,9 @@
         copy.start()
     done = 0
     for w_ref, (first, size) in zip(weights, segments):
-        block = size // 2
-
-        @pl.loop(0, 2)
+        block = size if size <= 2 * BLOCK else size // 2
+
+        @pl.loop(0, size // block)
         def _(c, first=first, done=done, block=block, w_ref=w_ref):
             columns = pl.ds(pl.multiple_of(first + c * block, BLOCK), block)
             out = jnp.dot(hidden_ref[...], w_ref[:, columns], preferred_element_type=jnp.float32)
@@ -324,8 +324,11 @@
     others = EXPERTS - 1
     ids = expert_ids.T
     own, *sends = pack(group, ids, activations, norm_gain)
-    far_own = swap(own, far)
-    now = [fetch(w, 0, spans(width)[0][1], own) for w in (w_gate, w_up)]
+    size = spans(width)[0][1]
+    now = [fetch(w_gate, 0, size, own)]
+    fetched = after(own, *now)
+    far_own = swap(fetched, far)
+    now.append(fetch(w_up, 0, size, fetched))
     blocks = []
     for k in range(HALVES):
         x = sends[k * others : (k + 1) * others]

time: 73.8 us -> 73.7 us (level)
  starting transfers between devices: 27.3 us -> 25.6 us
  waiting for transfers between devices: 20.8 us -> 22.5 us
    ppermute x10, waiting for transfers between devices: 12.8 us -> 14.9 us  [shift(): lax.ppermute(x, 'expert', [(i, (i + s * group) % devices) for i in range(...]
    ppermute x13, starting transfers between devices: 10.3 us -> 9.33 us  [swap(): return lax.ppermute(x, 'expert', [(i, i ^ bit) for i in range(devices)])]
    ppermute x10, starting transfers between devices: 17 us -> 16.3 us  [shift(): lax.ppermute(x, 'expert', [(i, (i + s * group) % devices) for i in range(...]
where the time goes in v18:
time: 73.7 us; the launch traced here: 73.5 us
  starting transfers between devices  25.6 us (35%)
  Pallas kernels  24.4 us (33%)
  waiting for transfers between devices  22.5 us (31%)
    ppermute x10, starting transfers between devices, shift(): lax.ppermute(x, 'expert', [(i, (i + s * group) % devices) for i in range(...  16.3 us
    ppermute x10, waiting for transfers between devices, shift(): lax.ppermute(x, 'expert', [(i, (i + s * group) % devices) for i in range(...  14.9 us
    pallas_call x2, Pallas kernels, gate_up(): pl.pallas_call(functools.partial(gate_up_kernel, len(pieces), len(later),...  9.56 us
    ppermute x13, starting transfers between devices, swap(): return lax.ppermute(x, 'expert', [(i, i ^ bit) for i in range(devices)])  9.33 us
    ppermute x13, waiting for transfers between devices, swap(): return lax.ppermute(x, 'expert', [(i, i ^ bit) for i in range(devices)])  7.66 us
    pallas_call x2, Pallas kernels, fetch(): pl.pallas_call(functools.partial(fetch_kernel, at), in_specs=[ANY, ANY],...  6.87 us
    pallas_call x2, Pallas kernels, down(): pl.pallas_call(functools.partial(down_kernel, ahead, segments), in_specs=...  5.11 us
    pallas_call x1, Pallas kernels, pack(): pl.pallas_call(functools.partial(pack_kernel, group), grid=(1,), in_specs...  1.48 us
  transfers between devices with their start and end apart: 23, of which 15 were waited for; matrix products, arithmetic and copies ran while one was open for 1% of the time, Pallas kernels for 21%

profile of v18, /device:TPU:0, one launch (start us, length us, event | category | flops | bytes accessed | tf_op | source)
XLA Modules:
  0.0 73.5 jit_solution(10947599958745730893)
XLA Ops:
  0.0 1.5 %norm_and_pack.1 = (bf16[16,6144]{1,0:T(8,128)(2,1)S(1)}, bf16[16,3584]{1,0:T(8,128)(2,1)S(1)}, bf16[16,3584]{1,0:T(8,128)(2,1)S(1)}, bf16[16,3584]{1,0:T(8,128)...) custom-call(s32[2,24]{1,0:T(2,128)} %bitcast.3, ...), custom_call_target="tpu_custom_call" | custom-call | tf_op jit(solution)/shard_map/norm_and_pack/pallas_call | solution.py:67
  1.5 3.1 %collective-permute-start.1 = (bf16[16,3584]{1,0:T(8,128)(2,1)S(1)}, bf16[16,3584]{1,0:T(8,128)(2,1)S(1)}, u32[]{:S(2)}, u32[]{:S(2)}) collective-permute-start(bf16[16,3584]{1,0:T(8,128)(2,1)S(1)} %get-tuple-element.47), channel_id=1, source_target_pairs={{0,4},{1,5},{2,6},{3,7},{4,8},{5,9},{6,10},{7,11},{8,12},{9,13},{1... | collective-permute-start | bytes 344072 | tf_op jit(solution)/shard_map/ppermute | solution.py:314
  4.6 2.1 %collective-permute-start.2 = (bf16[16,3584]{1,0:T(8,128)(2,1)S(1)}, bf16[16,3584]{1,0:T(8,128)(2,1)S(1)}, u32[]{:S(2)}, u32[]{:S(2)}) collective-permute-start(bf16[16,3584]{1,0:T(8,128)(2,1)S(1)} %get-tuple-element.48), channel_id=1, source_target_pairs={{0,12},{1,13},{2,14},{3,15},{4,0},{5,1},{6,2},{7,3},{8,4},{9,5},{1... | collective-permute-start | bytes 344072 | tf_op jit(solution)/shard_map/ppermute | solution.py:314
  6.7 0.9 %collective-permute-start.3 = (bf16[16,3584]{1,0:T(8,128)(2,1)S(1)}, bf16[16,3584]{1,0:T(8,128)(2,1)S(1)}, u32[]{:S(2)}, u32[]{:S(2)}) collective-permute-start(bf16[16,3584]{1,0:T(8,128)(2,1)S(1)} %get-tuple-element.49), channel_id=1, source_target_pairs={{0,8},{1,9},{2,10},{3,11},{4,12},{5,13},{6,14},{7,15},{8,0},{9,1},... | collective-permute-start | bytes 344072 | tf_op jit(solution)/shard_map/ppermute | solution.py:314
  7.6 3.4 %fetch.2.refs_5_ = bf16[1152,3584]{1,0:T(8,128)(2,1)S(1)} custom-call(bf16[1152,6144]{1,0:T(8,128)(2,1)} %refs_7_.1, bf16[16,6144]{1,0:T(8,128)(2,1)S(1)} %get-tuple-element.43.after_ref.refs_0_), custom_call_target="tpu_custom_call" | custom-call | bytes 16515072 | tf_op jit(solution)/shard_map/fetch/pallas_call | solution.py:100
  11.0 1.6 %collective-permute-start = (bf16[16,6144]{1,0:T(8,128)(2,1)S(1)}, bf16[16,6144]{1,0:T(8,128)(2,1)S(1)}, u32[]{:S(2)}, u32[]{:S(2)}) collective-permute-start(bf16[16,6144]{1,0:T(8,128)(2,1)S(1)} %get-tuple-element.43.after_ref.refs_0_), channel_id=1, source_target_pairs={{0,2},{1,3},{2,0},{3,1},{4,6},{5,7},{6,4},{7,5},{8,10},{9,11},{10,... | collective-permute-start | bytes 589832 | tf_op jit(solution)/shard_map/ppermute | solution.py:319
  12.7 3.4 %fetch.3.refs_6_ = bf16[1152,3584]{1,0:T(8,128)(2,1)S(1)} custom-call(bf16[1152,6144]{1,0:T(8,128)(2,1)} %refs_8_.2, bf16[16,6144]{1,0:T(8,128)(2,1)S(1)} %get-tuple-element.43.after_ref.refs_0_), custom_call_target="tpu_custom_call" | custom-call | bytes 16515072 | tf_op jit(solution)/shard_map/fetch/pallas_call | solution.py:100
  16.1 0.0 collective-permute-done.1
  16.1 0.0 collective-permute-done.2
  16.2 0.9 %collective-permute-done.3 = bf16[16,3584]{1,0:T(8,128)(2,1)S(1)} collective-permute-done((bf16[16,3584]{1,0:T(8,128)(2,1)S(1)}, bf16[16,3584]{1,0:T(8,128)(2,1)S(1)}, u32[]{:S(2)}, u32[]{:S(2)}) %collective-permute-start.3) | collective-permute-done | bytes 114720 | tf_op jit(solution)/shard_map/ppermute | solution.py:314
  17.1 1.6 %collective-permute-start.8 = (bf16[48,3584]{1,0:T(8,128)(2,1)S(1)}, bf16[48,3584]{1,0:T(8,128)(2,1)S(1)}, u32[]{:S(2)}, u32[]{:S(2)}) collective-permute-start(bf16[48,3584]{1,0:T(8,128)(2,1)S(1)} %get-tuple-element.53.refs_3_.refs_1_), channel_id=1, source_target_pairs={{0,2},{1,3},{2,0},{3,1},{4,6},{5,7},{6,4},{7,5},{8,10},{9,11},{10,... | collective-permute-start | bytes 1032200 | tf_op jit(solution)/shard_map/ppermute | solution.py:319
  18.7 0.0 collective-permute-done.refs_2_
  18.7 0.1 collective-permute-start.4
  18.8 3.8 %collective-permute-start.5 = (bf16[16,2560]{1,0:T(8,128)(2,1)S(1)}, bf16[16,2560]{1,0:T(8,128)(2,1)S(1)}, u32[]{:S(2)}, u32[]{:S(2)}) collective-permute-start(bf16[16,2560]{1,0:T(8,128)(2,1)S(1)} %get-tuple-element.51), channel_id=1, source_target_pairs={{0,12},{1,13},{2,14},{3,15},{4,0},{5,1},{6,2},{7,3},{8,4},{9,5},{1... | collective-permute-start | bytes 245768 | tf_op jit(solution)/shard_map/ppermute | solution.py:314
  22.6 0.0 collective-permute-start.6
  22.6 3.3 %collective-permute-done.4 = bf16[16,2560]{1,0:T(8,128)(2,1)S(1)} collective-permute-done((bf16[16,2560]{1,0:T(8,128)(2,1)S(1)}, bf16[16,2560]{1,0:T(8,128)(2,1)S(1)}, u32[]{:S(2)}, u32[]{:S(2)}) %collective-permute-start.4) | collective-permute-done | bytes 81952 | tf_op jit(solution)/shard_map/ppermute | solution.py:314
  26.0 0.0 collective-permute-done.5
  26.0 1.2 %collective-permute-done.8.refs_3_ = bf16[48,3584]{1,0:T(8,128)(2,1)S(1)} collective-permute-done((bf16[48,3584]{1,0:T(8,128)(2,1)S(1)}, bf16[48,3584]{1,0:T(8,128)(2,1)S(1)}, u32[]{:S(2)}, u32[]{:S(2)}) %collective-permute-start.8) | collective-permute-done | bytes 344096 | tf_op jit(solution)/shard_map/ppermute | solution.py:319
  27.2 0.1 collective-permute-start.9
  27.3 1.7 %collective-permute-done.6 = bf16[16,2560]{1,0:T(8,128)(2,1)S(1)} collective-permute-done((bf16[16,2560]{1,0:T(8,128)(2,1)S(1)}, bf16[16,2560]{1,0:T(8,128)(2,1)S(1)}, u32[]{:S(2)}, u32[]{:S(2)}) %collective-permute-start.6) | collective-permute-done | bytes 81952 | tf_op jit(solution)/shard_map/ppermute | solution.py:314
  29.0 0.7 collective-permute-start.7
  29.7 0.0 collective-permute-start.10
  29.7 0.0 collective-permute-done.9.refs_4_
  29.7 5.5 %gate_up.2 = (bf16[1152,2560]{1,0:T(8,128)(2,1)S(1)}, bf16[1152,2560]{1,0:T(8,128)(2,1)S(1)}, f32[1152,256]{1,0:T(8,128)S(1)}, f32[1152,256]{1,0:T(8,128)S(1)}) custom-call(bf16[16,6144]{1,0:T(8,128)(2,1)S(1)} %get-tuple-element.43.after_ref.refs_0_, bf16[48,3584]{1,0:T(8,128)(2,1)S(1)} %get-tuple-element.53.refs_3_.refs_1_, ...), custom_call_target="tpu_custom_call" | custom-call | flops 4227858432 | bytes 18874368 | tf_op jit(solution)/shard_map/gate_up/pallas_call | solution.py:182
  35.3 0.4 collective-permute-done.7.refs_3_
  35.7 0.1 collective-permute-start.11
  35.8 0.0 collective-permute-done.10.refs_4_
  35.8 1.4 %collective-permute-done.11.refs_5_ = bf16[48,2560]{1,0:T(8,128)(2,1)S(1)} collective-permute-done((bf16[48,2560]{1,0:T(8,128)(2,1)S(1)}, bf16[48,2560]{1,0:T(8,128)(2,1)S(1)}, u32[]{:S(2)}, u32[]{:S(2)}) %collective-permute-start.11) | collective-permute-done | bytes 245792 | tf_op jit(solution)/shard_map/ppermute | solution.py:319
  37.2 4.0 %gate_up.3 = (bf16[1152,4096]{1,0:T(8,128)(2,1)S(1)}, bf16[256,1152]{1,0:T(8,128)(2,1)S(1)}) custom-call(bf16[16,6144]{1,0:T(8,128)(2,1)S(1)} %get-tuple-element.43.after_ref.refs_0_, bf16[48,2560]{1,0:T(8,128)(2,1)S(1)} %get-tuple-element.94.refs_1_, bf16[16,6144]{1,0:T(8,128)(2,1)S(1)} %collective-permute-done.refs_2_, ...), custom_call_target="tpu_custom_call" | custom-call | flops 3019898880 | bytes 14155776 | tf_op jit(solution)/shard_map/gate_up/pallas_call | solution.py:182
  41.2 2.5 %down.2 = (bf16[1152,2048]{1,0:T(8,128)(2,1)S(1)}, bf16[128,3072]{1,0:T(8,128)(2,1)S(1)}, bf16[128,3072]{1,0:T(8,128)(2,1)S(1)}) custom-call(bf16[256,1152]{1,0:T(8,128)(2,1)S(1)} %get-tuple-element.61.after_ref.hidden_ref, bf16[1152,4096]{1,0:T(8,128)(2,1)S(1)} %get-tuple-element.62.refs_0_, bf16[1152,6144]{1,0:T(8,128)(2,1)} %refs_1_.1), custom_call_target="tpu_custom_call" | custom-call | flops 1811939328 | bytes 9240576 | tf_op jit(solution)/shard_map/down/pallas_call | solution.py:235
  43.8 0.2 collective-permute-start.12
  44.0 2.6 %down.3 = (bf16[128,3072]{1,0:T(8,128)(2,1)S(1)}, bf16[128,3072]{1,0:T(8,128)(2,1)S(1)}) custom-call(bf16[256,1152]{1,0:T(8,128)(2,1)S(1)} %get-tuple-element.61.after_ref.hidden_ref, bf16[1152,4096]{1,0:T(8,128)(2,1)S(1)} %get-tuple-element.62.refs_0_, bf16[1152,2048]{1,0:T(8,128)(2,1)S(1)} %get-tuple-element.65.refs_1_), custom_call_target="tpu_custom_call" | custom-call | flops 1811939328 | bytes 9240576 | tf_op jit(solution)/shard_map/down/pallas_call | solution.py:235
  46.6 0.4 collective-permute-start.13
  47.0 0.0 collective-permute-done.12
  47.0 0.0 copy-start.1
  47.0 0.0 copy-start.2
  47.0 0.2 add_convert_fusion.1
  47.2 0.0 copy-start
  47.3 1.5 %collective-permute-start.16 = (bf16[16,3072]{1,0:T(8,128)(2,1)S(1)}, bf16[16,3072]{1,0:T(8,128)(2,1)S(1)}, u32[]{:S(2)}, u32[]{:S(2)}) collective-permute-start(bf16[16,3072]{1,0:T(8,128)(2,1)S(1)} %get-tuple-element.83), channel_id=1, source_target_pairs={{0,2},{1,3},{2,0},{3,1},{4,6},{5,7},{6,4},{7,5},{8,10},{9,11},{10,... | collective-permute-start | bytes 294920 | tf_op jit(solution)/shard_map/ppermute | solution.py:319
  48.8 0.1 collective-permute-done.13
  48.9 0.2 add_convert_fusion
  49.2 1.5 %collective-permute-start.14 = (bf16[16,3072]{1,0:T(8,128)(2,1)S(1)}, bf16[16,3072]{1,0:T(8,128)(2,1)S(1)}, u32[]{:S(2)}, u32[]{:S(2)}) collective-permute-start(bf16[16,3072]{1,0:T(8,128)(2,1)S(1)} %get-tuple-element.77), channel_id=1, source_target_pairs={{0,2},{1,3},{2,0},{3,1},{4,6},{5,7},{6,4},{7,5},{8,10},{9,11},{10,... | collective-permute-start | bytes 294920 | tf_op jit(solution)/shard_map/ppermute | solution.py:319
  50.8 1.4 %collective-permute-done.16 = bf16[16,3072]{1,0:T(8,128)(2,1)S(1)} collective-permute-done((bf16[16,3072]{1,0:T(8,128)(2,1)S(1)}, bf16[16,3072]{1,0:T(8,128)(2,1)S(1)}, u32[]{:S(2)}, u32[]{:S(2)}) %collective-permute-start.16) | collective-permute-done | bytes 98336 | tf_op jit(solution)/shard_map/ppermute | solution.py:319
  52.2 0.7 collective-permute-start.21
  52.9 1.0 %collective-permute-start.17 = (bf16[16,6144]{1,0:T(8,128)(2,1)S(1)}, bf16[16,6144]{1,0:T(8,128)(2,1)S(1)}, u32[]{:S(2)}, u32[]{:S(2)}) collective-permute-start(bf16[16,6144]{1,0:T(8,128)(2,1)S(1)} %get-tuple-element.69), channel_id=1, source_target_pairs={{0,2},{1,3},{2,0},{3,1},{4,6},{5,7},{6,4},{7,5},{8,10},{9,11},{10,... | collective-permute-start | bytes 589832 | tf_op jit(solution)/shard_map/ppermute | solution.py:319
  54.0 0.4 collective-permute-done.14
  54.3 2.4 %collective-permute-start.19 = (bf16[16,3072]{1,0:T(8,128)(2,1)S(1)}, bf16[16,3072]{1,0:T(8,128)(2,1)S(1)}, u32[]{:S(2)}, u32[]{:S(2)}) collective-permute-start(bf16[16,3072]{1,0:T(8,128)(2,1)S(1)} %add_convert_fusion.5), channel_id=1, source_target_pairs={{0,8},{1,9},{2,10},{3,11},{4,12},{5,13},{6,14},{7,15},{8,0},{9,1},... | collective-permute-start | bytes 294920 | tf_op jit(solution)/shard_map/ppermute | solution.py:314
  56.8 0.6 collective-permute-start.15
  57.3 2.3 %collective-permute-done.17 = bf16[16,6144]{1,0:T(8,128)(2,1)S(1)} collective-permute-done((bf16[16,6144]{1,0:T(8,128)(2,1)S(1)}, bf16[16,6144]{1,0:T(8,128)(2,1)S(1)}, u32[]{:S(2)}, u32[]{:S(2)}) %collective-permute-start.17) | collective-permute-done | bytes 196640 | tf_op jit(solution)/shard_map/ppermute | solution.py:319
  59.7 1.7 %collective-permute-done.21.refs_2_ = bf16[16,3072]{1,0:T(8,128)(2,1)S(1)} collective-permute-done((bf16[16,3072]{1,0:T(8,128)(2,1)S(1)}, bf16[16,3072]{1,0:T(8,128)(2,1)S(1)}, u32[]{:S(2)}, u32[]{:S(2)}) %collective-permute-start.21) | collective-permute-done | bytes 98336 | tf_op jit(solution)/shard_map/ppermute | solution.py:314
  61.4 1.2 %collective-permute-start.22 = (bf16[16,6144]{1,0:T(8,128)(2,1)S(1)}, bf16[16,6144]{1,0:T(8,128)(2,1)S(1)}, u32[]{:S(2)}, u32[]{:S(2)}) collective-permute-start(bf16[16,6144]{1,0:T(8,128)(2,1)S(1)} %add_convert_fusion.2), channel_id=1, source_target_pairs={{0,4},{1,5},{2,6},{3,7},{4,8},{5,9},{6,10},{7,11},{8,12},{9,13},{1... | collective-permute-start | bytes 589832 | tf_op jit(solution)/shard_map/ppermute | solution.py:314
  62.6 0.4 collective-permute-done.15
  63.0 1.9 %collective-permute-done.19.refs_3_ = bf16[16,3072]{1,0:T(8,128)(2,1)S(1)} collective-permute-done((bf16[16,3072]{1,0:T(8,128)(2,1)S(1)}, bf16[16,3072]{1,0:T(8,128)(2,1)S(1)}, u32[]{:S(2)}, u32[]{:S(2)}) %collective-permute-start.19) | collective-permute-done | bytes 98336 | tf_op jit(solution)/shard_map/ppermute | solution.py:314
  65.0 0.0 collective-permute-start.18
  65.0 1.9 %collective-permute-start.20 = (bf16[16,6144]{1,0:T(8,128)(2,1)S(1)}, bf16[16,6144]{1,0:T(8,128)(2,1)S(1)}, u32[]{:S(2)}, u32[]{:S(2)}) collective-permute-start(bf16[16,6144]{1,0:T(8,128)(2,1)S(1)} %add_convert_fusion.3), channel_id=1, source_target_pairs={{0,12},{1,13},{2,14},{3,15},{4,0},{5,1},{6,2},{7,3},{8,4},{9,5},{1... | collective-permute-start | bytes 589832 | tf_op jit(solution)/shard_map/ppermute | solution.py:314
  66.9 0.0 copy-done.1
  66.9 0.0 copy-done.2
  66.9 0.2 shares.1.terms_ref
  67.1 3.8 %collective-permute-done.22.last = bf16[16,6144]{1,0:T(8,128)(2,1)S(1)} collective-permute-done((bf16[16,6144]{1,0:T(8,128)(2,1)S(1)}, bf16[16,6144]{1,0:T(8,128)(2,1)S(1)}, u32[]{:S(2)}, u32[]{:S(2)}) %collective-permute-start.22) | collective-permute-done | bytes 196640 | tf_op jit(solution)/shard_map/ppermute | solution.py:314
  70.9 0.0 collective-permute-done.18.arrived
  70.9 1.5 %collective-permute-done.20.near = bf16[16,6144]{1,0:T(8,128)(2,1)S(1)} collective-permute-done((bf16[16,6144]{1,0:T(8,128)(2,1)S(1)}, bf16[16,6144]{1,0:T(8,128)(2,1)S(1)}, u32[]{:S(2)}, u32[]{:S(2)}) %collective-permute-start.20) | collective-permute-done | bytes 196640 | tf_op jit(solution)/shard_map/ppermute | solution.py:314
  72.4 0.0 copy-done
  72.4 1.1 %mix.1 = bf16[24,6144]{1,0:T(8,128)(2,1)} custom-call(f32[72,64]{1,0:T(8,128)S(1)} %shares.1.terms_ref, bf16[24,6144]{1,0:T(8,128)(2,1)S(1)} %copy-done, bf16[16,6144]{1,0:T(8,128)(2,1)S(1)} %collective-permute-done.18.arrived, bf16[16,6144]{1,0:T(8,128)(2,1)S(1)} %collective-permute-done.20.near, bf16[16,6144]{1,0:T(8,128)(2,1)S(1)} %collective-permute-done.22.last, ...), custom_call_target="tpu_custom_call" | custom-call | tf_op jit(solution)/shard_map/mix/pallas_call | solution.py:293
  (20 shorter events, 0.4 us)
Async XLA Ops:
  1.5 14.6 %collective-permute-start.1 = (bf16[16,3584]{1,0:T(8,128)(2,1)S(1)}, bf16[16,3584]{1,0:T(8,128)(2,1)S(1)}, u32[]{:S(2)}, u32[]{:S(2)}) collective-permute-start(bf16[16,3584]{1,0:T(8,128)(2,1)S(1)} %get-tuple-element.47), channel_id=1, source_target_pairs={{0,4},{1,5},{2,6},{3,7},{4,8},{5,9},{6,10},{7,11},{8,12},{9,13},{1... | collective-permute-start | bytes 344072 | tf_op jit(solution)/shard_map/ppermute | solution.py:314
  4.6 11.6 %collective-permute-start.2 = (bf16[16,3584]{1,0:T(8,128)(2,1)S(1)}, bf16[16,3584]{1,0:T(8,128)(2,1)S(1)}, u32[]{:S(2)}, u32[]{:S(2)}) collective-permute-start(bf16[16,3584]{1,0:T(8,128)(2,1)S(1)} %get-tuple-element.48), channel_id=1, source_target_pairs={{0,12},{1,13},{2,14},{3,15},{4,0},{5,1},{6,2},{7,3},{8,4},{9,5},{1... | collective-permute-start | bytes 344072 | tf_op jit(solution)/shard_map/ppermute | solution.py:314
  6.7 10.4 %collective-permute-start.3 = (bf16[16,3584]{1,0:T(8,128)(2,1)S(1)}, bf16[16,3584]{1,0:T(8,128)(2,1)S(1)}, u32[]{:S(2)}, u32[]{:S(2)}) collective-permute-start(bf16[16,3584]{1,0:T(8,128)(2,1)S(1)} %get-tuple-element.49), channel_id=1, source_target_pairs={{0,8},{1,9},{2,10},{3,11},{4,12},{5,13},{6,14},{7,15},{8,0},{9,1},... | collective-permute-start | bytes 344072 | tf_op jit(solution)/shard_map/ppermute | solution.py:314
  11.0 7.7 %collective-permute-start = (bf16[16,6144]{1,0:T(8,128)(2,1)S(1)}, bf16[16,6144]{1,0:T(8,128)(2,1)S(1)}, u32[]{:S(2)}, u32[]{:S(2)}) collective-permute-start(bf16[16,6144]{1,0:T(8,128)(2,1)S(1)} %get-tuple-element.43.after_ref.refs_0_), channel_id=1, source_target_pairs={{0,2},{1,3},{2,0},{3,1},{4,6},{5,7},{6,4},{7,5},{8,10},{9,11},{10,... | collective-permute-start | bytes 589832 | tf_op jit(solution)/shard_map/ppermute | solution.py:319
  17.1 10.0 %collective-permute-start.8 = (bf16[48,3584]{1,0:T(8,128)(2,1)S(1)}, bf16[48,3584]{1,0:T(8,128)(2,1)S(1)}, u32[]{:S(2)}, u32[]{:S(2)}) collective-permute-start(bf16[48,3584]{1,0:T(8,128)(2,1)S(1)} %get-tuple-element.53.refs_3_.refs_1_), channel_id=1, source_target_pairs={{0,2},{1,3},{2,0},{3,1},{4,6},{5,7},{6,4},{7,5},{8,10},{9,11},{10,... | collective-permute-start | bytes 1032200 | tf_op jit(solution)/shard_map/ppermute | solution.py:319
  18.7 7.2 %collective-permute-start.4 = (bf16[16,2560]{1,0:T(8,128)(2,1)S(1)}, bf16[16,2560]{1,0:T(8,128)(2,1)S(1)}, u32[]{:S(2)}, u32[]{:S(2)}) collective-permute-start(bf16[16,2560]{1,0:T(8,128)(2,1)S(1)} %get-tuple-element.50), channel_id=1, source_target_pairs={{0,4},{1,5},{2,6},{3,7},{4,8},{5,9},{6,10},{7,11},{8,12},{9,13},{1... | collective-permute-start | bytes 245768 | tf_op jit(solution)/shard_map/ppermute | solution.py:314
  18.8 7.2 %collective-permute-start.5 = (bf16[16,2560]{1,0:T(8,128)(2,1)S(1)}, bf16[16,2560]{1,0:T(8,128)(2,1)S(1)}, u32[]{:S(2)}, u32[]{:S(2)}) collective-permute-start(bf16[16,2560]{1,0:T(8,128)(2,1)S(1)} %get-tuple-element.51), channel_id=1, source_target_pairs={{0,12},{1,13},{2,14},{3,15},{4,0},{5,1},{6,2},{7,3},{8,4},{9,5},{1... | collective-permute-start | bytes 245768 | tf_op jit(solution)/shard_map/ppermute | solution.py:314
  22.6 6.3 %collective-permute-start.6 = (bf16[16,2560]{1,0:T(8,128)(2,1)S(1)}, bf16[16,2560]{1,0:T(8,128)(2,1)S(1)}, u32[]{:S(2)}, u32[]{:S(2)}) collective-permute-start(bf16[16,2560]{1,0:T(8,128)(2,1)S(1)} %get-tuple-element.52), channel_id=1, source_target_pairs={{0,8},{1,9},{2,10},{3,11},{4,12},{5,13},{6,14},{7,15},{8,0},{9,1},... | collective-permute-start | bytes 245768 | tf_op jit(solution)/shard_map/ppermute | solution.py:314
  27.2 2.5 %collective-permute-start.9 = (bf16[128,3584]{1,0:T(8,128)(2,1)S(1)}, bf16[128,3584]{1,0:T(8,128)(2,1)S(1)}, u32[]{:S(2)}, u32[]{:S(2)}) collective-permute-start(bf16[128,3584]{1,0:T(8,128)(2,1)S(1)} %constant_dynamic-update-slice_fusion.6), channel_id=1, source_target_pairs={{0,1},{1,0},{2,3},{3,2},{4,5},{5,4},{6,7},{7,6},{8,9},{9,8},{10,11... | collective-permute-start | bytes 2752520 | tf_op jit(solution)/shard_map/ppermute | solution.py:319
  29.0 6.7 %collective-permute-start.7 = (bf16[48,2560]{1,0:T(8,128)(2,1)S(1)}, bf16[48,2560]{1,0:T(8,128)(2,1)S(1)}, u32[]{:S(2)}, u32[]{:S(2)}) collective-permute-start(bf16[48,2560]{1,0:T(8,128)(2,1)S(1)} %get-tuple-element.94.refs_1_), channel_id=1, source_target_pairs={{0,2},{1,3},{2,0},{3,1},{4,6},{5,7},{6,4},{7,5},{8,10},{9,11},{10,... | collective-permute-start | bytes 737288 | tf_op jit(solution)/shard_map/ppermute | solution.py:319
  29.7 6.1 %collective-permute-start.10 = (bf16[80,2560]{1,0:T(8,128)(2,1)S(1)}, bf16[80,2560]{1,0:T(8,128)(2,1)S(1)}, u32[]{:S(2)}, u32[]{:S(2)}) collective-permute-start(bf16[80,2560]{1,0:T(8,128)(2,1)S(1)} %slice_dynamic-update-slice_fusion.2), channel_id=1, source_target_pairs={{0,1},{1,0},{2,3},{3,2},{4,5},{5,4},{6,7},{7,6},{8,9},{9,8},{10,11... | collective-permute-start | bytes 1228808 | tf_op jit(solution)/shard_map/ppermute | solution.py:319
  35.7 1.5 %collective-permute-start.11 = (bf16[48,2560]{1,0:T(8,128)(2,1)S(1)}, bf16[48,2560]{1,0:T(8,128)(2,1)S(1)}, u32[]{:S(2)}, u32[]{:S(2)}) collective-permute-start(bf16[48,2560]{1,0:T(8,128)(2,1)S(1)} %collective-permute-done.7.refs_3_), channel_id=1, source_target_pairs={{0,1},{1,0},{2,3},{3,2},{4,5},{5,4},{6,7},{7,6},{8,9},{9,8},{10,11... | collective-permute-start | bytes 737288 | tf_op jit(solution)/shard_map/ppermute | solution.py:319
  43.8 3.3 %collective-permute-start.12 = (bf16[128,3072]{1,0:T(8,128)(2,1)S(1)}, bf16[128,3072]{1,0:T(8,128)(2,1)S(1)}, u32[]{:S(2)}, u32[]{:S(2)}) collective-permute-start(bf16[128,3072]{1,0:T(8,128)(2,1)S(1)} %get-tuple-element.64), channel_id=1, source_target_pairs={{0,1},{1,0},{2,3},{3,2},{4,5},{5,4},{6,7},{7,6},{8,9},{9,8},{10,11... | collective-permute-start | bytes 2359304 | tf_op jit(solution)/shard_map/ppermute | solution.py:319
  46.6 2.4 %collective-permute-start.13 = (bf16[128,3072]{1,0:T(8,128)(2,1)S(1)}, bf16[128,3072]{1,0:T(8,128)(2,1)S(1)}, u32[]{:S(2)}, u32[]{:S(2)}) collective-permute-start(bf16[128,3072]{1,0:T(8,128)(2,1)S(1)} %get-tuple-element.67), channel_id=1, source_target_pairs={{0,1},{1,0},{2,3},{3,2},{4,5},{5,4},{6,7},{7,6},{8,9},{9,8},{10,11... | collective-permute-start | bytes 2359304 | tf_op jit(solution)/shard_map/ppermute | solution.py:319
  47.0 19.9 %copy-start.1 = (s32[24,2]{0,1:T(2,128)S(1)}, s32[24,2]{0,1:T(2,128)}, u32[]{:S(2)}) copy-start(s32[24,2]{0,1:T(2,128)} %param.8) | copy-start | bytes 580
  47.0 19.9 %copy-start.2 = (f32[24,2]{0,1:T(2,128)S(1)}, f32[24,2]{0,1:T(2,128)}, u32[]{:S(2)}) copy-start(f32[24,2]{0,1:T(2,128)} %param.9) | copy-start | bytes 580
  47.2 25.2 %copy-start = (bf16[24,6144]{1,0:T(8,128)(2,1)S(1)}, bf16[24,6144]{1,0:T(8,128)(2,1)}, u32[]{:S(2)}) copy-start(bf16[24,6144]{1,0:T(8,128)(2,1)} %act_ref.3) | copy-start | bytes 884740
  47.3 4.9 %collective-permute-start.16 = (bf16[16,3072]{1,0:T(8,128)(2,1)S(1)}, bf16[16,3072]{1,0:T(8,128)(2,1)S(1)}, u32[]{:S(2)}, u32[]{:S(2)}) collective-permute-start(bf16[16,3072]{1,0:T(8,128)(2,1)S(1)} %get-tuple-element.83), channel_id=1, source_target_pairs={{0,2},{1,3},{2,0},{3,1},{4,6},{5,7},{6,4},{7,5},{8,10},{9,11},{10,... | collective-permute-start | bytes 294920 | tf_op jit(solution)/shard_map/ppermute | solution.py:319
  49.2 5.1 %collective-permute-start.14 = (bf16[16,3072]{1,0:T(8,128)(2,1)S(1)}, bf16[16,3072]{1,0:T(8,128)(2,1)S(1)}, u32[]{:S(2)}, u32[]{:S(2)}) collective-permute-start(bf16[16,3072]{1,0:T(8,128)(2,1)S(1)} %get-tuple-element.77), channel_id=1, source_target_pairs={{0,2},{1,3},{2,0},{3,1},{4,6},{5,7},{6,4},{7,5},{8,10},{9,11},{10,... | collective-permute-start | bytes 294920 | tf_op jit(solution)/shard_map/ppermute | solution.py:319
  52.2 9.2 %collective-permute-start.21 = (bf16[16,3072]{1,0:T(8,128)(2,1)S(1)}, bf16[16,3072]{1,0:T(8,128)(2,1)S(1)}, u32[]{:S(2)}, u32[]{:S(2)}) collective-permute-start(bf16[16,3072]{1,0:T(8,128)(2,1)S(1)} %add_convert_fusion.4), channel_id=1, source_target_pairs={{0,8},{1,9},{2,10},{3,11},{4,12},{5,13},{6,14},{7,15},{8,0},{9,1},... | collective-permute-start | bytes 294920 | tf_op jit(solution)/shard_map/ppermute | solution.py:314
  52.9 6.7 %collective-permute-start.17 = (bf16[16,6144]{1,0:T(8,128)(2,1)S(1)}, bf16[16,6144]{1,0:T(8,128)(2,1)S(1)}, u32[]{:S(2)}, u32[]{:S(2)}) collective-permute-start(bf16[16,6144]{1,0:T(8,128)(2,1)S(1)} %get-tuple-element.69), channel_id=1, source_target_pairs={{0,2},{1,3},{2,0},{3,1},{4,6},{5,7},{6,4},{7,5},{8,10},{9,11},{10,... | collective-permute-start | bytes 589832 | tf_op jit(solution)/shard_map/ppermute | solution.py:319
  54.3 10.6 %collective-permute-start.19 = (bf16[16,3072]{1,0:T(8,128)(2,1)S(1)}, bf16[16,3072]{1,0:T(8,128)(2,1)S(1)}, u32[]{:S(2)}, u32[]{:S(2)}) collective-permute-start(bf16[16,3072]{1,0:T(8,128)(2,1)S(1)} %add_convert_fusion.5), channel_id=1, source_target_pairs={{0,8},{1,9},{2,10},{3,11},{4,12},{5,13},{6,14},{7,15},{8,0},{9,1},... | collective-permute-start | bytes 294920 | tf_op jit(solution)/shard_map/ppermute | solution.py:314
  56.8 6.2 %collective-permute-start.15 = (bf16[16,6144]{1,0:T(8,128)(2,1)S(1)}, bf16[16,6144]{1,0:T(8,128)(2,1)S(1)}, u32[]{:S(2)}, u32[]{:S(2)}) collective-permute-start(bf16[16,6144]{1,0:T(8,128)(2,1)S(1)} %get-tuple-element.68), channel_id=1, source_target_pairs={{0,2},{1,3},{2,0},{3,1},{4,6},{5,7},{6,4},{7,5},{8,10},{9,11},{10,... | collective-permute-start | bytes 589832 | tf_op jit(solution)/shard_map/ppermute | solution.py:319
  61.4 9.5 %collective-permute-start.22 = (bf16[16,6144]{1,0:T(8,128)(2,1)S(1)}, bf16[16,6144]{1,0:T(8,128)(2,1)S(1)}, u32[]{:S(2)}, u32[]{:S(2)}) collective-permute-start(bf16[16,6144]{1,0:T(8,128)(2,1)S(1)} %add_convert_fusion.2), channel_id=1, source_target_pairs={{0,4},{1,5},{2,6},{3,7},{4,8},{5,9},{6,10},{7,11},{8,12},{9,13},{1... | collective-permute-start | bytes 589832 | tf_op jit(solution)/shard_map/ppermute | solution.py:314
  65.0 6.0 %collective-permute-start.18 = (bf16[16,6144]{1,0:T(8,128)(2,1)S(1)}, bf16[16,6144]{1,0:T(8,128)(2,1)S(1)}, u32[]{:S(2)}, u32[]{:S(2)}) collective-permute-start(bf16[16,6144]{1,0:T(8,128)(2,1)S(1)} %pad_maximum_fusion), channel_id=1, source_target_pairs={{0,2},{1,3},{2,0},{3,1},{4,6},{5,7},{6,4},{7,5},{8,10},{9,11},{10,... | collective-permute-start | bytes 589832 | tf_op jit(solution)/shard_map/ppermute | solution.py:319
  65.0 7.4 %collective-permute-start.20 = (bf16[16,6144]{1,0:T(8,128)(2,1)S(1)}, bf16[16,6144]{1,0:T(8,128)(2,1)S(1)}, u32[]{:S(2)}, u32[]{:S(2)}) collective-permute-start(bf16[16,6144]{1,0:T(8,128)(2,1)S(1)} %add_convert_fusion.3), channel_id=1, source_target_pairs={{0,12},{1,13},{2,14},{3,15},{4,0},{5,1},{6,2},{7,3},{8,4},{9,5},{1... | collective-permute-start | bytes 589832 | tf_op jit(solution)/shard_map/ppermute | solution.py:314

commit v19 on v18

--- a/solution.py
+++ b/solution.py
@@ -273,7 +273,7 @@
     )(ids, logits, after)
 
 
-def mix_kernel(terms_ref, act_ref, arrived, near, last, *refs):
+def mix_kernel(terms_ref, act_ref, arrived, last, near, *refs):
     out_ref, kept, middle_rows = refs[-1], refs[:HALVES], refs[HALVES:-1]
     tokens = act_ref.shape[0]
     terms = terms_ref[...].astype(jnp.bfloat16)
@@ -379,13 +379,13 @@
     middle = [shift(added(h[place[2]], x), -2) for h, x in zip(held, crossed)]
     mine = [jnp.concatenate([h[j] for h in held], axis=1) for j in range(2 * EXPERTS)]
     back = {}
-    back[1] = swap(after(mine[EXPERTS + place[1]], crossed[1]), far)
-    back[3] = swap(after(mine[EXPERTS + place[3]], crossed[0]), far)
-    back[0] = swap(after(mine[EXPERTS], back[1], back[3]), far)
-    near = shift(after(added(mine[place[1]], back[1]), middle[1]), -1)
-    last = shift(after(added(mine[place[3]], back[3]), middle[0]), -3)
+    back[3] = swap(after(mine[EXPERTS + place[3]], crossed[1]), far)
+    back[1] = swap(after(mine[EXPERTS + place[1]], crossed[0]), far)
+    back[0] = swap(after(mine[EXPERTS], back[3], back[1]), far)
+    last = shift(after(added(mine[place[3]], back[3]), middle[1]), -3)
+    near = shift(after(added(mine[place[1]], back[1]), middle[0]), -1)
     arrived = back[0]
-    pieces = [arrived, near, last, *[h[0] for h in held], *middle]
+    pieces = [arrived, last, near, *[h[0] for h in held], *middle]
     terms = shares(group, ids, route_logits.T, hidden)
     return mix(terms, activations, pieces)
 

time: 73.7 us -> 73.8 us (level)
  starting transfers between devices: 25.6 us -> 27.1 us
  waiting for transfers between devices: 22.5 us -> 21.1 us
    ppermute x10, waiting for transfers between devices: 14.9 us -> 12.8 us  [shift(): lax.ppermute(x, 'expert', [(i, (i + s * group) % devices) for i in range(...]
    ppermute x13, starting transfers between devices: 9.33 us -> 10.6 us  [swap(): return lax.ppermute(x, 'expert', [(i, i ^ bit) for i in range(devices)])]
  transfers between devices with their start and end apart: 23 -> 23, of which waited for: 15 -> 14; matrix products, arithmetic and copies ran while one was open for 1% -> 1% of each run, Pallas kernels for 21% -> 21%
where the time goes in v19:
time: 73.8 us; the launch traced here: 73.6 us
  starting transfers between devices  27.1 us (37%)
  Pallas kernels  24.4 us (33%)
  waiting for transfers between devices  21.1 us (29%)
    ppermute x10, starting transfers between devices, shift(): lax.ppermute(x, 'expert', [(i, (i + s * group) % devices) for i in range(...  16.6 us
    ppermute x10, waiting for transfers between devices, shift(): lax.ppermute(x, 'expert', [(i, (i + s * group) % devices) for i in range(...  12.8 us
    ppermute x13, starting transfers between devices, swap(): return lax.ppermute(x, 'expert', [(i, i ^ bit) for i in range(devices)])  10.6 us
    pallas_call x2, Pallas kernels, gate_up(): pl.pallas_call(functools.partial(gate_up_kernel, len(pieces), len(later),...  9.56 us
    ppermute x13, waiting for transfers between devices, swap(): return lax.ppermute(x, 'expert', [(i, i ^ bit) for i in range(devices)])  8.3 us
    pallas_call x2, Pallas kernels, fetch(): pl.pallas_call(functools.partial(fetch_kernel, at), in_specs=[ANY, ANY],...  6.87 us
    pallas_call x2, Pallas kernels, down(): pl.pallas_call(functools.partial(down_kernel, ahead, segments), in_specs=...  5.11 us
    pallas_call x1, Pallas kernels, pack(): pl.pallas_call(functools.partial(pack_kernel, group), grid=(1,), in_specs...  1.48 us
  transfers between devices with their start and end apart: 23, of which 14 were waited for; matrix products, arithmetic and copies ran while one was open for 1% of the time, Pallas kernels for 21%

profile of v19, /device:TPU:0, one launch (start us, length us, event | category | flops | bytes accessed | tf_op | source)
XLA Modules:
  0.0 73.6 jit_solution(4051356173351763049)
XLA Ops:
  0.0 1.5 %norm_and_pack.1 = (bf16[16,6144]{1,0:T(8,128)(2,1)S(1)}, bf16[16,3584]{1,0:T(8,128)(2,1)S(1)}, bf16[16,3584]{1,0:T(8,128)(2,1)S(1)}, bf16[16,3584]{1,0:T(8,128)...) custom-call(s32[2,24]{1,0:T(2,128)} %bitcast.3, ...), custom_call_target="tpu_custom_call" | custom-call | tf_op jit(solution)/shard_map/norm_and_pack/pallas_call | solution.py:67
  1.5 3.1 %collective-permute-start.1 = (bf16[16,3584]{1,0:T(8,128)(2,1)S(1)}, bf16[16,3584]{1,0:T(8,128)(2,1)S(1)}, u32[]{:S(2)}, u32[]{:S(2)}) collective-permute-start(bf16[16,3584]{1,0:T(8,128)(2,1)S(1)} %get-tuple-element.47), channel_id=1, source_target_pairs={{0,4},{1,5},{2,6},{3,7},{4,8},{5,9},{6,10},{7,11},{8,12},{9,13},{1... | collective-permute-start | bytes 344072 | tf_op jit(solution)/shard_map/ppermute | solution.py:314
  4.6 2.1 %collective-permute-start.2 = (bf16[16,3584]{1,0:T(8,128)(2,1)S(1)}, bf16[16,3584]{1,0:T(8,128)(2,1)S(1)}, u32[]{:S(2)}, u32[]{:S(2)}) collective-permute-start(bf16[16,3584]{1,0:T(8,128)(2,1)S(1)} %get-tuple-element.48), channel_id=1, source_target_pairs={{0,12},{1,13},{2,14},{3,15},{4,0},{5,1},{6,2},{7,3},{8,4},{9,5},{1... | collective-permute-start | bytes 344072 | tf_op jit(solution)/shard_map/ppermute | solution.py:314
  6.7 0.9 %collective-permute-start.3 = (bf16[16,3584]{1,0:T(8,128)(2,1)S(1)}, bf16[16,3584]{1,0:T(8,128)(2,1)S(1)}, u32[]{:S(2)}, u32[]{:S(2)}) collective-permute-start(bf16[16,3584]{1,0:T(8,128)(2,1)S(1)} %get-tuple-element.49), channel_id=1, source_target_pairs={{0,8},{1,9},{2,10},{3,11},{4,12},{5,13},{6,14},{7,15},{8,0},{9,1},... | collective-permute-start | bytes 344072 | tf_op jit(solution)/shard_map/ppermute | solution.py:314
  7.6 3.4 %fetch.2.refs_5_ = bf16[1152,3584]{1,0:T(8,128)(2,1)S(1)} custom-call(bf16[1152,6144]{1,0:T(8,128)(2,1)} %refs_7_.1, bf16[16,6144]{1,0:T(8,128)(2,1)S(1)} %get-tuple-element.43.after_ref.refs_0_), custom_call_target="tpu_custom_call" | custom-call | bytes 16515072 | tf_op jit(solution)/shard_map/fetch/pallas_call | solution.py:100
  11.0 1.6 %collective-permute-start = (bf16[16,6144]{1,0:T(8,128)(2,1)S(1)}, bf16[16,6144]{1,0:T(8,128)(2,1)S(1)}, u32[]{:S(2)}, u32[]{:S(2)}) collective-permute-start(bf16[16,6144]{1,0:T(8,128)(2,1)S(1)} %get-tuple-element.43.after_ref.refs_0_), channel_id=1, source_target_pairs={{0,2},{1,3},{2,0},{3,1},{4,6},{5,7},{6,4},{7,5},{8,10},{9,11},{10,... | collective-permute-start | bytes 589832 | tf_op jit(solution)/shard_map/ppermute | solution.py:319
  12.7 3.4 %fetch.3.refs_6_ = bf16[1152,3584]{1,0:T(8,128)(2,1)S(1)} custom-call(bf16[1152,6144]{1,0:T(8,128)(2,1)} %refs_8_.2, bf16[16,6144]{1,0:T(8,128)(2,1)S(1)} %get-tuple-element.43.after_ref.refs_0_), custom_call_target="tpu_custom_call" | custom-call | bytes 16515072 | tf_op jit(solution)/shard_map/fetch/pallas_call | solution.py:100
  16.1 0.0 collective-permute-done.1
  16.1 0.0 collective-permute-done.2
  16.2 0.9 %collective-permute-done.3 = bf16[16,3584]{1,0:T(8,128)(2,1)S(1)} collective-permute-done((bf16[16,3584]{1,0:T(8,128)(2,1)S(1)}, bf16[16,3584]{1,0:T(8,128)(2,1)S(1)}, u32[]{:S(2)}, u32[]{:S(2)}) %collective-permute-start.3) | collective-permute-done | bytes 114720 | tf_op jit(solution)/shard_map/ppermute | solution.py:314
  17.1 1.6 %collective-permute-start.8 = (bf16[48,3584]{1,0:T(8,128)(2,1)S(1)}, bf16[48,3584]{1,0:T(8,128)(2,1)S(1)}, u32[]{:S(2)}, u32[]{:S(2)}) collective-permute-start(bf16[48,3584]{1,0:T(8,128)(2,1)S(1)} %get-tuple-element.53.refs_3_.refs_1_), channel_id=1, source_target_pairs={{0,2},{1,3},{2,0},{3,1},{4,6},{5,7},{6,4},{7,5},{8,10},{9,11},{10,... | collective-permute-start | bytes 1032200 | tf_op jit(solution)/shard_map/ppermute | solution.py:319
  18.7 0.0 collective-permute-done.refs_2_
  18.7 0.1 collective-permute-start.4
  18.8 3.8 %collective-permute-start.5 = (bf16[16,2560]{1,0:T(8,128)(2,1)S(1)}, bf16[16,2560]{1,0:T(8,128)(2,1)S(1)}, u32[]{:S(2)}, u32[]{:S(2)}) collective-permute-start(bf16[16,2560]{1,0:T(8,128)(2,1)S(1)} %get-tuple-element.51), channel_id=1, source_target_pairs={{0,12},{1,13},{2,14},{3,15},{4,0},{5,1},{6,2},{7,3},{8,4},{9,5},{1... | collective-permute-start | bytes 245768 | tf_op jit(solution)/shard_map/ppermute | solution.py:314
  22.6 0.0 collective-permute-start.6
  22.6 3.3 %collective-permute-done.4 = bf16[16,2560]{1,0:T(8,128)(2,1)S(1)} collective-permute-done((bf16[16,2560]{1,0:T(8,128)(2,1)S(1)}, bf16[16,2560]{1,0:T(8,128)(2,1)S(1)}, u32[]{:S(2)}, u32[]{:S(2)}) %collective-permute-start.4) | collective-permute-done | bytes 81952 | tf_op jit(solution)/shard_map/ppermute | solution.py:314
  26.0 0.0 collective-permute-done.5
  26.0 1.2 %collective-permute-done.8.refs_3_ = bf16[48,3584]{1,0:T(8,128)(2,1)S(1)} collective-permute-done((bf16[48,3584]{1,0:T(8,128)(2,1)S(1)}, bf16[48,3584]{1,0:T(8,128)(2,1)S(1)}, u32[]{:S(2)}, u32[]{:S(2)}) %collective-permute-start.8) | collective-permute-done | bytes 344096 | tf_op jit(solution)/shard_map/ppermute | solution.py:319
  27.2 0.1 collective-permute-start.9
  27.3 1.7 %collective-permute-done.6 = bf16[16,2560]{1,0:T(8,128)(2,1)S(1)} collective-permute-done((bf16[16,2560]{1,0:T(8,128)(2,1)S(1)}, bf16[16,2560]{1,0:T(8,128)(2,1)S(1)}, u32[]{:S(2)}, u32[]{:S(2)}) %collective-permute-start.6) | collective-permute-done | bytes 81952 | tf_op jit(solution)/shard_map/ppermute | solution.py:314
  29.0 0.7 collective-permute-start.7
  29.7 0.0 collective-permute-start.10
  29.7 0.0 collective-permute-done.9.refs_4_
  29.7 5.5 %gate_up.2 = (bf16[1152,2560]{1,0:T(8,128)(2,1)S(1)}, bf16[1152,2560]{1,0:T(8,128)(2,1)S(1)}, f32[1152,256]{1,0:T(8,128)S(1)}, f32[1152,256]{1,0:T(8,128)S(1)}) custom-call(bf16[16,6144]{1,0:T(8,128)(2,1)S(1)} %get-tuple-element.43.after_ref.refs_0_, bf16[48,3584]{1,0:T(8,128)(2,1)S(1)} %get-tuple-element.53.refs_3_.refs_1_, ...), custom_call_target="tpu_custom_call" | custom-call | flops 4227858432 | bytes 18874368 | tf_op jit(solution)/shard_map/gate_up/pallas_call | solution.py:182
  35.3 0.4 collective-permute-done.7.refs_3_
  35.7 0.1 collective-permute-start.11
  35.8 0.0 collective-permute-done.10.refs_4_
  35.8 1.4 %collective-permute-done.11.refs_5_ = bf16[48,2560]{1,0:T(8,128)(2,1)S(1)} collective-permute-done((bf16[48,2560]{1,0:T(8,128)(2,1)S(1)}, bf16[48,2560]{1,0:T(8,128)(2,1)S(1)}, u32[]{:S(2)}, u32[]{:S(2)}) %collective-permute-start.11) | collective-permute-done | bytes 245792 | tf_op jit(solution)/shard_map/ppermute | solution.py:319
  37.2 4.0 %gate_up.3 = (bf16[1152,4096]{1,0:T(8,128)(2,1)S(1)}, bf16[256,1152]{1,0:T(8,128)(2,1)S(1)}) custom-call(bf16[16,6144]{1,0:T(8,128)(2,1)S(1)} %get-tuple-element.43.after_ref.refs_0_, bf16[48,2560]{1,0:T(8,128)(2,1)S(1)} %get-tuple-element.94.refs_1_, bf16[16,6144]{1,0:T(8,128)(2,1)S(1)} %collective-permute-done.refs_2_, ...), custom_call_target="tpu_custom_call" | custom-call | flops 3019898880 | bytes 14155776 | tf_op jit(solution)/shard_map/gate_up/pallas_call | solution.py:182
  41.2 2.5 %down.2 = (bf16[1152,2048]{1,0:T(8,128)(2,1)S(1)}, bf16[128,3072]{1,0:T(8,128)(2,1)S(1)}, bf16[128,3072]{1,0:T(8,128)(2,1)S(1)}) custom-call(bf16[256,1152]{1,0:T(8,128)(2,1)S(1)} %get-tuple-element.61.after_ref.hidden_ref, bf16[1152,4096]{1,0:T(8,128)(2,1)S(1)} %get-tuple-element.62.refs_0_, bf16[1152,6144]{1,0:T(8,128)(2,1)} %refs_1_.1), custom_call_target="tpu_custom_call" | custom-call | flops 1811939328 | bytes 9240576 | tf_op jit(solution)/shard_map/down/pallas_call | solution.py:235
  43.8 0.2 collective-permute-start.12
  44.0 2.6 %down.3 = (bf16[128,3072]{1,0:T(8,128)(2,1)S(1)}, bf16[128,3072]{1,0:T(8,128)(2,1)S(1)}) custom-call(bf16[256,1152]{1,0:T(8,128)(2,1)S(1)} %get-tuple-element.61.after_ref.hidden_ref, bf16[1152,4096]{1,0:T(8,128)(2,1)S(1)} %get-tuple-element.62.refs_0_, bf16[1152,2048]{1,0:T(8,128)(2,1)S(1)} %get-tuple-element.65.refs_1_), custom_call_target="tpu_custom_call" | custom-call | flops 1811939328 | bytes 9240576 | tf_op jit(solution)/shard_map/down/pallas_call | solution.py:235
  46.6 0.4 collective-permute-start.13
  47.0 0.0 collective-permute-done.12
  47.0 0.0 copy-start.1
  47.0 0.0 copy-start.2
  47.0 0.2 add_convert_fusion.1
  47.2 0.0 copy-start
  47.3 1.5 %collective-permute-start.16 = (bf16[16,3072]{1,0:T(8,128)(2,1)S(1)}, bf16[16,3072]{1,0:T(8,128)(2,1)S(1)}, u32[]{:S(2)}, u32[]{:S(2)}) collective-permute-start(bf16[16,3072]{1,0:T(8,128)(2,1)S(1)} %get-tuple-element.83), channel_id=1, source_target_pairs={{0,2},{1,3},{2,0},{3,1},{4,6},{5,7},{6,4},{7,5},{8,10},{9,11},{10,... | collective-permute-start | bytes 294920 | tf_op jit(solution)/shard_map/ppermute | solution.py:319
  48.8 0.1 collective-permute-done.13
  48.9 0.2 add_convert_fusion
  49.2 1.5 %collective-permute-start.14 = (bf16[16,3072]{1,0:T(8,128)(2,1)S(1)}, bf16[16,3072]{1,0:T(8,128)(2,1)S(1)}, u32[]{:S(2)}, u32[]{:S(2)}) collective-permute-start(bf16[16,3072]{1,0:T(8,128)(2,1)S(1)} %get-tuple-element.77), channel_id=1, source_target_pairs={{0,2},{1,3},{2,0},{3,1},{4,6},{5,7},{6,4},{7,5},{8,10},{9,11},{10,... | collective-permute-start | bytes 294920 | tf_op jit(solution)/shard_map/ppermute | solution.py:319
  50.8 1.4 %collective-permute-done.16 = bf16[16,3072]{1,0:T(8,128)(2,1)S(1)} collective-permute-done((bf16[16,3072]{1,0:T(8,128)(2,1)S(1)}, bf16[16,3072]{1,0:T(8,128)(2,1)S(1)}, u32[]{:S(2)}, u32[]{:S(2)}) %collective-permute-start.16) | collective-permute-done | bytes 98336 | tf_op jit(solution)/shard_map/ppermute | solution.py:319
  52.2 0.7 collective-permute-start.21
  52.9 1.0 %collective-permute-start.17 = (bf16[16,6144]{1,0:T(8,128)(2,1)S(1)}, bf16[16,6144]{1,0:T(8,128)(2,1)S(1)}, u32[]{:S(2)}, u32[]{:S(2)}) collective-permute-start(bf16[16,6144]{1,0:T(8,128)(2,1)S(1)} %get-tuple-element.69), channel_id=1, source_target_pairs={{0,2},{1,3},{2,0},{3,1},{4,6},{5,7},{6,4},{7,5},{8,10},{9,11},{10,... | collective-permute-start | bytes 589832 | tf_op jit(solution)/shard_map/ppermute | solution.py:319
  54.0 0.4 collective-permute-done.14
  54.3 2.4 %collective-permute-start.19 = (bf16[16,3072]{1,0:T(8,128)(2,1)S(1)}, bf16[16,3072]{1,0:T(8,128)(2,1)S(1)}, u32[]{:S(2)}, u32[]{:S(2)}) collective-permute-start(bf16[16,3072]{1,0:T(8,128)(2,1)S(1)} %add_convert_fusion.5), channel_id=1, source_target_pairs={{0,8},{1,9},{2,10},{3,11},{4,12},{5,13},{6,14},{7,15},{8,0},{9,1},... | collective-permute-start | bytes 294920 | tf_op jit(solution)/shard_map/ppermute | solution.py:314
  56.8 0.6 collective-permute-start.15
  57.3 2.3 %collective-permute-done.17 = bf16[16,6144]{1,0:T(8,128)(2,1)S(1)} collective-permute-done((bf16[16,6144]{1,0:T(8,128)(2,1)S(1)}, bf16[16,6144]{1,0:T(8,128)(2,1)S(1)}, u32[]{:S(2)}, u32[]{:S(2)}) %collective-permute-start.17) | collective-permute-done | bytes 196640 | tf_op jit(solution)/shard_map/ppermute | solution.py:319
  59.7 1.8 %collective-permute-done.21.refs_2_ = bf16[16,3072]{1,0:T(8,128)(2,1)S(1)} collective-permute-done((bf16[16,3072]{1,0:T(8,128)(2,1)S(1)}, bf16[16,3072]{1,0:T(8,128)(2,1)S(1)}, u32[]{:S(2)}, u32[]{:S(2)}) %collective-permute-start.21) | collective-permute-done | bytes 98336 | tf_op jit(solution)/shard_map/ppermute | solution.py:314
  61.5 2.2 %collective-permute-start.22 = (bf16[16,6144]{1,0:T(8,128)(2,1)S(1)}, bf16[16,6144]{1,0:T(8,128)(2,1)S(1)}, u32[]{:S(2)}, u32[]{:S(2)}) collective-permute-start(bf16[16,6144]{1,0:T(8,128)(2,1)S(1)} %add_convert_fusion.2), channel_id=1, source_target_pairs={{0,12},{1,13},{2,14},{3,15},{4,0},{5,1},{6,2},{7,3},{8,4},{9,5},{1... | collective-permute-start | bytes 589832 | tf_op jit(solution)/shard_map/ppermute | solution.py:314
  63.7 0.0 collective-permute-done.15
  63.8 0.0 collective-permute-done.19.refs_3_
  63.8 1.3 %collective-permute-start.18 = (bf16[16,6144]{1,0:T(8,128)(2,1)S(1)}, bf16[16,6144]{1,0:T(8,128)(2,1)S(1)}, u32[]{:S(2)}, u32[]{:S(2)}) collective-permute-start(bf16[16,6144]{1,0:T(8,128)(2,1)S(1)} %pad_maximum_fusion), channel_id=1, source_target_pairs={{0,2},{1,3},{2,0},{3,1},{4,6},{5,7},{6,4},{7,5},{8,10},{9,11},{10,... | collective-permute-start | bytes 589832 | tf_op jit(solution)/shard_map/ppermute | solution.py:319
  65.1 1.2 %collective-permute-start.20 = (bf16[16,6144]{1,0:T(8,128)(2,1)S(1)}, bf16[16,6144]{1,0:T(8,128)(2,1)S(1)}, u32[]{:S(2)}, u32[]{:S(2)}) collective-permute-start(bf16[16,6144]{1,0:T(8,128)(2,1)S(1)} %add_convert_fusion.3), channel_id=1, source_target_pairs={{0,4},{1,5},{2,6},{3,7},{4,8},{5,9},{6,10},{7,11},{8,12},{9,13},{1... | collective-permute-start | bytes 589832 | tf_op jit(solution)/shard_map/ppermute | solution.py:314
  66.3 0.0 copy-done.1
  66.3 0.0 copy-done.2
  66.3 0.2 shares.1.terms_ref
  66.5 2.0 %collective-permute-done.22.near = bf16[16,6144]{1,0:T(8,128)(2,1)S(1)} collective-permute-done((bf16[16,6144]{1,0:T(8,128)(2,1)S(1)}, bf16[16,6144]{1,0:T(8,128)(2,1)S(1)}, u32[]{:S(2)}, u32[]{:S(2)}) %collective-permute-start.22) | collective-permute-done | bytes 196640 | tf_op jit(solution)/shard_map/ppermute | solution.py:314
  68.5 1.0 %collective-permute-done.18.arrived = bf16[16,6144]{1,0:T(8,128)(2,1)S(1)} collective-permute-done((bf16[16,6144]{1,0:T(8,128)(2,1)S(1)}, bf16[16,6144]{1,0:T(8,128)(2,1)S(1)}, u32[]{:S(2)}, u32[]{:S(2)}) %collective-permute-start.18) | collective-permute-done | bytes 196640 | tf_op jit(solution)/shard_map/ppermute | solution.py:319
  69.5 3.0 %collective-permute-done.20.last = bf16[16,6144]{1,0:T(8,128)(2,1)S(1)} collective-permute-done((bf16[16,6144]{1,0:T(8,128)(2,1)S(1)}, bf16[16,6144]{1,0:T(8,128)(2,1)S(1)}, u32[]{:S(2)}, u32[]{:S(2)}) %collective-permute-start.20) | collective-permute-done | bytes 196640 | tf_op jit(solution)/shard_map/ppermute | solution.py:314
  72.5 0.0 copy-done
  72.5 1.1 %mix.1 = bf16[24,6144]{1,0:T(8,128)(2,1)} custom-call(f32[72,64]{1,0:T(8,128)S(1)} %shares.1.terms_ref, bf16[24,6144]{1,0:T(8,128)(2,1)S(1)} %copy-done, bf16[16,6144]{1,0:T(8,128)(2,1)S(1)} %collective-permute-done.18.arrived, bf16[16,6144]{1,0:T(8,128)(2,1)S(1)} %collective-permute-done.20.last, bf16[16,6144]{1,0:T(8,128)(2,1)S(1)} %collective-permute-done.22.near, ...), custom_call_target="tpu_custom_call" | custom-call | tf_op jit(solution)/shard_map/mix/pallas_call | solution.py:293
  (20 shorter events, 0.4 us)
Async XLA Ops:
  1.5 14.6 %collective-permute-start.1 = (bf16[16,3584]{1,0:T(8,128)(2,1)S(1)}, bf16[16,3584]{1,0:T(8,128)(2,1)S(1)}, u32[]{:S(2)}, u32[]{:S(2)}) collective-permute-start(bf16[16,3584]{1,0:T(8,128)(2,1)S(1)} %get-tuple-element.47), channel_id=1, source_target_pairs={{0,4},{1,5},{2,6},{3,7},{4,8},{5,9},{6,10},{7,11},{8,12},{9,13},{1... | collective-permute-start | bytes 344072 | tf_op jit(solution)/shard_map/ppermute | solution.py:314
  4.6 11.6 %collective-permute-start.2 = (bf16[16,3584]{1,0:T(8,128)(2,1)S(1)}, bf16[16,3584]{1,0:T(8,128)(2,1)S(1)}, u32[]{:S(2)}, u32[]{:S(2)}) collective-permute-start(bf16[16,3584]{1,0:T(8,128)(2,1)S(1)} %get-tuple-element.48), channel_id=1, source_target_pairs={{0,12},{1,13},{2,14},{3,15},{4,0},{5,1},{6,2},{7,3},{8,4},{9,5},{1... | collective-permute-start | bytes 344072 | tf_op jit(solution)/shard_map/ppermute | solution.py:314
  6.7 10.4 %collective-permute-start.3 = (bf16[16,3584]{1,0:T(8,128)(2,1)S(1)}, bf16[16,3584]{1,0:T(8,128)(2,1)S(1)}, u32[]{:S(2)}, u32[]{:S(2)}) collective-permute-start(bf16[16,3584]{1,0:T(8,128)(2,1)S(1)} %get-tuple-element.49), channel_id=1, source_target_pairs={{0,8},{1,9},{2,10},{3,11},{4,12},{5,13},{6,14},{7,15},{8,0},{9,1},... | collective-permute-start | bytes 344072 | tf_op jit(solution)/shard_map/ppermute | solution.py:314
  11.0 7.7 %collective-permute-start = (bf16[16,6144]{1,0:T(8,128)(2,1)S(1)}, bf16[16,6144]{1,0:T(8,128)(2,1)S(1)}, u32[]{:S(2)}, u32[]{:S(2)}) collective-permute-start(bf16[16,6144]{1,0:T(8,128)(2,1)S(1)} %get-tuple-element.43.after_ref.refs_0_), channel_id=1, source_target_pairs={{0,2},{1,3},{2,0},{3,1},{4,6},{5,7},{6,4},{7,5},{8,10},{9,11},{10,... | collective-permute-start | bytes 589832 | tf_op jit(solution)/shard_map/ppermute | solution.py:319
  17.1 10.0 %collective-permute-start.8 = (bf16[48,3584]{1,0:T(8,128)(2,1)S(1)}, bf16[48,3584]{1,0:T(8,128)(2,1)S(1)}, u32[]{:S(2)}, u32[]{:S(2)}) collective-permute-start(bf16[48,3584]{1,0:T(8,128)(2,1)S(1)} %get-tuple-element.53.refs_3_.refs_1_), channel_id=1, source_target_pairs={{0,2},{1,3},{2,0},{3,1},{4,6},{5,7},{6,4},{7,5},{8,10},{9,11},{10,... | collective-permute-start | bytes 1032200 | tf_op jit(solution)/shard_map/ppermute | solution.py:319
  18.7 7.2 %collective-permute-start.4 = (bf16[16,2560]{1,0:T(8,128)(2,1)S(1)}, bf16[16,2560]{1,0:T(8,128)(2,1)S(1)}, u32[]{:S(2)}, u32[]{:S(2)}) collective-permute-start(bf16[16,2560]{1,0:T(8,128)(2,1)S(1)} %get-tuple-element.50), channel_id=1, source_target_pairs={{0,4},{1,5},{2,6},{3,7},{4,8},{5,9},{6,10},{7,11},{8,12},{9,13},{1... | collective-permute-start | bytes 245768 | tf_op jit(solution)/shard_map/ppermute | solution.py:314
  18.8 7.2 %collective-permute-start.5 = (bf16[16,2560]{1,0:T(8,128)(2,1)S(1)}, bf16[16,2560]{1,0:T(8,128)(2,1)S(1)}, u32[]{:S(2)}, u32[]{:S(2)}) collective-permute-start(bf16[16,2560]{1,0:T(8,128)(2,1)S(1)} %get-tuple-element.51), channel_id=1, source_target_pairs={{0,12},{1,13},{2,14},{3,15},{4,0},{5,1},{6,2},{7,3},{8,4},{9,5},{1... | collective-permute-start | bytes 245768 | tf_op jit(solution)/shard_map/ppermute | solution.py:314
  22.6 6.3 %collective-permute-start.6 = (bf16[16,2560]{1,0:T(8,128)(2,1)S(1)}, bf16[16,2560]{1,0:T(8,128)(2,1)S(1)}, u32[]{:S(2)}, u32[]{:S(2)}) collective-permute-start(bf16[16,2560]{1,0:T(8,128)(2,1)S(1)} %get-tuple-element.52), channel_id=1, source_target_pairs={{0,8},{1,9},{2,10},{3,11},{4,12},{5,13},{6,14},{7,15},{8,0},{9,1},... | collective-permute-start | bytes 245768 | tf_op jit(solution)/shard_map/ppermute | solution.py:314
  27.2 2.5 %collective-permute-start.9 = (bf16[128,3584]{1,0:T(8,128)(2,1)S(1)}, bf16[128,3584]{1,0:T(8,128)(2,1)S(1)}, u32[]{:S(2)}, u32[]{:S(2)}) collective-permute-start(bf16[128,3584]{1,0:T(8,128)(2,1)S(1)} %constant_dynamic-update-slice_fusion.6), channel_id=1, source_target_pairs={{0,1},{1,0},{2,3},{3,2},{4,5},{5,4},{6,7},{7,6},{8,9},{9,8},{10,11... | collective-permute-start | bytes 2752520 | tf_op jit(solution)/shard_map/ppermute | solution.py:319
  29.0 6.7 %collective-permute-start.7 = (bf16[48,2560]{1,0:T(8,128)(2,1)S(1)}, bf16[48,2560]{1,0:T(8,128)(2,1)S(1)}, u32[]{:S(2)}, u32[]{:S(2)}) collective-permute-start(bf16[48,2560]{1,0:T(8,128)(2,1)S(1)} %get-tuple-element.94.refs_1_), channel_id=1, source_target_pairs={{0,2},{1,3},{2,0},{3,1},{4,6},{5,7},{6,4},{7,5},{8,10},{9,11},{10,... | collective-permute-start | bytes 737288 | tf_op jit(solution)/shard_map/ppermute | solution.py:319
  29.7 6.1 %collective-permute-start.10 = (bf16[80,2560]{1,0:T(8,128)(2,1)S(1)}, bf16[80,2560]{1,0:T(8,128)(2,1)S(1)}, u32[]{:S(2)}, u32[]{:S(2)}) collective-permute-start(bf16[80,2560]{1,0:T(8,128)(2,1)S(1)} %slice_dynamic-update-slice_fusion.2), channel_id=1, source_target_pairs={{0,1},{1,0},{2,3},{3,2},{4,5},{5,4},{6,7},{7,6},{8,9},{9,8},{10,11... | collective-permute-start | bytes 1228808 | tf_op jit(solution)/shard_map/ppermute | solution.py:319
  35.7 1.5 %collective-permute-start.11 = (bf16[48,2560]{1,0:T(8,128)(2,1)S(1)}, bf16[48,2560]{1,0:T(8,128)(2,1)S(1)}, u32[]{:S(2)}, u32[]{:S(2)}) collective-permute-start(bf16[48,2560]{1,0:T(8,128)(2,1)S(1)} %collective-permute-done.7.refs_3_), channel_id=1, source_target_pairs={{0,1},{1,0},{2,3},{3,2},{4,5},{5,4},{6,7},{7,6},{8,9},{9,8},{10,11... | collective-permute-start | bytes 737288 | tf_op jit(solution)/shard_map/ppermute | solution.py:319
  43.8 3.3 %collective-permute-start.12 = (bf16[128,3072]{1,0:T(8,128)(2,1)S(1)}, bf16[128,3072]{1,0:T(8,128)(2,1)S(1)}, u32[]{:S(2)}, u32[]{:S(2)}) collective-permute-start(bf16[128,3072]{1,0:T(8,128)(2,1)S(1)} %get-tuple-element.64), channel_id=1, source_target_pairs={{0,1},{1,0},{2,3},{3,2},{4,5},{5,4},{6,7},{7,6},{8,9},{9,8},{10,11... | collective-permute-start | bytes 2359304 | tf_op jit(solution)/shard_map/ppermute | solution.py:319
  46.6 2.4 %collective-permute-start.13 = (bf16[128,3072]{1,0:T(8,128)(2,1)S(1)}, bf16[128,3072]{1,0:T(8,128)(2,1)S(1)}, u32[]{:S(2)}, u32[]{:S(2)}) collective-permute-start(bf16[128,3072]{1,0:T(8,128)(2,1)S(1)} %get-tuple-element.67), channel_id=1, source_target_pairs={{0,1},{1,0},{2,3},{3,2},{4,5},{5,4},{6,7},{7,6},{8,9},{9,8},{10,11... | collective-permute-start | bytes 2359304 | tf_op jit(solution)/shard_map/ppermute | solution.py:319
  47.0 19.3 %copy-start.1 = (s32[24,2]{0,1:T(2,128)S(1)}, s32[24,2]{0,1:T(2,128)}, u32[]{:S(2)}) copy-start(s32[24,2]{0,1:T(2,128)} %param.8) | copy-start | bytes 580
  47.0 19.3 %copy-start.2 = (f32[24,2]{0,1:T(2,128)S(1)}, f32[24,2]{0,1:T(2,128)}, u32[]{:S(2)}) copy-start(f32[24,2]{0,1:T(2,128)} %param.9) | copy-start | bytes 580
  47.2 25.3 %copy-start = (bf16[24,6144]{1,0:T(8,128)(2,1)S(1)}, bf16[24,6144]{1,0:T(8,128)(2,1)}, u32[]{:S(2)}) copy-start(bf16[24,6144]{1,0:T(8,128)(2,1)} %act_ref.3) | copy-start | bytes 884740
  47.3 4.9 %collective-permute-start.16 = (bf16[16,3072]{1,0:T(8,128)(2,1)S(1)}, bf16[16,3072]{1,0:T(8,128)(2,1)S(1)}, u32[]{:S(2)}, u32[]{:S(2)}) collective-permute-start(bf16[16,3072]{1,0:T(8,128)(2,1)S(1)} %get-tuple-element.83), channel_id=1, source_target_pairs={{0,2},{1,3},{2,0},{3,1},{4,6},{5,7},{6,4},{7,5},{8,10},{9,11},{10,... | collective-permute-start | bytes 294920 | tf_op jit(solution)/shard_map/ppermute | solution.py:319
  49.2 5.1 %collective-permute-start.14 = (bf16[16,3072]{1,0:T(8,128)(2,1)S(1)}, bf16[16,3072]{1,0:T(8,128)(2,1)S(1)}, u32[]{:S(2)}, u32[]{:S(2)}) collective-permute-start(bf16[16,3072]{1,0:T(8,128)(2,1)S(1)} %get-tuple-element.77), channel_id=1, source_target_pairs={{0,2},{1,3},{2,0},{3,1},{4,6},{5,7},{6,4},{7,5},{8,10},{9,11},{10,... | collective-permute-start | bytes 294920 | tf_op jit(solution)/shard_map/ppermute | solution.py:319
  52.2 9.3 %collective-permute-start.21 = (bf16[16,3072]{1,0:T(8,128)(2,1)S(1)}, bf16[16,3072]{1,0:T(8,128)(2,1)S(1)}, u32[]{:S(2)}, u32[]{:S(2)}) collective-permute-start(bf16[16,3072]{1,0:T(8,128)(2,1)S(1)} %add_convert_fusion.4), channel_id=1, source_target_pairs={{0,8},{1,9},{2,10},{3,11},{4,12},{5,13},{6,14},{7,15},{8,0},{9,1},... | collective-permute-start | bytes 294920 | tf_op jit(solution)/shard_map/ppermute | solution.py:314
  52.9 6.7 %collective-permute-start.17 = (bf16[16,6144]{1,0:T(8,128)(2,1)S(1)}, bf16[16,6144]{1,0:T(8,128)(2,1)S(1)}, u32[]{:S(2)}, u32[]{:S(2)}) collective-permute-start(bf16[16,6144]{1,0:T(8,128)(2,1)S(1)} %get-tuple-element.69), channel_id=1, source_target_pairs={{0,2},{1,3},{2,0},{3,1},{4,6},{5,7},{6,4},{7,5},{8,10},{9,11},{10,... | collective-permute-start | bytes 589832 | tf_op jit(solution)/shard_map/ppermute | solution.py:319
  54.3 9.4 %collective-permute-start.19 = (bf16[16,3072]{1,0:T(8,128)(2,1)S(1)}, bf16[16,3072]{1,0:T(8,128)(2,1)S(1)}, u32[]{:S(2)}, u32[]{:S(2)}) collective-permute-start(bf16[16,3072]{1,0:T(8,128)(2,1)S(1)} %add_convert_fusion.5), channel_id=1, source_target_pairs={{0,8},{1,9},{2,10},{3,11},{4,12},{5,13},{6,14},{7,15},{8,0},{9,1},... | collective-permute-start | bytes 294920 | tf_op jit(solution)/shard_map/ppermute | solution.py:314
  56.8 7.0 %collective-permute-start.15 = (bf16[16,6144]{1,0:T(8,128)(2,1)S(1)}, bf16[16,6144]{1,0:T(8,128)(2,1)S(1)}, u32[]{:S(2)}, u32[]{:S(2)}) collective-permute-start(bf16[16,6144]{1,0:T(8,128)(2,1)S(1)} %get-tuple-element.68), channel_id=1, source_target_pairs={{0,2},{1,3},{2,0},{3,1},{4,6},{5,7},{6,4},{7,5},{8,10},{9,11},{10,... | collective-permute-start | bytes 589832 | tf_op jit(solution)/shard_map/ppermute | solution.py:319
  61.5 7.0 %collective-permute-start.22 = (bf16[16,6144]{1,0:T(8,128)(2,1)S(1)}, bf16[16,6144]{1,0:T(8,128)(2,1)S(1)}, u32[]{:S(2)}, u32[]{:S(2)}) collective-permute-start(bf16[16,6144]{1,0:T(8,128)(2,1)S(1)} %add_convert_fusion.2), channel_id=1, source_target_pairs={{0,12},{1,13},{2,14},{3,15},{4,0},{5,1},{6,2},{7,3},{8,4},{9,5},{1... | collective-permute-start | bytes 589832 | tf_op jit(solution)/shard_map/ppermute | solution.py:314
  63.8 5.7 %collective-permute-start.18 = (bf16[16,6144]{1,0:T(8,128)(2,1)S(1)}, bf16[16,6144]{1,0:T(8,128)(2,1)S(1)}, u32[]{:S(2)}, u32[]{:S(2)}) collective-permute-start(bf16[16,6144]{1,0:T(8,128)(2,1)S(1)} %pad_maximum_fusion), channel_id=1, source_target_pairs={{0,2},{1,3},{2,0},{3,1},{4,6},{5,7},{6,4},{7,5},{8,10},{9,11},{10,... | collective-permute-start | bytes 589832 | tf_op jit(solution)/shard_map/ppermute | solution.py:319
  65.1 7.5 %collective-permute-start.20 = (bf16[16,6144]{1,0:T(8,128)(2,1)S(1)}, bf16[16,6144]{1,0:T(8,128)(2,1)S(1)}, u32[]{:S(2)}, u32[]{:S(2)}) collective-permute-start(bf16[16,6144]{1,0:T(8,128)(2,1)S(1)} %add_convert_fusion.3), channel_id=1, source_target_pairs={{0,4},{1,5},{2,6},{3,7},{4,8},{5,9},{6,10},{7,11},{8,12},{9,13},{1... | collective-permute-start | bytes 589832 | tf_op jit(solution)/shard_map/ppermute | solution.py:314

commit v20 on v18

--- a/solution.py
+++ b/solution.py
@@ -150,12 +150,20 @@
             parts.append(p[:, pl.ds(pl.multiple_of(first, BLOCK), BLOCK)])
         turned[pl.ds(pl.multiple_of(c * BLOCK, BLOCK), BLOCK), :] = jnp.concatenate(parts, axis=0).T
 
-    for j in range(2):
-        total = jnp.dot(weights[j][...], turned[...], preferred_element_type=jnp.float32)
-        sums[j][...] = total if begin else total + before[j][...]
-    if end:
-        hidden = (jax.nn.silu(sums[0][...]) * sums[1][...]).astype(jnp.bfloat16)
-        hidden_ref[...] = hidden.T
+    units = weights[0].shape[0]
+    block = 384 if end and units % 384 == 0 else units
+    for first in range(0, units, block):
+        here = slice(first, first + block)
+        totals = []
+        for j in range(2):
+            total = jnp.dot(weights[j][here, :], turned[...], preferred_element_type=jnp.float32)
+            totals.append(total if begin else total + before[j][here, :])
+        if end:
+            hidden = (jax.nn.silu(totals[0]) * totals[1]).astype(jnp.bfloat16)
+            hidden_ref[:, here] = hidden.T
+        else:
+            sums[0][...] = totals[0]
+            sums[1][...] = totals[1]
     for copy in copies:
         copy.wait()
 
@@ -171,7 +179,6 @@
     scratch = []
     if end:
         out_shape.append(jax.ShapeDtypeStruct((rows, hidden), jnp.bfloat16))
-        scratch += [pltpu.VMEM((hidden, rows), jnp.float32)] * 2
     else:
         out_shape += [total] * 2
     out_specs += [VMEM] * (len(out_shape) - len(later))

time: 73.7 us -> 73.6 us (level)
  no operation moved by 1% of the time
where the time goes in v20:
time: 73.6 us; the launch traced here: 73.5 us
  starting transfers between devices  25.6 us (35%)
  Pallas kernels  24.3 us (33%)
  waiting for transfers between devices  22.5 us (31%)
    ppermute x10, starting transfers between devices, shift(): lax.ppermute(x, 'expert', [(i, (i + s * group) % devices) for i in range(...  16.3 us
    ppermute x10, waiting for transfers between devices, shift(): lax.ppermute(x, 'expert', [(i, (i + s * group) % devices) for i in range(...  14.9 us
    pallas_call x2, Pallas kernels, gate_up(): pl.pallas_call(functools.partial(gate_up_kernel, len(pieces), len(later),...  9.52 us
    ppermute x13, starting transfers between devices, swap(): return lax.ppermute(x, 'expert', [(i, i ^ bit) for i in range(devices)])  9.32 us
    ppermute x13, waiting for transfers between devices, swap(): return lax.ppermute(x, 'expert', [(i, i ^ bit) for i in range(devices)])  7.65 us
    pallas_call x2, Pallas kernels, fetch(): pl.pallas_call(functools.partial(fetch_kernel, at), in_specs=[ANY, ANY],...  6.87 us
    pallas_call x2, Pallas kernels, down(): pl.pallas_call(functools.partial(down_kernel, ahead, segments), in_specs=...  5.11 us
    pallas_call x1, Pallas kernels, pack(): pl.pallas_call(functools.partial(pack_kernel, group), grid=(1,), in_specs...  1.48 us
  transfers between devices with their start and end apart: 23, of which 15 were waited for; matrix products, arithmetic and copies ran while one was open for 1% of the time, Pallas kernels for 21%

profile of v20, /device:TPU:0, one launch (start us, length us, event | category | flops | bytes accessed | tf_op | source)
XLA Modules:
  0.0 73.5 jit_solution(11260773799492964595)
XLA Ops:
  0.0 1.5 %norm_and_pack.1 = (bf16[16,6144]{1,0:T(8,128)(2,1)S(1)}, bf16[16,3584]{1,0:T(8,128)(2,1)S(1)}, bf16[16,3584]{1,0:T(8,128)(2,1)S(1)}, bf16[16,3584]{1,0:T(8,128)...) custom-call(s32[2,24]{1,0:T(2,128)} %bitcast.3, ...), custom_call_target="tpu_custom_call" | custom-call | tf_op jit(solution)/shard_map/norm_and_pack/pallas_call | solution.py:67
  1.5 3.1 %collective-permute-start.1 = (bf16[16,3584]{1,0:T(8,128)(2,1)S(1)}, bf16[16,3584]{1,0:T(8,128)(2,1)S(1)}, u32[]{:S(2)}, u32[]{:S(2)}) collective-permute-start(bf16[16,3584]{1,0:T(8,128)(2,1)S(1)} %get-tuple-element.47), channel_id=1, source_target_pairs={{0,4},{1,5},{2,6},{3,7},{4,8},{5,9},{6,10},{7,11},{8,12},{9,13},{1... | collective-permute-start | bytes 344072 | tf_op jit(solution)/shard_map/ppermute | solution.py:321
  4.6 2.1 %collective-permute-start.2 = (bf16[16,3584]{1,0:T(8,128)(2,1)S(1)}, bf16[16,3584]{1,0:T(8,128)(2,1)S(1)}, u32[]{:S(2)}, u32[]{:S(2)}) collective-permute-start(bf16[16,3584]{1,0:T(8,128)(2,1)S(1)} %get-tuple-element.48), channel_id=1, source_target_pairs={{0,12},{1,13},{2,14},{3,15},{4,0},{5,1},{6,2},{7,3},{8,4},{9,5},{1... | collective-permute-start | bytes 344072 | tf_op jit(solution)/shard_map/ppermute | solution.py:321
  6.7 0.9 %collective-permute-start.3 = (bf16[16,3584]{1,0:T(8,128)(2,1)S(1)}, bf16[16,3584]{1,0:T(8,128)(2,1)S(1)}, u32[]{:S(2)}, u32[]{:S(2)}) collective-permute-start(bf16[16,3584]{1,0:T(8,128)(2,1)S(1)} %get-tuple-element.49), channel_id=1, source_target_pairs={{0,8},{1,9},{2,10},{3,11},{4,12},{5,13},{6,14},{7,15},{8,0},{9,1},... | collective-permute-start | bytes 344072 | tf_op jit(solution)/shard_map/ppermute | solution.py:321
  7.6 3.4 %fetch.2.refs_5_ = bf16[1152,3584]{1,0:T(8,128)(2,1)S(1)} custom-call(bf16[1152,6144]{1,0:T(8,128)(2,1)} %refs_7_.1, bf16[16,6144]{1,0:T(8,128)(2,1)S(1)} %get-tuple-element.43.after_ref.refs_0_), custom_call_target="tpu_custom_call" | custom-call | bytes 16515072 | tf_op jit(solution)/shard_map/fetch/pallas_call | solution.py:100
  11.0 1.6 %collective-permute-start = (bf16[16,6144]{1,0:T(8,128)(2,1)S(1)}, bf16[16,6144]{1,0:T(8,128)(2,1)S(1)}, u32[]{:S(2)}, u32[]{:S(2)}) collective-permute-start(bf16[16,6144]{1,0:T(8,128)(2,1)S(1)} %get-tuple-element.43.after_ref.refs_0_), channel_id=1, source_target_pairs={{0,2},{1,3},{2,0},{3,1},{4,6},{5,7},{6,4},{7,5},{8,10},{9,11},{10,... | collective-permute-start | bytes 589832 | tf_op jit(solution)/shard_map/ppermute | solution.py:326
  12.7 3.4 %fetch.3.refs_6_ = bf16[1152,3584]{1,0:T(8,128)(2,1)S(1)} custom-call(bf16[1152,6144]{1,0:T(8,128)(2,1)} %refs_8_.2, bf16[16,6144]{1,0:T(8,128)(2,1)S(1)} %get-tuple-element.43.after_ref.refs_0_), custom_call_target="tpu_custom_call" | custom-call | bytes 16515072 | tf_op jit(solution)/shard_map/fetch/pallas_call | solution.py:100
  16.1 0.0 collective-permute-done.1
  16.1 0.0 collective-permute-done.2
  16.2 0.9 %collective-permute-done.3 = bf16[16,3584]{1,0:T(8,128)(2,1)S(1)} collective-permute-done((bf16[16,3584]{1,0:T(8,128)(2,1)S(1)}, bf16[16,3584]{1,0:T(8,128)(2,1)S(1)}, u32[]{:S(2)}, u32[]{:S(2)}) %collective-permute-start.3) | collective-permute-done | bytes 114720 | tf_op jit(solution)/shard_map/ppermute | solution.py:321
  17.1 1.6 %collective-permute-start.8 = (bf16[48,3584]{1,0:T(8,128)(2,1)S(1)}, bf16[48,3584]{1,0:T(8,128)(2,1)S(1)}, u32[]{:S(2)}, u32[]{:S(2)}) collective-permute-start(bf16[48,3584]{1,0:T(8,128)(2,1)S(1)} %get-tuple-element.53.refs_3_.refs_1_), channel_id=1, source_target_pairs={{0,2},{1,3},{2,0},{3,1},{4,6},{5,7},{6,4},{7,5},{8,10},{9,11},{10,... | collective-permute-start | bytes 1032200 | tf_op jit(solution)/shard_map/ppermute | solution.py:326
  18.7 0.0 collective-permute-done.refs_2_
  18.7 0.1 collective-permute-start.4
  18.8 3.8 %collective-permute-start.5 = (bf16[16,2560]{1,0:T(8,128)(2,1)S(1)}, bf16[16,2560]{1,0:T(8,128)(2,1)S(1)}, u32[]{:S(2)}, u32[]{:S(2)}) collective-permute-start(bf16[16,2560]{1,0:T(8,128)(2,1)S(1)} %get-tuple-element.51), channel_id=1, source_target_pairs={{0,12},{1,13},{2,14},{3,15},{4,0},{5,1},{6,2},{7,3},{8,4},{9,5},{1... | collective-permute-start | bytes 245768 | tf_op jit(solution)/shard_map/ppermute | solution.py:321
  22.6 0.0 collective-permute-start.6
  22.6 3.3 %collective-permute-done.4 = bf16[16,2560]{1,0:T(8,128)(2,1)S(1)} collective-permute-done((bf16[16,2560]{1,0:T(8,128)(2,1)S(1)}, bf16[16,2560]{1,0:T(8,128)(2,1)S(1)}, u32[]{:S(2)}, u32[]{:S(2)}) %collective-permute-start.4) | collective-permute-done | bytes 81952 | tf_op jit(solution)/shard_map/ppermute | solution.py:321
  26.0 0.0 collective-permute-done.5
  26.0 1.2 %collective-permute-done.8.refs_3_ = bf16[48,3584]{1,0:T(8,128)(2,1)S(1)} collective-permute-done((bf16[48,3584]{1,0:T(8,128)(2,1)S(1)}, bf16[48,3584]{1,0:T(8,128)(2,1)S(1)}, u32[]{:S(2)}, u32[]{:S(2)}) %collective-permute-start.8) | collective-permute-done | bytes 344096 | tf_op jit(solution)/shard_map/ppermute | solution.py:326
  27.2 0.1 collective-permute-start.9
  27.3 1.7 %collective-permute-done.6 = bf16[16,2560]{1,0:T(8,128)(2,1)S(1)} collective-permute-done((bf16[16,2560]{1,0:T(8,128)(2,1)S(1)}, bf16[16,2560]{1,0:T(8,128)(2,1)S(1)}, u32[]{:S(2)}, u32[]{:S(2)}) %collective-permute-start.6) | collective-permute-done | bytes 81952 | tf_op jit(solution)/shard_map/ppermute | solution.py:321
  29.0 0.7 collective-permute-start.7
  29.7 0.0 collective-permute-start.10
  29.7 0.0 collective-permute-done.9.refs_4_
  29.7 5.5 %gate_up.2 = (bf16[1152,2560]{1,0:T(8,128)(2,1)S(1)}, bf16[1152,2560]{1,0:T(8,128)(2,1)S(1)}, f32[1152,256]{1,0:T(8,128)S(1)}, f32[1152,256]{1,0:T(8,128)S(1)}) custom-call(bf16[16,6144]{1,0:T(8,128)(2,1)S(1)} %get-tuple-element.43.after_ref.refs_0_, bf16[48,3584]{1,0:T(8,128)(2,1)S(1)} %get-tuple-element.53.refs_3_.refs_1_, ...), custom_call_target="tpu_custom_call" | custom-call | flops 4227858432 | bytes 18874368 | tf_op jit(solution)/shard_map/gate_up/pallas_call | solution.py:189
  35.3 0.4 collective-permute-done.7.refs_3_
  35.7 0.1 collective-permute-start.11
  35.8 0.0 collective-permute-done.10.refs_4_
  35.8 1.4 %collective-permute-done.11.refs_5_ = bf16[48,2560]{1,0:T(8,128)(2,1)S(1)} collective-permute-done((bf16[48,2560]{1,0:T(8,128)(2,1)S(1)}, bf16[48,2560]{1,0:T(8,128)(2,1)S(1)}, u32[]{:S(2)}, u32[]{:S(2)}) %collective-permute-start.11) | collective-permute-done | bytes 245792 | tf_op jit(solution)/shard_map/ppermute | solution.py:326
  37.2 4.0 %gate_up.3 = (bf16[1152,4096]{1,0:T(8,128)(2,1)S(1)}, bf16[256,1152]{1,0:T(8,128)(2,1)S(1)}) custom-call(bf16[16,6144]{1,0:T(8,128)(2,1)S(1)} %get-tuple-element.43.after_ref.refs_0_, bf16[48,2560]{1,0:T(8,128)(2,1)S(1)} %get-tuple-element.94.refs_1_, bf16[16,6144]{1,0:T(8,128)(2,1)S(1)} %collective-permute-done.refs_2_, ...), custom_call_target="tpu_custom_call" | custom-call | flops 3019898880 | bytes 14155776 | tf_op jit(solution)/shard_map/gate_up/pallas_call | solution.py:189
  41.2 2.5 %down.2 = (bf16[1152,2048]{1,0:T(8,128)(2,1)S(1)}, bf16[128,3072]{1,0:T(8,128)(2,1)S(1)}, bf16[128,3072]{1,0:T(8,128)(2,1)S(1)}) custom-call(bf16[256,1152]{1,0:T(8,128)(2,1)S(1)} %get-tuple-element.61.after_ref.hidden_ref, bf16[1152,4096]{1,0:T(8,128)(2,1)S(1)} %get-tuple-element.62.refs_0_, bf16[1152,6144]{1,0:T(8,128)(2,1)} %refs_1_.1), custom_call_target="tpu_custom_call" | custom-call | flops 1811939328 | bytes 9240576 | tf_op jit(solution)/shard_map/down/pallas_call | solution.py:242
  43.7 0.2 collective-permute-start.12
  43.9 2.6 %down.3 = (bf16[128,3072]{1,0:T(8,128)(2,1)S(1)}, bf16[128,3072]{1,0:T(8,128)(2,1)S(1)}) custom-call(bf16[256,1152]{1,0:T(8,128)(2,1)S(1)} %get-tuple-element.61.after_ref.hidden_ref, bf16[1152,4096]{1,0:T(8,128)(2,1)S(1)} %get-tuple-element.62.refs_0_, bf16[1152,2048]{1,0:T(8,128)(2,1)S(1)} %get-tuple-element.65.refs_1_), custom_call_target="tpu_custom_call" | custom-call | flops 1811939328 | bytes 9240576 | tf_op jit(solution)/shard_map/down/pallas_call | solution.py:242
  46.5 0.4 collective-permute-start.13
  47.0 0.0 collective-permute-done.12
  47.0 0.0 copy-start.1
  47.0 0.0 copy-start.2
  47.0 0.2 add_convert_fusion.1
  47.2 0.0 copy-start
  47.2 1.5 %collective-permute-start.16 = (bf16[16,3072]{1,0:T(8,128)(2,1)S(1)}, bf16[16,3072]{1,0:T(8,128)(2,1)S(1)}, u32[]{:S(2)}, u32[]{:S(2)}) collective-permute-start(bf16[16,3072]{1,0:T(8,128)(2,1)S(1)} %get-tuple-element.83), channel_id=1, source_target_pairs={{0,2},{1,3},{2,0},{3,1},{4,6},{5,7},{6,4},{7,5},{8,10},{9,11},{10,... | collective-permute-start | bytes 294920 | tf_op jit(solution)/shard_map/ppermute | solution.py:326
  48.8 0.1 collective-permute-done.13
  48.9 0.2 add_convert_fusion
  49.1 1.5 %collective-permute-start.14 = (bf16[16,3072]{1,0:T(8,128)(2,1)S(1)}, bf16[16,3072]{1,0:T(8,128)(2,1)S(1)}, u32[]{:S(2)}, u32[]{:S(2)}) collective-permute-start(bf16[16,3072]{1,0:T(8,128)(2,1)S(1)} %get-tuple-element.77), channel_id=1, source_target_pairs={{0,2},{1,3},{2,0},{3,1},{4,6},{5,7},{6,4},{7,5},{8,10},{9,11},{10,... | collective-permute-start | bytes 294920 | tf_op jit(solution)/shard_map/ppermute | solution.py:326
  50.7 1.4 %collective-permute-done.16 = bf16[16,3072]{1,0:T(8,128)(2,1)S(1)} collective-permute-done((bf16[16,3072]{1,0:T(8,128)(2,1)S(1)}, bf16[16,3072]{1,0:T(8,128)(2,1)S(1)}, u32[]{:S(2)}, u32[]{:S(2)}) %collective-permute-start.16) | collective-permute-done | bytes 98336 | tf_op jit(solution)/shard_map/ppermute | solution.py:326
  52.2 0.7 collective-permute-start.21
  52.9 1.0 %collective-permute-start.17 = (bf16[16,6144]{1,0:T(8,128)(2,1)S(1)}, bf16[16,6144]{1,0:T(8,128)(2,1)S(1)}, u32[]{:S(2)}, u32[]{:S(2)}) collective-permute-start(bf16[16,6144]{1,0:T(8,128)(2,1)S(1)} %get-tuple-element.69), channel_id=1, source_target_pairs={{0,2},{1,3},{2,0},{3,1},{4,6},{5,7},{6,4},{7,5},{8,10},{9,11},{10,... | collective-permute-start | bytes 589832 | tf_op jit(solution)/shard_map/ppermute | solution.py:326
  53.9 0.4 collective-permute-done.14
  54.3 2.4 %collective-permute-start.19 = (bf16[16,3072]{1,0:T(8,128)(2,1)S(1)}, bf16[16,3072]{1,0:T(8,128)(2,1)S(1)}, u32[]{:S(2)}, u32[]{:S(2)}) collective-permute-start(bf16[16,3072]{1,0:T(8,128)(2,1)S(1)} %add_convert_fusion.5), channel_id=1, source_target_pairs={{0,8},{1,9},{2,10},{3,11},{4,12},{5,13},{6,14},{7,15},{8,0},{9,1},... | collective-permute-start | bytes 294920 | tf_op jit(solution)/shard_map/ppermute | solution.py:321
  56.7 0.6 collective-permute-start.15
  57.3 2.3 %collective-permute-done.17 = bf16[16,6144]{1,0:T(8,128)(2,1)S(1)} collective-permute-done((bf16[16,6144]{1,0:T(8,128)(2,1)S(1)}, bf16[16,6144]{1,0:T(8,128)(2,1)S(1)}, u32[]{:S(2)}, u32[]{:S(2)}) %collective-permute-start.17) | collective-permute-done | bytes 196640 | tf_op jit(solution)/shard_map/ppermute | solution.py:326
  59.7 1.7 %collective-permute-done.21.refs_2_ = bf16[16,3072]{1,0:T(8,128)(2,1)S(1)} collective-permute-done((bf16[16,3072]{1,0:T(8,128)(2,1)S(1)}, bf16[16,3072]{1,0:T(8,128)(2,1)S(1)}, u32[]{:S(2)}, u32[]{:S(2)}) %collective-permute-start.21) | collective-permute-done | bytes 98336 | tf_op jit(solution)/shard_map/ppermute | solution.py:321
  61.4 1.2 %collective-permute-start.22 = (bf16[16,6144]{1,0:T(8,128)(2,1)S(1)}, bf16[16,6144]{1,0:T(8,128)(2,1)S(1)}, u32[]{:S(2)}, u32[]{:S(2)}) collective-permute-start(bf16[16,6144]{1,0:T(8,128)(2,1)S(1)} %add_convert_fusion.2), channel_id=1, source_target_pairs={{0,4},{1,5},{2,6},{3,7},{4,8},{5,9},{6,10},{7,11},{8,12},{9,13},{1... | collective-permute-start | bytes 589832 | tf_op jit(solution)/shard_map/ppermute | solution.py:321
  62.6 0.4 collective-permute-done.15
  63.0 1.9 %collective-permute-done.19.refs_3_ = bf16[16,3072]{1,0:T(8,128)(2,1)S(1)} collective-permute-done((bf16[16,3072]{1,0:T(8,128)(2,1)S(1)}, bf16[16,3072]{1,0:T(8,128)(2,1)S(1)}, u32[]{:S(2)}, u32[]{:S(2)}) %collective-permute-start.19) | collective-permute-done | bytes 98336 | tf_op jit(solution)/shard_map/ppermute | solution.py:321
  64.9 0.0 collective-permute-start.18
  64.9 1.9 %collective-permute-start.20 = (bf16[16,6144]{1,0:T(8,128)(2,1)S(1)}, bf16[16,6144]{1,0:T(8,128)(2,1)S(1)}, u32[]{:S(2)}, u32[]{:S(2)}) collective-permute-start(bf16[16,6144]{1,0:T(8,128)(2,1)S(1)} %add_convert_fusion.3), channel_id=1, source_target_pairs={{0,12},{1,13},{2,14},{3,15},{4,0},{5,1},{6,2},{7,3},{8,4},{9,5},{1... | collective-permute-start | bytes 589832 | tf_op jit(solution)/shard_map/ppermute | solution.py:321
  66.9 0.0 copy-done.1
  66.9 0.0 copy-done.2
  66.9 0.2 shares.1.terms_ref
  67.1 3.8 %collective-permute-done.22.last = bf16[16,6144]{1,0:T(8,128)(2,1)S(1)} collective-permute-done((bf16[16,6144]{1,0:T(8,128)(2,1)S(1)}, bf16[16,6144]{1,0:T(8,128)(2,1)S(1)}, u32[]{:S(2)}, u32[]{:S(2)}) %collective-permute-start.22) | collective-permute-done | bytes 196640 | tf_op jit(solution)/shard_map/ppermute | solution.py:321
  70.9 0.0 collective-permute-done.18.arrived
  70.9 1.5 %collective-permute-done.20.near = bf16[16,6144]{1,0:T(8,128)(2,1)S(1)} collective-permute-done((bf16[16,6144]{1,0:T(8,128)(2,1)S(1)}, bf16[16,6144]{1,0:T(8,128)(2,1)S(1)}, u32[]{:S(2)}, u32[]{:S(2)}) %collective-permute-start.20) | collective-permute-done | bytes 196640 | tf_op jit(solution)/shard_map/ppermute | solution.py:321
  72.4 0.0 copy-done
  72.4 1.1 %mix.1 = bf16[24,6144]{1,0:T(8,128)(2,1)} custom-call(f32[72,64]{1,0:T(8,128)S(1)} %shares.1.terms_ref, bf16[24,6144]{1,0:T(8,128)(2,1)S(1)} %copy-done, bf16[16,6144]{1,0:T(8,128)(2,1)S(1)} %collective-permute-done.18.arrived, bf16[16,6144]{1,0:T(8,128)(2,1)S(1)} %collective-permute-done.20.near, bf16[16,6144]{1,0:T(8,128)(2,1)S(1)} %collective-permute-done.22.last, ...), custom_call_target="tpu_custom_call" | custom-call | tf_op jit(solution)/shard_map/mix/pallas_call | solution.py:300
  (20 shorter events, 0.4 us)
Async XLA Ops:
  1.5 14.6 %collective-permute-start.1 = (bf16[16,3584]{1,0:T(8,128)(2,1)S(1)}, bf16[16,3584]{1,0:T(8,128)(2,1)S(1)}, u32[]{:S(2)}, u32[]{:S(2)}) collective-permute-start(bf16[16,3584]{1,0:T(8,128)(2,1)S(1)} %get-tuple-element.47), channel_id=1, source_target_pairs={{0,4},{1,5},{2,6},{3,7},{4,8},{5,9},{6,10},{7,11},{8,12},{9,13},{1... | collective-permute-start | bytes 344072 | tf_op jit(solution)/shard_map/ppermute | solution.py:321
  4.6 11.6 %collective-permute-start.2 = (bf16[16,3584]{1,0:T(8,128)(2,1)S(1)}, bf16[16,3584]{1,0:T(8,128)(2,1)S(1)}, u32[]{:S(2)}, u32[]{:S(2)}) collective-permute-start(bf16[16,3584]{1,0:T(8,128)(2,1)S(1)} %get-tuple-element.48), channel_id=1, source_target_pairs={{0,12},{1,13},{2,14},{3,15},{4,0},{5,1},{6,2},{7,3},{8,4},{9,5},{1... | collective-permute-start | bytes 344072 | tf_op jit(solution)/shard_map/ppermute | solution.py:321
  6.7 10.4 %collective-permute-start.3 = (bf16[16,3584]{1,0:T(8,128)(2,1)S(1)}, bf16[16,3584]{1,0:T(8,128)(2,1)S(1)}, u32[]{:S(2)}, u32[]{:S(2)}) collective-permute-start(bf16[16,3584]{1,0:T(8,128)(2,1)S(1)} %get-tuple-element.49), channel_id=1, source_target_pairs={{0,8},{1,9},{2,10},{3,11},{4,12},{5,13},{6,14},{7,15},{8,0},{9,1},... | collective-permute-start | bytes 344072 | tf_op jit(solution)/shard_map/ppermute | solution.py:321
  11.0 7.7 %collective-permute-start = (bf16[16,6144]{1,0:T(8,128)(2,1)S(1)}, bf16[16,6144]{1,0:T(8,128)(2,1)S(1)}, u32[]{:S(2)}, u32[]{:S(2)}) collective-permute-start(bf16[16,6144]{1,0:T(8,128)(2,1)S(1)} %get-tuple-element.43.after_ref.refs_0_), channel_id=1, source_target_pairs={{0,2},{1,3},{2,0},{3,1},{4,6},{5,7},{6,4},{7,5},{8,10},{9,11},{10,... | collective-permute-start | bytes 589832 | tf_op jit(solution)/shard_map/ppermute | solution.py:326
  17.1 10.0 %collective-permute-start.8 = (bf16[48,3584]{1,0:T(8,128)(2,1)S(1)}, bf16[48,3584]{1,0:T(8,128)(2,1)S(1)}, u32[]{:S(2)}, u32[]{:S(2)}) collective-permute-start(bf16[48,3584]{1,0:T(8,128)(2,1)S(1)} %get-tuple-element.53.refs_3_.refs_1_), channel_id=1, source_target_pairs={{0,2},{1,3},{2,0},{3,1},{4,6},{5,7},{6,4},{7,5},{8,10},{9,11},{10,... | collective-permute-start | bytes 1032200 | tf_op jit(solution)/shard_map/ppermute | solution.py:326
  18.7 7.2 %collective-permute-start.4 = (bf16[16,2560]{1,0:T(8,128)(2,1)S(1)}, bf16[16,2560]{1,0:T(8,128)(2,1)S(1)}, u32[]{:S(2)}, u32[]{:S(2)}) collective-permute-start(bf16[16,2560]{1,0:T(8,128)(2,1)S(1)} %get-tuple-element.50), channel_id=1, source_target_pairs={{0,4},{1,5},{2,6},{3,7},{4,8},{5,9},{6,10},{7,11},{8,12},{9,13},{1... | collective-permute-start | bytes 245768 | tf_op jit(solution)/shard_map/ppermute | solution.py:321
  18.8 7.2 %collective-permute-start.5 = (bf16[16,2560]{1,0:T(8,128)(2,1)S(1)}, bf16[16,2560]{1,0:T(8,128)(2,1)S(1)}, u32[]{:S(2)}, u32[]{:S(2)}) collective-permute-start(bf16[16,2560]{1,0:T(8,128)(2,1)S(1)} %get-tuple-element.51), channel_id=1, source_target_pairs={{0,12},{1,13},{2,14},{3,15},{4,0},{5,1},{6,2},{7,3},{8,4},{9,5},{1... | collective-permute-start | bytes 245768 | tf_op jit(solution)/shard_map/ppermute | solution.py:321
  22.6 6.3 %collective-permute-start.6 = (bf16[16,2560]{1,0:T(8,128)(2,1)S(1)}, bf16[16,2560]{1,0:T(8,128)(2,1)S(1)}, u32[]{:S(2)}, u32[]{:S(2)}) collective-permute-start(bf16[16,2560]{1,0:T(8,128)(2,1)S(1)} %get-tuple-element.52), channel_id=1, source_target_pairs={{0,8},{1,9},{2,10},{3,11},{4,12},{5,13},{6,14},{7,15},{8,0},{9,1},... | collective-permute-start | bytes 245768 | tf_op jit(solution)/shard_map/ppermute | solution.py:321
  27.2 2.5 %collective-permute-start.9 = (bf16[128,3584]{1,0:T(8,128)(2,1)S(1)}, bf16[128,3584]{1,0:T(8,128)(2,1)S(1)}, u32[]{:S(2)}, u32[]{:S(2)}) collective-permute-start(bf16[128,3584]{1,0:T(8,128)(2,1)S(1)} %constant_dynamic-update-slice_fusion.6), channel_id=1, source_target_pairs={{0,1},{1,0},{2,3},{3,2},{4,5},{5,4},{6,7},{7,6},{8,9},{9,8},{10,11... | collective-permute-start | bytes 2752520 | tf_op jit(solution)/shard_map/ppermute | solution.py:326
  29.0 6.7 %collective-permute-start.7 = (bf16[48,2560]{1,0:T(8,128)(2,1)S(1)}, bf16[48,2560]{1,0:T(8,128)(2,1)S(1)}, u32[]{:S(2)}, u32[]{:S(2)}) collective-permute-start(bf16[48,2560]{1,0:T(8,128)(2,1)S(1)} %get-tuple-element.94.refs_1_), channel_id=1, source_target_pairs={{0,2},{1,3},{2,0},{3,1},{4,6},{5,7},{6,4},{7,5},{8,10},{9,11},{10,... | collective-permute-start | bytes 737288 | tf_op jit(solution)/shard_map/ppermute | solution.py:326
  29.7 6.1 %collective-permute-start.10 = (bf16[80,2560]{1,0:T(8,128)(2,1)S(1)}, bf16[80,2560]{1,0:T(8,128)(2,1)S(1)}, u32[]{:S(2)}, u32[]{:S(2)}) collective-permute-start(bf16[80,2560]{1,0:T(8,128)(2,1)S(1)} %slice_dynamic-update-slice_fusion.2), channel_id=1, source_target_pairs={{0,1},{1,0},{2,3},{3,2},{4,5},{5,4},{6,7},{7,6},{8,9},{9,8},{10,11... | collective-permute-start | bytes 1228808 | tf_op jit(solution)/shard_map/ppermute | solution.py:326
  35.7 1.5 %collective-permute-start.11 = (bf16[48,2560]{1,0:T(8,128)(2,1)S(1)}, bf16[48,2560]{1,0:T(8,128)(2,1)S(1)}, u32[]{:S(2)}, u32[]{:S(2)}) collective-permute-start(bf16[48,2560]{1,0:T(8,128)(2,1)S(1)} %collective-permute-done.7.refs_3_), channel_id=1, source_target_pairs={{0,1},{1,0},{2,3},{3,2},{4,5},{5,4},{6,7},{7,6},{8,9},{9,8},{10,11... | collective-permute-start | bytes 737288 | tf_op jit(solution)/shard_map/ppermute | solution.py:326
  43.7 3.3 %collective-permute-start.12 = (bf16[128,3072]{1,0:T(8,128)(2,1)S(1)}, bf16[128,3072]{1,0:T(8,128)(2,1)S(1)}, u32[]{:S(2)}, u32[]{:S(2)}) collective-permute-start(bf16[128,3072]{1,0:T(8,128)(2,1)S(1)} %get-tuple-element.64), channel_id=1, source_target_pairs={{0,1},{1,0},{2,3},{3,2},{4,5},{5,4},{6,7},{7,6},{8,9},{9,8},{10,11... | collective-permute-start | bytes 2359304 | tf_op jit(solution)/shard_map/ppermute | solution.py:326
  46.5 2.4 %collective-permute-start.13 = (bf16[128,3072]{1,0:T(8,128)(2,1)S(1)}, bf16[128,3072]{1,0:T(8,128)(2,1)S(1)}, u32[]{:S(2)}, u32[]{:S(2)}) collective-permute-start(bf16[128,3072]{1,0:T(8,128)(2,1)S(1)} %get-tuple-element.67), channel_id=1, source_target_pairs={{0,1},{1,0},{2,3},{3,2},{4,5},{5,4},{6,7},{7,6},{8,9},{9,8},{10,11... | collective-permute-start | bytes 2359304 | tf_op jit(solution)/shard_map/ppermute | solution.py:326
  47.0 19.9 %copy-start.1 = (s32[24,2]{0,1:T(2,128)S(1)}, s32[24,2]{0,1:T(2,128)}, u32[]{:S(2)}) copy-start(s32[24,2]{0,1:T(2,128)} %param.8) | copy-start | bytes 580
  47.0 19.9 %copy-start.2 = (f32[24,2]{0,1:T(2,128)S(1)}, f32[24,2]{0,1:T(2,128)}, u32[]{:S(2)}) copy-start(f32[24,2]{0,1:T(2,128)} %param.9) | copy-start | bytes 580
  47.2 25.2 %copy-start = (bf16[24,6144]{1,0:T(8,128)(2,1)S(1)}, bf16[24,6144]{1,0:T(8,128)(2,1)}, u32[]{:S(2)}) copy-start(bf16[24,6144]{1,0:T(8,128)(2,1)} %act_ref.3) | copy-start | bytes 884740
  47.2 4.9 %collective-permute-start.16 = (bf16[16,3072]{1,0:T(8,128)(2,1)S(1)}, bf16[16,3072]{1,0:T(8,128)(2,1)S(1)}, u32[]{:S(2)}, u32[]{:S(2)}) collective-permute-start(bf16[16,3072]{1,0:T(8,128)(2,1)S(1)} %get-tuple-element.83), channel_id=1, source_target_pairs={{0,2},{1,3},{2,0},{3,1},{4,6},{5,7},{6,4},{7,5},{8,10},{9,11},{10,... | collective-permute-start | bytes 294920 | tf_op jit(solution)/shard_map/ppermute | solution.py:326
  49.1 5.1 %collective-permute-start.14 = (bf16[16,3072]{1,0:T(8,128)(2,1)S(1)}, bf16[16,3072]{1,0:T(8,128)(2,1)S(1)}, u32[]{:S(2)}, u32[]{:S(2)}) collective-permute-start(bf16[16,3072]{1,0:T(8,128)(2,1)S(1)} %get-tuple-element.77), channel_id=1, source_target_pairs={{0,2},{1,3},{2,0},{3,1},{4,6},{5,7},{6,4},{7,5},{8,10},{9,11},{10,... | collective-permute-start | bytes 294920 | tf_op jit(solution)/shard_map/ppermute | solution.py:326
  52.2 9.2 %collective-permute-start.21 = (bf16[16,3072]{1,0:T(8,128)(2,1)S(1)}, bf16[16,3072]{1,0:T(8,128)(2,1)S(1)}, u32[]{:S(2)}, u32[]{:S(2)}) collective-permute-start(bf16[16,3072]{1,0:T(8,128)(2,1)S(1)} %add_convert_fusion.4), channel_id=1, source_target_pairs={{0,8},{1,9},{2,10},{3,11},{4,12},{5,13},{6,14},{7,15},{8,0},{9,1},... | collective-permute-start | bytes 294920 | tf_op jit(solution)/shard_map/ppermute | solution.py:321
  52.9 6.7 %collective-permute-start.17 = (bf16[16,6144]{1,0:T(8,128)(2,1)S(1)}, bf16[16,6144]{1,0:T(8,128)(2,1)S(1)}, u32[]{:S(2)}, u32[]{:S(2)}) collective-permute-start(bf16[16,6144]{1,0:T(8,128)(2,1)S(1)} %get-tuple-element.69), channel_id=1, source_target_pairs={{0,2},{1,3},{2,0},{3,1},{4,6},{5,7},{6,4},{7,5},{8,10},{9,11},{10,... | collective-permute-start | bytes 589832 | tf_op jit(solution)/shard_map/ppermute | solution.py:326
  54.3 10.6 %collective-permute-start.19 = (bf16[16,3072]{1,0:T(8,128)(2,1)S(1)}, bf16[16,3072]{1,0:T(8,128)(2,1)S(1)}, u32[]{:S(2)}, u32[]{:S(2)}) collective-permute-start(bf16[16,3072]{1,0:T(8,128)(2,1)S(1)} %add_convert_fusion.5), channel_id=1, source_target_pairs={{0,8},{1,9},{2,10},{3,11},{4,12},{5,13},{6,14},{7,15},{8,0},{9,1},... | collective-permute-start | bytes 294920 | tf_op jit(solution)/shard_map/ppermute | solution.py:321
  56.7 6.2 %collective-permute-start.15 = (bf16[16,6144]{1,0:T(8,128)(2,1)S(1)}, bf16[16,6144]{1,0:T(8,128)(2,1)S(1)}, u32[]{:S(2)}, u32[]{:S(2)}) collective-permute-start(bf16[16,6144]{1,0:T(8,128)(2,1)S(1)} %get-tuple-element.68), channel_id=1, source_target_pairs={{0,2},{1,3},{2,0},{3,1},{4,6},{5,7},{6,4},{7,5},{8,10},{9,11},{10,... | collective-permute-start | bytes 589832 | tf_op jit(solution)/shard_map/ppermute | solution.py:326
  61.4 9.5 %collective-permute-start.22 = (bf16[16,6144]{1,0:T(8,128)(2,1)S(1)}, bf16[16,6144]{1,0:T(8,128)(2,1)S(1)}, u32[]{:S(2)}, u32[]{:S(2)}) collective-permute-start(bf16[16,6144]{1,0:T(8,128)(2,1)S(1)} %add_convert_fusion.2), channel_id=1, source_target_pairs={{0,4},{1,5},{2,6},{3,7},{4,8},{5,9},{6,10},{7,11},{8,12},{9,13},{1... | collective-permute-start | bytes 589832 | tf_op jit(solution)/shard_map/ppermute | solution.py:321
  64.9 5.9 %collective-permute-start.18 = (bf16[16,6144]{1,0:T(8,128)(2,1)S(1)}, bf16[16,6144]{1,0:T(8,128)(2,1)S(1)}, u32[]{:S(2)}, u32[]{:S(2)}) collective-permute-start(bf16[16,6144]{1,0:T(8,128)(2,1)S(1)} %pad_maximum_fusion), channel_id=1, source_target_pairs={{0,2},{1,3},{2,0},{3,1},{4,6},{5,7},{6,4},{7,5},{8,10},{9,11},{10,... | collective-permute-start | bytes 589832 | tf_op jit(solution)/shard_map/ppermute | solution.py:326
  64.9 7.4 %collective-permute-start.20 = (bf16[16,6144]{1,0:T(8,128)(2,1)S(1)}, bf16[16,6144]{1,0:T(8,128)(2,1)S(1)}, u32[]{:S(2)}, u32[]{:S(2)}) collective-permute-start(bf16[16,6144]{1,0:T(8,128)(2,1)S(1)} %add_convert_fusion.3), channel_id=1, source_target_pairs={{0,12},{1,13},{2,14},{3,15},{4,0},{5,1},{6,2},{7,3},{8,4},{9,5},{1... | collective-permute-start | bytes 589832 | tf_op jit(solution)/shard_map/ppermute | solution.py:321
